TPU v7x, 32 devices: a whole 2x2x4 slice. The times are simulated.
32 devices in a mesh: row: 4 (over y, core), col: 8 (over z, x).
Axes of the slice: x: 2, y: 2, z: 4, core: 2. Of those that a mesh axis runs over, the one named last changes fastest.
Arguments:
- source: bfloat16 [8192, 512], P('row'), may hold values from -16 to 16
- target: bfloat16 [4096, 512], P('col'), may hold values from -6 to 6
- log_source_mass: float32 [8192], P('row'), may hold values from -1.5 to 1.5
- log_target_mass: float32 [4096], P('col'), may hold values from -1.5 to 1.5
Outputs:
- source_image: float32 [8192, 512], P(('row', 'col'))
- target_image: float32 [4096, 512], P('col')
All inputs are finite; a program needn't handle non-finite values.
Results may differ from a plain program's by a relative error of at most 0.0055.
Values sent between devices are 32-bit elements; how exact they have to be, the bound alone decides.
No kernel may reach another device: no remote copies, remote signals or barrier semaphores. Data moves between devices by JAX's collectives and lax.ppermute only.
A program may use at most 64 MiB of HBM per device.

v0:
```python
import jax
import jax.numpy as jnp
from jax import lax
from jax.sharding import PartitionSpec as P

D = 512
ITERS = 2


blur = 0.1


def tile_cost(source, target, sqx, sqy):
    inner = jnp.dot(source, target.T, preferred_element_type=jnp.float32)
    return (sqx[:, None] + sqy[None, :] - 2.0 * inner) / D


def across_targets(scores):
    local_peak = jnp.max(scores, axis=1)
    peak = lax.pmax(local_peak, "col")
    total = lax.psum(jnp.sum(jnp.exp(scores - peak[:, None]), axis=1), "col")
    return peak + jnp.log(total)


def across_sources(scores):
    local_peak = jnp.max(scores, axis=0)
    peak = lax.pmax(local_peak, "row")
    total = lax.psum(jnp.sum(jnp.exp(scores - peak[None, :]), axis=0), "row")
    return peak + jnp.log(total)


def on_device(source, target, log_source_mass, log_target_mass):
    sqx = jnp.einsum("id,id->i", source, source, preferred_element_type=jnp.float32)
    sqy = jnp.einsum("id,id->i", target, target, preferred_element_type=jnp.float32)
    g_pot = jnp.zeros((target.shape[0],), jnp.float32)
    f_pot = jnp.zeros((source.shape[0],), jnp.float32)
    for step in range(ITERS):
        cost = tile_cost(source, target, sqx, sqy)
        f_pot = -blur * across_targets(log_target_mass[None, :] + (g_pot[None, :] - cost) / blur)
        cost = tile_cost(source, target, sqx, sqy)
        g_pot = -blur * across_sources(log_source_mass[:, None] + (f_pot[:, None] - cost) / blur)
    cost = tile_cost(source, target, sqx, sqy)
    plan = jnp.exp(
        log_source_mass[:, None]
        + log_target_mass[None, :]
        + (f_pot[:, None] + g_pot[None, :] - cost) / blur
    )
    weights = plan.astype(jnp.bfloat16)
    src_numer = jnp.dot(weights, target, preferred_element_type=jnp.float32)
    src_denom = jnp.sum(plan, axis=1)
    tgt_numer = lax.dot_general(
        weights, source, (((0,), (0,)), ((), ())), preferred_element_type=jnp.float32
    )
    tgt_denom = jnp.sum(plan, axis=0)
    full_numer, full_denom = lax.psum((src_numer, src_denom), "col")
    count = source.shape[0] // lax.axis_size("col")
    start = lax.axis_index("col") * count
    own_numer = lax.dynamic_slice_in_dim(full_numer, start, count, 0)
    own_denom = lax.dynamic_slice_in_dim(full_denom, start, count, 0)
    source_image = own_numer / own_denom[:, None]
    all_numer, all_denom = lax.psum((tgt_numer, tgt_denom), "row")
    target_image = all_numer / all_denom[:, None]
    return (source_image, target_image)


def solution(mesh):
    in_specs = (P("row", None), P("col", None), P("row"), P("col"))
    out_specs = (P(("row", "col"), None), P("col", None))
    return jax.shard_map(
        on_device, mesh=mesh, in_specs=in_specs, out_specs=out_specs, check_vma=False
    )
```

profile of v0, /device:TPU:0, one launch (start us, length us, event | category | flops | bytes accessed | tf_op | source)
XLA Modules:
  0.0 348.5 jit_solution(4899817545549469030)
XLA Ops:
  7.2 0.0 all-reduce.5.cloned.1.call-start
  7.2 2.1 fusion
  9.3 1.2 fusion.5
  10.5 0.0 copy-start.3
  10.5 5.7 %fusion.1 = (f32[2048]{0:T(1024)S(1)}, f32[2048,512]{1,0:T(8,128)}) fusion(f32[512]{0:T(512)} %param.7, bf16[2048,512]{1,0:T(8,128)(2,1)} %param.4, bf16[512,512]{1,0:T(8,128)(2,1)} %param.5, f32[512]{0:T(512)S(1)} %fusion.5, f32[2048]{0:T(1024)S(1)} %fusion), kind=kOutput, calls=%fused_computation.12 | convolution fusion | flops 1082128384 | bytes 6836224 | tf_op jit(solution)/shard_map/dot_general | solution.py:14
  16.2 0.0 copy-start.2
  16.2 23.3 %pmax.28 = f32[2048]{0:T(1024)S(1)} all-reduce(f32[2048]{0:T(1024)S(1)} %get-tuple-element.4), channel_id=1, replica_groups=mesh['row'=4,'col'=8] {'col'}, use_global_device_ids=true, to_apply=%region_1.0 | all-reduce | flops 2048 | bytes 16384 | tf_op jit(solution)/shard_map/pmax | solution.py:20
  39.5 0.0 copy-done.3
  39.5 3.4 exponential_reduce_fusion.3
  42.9 17.4 %psum.56 = f32[2048]{0:T(1024)S(1)} all-reduce(f32[2048]{0:T(1024)S(1)} %exponential_reduce_fusion.3), channel_id=1, replica_groups=mesh['row'=4,'col'=8] {'col'}, use_global_device_ids=true, to_apply=%region_3.0 | all-reduce | flops 2048 | bytes 16384 | tf_op jit(solution)/shard_map/psum | solution.py:21
  60.3 0.0 copy-done.2
  60.3 2.6 fusion.2
  62.9 5.7 %pmax.29 = f32[512]{0:T(512)S(1)} all-reduce(f32[512]{0:T(512)S(1)} %fusion.2), channel_id=1, replica_groups=mesh['row'=4,'col'=8] {'row'}, use_global_device_ids=true, to_apply=%region_5.0 | all-reduce | flops 512 | bytes 4096 | tf_op jit(solution)/shard_map/pmax | solution.py:27
  68.6 2.8 exponential_reduce_fusion.2
  71.3 6.7 %psum.57 = f32[512]{0:T(512)S(1)} all-reduce(f32[512]{0:T(512)S(1)} %exponential_reduce_fusion.2), channel_id=1, replica_groups=mesh['row'=4,'col'=8] {'row'}, use_global_device_ids=true, to_apply=%region_7.0 | all-reduce | flops 512 | bytes 4096 | tf_op jit(solution)/shard_map/psum | solution.py:28
  78.0 2.8 fusion.3
  80.8 19.4 %pmax.30 = f32[2048]{0:T(1024)S(1)} all-reduce(f32[2048]{0:T(1024)S(1)} %fusion.3), channel_id=1, replica_groups=mesh['row'=4,'col'=8] {'col'}, use_global_device_ids=true, to_apply=%region_9.0 | all-reduce | flops 2048 | bytes 16384 | tf_op jit(solution)/shard_map/pmax | solution.py:20
  100.2 3.4 exponential_reduce_fusion.1
  103.6 17.5 %psum.58 = f32[2048]{0:T(1024)S(1)} all-reduce(f32[2048]{0:T(1024)S(1)} %exponential_reduce_fusion.1), channel_id=1, replica_groups=mesh['row'=4,'col'=8] {'col'}, use_global_device_ids=true, to_apply=%region_11.0 | all-reduce | flops 2048 | bytes 16384 | tf_op jit(solution)/shard_map/psum | solution.py:21
  121.1 0.0 copy-start
  121.1 2.7 fusion.4
  123.8 5.7 %pmax.31 = f32[512]{0:T(512)S(1)} all-reduce(f32[512]{0:T(512)S(1)} %fusion.4), channel_id=1, replica_groups=mesh['row'=4,'col'=8] {'row'}, use_global_device_ids=true, to_apply=%region_13.0 | all-reduce | flops 512 | bytes 4096 | tf_op jit(solution)/shard_map/pmax | solution.py:27
  129.5 2.8 exponential_reduce_fusion
  132.3 6.1 %psum.59 = f32[512]{0:T(512)S(1)} all-reduce(f32[512]{0:T(512)S(1)} %exponential_reduce_fusion), channel_id=1, replica_groups=mesh['row'=4,'col'=8] {'row'}, use_global_device_ids=true, to_apply=%region_15.0 | all-reduce | flops 512 | bytes 4096 | tf_op jit(solution)/shard_map/psum | solution.py:28
  138.5 0.0 copy-done
  138.5 0.0 copy-start.1
  138.5 5.6 %fusion.6 = f32[512,512]{1,0:T(8,128)} fusion(bf16[2048,512]{1,0:T(8,128)(2,1)S(1)} %copy-done, f32[2048,512]{1,0:T(8,128)} %get-tuple-element.5, f32[512]{0:T(512)S(1)} %add_multiply_fusion.2, f32[2048]{0:T(1024)S(1)} %add_multiply_fusion, f32[512]{0:T(512)S(1)} %copy-done.3, f32[2048]{0:T(1024)S(1)} %copy-done.2), kind=kOutput, calls=%fused_computation.18 | convolution fusion | flops 1080033280 | bytes 7360512 | tf_op jit(solution)/shard_map/dot_general | solution.py:51
  144.0 0.0 all-reduce.5.cloned.1.call-update
  144.1 0.2 all-reduce.3.cloned.1.call-start
  144.3 0.0 copy-done.1
  144.3 5.8 %fusion.8 = f32[2048,512]{1,0:T(8,128)} fusion(bf16[512,512]{1,0:T(8,128)(2,1)S(1)} %copy-done.1, f32[2048,512]{1,0:T(8,128)} %get-tuple-element.5, f32[512]{0:T(512)S(1)} %add_multiply_fusion.2, f32[2048]{0:T(1024)S(1)} %add_multiply_fusion, f32[512]{0:T(512)S(1)} %copy-done.3, f32[2048]{0:T(1024)S(1)} %copy-done.2), kind=kOutput, calls=%fused_computation.20 | convolution fusion | flops 1080033280 | bytes 8933376 | tf_op jit(solution)/shard_map/dot_general | solution.py:49
  150.1 0.0 all-reduce.3.cloned.1.call-update
  150.1 3.2 fusion.10
  153.3 19.4 %psum.61 = f32[2048]{0:T(1024)S(1)} all-reduce(f32[2048]{0:T(1024)S(1)} %get-tuple-element.3), channel_id=1, replica_groups=mesh['row'=4,'col'=8] {'col'}, use_global_device_ids=true, to_apply=%region_18.0 | all-reduce | flops 2048 | bytes 16384 | tf_op jit(solution)/shard_map/psum | solution.py:55
  172.8 0.1 dynamic_slice.7
  172.8 6.0 %psum.63 = f32[512]{0:T(512)S(1)} all-reduce(f32[512]{0:T(512)S(1)} %get-tuple-element.2), channel_id=1, replica_groups=mesh['row'=4,'col'=8] {'row'}, use_global_device_ids=true, to_apply=%region_21.0 | all-reduce | flops 512 | bytes 4096 | tf_op jit(solution)/shard_map/psum | solution.py:61
  178.9 0.0 all-reduce.5.cloned.1.call-done
  178.9 2.3 broadcast_divide_fusion
  181.2 158.4 %all-reduce.3.cloned.1.call-done = f32[2048,512]{1,0:T(8,128)} async-done(((f32[2048,512]{1,0:T(8,128)}), f32[2048,512]{1,0:T(8,128)}) %all-reduce.3.cloned.1.call-update) | async-done | bytes 4194320 | tf_op jit(solution)/shard_map/psum | solution.py:55
  339.7 1.9 dynamic-slice_divide_fusion
  (4 shorter events, 0.0 us)
Async XLA Ops:
  7.2 171.7 %all-reduce.5.cloned.1.call-start = ((), (), s32[]{:S(2)}) async-start(), calls=%async_computation.1 | async-start | bytes 2097152 | tf_op jit(solution)/shard_map/psum | solution.py:61
  10.5 29.0 %copy-start.3 = (f32[512]{0:T(512)S(1)}, f32[512]{0:T(512)}, u32[]{:S(2)}) copy-start(f32[512]{0:T(512)} %param.7) | copy-start | bytes 6148
  16.2 44.1 %copy-start.2 = (f32[2048]{0:T(1024)S(1)}, f32[2048]{0:T(1024)}, u32[]{:S(2)}) copy-start(f32[2048]{0:T(1024)} %param.6) | copy-start | bytes 24580
  121.1 17.4 %copy-start = (bf16[2048,512]{1,0:T(8,128)(2,1)S(1)}, bf16[2048,512]{1,0:T(8,128)(2,1)}, u32[]{:S(2)}) copy-start(bf16[2048,512]{1,0:T(8,128)(2,1)} %param.4) | copy-start | bytes 6291460
  138.5 5.8 %copy-start.1 = (bf16[512,512]{1,0:T(8,128)(2,1)S(1)}, bf16[512,512]{1,0:T(8,128)(2,1)}, u32[]{:S(2)}) copy-start(bf16[512,512]{1,0:T(8,128)(2,1)} %param.5) | copy-start | bytes 1572868
  144.1 195.6 %all-reduce.3.cloned.1.call-start = ((), (), s32[]{:S(2)}) async-start(), calls=%async_computation | async-start | bytes 8388608 | tf_op jit(solution)/shard_map/psum | solution.py:55
Sparse Core Ops, SparseCore 0:
  144.2 34.5 all-reduce.4
  182.9 156.7 all-reduce.2
where the time goes:
time: 349 us; the launch traced here: 348 us
  waiting for transfers between devices  158 us (45%)
  blocking collectives  127 us (36%)
  other arithmetic  31.2 us (9%)
  matrix products  17 us (5%)
  between operations  14.2 us (4%)
    psum x1, waiting for transfers between devices, on_device(): full_numer, full_denom = lax.psum((src_numer, src_denom), 'col')  158 us
    pmax x2, blocking collectives, across_targets(): peak = lax.pmax(local_peak, 'col')  42.7 us
    psum x2, blocking collectives, across_targets(): total = lax.psum(jnp.sum(jnp.exp(scores - peak[:, None]), axis=1), 'col')  34.8 us
    psum x1, blocking collectives, on_device(): full_numer, full_denom = lax.psum((src_numer, src_denom), 'col')  19.4 us
    psum x2, blocking collectives, across_sources(): total = lax.psum(jnp.sum(jnp.exp(scores - peak[None, :]), axis=0), 'row')  12.8 us
    pmax x2, blocking collectives, across_sources(): peak = lax.pmax(local_peak, 'row')  11.3 us
  transfers between devices with their start and end apart: 2, of which 1 were waited for; matrix products, arithmetic and copies ran while one was open for 3% of the time, Pallas kernels for 0%

commit v1 on v0

v1 whole, which is shorter than its diff:
```python
import math

import jax
import jax.numpy as jnp
from jax import lax
from jax.experimental import pallas as pl
from jax.experimental.pallas import tpu as pltpu
from jax.sharding import PartitionSpec as P

ITERS = 2
BLUR = 0.1
LOG2E = math.log2(math.e)
LANES = 128
NT_DIMS = (((1,), (1,)), ((), ()))
VMEM = pl.BlockSpec(memory_space=pltpu.VMEM)
HBM = pl.BlockSpec(memory_space=pltpu.HBM)
ANY = pl.BlockSpec(memory_space=pl.ANY)
DMA = pltpu.SemaphoreType.DMA


def call(kernel, out_shape, *args, in_specs=None, out_specs=None, scratch=(), limit=40):
    return pl.pallas_call(
        kernel,
        out_shape=out_shape,
        in_specs=in_specs or [VMEM] * len(args),
        out_specs=out_specs or jax.tree.map(lambda _: VMEM, out_shape),
        scratch_shapes=list(scratch),
        compiler_params=pltpu.CompilerParams(vmem_limit_bytes=limit << 20),
    )(*args)


def f32(*shape):
    return jax.ShapeDtypeStruct(shape, jnp.float32)


def bf16(*shape):
    return jax.ShapeDtypeStruct(shape, jnp.bfloat16)


def scale(width):
    return LOG2E / (width * BLUR)


def to_column(dense):
    n = dense.shape[0]
    square = jnp.concatenate([dense, jnp.zeros((LANES - n, LANES), jnp.float32)], axis=0).T
    return jnp.concatenate([square[:, b : b + 1] for b in range(n)], axis=0)


def to_dense(columns):
    lane = lax.broadcasted_iota(jnp.int32, (LANES, LANES), 1)
    square = jnp.zeros((LANES, LANES), jnp.float32)
    for b, column in enumerate(columns):
        square = jnp.where(lane == b, column, square)
    return square.T[: len(columns)]


def to_row(dense):
    return jnp.concatenate([dense[b : b + 1, :] for b in range(dense.shape[0])], axis=1)


def over_targets(scores):
    peak = jnp.max(scores, axis=0, keepdims=True)
    total = jnp.sum(jnp.exp2(scores - peak), axis=0, keepdims=True)
    return peak + jnp.log2(total)


def half_at(ref, place):
    half = ref.shape[0] // 2
    return ref[pl.ds(place * half, half), :]


def merge_all(parts):
    peak = parts[0]
    for part in parts[1:]:
        peak = jnp.maximum(peak, part)
    return peak + jnp.log2(sum(jnp.exp2(part - peak) for part in parts))


def norms(block):
    wide = block.astype(jnp.float32)
    return jnp.sum(wide * wide, axis=1, keepdims=True) * scale(block.shape[1])


def half_kernel(y_hbm, out_ref, held, sem):
    half = out_ref.shape[0]
    core = lax.axis_index("row") % 2
    copy = pltpu.make_async_copy(y_hbm.at[pl.ds(core * half, half), :], held, sem)
    copy.start()
    copy.wait()
    out_ref[...] = held[...].astype(jnp.float32)


def first_kernel(y_hbm, x_hbm, tile_ref, sqx_ref, sqy_ref, y_ref, x_ref, x_sems, y_sem):
    wide = 256
    blocks = [pl.ds(b * wide, wide) for b in range(x_hbm.shape[0] // wide)]
    y_copy = pltpu.make_async_copy(y_hbm, y_ref, y_sem)
    x_copies = [pltpu.make_async_copy(x_hbm.at[at, :], x_ref.at[at, :], x_sems.at[b]) for b, at in enumerate(blocks)]
    for copy in (y_copy, *x_copies):
        copy.start()
    y_copy.wait()
    y = y_ref[...]
    unit = scale(y.shape[1])
    sqy_ref[...] = to_dense([norms(y[b : b + LANES]) for b in range(0, y.shape[0], LANES)])
    columns = []
    for b, at in enumerate(blocks):
        x_copies[b].wait()
        x = x_ref[at, :]
        tile_ref[:, at] = lax.dot_general(y, x, NT_DIMS, preferred_element_type=jnp.float32) * (2.0 * unit)
        columns += [norms(x[c : c + LANES]) for c in range(0, wide, LANES)]
    sqx_ref[...] = to_dense(columns)


def targets_kernel(tile_ref, lt_ref, sqy_ref, total_ref, lse_ref):
    g_pot = sqy_ref[...] - total_ref[...]
    bias = to_column(lt_ref[...] * LOG2E + g_pot - sqy_ref[...])
    for b in range(tile_ref.shape[1] // LANES):
        row = over_targets(tile_ref[:, pl.ds(b * LANES, LANES)] + bias)
        for k in range(lse_ref.shape[0]):
            lse_ref[k, pl.ds(b, 1), :] = row


def sources_kernel(tile_ref, ls_ref, sqx_ref, parts_ref, bias_ref, lse_ref):
    f_pot = sqx_ref[...] - merge_all([parts_ref[k] for k in range(parts_ref.shape[0])])
    bias = ls_ref[...] * LOG2E + f_pot - sqx_ref[...]
    bias_ref[...] = bias
    blocks = range(bias.shape[0])
    columns = []
    for j in range(tile_ref.shape[0] // LANES):
        at = pl.ds(j * LANES, LANES)
        scores = [tile_ref[at, pl.ds(b * LANES, LANES)] + bias[b : b + 1, :] for b in blocks]
        top = scores[0]
        for block in scores[1:]:
            top = jnp.maximum(top, block)
        peak = jnp.max(top, axis=1, keepdims=True)
        total = jnp.sum(sum(jnp.exp2(block - peak) for block in scores), axis=1, keepdims=True)
        columns.append(peak + jnp.log2(total))
    lse_ref[...] = to_dense(columns)


def means_kernel(tile_ref, x_ref, bias_ref, total_ref, *refs):
    bias_refs, (sent_ref, mine_ref, biases_ref) = refs[:-3], refs[-3:]
    for k, ref in enumerate(bias_refs):
        biases_ref[k] = ref[...]
    bias = bias_ref[...]
    x = x_ref[...]
    half = mine_ref.shape[0]
    n_rows = half // LANES
    core = lax.axis_index("row") % 2
    for out_ref, place in ((sent_ref, 1 - core), (mine_ref, core)):
        total = to_column(total_ref[pl.ds(place * n_rows, n_rows), :])
        for j in range(n_rows):
            at = pl.ds(pl.multiple_of(place * half + j * LANES, LANES), LANES)
            norm = total[j * LANES : (j + 1) * LANES]
            exps = [
                jnp.exp2(tile_ref[at, pl.ds(b * LANES, LANES)] + bias[b : b + 1, :] - norm)
                for b in range(bias.shape[0])
            ]
            weights = jnp.concatenate([block.astype(jnp.bfloat16) for block in exps], axis=1)
            out_ref[pl.ds(j * LANES, LANES), :] = jnp.dot(weights, x, preferred_element_type=jnp.float32)


def pack_kernel(parts_hbm, total_ref, out_ref, sem):
    copy = pltpu.make_async_copy(parts_hbm, out_ref, sem)
    copy.start()
    copy.wait()


def add_kernel(one_ref, two_ref, *refs):
    refs[-1][...] = one_ref[...] + two_ref[...]


def join_kernel(n_parts, *refs):
    means, lses, out_ref = refs[:n_parts], refs[n_parts:-1], refs[-1]
    rows = out_ref.shape[0]
    total = merge_all([ref[...] for ref in lses])
    shares = [to_column(jnp.exp2(ref[...] - total))[:rows] for ref in lses]
    out_ref[...] = sum(ref[...] * share for ref, share in zip(means, shares))


def place_kernel(mine_ref, other_ref, out_hbm, sems):
    half = mine_ref.shape[0]
    core = lax.axis_index("row") % 2
    mine = pltpu.make_async_copy(mine_ref, out_hbm.at[pl.ds(core * half, half), :], sems.at[0])
    other = pltpu.make_async_copy(other_ref, out_hbm.at[pl.ds((1 - core) * half, half), :], sems.at[1])
    mine.start()
    other.start()
    mine.wait()
    other.wait()


def images(flip, n_x, x_ref, y_ref, biases_ref, mean_ref, lse_ref, scores_ref):
    rows = mean_ref.shape[0]
    n_shards = biases_ref.shape[0]
    n_tgt = y_ref.shape[0] // n_shards
    col = lax.axis_index("col")
    own = x_ref[pl.ds(pl.multiple_of((col ^ flip) * rows, rows), rows), :]
    unit = scale(own.shape[1])
    peak = jnp.full((rows, 1), -jnp.inf, jnp.float32)
    for k in range(n_shards):
        at = pl.ds(k * n_tgt, n_tgt)
        inner = lax.dot_general(own, y_ref[at, :], NT_DIMS, preferred_element_type=jnp.float32)
        scores = inner * (2.0 * unit) + to_row(biases_ref[k])
        scores_ref[:, at] = scores
        peak = jnp.maximum(peak, jnp.max(scores, axis=1, keepdims=True))
    total = jnp.zeros((rows, 1), jnp.float32)
    numer = jnp.zeros((rows, own.shape[1]), jnp.float32)
    for k in range(n_shards):
        at = pl.ds(k * n_tgt, n_tgt)
        plan = jnp.exp2(scores_ref[:, at] - peak)
        total = total + jnp.sum(plan, axis=1, keepdims=True)
        numer = numer + jnp.dot(plan.astype(jnp.bfloat16), y_ref[at, :], preferred_element_type=jnp.float32)
    mean_ref[...] = numer * (1.0 / total)
    lse = peak + jnp.log2(total)
    if rows % LANES:
        lse = jnp.concatenate([lse, jnp.zeros((-rows % LANES, 1), jnp.float32)], axis=0)
    lse_ref[...] = to_dense([lse[b * LANES : (b + 1) * LANES] for b in range(lse.shape[0] // LANES)])


def others_kernel(n_x, x_ref, mine_ref, other_ref, biases_ref, *refs):
    n_z, half, _ = mine_ref.shape
    y_ref, scores_ref = refs[0], refs[-1]
    core = lax.axis_index("row") % 2
    z = lax.axis_index("col") // n_x
    for k in range(n_z):
        for ref, place in ((mine_ref, core), (other_ref, 1 - core)):
            at = pl.ds(pl.multiple_of((2 * k + place) * half, half), half)
            y_ref[at, :] = ref[z ^ k].astype(jnp.bfloat16)
    for flip in range(1, n_x):
        images(flip, n_x, x_ref, y_ref, biases_ref, refs[2 * flip - 1], refs[2 * flip], scores_ref)


def own_kernel(n_x, x_ref, y_ref, biases_ref, mean_ref, lse_ref, scores_ref):
    images(0, n_x, x_ref, y_ref, biases_ref, mean_ref, lse_ref, scores_ref)


def swap(value, axis, distance):
    n = lax.axis_size(axis)
    return lax.ppermute(value, axis, [(i, i ^ distance) for i in range(n)])


def bits_of(n):
    return [1 << b for b in range(n.bit_length() - 1)]


def on_device(source, target, log_source_mass, log_target_mass):
    n_src, width = source.shape
    n_tgt = target.shape[0]
    n_col, n_row = lax.axis_size("col"), lax.axis_size("row")
    count = n_src // n_col
    n_x = 1 << (len(bits_of(n_col)) // 2)
    n_z = n_col // n_x
    along_z = [[z * n_x + x for z in range(n_z)] for x in range(n_x)]
    ls = log_source_mass.reshape(-1, LANES)
    lt = log_target_mass.reshape(-1, LANES)
    src_dense, tgt_dense = f32(*ls.shape), f32(*lt.shape)
    half = n_tgt // 2

    own_half = call(
        half_kernel, f32(half, width), target,
        in_specs=[ANY], scratch=[pltpu.VMEM((half, width), target.dtype), DMA], limit=58,
    )
    gathered = lax.all_gather(own_half, "col", axis_index_groups=along_z)

    tile, sqx, sqy = call(
        first_kernel,
        (f32(n_tgt, n_src), src_dense, tgt_dense),
        target, source,
        in_specs=[ANY] * 2,
        scratch=[
            pltpu.VMEM(target.shape, target.dtype), pltpu.VMEM(source.shape, source.dtype), DMA((n_src // 256,)), DMA
        ],
        limit=58,
    )

    def iteration(step, carry):
        total, _ = carry
        copies = call(targets_kernel, f32(n_col, *ls.shape), tile, lt, sqy, total)
        parts = lax.all_to_all(copies, "col", 0, 0)
        bias, lse = call(sources_kernel, (src_dense, tgt_dense), tile, ls, sqx, parts)
        return merge_all([lse] + [swap(lse, "row", k) for k in range(1, n_row)]), bias

    total, src_bias = lax.fori_loop(0, ITERS, iteration, (sqy, sqx))

    gathered = call(
        pack_kernel, f32(*gathered.shape), gathered, total, in_specs=[ANY, VMEM], scratch=[DMA], limit=58
    )
    bias = lt * LOG2E + (sqy - total) - sqy
    biases = [bias] + [swap(bias, "col", k * n_x) for k in range(1, n_z)]

    sent, mine, biases = call(
        means_kernel,
        (f32(half, width), f32(half, width), f32(n_z, *lt.shape)),
        tile, source, src_bias, total, *biases,
    )
    mine = call(add_kernel, f32(half, width), mine, swap(sent, "row", 1))
    rest = bits_of(n_row)[1:]
    for distance in rest[:-1]:
        mine = call(add_kernel, f32(half, width), mine, swap(mine, "row", distance))
    came = swap(mine, "row", rest[-1])

    scores = pltpu.VMEM((count, n_z * n_tgt), jnp.float32)
    image = [f32(count, width), f32(pl.cdiv(count, LANES), LANES)]
    all_y, *others = call(
        lambda *refs: others_kernel(n_x, *refs),
        (bf16(n_z * n_tgt, width), *image * (n_x - 1)),
        source, gathered, swap(gathered, "row", 1), biases,
        scratch=[scores],
    )
    joined = [swap(part, "col", 1 + k // 2) for k, part in enumerate(others)]
    own, own_lse = call(
        lambda *refs: own_kernel(n_x, *refs), tuple(image), source, all_y, biases, scratch=[scores]
    )
    mine = call(add_kernel, f32(half, width), mine, came, own_lse)
    target_image = call(
        place_kernel, f32(n_tgt, width), mine, swap(mine, "row", 1), out_specs=HBM, scratch=[DMA((2,))]
    )
    source_image = call(
        lambda *refs: join_kernel(n_x, *refs), f32(count, width), own, *joined[::2], own_lse, *joined[1::2]
    )
    return source_image, target_image


def solution(mesh):
    in_specs = (P("row", None), P("col", None), P("row"), P("col"))
    out_specs = (P(("row", "col"), None), P("col", None))
    return jax.shard_map(
        on_device, mesh=mesh, in_specs=in_specs, out_specs=out_specs, check_vma=False
    )
```

time: 349 us -> 114 us (0.33)
  waiting for transfers between devices: 158 us -> 30 us
  blocking collectives: 127 us -> 26.4 us
  other arithmetic: 31.2 us -> 0.05 us
  Pallas kernels: 0 us -> 30.9 us
  matrix products: 17 us -> 0 us
  starting transfers between devices: 0.26 us -> 12.1 us
    psum x2 -> x0, waiting for transfers between devices: 158 us -> none  [the longest x1 158 us: on_device(): full_numer, full_denom = lax.psum((src_numer, src_denom), 'col')]
    psum x6 -> x0, blocking collectives: 73.1 us -> none  [the longest x2 34.8 us: across_targets(): total = lax.psum(jnp.sum(jnp.exp(scores - peak[:, None]), axis=1), 'col')]
    pmax x4 -> x0, blocking collectives: 54 us -> none  [the longest x2 42.7 us: across_targets(): peak = lax.pmax(local_peak, 'col')]
    pallas_call x0 -> x14, Pallas kernels: none -> 30.9 us  [call(): pl.pallas_call(kernel, out_shape=out_shape, in_specs=in_specs or [VMEM] *...]
    ppermute x0 -> x15, waiting for transfers between devices: none -> 28.2 us  [swap(): return lax.ppermute(value, axis, [(i, i ^ distance) for i in range(n)])]
    all_to_all x0 -> x2, blocking collectives: none -> 26.4 us  [iteration(): parts = lax.all_to_all(copies, 'col', 0, 0)]
    dot_general x3 -> x0, matrix products: 17 us -> none  [the longest x1 5.78 us: on_device(): src_numer = jnp.dot(weights, target, preferred_element_type=jnp.float32)]
    reduce_sum x5 -> x0, other arithmetic: 15.5 us -> none  [the longest x2 6.74 us: across_targets(): total = lax.psum(jnp.sum(jnp.exp(scores - peak[:, None]), axis=1), 'col')]
  transfers between devices with their start and end apart: 2 -> 16, of which waited for: 1 -> 10; matrix products, arithmetic and copies ran while one was open for 3% -> 1% of each run, Pallas kernels for 0% -> 22%
where the time goes in v1:
time: 114 us
  Pallas kernels  30.9 us (27%)
  waiting for transfers between devices  30 us (26%)
  blocking collectives  26.4 us (23%)
  between operations  14.2 us (12%)
  starting transfers between devices  12.1 us (11%)
    pallas_call x14, Pallas kernels, call(): pl.pallas_call(kernel, out_shape=out_shape, in_specs=in_specs or [VMEM] *...  30.9 us
    ppermute x15, waiting for transfers between devices, swap(): return lax.ppermute(value, axis, [(i, i ^ distance) for i in range(n)])  28.2 us
    all_to_all x2, blocking collectives, iteration(): parts = lax.all_to_all(copies, 'col', 0, 0)  26.4 us
    ppermute x15, starting transfers between devices, swap(): return lax.ppermute(value, axis, [(i, i ^ distance) for i in range(n)])  12.1 us
  transfers between devices with their start and end apart: 16, of which 10 were waited for; matrix products, arithmetic and copies ran while one was open for 1% of the time, Pallas kernels for 22%

profile of v1, /device:TPU:0, one launch (start us, length us, event | category | flops | bytes accessed | tf_op | source)
XLA Modules:
  0.0 114.2 jit_solution(6304964461697436851)
XLA Ops:
  7.2 0.0 copy-start.4
  7.2 0.0 copy-start.3
  7.2 0.0 all-gather.3.cloned.1.call-start
  7.2 1.8 %shard_map.59 = f32[256,512]{1,0:T(8,128)} custom-call(bf16[512,512]{1,0:T(8,128)(2,1)} %y_hbm.3), custom_call_target="tpu_custom_call" | custom-call | tf_op jit(solution)/shard_map/pallas_call | solution.py:22
  9.0 0.0 all-gather.3.cloned.1.call-update
  9.1 7.5 %shard_map.60 = (f32[512,2048]{1,0:T(8,128)}, f32[16,128]{1,0:T(8,128)S(1)}, f32[4,128]{1,0:T(4,128)S(1)}) custom-call(bf16[512,512]{1,0:T(8,128)(2,1)} %y_hbm.3, bf16[2048,512]{1,0:T(8,128)(2,1)} %refs_0_.3), custom_call_target="tpu_custom_call" | custom-call | tf_op jit(solution)/shard_map/pallas_call | solution.py:22
  16.6 0.6 copy.8
  17.2 0.0 copy-done.4
  17.2 0.0 copy-done.3
  17.2 42.7 %while.12 = (s32[]{:T(128)}, f32[4,128]{1,0:T(4,128)S(1)}, f32[16,128]{1,0:T(8,128)}, f32[512,2048]{1,0:T(8,128)}, f32[4,128]{1,0:T(4,128)S(1)}, /*index=5*/f32[...) while((s32[]{:T(128)}, f32[4,128]{1,0:T(4,128)S(1)}, f32[16,128]{1,0:T(8,128)}, ...), condition=%wide.region_1.0_spmd, body=%wide.region_0.0_spmd.sunk | while | flops 8194 | bytes 16943344 | solution.py:283
  17.2 0.0 copy-start.2
  17.2 3.4 %eval_jaxpr.2 = f32[8,16,128]{2,1,0:T(8,128)S(1)} custom-call(f32[512,2048]{1,0:T(8,128)} %get-tuple-element.158.tile_ref, f32[4,128]{1,0:T(4,128)S(1)} %get-tuple-element.159.lt_ref, f32[4,128]{1,0:T(4,128)S(1)} %get-tuple-element.160.sqy_ref, f32[4,128]{1,0:T(4,128)S(1)} %get-tuple-element.147.total_ref), custom_call_target="tpu_custom_call" | custom-call | tf_op jit(solution)/shard_map/while/body/eval_jaxpr/pallas_call | solution.py:22
  20.6 15.1 %all_to_all.6.parts_ref = f32[8,16,128]{2,1,0:T(8,128)S(1)} all-to-all(f32[8,16,128]{2,1,0:T(8,128)S(1)} %eval_jaxpr.2), channel_id=1, replica_groups=mesh['row'=4,'col'=8] {'col'}, dimensions={0} | all-to-all | bytes 131072 | tf_op jit(solution)/shard_map/while/body/eval_jaxpr/all_to_all | solution.py:279
  35.6 0.0 copy-done.2
  35.6 1.0 eval_jaxpr.3
  36.6 0.0 collective-permute-start
  36.7 1.6 %collective-permute-start.1 = (f32[4,128]{1,0:T(4,128)S(1)}, f32[4,128]{1,0:T(4,128)S(1)}, u32[]{:S(2)}, u32[]{:S(2)}) collective-permute-start(f32[4,128]{1,0:T(4,128)S(1)} %get-tuple-element.135), channel_id=1, source_target_pairs={{0,16},{8,24},{16,0},{24,8},{1,17},{9,25},{17,1},{25,9},{2,18},{10... | collective-permute-start | bytes 6152 | tf_op jit(solution)/shard_map/while/body/eval_jaxpr/ppermute | solution.py:239
  38.3 0.3 collective-permute-start.2
  38.5 1.1 %collective-permute-done = f32[4,128]{1,0:T(4,128)S(1)} collective-permute-done((f32[4,128]{1,0:T(4,128)S(1)}, f32[4,128]{1,0:T(4,128)S(1)}, u32[]{:S(2)}, u32[]{:S(2)}) %collective-permute-start) | collective-permute-done | bytes 2080 | tf_op jit(solution)/shard_map/while/body/eval_jaxpr/ppermute | solution.py:239
  39.7 0.7 collective-permute-done.1
  40.3 0.0 collective-permute-done.2
  40.4 0.0 copy-start.2
  40.4 3.4 %eval_jaxpr.2 = f32[8,16,128]{2,1,0:T(8,128)S(1)} custom-call(f32[512,2048]{1,0:T(8,128)} %get-tuple-element.158.tile_ref, f32[4,128]{1,0:T(4,128)S(1)} %get-tuple-element.159.lt_ref, f32[4,128]{1,0:T(4,128)S(1)} %get-tuple-element.160.sqy_ref, f32[4,128]{1,0:T(4,128)S(1)} %get-tuple-element.147.total_ref), custom_call_target="tpu_custom_call" | custom-call | tf_op jit(solution)/shard_map/while/body/eval_jaxpr/pallas_call | solution.py:22
  43.8 11.3 %all_to_all.6.parts_ref = f32[8,16,128]{2,1,0:T(8,128)S(1)} all-to-all(f32[8,16,128]{2,1,0:T(8,128)S(1)} %eval_jaxpr.2), channel_id=1, replica_groups=mesh['row'=4,'col'=8] {'col'}, dimensions={0} | all-to-all | bytes 131072 | tf_op jit(solution)/shard_map/while/body/eval_jaxpr/all_to_all | solution.py:279
  55.1 0.0 copy-done.2
  55.1 1.0 eval_jaxpr.3
  56.1 0.0 collective-permute-start
  56.2 1.4 %collective-permute-start.1 = (f32[4,128]{1,0:T(4,128)S(1)}, f32[4,128]{1,0:T(4,128)S(1)}, u32[]{:S(2)}, u32[]{:S(2)}) collective-permute-start(f32[4,128]{1,0:T(4,128)S(1)} %get-tuple-element.135), channel_id=1, source_target_pairs={{0,16},{8,24},{16,0},{24,8},{1,17},{9,25},{17,1},{25,9},{2,18},{10... | collective-permute-start | bytes 6152 | tf_op jit(solution)/shard_map/while/body/eval_jaxpr/ppermute | solution.py:239
  57.5 0.5 collective-permute-start.2
  58.0 1.1 %collective-permute-done = f32[4,128]{1,0:T(4,128)S(1)} collective-permute-done((f32[4,128]{1,0:T(4,128)S(1)}, f32[4,128]{1,0:T(4,128)S(1)}, u32[]{:S(2)}, u32[]{:S(2)}) %collective-permute-start) | collective-permute-done | bytes 2080 | tf_op jit(solution)/shard_map/while/body/eval_jaxpr/ppermute | solution.py:239
  59.2 0.7 collective-permute-done.1
  59.8 0.0 collective-permute-done.2
  59.9 1.7 %all-gather.3.cloned.1.call-done = f32[1024,512]{1,0:T(8,128)} async-done(((f32[256,512]{1,0:T(8,128)}), f32[1024,512]{1,0:T(8,128)}) %all-gather.3.cloned.1.call-update) | async-done | bytes 2097168 | tf_op jit(solution)/shard_map/all_gather | solution.py:263
  61.6 0.0 copy-start
  61.6 0.0 copy-start.5
  61.6 3.1 %shard_map.61.refs_1_ = f32[4,256,512]{2,1,0:T(8,128)} custom-call(f32[4,256,512]{2,1,0:T(8,128)} %bitcast.4, f32[4,128]{1,0:T(4,128)S(1)} %get-tuple-element.60.total_ref), custom_call_target="tpu_custom_call" | custom-call | tf_op jit(solution)/shard_map/pallas_call | solution.py:22
  64.7 0.1 collective-permute-start.3
  64.8 0.1 collective-permute-start.4
  64.9 1.7 %collective-permute-start.5 = (f32[4,128]{1,0:T(4,128)S(1)}, f32[4,128]{1,0:T(4,128)S(1)}, u32[]{:S(2)}, u32[]{:S(2)}) collective-permute-start(f32[4,128]{1,0:T(4,128)S(1)} %add_subtract_fusion.refs_0_), channel_id=1, source_target_pairs={{0,4},{1,5},{2,6},{3,7},{4,0},{5,1},{6,2},{7,3},{8,12},{9,13},{10,... | collective-permute-start | bytes 6152 | tf_op jit(solution)/shard_map/ppermute | solution.py:239
  66.6 2.7 %collective-permute-start.6 = (f32[4,128]{1,0:T(4,128)S(1)}, f32[4,128]{1,0:T(4,128)S(1)}, u32[]{:S(2)}, u32[]{:S(2)}) collective-permute-start(f32[4,128]{1,0:T(4,128)S(1)} %add_subtract_fusion.refs_0_), channel_id=1, source_target_pairs={{0,6},{1,7},{2,4},{3,5},{4,2},{5,3},{6,0},{7,1},{8,14},{9,15},{10,... | collective-permute-start | bytes 6152 | tf_op jit(solution)/shard_map/ppermute | solution.py:239
  69.3 0.0 collective-permute-done.4.refs_1_
  69.3 0.2 collective-permute-done.5.refs_2_
  69.5 2.5 %collective-permute-done.6.refs_3_ = f32[4,128]{1,0:T(4,128)S(1)} collective-permute-done((f32[4,128]{1,0:T(4,128)S(1)}, f32[4,128]{1,0:T(4,128)S(1)}, u32[]{:S(2)}, u32[]{:S(2)}) %collective-permute-start.6) | collective-permute-done | bytes 2080 | tf_op jit(solution)/shard_map/ppermute | solution.py:239
  72.0 0.0 copy-done
  72.0 0.0 copy-done.5
  72.0 3.7 %shard_map.62 = (f32[256,512]{1,0:T(8,128)S(1)}, f32[256,512]{1,0:T(8,128)S(1)}, f32[4,4,128]{2,1,0:T(4,128)S(1)}) custom-call(f32[512,2048]{1,0:T(8,128)} %get-tuple-element.186, bf16[2048,512]{1,0:T(8,128)(2,1)S(1)} %copy-done, f32[16,128]{1,0:T(8,128)S(1)} %copy-done.5, f32[4,128]{1,0:T(4,128)S(1)} %get-tuple-element.60.total_ref, ...), custom_call_target="tpu_custom_call" | custom-call | tf_op jit(solution)/shard_map/pallas_call | solution.py:22
  75.7 0.1 collective-permute-start.9
  75.8 1.9 %collective-permute-done.9.two_ref = f32[256,512]{1,0:T(8,128)S(1)} collective-permute-done((f32[256,512]{1,0:T(8,128)S(1)}, f32[256,512]{1,0:T(8,128)S(1)}, u32[]{:S(2)}, u32[]{:S(2)}) %collective-permute-start.9) | collective-permute-done | bytes 524320 | tf_op jit(solution)/shard_map/ppermute | solution.py:239
  77.7 0.1 shard_map.66.one_ref
  77.7 1.6 %collective-permute-start.10 = (f32[256,512]{1,0:T(8,128)S(1)}, f32[256,512]{1,0:T(8,128)S(1)}, u32[]{:S(2)}, u32[]{:S(2)}) collective-permute-start(f32[256,512]{1,0:T(8,128)S(1)} %shard_map.66.one_ref), channel_id=1, source_target_pairs={{0,16},{8,24},{16,0},{24,8},{1,17},{9,25},{17,1},{25,9},{2,18},{10... | collective-permute-start | bytes 1572872 | tf_op jit(solution)/shard_map/ppermute | solution.py:239
  79.3 0.0 collective-permute-done.3.refs_2_
  79.3 0.0 copy-done.1
  79.3 2.1 %shard_map.63 = (bf16[2048,512]{1,0:T(8,128)(2,1)S(1)}, f32[256,512]{1,0:T(8,128)S(1)}, f32[2,128]{1,0:T(2,128)S(1)}) custom-call(bf16[2048,512]{1,0:T(8,128)(2,1)S(1)} %copy-done, f32[4,256,512]{2,1,0:T(8,128)S(1)} %copy-done.1, f32[4,256,512]{2,1,0:T(8,128)S(1)} %collective-permute-done.3.refs_2_, f32[4,4,128]{2,1,0:T(4,128)S(1)} %get-tuple-element.62.refs_3_.refs_2_), custom_call_target="tpu_custom_call" | custom-call | tf_op jit(solution)/shard_map/pallas_call | solution.py:22
  81.4 1.7 %shard_map.64 = (f32[256,512]{1,0:T(8,128)S(1)}, f32[2,128]{1,0:T(2,128)S(1)}) custom-call(bf16[2048,512]{1,0:T(8,128)(2,1)S(1)} %copy-done, bf16[2048,512]{1,0:T(8,128)(2,1)S(1)} %get-tuple-element.63.refs_1_, f32[4,4,128]{2,1,0:T(4,128)S(1)} %get-tuple-element.62.refs_3_.refs_2_), custom_call_target="tpu_custom_call" | custom-call | tf_op jit(solution)/shard_map/pallas_call | solution.py:22
  83.1 8.7 %collective-permute-done.10.two_ref = f32[256,512]{1,0:T(8,128)S(1)} collective-permute-done((f32[256,512]{1,0:T(8,128)S(1)}, f32[256,512]{1,0:T(8,128)S(1)}, u32[]{:S(2)}, u32[]{:S(2)}) %collective-permute-start.10) | collective-permute-done | bytes 524320 | tf_op jit(solution)/shard_map/ppermute | solution.py:239
  91.8 0.1 shard_map.67.mine_ref
  91.8 0.1 collective-permute-start.11
  91.9 1.6 %collective-permute-start.7 = (f32[256,512]{1,0:T(8,128)S(1)}, f32[256,512]{1,0:T(8,128)S(1)}, u32[]{:S(2)}, u32[]{:S(2)}) collective-permute-start(f32[256,512]{1,0:T(8,128)S(1)} %get-tuple-element.65), channel_id=1, source_target_pairs={{0,1},{1,0},{2,3},{3,2},{4,5},{5,4},{6,7},{7,6},{8,9},{9,8},{10,11... | collective-permute-start | bytes 1572872 | tf_op jit(solution)/shard_map/ppermute | solution.py:239
  93.5 0.5 collective-permute-start.8
  94.0 0.0 collective-permute-done.11.other_ref
  94.0 1.0 shard_map.68
  95.0 11.3 %collective-permute-done.8.refs_3_ = f32[2,128]{1,0:T(2,128)S(1)} collective-permute-done((f32[2,128]{1,0:T(2,128)S(1)}, f32[2,128]{1,0:T(2,128)S(1)}, u32[]{:S(2)}, u32[]{:S(2)}) %collective-permute-start.8) | collective-permute-done | bytes 1056 | tf_op jit(solution)/shard_map/ppermute | solution.py:239
  106.3 0.0 collective-permute-done.7.refs_1_
  106.3 1.1 shard_map.65
  (5 shorter events, 0.0 us)
Async XLA Ops:
  7.2 10.0 %copy-start.4 = (f32[512]{0:T(512)S(1)}, f32[512]{0:T(512)}, u32[]{:S(2)}) copy-start(f32[512]{0:T(512)} %param.9) | copy-start | bytes 6148
  7.2 10.0 %copy-start.3 = (f32[2048]{0:T(1024)S(1)}, f32[2048]{0:T(1024)}, u32[]{:S(2)}) copy-start(f32[2048]{0:T(1024)} %param.8) | copy-start | bytes 24580
  7.2 54.4 %all-gather.3.cloned.1.call-start = ((), (), s32[]{:S(2)}) async-start(), calls=%async_computation.1 | async-start | bytes 2621440 | tf_op jit(solution)/shard_map/all_gather | solution.py:263
  17.2 18.5 %copy-start.2 = (f32[512,2048]{1,0:T(8,128)S(1)}, f32[512,2048]{1,0:T(8,128)}, u32[]{:S(2)}) copy-start(f32[512,2048]{1,0:T(8,128)} %get-tuple-element.158.tile_ref) | copy-start | bytes 12582916 | tf_op jit(solution)/shard_map/while
  36.6 3.1 %collective-permute-start = (f32[4,128]{1,0:T(4,128)S(1)}, f32[4,128]{1,0:T(4,128)S(1)}, u32[]{:S(2)}, u32[]{:S(2)}) collective-permute-start(f32[4,128]{1,0:T(4,128)S(1)} %get-tuple-element.135), channel_id=1, source_target_pairs={{0,24},{8,16},{16,8},{24,0},{1,25},{9,17},{17,9},{25,1},{2,26},{10... | collective-permute-start | bytes 6152 | tf_op jit(solution)/shard_map/while/body/eval_jaxpr/ppermute | solution.py:239
  36.7 3.7 %collective-permute-start.1 = (f32[4,128]{1,0:T(4,128)S(1)}, f32[4,128]{1,0:T(4,128)S(1)}, u32[]{:S(2)}, u32[]{:S(2)}) collective-permute-start(f32[4,128]{1,0:T(4,128)S(1)} %get-tuple-element.135), channel_id=1, source_target_pairs={{0,16},{8,24},{16,0},{24,8},{1,17},{9,25},{17,1},{25,9},{2,18},{10... | collective-permute-start | bytes 6152 | tf_op jit(solution)/shard_map/while/body/eval_jaxpr/ppermute | solution.py:239
  38.3 2.1 %collective-permute-start.2 = (f32[4,128]{1,0:T(4,128)S(1)}, f32[4,128]{1,0:T(4,128)S(1)}, u32[]{:S(2)}, u32[]{:S(2)}) collective-permute-start(f32[4,128]{1,0:T(4,128)S(1)} %get-tuple-element.135), channel_id=1, source_target_pairs={{0,8},{8,0},{16,24},{24,16},{1,9},{9,1},{17,25},{25,17},{2,10},{10... | collective-permute-start | bytes 6152 | tf_op jit(solution)/shard_map/while/body/eval_jaxpr/ppermute | solution.py:239
  40.4 14.7 %copy-start.2 = (f32[512,2048]{1,0:T(8,128)S(1)}, f32[512,2048]{1,0:T(8,128)}, u32[]{:S(2)}) copy-start(f32[512,2048]{1,0:T(8,128)} %get-tuple-element.158.tile_ref) | copy-start | bytes 12582916 | tf_op jit(solution)/shard_map/while
  56.1 3.1 %collective-permute-start = (f32[4,128]{1,0:T(4,128)S(1)}, f32[4,128]{1,0:T(4,128)S(1)}, u32[]{:S(2)}, u32[]{:S(2)}) collective-permute-start(f32[4,128]{1,0:T(4,128)S(1)} %get-tuple-element.135), channel_id=1, source_target_pairs={{0,24},{8,16},{16,8},{24,0},{1,25},{9,17},{17,9},{25,1},{2,26},{10... | collective-permute-start | bytes 6152 | tf_op jit(solution)/shard_map/while/body/eval_jaxpr/ppermute | solution.py:239
  56.2 3.7 %collective-permute-start.1 = (f32[4,128]{1,0:T(4,128)S(1)}, f32[4,128]{1,0:T(4,128)S(1)}, u32[]{:S(2)}, u32[]{:S(2)}) collective-permute-start(f32[4,128]{1,0:T(4,128)S(1)} %get-tuple-element.135), channel_id=1, source_target_pairs={{0,16},{8,24},{16,0},{24,8},{1,17},{9,25},{17,1},{25,9},{2,18},{10... | collective-permute-start | bytes 6152 | tf_op jit(solution)/shard_map/while/body/eval_jaxpr/ppermute | solution.py:239
  57.5 2.3 %collective-permute-start.2 = (f32[4,128]{1,0:T(4,128)S(1)}, f32[4,128]{1,0:T(4,128)S(1)}, u32[]{:S(2)}, u32[]{:S(2)}) collective-permute-start(f32[4,128]{1,0:T(4,128)S(1)} %get-tuple-element.135), channel_id=1, source_target_pairs={{0,8},{8,0},{16,24},{24,16},{1,9},{9,1},{17,25},{25,17},{2,10},{10... | collective-permute-start | bytes 6152 | tf_op jit(solution)/shard_map/while/body/eval_jaxpr/ppermute | solution.py:239
  61.6 10.4 %copy-start = (bf16[2048,512]{1,0:T(8,128)(2,1)S(1)}, bf16[2048,512]{1,0:T(8,128)(2,1)}, u32[]{:S(2)}) copy-start(bf16[2048,512]{1,0:T(8,128)(2,1)} %refs_0_.3) | copy-start | bytes 6291460
  61.6 10.4 %copy-start.5 = (f32[16,128]{1,0:T(8,128)S(1)}, f32[16,128]{1,0:T(8,128)}, u32[]{:S(2)}) copy-start(f32[16,128]{1,0:T(8,128)} %get-tuple-element.61.bias_ref) | copy-start | bytes 24580
  64.7 14.6 %collective-permute-start.3 = (f32[4,256,512]{2,1,0:T(8,128)}, f32[4,256,512]{2,1,0:T(8,128)S(1)}, u32[]{:S(2)}, u32[]{:S(2)}) collective-permute-start(f32[4,256,512]{2,1,0:T(8,128)} %shard_map.61.refs_1_), channel_id=1, source_target_pairs={{0,8},{8,0},{16,24},{24,16},{1,9},{9,1},{17,25},{25,17},{2,10},{10... | collective-permute-start | bytes 6291464 | tf_op jit(solution)/shard_map/ppermute | solution.py:239
  64.8 4.5 %collective-permute-start.4 = (f32[4,128]{1,0:T(4,128)S(1)}, f32[4,128]{1,0:T(4,128)S(1)}, u32[]{:S(2)}, u32[]{:S(2)}) collective-permute-start(f32[4,128]{1,0:T(4,128)S(1)} %add_subtract_fusion.refs_0_), channel_id=1, source_target_pairs={{0,2},{1,3},{2,0},{3,1},{4,6},{5,7},{6,4},{7,5},{8,10},{9,11},{10,... | collective-permute-start | bytes 6152 | tf_op jit(solution)/shard_map/ppermute | solution.py:239
  64.9 4.5 %collective-permute-start.5 = (f32[4,128]{1,0:T(4,128)S(1)}, f32[4,128]{1,0:T(4,128)S(1)}, u32[]{:S(2)}, u32[]{:S(2)}) collective-permute-start(f32[4,128]{1,0:T(4,128)S(1)} %add_subtract_fusion.refs_0_), channel_id=1, source_target_pairs={{0,4},{1,5},{2,6},{3,7},{4,0},{5,1},{6,2},{7,3},{8,12},{9,13},{10,... | collective-permute-start | bytes 6152 | tf_op jit(solution)/shard_map/ppermute | solution.py:239
  66.6 5.4 %collective-permute-start.6 = (f32[4,128]{1,0:T(4,128)S(1)}, f32[4,128]{1,0:T(4,128)S(1)}, u32[]{:S(2)}, u32[]{:S(2)}) collective-permute-start(f32[4,128]{1,0:T(4,128)S(1)} %add_subtract_fusion.refs_0_), channel_id=1, source_target_pairs={{0,6},{1,7},{2,4},{3,5},{4,2},{5,3},{6,0},{7,1},{8,14},{9,15},{10,... | collective-permute-start | bytes 6152 | tf_op jit(solution)/shard_map/ppermute | solution.py:239
  72.0 7.3 %copy-start.1 = (f32[4,256,512]{2,1,0:T(8,128)S(1)}, f32[4,256,512]{2,1,0:T(8,128)}, u32[]{:S(2)}) copy-start(f32[4,256,512]{2,1,0:T(8,128)} %shard_map.61.refs_1_) | copy-start | bytes 6291460
  75.7 2.0 %collective-permute-start.9 = (f32[256,512]{1,0:T(8,128)S(1)}, f32[256,512]{1,0:T(8,128)S(1)}, u32[]{:S(2)}, u32[]{:S(2)}) collective-permute-start(f32[256,512]{1,0:T(8,128)S(1)} %get-tuple-element.69), channel_id=1, source_target_pairs={{0,8},{8,0},{16,24},{24,16},{1,9},{9,1},{17,25},{25,17},{2,10},{10... | collective-permute-start | bytes 1572872 | tf_op jit(solution)/shard_map/ppermute | solution.py:239
  77.7 14.0 %collective-permute-start.10 = (f32[256,512]{1,0:T(8,128)S(1)}, f32[256,512]{1,0:T(8,128)S(1)}, u32[]{:S(2)}, u32[]{:S(2)}) collective-permute-start(f32[256,512]{1,0:T(8,128)S(1)} %shard_map.66.one_ref), channel_id=1, source_target_pairs={{0,16},{8,24},{16,0},{24,8},{1,17},{9,25},{17,1},{25,9},{2,18},{10... | collective-permute-start | bytes 1572872 | tf_op jit(solution)/shard_map/ppermute | solution.py:239
  91.8 2.2 %collective-permute-start.11 = (f32[256,512]{1,0:T(8,128)S(1)}, f32[256,512]{1,0:T(8,128)S(1)}, u32[]{:S(2)}, u32[]{:S(2)}) collective-permute-start(f32[256,512]{1,0:T(8,128)S(1)} %shard_map.67.mine_ref), channel_id=1, source_target_pairs={{0,8},{8,0},{16,24},{24,16},{1,9},{9,1},{17,25},{25,17},{2,10},{10... | collective-permute-start | bytes 1572872 | tf_op jit(solution)/shard_map/ppermute | solution.py:239
  91.9 14.4 %collective-permute-start.7 = (f32[256,512]{1,0:T(8,128)S(1)}, f32[256,512]{1,0:T(8,128)S(1)}, u32[]{:S(2)}, u32[]{:S(2)}) collective-permute-start(f32[256,512]{1,0:T(8,128)S(1)} %get-tuple-element.65), channel_id=1, source_target_pairs={{0,1},{1,0},{2,3},{3,2},{4,5},{5,4},{6,7},{7,6},{8,9},{9,8},{10,11... | collective-permute-start | bytes 1572872 | tf_op jit(solution)/shard_map/ppermute | solution.py:239
  93.5 12.8 %collective-permute-start.8 = (f32[2,128]{1,0:T(2,128)S(1)}, f32[2,128]{1,0:T(2,128)S(1)}, u32[]{:S(2)}, u32[]{:S(2)}) collective-permute-start(f32[2,128]{1,0:T(2,128)S(1)} %get-tuple-element.67), channel_id=1, source_target_pairs={{0,1},{1,0},{2,3},{3,2},{4,5},{5,4},{6,7},{7,6},{8,9},{9,8},{10,11... | collective-permute-start | bytes 3080 | tf_op jit(solution)/shard_map/ppermute | solution.py:239
Sparse Core Ops, SparseCore 0:
  10.2 51.3 all-gather.2

commit v2 on v1

v2 whole, which is shorter than its diff:
```python
import math

import jax
import jax.numpy as jnp
from jax import lax
from jax.experimental import pallas as pl
from jax.experimental.pallas import tpu as pltpu
from jax.sharding import PartitionSpec as P

ITERS = 2
BLUR = 0.1
LOG2E = math.log2(math.e)
LANES = 128
NT_DIMS = (((1,), (1,)), ((), ()))
VMEM = pl.BlockSpec(memory_space=pltpu.VMEM)
HBM = pl.BlockSpec(memory_space=pltpu.HBM)
ANY = pl.BlockSpec(memory_space=pl.ANY)
DMA = pltpu.SemaphoreType.DMA


def call(kernel, out_shape, *args, in_specs=None, out_specs=None, scratch=(), limit=24):
    return pl.pallas_call(
        kernel,
        out_shape=out_shape,
        in_specs=in_specs or [VMEM] * len(args),
        out_specs=out_specs or jax.tree.map(lambda _: VMEM, out_shape),
        scratch_shapes=list(scratch),
        compiler_params=pltpu.CompilerParams(vmem_limit_bytes=limit << 20),
    )(*args)


def f32(*shape):
    return jax.ShapeDtypeStruct(shape, jnp.float32)


def bf16(*shape):
    return jax.ShapeDtypeStruct(shape, jnp.bfloat16)


def scale(width):
    return LOG2E / (width * BLUR)


def to_column(dense):
    n = dense.shape[0]
    square = jnp.concatenate([dense, jnp.zeros((LANES - n, LANES), jnp.float32)], axis=0).T
    return jnp.concatenate([square[:, b : b + 1] for b in range(n)], axis=0)


def to_dense(columns):
    lane = lax.broadcasted_iota(jnp.int32, (LANES, LANES), 1)
    square = jnp.zeros((LANES, LANES), jnp.float32)
    for b, column in enumerate(columns):
        square = jnp.where(lane == b, column, square)
    return square.T[: len(columns)]


def to_row(dense):
    return jnp.concatenate([dense[b : b + 1, :] for b in range(dense.shape[0])], axis=1)


def over_targets(scores):
    peak = jnp.max(scores, axis=0, keepdims=True)
    total = jnp.sum(jnp.exp2(scores - peak), axis=0, keepdims=True)
    return peak + jnp.log2(total)


def half_at(ref, place):
    half = ref.shape[0] // 2
    return ref[pl.ds(place * half, half), :]


def merge_all(parts):
    peak = parts[0]
    for part in parts[1:]:
        peak = jnp.maximum(peak, part)
    return peak + jnp.log2(sum(jnp.exp2(part - peak) for part in parts))


def norms(block):
    wide = block.astype(jnp.float32)
    return jnp.sum(wide * wide, axis=1, keepdims=True) * scale(block.shape[1])


def half_kernel(y_ref, *out_refs):
    part = out_refs[0].shape[0]
    start = lax.axis_index("row") % 2 * part * len(out_refs)
    for k, ref in enumerate(out_refs):
        ref[...] = y_ref[pl.ds(pl.multiple_of(start + k * part, part), part), :].astype(jnp.float32)


def first_kernel(y_ref, x_ref, lt_ref, tile_ref, lse_ref, sqx_ref, sqy_ref):
    wide = 256
    y = y_ref[...]
    unit = scale(y.shape[1])
    sqy = norms(y)
    sqy_ref[...] = to_dense([sqy[b : b + LANES] for b in range(0, y.shape[0], LANES)])
    bias = to_column(lt_ref[...]) * LOG2E - sqy
    columns = []
    for b in range(x_ref.shape[0] // wide):
        at = pl.ds(b * wide, wide)
        x = x_ref[at, :]
        tile = lax.dot_general(y, x, NT_DIMS, preferred_element_type=jnp.float32) * (2.0 * unit)
        tile_ref[:, at] = tile
        row = over_targets(tile + bias)
        for c in range(wide // LANES):
            lse_ref[pl.ds(b * (wide // LANES) + c, 1), :] = row[:, c * LANES : (c + 1) * LANES]
        columns += [norms(x[c : c + LANES]) for c in range(0, wide, LANES)]
    sqx_ref[...] = to_dense(columns)


def targets_kernel(tile_ref, lt_ref, sqy_ref, *refs):
    parts, lse_ref = refs[:-1], refs[-1]
    g_pot = sqy_ref[...] - merge_all([ref[...] for ref in parts])
    bias = to_column(lt_ref[...] * LOG2E + g_pot - sqy_ref[...])
    for b in range(tile_ref.shape[1] // LANES):
        lse_ref[pl.ds(b, 1), :] = over_targets(tile_ref[:, pl.ds(b * LANES, LANES)] + bias)


def sources_kernel(tile_ref, ls_ref, sqx_ref, *refs):
    parts, (bias_ref, lse_ref) = refs[:-2], refs[-2:]
    f_pot = sqx_ref[...] - merge_all([ref[...] for ref in parts])
    bias = ls_ref[...] * LOG2E + f_pot - sqx_ref[...]
    bias_ref[...] = bias
    blocks = range(bias.shape[0])
    columns = []
    for j in range(tile_ref.shape[0] // LANES):
        at = pl.ds(j * LANES, LANES)
        scores = [tile_ref[at, pl.ds(b * LANES, LANES)] + bias[b : b + 1, :] for b in blocks]
        top = scores[0]
        for block in scores[1:]:
            top = jnp.maximum(top, block)
        peak = jnp.max(top, axis=1, keepdims=True)
        total = jnp.sum(sum(jnp.exp2(block - peak) for block in scores), axis=1, keepdims=True)
        columns.append(peak + jnp.log2(total))
    lse_ref[...] = to_dense(columns)


def means_kernel(tile_ref, x_ref, bias_ref, total_ref, after_ref, sent_ref, mine_ref):
    bias = bias_ref[...]
    x = x_ref[...]
    half = mine_ref.shape[0]
    n_rows = half // LANES
    core = lax.axis_index("row") % 2
    for out_ref, place in ((sent_ref, 1 - core), (mine_ref, core)):
        total = to_column(total_ref[pl.ds(place * n_rows, n_rows), :])
        for j in range(n_rows):
            at = pl.ds(pl.multiple_of(place * half + j * LANES, LANES), LANES)
            norm = total[j * LANES : (j + 1) * LANES]
            exps = [
                jnp.exp2(tile_ref[at, pl.ds(b * LANES, LANES)] + bias[b : b + 1, :] - norm)
                for b in range(bias.shape[0])
            ]
            weights = jnp.concatenate([block.astype(jnp.bfloat16) for block in exps], axis=1)
            out_ref[pl.ds(j * LANES, LANES), :] = jnp.dot(weights, x, preferred_element_type=jnp.float32)


def add_kernel(one_ref, two_ref, *refs):
    refs[-1][...] = one_ref[...] + two_ref[...]


def join_kernel(own_ref, shares_ref, *refs):
    out_ref = refs[-1]
    rows = out_ref.shape[0]
    out_ref[...] = own_ref[...] + sum(ref[...] * to_column(shares_ref[k])[:rows] for k, ref in enumerate(refs[:-1]))


def place_kernel(mine_ref, other_ref, out_hbm, sems):
    half = mine_ref.shape[0]
    core = lax.axis_index("row") % 2
    mine = pltpu.make_async_copy(mine_ref, out_hbm.at[pl.ds(core * half, half), :], sems.at[0])
    other = pltpu.make_async_copy(other_ref, out_hbm.at[pl.ds((1 - core) * half, half), :], sems.at[1])
    mine.start()
    other.start()
    mine.wait()
    other.wait()


def scores_kernel(n_x, x_ref, *refs):
    parts, (y_ref, inner_ref) = refs[:-2], refs[-2:]
    rows = inner_ref.shape[0]
    start = lax.axis_index("col") // n_x * rows
    own = x_ref[pl.ds(pl.multiple_of(start, rows), rows), :]
    unit = scale(own.shape[1])
    piece = 128
    wide = piece * len(parts)
    for b in range(y_ref.shape[0] // wide):
        at = pl.ds(b * wide, wide)
        y = jnp.concatenate([ref[pl.ds(b * piece, piece), :] for ref in parts], axis=0).astype(jnp.bfloat16)
        y_ref[at, :] = y
        inner_ref[:, at] = lax.dot_general(own, y, NT_DIMS, preferred_element_type=jnp.float32) * (2.0 * unit)


def images(flip, n_x, inner_ref, y_ref, bias_refs, scores_ref):
    rows = scores_ref.shape[0]
    n_shards = len(bias_refs)
    n_tgt = y_ref.shape[0] // n_shards
    start = ((lax.axis_index("col") ^ flip) % n_x) * rows
    block = pl.ds(pl.multiple_of(start, rows), rows)
    peak = jnp.full((rows, 1), -jnp.inf, jnp.float32)
    z = lax.axis_index("col") // n_x
    for k in range(n_shards):
        at = pl.ds(pl.multiple_of((z ^ k) * n_tgt, n_tgt), n_tgt)
        scores = inner_ref[block, at] + to_row(bias_refs[k][...])
        scores_ref[:, at] = scores
        peak = jnp.maximum(peak, jnp.max(scores, axis=1, keepdims=True))
    total = jnp.zeros((rows, 1), jnp.float32)
    numer = jnp.zeros((rows, y_ref.shape[1]), jnp.float32)
    for k in range(n_shards):
        at = pl.ds(k * n_tgt, n_tgt)
        plan = jnp.exp2(scores_ref[:, at] - peak)
        total = total + jnp.sum(plan, axis=1, keepdims=True)
        numer = numer + jnp.dot(plan.astype(jnp.bfloat16), y_ref[at, :], preferred_element_type=jnp.float32)
    return numer, total, peak


def lanes_of(column):
    rows = column.shape[0]
    if rows % LANES:
        column = jnp.concatenate([column, jnp.zeros((-rows % LANES, 1), jnp.float32)], axis=0)
    return to_dense([column[b : b + LANES] for b in range(0, column.shape[0], LANES)])


def others_kernel(n_x, n_z, inner_ref, y_ref, *refs):
    bias_refs, refs = refs[:n_z], refs[n_z:]
    for flip in range(1, n_x):
        numer, total, peak = images(flip, n_x, inner_ref, y_ref, bias_refs, refs[-1])
        refs[2 * flip - 2][...] = numer * (1.0 / total)
        refs[2 * flip - 1][...] = lanes_of(peak + jnp.log2(total))


def own_kernel(n_x, n_z, inner_ref, y_ref, *refs):
    bias_refs, lses, (out_ref, shares_ref, scores_ref) = refs[:n_z], refs[n_z:-3], refs[-3:]
    numer, total, peak = images(0, n_x, inner_ref, y_ref, bias_refs, scores_ref)
    rows = numer.shape[0]
    lse = lanes_of(peak + jnp.log2(total))
    came = [ref[...] for ref in lses]
    whole = merge_all([lse] + came)
    out_ref[...] = numer * (to_column(jnp.exp2(lse - whole))[:rows] / total)
    for k, part in enumerate(came):
        shares_ref[k] = jnp.exp2(part - whole)


def swap(value, axis, distance):
    n = lax.axis_size(axis)
    return lax.ppermute(value, axis, [(i, i ^ distance) for i in range(n)])


def bits_of(n):
    return [1 << b for b in range(n.bit_length() - 1)]


def on_device(source, target, log_source_mass, log_target_mass):
    n_src, width = source.shape
    n_tgt = target.shape[0]
    n_col, n_row = lax.axis_size("col"), lax.axis_size("row")
    count = n_src // n_col
    n_x = 1 << (len(bits_of(n_col)) // 2)
    n_z = n_col // n_x
    along_z = [[z * n_x + x for z in range(n_z)] for x in range(n_x)]
    around = [
        [(y + core) * n_col + col for col in group for core in range(2)] for y in range(0, n_row, 2) for group in along_z
    ]
    ls = log_source_mass.reshape(-1, LANES)
    lt = log_target_mass.reshape(-1, LANES)
    src_dense, tgt_dense = f32(*ls.shape), f32(*lt.shape)
    half = n_tgt // 2

    n_parts = 2
    parts = call(half_kernel, (f32(half // n_parts, width),) * n_parts, target)
    gathered = [lax.all_gather(part, ("row", "col"), axis_index_groups=around, tiled=True) for part in parts]

    tile, lse, sqx, sqy = call(
        first_kernel, (f32(n_tgt, n_src), src_dense, src_dense, tgt_dense), target, source, lt
    )
    for step in range(ITERS):
        if step > 0:
            lse = call(targets_kernel, src_dense, tile, lt, sqy, *parts)
        for distance in bits_of(n_x):
            lse = merge_all([lse, swap(lse, "col", distance)])
        parts = [lse] + [swap(lse, "col", k * n_x) for k in range(1, n_z)]
        src_bias, lse = call(sources_kernel, (src_dense, tgt_dense), tile, ls, sqx, *parts)
        parts = [lse] + [swap(lse, "row", k) for k in range(1, n_row)]
    total = merge_all(parts)

    bias = lt * LOG2E + (sqy - total) - sqy
    biases = [bias] + [swap(bias, "col", k * n_x) for k in range(1, n_z)]

    sent, mine = call(
        means_kernel, (f32(half, width), f32(half, width)), tile, source, src_bias, total, biases[1]
    )
    mine = call(add_kernel, f32(half, width), mine, swap(sent, "row", 1))
    rest = bits_of(n_row)[1:]
    for distance in rest[:-1]:
        mine = call(add_kernel, f32(half, width), mine, swap(mine, "row", distance))
    came = swap(mine, "row", rest[-1])

    n_all = n_z * n_tgt
    all_y, inner = call(
        lambda *refs: scores_kernel(n_x, *refs),
        (bf16(n_all, width), f32(n_x * count, n_all)),
        source, *gathered,
    )
    scores = pltpu.VMEM((count, n_all), jnp.float32)
    lse_dense = f32(pl.cdiv(count, LANES), LANES)
    others = call(
        lambda *refs: others_kernel(n_x, n_z, *refs),
        (f32(count, width), lse_dense) * (n_x - 1),
        inner, all_y, *biases,
        scratch=[scores],
    )
    joined = [swap(part, "col", 1 + k // 2) for k, part in enumerate(others)]
    own, own_shares = call(
        lambda *refs: own_kernel(n_x, n_z, *refs),
        (f32(count, width), f32(n_x - 1, *lse_dense.shape)),
        inner, all_y, *biases, *joined[1::2],
        scratch=[scores],
    )
    mine = call(add_kernel, f32(half, width), mine, came, joined[0], own_shares)
    target_image = call(
        place_kernel, f32(n_tgt, width), mine, swap(mine, "row", 1), out_specs=HBM, scratch=[DMA((2,))]
    )
    source_image = call(join_kernel, f32(count, width), own, own_shares, *joined[::2])
    return source_image, target_image


def solution(mesh):
    in_specs = (P("row", None), P("col", None), P("row"), P("col"))
    out_specs = (P(("row", "col"), None), P("col", None))
    return jax.shard_map(
        on_device, mesh=mesh, in_specs=in_specs, out_specs=out_specs, check_vma=False
    )
```

time: 114 us -> 105 us (0.921)
  blocking collectives: 26.4 us -> 0 us
  Pallas kernels: 30.9 us -> 13.1 us
  waiting for transfers between devices: 30 us -> 44.1 us
  starting transfers between devices: 12.1 us -> 25.6 us
  local copies, waits for them, and re-layouts: 0.63 us -> 7.54 us
    all_to_all x2 -> x0, blocking collectives: 26.4 us -> none  [iteration(): parts = lax.all_to_all(copies, 'col', 0, 0)]
    pallas_call x14 -> x13, Pallas kernels: 30.9 us -> 13.1 us  [call(): pl.pallas_call(kernel, out_shape=out_shape, in_specs=in_specs or [VMEM] *...]
    ppermute x15 -> x22, starting transfers between devices: 12.1 us -> 25.5 us  [swap(): return lax.ppermute(value, axis, [(i, i ^ distance) for i in range(n)])]
    all_gather x1 -> x2, waiting for transfers between devices: 1.73 us -> 12.2 us  [on_device(): lax.all_gather(part, ('row', 'col'), axis_index_groups=around, tiled=True)]
    unnamed x12 -> x18, local copies, waits for them, and re-layouts: 0.62 us -> 7.54 us
    ppermute x15 -> x22, waiting for transfers between devices: 28.2 us -> 31.2 us  [swap(): return lax.ppermute(value, axis, [(i, i ^ distance) for i in range(n)])]
  transfers between devices with their start and end apart: 16 -> 24, of which waited for: 10 -> 13; matrix products, arithmetic and copies ran while one was open for 1% -> 0% of each run, Pallas kernels for 22% -> 11%
where the time goes in v2:
time: 105 us
  waiting for transfers between devices  44.1 us (42%)
  starting transfers between devices  25.6 us (24%)
  between operations  14.2 us (14%)
  Pallas kernels  13.1 us (12%)
  local copies, waits for them, and re-layouts  7.54 us (7%)
    ppermute x22, waiting for transfers between devices, swap(): return lax.ppermute(value, axis, [(i, i ^ distance) for i in range(n)])  31.2 us
    ppermute x22, starting transfers between devices, swap(): return lax.ppermute(value, axis, [(i, i ^ distance) for i in range(n)])  25.5 us
    pallas_call x13, Pallas kernels, call(): pl.pallas_call(kernel, out_shape=out_shape, in_specs=in_specs or [VMEM] *...  13.1 us
    all_gather x2, waiting for transfers between devices, on_device(): lax.all_gather(part, ('row', 'col'), axis_index_groups=around, tiled=True)  12.2 us
    unnamed x18, local copies, waits for them, and re-layouts  7.54 us
  transfers between devices with their start and end apart: 24, of which 13 were waited for; matrix products, arithmetic and copies ran while one was open for 0% of the time, Pallas kernels for 11%

profile of v2, /device:TPU:0, one launch (start us, length us, event | category | flops | bytes accessed | tf_op | source)
XLA Modules:
  0.0 104.6 jit_solution(16711819525807151782)
XLA Ops:
  7.2 0.0 all-gather.3.cloned.1.call-start
  7.2 0.0 copy-start.4
  7.2 1.0 copy-done.4
  8.3 0.8 shard_map.59
  9.1 0.0 all-gather.3.cloned.1.call-update
  9.1 0.0 all-gather.5.cloned.1.call-start
  9.1 0.7 all-gather.5.cloned.1.call-update
  9.8 0.0 copy-start
  9.9 1.6 %copy-done = bf16[2048,512]{1,0:T(8,128)(2,1)S(1)} copy-done((bf16[2048,512]{1,0:T(8,128)(2,1)S(1)}, bf16[2048,512]{1,0:T(8,128)(2,1)}, u32[]{:S(2)}) %copy-start) | copy-done | bytes 2097176
  11.4 1.0 copy-done.5
  12.5 0.7 copy-done.7
  13.2 2.3 %shard_map.61 = (f32[512,2048]{1,0:T(8,128)S(1)}, f32[16,128]{1,0:T(8,128)S(1)}, f32[16,128]{1,0:T(8,128)S(1)}, f32[4,128]{1,0:T(4,128)S(1)}) custom-call(bf16[512,512]{1,0:T(8,128)(2,1)S(1)} %copy-done.5, bf16[2048,512]{1,0:T(8,128)(2,1)S(1)} %copy-done, f32[4,128]{1,0:T(4,128)S(1)} %bitcast.5), custom_call_target="tpu_custom_call" | custom-call | tf_op jit(solution)/shard_map/pallas_call | solution.py:22
  15.5 3.0 %collective-permute-start = (f32[16,128]{1,0:T(8,128)S(1)}, f32[16,128]{1,0:T(8,128)S(1)}, u32[]{:S(2)}, u32[]{:S(2)}) collective-permute-start(f32[16,128]{1,0:T(8,128)S(1)} %get-tuple-element.26), channel_id=1, source_target_pairs={{0,1},{1,0},{2,3},{3,2},{4,5},{5,4},{6,7},{7,6},{8,9},{9,8},{10,11... | collective-permute-start | bytes 24584 | tf_op jit(solution)/shard_map/ppermute | solution.py:246
  18.5 1.6 %collective-permute-done = f32[16,128]{1,0:T(8,128)S(1)} collective-permute-done((f32[16,128]{1,0:T(8,128)S(1)}, f32[16,128]{1,0:T(8,128)S(1)}, u32[]{:S(2)}, u32[]{:S(2)}) %collective-permute-start) | collective-permute-done | bytes 8224 | tf_op jit(solution)/shard_map/ppermute | solution.py:246
  20.1 2.2 %collective-permute-start.1 = (f32[16,128]{1,0:T(8,128)S(1)}, f32[16,128]{1,0:T(8,128)S(1)}, u32[]{:S(2)}, u32[]{:S(2)}) collective-permute-start(f32[16,128]{1,0:T(8,128)S(1)} %multiply_add_fusion.1.refs_0_), channel_id=1, source_target_pairs={{0,2},{1,3},{2,0},{3,1},{4,6},{5,7},{6,4},{7,5},{8,10},{9,11},{10,... | collective-permute-start | bytes 24584 | tf_op jit(solution)/shard_map/ppermute | solution.py:246
  22.3 2.6 %collective-permute-start.2 = (f32[16,128]{1,0:T(8,128)S(1)}, f32[16,128]{1,0:T(8,128)S(1)}, u32[]{:S(2)}, u32[]{:S(2)}) collective-permute-start(f32[16,128]{1,0:T(8,128)S(1)} %multiply_add_fusion.1.refs_0_), channel_id=1, source_target_pairs={{0,4},{1,5},{2,6},{3,7},{4,0},{5,1},{6,2},{7,3},{8,12},{9,13},{10,... | collective-permute-start | bytes 24584 | tf_op jit(solution)/shard_map/ppermute | solution.py:246
  24.9 2.6 %collective-permute-done.2.refs_2_ = f32[16,128]{1,0:T(8,128)S(1)} collective-permute-done((f32[16,128]{1,0:T(8,128)S(1)}, f32[16,128]{1,0:T(8,128)S(1)}, u32[]{:S(2)}, u32[]{:S(2)}) %collective-permute-start.2) | collective-permute-done | bytes 8224 | tf_op jit(solution)/shard_map/ppermute | solution.py:246
  27.5 3.0 %collective-permute-done.3.refs_3_ = f32[16,128]{1,0:T(8,128)S(1)} collective-permute-done((f32[16,128]{1,0:T(8,128)S(1)}, f32[16,128]{1,0:T(8,128)S(1)}, u32[]{:S(2)}, u32[]{:S(2)}) %collective-permute-start.3) | collective-permute-done | bytes 8224 | tf_op jit(solution)/shard_map/ppermute | solution.py:246
  30.5 1.0 shard_map.62
  31.5 0.0 collective-permute-start.4
  31.5 1.6 %collective-permute-start.5 = (f32[4,128]{1,0:T(4,128)S(1)}, f32[4,128]{1,0:T(4,128)S(1)}, u32[]{:S(2)}, u32[]{:S(2)}) collective-permute-start(f32[4,128]{1,0:T(4,128)S(1)} %get-tuple-element.27.refs_0_), channel_id=1, source_target_pairs={{0,16},{8,24},{16,0},{24,8},{1,17},{9,25},{17,1},{25,9},{2,18},{10... | collective-permute-start | bytes 6152 | tf_op jit(solution)/shard_map/ppermute | solution.py:246
  33.1 0.3 collective-permute-start.6
  33.4 0.0 collective-permute-done.4.refs_1_
  33.4 1.8 %collective-permute-done.5.refs_2_ = f32[4,128]{1,0:T(4,128)S(1)} collective-permute-done((f32[4,128]{1,0:T(4,128)S(1)}, f32[4,128]{1,0:T(4,128)S(1)}, u32[]{:S(2)}, u32[]{:S(2)}) %collective-permute-start.5) | collective-permute-done | bytes 2080 | tf_op jit(solution)/shard_map/ppermute | solution.py:246
  35.2 0.9 collective-permute-done.6.refs_3_
  36.1 1.0 shard_map.63
  37.1 1.6 %collective-permute-start.7 = (f32[16,128]{1,0:T(8,128)S(1)}, f32[16,128]{1,0:T(8,128)S(1)}, u32[]{:S(2)}, u32[]{:S(2)}) collective-permute-start(f32[16,128]{1,0:T(8,128)S(1)} %shard_map.63), channel_id=1, source_target_pairs={{0,1},{1,0},{2,3},{3,2},{4,5},{5,4},{6,7},{7,6},{8,9},{9,8},{10,11... | collective-permute-start | bytes 24584 | tf_op jit(solution)/shard_map/ppermute | solution.py:246
  38.7 2.1 %collective-permute-done.7 = f32[16,128]{1,0:T(8,128)S(1)} collective-permute-done((f32[16,128]{1,0:T(8,128)S(1)}, f32[16,128]{1,0:T(8,128)S(1)}, u32[]{:S(2)}, u32[]{:S(2)}) %collective-permute-start.7) | collective-permute-done | bytes 8224 | tf_op jit(solution)/shard_map/ppermute | solution.py:246
  40.9 0.3 collective-permute-start.10
  41.2 0.0 collective-permute-start.8
  41.2 4.1 %collective-permute-start.9 = (f32[16,128]{1,0:T(8,128)S(1)}, f32[16,128]{1,0:T(8,128)S(1)}, u32[]{:S(2)}, u32[]{:S(2)}) collective-permute-start(f32[16,128]{1,0:T(8,128)S(1)} %multiply_add_fusion.refs_0_), channel_id=1, source_target_pairs={{0,4},{1,5},{2,6},{3,7},{4,0},{5,1},{6,2},{7,3},{8,12},{9,13},{10,... | collective-permute-start | bytes 24584 | tf_op jit(solution)/shard_map/ppermute | solution.py:246
  45.3 1.1 %collective-permute-done.10.refs_3_ = f32[16,128]{1,0:T(8,128)S(1)} collective-permute-done((f32[16,128]{1,0:T(8,128)S(1)}, f32[16,128]{1,0:T(8,128)S(1)}, u32[]{:S(2)}, u32[]{:S(2)}) %collective-permute-start.10) | collective-permute-done | bytes 8224 | tf_op jit(solution)/shard_map/ppermute | solution.py:246
  46.4 0.6 collective-permute-done.9.refs_2_
  47.0 1.0 shard_map.64
  48.0 0.0 collective-permute-start.11
  48.0 0.6 collective-permute-start.12
  48.7 1.2 %collective-permute-start.13 = (f32[4,128]{1,0:T(4,128)S(1)}, f32[4,128]{1,0:T(4,128)S(1)}, u32[]{:S(2)}, u32[]{:S(2)}) collective-permute-start(f32[4,128]{1,0:T(4,128)S(1)} %get-tuple-element.28), channel_id=1, source_target_pairs={{0,24},{8,16},{16,8},{24,0},{1,25},{9,17},{17,9},{25,1},{2,26},{10... | collective-permute-start | bytes 6152 | tf_op jit(solution)/shard_map/ppermute | solution.py:246
  49.9 0.0 collective-permute-done.11
  49.9 1.8 %collective-permute-done.12 = f32[4,128]{1,0:T(4,128)S(1)} collective-permute-done((f32[4,128]{1,0:T(4,128)S(1)}, f32[4,128]{1,0:T(4,128)S(1)}, u32[]{:S(2)}, u32[]{:S(2)}) %collective-permute-start.12) | collective-permute-done | bytes 2080 | tf_op jit(solution)/shard_map/ppermute | solution.py:246
  51.7 0.0 collective-permute-done.13
  51.7 0.9 collective-permute-start.14
  52.6 2.7 %collective-permute-done.14.refs_3_.after_ref = f32[4,128]{1,0:T(4,128)S(1)} collective-permute-done((f32[4,128]{1,0:T(4,128)S(1)}, f32[4,128]{1,0:T(4,128)S(1)}, u32[]{:S(2)}, u32[]{:S(2)}) %collective-permute-start.14) | collective-permute-done | bytes 2080 | tf_op jit(solution)/shard_map/ppermute | solution.py:246
  55.4 1.4 %shard_map.68 = (f32[256,512]{1,0:T(8,128)S(1)}, f32[256,512]{1,0:T(8,128)S(1)}) custom-call(f32[512,2048]{1,0:T(8,128)S(1)} %get-tuple-element.24.tile_ref, bf16[2048,512]{1,0:T(8,128)(2,1)S(1)} %copy-done, f32[16,128]{1,0:T(8,128)S(1)} %get-tuple-element.33.bias_ref, f32[4,128]{1,0:T(4,128)S(1)} %get-tuple-element.37.total_ref, ...), custom_call_target="tpu_custom_call" | custom-call | tf_op jit(solution)/shard_map/pallas_call | solution.py:22
  56.7 0.1 collective-permute-start.19
  56.8 3.0 %collective-permute-start.15 = (f32[4,128]{1,0:T(4,128)S(1)}, f32[4,128]{1,0:T(4,128)S(1)}, u32[]{:S(2)}, u32[]{:S(2)}) collective-permute-start(f32[4,128]{1,0:T(4,128)S(1)} %get-tuple-element.36.refs_2_), channel_id=1, source_target_pairs={{0,4},{1,5},{2,6},{3,7},{4,0},{5,1},{6,2},{7,3},{8,12},{9,13},{10,... | collective-permute-start | bytes 6152 | tf_op jit(solution)/shard_map/ppermute | solution.py:246
  59.8 0.3 collective-permute-start.16
  60.1 0.1 shard_map.69.one_ref
  60.2 1.4 %collective-permute-start.20 = (f32[256,512]{1,0:T(8,128)S(1)}, f32[256,512]{1,0:T(8,128)S(1)}, u32[]{:S(2)}, u32[]{:S(2)}) collective-permute-start(f32[256,512]{1,0:T(8,128)S(1)} %shard_map.69.one_ref), channel_id=1, source_target_pairs={{0,16},{8,24},{16,0},{24,8},{1,17},{9,25},{17,1},{25,9},{2,18},{10... | collective-permute-start | bytes 1572872 | tf_op jit(solution)/shard_map/ppermute | solution.py:246
  61.6 12.1 %all-gather.5.cloned.1.call-done.refs_2_ = f32[1024,512]{1,0:T(8,128)} async-done(((f32[128,512]{1,0:T(8,128)}), f32[1024,512]{1,0:T(8,128)}) %all-gather.5.cloned.1.call-update) | async-done | bytes 2097168 | tf_op jit(solution)/shard_map/all_gather | solution.py:271
  73.8 1.6 %copy-done.2 = f32[1024,512]{1,0:T(8,128)S(1)} copy-done((f32[1024,512]{1,0:T(8,128)S(1)}, f32[1024,512]{1,0:T(8,128)}, u32[]{:S(2)}) %copy-start.2) | copy-done | bytes 2097176
  75.4 1.6 %copy-done.3 = f32[1024,512]{1,0:T(8,128)S(1)} copy-done((f32[1024,512]{1,0:T(8,128)S(1)}, f32[1024,512]{1,0:T(8,128)}, u32[]{:S(2)}) %copy-start.3) | copy-done | bytes 2097176
  77.0 1.3 %shard_map.60 = (bf16[2048,512]{1,0:T(8,128)(2,1)S(1)}, f32[512,2048]{1,0:T(8,128)S(1)}) custom-call(bf16[2048,512]{1,0:T(8,128)(2,1)S(1)} %copy-done.1, f32[1024,512]{1,0:T(8,128)S(1)} %copy-done.2, f32[1024,512]{1,0:T(8,128)S(1)} %copy-done.3), custom_call_target="tpu_custom_call" | custom-call | tf_op jit(solution)/shard_map/pallas_call | solution.py:22
  78.3 0.0 collective-permute-done.15.refs_4_
  78.3 1.0 shard_map.65
  79.3 1.5 %collective-permute-start.18 = (f32[256,512]{1,0:T(8,128)S(1)}, f32[256,512]{1,0:T(8,128)S(1)}, u32[]{:S(2)}, u32[]{:S(2)}) collective-permute-start(f32[256,512]{1,0:T(8,128)S(1)} %get-tuple-element.32), channel_id=1, source_target_pairs={{0,1},{1,0},{2,3},{3,2},{4,5},{5,4},{6,7},{7,6},{8,9},{9,8},{10,11... | collective-permute-start | bytes 1572872 | tf_op jit(solution)/shard_map/ppermute | solution.py:246
  80.9 0.6 collective-permute-start.17
  81.4 12.1 %collective-permute-done.17.refs_6_ = f32[2,128]{1,0:T(2,128)S(1)} collective-permute-done((f32[2,128]{1,0:T(2,128)S(1)}, f32[2,128]{1,0:T(2,128)S(1)}, u32[]{:S(2)}, u32[]{:S(2)}) %collective-permute-start.17) | collective-permute-done | bytes 1056 | tf_op jit(solution)/shard_map/ppermute | solution.py:246
  93.5 1.1 %shard_map.66 = (f32[256,512]{1,0:T(8,128)S(1)}, f32[1,2,128]{2,1,0:T(2,128)S(1)}) custom-call(f32[512,2048]{1,0:T(8,128)S(1)} %get-tuple-element.21.refs_0_, bf16[2048,512]{1,0:T(8,128)(2,1)S(1)} %get-tuple-element.22.refs_1_, f32[4,128]{1,0:T(4,128)S(1)} %get-tuple-element.36.refs_2_, f32[4,128]{1,0:T(4,128)S(1)} %collective-permute-done.14.refs_3_.after_ref, ...), custom_call_target="tpu_custom_call" | custom-call | tf_op jit(solution)/shard_map/pallas_call | solution.py:22
  94.7 0.0 collective-permute-done.20.two_ref
  94.7 0.1 shard_map.70.mine_ref
  94.7 0.1 collective-permute-start.21
  94.8 1.0 shard_map.67
  95.9 0.9 collective-permute-done.21.other_ref
  96.7 1.0 shard_map.71
  (20 shorter events, 0.1 us)
Async XLA Ops:
  7.2 54.5 %all-gather.3.cloned.1.call-start = ((), (), s32[]{:S(2)}) async-start(), calls=%async_computation | async-start | bytes 2359296 | tf_op jit(solution)/shard_map/all_gather | solution.py:271
  7.2 1.0 copy-start.4
  8.3 22.2 %copy-start.6 = (f32[2048]{0:T(1024)S(1)}, f32[2048]{0:T(1024)}, u32[]{:S(2)}) copy-start(f32[2048]{0:T(1024)} %param.6) | copy-start | bytes 24580
  9.1 64.7 %all-gather.5.cloned.1.call-start = ((), (), s32[]{:S(2)}) async-start(), calls=%async_computation.1 | async-start | bytes 2359296 | tf_op jit(solution)/shard_map/all_gather | solution.py:271
  9.8 1.6 %copy-start = (bf16[2048,512]{1,0:T(8,128)(2,1)S(1)}, bf16[2048,512]{1,0:T(8,128)(2,1)}, u32[]{:S(2)}) copy-start(bf16[2048,512]{1,0:T(8,128)(2,1)} %x_ref.3) | copy-start | bytes 6291460
  11.4 1.0 copy-start.5
  12.5 0.7 copy-start.7
  15.5 4.6 %collective-permute-start = (f32[16,128]{1,0:T(8,128)S(1)}, f32[16,128]{1,0:T(8,128)S(1)}, u32[]{:S(2)}, u32[]{:S(2)}) collective-permute-start(f32[16,128]{1,0:T(8,128)S(1)} %get-tuple-element.26), channel_id=1, source_target_pairs={{0,1},{1,0},{2,3},{3,2},{4,5},{5,4},{6,7},{7,6},{8,9},{9,8},{10,11... | collective-permute-start | bytes 24584 | tf_op jit(solution)/shard_map/ppermute | solution.py:246
  20.1 4.8 %collective-permute-start.1 = (f32[16,128]{1,0:T(8,128)S(1)}, f32[16,128]{1,0:T(8,128)S(1)}, u32[]{:S(2)}, u32[]{:S(2)}) collective-permute-start(f32[16,128]{1,0:T(8,128)S(1)} %multiply_add_fusion.1.refs_0_), channel_id=1, source_target_pairs={{0,2},{1,3},{2,0},{3,1},{4,6},{5,7},{6,4},{7,5},{8,10},{9,11},{10,... | collective-permute-start | bytes 24584 | tf_op jit(solution)/shard_map/ppermute | solution.py:246
  22.3 5.2 %collective-permute-start.2 = (f32[16,128]{1,0:T(8,128)S(1)}, f32[16,128]{1,0:T(8,128)S(1)}, u32[]{:S(2)}, u32[]{:S(2)}) collective-permute-start(f32[16,128]{1,0:T(8,128)S(1)} %multiply_add_fusion.1.refs_0_), channel_id=1, source_target_pairs={{0,4},{1,5},{2,6},{3,7},{4,0},{5,1},{6,2},{7,3},{8,12},{9,13},{10,... | collective-permute-start | bytes 24584 | tf_op jit(solution)/shard_map/ppermute | solution.py:246
  24.9 5.6 %collective-permute-start.3 = (f32[16,128]{1,0:T(8,128)S(1)}, f32[16,128]{1,0:T(8,128)S(1)}, u32[]{:S(2)}, u32[]{:S(2)}) collective-permute-start(f32[16,128]{1,0:T(8,128)S(1)} %multiply_add_fusion.1.refs_0_), channel_id=1, source_target_pairs={{0,6},{1,7},{2,4},{3,5},{4,2},{5,3},{6,0},{7,1},{8,14},{9,15},{10,... | collective-permute-start | bytes 24584 | tf_op jit(solution)/shard_map/ppermute | solution.py:246
  30.5 5.7 %copy-start.8 = (f32[512]{0:T(512)S(1)}, f32[512]{0:T(512)}, u32[]{:S(2)}) copy-start(f32[512]{0:T(512)} %param.7) | copy-start | bytes 6148
  31.5 1.9 %collective-permute-start.4 = (f32[4,128]{1,0:T(4,128)S(1)}, f32[4,128]{1,0:T(4,128)S(1)}, u32[]{:S(2)}, u32[]{:S(2)}) collective-permute-start(f32[4,128]{1,0:T(4,128)S(1)} %get-tuple-element.27.refs_0_), channel_id=1, source_target_pairs={{0,8},{8,0},{16,24},{24,16},{1,9},{9,1},{17,25},{25,17},{2,10},{10... | collective-permute-start | bytes 6152 | tf_op jit(solution)/shard_map/ppermute | solution.py:246
  31.5 3.7 %collective-permute-start.5 = (f32[4,128]{1,0:T(4,128)S(1)}, f32[4,128]{1,0:T(4,128)S(1)}, u32[]{:S(2)}, u32[]{:S(2)}) collective-permute-start(f32[4,128]{1,0:T(4,128)S(1)} %get-tuple-element.27.refs_0_), channel_id=1, source_target_pairs={{0,16},{8,24},{16,0},{24,8},{1,17},{9,25},{17,1},{25,9},{2,18},{10... | collective-permute-start | bytes 6152 | tf_op jit(solution)/shard_map/ppermute | solution.py:246
  33.1 3.0 %collective-permute-start.6 = (f32[4,128]{1,0:T(4,128)S(1)}, f32[4,128]{1,0:T(4,128)S(1)}, u32[]{:S(2)}, u32[]{:S(2)}) collective-permute-start(f32[4,128]{1,0:T(4,128)S(1)} %get-tuple-element.27.refs_0_), channel_id=1, source_target_pairs={{0,24},{8,16},{16,8},{24,0},{1,25},{9,17},{17,9},{25,1},{2,26},{10... | collective-permute-start | bytes 6152 | tf_op jit(solution)/shard_map/ppermute | solution.py:246
  37.1 3.7 %collective-permute-start.7 = (f32[16,128]{1,0:T(8,128)S(1)}, f32[16,128]{1,0:T(8,128)S(1)}, u32[]{:S(2)}, u32[]{:S(2)}) collective-permute-start(f32[16,128]{1,0:T(8,128)S(1)} %shard_map.63), channel_id=1, source_target_pairs={{0,1},{1,0},{2,3},{3,2},{4,5},{5,4},{6,7},{7,6},{8,9},{9,8},{10,11... | collective-permute-start | bytes 24584 | tf_op jit(solution)/shard_map/ppermute | solution.py:246
  40.9 5.5 %collective-permute-start.10 = (f32[16,128]{1,0:T(8,128)S(1)}, f32[16,128]{1,0:T(8,128)S(1)}, u32[]{:S(2)}, u32[]{:S(2)}) collective-permute-start(f32[16,128]{1,0:T(8,128)S(1)} %multiply_add_fusion.refs_0_), channel_id=1, source_target_pairs={{0,6},{1,7},{2,4},{3,5},{4,2},{5,3},{6,0},{7,1},{8,14},{9,15},{10,... | collective-permute-start | bytes 24584 | tf_op jit(solution)/shard_map/ppermute | solution.py:246
  41.2 5.2 %collective-permute-start.8 = (f32[16,128]{1,0:T(8,128)S(1)}, f32[16,128]{1,0:T(8,128)S(1)}, u32[]{:S(2)}, u32[]{:S(2)}) collective-permute-start(f32[16,128]{1,0:T(8,128)S(1)} %multiply_add_fusion.refs_0_), channel_id=1, source_target_pairs={{0,2},{1,3},{2,0},{3,1},{4,6},{5,7},{6,4},{7,5},{8,10},{9,11},{10,... | collective-permute-start | bytes 24584 | tf_op jit(solution)/shard_map/ppermute | solution.py:246
  41.2 5.8 %collective-permute-start.9 = (f32[16,128]{1,0:T(8,128)S(1)}, f32[16,128]{1,0:T(8,128)S(1)}, u32[]{:S(2)}, u32[]{:S(2)}) collective-permute-start(f32[16,128]{1,0:T(8,128)S(1)} %multiply_add_fusion.refs_0_), channel_id=1, source_target_pairs={{0,4},{1,5},{2,6},{3,7},{4,0},{5,1},{6,2},{7,3},{8,12},{9,13},{10,... | collective-permute-start | bytes 24584 | tf_op jit(solution)/shard_map/ppermute | solution.py:246
  48.0 1.9 %collective-permute-start.11 = (f32[4,128]{1,0:T(4,128)S(1)}, f32[4,128]{1,0:T(4,128)S(1)}, u32[]{:S(2)}, u32[]{:S(2)}) collective-permute-start(f32[4,128]{1,0:T(4,128)S(1)} %get-tuple-element.28), channel_id=1, source_target_pairs={{0,8},{8,0},{16,24},{24,16},{1,9},{9,1},{17,25},{25,17},{2,10},{10... | collective-permute-start | bytes 6152 | tf_op jit(solution)/shard_map/ppermute | solution.py:246
  48.0 3.7 %collective-permute-start.12 = (f32[4,128]{1,0:T(4,128)S(1)}, f32[4,128]{1,0:T(4,128)S(1)}, u32[]{:S(2)}, u32[]{:S(2)}) collective-permute-start(f32[4,128]{1,0:T(4,128)S(1)} %get-tuple-element.28), channel_id=1, source_target_pairs={{0,16},{8,24},{16,0},{24,8},{1,17},{9,25},{17,1},{25,9},{2,18},{10... | collective-permute-start | bytes 6152 | tf_op jit(solution)/shard_map/ppermute | solution.py:246
  48.7 3.0 %collective-permute-start.13 = (f32[4,128]{1,0:T(4,128)S(1)}, f32[4,128]{1,0:T(4,128)S(1)}, u32[]{:S(2)}, u32[]{:S(2)}) collective-permute-start(f32[4,128]{1,0:T(4,128)S(1)} %get-tuple-element.28), channel_id=1, source_target_pairs={{0,24},{8,16},{16,8},{24,0},{1,25},{9,17},{17,9},{25,1},{2,26},{10... | collective-permute-start | bytes 6152 | tf_op jit(solution)/shard_map/ppermute | solution.py:246
  51.7 3.7 %collective-permute-start.14 = (f32[4,128]{1,0:T(4,128)S(1)}, f32[4,128]{1,0:T(4,128)S(1)}, u32[]{:S(2)}, u32[]{:S(2)}) collective-permute-start(f32[4,128]{1,0:T(4,128)S(1)} %get-tuple-element.36.refs_2_), channel_id=1, source_target_pairs={{0,2},{1,3},{2,0},{3,1},{4,6},{5,7},{6,4},{7,5},{8,10},{9,11},{10,... | collective-permute-start | bytes 6152 | tf_op jit(solution)/shard_map/ppermute | solution.py:246
  55.4 18.4 %copy-start.1 = (bf16[2048,512]{1,0:T(8,128)(2,1)S(1)}, bf16[2048,512]{1,0:T(8,128)(2,1)}, u32[]{:S(2)}) copy-start(bf16[2048,512]{1,0:T(8,128)(2,1)} %x_ref.3) | copy-start | bytes 6291460
  56.7 3.4 %collective-permute-start.19 = (f32[256,512]{1,0:T(8,128)S(1)}, f32[256,512]{1,0:T(8,128)S(1)}, u32[]{:S(2)}, u32[]{:S(2)}) collective-permute-start(f32[256,512]{1,0:T(8,128)S(1)} %get-tuple-element.35), channel_id=1, source_target_pairs={{0,8},{8,0},{16,24},{24,16},{1,9},{9,1},{17,25},{25,17},{2,10},{10... | collective-permute-start | bytes 1572872 | tf_op jit(solution)/shard_map/ppermute | solution.py:246
  56.8 21.5 %collective-permute-start.15 = (f32[4,128]{1,0:T(4,128)S(1)}, f32[4,128]{1,0:T(4,128)S(1)}, u32[]{:S(2)}, u32[]{:S(2)}) collective-permute-start(f32[4,128]{1,0:T(4,128)S(1)} %get-tuple-element.36.refs_2_), channel_id=1, source_target_pairs={{0,4},{1,5},{2,6},{3,7},{4,0},{5,1},{6,2},{7,3},{8,12},{9,13},{10,... | collective-permute-start | bytes 6152 | tf_op jit(solution)/shard_map/ppermute | solution.py:246
  59.8 18.5 %collective-permute-start.16 = (f32[4,128]{1,0:T(4,128)S(1)}, f32[4,128]{1,0:T(4,128)S(1)}, u32[]{:S(2)}, u32[]{:S(2)}) collective-permute-start(f32[4,128]{1,0:T(4,128)S(1)} %get-tuple-element.36.refs_2_), channel_id=1, source_target_pairs={{0,6},{1,7},{2,4},{3,5},{4,2},{5,3},{6,0},{7,1},{8,14},{9,15},{10,... | collective-permute-start | bytes 6152 | tf_op jit(solution)/shard_map/ppermute | solution.py:246
  60.2 34.5 %collective-permute-start.20 = (f32[256,512]{1,0:T(8,128)S(1)}, f32[256,512]{1,0:T(8,128)S(1)}, u32[]{:S(2)}, u32[]{:S(2)}) collective-permute-start(f32[256,512]{1,0:T(8,128)S(1)} %shard_map.69.one_ref), channel_id=1, source_target_pairs={{0,16},{8,24},{16,0},{24,8},{1,17},{9,25},{17,1},{25,9},{2,18},{10... | collective-permute-start | bytes 1572872 | tf_op jit(solution)/shard_map/ppermute | solution.py:246
  73.8 1.6 %copy-start.2 = (f32[1024,512]{1,0:T(8,128)S(1)}, f32[1024,512]{1,0:T(8,128)}, u32[]{:S(2)}) copy-start(f32[1024,512]{1,0:T(8,128)} %all-gather.3.cloned.1.call-done.refs_1_) | copy-start | bytes 6291460
  75.4 1.6 %copy-start.3 = (f32[1024,512]{1,0:T(8,128)S(1)}, f32[1024,512]{1,0:T(8,128)}, u32[]{:S(2)}) copy-start(f32[1024,512]{1,0:T(8,128)} %all-gather.5.cloned.1.call-done.refs_2_) | copy-start | bytes 6291460
  79.3 15.3 %collective-permute-start.18 = (f32[256,512]{1,0:T(8,128)S(1)}, f32[256,512]{1,0:T(8,128)S(1)}, u32[]{:S(2)}, u32[]{:S(2)}) collective-permute-start(f32[256,512]{1,0:T(8,128)S(1)} %get-tuple-element.32), channel_id=1, source_target_pairs={{0,1},{1,0},{2,3},{3,2},{4,5},{5,4},{6,7},{7,6},{8,9},{9,8},{10,11... | collective-permute-start | bytes 1572872 | tf_op jit(solution)/shard_map/ppermute | solution.py:246
  80.9 12.7 %collective-permute-start.17 = (f32[2,128]{1,0:T(2,128)S(1)}, f32[2,128]{1,0:T(2,128)S(1)}, u32[]{:S(2)}, u32[]{:S(2)}) collective-permute-start(f32[2,128]{1,0:T(2,128)S(1)} %get-tuple-element.29), channel_id=1, source_target_pairs={{0,1},{1,0},{2,3},{3,2},{4,5},{5,4},{6,7},{7,6},{8,9},{9,8},{10,11... | collective-permute-start | bytes 3080 | tf_op jit(solution)/shard_map/ppermute | solution.py:246
  94.7 2.0 %collective-permute-start.21 = (f32[256,512]{1,0:T(8,128)S(1)}, f32[256,512]{1,0:T(8,128)S(1)}, u32[]{:S(2)}, u32[]{:S(2)}) collective-permute-start(f32[256,512]{1,0:T(8,128)S(1)} %shard_map.70.mine_ref), channel_id=1, source_target_pairs={{0,8},{8,0},{16,24},{24,16},{1,9},{9,1},{17,25},{25,17},{2,10},{10... | collective-permute-start | bytes 1572872 | tf_op jit(solution)/shard_map/ppermute | solution.py:246
Sparse Core Ops, SparseCore 0:
  10.2 32.9 all-gather.2
  45.3 28.4 all-gather.4

commit v3 on v2

--- a/solution.py
+++ b/solution.py
@@ -159,10 +159,13 @@
     refs[-1][...] = one_ref[...] + two_ref[...]
 
 
-def join_kernel(own_ref, shares_ref, *refs):
-    out_ref = refs[-1]
+def join_kernel(*refs):
+    parts, out_ref = refs[:-1], refs[-1]
     rows = out_ref.shape[0]
-    out_ref[...] = own_ref[...] + sum(ref[...] * to_column(shares_ref[k])[:rows] for k, ref in enumerate(refs[:-1]))
+    lses = [ref[rows : rows + pl.cdiv(rows, LANES), :LANES] for ref in parts]
+    whole = merge_all(lses)
+    shares = [to_column(jnp.exp2(lse - whole))[:rows] for lse in lses]
+    out_ref[...] = sum(ref[:rows, :] * share for ref, share in zip(parts, shares))
 
 
 def place_kernel(mine_ref, other_ref, out_hbm, sems):
@@ -176,17 +179,15 @@
     other.wait()
 
 
-def scores_kernel(n_x, x_ref, *refs):
-    parts, (y_ref, inner_ref) = refs[:-2], refs[-2:]
+def scores_kernel(n_x, x_ref, all_ref, y_ref, inner_ref):
     rows = inner_ref.shape[0]
     start = lax.axis_index("col") // n_x * rows
     own = x_ref[pl.ds(pl.multiple_of(start, rows), rows), :]
     unit = scale(own.shape[1])
-    piece = 128
-    wide = piece * len(parts)
+    wide = 512
     for b in range(y_ref.shape[0] // wide):
         at = pl.ds(b * wide, wide)
-        y = jnp.concatenate([ref[pl.ds(b * piece, piece), :] for ref in parts], axis=0).astype(jnp.bfloat16)
+        y = all_ref[at, :].astype(jnp.bfloat16)
         y_ref[at, :] = y
         inner_ref[:, at] = lax.dot_general(own, y, NT_DIMS, preferred_element_type=jnp.float32) * (2.0 * unit)
 
@@ -195,12 +196,11 @@
     rows = scores_ref.shape[0]
     n_shards = len(bias_refs)
     n_tgt = y_ref.shape[0] // n_shards
-    start = ((lax.axis_index("col") ^ flip) % n_x) * rows
-    block = pl.ds(pl.multiple_of(start, rows), rows)
+    col = lax.axis_index("col")
+    block = pl.ds(pl.multiple_of((col ^ flip) % n_x * rows, rows), rows)
     peak = jnp.full((rows, 1), -jnp.inf, jnp.float32)
-    z = lax.axis_index("col") // n_x
     for k in range(n_shards):
-        at = pl.ds(pl.multiple_of((z ^ k) * n_tgt, n_tgt), n_tgt)
+        at = pl.ds(pl.multiple_of((col // n_x ^ k) * n_tgt, n_tgt), n_tgt)
         scores = inner_ref[block, at] + to_row(bias_refs[k][...])
         scores_ref[:, at] = scores
         peak = jnp.maximum(peak, jnp.max(scores, axis=1, keepdims=True))
@@ -221,24 +221,28 @@
     return to_dense([column[b : b + LANES] for b in range(0, column.shape[0], LANES)])
 
 
-def others_kernel(n_x, n_z, inner_ref, y_ref, *refs):
-    bias_refs, refs = refs[:n_z], refs[n_z:]
-    for flip in range(1, n_x):
-        numer, total, peak = images(flip, n_x, inner_ref, y_ref, bias_refs, refs[-1])
-        refs[2 * flip - 2][...] = numer * (1.0 / total)
-        refs[2 * flip - 1][...] = lanes_of(peak + jnp.log2(total))
-
-
-def own_kernel(n_x, n_z, inner_ref, y_ref, *refs):
-    bias_refs, lses, (out_ref, shares_ref, scores_ref) = refs[:n_z], refs[n_z:-3], refs[-3:]
+EXTRA = 8
+
+
+def others_kernel(n_x, inner_ref, y_ref, *refs):
+    bias_refs, image_refs, scores_ref = refs[: -n_x], refs[-n_x:-1], refs[-1]
+    for flip, image_ref in enumerate(image_refs, 1):
+        numer, total, peak = images(flip, n_x, inner_ref, y_ref, bias_refs, scores_ref)
+        rows = numer.shape[0]
+        lse = lanes_of(peak + jnp.log2(total))
+        image_ref[:rows, :] = numer * (1.0 / total)
+        image_ref[rows:, :] = jnp.zeros((EXTRA, image_ref.shape[1]), jnp.float32)
+        image_ref[rows : rows + lse.shape[0], :LANES] = lse
+
+
+def own_kernel(n_x, inner_ref, y_ref, *refs):
+    bias_refs, (image_ref, scores_ref) = refs[:-2], refs[-2:]
     numer, total, peak = images(0, n_x, inner_ref, y_ref, bias_refs, scores_ref)
     rows = numer.shape[0]
     lse = lanes_of(peak + jnp.log2(total))
-    came = [ref[...] for ref in lses]
-    whole = merge_all([lse] + came)
-    out_ref[...] = numer * (to_column(jnp.exp2(lse - whole))[:rows] / total)
-    for k, part in enumerate(came):
-        shares_ref[k] = jnp.exp2(part - whole)
+    image_ref[:rows, :] = numer * (1.0 / total)
+    image_ref[rows:, :] = jnp.zeros((EXTRA, image_ref.shape[1]), jnp.float32)
+    image_ref[rows : rows + lse.shape[0], :LANES] = lse
 
 
 def swap(value, axis, distance):
@@ -257,16 +261,17 @@
     count = n_src // n_col
     n_x = 1 << (len(bits_of(n_col)) // 2)
     n_z = n_col // n_x
-    along_z = [[z * n_x + x for z in range(n_z)] for x in range(n_x)]
     around = [
-        [(y + core) * n_col + col for col in group for core in range(2)] for y in range(0, n_row, 2) for group in along_z
+        [(y + core) * n_col + z * n_x + x for z in range(n_z) for core in range(2)]
+        for y in range(0, n_row, 2)
+        for x in range(n_x)
     ]
     ls = log_source_mass.reshape(-1, LANES)
     lt = log_target_mass.reshape(-1, LANES)
     src_dense, tgt_dense = f32(*ls.shape), f32(*lt.shape)
     half = n_tgt // 2
 
-    n_parts = 2
+    n_parts = 1
     parts = call(half_kernel, (f32(half // n_parts, width),) * n_parts, target)
     gathered = [lax.all_gather(part, ("row", "col"), axis_index_groups=around, tiled=True) for part in parts]
 
@@ -300,27 +305,20 @@
         lambda *refs: scores_kernel(n_x, *refs),
         (bf16(n_all, width), f32(n_x * count, n_all)),
         source, *gathered,
+        limit=44,
     )
     scores = pltpu.VMEM((count, n_all), jnp.float32)
-    lse_dense = f32(pl.cdiv(count, LANES), LANES)
+    image = f32(count + EXTRA, width)
     others = call(
-        lambda *refs: others_kernel(n_x, n_z, *refs),
-        (f32(count, width), lse_dense) * (n_x - 1),
-        inner, all_y, *biases,
-        scratch=[scores],
-    )
-    joined = [swap(part, "col", 1 + k // 2) for k, part in enumerate(others)]
-    own, own_shares = call(
-        lambda *refs: own_kernel(n_x, n_z, *refs),
-        (f32(count, width), f32(n_x - 1, *lse_dense.shape)),
-        inner, all_y, *biases, *joined[1::2],
-        scratch=[scores],
-    )
-    mine = call(add_kernel, f32(half, width), mine, came, joined[0], own_shares)
+        lambda *refs: others_kernel(n_x, *refs), (image,) * (n_x - 1), inner, all_y, *biases, scratch=[scores]
+    )
+    joined = [swap(part, "col", flip) for flip, part in enumerate(others, 1)]
+    own = call(lambda *refs: own_kernel(n_x, *refs), image, inner, all_y, *biases, scratch=[scores])
+    mine = call(add_kernel, f32(half, width), mine, came, joined[0], own)
     target_image = call(
         place_kernel, f32(n_tgt, width), mine, swap(mine, "row", 1), out_specs=HBM, scratch=[DMA((2,))]
     )
-    source_image = call(join_kernel, f32(count, width), own, own_shares, *joined[::2])
+    source_image = call(join_kernel, f32(count, width), own, *joined)
     return source_image, target_image
 
 

time: 105 us -> 91.5 us (0.87)
  waiting for transfers between devices: 44.1 us -> 33.3 us
  local copies, waits for them, and re-layouts: 7.54 us -> 4.36 us
  Pallas kernels: 13.1 us -> 15.9 us
  starting transfers between devices: 25.6 us -> 23.3 us
    all_gather x2 -> x1, waiting for transfers between devices: 12.2 us -> 0.9 us  [on_device(): lax.all_gather(part, ('row', 'col'), axis_index_groups=around, tiled=True)]
    unnamed x18 -> x14, local copies, waits for them, and re-layouts: 7.54 us -> 4.36 us
    pallas_call x13, Pallas kernels: 13.1 us -> 15.9 us  [call(): pl.pallas_call(kernel, out_shape=out_shape, in_specs=in_specs or [VMEM] *...]
    ppermute x22 -> x21, starting transfers between devices: 25.5 us -> 23.3 us  [swap(): return lax.ppermute(value, axis, [(i, i ^ distance) for i in range(n)])]
    ppermute x22 -> x21, waiting for transfers between devices: 31.2 us -> 32.4 us  [swap(): return lax.ppermute(value, axis, [(i, i ^ distance) for i in range(n)])]
  transfers between devices with their start and end apart: 24 -> 22, of which waited for: 13 -> 14; matrix products, arithmetic and copies ran while one was open for 0% -> 0% of each run, Pallas kernels for 11% -> 15%
where the time goes in v3:
time: 91.5 us; the launch traced here: 91.2 us
  waiting for transfers between devices  33.3 us (36%)
  starting transfers between devices  23.3 us (25%)
  Pallas kernels  15.9 us (17%)
  between operations  14.2 us (16%)
  local copies, waits for them, and re-layouts  4.36 us (5%)
    ppermute x21, waiting for transfers between devices, swap(): return lax.ppermute(value, axis, [(i, i ^ distance) for i in range(n)])  32.4 us
    ppermute x21, starting transfers between devices, swap(): return lax.ppermute(value, axis, [(i, i ^ distance) for i in range(n)])  23.3 us
    pallas_call x13, Pallas kernels, call(): pl.pallas_call(kernel, out_shape=out_shape, in_specs=in_specs or [VMEM] *...  15.9 us
    unnamed x14, local copies, waits for them, and re-layouts  4.36 us
  transfers between devices with their start and end apart: 22, of which 14 were waited for; matrix products, arithmetic and copies ran while one was open for 0% of the time, Pallas kernels for 15%

profile of v3, /device:TPU:0, one launch (start us, length us, event | category | flops | bytes accessed | tf_op | source)
XLA Modules:
  0.0 91.2 jit_solution(11404653637865578068)
XLA Ops:
  7.2 0.0 all-gather.2.cloned.1.call-start
  7.2 0.0 copy-start.2
  7.2 1.0 %copy-done.2 = bf16[512,512]{1,0:T(8,128)(2,1)S(1)} copy-done((bf16[512,512]{1,0:T(8,128)(2,1)S(1)}, bf16[512,512]{1,0:T(8,128)(2,1)}, u32[]{:S(2)}) %copy-start.2) | copy-done | bytes 524312
  8.3 0.8 shard_map.59
  9.1 0.0 all-gather.2.cloned.1.call-update
  9.1 0.0 copy-start
  9.1 1.6 %copy-done = bf16[2048,512]{1,0:T(8,128)(2,1)S(1)} copy-done((bf16[2048,512]{1,0:T(8,128)(2,1)S(1)}, bf16[2048,512]{1,0:T(8,128)(2,1)}, u32[]{:S(2)}) %copy-start) | copy-done | bytes 2097176
  10.7 1.0 %copy-done.3 = bf16[512,512]{1,0:T(8,128)(2,1)S(1)} copy-done((bf16[512,512]{1,0:T(8,128)(2,1)S(1)}, bf16[512,512]{1,0:T(8,128)(2,1)}, u32[]{:S(2)}) %copy-start.3) | copy-done | bytes 524312
  11.8 0.7 copy-done.5
  12.4 2.3 %shard_map.61 = (f32[512,2048]{1,0:T(8,128)S(1)}, f32[16,128]{1,0:T(8,128)S(1)}, f32[16,128]{1,0:T(8,128)S(1)}, f32[4,128]{1,0:T(4,128)S(1)}) custom-call(bf16[512,512]{1,0:T(8,128)(2,1)S(1)} %copy-done.3, bf16[2048,512]{1,0:T(8,128)(2,1)S(1)} %copy-done, f32[4,128]{1,0:T(4,128)S(1)} %bitcast.5), custom_call_target="tpu_custom_call" | custom-call | tf_op jit(solution)/shard_map/pallas_call | solution.py:22
  14.7 3.0 %collective-permute-start = (f32[16,128]{1,0:T(8,128)S(1)}, f32[16,128]{1,0:T(8,128)S(1)}, u32[]{:S(2)}, u32[]{:S(2)}) collective-permute-start(f32[16,128]{1,0:T(8,128)S(1)} %get-tuple-element.18), channel_id=1, source_target_pairs={{0,1},{1,0},{2,3},{3,2},{4,5},{5,4},{6,7},{7,6},{8,9},{9,8},{10,11... | collective-permute-start | bytes 24584 | tf_op jit(solution)/shard_map/ppermute | solution.py:250
  17.7 1.6 %collective-permute-done = f32[16,128]{1,0:T(8,128)S(1)} collective-permute-done((f32[16,128]{1,0:T(8,128)S(1)}, f32[16,128]{1,0:T(8,128)S(1)}, u32[]{:S(2)}, u32[]{:S(2)}) %collective-permute-start) | collective-permute-done | bytes 8224 | tf_op jit(solution)/shard_map/ppermute | solution.py:250
  19.4 2.2 %collective-permute-start.1 = (f32[16,128]{1,0:T(8,128)S(1)}, f32[16,128]{1,0:T(8,128)S(1)}, u32[]{:S(2)}, u32[]{:S(2)}) collective-permute-start(f32[16,128]{1,0:T(8,128)S(1)} %multiply_add_fusion.1.refs_0_), channel_id=1, source_target_pairs={{0,2},{1,3},{2,0},{3,1},{4,6},{5,7},{6,4},{7,5},{8,10},{9,11},{10,... | collective-permute-start | bytes 24584 | tf_op jit(solution)/shard_map/ppermute | solution.py:250
  21.5 2.6 %collective-permute-start.2 = (f32[16,128]{1,0:T(8,128)S(1)}, f32[16,128]{1,0:T(8,128)S(1)}, u32[]{:S(2)}, u32[]{:S(2)}) collective-permute-start(f32[16,128]{1,0:T(8,128)S(1)} %multiply_add_fusion.1.refs_0_), channel_id=1, source_target_pairs={{0,4},{1,5},{2,6},{3,7},{4,0},{5,1},{6,2},{7,3},{8,12},{9,13},{10,... | collective-permute-start | bytes 24584 | tf_op jit(solution)/shard_map/ppermute | solution.py:250
  24.1 0.0 collective-permute-start.3
  24.1 0.0 collective-permute-done.1.refs_1_
  24.1 2.7 %collective-permute-done.2.refs_2_ = f32[16,128]{1,0:T(8,128)S(1)} collective-permute-done((f32[16,128]{1,0:T(8,128)S(1)}, f32[16,128]{1,0:T(8,128)S(1)}, u32[]{:S(2)}, u32[]{:S(2)}) %collective-permute-start.2) | collective-permute-done | bytes 8224 | tf_op jit(solution)/shard_map/ppermute | solution.py:250
  26.9 2.9 %collective-permute-done.3.refs_3_ = f32[16,128]{1,0:T(8,128)S(1)} collective-permute-done((f32[16,128]{1,0:T(8,128)S(1)}, f32[16,128]{1,0:T(8,128)S(1)}, u32[]{:S(2)}, u32[]{:S(2)}) %collective-permute-start.3) | collective-permute-done | bytes 8224 | tf_op jit(solution)/shard_map/ppermute | solution.py:250
  29.8 1.0 %shard_map.62 = (f32[16,128]{1,0:T(8,128)}, f32[4,128]{1,0:T(4,128)S(1)}) custom-call(f32[512,2048]{1,0:T(8,128)S(1)} %get-tuple-element.16.tile_ref, f32[16,128]{1,0:T(8,128)S(1)} %bitcast.3, f32[16,128]{1,0:T(8,128)S(1)} %get-tuple-element.17.sqx_ref, f32[16,128]{1,0:T(8,128)S(1)} %multiply_add_fusion.1.refs_0_, ...), custom_call_target="tpu_custom_call" | custom-call | tf_op jit(solution)/shard_map/pallas_call | solution.py:22
  30.8 0.0 collective-permute-start.4
  30.8 1.6 %collective-permute-start.5 = (f32[4,128]{1,0:T(4,128)S(1)}, f32[4,128]{1,0:T(4,128)S(1)}, u32[]{:S(2)}, u32[]{:S(2)}) collective-permute-start(f32[4,128]{1,0:T(4,128)S(1)} %get-tuple-element.19.refs_0_), channel_id=1, source_target_pairs={{0,16},{8,24},{16,0},{24,8},{1,17},{9,25},{17,1},{25,9},{2,18},{10... | collective-permute-start | bytes 6152 | tf_op jit(solution)/shard_map/ppermute | solution.py:250
  32.4 0.3 collective-permute-start.6
  32.7 0.0 collective-permute-done.4.refs_1_
  32.7 1.8 %collective-permute-done.5.refs_2_ = f32[4,128]{1,0:T(4,128)S(1)} collective-permute-done((f32[4,128]{1,0:T(4,128)S(1)}, f32[4,128]{1,0:T(4,128)S(1)}, u32[]{:S(2)}, u32[]{:S(2)}) %collective-permute-start.5) | collective-permute-done | bytes 2080 | tf_op jit(solution)/shard_map/ppermute | solution.py:250
  34.5 0.9 %collective-permute-done.6.refs_3_ = f32[4,128]{1,0:T(4,128)S(1)} collective-permute-done((f32[4,128]{1,0:T(4,128)S(1)}, f32[4,128]{1,0:T(4,128)S(1)}, u32[]{:S(2)}, u32[]{:S(2)}) %collective-permute-start.6) | collective-permute-done | bytes 2080 | tf_op jit(solution)/shard_map/ppermute | solution.py:250
  35.4 1.0 %shard_map.63 = f32[16,128]{1,0:T(8,128)S(1)} custom-call(f32[512,2048]{1,0:T(8,128)S(1)} %get-tuple-element.16.tile_ref, f32[4,128]{1,0:T(4,128)S(1)} %bitcast.6, f32[4,128]{1,0:T(4,128)S(1)} %get-tuple-element.15.sqy_ref, f32[4,128]{1,0:T(4,128)S(1)} %get-tuple-element.19.refs_0_, f32[4,128]{1,0:T(4,128)S(1)} %collective-permute-done.4.refs_1_, ...), custom_call_target="tpu_custom_call" | custom-call | tf_op jit(solution)/shard_map/pallas_call | solution.py:22
  36.5 1.5 %collective-permute-start.7 = (f32[16,128]{1,0:T(8,128)S(1)}, f32[16,128]{1,0:T(8,128)S(1)}, u32[]{:S(2)}, u32[]{:S(2)}) collective-permute-start(f32[16,128]{1,0:T(8,128)S(1)} %shard_map.63), channel_id=1, source_target_pairs={{0,1},{1,0},{2,3},{3,2},{4,5},{5,4},{6,7},{7,6},{8,9},{9,8},{10,11... | collective-permute-start | bytes 24584 | tf_op jit(solution)/shard_map/ppermute | solution.py:250
  38.0 2.2 %collective-permute-done.7 = f32[16,128]{1,0:T(8,128)S(1)} collective-permute-done((f32[16,128]{1,0:T(8,128)S(1)}, f32[16,128]{1,0:T(8,128)S(1)}, u32[]{:S(2)}, u32[]{:S(2)}) %collective-permute-start.7) | collective-permute-done | bytes 8224 | tf_op jit(solution)/shard_map/ppermute | solution.py:250
  40.2 0.4 collective-permute-start.10
  40.6 0.1 collective-permute-start.8
  40.7 3.9 %collective-permute-start.9 = (f32[16,128]{1,0:T(8,128)S(1)}, f32[16,128]{1,0:T(8,128)S(1)}, u32[]{:S(2)}, u32[]{:S(2)}) collective-permute-start(f32[16,128]{1,0:T(8,128)S(1)} %multiply_add_fusion.refs_0_), channel_id=1, source_target_pairs={{0,4},{1,5},{2,6},{3,7},{4,0},{5,1},{6,2},{7,3},{8,12},{9,13},{10,... | collective-permute-start | bytes 24584 | tf_op jit(solution)/shard_map/ppermute | solution.py:250
  44.6 1.2 %collective-permute-done.10.refs_3_ = f32[16,128]{1,0:T(8,128)S(1)} collective-permute-done((f32[16,128]{1,0:T(8,128)S(1)}, f32[16,128]{1,0:T(8,128)S(1)}, u32[]{:S(2)}, u32[]{:S(2)}) %collective-permute-start.10) | collective-permute-done | bytes 8224 | tf_op jit(solution)/shard_map/ppermute | solution.py:250
  45.8 0.0 collective-permute-done.8.refs_1_
  45.9 1.6 %collective-permute-done.9.refs_2_ = f32[16,128]{1,0:T(8,128)S(1)} collective-permute-done((f32[16,128]{1,0:T(8,128)S(1)}, f32[16,128]{1,0:T(8,128)S(1)}, u32[]{:S(2)}, u32[]{:S(2)}) %collective-permute-start.9) | collective-permute-done | bytes 8224 | tf_op jit(solution)/shard_map/ppermute | solution.py:250
  47.5 1.0 %shard_map.64 = (f32[16,128]{1,0:T(8,128)S(1)}, f32[4,128]{1,0:T(4,128)S(1)}) custom-call(f32[512,2048]{1,0:T(8,128)S(1)} %get-tuple-element.16.tile_ref, f32[16,128]{1,0:T(8,128)S(1)} %bitcast.4, f32[16,128]{1,0:T(8,128)S(1)} %get-tuple-element.17.sqx_ref, f32[16,128]{1,0:T(8,128)S(1)} %multiply_add_fusion.refs_0_, ...), custom_call_target="tpu_custom_call" | custom-call | tf_op jit(solution)/shard_map/pallas_call | solution.py:22
  48.5 0.1 collective-permute-start.11
  48.5 0.1 collective-permute-start.12
  48.6 1.8 %collective-permute-start.13 = (f32[4,128]{1,0:T(4,128)S(1)}, f32[4,128]{1,0:T(4,128)S(1)}, u32[]{:S(2)}, u32[]{:S(2)}) collective-permute-start(f32[4,128]{1,0:T(4,128)S(1)} %get-tuple-element.20), channel_id=1, source_target_pairs={{0,24},{8,16},{16,8},{24,0},{1,25},{9,17},{17,9},{25,1},{2,26},{10... | collective-permute-start | bytes 6152 | tf_op jit(solution)/shard_map/ppermute | solution.py:250
  50.4 0.0 collective-permute-done.11
  50.4 1.8 %collective-permute-done.12 = f32[4,128]{1,0:T(4,128)S(1)} collective-permute-done((f32[4,128]{1,0:T(4,128)S(1)}, f32[4,128]{1,0:T(4,128)S(1)}, u32[]{:S(2)}, u32[]{:S(2)}) %collective-permute-start.12) | collective-permute-done | bytes 2080 | tf_op jit(solution)/shard_map/ppermute | solution.py:250
  52.2 0.0 collective-permute-done.13
  52.2 0.1 collective-permute-start.14
  52.3 3.5 %collective-permute-done.14.refs_3_.after_ref = f32[4,128]{1,0:T(4,128)S(1)} collective-permute-done((f32[4,128]{1,0:T(4,128)S(1)}, f32[4,128]{1,0:T(4,128)S(1)}, u32[]{:S(2)}, u32[]{:S(2)}) %collective-permute-start.14) | collective-permute-done | bytes 2080 | tf_op jit(solution)/shard_map/ppermute | solution.py:250
  55.9 2.0 %shard_map.68 = (f32[256,512]{1,0:T(8,128)}, f32[256,512]{1,0:T(8,128)S(1)}) custom-call(f32[512,2048]{1,0:T(8,128)S(1)} %get-tuple-element.16.tile_ref, bf16[2048,512]{1,0:T(8,128)(2,1)S(1)} %copy-done, f32[16,128]{1,0:T(8,128)S(1)} %get-tuple-element.21.bias_ref, f32[4,128]{1,0:T(4,128)S(1)} %get-tuple-element.25.total_ref, ...), custom_call_target="tpu_custom_call" | custom-call | tf_op jit(solution)/shard_map/pallas_call | solution.py:22
  57.9 0.0 collective-permute-start.18
  57.9 1.9 %collective-permute-start.15 = (f32[4,128]{1,0:T(4,128)S(1)}, f32[4,128]{1,0:T(4,128)S(1)}, u32[]{:S(2)}, u32[]{:S(2)}) collective-permute-start(f32[4,128]{1,0:T(4,128)S(1)} %get-tuple-element.24.refs_2_), channel_id=1, source_target_pairs={{0,4},{1,5},{2,6},{3,7},{4,0},{5,1},{6,2},{7,3},{8,12},{9,13},{10,... | collective-permute-start | bytes 6152 | tf_op jit(solution)/shard_map/ppermute | solution.py:250
  59.8 0.6 collective-permute-start.16
  60.3 0.9 all-gather.2.cloned.1.call-done.refs_1_
  61.2 3.5 %shard_map.60 = (bf16[2048,512]{1,0:T(8,128)(2,1)S(1)}, f32[512,2048]{1,0:T(8,128)S(1)}) custom-call(bf16[2048,512]{1,0:T(8,128)(2,1)S(1)} %copy-done.1, f32[2048,512]{1,0:T(8,128)} %all-gather.2.cloned.1.call-done.refs_1_), custom_call_target="tpu_custom_call" | custom-call | tf_op jit(solution)/shard_map/pallas_call | solution.py:22
  64.7 0.0 collective-permute-done.15.refs_4_
  64.8 0.4 collective-permute-done.16.refs_5_
  65.2 1.0 %shard_map.66 = f32[264,512]{1,0:T(8,128)S(1)} custom-call(f32[512,2048]{1,0:T(8,128)S(1)} %get-tuple-element.13.refs_0_, bf16[2048,512]{1,0:T(8,128)(2,1)S(1)} %get-tuple-element.14.refs_1_, f32[4,128]{1,0:T(4,128)S(1)} %get-tuple-element.24.refs_2_, f32[4,128]{1,0:T(4,128)S(1)} %collective-permute-done.14.refs_3_.after_ref, ...), custom_call_target="tpu_custom_call" | custom-call | tf_op jit(solution)/shard_map/pallas_call | solution.py:22
  66.2 1.6 %collective-permute-start.17 = (f32[264,512]{1,0:T(8,128)S(1)}, f32[264,512]{1,0:T(8,128)S(1)}, u32[]{:S(2)}, u32[]{:S(2)}) collective-permute-start(f32[264,512]{1,0:T(8,128)S(1)} %shard_map.66), channel_id=1, source_target_pairs={{0,1},{1,0},{2,3},{3,2},{4,5},{5,4},{6,7},{7,6},{8,9},{9,8},{10,11... | collective-permute-start | bytes 1622024 | tf_op jit(solution)/shard_map/ppermute | solution.py:250
  67.8 0.0 collective-permute-done.18.two_ref
  67.8 0.1 shard_map.69.one_ref
  67.8 1.5 %collective-permute-start.19 = (f32[256,512]{1,0:T(8,128)S(1)}, f32[256,512]{1,0:T(8,128)S(1)}, u32[]{:S(2)}, u32[]{:S(2)}) collective-permute-start(f32[256,512]{1,0:T(8,128)S(1)} %shard_map.69.one_ref), channel_id=1, source_target_pairs={{0,16},{8,24},{16,0},{24,8},{1,17},{9,25},{17,1},{25,9},{2,18},{10... | collective-permute-start | bytes 1572872 | tf_op jit(solution)/shard_map/ppermute | solution.py:250
  69.3 1.0 %shard_map.65.refs_0_.refs_1_ = f32[264,512]{1,0:T(8,128)S(1)} custom-call(f32[512,2048]{1,0:T(8,128)S(1)} %get-tuple-element.13.refs_0_, bf16[2048,512]{1,0:T(8,128)(2,1)S(1)} %get-tuple-element.14.refs_1_, f32[4,128]{1,0:T(4,128)S(1)} %get-tuple-element.24.refs_2_, f32[4,128]{1,0:T(4,128)S(1)} %collective-permute-done.14.refs_3_.after_ref, ...), custom_call_target="tpu_custom_call" | custom-call | tf_op jit(solution)/shard_map/pallas_call | solution.py:22
  70.3 10.9 %collective-permute-done.19.two_ref = f32[256,512]{1,0:T(8,128)S(1)} collective-permute-done((f32[256,512]{1,0:T(8,128)S(1)}, f32[256,512]{1,0:T(8,128)S(1)}, u32[]{:S(2)}, u32[]{:S(2)}) %collective-permute-start.19) | collective-permute-done | bytes 524320 | tf_op jit(solution)/shard_map/ppermute | solution.py:250
  81.3 0.0 collective-permute-done.17.refs_1_.refs_0_
  81.3 0.1 shard_map.70.mine_ref
  81.3 0.1 collective-permute-start.20
  81.4 1.1 %shard_map.67 = f32[256,512]{1,0:T(8,128)} custom-call(f32[264,512]{1,0:T(8,128)S(1)} %shard_map.65.refs_0_.refs_1_, f32[264,512]{1,0:T(8,128)S(1)} %collective-permute-done.17.refs_1_.refs_0_), custom_call_target="tpu_custom_call" | custom-call | tf_op jit(solution)/shard_map/pallas_call | solution.py:22
  82.5 0.8 collective-permute-done.20.other_ref
  83.3 1.0 %shard_map.71 = f32[512,512]{1,0:T(8,128)} custom-call(f32[256,512]{1,0:T(8,128)S(1)} %shard_map.70.mine_ref, f32[256,512]{1,0:T(8,128)S(1)} %collective-permute-done.20.other_ref), custom_call_target="tpu_custom_call" | custom-call | tf_op jit(solution)/shard_map/pallas_call | solution.py:22
  (11 shorter events, 0.1 us)
Async XLA Ops:
  7.2 54.1 %all-gather.2.cloned.1.call-start = ((), (), s32[]{:S(2)}) async-start(), calls=%async_computation | async-start | bytes 4718592 | tf_op jit(solution)/shard_map/all_gather | solution.py:276
  7.2 1.0 %copy-start.2 = (bf16[512,512]{1,0:T(8,128)(2,1)S(1)}, bf16[512,512]{1,0:T(8,128)(2,1)}, u32[]{:S(2)}) copy-start(bf16[512,512]{1,0:T(8,128)(2,1)} %y_ref.3) | copy-start | bytes 1572868
  8.3 21.5 %copy-start.4 = (f32[2048]{0:T(1024)S(1)}, f32[2048]{0:T(1024)}, u32[]{:S(2)}) copy-start(f32[2048]{0:T(1024)} %param.6) | copy-start | bytes 24580
  8.3 27.2 %copy-start.6 = (f32[512]{0:T(512)S(1)}, f32[512]{0:T(512)}, u32[]{:S(2)}) copy-start(f32[512]{0:T(512)} %param.7) | copy-start | bytes 6148
  9.1 1.6 %copy-start = (bf16[2048,512]{1,0:T(8,128)(2,1)S(1)}, bf16[2048,512]{1,0:T(8,128)(2,1)}, u32[]{:S(2)}) copy-start(bf16[2048,512]{1,0:T(8,128)(2,1)} %x_ref.3) | copy-start | bytes 6291460
  10.7 1.0 %copy-start.3 = (bf16[512,512]{1,0:T(8,128)(2,1)S(1)}, bf16[512,512]{1,0:T(8,128)(2,1)}, u32[]{:S(2)}) copy-start(bf16[512,512]{1,0:T(8,128)(2,1)} %y_ref.3) | copy-start | bytes 1572868
  11.7 0.7 copy-start.5
  14.7 4.6 %collective-permute-start = (f32[16,128]{1,0:T(8,128)S(1)}, f32[16,128]{1,0:T(8,128)S(1)}, u32[]{:S(2)}, u32[]{:S(2)}) collective-permute-start(f32[16,128]{1,0:T(8,128)S(1)} %get-tuple-element.18), channel_id=1, source_target_pairs={{0,1},{1,0},{2,3},{3,2},{4,5},{5,4},{6,7},{7,6},{8,9},{9,8},{10,11... | collective-permute-start | bytes 24584 | tf_op jit(solution)/shard_map/ppermute | solution.py:250
  19.4 4.8 %collective-permute-start.1 = (f32[16,128]{1,0:T(8,128)S(1)}, f32[16,128]{1,0:T(8,128)S(1)}, u32[]{:S(2)}, u32[]{:S(2)}) collective-permute-start(f32[16,128]{1,0:T(8,128)S(1)} %multiply_add_fusion.1.refs_0_), channel_id=1, source_target_pairs={{0,2},{1,3},{2,0},{3,1},{4,6},{5,7},{6,4},{7,5},{8,10},{9,11},{10,... | collective-permute-start | bytes 24584 | tf_op jit(solution)/shard_map/ppermute | solution.py:250
  21.5 5.3 %collective-permute-start.2 = (f32[16,128]{1,0:T(8,128)S(1)}, f32[16,128]{1,0:T(8,128)S(1)}, u32[]{:S(2)}, u32[]{:S(2)}) collective-permute-start(f32[16,128]{1,0:T(8,128)S(1)} %multiply_add_fusion.1.refs_0_), channel_id=1, source_target_pairs={{0,4},{1,5},{2,6},{3,7},{4,0},{5,1},{6,2},{7,3},{8,12},{9,13},{10,... | collective-permute-start | bytes 24584 | tf_op jit(solution)/shard_map/ppermute | solution.py:250
  24.1 5.6 %collective-permute-start.3 = (f32[16,128]{1,0:T(8,128)S(1)}, f32[16,128]{1,0:T(8,128)S(1)}, u32[]{:S(2)}, u32[]{:S(2)}) collective-permute-start(f32[16,128]{1,0:T(8,128)S(1)} %multiply_add_fusion.1.refs_0_), channel_id=1, source_target_pairs={{0,6},{1,7},{2,4},{3,5},{4,2},{5,3},{6,0},{7,1},{8,14},{9,15},{10,... | collective-permute-start | bytes 24584 | tf_op jit(solution)/shard_map/ppermute | solution.py:250
  30.8 1.9 %collective-permute-start.4 = (f32[4,128]{1,0:T(4,128)S(1)}, f32[4,128]{1,0:T(4,128)S(1)}, u32[]{:S(2)}, u32[]{:S(2)}) collective-permute-start(f32[4,128]{1,0:T(4,128)S(1)} %get-tuple-element.19.refs_0_), channel_id=1, source_target_pairs={{0,8},{8,0},{16,24},{24,16},{1,9},{9,1},{17,25},{25,17},{2,10},{10... | collective-permute-start | bytes 6152 | tf_op jit(solution)/shard_map/ppermute | solution.py:250
  30.8 3.7 %collective-permute-start.5 = (f32[4,128]{1,0:T(4,128)S(1)}, f32[4,128]{1,0:T(4,128)S(1)}, u32[]{:S(2)}, u32[]{:S(2)}) collective-permute-start(f32[4,128]{1,0:T(4,128)S(1)} %get-tuple-element.19.refs_0_), channel_id=1, source_target_pairs={{0,16},{8,24},{16,0},{24,8},{1,17},{9,25},{17,1},{25,9},{2,18},{10... | collective-permute-start | bytes 6152 | tf_op jit(solution)/shard_map/ppermute | solution.py:250
  32.4 3.0 %collective-permute-start.6 = (f32[4,128]{1,0:T(4,128)S(1)}, f32[4,128]{1,0:T(4,128)S(1)}, u32[]{:S(2)}, u32[]{:S(2)}) collective-permute-start(f32[4,128]{1,0:T(4,128)S(1)} %get-tuple-element.19.refs_0_), channel_id=1, source_target_pairs={{0,24},{8,16},{16,8},{24,0},{1,25},{9,17},{17,9},{25,1},{2,26},{10... | collective-permute-start | bytes 6152 | tf_op jit(solution)/shard_map/ppermute | solution.py:250
  36.5 3.7 %collective-permute-start.7 = (f32[16,128]{1,0:T(8,128)S(1)}, f32[16,128]{1,0:T(8,128)S(1)}, u32[]{:S(2)}, u32[]{:S(2)}) collective-permute-start(f32[16,128]{1,0:T(8,128)S(1)} %shard_map.63), channel_id=1, source_target_pairs={{0,1},{1,0},{2,3},{3,2},{4,5},{5,4},{6,7},{7,6},{8,9},{9,8},{10,11... | collective-permute-start | bytes 24584 | tf_op jit(solution)/shard_map/ppermute | solution.py:250
  40.2 5.7 %collective-permute-start.10 = (f32[16,128]{1,0:T(8,128)S(1)}, f32[16,128]{1,0:T(8,128)S(1)}, u32[]{:S(2)}, u32[]{:S(2)}) collective-permute-start(f32[16,128]{1,0:T(8,128)S(1)} %multiply_add_fusion.refs_0_), channel_id=1, source_target_pairs={{0,6},{1,7},{2,4},{3,5},{4,2},{5,3},{6,0},{7,1},{8,14},{9,15},{10,... | collective-permute-start | bytes 24584 | tf_op jit(solution)/shard_map/ppermute | solution.py:250
  40.6 5.3 %collective-permute-start.8 = (f32[16,128]{1,0:T(8,128)S(1)}, f32[16,128]{1,0:T(8,128)S(1)}, u32[]{:S(2)}, u32[]{:S(2)}) collective-permute-start(f32[16,128]{1,0:T(8,128)S(1)} %multiply_add_fusion.refs_0_), channel_id=1, source_target_pairs={{0,2},{1,3},{2,0},{3,1},{4,6},{5,7},{6,4},{7,5},{8,10},{9,11},{10,... | collective-permute-start | bytes 24584 | tf_op jit(solution)/shard_map/ppermute | solution.py:250
  40.7 6.8 %collective-permute-start.9 = (f32[16,128]{1,0:T(8,128)S(1)}, f32[16,128]{1,0:T(8,128)S(1)}, u32[]{:S(2)}, u32[]{:S(2)}) collective-permute-start(f32[16,128]{1,0:T(8,128)S(1)} %multiply_add_fusion.refs_0_), channel_id=1, source_target_pairs={{0,4},{1,5},{2,6},{3,7},{4,0},{5,1},{6,2},{7,3},{8,12},{9,13},{10,... | collective-permute-start | bytes 24584 | tf_op jit(solution)/shard_map/ppermute | solution.py:250
  48.5 12.8 %copy-start.1 = (bf16[2048,512]{1,0:T(8,128)(2,1)S(1)}, bf16[2048,512]{1,0:T(8,128)(2,1)}, u32[]{:S(2)}) copy-start(bf16[2048,512]{1,0:T(8,128)(2,1)} %x_ref.3) | copy-start | bytes 6291460
  48.5 1.9 %collective-permute-start.11 = (f32[4,128]{1,0:T(4,128)S(1)}, f32[4,128]{1,0:T(4,128)S(1)}, u32[]{:S(2)}, u32[]{:S(2)}) collective-permute-start(f32[4,128]{1,0:T(4,128)S(1)} %get-tuple-element.20), channel_id=1, source_target_pairs={{0,8},{8,0},{16,24},{24,16},{1,9},{9,1},{17,25},{25,17},{2,10},{10... | collective-permute-start | bytes 6152 | tf_op jit(solution)/shard_map/ppermute | solution.py:250
  48.5 3.7 %collective-permute-start.12 = (f32[4,128]{1,0:T(4,128)S(1)}, f32[4,128]{1,0:T(4,128)S(1)}, u32[]{:S(2)}, u32[]{:S(2)}) collective-permute-start(f32[4,128]{1,0:T(4,128)S(1)} %get-tuple-element.20), channel_id=1, source_target_pairs={{0,16},{8,24},{16,0},{24,8},{1,17},{9,25},{17,1},{25,9},{2,18},{10... | collective-permute-start | bytes 6152 | tf_op jit(solution)/shard_map/ppermute | solution.py:250
  48.6 3.6 %collective-permute-start.13 = (f32[4,128]{1,0:T(4,128)S(1)}, f32[4,128]{1,0:T(4,128)S(1)}, u32[]{:S(2)}, u32[]{:S(2)}) collective-permute-start(f32[4,128]{1,0:T(4,128)S(1)} %get-tuple-element.20), channel_id=1, source_target_pairs={{0,24},{8,16},{16,8},{24,0},{1,25},{9,17},{17,9},{25,1},{2,26},{10... | collective-permute-start | bytes 6152 | tf_op jit(solution)/shard_map/ppermute | solution.py:250
  52.2 3.7 %collective-permute-start.14 = (f32[4,128]{1,0:T(4,128)S(1)}, f32[4,128]{1,0:T(4,128)S(1)}, u32[]{:S(2)}, u32[]{:S(2)}) collective-permute-start(f32[4,128]{1,0:T(4,128)S(1)} %get-tuple-element.24.refs_2_), channel_id=1, source_target_pairs={{0,2},{1,3},{2,0},{3,1},{4,6},{5,7},{6,4},{7,5},{8,10},{9,11},{10,... | collective-permute-start | bytes 6152 | tf_op jit(solution)/shard_map/ppermute | solution.py:250
  57.9 9.9 %collective-permute-start.18 = (f32[256,512]{1,0:T(8,128)}, f32[256,512]{1,0:T(8,128)S(1)}, u32[]{:S(2)}, u32[]{:S(2)}) collective-permute-start(f32[256,512]{1,0:T(8,128)} %get-tuple-element.23), channel_id=1, source_target_pairs={{0,8},{8,0},{16,24},{24,16},{1,9},{9,1},{17,25},{25,17},{2,10},{10... | collective-permute-start | bytes 1572872 | tf_op jit(solution)/shard_map/ppermute | solution.py:250
  57.9 6.9 %collective-permute-start.15 = (f32[4,128]{1,0:T(4,128)S(1)}, f32[4,128]{1,0:T(4,128)S(1)}, u32[]{:S(2)}, u32[]{:S(2)}) collective-permute-start(f32[4,128]{1,0:T(4,128)S(1)} %get-tuple-element.24.refs_2_), channel_id=1, source_target_pairs={{0,4},{1,5},{2,6},{3,7},{4,0},{5,1},{6,2},{7,3},{8,12},{9,13},{10,... | collective-permute-start | bytes 6152 | tf_op jit(solution)/shard_map/ppermute | solution.py:250
  59.8 5.4 %collective-permute-start.16 = (f32[4,128]{1,0:T(4,128)S(1)}, f32[4,128]{1,0:T(4,128)S(1)}, u32[]{:S(2)}, u32[]{:S(2)}) collective-permute-start(f32[4,128]{1,0:T(4,128)S(1)} %get-tuple-element.24.refs_2_), channel_id=1, source_target_pairs={{0,6},{1,7},{2,4},{3,5},{4,2},{5,3},{6,0},{7,1},{8,14},{9,15},{10,... | collective-permute-start | bytes 6152 | tf_op jit(solution)/shard_map/ppermute | solution.py:250
  66.2 15.1 %collective-permute-start.17 = (f32[264,512]{1,0:T(8,128)S(1)}, f32[264,512]{1,0:T(8,128)S(1)}, u32[]{:S(2)}, u32[]{:S(2)}) collective-permute-start(f32[264,512]{1,0:T(8,128)S(1)} %shard_map.66), channel_id=1, source_target_pairs={{0,1},{1,0},{2,3},{3,2},{4,5},{5,4},{6,7},{7,6},{8,9},{9,8},{10,11... | collective-permute-start | bytes 1622024 | tf_op jit(solution)/shard_map/ppermute | solution.py:250
  67.8 13.4 %collective-permute-start.19 = (f32[256,512]{1,0:T(8,128)S(1)}, f32[256,512]{1,0:T(8,128)S(1)}, u32[]{:S(2)}, u32[]{:S(2)}) collective-permute-start(f32[256,512]{1,0:T(8,128)S(1)} %shard_map.69.one_ref), channel_id=1, source_target_pairs={{0,16},{8,24},{16,0},{24,8},{1,17},{9,25},{17,1},{25,9},{2,18},{10... | collective-permute-start | bytes 1572872 | tf_op jit(solution)/shard_map/ppermute | solution.py:250
  81.3 2.0 %collective-permute-start.20 = (f32[256,512]{1,0:T(8,128)S(1)}, f32[256,512]{1,0:T(8,128)S(1)}, u32[]{:S(2)}, u32[]{:S(2)}) collective-permute-start(f32[256,512]{1,0:T(8,128)S(1)} %shard_map.70.mine_ref), channel_id=1, source_target_pairs={{0,8},{8,0},{16,24},{24,16},{1,9},{9,1},{17,25},{25,17},{2,10},{10... | collective-permute-start | bytes 1572872 | tf_op jit(solution)/shard_map/ppermute | solution.py:250
Sparse Core Ops, SparseCore 0:
  10.2 51.0 all-gather.1

commit v4 on v3

--- a/solution.py
+++ b/solution.py
@@ -82,11 +82,9 @@
     return jnp.sum(wide * wide, axis=1, keepdims=True) * scale(block.shape[1])
 
 
-def half_kernel(y_ref, *out_refs):
-    part = out_refs[0].shape[0]
-    start = lax.axis_index("row") % 2 * part * len(out_refs)
-    for k, ref in enumerate(out_refs):
-        ref[...] = y_ref[pl.ds(pl.multiple_of(start + k * part, part), part), :].astype(jnp.float32)
+def quarter_kernel(y_ref, out_ref):
+    rows = out_ref.shape[0]
+    out_ref[...] = y_ref[pl.ds(pl.multiple_of(lax.axis_index("row") * rows, rows), rows), :].astype(jnp.float32)
 
 
 def first_kernel(y_ref, x_ref, lt_ref, tile_ref, lse_ref, sqx_ref, sqy_ref):
@@ -109,16 +107,50 @@
     sqx_ref[...] = to_dense(columns)
 
 
-def targets_kernel(tile_ref, lt_ref, sqy_ref, *refs):
-    parts, lse_ref = refs[:-1], refs[-1]
+def targets_kernel(n_parts, tile_ref, lt_ref, sqy_ref, *refs):
+    parts, pieces, (lse_ref, pack_ref) = refs[:n_parts], refs[n_parts:-2], refs[-2:]
+    half = pieces[0].shape[0] // 2
+    pack_ref[:half, :] = pieces[0][half:, :]
+    for k, piece in enumerate(pieces[1:]):
+        pack_ref[pl.ds(half + 2 * half * k, 2 * half), :] = piece[...]
     g_pot = sqy_ref[...] - merge_all([ref[...] for ref in parts])
     bias = to_column(lt_ref[...] * LOG2E + g_pot - sqy_ref[...])
     for b in range(tile_ref.shape[1] // LANES):
         lse_ref[pl.ds(b, 1), :] = over_targets(tile_ref[:, pl.ds(b * LANES, LANES)] + bias)
 
 
-def sources_kernel(tile_ref, ls_ref, sqx_ref, *refs):
-    parts, (bias_ref, lse_ref) = refs[:-2], refs[-2:]
+def merge_kernel(one_ref, two_ref, *refs):
+    n_pieces = len(refs) // 2
+    pieces, (out_ref, pack_ref, *copies) = refs[:n_pieces], refs[n_pieces:]
+    out_ref[...] = merge_all([one_ref[...], two_ref[...]])
+    rows = pieces[0].shape[0]
+    pack_ref[:rows, :] = pieces[0][...]
+    pack_ref[rows:, :] = pieces[1][: rows // 2, :]
+    for piece, copy in zip(pieces[1:], copies):
+        copy[...] = piece[...]
+
+
+def sources_kernel(n_parts, tile_ref, ls_ref, sqx_ref, *refs):
+    sources_pass(tile_ref, ls_ref, sqx_ref, refs[:n_parts], *refs[-2:])
+
+
+def last_sources_kernel(n_parts, tile_ref, ls_ref, sqx_ref, *refs):
+    pieces, (bias_ref, lse_ref, pack_ref) = refs[n_parts:-3], refs[-3:]
+    n_shards, n_y, rows, _ = pack_ref.shape
+    y = lax.axis_index("row") // 2
+    early, late = pieces[:n_y], pieces[n_y:]
+    half = rows // 2
+    for j in range(n_y):
+        place = y ^ j
+        pack_ref[0, place] = early[j][:rows, :]
+        pack_ref[1, place, :half, :] = early[j][rows:, :]
+        pack_ref[1, place, half:, :] = late[j][:half, :]
+        for k in range(2, n_shards):
+            pack_ref[k, place] = late[j][pl.ds(half + (k - 2) * rows, rows), :]
+    sources_pass(tile_ref, ls_ref, sqx_ref, refs[:n_parts], bias_ref, lse_ref)
+
+
+def sources_pass(tile_ref, ls_ref, sqx_ref, parts, bias_ref, lse_ref):
     f_pot = sqx_ref[...] - merge_all([ref[...] for ref in parts])
     bias = ls_ref[...] * LOG2E + f_pot - sqx_ref[...]
     bias_ref[...] = bias
@@ -136,7 +168,7 @@
     lse_ref[...] = to_dense(columns)
 
 
-def means_kernel(tile_ref, x_ref, bias_ref, total_ref, after_ref, sent_ref, mine_ref):
+def means_kernel(tile_ref, x_ref, bias_ref, total_ref, sent_ref, mine_ref):
     bias = bias_ref[...]
     x = x_ref[...]
     half = mine_ref.shape[0]
@@ -179,28 +211,36 @@
     other.wait()
 
 
-def scores_kernel(n_x, x_ref, all_ref, y_ref, inner_ref):
-    rows = inner_ref.shape[0]
-    start = lax.axis_index("col") // n_x * rows
-    own = x_ref[pl.ds(pl.multiple_of(start, rows), rows), :]
-    unit = scale(own.shape[1])
-    wide = 512
-    for b in range(y_ref.shape[0] // wide):
-        at = pl.ds(b * wide, wide)
-        y = all_ref[at, :].astype(jnp.bfloat16)
-        y_ref[at, :] = y
-        inner_ref[:, at] = lax.dot_general(own, y, NT_DIMS, preferred_element_type=jnp.float32) * (2.0 * unit)
-
-
-def images(flip, n_x, inner_ref, y_ref, bias_refs, scores_ref):
+def scores_kernel(near, x_ref, own_ref, mine_ref, other_ref, y_ref, inner_ref):
+    rows = inner_ref.shape[0] // 2
+    n_tgt = own_ref.shape[0]
+    n_came, n_y, part, _ = mine_ref.shape
+    col, core = lax.axis_index("col"), lax.axis_index("row") % 2
+    y_ref[:n_tgt, :] = own_ref[...]
+    for k in range(n_came):
+        for ref, place in ((mine_ref, core), (other_ref, 1 - core)):
+            for y in range(n_y):
+                start = (k + 1) * n_tgt + (2 * y + place) * part
+                y_ref[pl.ds(pl.multiple_of(start, part), part), :] = ref[k, y].astype(jnp.bfloat16)
+    blocks = [x_ref[pl.ds(pl.multiple_of((col ^ flip) * rows, rows), rows), :] for flip in (0, near)]
+    x = jnp.concatenate(blocks, axis=0)
+    unit = scale(x.shape[1])
+    for b in range(y_ref.shape[0] // n_tgt):
+        at = pl.ds(b * n_tgt, n_tgt)
+        inner_ref[:, at] = lax.dot_general(x, y_ref[at, :], NT_DIMS, preferred_element_type=jnp.float32) * (2.0 * unit)
+
+
+EXTRA = 8
+
+
+def images(flip, inner_ref, y_ref, bias_refs, scores_ref):
     rows = scores_ref.shape[0]
     n_shards = len(bias_refs)
     n_tgt = y_ref.shape[0] // n_shards
-    col = lax.axis_index("col")
-    block = pl.ds(pl.multiple_of((col ^ flip) % n_x * rows, rows), rows)
+    block = pl.ds(flip * rows, rows)
     peak = jnp.full((rows, 1), -jnp.inf, jnp.float32)
     for k in range(n_shards):
-        at = pl.ds(pl.multiple_of((col // n_x ^ k) * n_tgt, n_tgt), n_tgt)
+        at = pl.ds(k * n_tgt, n_tgt)
         scores = inner_ref[block, at] + to_row(bias_refs[k][...])
         scores_ref[:, at] = scores
         peak = jnp.maximum(peak, jnp.max(scores, axis=1, keepdims=True))
@@ -224,20 +264,9 @@
 EXTRA = 8
 
 
-def others_kernel(n_x, inner_ref, y_ref, *refs):
-    bias_refs, image_refs, scores_ref = refs[: -n_x], refs[-n_x:-1], refs[-1]
-    for flip, image_ref in enumerate(image_refs, 1):
-        numer, total, peak = images(flip, n_x, inner_ref, y_ref, bias_refs, scores_ref)
-        rows = numer.shape[0]
-        lse = lanes_of(peak + jnp.log2(total))
-        image_ref[:rows, :] = numer * (1.0 / total)
-        image_ref[rows:, :] = jnp.zeros((EXTRA, image_ref.shape[1]), jnp.float32)
-        image_ref[rows : rows + lse.shape[0], :LANES] = lse
-
-
-def own_kernel(n_x, inner_ref, y_ref, *refs):
-    bias_refs, (image_ref, scores_ref) = refs[:-2], refs[-2:]
-    numer, total, peak = images(0, n_x, inner_ref, y_ref, bias_refs, scores_ref)
+def image_kernel(flip, inner_ref, y_ref, *refs):
+    bias_refs, (image_ref, scores_ref) = refs[:-3], refs[-2:]
+    numer, total, peak = images(flip, inner_ref, y_ref, bias_refs, scores_ref)
     rows = numer.shape[0]
     lse = lanes_of(peak + jnp.log2(total))
     image_ref[:rows, :] = numer * (1.0 / total)
@@ -261,64 +290,99 @@
     count = n_src // n_col
     n_x = 1 << (len(bits_of(n_col)) // 2)
     n_z = n_col // n_x
-    around = [
-        [(y + core) * n_col + z * n_x + x for z in range(n_z) for core in range(2)]
-        for y in range(0, n_row, 2)
-        for x in range(n_x)
-    ]
+    y_bits = bits_of(n_row)[1:]
     ls = log_source_mass.reshape(-1, LANES)
     lt = log_target_mass.reshape(-1, LANES)
     src_dense, tgt_dense = f32(*ls.shape), f32(*lt.shape)
     half = n_tgt // 2
 
-    n_parts = 1
-    parts = call(half_kernel, (f32(half // n_parts, width),) * n_parts, target)
-    gathered = [lax.all_gather(part, ("row", "col"), axis_index_groups=around, tiled=True) for part in parts]
+    part = f32(n_tgt // n_row, width)
+    pieces = {0: call(quarter_kernel, part, target)}
+    for distance in [bit for bit in bits_of(n_col) if bit > n_x][::-1]:
+        pieces |= {k ^ distance: swap(piece, "col", distance) for k, piece in pieces.items()}
+    early = swap(pieces[0], "col", 1)
+
+    def along_y(piece):
+        held = [piece]
+        for distance in y_bits:
+            held += [swap(one, "row", distance) for one in held]
+        return held
 
     tile, lse, sqx, sqy = call(
         first_kernel, (f32(n_tgt, n_src), src_dense, src_dense, tgt_dense), target, source, lt
     )
     for step in range(ITERS):
         if step > 0:
-            lse = call(targets_kernel, src_dense, tile, lt, sqy, *parts)
+            apart = [0, 1] + [k for k in pieces if k > 1]
+            lse, late = call(
+                lambda *refs: targets_kernel(n_row, *refs),
+                (src_dense, f32((2 * len(apart) - 5) * part.shape[0] // 2, width)),
+                tile, lt, sqy, *parts, *[pieces[k] for k in apart[2:]],
+            )
+            late = along_y(late)
         for distance in bits_of(n_x):
-            lse = merge_all([lse, swap(lse, "col", distance)])
+            came = swap(lse, "col", distance)
+            if step > 0 or distance > 1:
+                lse = merge_all([lse, came])
+                continue
+            far = [k for k in pieces if k > 0]
+            lse, early, *copies = call(
+                merge_kernel,
+                (src_dense, f32(part.shape[0] * 3 // 2, width), *(part,) * len(far)),
+                lse, came, early, *[pieces[k] for k in far],
+            )
+            early = along_y(early)
+            pieces |= dict(zip(far, copies))
+            for bit in bits_of(n_x)[::-1]:
+                pieces |= {k ^ bit: swap(piece, "col", bit) for k, piece in pieces.items() if k ^ bit != 1}
         parts = [lse] + [swap(lse, "col", k * n_x) for k in range(1, n_z)]
-        src_bias, lse = call(sources_kernel, (src_dense, tgt_dense), tile, ls, sqx, *parts)
+        if step < ITERS - 1:
+            src_bias, lse = call(
+                lambda *refs: sources_kernel(n_z, *refs), (src_dense, tgt_dense), tile, ls, sqx, *parts, *early
+            )
+        else:
+            src_bias, lse, came = call(
+                lambda *refs: last_sources_kernel(n_z, *refs),
+                (src_dense, tgt_dense, f32(len(apart) - 1, n_row // 2, *part.shape)),
+                tile, ls, sqx, *parts, *early, *late,
+            )
         parts = [lse] + [swap(lse, "row", k) for k in range(1, n_row)]
     total = merge_all(parts)
 
     bias = lt * LOG2E + (sqy - total) - sqy
-    biases = [bias] + [swap(bias, "col", k * n_x) for k in range(1, n_z)]
-
-    sent, mine = call(
-        means_kernel, (f32(half, width), f32(half, width)), tile, source, src_bias, total, biases[1]
-    )
+    biases = [bias] + [swap(bias, "col", distance) for distance in apart[1:]]
+
+    sent, mine = call(means_kernel, (f32(half, width), f32(half, width)), tile, source, src_bias, total)
     mine = call(add_kernel, f32(half, width), mine, swap(sent, "row", 1))
     rest = bits_of(n_row)[1:]
     for distance in rest[:-1]:
         mine = call(add_kernel, f32(half, width), mine, swap(mine, "row", distance))
-    came = swap(mine, "row", rest[-1])
-
-    n_all = n_z * n_tgt
+    mine_came = swap(mine, "row", rest[-1])
+
+    n_all = len(apart) * n_tgt
     all_y, inner = call(
         lambda *refs: scores_kernel(n_x, *refs),
-        (bf16(n_all, width), f32(n_x * count, n_all)),
-        source, *gathered,
-        limit=44,
+        (bf16(n_all, width), f32(2 * count, n_all)),
+        source, target, came, swap(came, "row", 1),
+        limit=32,
     )
-    scores = pltpu.VMEM((count, n_all), jnp.float32)
-    image = f32(count + EXTRA, width)
-    others = call(
-        lambda *refs: others_kernel(n_x, *refs), (image,) * (n_x - 1), inner, all_y, *biases, scratch=[scores]
-    )
-    joined = [swap(part, "col", flip) for flip, part in enumerate(others, 1)]
-    own = call(lambda *refs: own_kernel(n_x, *refs), image, inner, all_y, *biases, scratch=[scores])
-    mine = call(add_kernel, f32(half, width), mine, came, joined[0], own)
+
+    def image(flip, after):
+        return call(
+            lambda *refs: image_kernel(flip, *refs),
+            f32(count + EXTRA, width),
+            inner, all_y, *biases, after,
+            scratch=[pltpu.VMEM((count, n_all), jnp.float32)],
+        )
+
+    sent = image(1, mine)
+    came = swap(sent, "col", n_x)
+    own = image(0, sent)
+    mine = call(add_kernel, f32(half, width), mine, mine_came, came, own)
     target_image = call(
         place_kernel, f32(n_tgt, width), mine, swap(mine, "row", 1), out_specs=HBM, scratch=[DMA((2,))]
     )
-    source_image = call(join_kernel, f32(count, width), own, *joined)
+    source_image = call(join_kernel, f32(count, width), own, came)
     return source_image, target_image
 
 

time: 91.5 us -> 82.5 us (0.902)
  between operations: 14.2 us -> 0.81 us
  starting transfers between devices: 23.3 us -> 31.6 us
  Pallas kernels: 15.9 us -> 12.3 us
  local copies, waits for them, and re-layouts: 4.36 us -> 3.32 us
    ppermute x21 -> x27, starting transfers between devices: 23.3 us -> 31.6 us  [swap(): return lax.ppermute(value, axis, [(i, i ^ distance) for i in range(n)])]
    pallas_call x13 -> x14, Pallas kernels: 15.9 us -> 12.3 us  [call(): pl.pallas_call(kernel, out_shape=out_shape, in_specs=in_specs or [VMEM] *...]
    ppermute x21 -> x27, waiting for transfers between devices: 32.4 us -> 34.1 us  [swap(): return lax.ppermute(value, axis, [(i, i ^ distance) for i in range(n)])]
    unnamed x14 -> x12, local copies, waits for them, and re-layouts: 4.36 us -> 3.32 us
  transfers between devices with their start and end apart: 22 -> 27, of which waited for: 14 -> 14; matrix products, arithmetic and copies ran while one was open for 0% -> 0% of each run, Pallas kernels for 15% -> 10%
where the time goes in v4:
time: 82.5 us; the launch traced here: 82.3 us
  waiting for transfers between devices  34.1 us (41%)
  starting transfers between devices  31.6 us (38%)
  Pallas kernels  12.3 us (15%)
  local copies, waits for them, and re-layouts  3.32 us (4%)
    ppermute x27, waiting for transfers between devices, swap(): return lax.ppermute(value, axis, [(i, i ^ distance) for i in range(n)])  34.1 us
    ppermute x27, starting transfers between devices, swap(): return lax.ppermute(value, axis, [(i, i ^ distance) for i in range(n)])  31.6 us
    pallas_call x14, Pallas kernels, call(): pl.pallas_call(kernel, out_shape=out_shape, in_specs=in_specs or [VMEM] *...  12.3 us
    unnamed x12, local copies, waits for them, and re-layouts  3.32 us
  transfers between devices with their start and end apart: 27, of which 14 were waited for; matrix products, arithmetic and copies ran while one was open for 0% of the time, Pallas kernels for 10%

profile of v4, /device:TPU:0, one launch (start us, length us, event | category | flops | bytes accessed | tf_op | source)
XLA Modules:
  0.0 82.3 jit_solution(13545204788825649217)
XLA Ops:
  0.6 0.0 copy-start.2
  0.6 1.0 %copy-done.2 = bf16[512,512]{1,0:T(8,128)(2,1)S(1)} copy-done((bf16[512,512]{1,0:T(8,128)(2,1)S(1)}, bf16[512,512]{1,0:T(8,128)(2,1)}, u32[]{:S(2)}) %copy-start.2) | copy-done | bytes 524312
  1.7 3.0 %collective-permute-start.1 = (f32[128,512]{1,0:T(8,128)S(1)}, f32[128,512]{1,0:T(8,128)S(1)}, u32[]{:S(2)}, u32[]{:S(2)}) collective-permute-start(f32[128,512]{1,0:T(8,128)S(1)} %shard_map.60), channel_id=1, source_target_pairs={{0,1},{1,0},{2,3},{3,2},{4,5},{5,4},{6,7},{7,6},{8,9},{9,8},{10,11... | collective-permute-start | bytes 786440 | tf_op jit(solution)/shard_map/ppermute | solution.py:279
  4.7 2.6 %collective-permute-start.2 = (f32[128,512]{1,0:T(8,128)S(1)}, f32[128,512]{1,0:T(8,128)S(1)}, u32[]{:S(2)}, u32[]{:S(2)}) collective-permute-start(f32[128,512]{1,0:T(8,128)S(1)} %shard_map.60), channel_id=1, source_target_pairs={{0,4},{1,5},{2,6},{3,7},{4,0},{5,1},{6,2},{7,3},{8,12},{9,13},{10,... | collective-permute-start | bytes 786440 | tf_op jit(solution)/shard_map/ppermute | solution.py:279
  7.3 1.6 %copy-done = bf16[2048,512]{1,0:T(8,128)(2,1)S(1)} copy-done((bf16[2048,512]{1,0:T(8,128)(2,1)S(1)}, bf16[2048,512]{1,0:T(8,128)(2,1)}, u32[]{:S(2)}) %copy-start) | copy-done | bytes 2097176
  8.9 0.7 copy-done.5
  9.6 2.3 %shard_map.59 = (f32[512,2048]{1,0:T(8,128)S(1)}, f32[16,128]{1,0:T(8,128)S(1)}, f32[16,128]{1,0:T(8,128)S(1)}, f32[4,128]{1,0:T(4,128)S(1)}) custom-call(bf16[512,512]{1,0:T(8,128)(2,1)S(1)} %copy-done.2, bf16[2048,512]{1,0:T(8,128)(2,1)S(1)} %copy-done, f32[4,128]{1,0:T(4,128)S(1)} %bitcast.5), custom_call_target="tpu_custom_call" | custom-call | tf_op jit(solution)/shard_map/pallas_call | solution.py:22
  11.9 0.6 collective-permute-start
  12.5 3.1 %collective-permute-done.two_ref = f32[16,128]{1,0:T(8,128)S(1)} collective-permute-done((f32[16,128]{1,0:T(8,128)S(1)}, f32[16,128]{1,0:T(8,128)S(1)}, u32[]{:S(2)}, u32[]{:S(2)}) %collective-permute-start) | collective-permute-done | bytes 8224 | tf_op jit(solution)/shard_map/ppermute | solution.py:279
  15.6 0.0 collective-permute-done.1.refs_0_
  15.6 3.4 %collective-permute-done.2.refs_1_ = f32[128,512]{1,0:T(8,128)S(1)} collective-permute-done((f32[128,512]{1,0:T(8,128)S(1)}, f32[128,512]{1,0:T(8,128)S(1)}, u32[]{:S(2)}, u32[]{:S(2)}) %collective-permute-start.2) | collective-permute-done | bytes 262176 | tf_op jit(solution)/shard_map/ppermute | solution.py:279
  19.0 1.6 %collective-permute-start.6 = (f32[192,512]{1,0:T(8,128)S(1)}, f32[192,512]{1,0:T(8,128)S(1)}, u32[]{:S(2)}, u32[]{:S(2)}) collective-permute-start(f32[192,512]{1,0:T(8,128)S(1)} %get-tuple-element.24.refs_7_), channel_id=1, source_target_pairs={{0,16},{8,24},{16,0},{24,8},{1,17},{9,25},{17,1},{25,9},{2,18},{10... | collective-permute-start | bytes 1179656 | tf_op jit(solution)/shard_map/ppermute | solution.py:279
  20.6 0.5 collective-permute-start.10
  21.2 0.7 collective-permute-start.3
  21.8 3.4 %collective-permute-start.4 = (f32[16,128]{1,0:T(8,128)S(1)}, f32[16,128]{1,0:T(8,128)S(1)}, u32[]{:S(2)}, u32[]{:S(2)}) collective-permute-start(f32[16,128]{1,0:T(8,128)S(1)} %get-tuple-element.23.refs_3_), channel_id=1, source_target_pairs={{0,4},{1,5},{2,6},{3,7},{4,0},{5,1},{6,2},{7,3},{8,12},{9,13},{10,... | collective-permute-start | bytes 24584 | tf_op jit(solution)/shard_map/ppermute | solution.py:279
  25.2 0.3 collective-permute-start.5
  25.5 1.3 %collective-permute-done.4.refs_5_ = f32[16,128]{1,0:T(8,128)S(1)} collective-permute-done((f32[16,128]{1,0:T(8,128)S(1)}, f32[16,128]{1,0:T(8,128)S(1)}, u32[]{:S(2)}, u32[]{:S(2)}) %collective-permute-start.4) | collective-permute-done | bytes 8224 | tf_op jit(solution)/shard_map/ppermute | solution.py:279
  26.8 3.8 %collective-permute-done.5.refs_6_ = f32[16,128]{1,0:T(8,128)S(1)} collective-permute-done((f32[16,128]{1,0:T(8,128)S(1)}, f32[16,128]{1,0:T(8,128)S(1)}, u32[]{:S(2)}, u32[]{:S(2)}) %collective-permute-start.5) | collective-permute-done | bytes 8224 | tf_op jit(solution)/shard_map/ppermute | solution.py:279
  30.7 0.0 collective-permute-done.6.refs_8_
  30.7 1.0 %shard_map.62 = (f32[16,128]{1,0:T(8,128)}, f32[4,128]{1,0:T(4,128)S(1)}) custom-call(f32[512,2048]{1,0:T(8,128)S(1)} %get-tuple-element.19.refs_0_.tile_ref, f32[16,128]{1,0:T(8,128)S(1)} %bitcast.3, f32[16,128]{1,0:T(8,128)S(1)} %get-tuple-element.20.refs_2_, f32[16,128]{1,0:T(8,128)S(1)} %get-tuple-element.23.refs_3_, ...), custom_call_target="tpu_custom_call" | custom-call | tf_op jit(solution)/shard_map/pallas_call | solution.py:22
  31.7 0.0 collective-permute-start.7
  31.7 0.6 collective-permute-start.8
  32.3 1.3 %collective-permute-start.9 = (f32[4,128]{1,0:T(4,128)S(1)}, f32[4,128]{1,0:T(4,128)S(1)}, u32[]{:S(2)}, u32[]{:S(2)}) collective-permute-start(f32[4,128]{1,0:T(4,128)S(1)} %get-tuple-element.25.refs_3_), channel_id=1, source_target_pairs={{0,24},{8,16},{16,8},{24,0},{1,25},{9,17},{17,9},{25,1},{2,26},{10... | collective-permute-start | bytes 6152 | tf_op jit(solution)/shard_map/ppermute | solution.py:279
  33.6 0.0 collective-permute-done.10.refs_8_
  33.6 0.0 collective-permute-done.7.refs_4_
  33.6 1.8 %collective-permute-done.8.refs_5_ = f32[4,128]{1,0:T(4,128)S(1)} collective-permute-done((f32[4,128]{1,0:T(4,128)S(1)}, f32[4,128]{1,0:T(4,128)S(1)}, u32[]{:S(2)}, u32[]{:S(2)}) %collective-permute-start.8) | collective-permute-done | bytes 2080 | tf_op jit(solution)/shard_map/ppermute | solution.py:279
  35.4 0.0 collective-permute-done.9.refs_6_
  35.4 1.1 %shard_map.63 = (f32[16,128]{1,0:T(8,128)S(1)}, f32[192,512]{1,0:T(8,128)S(1)}) custom-call(f32[512,2048]{1,0:T(8,128)S(1)} %get-tuple-element.19.refs_0_.tile_ref, f32[4,128]{1,0:T(4,128)S(1)} %bitcast.6, f32[4,128]{1,0:T(4,128)S(1)} %get-tuple-element.21.refs_2_, f32[4,128]{1,0:T(4,128)S(1)} %get-tuple-element.25.refs_3_, ...), custom_call_target="tpu_custom_call" | custom-call | tf_op jit(solution)/shard_map/pallas_call | solution.py:22
  36.5 1.5 %collective-permute-start.15 = (f32[192,512]{1,0:T(8,128)S(1)}, f32[192,512]{1,0:T(8,128)S(1)}, u32[]{:S(2)}, u32[]{:S(2)}) collective-permute-start(f32[192,512]{1,0:T(8,128)S(1)} %get-tuple-element.28.refs_9_), channel_id=1, source_target_pairs={{0,16},{8,24},{16,0},{24,8},{1,17},{9,25},{17,1},{25,9},{2,18},{10... | collective-permute-start | bytes 1179656 | tf_op jit(solution)/shard_map/ppermute | solution.py:279
  38.0 1.5 %collective-permute-start.11 = (f32[16,128]{1,0:T(8,128)S(1)}, f32[16,128]{1,0:T(8,128)S(1)}, u32[]{:S(2)}, u32[]{:S(2)}) collective-permute-start(f32[16,128]{1,0:T(8,128)S(1)} %get-tuple-element.27), channel_id=1, source_target_pairs={{0,1},{1,0},{2,3},{3,2},{4,5},{5,4},{6,7},{7,6},{8,9},{9,8},{10,11... | collective-permute-start | bytes 24584 | tf_op jit(solution)/shard_map/ppermute | solution.py:279
  39.5 2.2 %collective-permute-done.11 = f32[16,128]{1,0:T(8,128)S(1)} collective-permute-done((f32[16,128]{1,0:T(8,128)S(1)}, f32[16,128]{1,0:T(8,128)S(1)}, u32[]{:S(2)}, u32[]{:S(2)}) %collective-permute-start.11) | collective-permute-done | bytes 8224 | tf_op jit(solution)/shard_map/ppermute | solution.py:279
  41.7 0.0 copy-start.1
  41.7 0.3 collective-permute-start.12
  42.0 3.4 %collective-permute-start.13 = (f32[16,128]{1,0:T(8,128)S(1)}, f32[16,128]{1,0:T(8,128)S(1)}, u32[]{:S(2)}, u32[]{:S(2)}) collective-permute-start(f32[16,128]{1,0:T(8,128)S(1)} %multiply_add_fusion.refs_3_), channel_id=1, source_target_pairs={{0,4},{1,5},{2,6},{3,7},{4,0},{5,1},{6,2},{7,3},{8,12},{9,13},{10,... | collective-permute-start | bytes 24584 | tf_op jit(solution)/shard_map/ppermute | solution.py:279
  45.3 0.8 collective-permute-start.14
  46.1 0.8 %collective-permute-done.13.refs_5_ = f32[16,128]{1,0:T(8,128)S(1)} collective-permute-done((f32[16,128]{1,0:T(8,128)S(1)}, f32[16,128]{1,0:T(8,128)S(1)}, u32[]{:S(2)}, u32[]{:S(2)}) %collective-permute-start.13) | collective-permute-done | bytes 8224 | tf_op jit(solution)/shard_map/ppermute | solution.py:279
  47.0 3.8 %collective-permute-done.14.refs_6_ = f32[16,128]{1,0:T(8,128)S(1)} collective-permute-done((f32[16,128]{1,0:T(8,128)S(1)}, f32[16,128]{1,0:T(8,128)S(1)}, u32[]{:S(2)}, u32[]{:S(2)}) %collective-permute-start.14) | collective-permute-done | bytes 8224 | tf_op jit(solution)/shard_map/ppermute | solution.py:279
  50.8 0.0 collective-permute-done.15.refs_10_
  50.8 1.0 %shard_map.64 = (f32[16,128]{1,0:T(8,128)S(1)}, f32[4,128]{1,0:T(4,128)S(1)}, f32[3,2,128,512]{3,2,1,0:T(8,128)S(1)}) custom-call(f32[512,2048]{1,0:T(8,128)S(1)} %get-tuple-element.19.refs_0_.tile_ref, f32[16,128]{1,0:T(8,128)S(1)} %bitcast.4, f32[16,128]{1,0:T(8,128)S(1)} %get-tuple-element.20.refs_2_, f32[16,128]{1,0:T(8,128)S(1)} %multiply_add_fusion.refs_3_, ...), custom_call_target="tpu_custom_call" | custom-call | tf_op jit(solution)/shard_map/pallas_call | solution.py:22
  51.8 0.1 collective-permute-start.16
  51.9 0.5 collective-permute-start.17
  52.4 1.5 %collective-permute-start.18 = (f32[4,128]{1,0:T(4,128)S(1)}, f32[4,128]{1,0:T(4,128)S(1)}, u32[]{:S(2)}, u32[]{:S(2)}) collective-permute-start(f32[4,128]{1,0:T(4,128)S(1)} %get-tuple-element.32), channel_id=1, source_target_pairs={{0,16},{8,24},{16,0},{24,8},{1,17},{9,25},{17,1},{25,9},{2,18},{10... | collective-permute-start | bytes 6152 | tf_op jit(solution)/shard_map/ppermute | solution.py:279
  53.9 1.4 %collective-permute-done.17 = f32[4,128]{1,0:T(4,128)S(1)} collective-permute-done((f32[4,128]{1,0:T(4,128)S(1)}, f32[4,128]{1,0:T(4,128)S(1)}, u32[]{:S(2)}, u32[]{:S(2)}) %collective-permute-start.17) | collective-permute-done | bytes 2080 | tf_op jit(solution)/shard_map/ppermute | solution.py:279
  55.3 0.7 collective-permute-done.18
  56.0 0.9 %collective-permute-done.19 = f32[4,128]{1,0:T(4,128)S(1)} collective-permute-done((f32[4,128]{1,0:T(4,128)S(1)}, f32[4,128]{1,0:T(4,128)S(1)}, u32[]{:S(2)}, u32[]{:S(2)}) %collective-permute-start.19) | collective-permute-done | bytes 2080 | tf_op jit(solution)/shard_map/ppermute | solution.py:279
  56.9 0.0 copy-start.3
  56.9 1.6 %shard_map.66 = (f32[256,512]{1,0:T(8,128)S(1)}, f32[256,512]{1,0:T(8,128)S(1)}) custom-call(f32[512,2048]{1,0:T(8,128)S(1)} %get-tuple-element.19.refs_0_.tile_ref, bf16[2048,512]{1,0:T(8,128)(2,1)S(1)} %copy-done.1, f32[16,128]{1,0:T(8,128)S(1)} %get-tuple-element.33.bias_ref, f32[4,128]{1,0:T(4,128)S(1)} %get-tuple-element.37.total_ref), custom_call_target="tpu_custom_call" | custom-call | tf_op jit(solution)/shard_map/pallas_call | solution.py:22
  58.5 0.1 collective-permute-start.23
  58.6 0.6 collective-permute-start.20
  59.2 0.0 collective-permute-start.21
  59.2 3.8 %collective-permute-start.22 = (f32[4,128]{1,0:T(4,128)S(1)}, f32[4,128]{1,0:T(4,128)S(1)}, u32[]{:S(2)}, u32[]{:S(2)}) collective-permute-start(f32[4,128]{1,0:T(4,128)S(1)} %get-tuple-element.36.refs_2_), channel_id=1, source_target_pairs={{0,5},{1,4},{2,7},{3,6},{4,1},{5,0},{6,3},{7,2},{8,13},{9,12},{10,... | collective-permute-start | bytes 6152 | tf_op jit(solution)/shard_map/ppermute | solution.py:279
  63.0 0.1 shard_map.67.refs_6_.one_ref
  63.1 1.3 %shard_map.65 = (bf16[2048,512]{1,0:T(8,128)(2,1)S(1)}, f32[512,2048]{1,0:T(8,128)S(1)}) custom-call(bf16[2048,512]{1,0:T(8,128)(2,1)S(1)} %copy-done.1, bf16[512,512]{1,0:T(8,128)(2,1)S(1)} %copy-done.3, f32[3,2,128,512]{3,2,1,0:T(8,128)S(1)} %get-tuple-element.29.refs_2_, f32[3,2,128,512]{3,2,1,0:T(8,128)S(1)} %collective-permute-done.16.refs_3_), custom_call_target="tpu_custom_call" | custom-call | tf_op jit(solution)/shard_map/pallas_call | solution.py:22
  64.5 0.1 collective-permute-done.22.refs_5_
  64.6 0.9 %shard_map.68.refs_6_ = f32[264,512]{1,0:T(8,128)S(1)} custom-call(f32[512,2048]{1,0:T(8,128)S(1)} %get-tuple-element.30.refs_0_, bf16[2048,512]{1,0:T(8,128)(2,1)S(1)} %get-tuple-element.31.refs_1_, f32[4,128]{1,0:T(4,128)S(1)} %get-tuple-element.36.refs_2_, f32[4,128]{1,0:T(4,128)S(1)} %collective-permute-done.20.refs_3_, ...), custom_call_target="tpu_custom_call" | custom-call | tf_op jit(solution)/shard_map/pallas_call | solution.py:22
  65.5 1.5 %collective-permute-start.24 = (f32[264,512]{1,0:T(8,128)S(1)}, f32[264,512]{1,0:T(8,128)S(1)}, u32[]{:S(2)}, u32[]{:S(2)}) collective-permute-start(f32[264,512]{1,0:T(8,128)S(1)} %shard_map.68.refs_6_), channel_id=1, source_target_pairs={{0,2},{1,3},{2,0},{3,1},{4,6},{5,7},{6,4},{7,5},{8,10},{9,11},{10,... | collective-permute-start | bytes 1622024 | tf_op jit(solution)/shard_map/ppermute | solution.py:279
  67.0 1.4 %collective-permute-start.25 = (f32[256,512]{1,0:T(8,128)S(1)}, f32[256,512]{1,0:T(8,128)S(1)}, u32[]{:S(2)}, u32[]{:S(2)}) collective-permute-start(f32[256,512]{1,0:T(8,128)S(1)} %shard_map.67.refs_6_.one_ref), channel_id=1, source_target_pairs={{0,16},{8,24},{16,0},{24,8},{1,17},{9,25},{17,1},{25,9},{2,18},{10... | collective-permute-start | bytes 1572872 | tf_op jit(solution)/shard_map/ppermute | solution.py:279
  68.4 0.9 %shard_map.69.refs_0_.refs_1_ = f32[264,512]{1,0:T(8,128)S(1)} custom-call(f32[512,2048]{1,0:T(8,128)S(1)} %get-tuple-element.30.refs_0_, bf16[2048,512]{1,0:T(8,128)(2,1)S(1)} %get-tuple-element.31.refs_1_, f32[4,128]{1,0:T(4,128)S(1)} %get-tuple-element.36.refs_2_, f32[4,128]{1,0:T(4,128)S(1)} %collective-permute-done.20.refs_3_, ...), custom_call_target="tpu_custom_call" | custom-call | tf_op jit(solution)/shard_map/pallas_call | solution.py:22
  69.3 10.0 %collective-permute-done.25.two_ref = f32[256,512]{1,0:T(8,128)S(1)} collective-permute-done((f32[256,512]{1,0:T(8,128)S(1)}, f32[256,512]{1,0:T(8,128)S(1)}, u32[]{:S(2)}, u32[]{:S(2)}) %collective-permute-start.25) | collective-permute-done | bytes 524320 | tf_op jit(solution)/shard_map/ppermute | solution.py:279
  79.2 0.1 shard_map.71.mine_ref
  79.3 0.1 collective-permute-start.26
  79.4 1.1 %shard_map.70 = f32[256,512]{1,0:T(8,128)} custom-call(f32[264,512]{1,0:T(8,128)S(1)} %shard_map.69.refs_0_.refs_1_, f32[264,512]{1,0:T(8,128)S(1)} %collective-permute-done.24.refs_1_.refs_0_), custom_call_target="tpu_custom_call" | custom-call | tf_op jit(solution)/shard_map/pallas_call | solution.py:22
  80.5 0.8 collective-permute-done.26.other_ref
  81.3 1.0 %shard_map.72 = f32[512,512]{1,0:T(8,128)} custom-call(f32[256,512]{1,0:T(8,128)S(1)} %shard_map.71.mine_ref, f32[256,512]{1,0:T(8,128)S(1)} %collective-permute-done.26.other_ref), custom_call_target="tpu_custom_call" | custom-call | tf_op jit(solution)/shard_map/pallas_call | solution.py:22
  (18 shorter events, 0.1 us)
Async XLA Ops:
  0.6 1.0 %copy-start.2 = (bf16[512,512]{1,0:T(8,128)(2,1)S(1)}, bf16[512,512]{1,0:T(8,128)(2,1)}, u32[]{:S(2)}) copy-start(bf16[512,512]{1,0:T(8,128)(2,1)} %refs_1_.1) | copy-start | bytes 1572868
  1.7 29.0 %copy-start.4 = (f32[2048]{0:T(1024)S(1)}, f32[2048]{0:T(1024)}, u32[]{:S(2)}) copy-start(f32[2048]{0:T(1024)} %param.6) | copy-start | bytes 24580
  1.7 13.9 %collective-permute-start.1 = (f32[128,512]{1,0:T(8,128)S(1)}, f32[128,512]{1,0:T(8,128)S(1)}, u32[]{:S(2)}, u32[]{:S(2)}) collective-permute-start(f32[128,512]{1,0:T(8,128)S(1)} %shard_map.60), channel_id=1, source_target_pairs={{0,1},{1,0},{2,3},{3,2},{4,5},{5,4},{6,7},{7,6},{8,9},{9,8},{10,11... | collective-permute-start | bytes 786440 | tf_op jit(solution)/shard_map/ppermute | solution.py:279
  4.7 14.3 %collective-permute-start.2 = (f32[128,512]{1,0:T(8,128)S(1)}, f32[128,512]{1,0:T(8,128)S(1)}, u32[]{:S(2)}, u32[]{:S(2)}) collective-permute-start(f32[128,512]{1,0:T(8,128)S(1)} %shard_map.60), channel_id=1, source_target_pairs={{0,4},{1,5},{2,6},{3,7},{4,0},{5,1},{6,2},{7,3},{8,12},{9,13},{10,... | collective-permute-start | bytes 786440 | tf_op jit(solution)/shard_map/ppermute | solution.py:279
  7.3 1.6 %copy-start = (bf16[2048,512]{1,0:T(8,128)(2,1)S(1)}, bf16[2048,512]{1,0:T(8,128)(2,1)}, u32[]{:S(2)}) copy-start(bf16[2048,512]{1,0:T(8,128)(2,1)} %x_ref.3) | copy-start | bytes 6291460
  8.9 0.7 copy-start.5
  11.9 3.7 %collective-permute-start = (f32[16,128]{1,0:T(8,128)S(1)}, f32[16,128]{1,0:T(8,128)S(1)}, u32[]{:S(2)}, u32[]{:S(2)}) collective-permute-start(f32[16,128]{1,0:T(8,128)S(1)} %get-tuple-element.22.one_ref), channel_id=1, source_target_pairs={{0,1},{1,0},{2,3},{3,2},{4,5},{5,4},{6,7},{7,6},{8,9},{9,8},{10,11... | collective-permute-start | bytes 24584 | tf_op jit(solution)/shard_map/ppermute | solution.py:279
  19.0 11.6 %collective-permute-start.6 = (f32[192,512]{1,0:T(8,128)S(1)}, f32[192,512]{1,0:T(8,128)S(1)}, u32[]{:S(2)}, u32[]{:S(2)}) collective-permute-start(f32[192,512]{1,0:T(8,128)S(1)} %get-tuple-element.24.refs_7_), channel_id=1, source_target_pairs={{0,16},{8,24},{16,0},{24,8},{1,17},{9,25},{17,1},{25,9},{2,18},{10... | collective-permute-start | bytes 1179656 | tf_op jit(solution)/shard_map/ppermute | solution.py:279
  20.6 13.0 %collective-permute-start.10 = (f32[128,512]{1,0:T(8,128)S(1)}, f32[128,512]{1,0:T(8,128)S(1)}, u32[]{:S(2)}, u32[]{:S(2)}) collective-permute-start(f32[128,512]{1,0:T(8,128)S(1)} %get-tuple-element.26.refs_7_), channel_id=1, source_target_pairs={{0,1},{1,0},{2,3},{3,2},{4,5},{5,4},{6,7},{7,6},{8,9},{9,8},{10,11... | collective-permute-start | bytes 786440 | tf_op jit(solution)/shard_map/ppermute | solution.py:279
  21.2 4.4 %collective-permute-start.3 = (f32[16,128]{1,0:T(8,128)S(1)}, f32[16,128]{1,0:T(8,128)S(1)}, u32[]{:S(2)}, u32[]{:S(2)}) collective-permute-start(f32[16,128]{1,0:T(8,128)S(1)} %get-tuple-element.23.refs_3_), channel_id=1, source_target_pairs={{0,2},{1,3},{2,0},{3,1},{4,6},{5,7},{6,4},{7,5},{8,10},{9,11},{10,... | collective-permute-start | bytes 24584 | tf_op jit(solution)/shard_map/ppermute | solution.py:279
  21.8 5.0 %collective-permute-start.4 = (f32[16,128]{1,0:T(8,128)S(1)}, f32[16,128]{1,0:T(8,128)S(1)}, u32[]{:S(2)}, u32[]{:S(2)}) collective-permute-start(f32[16,128]{1,0:T(8,128)S(1)} %get-tuple-element.23.refs_3_), channel_id=1, source_target_pairs={{0,4},{1,5},{2,6},{3,7},{4,0},{5,1},{6,2},{7,3},{8,12},{9,13},{10,... | collective-permute-start | bytes 24584 | tf_op jit(solution)/shard_map/ppermute | solution.py:279
  25.2 5.4 %collective-permute-start.5 = (f32[16,128]{1,0:T(8,128)S(1)}, f32[16,128]{1,0:T(8,128)S(1)}, u32[]{:S(2)}, u32[]{:S(2)}) collective-permute-start(f32[16,128]{1,0:T(8,128)S(1)} %get-tuple-element.23.refs_3_), channel_id=1, source_target_pairs={{0,6},{1,7},{2,4},{3,5},{4,2},{5,3},{6,0},{7,1},{8,14},{9,15},{10,... | collective-permute-start | bytes 24584 | tf_op jit(solution)/shard_map/ppermute | solution.py:279
  31.7 1.9 %collective-permute-start.7 = (f32[4,128]{1,0:T(4,128)S(1)}, f32[4,128]{1,0:T(4,128)S(1)}, u32[]{:S(2)}, u32[]{:S(2)}) collective-permute-start(f32[4,128]{1,0:T(4,128)S(1)} %get-tuple-element.25.refs_3_), channel_id=1, source_target_pairs={{0,8},{8,0},{16,24},{24,16},{1,9},{9,1},{17,25},{25,17},{2,10},{10... | collective-permute-start | bytes 6152 | tf_op jit(solution)/shard_map/ppermute | solution.py:279
  31.7 3.7 %collective-permute-start.8 = (f32[4,128]{1,0:T(4,128)S(1)}, f32[4,128]{1,0:T(4,128)S(1)}, u32[]{:S(2)}, u32[]{:S(2)}) collective-permute-start(f32[4,128]{1,0:T(4,128)S(1)} %get-tuple-element.25.refs_3_), channel_id=1, source_target_pairs={{0,16},{8,24},{16,0},{24,8},{1,17},{9,25},{17,1},{25,9},{2,18},{10... | collective-permute-start | bytes 6152 | tf_op jit(solution)/shard_map/ppermute | solution.py:279
  32.3 3.1 %collective-permute-start.9 = (f32[4,128]{1,0:T(4,128)S(1)}, f32[4,128]{1,0:T(4,128)S(1)}, u32[]{:S(2)}, u32[]{:S(2)}) collective-permute-start(f32[4,128]{1,0:T(4,128)S(1)} %get-tuple-element.25.refs_3_), channel_id=1, source_target_pairs={{0,24},{8,16},{16,8},{24,0},{1,25},{9,17},{17,9},{25,1},{2,26},{10... | collective-permute-start | bytes 6152 | tf_op jit(solution)/shard_map/ppermute | solution.py:279
  36.5 14.3 %collective-permute-start.15 = (f32[192,512]{1,0:T(8,128)S(1)}, f32[192,512]{1,0:T(8,128)S(1)}, u32[]{:S(2)}, u32[]{:S(2)}) collective-permute-start(f32[192,512]{1,0:T(8,128)S(1)} %get-tuple-element.28.refs_9_), channel_id=1, source_target_pairs={{0,16},{8,24},{16,0},{24,8},{1,17},{9,25},{17,1},{25,9},{2,18},{10... | collective-permute-start | bytes 1179656 | tf_op jit(solution)/shard_map/ppermute | solution.py:279
  38.0 3.7 %collective-permute-start.11 = (f32[16,128]{1,0:T(8,128)S(1)}, f32[16,128]{1,0:T(8,128)S(1)}, u32[]{:S(2)}, u32[]{:S(2)}) collective-permute-start(f32[16,128]{1,0:T(8,128)S(1)} %get-tuple-element.27), channel_id=1, source_target_pairs={{0,1},{1,0},{2,3},{3,2},{4,5},{5,4},{6,7},{7,6},{8,9},{9,8},{10,11... | collective-permute-start | bytes 24584 | tf_op jit(solution)/shard_map/ppermute | solution.py:279
  41.7 15.2 %copy-start.1 = (bf16[2048,512]{1,0:T(8,128)(2,1)S(1)}, bf16[2048,512]{1,0:T(8,128)(2,1)}, u32[]{:S(2)}) copy-start(bf16[2048,512]{1,0:T(8,128)(2,1)} %x_ref.3) | copy-start | bytes 6291460
  41.7 4.5 %collective-permute-start.12 = (f32[16,128]{1,0:T(8,128)S(1)}, f32[16,128]{1,0:T(8,128)S(1)}, u32[]{:S(2)}, u32[]{:S(2)}) collective-permute-start(f32[16,128]{1,0:T(8,128)S(1)} %multiply_add_fusion.refs_3_), channel_id=1, source_target_pairs={{0,2},{1,3},{2,0},{3,1},{4,6},{5,7},{6,4},{7,5},{8,10},{9,11},{10,... | collective-permute-start | bytes 24584 | tf_op jit(solution)/shard_map/ppermute | solution.py:279
  42.0 5.0 %collective-permute-start.13 = (f32[16,128]{1,0:T(8,128)S(1)}, f32[16,128]{1,0:T(8,128)S(1)}, u32[]{:S(2)}, u32[]{:S(2)}) collective-permute-start(f32[16,128]{1,0:T(8,128)S(1)} %multiply_add_fusion.refs_3_), channel_id=1, source_target_pairs={{0,4},{1,5},{2,6},{3,7},{4,0},{5,1},{6,2},{7,3},{8,12},{9,13},{10,... | collective-permute-start | bytes 24584 | tf_op jit(solution)/shard_map/ppermute | solution.py:279
  45.3 5.4 %collective-permute-start.14 = (f32[16,128]{1,0:T(8,128)S(1)}, f32[16,128]{1,0:T(8,128)S(1)}, u32[]{:S(2)}, u32[]{:S(2)}) collective-permute-start(f32[16,128]{1,0:T(8,128)S(1)} %multiply_add_fusion.refs_3_), channel_id=1, source_target_pairs={{0,6},{1,7},{2,4},{3,5},{4,2},{5,3},{6,0},{7,1},{8,14},{9,15},{10,... | collective-permute-start | bytes 24584 | tf_op jit(solution)/shard_map/ppermute | solution.py:279
  51.8 11.3 %collective-permute-start.16 = (f32[3,2,128,512]{3,2,1,0:T(8,128)S(1)}, f32[3,2,128,512]{3,2,1,0:T(8,128)S(1)}, u32[]{:S(2)}, u32[]{:S(2)}) collective-permute-start(f32[3,2,128,512]{3,2,1,0:T(8,128)S(1)} %get-tuple-element.29.refs_2_), channel_id=1, source_target_pairs={{0,8},{8,0},{16,24},{24,16},{1,9},{9,1},{17,25},{25,17},{2,10},{10... | collective-permute-start | bytes 4718600 | tf_op jit(solution)/shard_map/ppermute | solution.py:279
  51.9 3.4 %collective-permute-start.17 = (f32[4,128]{1,0:T(4,128)S(1)}, f32[4,128]{1,0:T(4,128)S(1)}, u32[]{:S(2)}, u32[]{:S(2)}) collective-permute-start(f32[4,128]{1,0:T(4,128)S(1)} %get-tuple-element.32), channel_id=1, source_target_pairs={{0,8},{8,0},{16,24},{24,16},{1,9},{9,1},{17,25},{25,17},{2,10},{10... | collective-permute-start | bytes 6152 | tf_op jit(solution)/shard_map/ppermute | solution.py:279
  52.4 3.6 %collective-permute-start.18 = (f32[4,128]{1,0:T(4,128)S(1)}, f32[4,128]{1,0:T(4,128)S(1)}, u32[]{:S(2)}, u32[]{:S(2)}) collective-permute-start(f32[4,128]{1,0:T(4,128)S(1)} %get-tuple-element.32), channel_id=1, source_target_pairs={{0,16},{8,24},{16,0},{24,8},{1,17},{9,25},{17,1},{25,9},{2,18},{10... | collective-permute-start | bytes 6152 | tf_op jit(solution)/shard_map/ppermute | solution.py:279
  53.9 3.0 %collective-permute-start.19 = (f32[4,128]{1,0:T(4,128)S(1)}, f32[4,128]{1,0:T(4,128)S(1)}, u32[]{:S(2)}, u32[]{:S(2)}) collective-permute-start(f32[4,128]{1,0:T(4,128)S(1)} %get-tuple-element.32), channel_id=1, source_target_pairs={{0,24},{8,16},{16,8},{24,0},{1,25},{9,17},{17,9},{25,1},{2,26},{10... | collective-permute-start | bytes 6152 | tf_op jit(solution)/shard_map/ppermute | solution.py:279
  56.9 6.2 %copy-start.3 = (bf16[512,512]{1,0:T(8,128)(2,1)S(1)}, bf16[512,512]{1,0:T(8,128)(2,1)}, u32[]{:S(2)}) copy-start(bf16[512,512]{1,0:T(8,128)(2,1)} %refs_1_.1) | copy-start | bytes 1572868
  58.5 4.5 %collective-permute-start.23 = (f32[256,512]{1,0:T(8,128)S(1)}, f32[256,512]{1,0:T(8,128)S(1)}, u32[]{:S(2)}, u32[]{:S(2)}) collective-permute-start(f32[256,512]{1,0:T(8,128)S(1)} %get-tuple-element.35), channel_id=1, source_target_pairs={{0,8},{8,0},{16,24},{24,16},{1,9},{9,1},{17,25},{25,17},{2,10},{10... | collective-permute-start | bytes 1572872 | tf_op jit(solution)/shard_map/ppermute | solution.py:279
  58.6 5.9 %collective-permute-start.20 = (f32[4,128]{1,0:T(4,128)S(1)}, f32[4,128]{1,0:T(4,128)S(1)}, u32[]{:S(2)}, u32[]{:S(2)}) collective-permute-start(f32[4,128]{1,0:T(4,128)S(1)} %get-tuple-element.36.refs_2_), channel_id=1, source_target_pairs={{0,1},{1,0},{2,3},{3,2},{4,5},{5,4},{6,7},{7,6},{8,9},{9,8},{10,11... | collective-permute-start | bytes 6152 | tf_op jit(solution)/shard_map/ppermute | solution.py:279
  59.2 5.3 %collective-permute-start.21 = (f32[4,128]{1,0:T(4,128)S(1)}, f32[4,128]{1,0:T(4,128)S(1)}, u32[]{:S(2)}, u32[]{:S(2)}) collective-permute-start(f32[4,128]{1,0:T(4,128)S(1)} %get-tuple-element.36.refs_2_), channel_id=1, source_target_pairs={{0,4},{1,5},{2,6},{3,7},{4,0},{5,1},{6,2},{7,3},{8,12},{9,13},{10,... | collective-permute-start | bytes 6152 | tf_op jit(solution)/shard_map/ppermute | solution.py:279
  59.2 5.4 %collective-permute-start.22 = (f32[4,128]{1,0:T(4,128)S(1)}, f32[4,128]{1,0:T(4,128)S(1)}, u32[]{:S(2)}, u32[]{:S(2)}) collective-permute-start(f32[4,128]{1,0:T(4,128)S(1)} %get-tuple-element.36.refs_2_), channel_id=1, source_target_pairs={{0,5},{1,4},{2,7},{3,6},{4,1},{5,0},{6,3},{7,2},{8,13},{9,12},{10,... | collective-permute-start | bytes 6152 | tf_op jit(solution)/shard_map/ppermute | solution.py:279
  65.5 13.7 %collective-permute-start.24 = (f32[264,512]{1,0:T(8,128)S(1)}, f32[264,512]{1,0:T(8,128)S(1)}, u32[]{:S(2)}, u32[]{:S(2)}) collective-permute-start(f32[264,512]{1,0:T(8,128)S(1)} %shard_map.68.refs_6_), channel_id=1, source_target_pairs={{0,2},{1,3},{2,0},{3,1},{4,6},{5,7},{6,4},{7,5},{8,10},{9,11},{10,... | collective-permute-start | bytes 1622024 | tf_op jit(solution)/shard_map/ppermute | solution.py:279
  67.0 12.2 %collective-permute-start.25 = (f32[256,512]{1,0:T(8,128)S(1)}, f32[256,512]{1,0:T(8,128)S(1)}, u32[]{:S(2)}, u32[]{:S(2)}) collective-permute-start(f32[256,512]{1,0:T(8,128)S(1)} %shard_map.67.refs_6_.one_ref), channel_id=1, source_target_pairs={{0,16},{8,24},{16,0},{24,8},{1,17},{9,25},{17,1},{25,9},{2,18},{10... | collective-permute-start | bytes 1572872 | tf_op jit(solution)/shard_map/ppermute | solution.py:279
  79.3 2.0 %collective-permute-start.26 = (f32[256,512]{1,0:T(8,128)S(1)}, f32[256,512]{1,0:T(8,128)S(1)}, u32[]{:S(2)}, u32[]{:S(2)}) collective-permute-start(f32[256,512]{1,0:T(8,128)S(1)} %shard_map.71.mine_ref), channel_id=1, source_target_pairs={{0,8},{8,0},{16,24},{24,16},{1,9},{9,1},{17,25},{25,17},{2,10},{10... | collective-permute-start | bytes 1572872 | tf_op jit(solution)/shard_map/ppermute | solution.py:279

commit v5 on v4

--- a/solution.py
+++ b/solution.py
@@ -123,10 +123,10 @@
     n_pieces = len(refs) // 2
     pieces, (out_ref, pack_ref, *copies) = refs[:n_pieces], refs[n_pieces:]
     out_ref[...] = merge_all([one_ref[...], two_ref[...]])
-    rows = pieces[0].shape[0]
-    pack_ref[:rows, :] = pieces[0][...]
-    pack_ref[rows:, :] = pieces[1][: rows // 2, :]
-    for piece, copy in zip(pieces[1:], copies):
+    rows = pieces[-1].shape[0]
+    pack_ref[:rows, :] = pieces[-1][...]
+    pack_ref[rows:, :] = pieces[0][: rows // 2, :]
+    for piece, copy in zip(pieces[:-1], copies):
         copy[...] = piece[...]
 
 
@@ -239,9 +239,9 @@
     n_tgt = y_ref.shape[0] // n_shards
     block = pl.ds(flip * rows, rows)
     peak = jnp.full((rows, 1), -jnp.inf, jnp.float32)
-    for k in range(n_shards):
+    for k, bias_ref in enumerate(bias_refs[::-1]):
         at = pl.ds(k * n_tgt, n_tgt)
-        scores = inner_ref[block, at] + to_row(bias_refs[k][...])
+        scores = inner_ref[block, at] + to_row(bias_ref[...])
         scores_ref[:, at] = scores
         peak = jnp.maximum(peak, jnp.max(scores, axis=1, keepdims=True))
     total = jnp.zeros((rows, 1), jnp.float32)
@@ -329,20 +329,21 @@
             lse, early, *copies = call(
                 merge_kernel,
                 (src_dense, f32(part.shape[0] * 3 // 2, width), *(part,) * len(far)),
-                lse, came, early, *[pieces[k] for k in far],
+                lse, came, *[pieces[k] for k in far], early,
             )
             early = along_y(early)
             pieces |= dict(zip(far, copies))
             for bit in bits_of(n_x)[::-1]:
                 pieces |= {k ^ bit: swap(piece, "col", bit) for k, piece in pieces.items() if k ^ bit != 1}
-        parts = [lse] + [swap(lse, "col", k * n_x) for k in range(1, n_z)]
+        parts = [merge_all([lse, swap(lse, "col", (n_z - 1) * n_x)])]
+        parts += [swap(lse, "col", k * n_x) for k in range(n_z - 2, 0, -1)]
         if step < ITERS - 1:
             src_bias, lse = call(
-                lambda *refs: sources_kernel(n_z, *refs), (src_dense, tgt_dense), tile, ls, sqx, *parts, *early
+                lambda *refs: sources_kernel(n_z - 1, *refs), (src_dense, tgt_dense), tile, ls, sqx, *parts, *early
             )
         else:
             src_bias, lse, came = call(
-                lambda *refs: last_sources_kernel(n_z, *refs),
+                lambda *refs: last_sources_kernel(n_z - 1, *refs),
                 (src_dense, tgt_dense, f32(len(apart) - 1, n_row // 2, *part.shape)),
                 tile, ls, sqx, *parts, *early, *late,
             )
@@ -371,7 +372,7 @@
         return call(
             lambda *refs: image_kernel(flip, *refs),
             f32(count + EXTRA, width),
-            inner, all_y, *biases, after,
+            inner, all_y, *biases[::-1], after,
             scratch=[pltpu.VMEM((count, n_all), jnp.float32)],
         )
 

time: 82.5 us -> 80.4 us (0.975)
  waiting for transfers between devices: 34.1 us -> 31.1 us
  starting transfers between devices: 31.6 us -> 32.5 us
    ppermute x27, waiting for transfers between devices: 34.1 us -> 31.1 us  [swap(): return lax.ppermute(value, axis, [(i, i ^ distance) for i in range(n)])]
    ppermute x27, starting transfers between devices: 31.6 us -> 32.5 us  [swap(): return lax.ppermute(value, axis, [(i, i ^ distance) for i in range(n)])]
  transfers between devices with their start and end apart: 27 -> 27, of which waited for: 14 -> 13; matrix products, arithmetic and copies ran while one was open for 0% -> 0% of each run, Pallas kernels for 10% -> 10%
where the time goes in v5:
time: 80.4 us; the launch traced here: 80.2 us
  starting transfers between devices  32.5 us (40%)
  waiting for transfers between devices  31.1 us (39%)
  Pallas kernels  12.4 us (15%)
  local copies, waits for them, and re-layouts  3.32 us (4%)
    ppermute x27, starting transfers between devices, swap(): return lax.ppermute(value, axis, [(i, i ^ distance) for i in range(n)])  32.5 us
    ppermute x27, waiting for transfers between devices, swap(): return lax.ppermute(value, axis, [(i, i ^ distance) for i in range(n)])  31.1 us
    pallas_call x14, Pallas kernels, call(): pl.pallas_call(kernel, out_shape=out_shape, in_specs=in_specs or [VMEM] *...  12.4 us
    unnamed x12, local copies, waits for them, and re-layouts  3.32 us
  transfers between devices with their start and end apart: 27, of which 13 were waited for; matrix products, arithmetic and copies ran while one was open for 0% of the time, Pallas kernels for 10%

profile of v5, /device:TPU:0, one launch (start us, length us, event | category | flops | bytes accessed | tf_op | source)
XLA Modules:
  0.0 80.2 jit_solution(8768378985432776959)
XLA Ops:
  0.6 0.0 copy-start.2
  0.6 1.0 %copy-done.2 = bf16[512,512]{1,0:T(8,128)(2,1)S(1)} copy-done((bf16[512,512]{1,0:T(8,128)(2,1)S(1)}, bf16[512,512]{1,0:T(8,128)(2,1)}, u32[]{:S(2)}) %copy-start.2) | copy-done | bytes 524312
  1.7 4.1 %collective-permute-start.1 = (f32[128,512]{1,0:T(8,128)S(1)}, f32[128,512]{1,0:T(8,128)S(1)}, u32[]{:S(2)}, u32[]{:S(2)}) collective-permute-start(f32[128,512]{1,0:T(8,128)S(1)} %shard_map.60), channel_id=1, source_target_pairs={{0,4},{1,5},{2,6},{3,7},{4,0},{5,1},{6,2},{7,3},{8,12},{9,13},{10,... | collective-permute-start | bytes 786440 | tf_op jit(solution)/shard_map/ppermute | solution.py:279
  5.8 1.5 %collective-permute-start.2 = (f32[128,512]{1,0:T(8,128)S(1)}, f32[128,512]{1,0:T(8,128)S(1)}, u32[]{:S(2)}, u32[]{:S(2)}) collective-permute-start(f32[128,512]{1,0:T(8,128)S(1)} %shard_map.60), channel_id=1, source_target_pairs={{0,1},{1,0},{2,3},{3,2},{4,5},{5,4},{6,7},{7,6},{8,9},{9,8},{10,11... | collective-permute-start | bytes 786440 | tf_op jit(solution)/shard_map/ppermute | solution.py:279
  7.3 1.6 %copy-done = bf16[2048,512]{1,0:T(8,128)(2,1)S(1)} copy-done((bf16[2048,512]{1,0:T(8,128)(2,1)S(1)}, bf16[2048,512]{1,0:T(8,128)(2,1)}, u32[]{:S(2)}) %copy-start) | copy-done | bytes 2097176
  8.9 0.7 copy-done.5
  9.6 2.3 %shard_map.59 = (f32[512,2048]{1,0:T(8,128)S(1)}, f32[16,128]{1,0:T(8,128)S(1)}, f32[16,128]{1,0:T(8,128)S(1)}, f32[4,128]{1,0:T(4,128)S(1)}) custom-call(bf16[512,512]{1,0:T(8,128)(2,1)S(1)} %copy-done.2, bf16[2048,512]{1,0:T(8,128)(2,1)S(1)} %copy-done, f32[4,128]{1,0:T(4,128)S(1)} %bitcast.5), custom_call_target="tpu_custom_call" | custom-call | tf_op jit(solution)/shard_map/pallas_call | solution.py:22
  11.9 0.6 collective-permute-start
  12.5 3.1 %collective-permute-done.two_ref = f32[16,128]{1,0:T(8,128)S(1)} collective-permute-done((f32[16,128]{1,0:T(8,128)S(1)}, f32[16,128]{1,0:T(8,128)S(1)}, u32[]{:S(2)}, u32[]{:S(2)}) %collective-permute-start) | collective-permute-done | bytes 8224 | tf_op jit(solution)/shard_map/ppermute | solution.py:279
  15.6 2.1 %collective-permute-done.1.refs_0_ = f32[128,512]{1,0:T(8,128)S(1)} collective-permute-done((f32[128,512]{1,0:T(8,128)S(1)}, f32[128,512]{1,0:T(8,128)S(1)}, u32[]{:S(2)}, u32[]{:S(2)}) %collective-permute-start.1) | collective-permute-done | bytes 262176 | tf_op jit(solution)/shard_map/ppermute | solution.py:279
  17.8 1.6 %collective-permute-start.6 = (f32[192,512]{1,0:T(8,128)S(1)}, f32[192,512]{1,0:T(8,128)S(1)}, u32[]{:S(2)}, u32[]{:S(2)}) collective-permute-start(f32[192,512]{1,0:T(8,128)S(1)} %get-tuple-element.24.refs_6_), channel_id=1, source_target_pairs={{0,16},{8,24},{16,0},{24,8},{1,17},{9,25},{17,1},{25,9},{2,18},{10... | collective-permute-start | bytes 1179656 | tf_op jit(solution)/shard_map/ppermute | solution.py:279
  19.4 1.5 %collective-permute-start.10 = (f32[128,512]{1,0:T(8,128)S(1)}, f32[128,512]{1,0:T(8,128)S(1)}, u32[]{:S(2)}, u32[]{:S(2)}) collective-permute-start(f32[128,512]{1,0:T(8,128)S(1)} %get-tuple-element.26.refs_7_), channel_id=1, source_target_pairs={{0,1},{1,0},{2,3},{3,2},{4,5},{5,4},{6,7},{7,6},{8,9},{9,8},{10,11... | collective-permute-start | bytes 786440 | tf_op jit(solution)/shard_map/ppermute | solution.py:279
  20.9 3.5 %collective-permute-start.3 = (f32[16,128]{1,0:T(8,128)S(1)}, f32[16,128]{1,0:T(8,128)S(1)}, u32[]{:S(2)}, u32[]{:S(2)}) collective-permute-start(f32[16,128]{1,0:T(8,128)S(1)} %get-tuple-element.23), channel_id=1, source_target_pairs={{0,6},{1,7},{2,4},{3,5},{4,2},{5,3},{6,0},{7,1},{8,14},{9,15},{10,... | collective-permute-start | bytes 24584 | tf_op jit(solution)/shard_map/ppermute | solution.py:279
  24.4 0.0 collective-permute-start.4
  24.4 0.9 %collective-permute-start.5 = (f32[16,128]{1,0:T(8,128)S(1)}, f32[16,128]{1,0:T(8,128)S(1)}, u32[]{:S(2)}, u32[]{:S(2)}) collective-permute-start(f32[16,128]{1,0:T(8,128)S(1)} %get-tuple-element.23), channel_id=1, source_target_pairs={{0,2},{1,3},{2,0},{3,1},{4,6},{5,7},{6,4},{7,5},{8,10},{9,11},{10,... | collective-permute-start | bytes 24584 | tf_op jit(solution)/shard_map/ppermute | solution.py:279
  25.3 1.1 %collective-permute-done.3 = f32[16,128]{1,0:T(8,128)S(1)} collective-permute-done((f32[16,128]{1,0:T(8,128)S(1)}, f32[16,128]{1,0:T(8,128)S(1)}, u32[]{:S(2)}, u32[]{:S(2)}) %collective-permute-start.3) | collective-permute-done | bytes 8224 | tf_op jit(solution)/shard_map/ppermute | solution.py:279
  26.4 2.6 %collective-permute-done.4.refs_4_ = f32[16,128]{1,0:T(8,128)S(1)} collective-permute-done((f32[16,128]{1,0:T(8,128)S(1)}, f32[16,128]{1,0:T(8,128)S(1)}, u32[]{:S(2)}, u32[]{:S(2)}) %collective-permute-start.4) | collective-permute-done | bytes 8224 | tf_op jit(solution)/shard_map/ppermute | solution.py:279
  28.9 0.0 collective-permute-done.5.refs_5_
  28.9 0.0 collective-permute-done.6.refs_7_
  29.0 1.0 %shard_map.62 = (f32[16,128]{1,0:T(8,128)}, f32[4,128]{1,0:T(4,128)S(1)}) custom-call(f32[512,2048]{1,0:T(8,128)S(1)} %get-tuple-element.19.refs_0_.tile_ref, f32[16,128]{1,0:T(8,128)S(1)} %bitcast.3, f32[16,128]{1,0:T(8,128)S(1)} %get-tuple-element.20.refs_2_, f32[16,128]{1,0:T(8,128)S(1)} %multiply_add_fusion.2.refs_3_, ...), custom_call_target="tpu_custom_call" | custom-call | tf_op jit(solution)/shard_map/pallas_call | solution.py:22
  30.0 0.0 collective-permute-start.7
  30.0 0.6 collective-permute-start.8
  30.6 1.3 %collective-permute-start.9 = (f32[4,128]{1,0:T(4,128)S(1)}, f32[4,128]{1,0:T(4,128)S(1)}, u32[]{:S(2)}, u32[]{:S(2)}) collective-permute-start(f32[4,128]{1,0:T(4,128)S(1)} %get-tuple-element.25.refs_3_), channel_id=1, source_target_pairs={{0,24},{8,16},{16,8},{24,0},{1,25},{9,17},{17,9},{25,1},{2,26},{10... | collective-permute-start | bytes 6152 | tf_op jit(solution)/shard_map/ppermute | solution.py:279
  31.9 0.0 collective-permute-done.7.refs_4_
  31.9 1.8 %collective-permute-done.8.refs_5_ = f32[4,128]{1,0:T(4,128)S(1)} collective-permute-done((f32[4,128]{1,0:T(4,128)S(1)}, f32[4,128]{1,0:T(4,128)S(1)}, u32[]{:S(2)}, u32[]{:S(2)}) %collective-permute-start.8) | collective-permute-done | bytes 2080 | tf_op jit(solution)/shard_map/ppermute | solution.py:279
  33.7 1.1 %shard_map.63 = (f32[16,128]{1,0:T(8,128)S(1)}, f32[192,512]{1,0:T(8,128)S(1)}) custom-call(f32[512,2048]{1,0:T(8,128)S(1)} %get-tuple-element.19.refs_0_.tile_ref, f32[4,128]{1,0:T(4,128)S(1)} %bitcast.6, f32[4,128]{1,0:T(4,128)S(1)} %get-tuple-element.21.refs_2_, f32[4,128]{1,0:T(4,128)S(1)} %get-tuple-element.25.refs_3_, ...), custom_call_target="tpu_custom_call" | custom-call | tf_op jit(solution)/shard_map/pallas_call | solution.py:22
  34.8 1.4 %collective-permute-start.11 = (f32[16,128]{1,0:T(8,128)S(1)}, f32[16,128]{1,0:T(8,128)S(1)}, u32[]{:S(2)}, u32[]{:S(2)}) collective-permute-start(f32[16,128]{1,0:T(8,128)S(1)} %get-tuple-element.27), channel_id=1, source_target_pairs={{0,1},{1,0},{2,3},{3,2},{4,5},{5,4},{6,7},{7,6},{8,9},{9,8},{10,11... | collective-permute-start | bytes 24584 | tf_op jit(solution)/shard_map/ppermute | solution.py:279
  36.2 0.6 collective-permute-start.15
  36.8 1.7 %collective-permute-done.11 = f32[16,128]{1,0:T(8,128)S(1)} collective-permute-done((f32[16,128]{1,0:T(8,128)S(1)}, f32[16,128]{1,0:T(8,128)S(1)}, u32[]{:S(2)}, u32[]{:S(2)}) %collective-permute-start.11) | collective-permute-done | bytes 8224 | tf_op jit(solution)/shard_map/ppermute | solution.py:279
  38.5 4.5 %collective-permute-start.12 = (f32[16,128]{1,0:T(8,128)S(1)}, f32[16,128]{1,0:T(8,128)S(1)}, u32[]{:S(2)}, u32[]{:S(2)}) collective-permute-start(f32[16,128]{1,0:T(8,128)S(1)} %multiply_add_fusion.1), channel_id=1, source_target_pairs={{0,6},{1,7},{2,4},{3,5},{4,2},{5,3},{6,0},{7,1},{8,14},{9,15},{10,... | collective-permute-start | bytes 24584 | tf_op jit(solution)/shard_map/ppermute | solution.py:279
  43.0 0.0 collective-permute-start.13
  43.0 0.6 collective-permute-start.14
  43.6 1.0 %collective-permute-done.12 = f32[16,128]{1,0:T(8,128)S(1)} collective-permute-done((f32[16,128]{1,0:T(8,128)S(1)}, f32[16,128]{1,0:T(8,128)S(1)}, u32[]{:S(2)}, u32[]{:S(2)}) %collective-permute-start.12) | collective-permute-done | bytes 8224 | tf_op jit(solution)/shard_map/ppermute | solution.py:279
  44.6 0.0 copy-start.1
  44.6 2.9 %collective-permute-done.13.refs_4_ = f32[16,128]{1,0:T(8,128)S(1)} collective-permute-done((f32[16,128]{1,0:T(8,128)S(1)}, f32[16,128]{1,0:T(8,128)S(1)}, u32[]{:S(2)}, u32[]{:S(2)}) %collective-permute-start.13) | collective-permute-done | bytes 8224 | tf_op jit(solution)/shard_map/ppermute | solution.py:279
  47.5 0.0 collective-permute-done.14.refs_5_
  47.5 0.0 collective-permute-done.15.refs_9_
  47.5 1.0 %shard_map.64 = (f32[16,128]{1,0:T(8,128)S(1)}, f32[4,128]{1,0:T(4,128)S(1)}, f32[3,2,128,512]{3,2,1,0:T(8,128)S(1)}) custom-call(f32[512,2048]{1,0:T(8,128)S(1)} %get-tuple-element.19.refs_0_.tile_ref, f32[16,128]{1,0:T(8,128)S(1)} %bitcast.4, f32[16,128]{1,0:T(8,128)S(1)} %get-tuple-element.20.refs_2_, f32[16,128]{1,0:T(8,128)S(1)} %multiply_add_fusion.refs_3_, ...), custom_call_target="tpu_custom_call" | custom-call | tf_op jit(solution)/shard_map/pallas_call | solution.py:22
  48.6 0.1 collective-permute-start.16
  48.7 0.5 collective-permute-start.17
  49.2 0.6 collective-permute-start.18
  49.7 0.9 %collective-permute-start.19 = (f32[4,128]{1,0:T(4,128)S(1)}, f32[4,128]{1,0:T(4,128)S(1)}, u32[]{:S(2)}, u32[]{:S(2)}) collective-permute-start(f32[4,128]{1,0:T(4,128)S(1)} %get-tuple-element.32), channel_id=1, source_target_pairs={{0,24},{8,16},{16,8},{24,0},{1,25},{9,17},{17,9},{25,1},{2,26},{10... | collective-permute-start | bytes 6152 | tf_op jit(solution)/shard_map/ppermute | solution.py:279
  50.6 1.5 %collective-permute-done.17 = f32[4,128]{1,0:T(4,128)S(1)} collective-permute-done((f32[4,128]{1,0:T(4,128)S(1)}, f32[4,128]{1,0:T(4,128)S(1)}, u32[]{:S(2)}, u32[]{:S(2)}) %collective-permute-start.17) | collective-permute-done | bytes 2080 | tf_op jit(solution)/shard_map/ppermute | solution.py:279
  52.1 0.7 collective-permute-done.18
  52.8 0.0 collective-permute-done.19
  52.8 0.0 copy-start.3
  52.8 1.6 %shard_map.66 = (f32[256,512]{1,0:T(8,128)S(1)}, f32[256,512]{1,0:T(8,128)S(1)}) custom-call(f32[512,2048]{1,0:T(8,128)S(1)} %get-tuple-element.19.refs_0_.tile_ref, bf16[2048,512]{1,0:T(8,128)(2,1)S(1)} %copy-done.1, f32[16,128]{1,0:T(8,128)S(1)} %get-tuple-element.33.bias_ref, f32[4,128]{1,0:T(4,128)S(1)} %get-tuple-element.37.total_ref), custom_call_target="tpu_custom_call" | custom-call | tf_op jit(solution)/shard_map/pallas_call | solution.py:22
  54.4 0.2 collective-permute-start.23
  54.6 3.0 %collective-permute-start.20 = (f32[4,128]{1,0:T(4,128)S(1)}, f32[4,128]{1,0:T(4,128)S(1)}, u32[]{:S(2)}, u32[]{:S(2)}) collective-permute-start(f32[4,128]{1,0:T(4,128)S(1)} %get-tuple-element.36.refs_5_), channel_id=1, source_target_pairs={{0,5},{1,4},{2,7},{3,6},{4,1},{5,0},{6,3},{7,2},{8,13},{9,12},{10,... | collective-permute-start | bytes 6152 | tf_op jit(solution)/shard_map/ppermute | solution.py:279
  57.6 0.9 %collective-permute-start.21 = (f32[4,128]{1,0:T(4,128)S(1)}, f32[4,128]{1,0:T(4,128)S(1)}, u32[]{:S(2)}, u32[]{:S(2)}) collective-permute-start(f32[4,128]{1,0:T(4,128)S(1)} %get-tuple-element.36.refs_5_), channel_id=1, source_target_pairs={{0,4},{1,5},{2,6},{3,7},{4,0},{5,1},{6,2},{7,3},{8,12},{9,13},{10,... | collective-permute-start | bytes 6152 | tf_op jit(solution)/shard_map/ppermute | solution.py:279
  58.4 0.5 collective-permute-start.22
  59.0 0.1 shard_map.67.refs_6_.one_ref
  59.1 1.3 %shard_map.65 = (bf16[2048,512]{1,0:T(8,128)(2,1)S(1)}, f32[512,2048]{1,0:T(8,128)S(1)}) custom-call(bf16[2048,512]{1,0:T(8,128)(2,1)S(1)} %copy-done.1, bf16[512,512]{1,0:T(8,128)(2,1)S(1)} %copy-done.3, f32[3,2,128,512]{3,2,1,0:T(8,128)S(1)} %get-tuple-element.29.refs_2_, f32[3,2,128,512]{3,2,1,0:T(8,128)S(1)} %collective-permute-done.16.refs_3_), custom_call_target="tpu_custom_call" | custom-call | tf_op jit(solution)/shard_map/pallas_call | solution.py:22
  60.4 1.7 %collective-permute-done.21.refs_3_ = f32[4,128]{1,0:T(4,128)S(1)} collective-permute-done((f32[4,128]{1,0:T(4,128)S(1)}, f32[4,128]{1,0:T(4,128)S(1)}, u32[]{:S(2)}, u32[]{:S(2)}) %collective-permute-start.21) | collective-permute-done | bytes 2080 | tf_op jit(solution)/shard_map/ppermute | solution.py:279
  62.1 0.9 %shard_map.68.refs_6_ = f32[264,512]{1,0:T(8,128)S(1)} custom-call(f32[512,2048]{1,0:T(8,128)S(1)} %get-tuple-element.30.refs_0_, bf16[2048,512]{1,0:T(8,128)(2,1)S(1)} %get-tuple-element.31.refs_1_, f32[4,128]{1,0:T(4,128)S(1)} %collective-permute-done.20.refs_2_, f32[4,128]{1,0:T(4,128)S(1)} %collective-permute-done.21.refs_3_, ...), custom_call_target="tpu_custom_call" | custom-call | tf_op jit(solution)/shard_map/pallas_call | solution.py:22
  62.9 1.7 %collective-permute-start.24 = (f32[264,512]{1,0:T(8,128)S(1)}, f32[264,512]{1,0:T(8,128)S(1)}, u32[]{:S(2)}, u32[]{:S(2)}) collective-permute-start(f32[264,512]{1,0:T(8,128)S(1)} %shard_map.68.refs_6_), channel_id=1, source_target_pairs={{0,2},{1,3},{2,0},{3,1},{4,6},{5,7},{6,4},{7,5},{8,10},{9,11},{10,... | collective-permute-start | bytes 1622024 | tf_op jit(solution)/shard_map/ppermute | solution.py:279
  64.7 1.4 %collective-permute-start.25 = (f32[256,512]{1,0:T(8,128)S(1)}, f32[256,512]{1,0:T(8,128)S(1)}, u32[]{:S(2)}, u32[]{:S(2)}) collective-permute-start(f32[256,512]{1,0:T(8,128)S(1)} %shard_map.67.refs_6_.one_ref), channel_id=1, source_target_pairs={{0,16},{8,24},{16,0},{24,8},{1,17},{9,25},{17,1},{25,9},{2,18},{10... | collective-permute-start | bytes 1572872 | tf_op jit(solution)/shard_map/ppermute | solution.py:279
  66.1 0.9 %shard_map.69.refs_0_.refs_1_ = f32[264,512]{1,0:T(8,128)S(1)} custom-call(f32[512,2048]{1,0:T(8,128)S(1)} %get-tuple-element.30.refs_0_, bf16[2048,512]{1,0:T(8,128)(2,1)S(1)} %get-tuple-element.31.refs_1_, f32[4,128]{1,0:T(4,128)S(1)} %collective-permute-done.20.refs_2_, f32[4,128]{1,0:T(4,128)S(1)} %collective-permute-done.21.refs_3_, ...), custom_call_target="tpu_custom_call" | custom-call | tf_op jit(solution)/shard_map/pallas_call | solution.py:22
  66.9 10.2 %collective-permute-done.25.two_ref = f32[256,512]{1,0:T(8,128)S(1)} collective-permute-done((f32[256,512]{1,0:T(8,128)S(1)}, f32[256,512]{1,0:T(8,128)S(1)}, u32[]{:S(2)}, u32[]{:S(2)}) %collective-permute-start.25) | collective-permute-done | bytes 524320 | tf_op jit(solution)/shard_map/ppermute | solution.py:279
  77.2 0.1 shard_map.71.mine_ref
  77.2 0.1 collective-permute-start.26
  77.3 1.1 %shard_map.70 = f32[256,512]{1,0:T(8,128)} custom-call(f32[264,512]{1,0:T(8,128)S(1)} %shard_map.69.refs_0_.refs_1_, f32[264,512]{1,0:T(8,128)S(1)} %collective-permute-done.24.refs_1_.refs_0_), custom_call_target="tpu_custom_call" | custom-call | tf_op jit(solution)/shard_map/pallas_call | solution.py:22
  78.4 0.8 %collective-permute-done.26.other_ref = f32[256,512]{1,0:T(8,128)S(1)} collective-permute-done((f32[256,512]{1,0:T(8,128)S(1)}, f32[256,512]{1,0:T(8,128)S(1)}, u32[]{:S(2)}, u32[]{:S(2)}) %collective-permute-start.26) | collective-permute-done | bytes 524320 | tf_op jit(solution)/shard_map/ppermute | solution.py:279
  79.2 1.0 %shard_map.72 = f32[512,512]{1,0:T(8,128)} custom-call(f32[256,512]{1,0:T(8,128)S(1)} %shard_map.71.mine_ref, f32[256,512]{1,0:T(8,128)S(1)} %collective-permute-done.26.other_ref), custom_call_target="tpu_custom_call" | custom-call | tf_op jit(solution)/shard_map/pallas_call | solution.py:22
  (20 shorter events, 0.2 us)
Async XLA Ops:
  0.6 1.0 %copy-start.2 = (bf16[512,512]{1,0:T(8,128)(2,1)S(1)}, bf16[512,512]{1,0:T(8,128)(2,1)}, u32[]{:S(2)}) copy-start(bf16[512,512]{1,0:T(8,128)(2,1)} %refs_1_.1) | copy-start | bytes 1572868
  1.7 27.3 %copy-start.4 = (f32[2048]{0:T(1024)S(1)}, f32[2048]{0:T(1024)}, u32[]{:S(2)}) copy-start(f32[2048]{0:T(1024)} %param.6) | copy-start | bytes 24580
  1.7 16.0 %collective-permute-start.1 = (f32[128,512]{1,0:T(8,128)S(1)}, f32[128,512]{1,0:T(8,128)S(1)}, u32[]{:S(2)}, u32[]{:S(2)}) collective-permute-start(f32[128,512]{1,0:T(8,128)S(1)} %shard_map.60), channel_id=1, source_target_pairs={{0,4},{1,5},{2,6},{3,7},{4,0},{5,1},{6,2},{7,3},{8,12},{9,13},{10,... | collective-permute-start | bytes 786440 | tf_op jit(solution)/shard_map/ppermute | solution.py:279
  5.8 11.9 %collective-permute-start.2 = (f32[128,512]{1,0:T(8,128)S(1)}, f32[128,512]{1,0:T(8,128)S(1)}, u32[]{:S(2)}, u32[]{:S(2)}) collective-permute-start(f32[128,512]{1,0:T(8,128)S(1)} %shard_map.60), channel_id=1, source_target_pairs={{0,1},{1,0},{2,3},{3,2},{4,5},{5,4},{6,7},{7,6},{8,9},{9,8},{10,11... | collective-permute-start | bytes 786440 | tf_op jit(solution)/shard_map/ppermute | solution.py:279
  7.3 1.6 %copy-start = (bf16[2048,512]{1,0:T(8,128)(2,1)S(1)}, bf16[2048,512]{1,0:T(8,128)(2,1)}, u32[]{:S(2)}) copy-start(bf16[2048,512]{1,0:T(8,128)(2,1)} %x_ref.3) | copy-start | bytes 6291460
  8.9 0.7 copy-start.5
  11.9 3.7 %collective-permute-start = (f32[16,128]{1,0:T(8,128)S(1)}, f32[16,128]{1,0:T(8,128)S(1)}, u32[]{:S(2)}, u32[]{:S(2)}) collective-permute-start(f32[16,128]{1,0:T(8,128)S(1)} %get-tuple-element.22.one_ref), channel_id=1, source_target_pairs={{0,1},{1,0},{2,3},{3,2},{4,5},{5,4},{6,7},{7,6},{8,9},{9,8},{10,11... | collective-permute-start | bytes 24584 | tf_op jit(solution)/shard_map/ppermute | solution.py:279
  17.8 11.2 %collective-permute-start.6 = (f32[192,512]{1,0:T(8,128)S(1)}, f32[192,512]{1,0:T(8,128)S(1)}, u32[]{:S(2)}, u32[]{:S(2)}) collective-permute-start(f32[192,512]{1,0:T(8,128)S(1)} %get-tuple-element.24.refs_6_), channel_id=1, source_target_pairs={{0,16},{8,24},{16,0},{24,8},{1,17},{9,25},{17,1},{25,9},{2,18},{10... | collective-permute-start | bytes 1179656 | tf_op jit(solution)/shard_map/ppermute | solution.py:279
  19.4 12.5 %collective-permute-start.10 = (f32[128,512]{1,0:T(8,128)S(1)}, f32[128,512]{1,0:T(8,128)S(1)}, u32[]{:S(2)}, u32[]{:S(2)}) collective-permute-start(f32[128,512]{1,0:T(8,128)S(1)} %get-tuple-element.26.refs_7_), channel_id=1, source_target_pairs={{0,1},{1,0},{2,3},{3,2},{4,5},{5,4},{6,7},{7,6},{8,9},{9,8},{10,11... | collective-permute-start | bytes 786440 | tf_op jit(solution)/shard_map/ppermute | solution.py:279
  20.9 5.4 %collective-permute-start.3 = (f32[16,128]{1,0:T(8,128)S(1)}, f32[16,128]{1,0:T(8,128)S(1)}, u32[]{:S(2)}, u32[]{:S(2)}) collective-permute-start(f32[16,128]{1,0:T(8,128)S(1)} %get-tuple-element.23), channel_id=1, source_target_pairs={{0,6},{1,7},{2,4},{3,5},{4,2},{5,3},{6,0},{7,1},{8,14},{9,15},{10,... | collective-permute-start | bytes 24584 | tf_op jit(solution)/shard_map/ppermute | solution.py:279
  24.4 4.5 %collective-permute-start.4 = (f32[16,128]{1,0:T(8,128)S(1)}, f32[16,128]{1,0:T(8,128)S(1)}, u32[]{:S(2)}, u32[]{:S(2)}) collective-permute-start(f32[16,128]{1,0:T(8,128)S(1)} %get-tuple-element.23), channel_id=1, source_target_pairs={{0,4},{1,5},{2,6},{3,7},{4,0},{5,1},{6,2},{7,3},{8,12},{9,13},{10,... | collective-permute-start | bytes 24584 | tf_op jit(solution)/shard_map/ppermute | solution.py:279
  24.4 4.5 %collective-permute-start.5 = (f32[16,128]{1,0:T(8,128)S(1)}, f32[16,128]{1,0:T(8,128)S(1)}, u32[]{:S(2)}, u32[]{:S(2)}) collective-permute-start(f32[16,128]{1,0:T(8,128)S(1)} %get-tuple-element.23), channel_id=1, source_target_pairs={{0,2},{1,3},{2,0},{3,1},{4,6},{5,7},{6,4},{7,5},{8,10},{9,11},{10,... | collective-permute-start | bytes 24584 | tf_op jit(solution)/shard_map/ppermute | solution.py:279
  30.0 1.9 %collective-permute-start.7 = (f32[4,128]{1,0:T(4,128)S(1)}, f32[4,128]{1,0:T(4,128)S(1)}, u32[]{:S(2)}, u32[]{:S(2)}) collective-permute-start(f32[4,128]{1,0:T(4,128)S(1)} %get-tuple-element.25.refs_3_), channel_id=1, source_target_pairs={{0,8},{8,0},{16,24},{24,16},{1,9},{9,1},{17,25},{25,17},{2,10},{10... | collective-permute-start | bytes 6152 | tf_op jit(solution)/shard_map/ppermute | solution.py:279
  30.0 3.7 %collective-permute-start.8 = (f32[4,128]{1,0:T(4,128)S(1)}, f32[4,128]{1,0:T(4,128)S(1)}, u32[]{:S(2)}, u32[]{:S(2)}) collective-permute-start(f32[4,128]{1,0:T(4,128)S(1)} %get-tuple-element.25.refs_3_), channel_id=1, source_target_pairs={{0,16},{8,24},{16,0},{24,8},{1,17},{9,25},{17,1},{25,9},{2,18},{10... | collective-permute-start | bytes 6152 | tf_op jit(solution)/shard_map/ppermute | solution.py:279
  30.6 3.1 %collective-permute-start.9 = (f32[4,128]{1,0:T(4,128)S(1)}, f32[4,128]{1,0:T(4,128)S(1)}, u32[]{:S(2)}, u32[]{:S(2)}) collective-permute-start(f32[4,128]{1,0:T(4,128)S(1)} %get-tuple-element.25.refs_3_), channel_id=1, source_target_pairs={{0,24},{8,16},{16,8},{24,0},{1,25},{9,17},{17,9},{25,1},{2,26},{10... | collective-permute-start | bytes 6152 | tf_op jit(solution)/shard_map/ppermute | solution.py:279
  34.8 3.7 %collective-permute-start.11 = (f32[16,128]{1,0:T(8,128)S(1)}, f32[16,128]{1,0:T(8,128)S(1)}, u32[]{:S(2)}, u32[]{:S(2)}) collective-permute-start(f32[16,128]{1,0:T(8,128)S(1)} %get-tuple-element.27), channel_id=1, source_target_pairs={{0,1},{1,0},{2,3},{3,2},{4,5},{5,4},{6,7},{7,6},{8,9},{9,8},{10,11... | collective-permute-start | bytes 24584 | tf_op jit(solution)/shard_map/ppermute | solution.py:279
  36.2 11.3 %collective-permute-start.15 = (f32[192,512]{1,0:T(8,128)S(1)}, f32[192,512]{1,0:T(8,128)S(1)}, u32[]{:S(2)}, u32[]{:S(2)}) collective-permute-start(f32[192,512]{1,0:T(8,128)S(1)} %get-tuple-element.28.refs_8_), channel_id=1, source_target_pairs={{0,16},{8,24},{16,0},{24,8},{1,17},{9,25},{17,1},{25,9},{2,18},{10... | collective-permute-start | bytes 1179656 | tf_op jit(solution)/shard_map/ppermute | solution.py:279
  38.5 6.1 %collective-permute-start.12 = (f32[16,128]{1,0:T(8,128)S(1)}, f32[16,128]{1,0:T(8,128)S(1)}, u32[]{:S(2)}, u32[]{:S(2)}) collective-permute-start(f32[16,128]{1,0:T(8,128)S(1)} %multiply_add_fusion.1), channel_id=1, source_target_pairs={{0,6},{1,7},{2,4},{3,5},{4,2},{5,3},{6,0},{7,1},{8,14},{9,15},{10,... | collective-permute-start | bytes 24584 | tf_op jit(solution)/shard_map/ppermute | solution.py:279
  43.0 4.5 %collective-permute-start.13 = (f32[16,128]{1,0:T(8,128)S(1)}, f32[16,128]{1,0:T(8,128)S(1)}, u32[]{:S(2)}, u32[]{:S(2)}) collective-permute-start(f32[16,128]{1,0:T(8,128)S(1)} %multiply_add_fusion.1), channel_id=1, source_target_pairs={{0,4},{1,5},{2,6},{3,7},{4,0},{5,1},{6,2},{7,3},{8,12},{9,13},{10,... | collective-permute-start | bytes 24584 | tf_op jit(solution)/shard_map/ppermute | solution.py:279
  43.0 4.5 %collective-permute-start.14 = (f32[16,128]{1,0:T(8,128)S(1)}, f32[16,128]{1,0:T(8,128)S(1)}, u32[]{:S(2)}, u32[]{:S(2)}) collective-permute-start(f32[16,128]{1,0:T(8,128)S(1)} %multiply_add_fusion.1), channel_id=1, source_target_pairs={{0,2},{1,3},{2,0},{3,1},{4,6},{5,7},{6,4},{7,5},{8,10},{9,11},{10,... | collective-permute-start | bytes 24584 | tf_op jit(solution)/shard_map/ppermute | solution.py:279
  44.6 8.2 %copy-start.1 = (bf16[2048,512]{1,0:T(8,128)(2,1)S(1)}, bf16[2048,512]{1,0:T(8,128)(2,1)}, u32[]{:S(2)}) copy-start(bf16[2048,512]{1,0:T(8,128)(2,1)} %x_ref.3) | copy-start | bytes 6291460
  48.6 10.5 %collective-permute-start.16 = (f32[3,2,128,512]{3,2,1,0:T(8,128)S(1)}, f32[3,2,128,512]{3,2,1,0:T(8,128)S(1)}, u32[]{:S(2)}, u32[]{:S(2)}) collective-permute-start(f32[3,2,128,512]{3,2,1,0:T(8,128)S(1)} %get-tuple-element.29.refs_2_), channel_id=1, source_target_pairs={{0,8},{8,0},{16,24},{24,16},{1,9},{9,1},{17,25},{25,17},{2,10},{10... | collective-permute-start | bytes 4718600 | tf_op jit(solution)/shard_map/ppermute | solution.py:279
  48.7 3.4 %collective-permute-start.17 = (f32[4,128]{1,0:T(4,128)S(1)}, f32[4,128]{1,0:T(4,128)S(1)}, u32[]{:S(2)}, u32[]{:S(2)}) collective-permute-start(f32[4,128]{1,0:T(4,128)S(1)} %get-tuple-element.32), channel_id=1, source_target_pairs={{0,8},{8,0},{16,24},{24,16},{1,9},{9,1},{17,25},{25,17},{2,10},{10... | collective-permute-start | bytes 6152 | tf_op jit(solution)/shard_map/ppermute | solution.py:279
  49.2 3.6 %collective-permute-start.18 = (f32[4,128]{1,0:T(4,128)S(1)}, f32[4,128]{1,0:T(4,128)S(1)}, u32[]{:S(2)}, u32[]{:S(2)}) collective-permute-start(f32[4,128]{1,0:T(4,128)S(1)} %get-tuple-element.32), channel_id=1, source_target_pairs={{0,16},{8,24},{16,0},{24,8},{1,17},{9,25},{17,1},{25,9},{2,18},{10... | collective-permute-start | bytes 6152 | tf_op jit(solution)/shard_map/ppermute | solution.py:279
  49.7 3.0 %collective-permute-start.19 = (f32[4,128]{1,0:T(4,128)S(1)}, f32[4,128]{1,0:T(4,128)S(1)}, u32[]{:S(2)}, u32[]{:S(2)}) collective-permute-start(f32[4,128]{1,0:T(4,128)S(1)} %get-tuple-element.32), channel_id=1, source_target_pairs={{0,24},{8,16},{16,8},{24,0},{1,25},{9,17},{17,9},{25,1},{2,26},{10... | collective-permute-start | bytes 6152 | tf_op jit(solution)/shard_map/ppermute | solution.py:279
  52.8 6.2 %copy-start.3 = (bf16[512,512]{1,0:T(8,128)(2,1)S(1)}, bf16[512,512]{1,0:T(8,128)(2,1)}, u32[]{:S(2)}) copy-start(bf16[512,512]{1,0:T(8,128)(2,1)} %refs_1_.1) | copy-start | bytes 1572868
  54.4 4.6 %collective-permute-start.23 = (f32[256,512]{1,0:T(8,128)S(1)}, f32[256,512]{1,0:T(8,128)S(1)}, u32[]{:S(2)}, u32[]{:S(2)}) collective-permute-start(f32[256,512]{1,0:T(8,128)S(1)} %get-tuple-element.35), channel_id=1, source_target_pairs={{0,8},{8,0},{16,24},{24,16},{1,9},{9,1},{17,25},{25,17},{2,10},{10... | collective-permute-start | bytes 1572872 | tf_op jit(solution)/shard_map/ppermute | solution.py:279
  54.6 5.8 %collective-permute-start.20 = (f32[4,128]{1,0:T(4,128)S(1)}, f32[4,128]{1,0:T(4,128)S(1)}, u32[]{:S(2)}, u32[]{:S(2)}) collective-permute-start(f32[4,128]{1,0:T(4,128)S(1)} %get-tuple-element.36.refs_5_), channel_id=1, source_target_pairs={{0,5},{1,4},{2,7},{3,6},{4,1},{5,0},{6,3},{7,2},{8,13},{9,12},{10,... | collective-permute-start | bytes 6152 | tf_op jit(solution)/shard_map/ppermute | solution.py:279
  57.6 4.5 %collective-permute-start.21 = (f32[4,128]{1,0:T(4,128)S(1)}, f32[4,128]{1,0:T(4,128)S(1)}, u32[]{:S(2)}, u32[]{:S(2)}) collective-permute-start(f32[4,128]{1,0:T(4,128)S(1)} %get-tuple-element.36.refs_5_), channel_id=1, source_target_pairs={{0,4},{1,5},{2,6},{3,7},{4,0},{5,1},{6,2},{7,3},{8,12},{9,13},{10,... | collective-permute-start | bytes 6152 | tf_op jit(solution)/shard_map/ppermute | solution.py:279
  58.4 3.6 %collective-permute-start.22 = (f32[4,128]{1,0:T(4,128)S(1)}, f32[4,128]{1,0:T(4,128)S(1)}, u32[]{:S(2)}, u32[]{:S(2)}) collective-permute-start(f32[4,128]{1,0:T(4,128)S(1)} %get-tuple-element.36.refs_5_), channel_id=1, source_target_pairs={{0,1},{1,0},{2,3},{3,2},{4,5},{5,4},{6,7},{7,6},{8,9},{9,8},{10,11... | collective-permute-start | bytes 6152 | tf_op jit(solution)/shard_map/ppermute | solution.py:279
  62.9 14.2 %collective-permute-start.24 = (f32[264,512]{1,0:T(8,128)S(1)}, f32[264,512]{1,0:T(8,128)S(1)}, u32[]{:S(2)}, u32[]{:S(2)}) collective-permute-start(f32[264,512]{1,0:T(8,128)S(1)} %shard_map.68.refs_6_), channel_id=1, source_target_pairs={{0,2},{1,3},{2,0},{3,1},{4,6},{5,7},{6,4},{7,5},{8,10},{9,11},{10,... | collective-permute-start | bytes 1622024 | tf_op jit(solution)/shard_map/ppermute | solution.py:279
  64.7 12.5 %collective-permute-start.25 = (f32[256,512]{1,0:T(8,128)S(1)}, f32[256,512]{1,0:T(8,128)S(1)}, u32[]{:S(2)}, u32[]{:S(2)}) collective-permute-start(f32[256,512]{1,0:T(8,128)S(1)} %shard_map.67.refs_6_.one_ref), channel_id=1, source_target_pairs={{0,16},{8,24},{16,0},{24,8},{1,17},{9,25},{17,1},{25,9},{2,18},{10... | collective-permute-start | bytes 1572872 | tf_op jit(solution)/shard_map/ppermute | solution.py:279
  77.2 2.0 %collective-permute-start.26 = (f32[256,512]{1,0:T(8,128)S(1)}, f32[256,512]{1,0:T(8,128)S(1)}, u32[]{:S(2)}, u32[]{:S(2)}) collective-permute-start(f32[256,512]{1,0:T(8,128)S(1)} %shard_map.71.mine_ref), channel_id=1, source_target_pairs={{0,8},{8,0},{16,24},{24,16},{1,9},{9,1},{17,25},{25,17},{2,10},{10... | collective-permute-start | bytes 1572872 | tf_op jit(solution)/shard_map/ppermute | solution.py:279

commit v6 on v5

--- a/solution.py
+++ b/solution.py
@@ -107,12 +107,17 @@
     sqx_ref[...] = to_dense(columns)
 
 
+def early_rows(rows):
+    return rows // 4
+
+
 def targets_kernel(n_parts, tile_ref, lt_ref, sqy_ref, *refs):
-    parts, pieces, (lse_ref, pack_ref) = refs[:n_parts], refs[n_parts:-2], refs[-2:]
-    half = pieces[0].shape[0] // 2
-    pack_ref[:half, :] = pieces[0][half:, :]
-    for k, piece in enumerate(pieces[1:]):
-        pack_ref[pl.ds(half + 2 * half * k, 2 * half), :] = piece[...]
+    parts, pieces, (lse_ref, pack_ref) = refs[:n_parts], refs[n_parts:-3], refs[-2:]
+    rows = pieces[0].shape[0]
+    cut = early_rows(rows)
+    pack_ref[: rows - cut, :] = pieces[0][cut:, :]
+    for k, piece in enumerate(pieces[1:], 1):
+        pack_ref[pl.ds(rows * k - cut, rows), :] = piece[...]
     g_pot = sqy_ref[...] - merge_all([ref[...] for ref in parts])
     bias = to_column(lt_ref[...] * LOG2E + g_pot - sqy_ref[...])
     for b in range(tile_ref.shape[1] // LANES):
@@ -125,70 +130,77 @@
     out_ref[...] = merge_all([one_ref[...], two_ref[...]])
     rows = pieces[-1].shape[0]
     pack_ref[:rows, :] = pieces[-1][...]
-    pack_ref[rows:, :] = pieces[0][: rows // 2, :]
+    pack_ref[rows:, :] = pieces[0][: early_rows(rows), :]
     for piece, copy in zip(pieces[:-1], copies):
         copy[...] = piece[...]
 
 
 def sources_kernel(n_parts, tile_ref, ls_ref, sqx_ref, *refs):
-    sources_pass(tile_ref, ls_ref, sqx_ref, refs[:n_parts], *refs[-2:])
-
-
-def last_sources_kernel(n_parts, tile_ref, ls_ref, sqx_ref, *refs):
-    pieces, (bias_ref, lse_ref, pack_ref) = refs[n_parts:-3], refs[-3:]
+    bias = source_bias(ls_ref, sqx_ref, refs[:n_parts])
+    columns = []
+    for j in range(tile_ref.shape[0] // LANES):
+        peak, total, _ = over_sources(tile_ref, pl.ds(j * LANES, LANES), bias)
+        columns.append(peak + jnp.log2(total))
+    refs[-1][...] = to_dense(columns)
+
+
+def last_sources_kernel(n_parts, tile_ref, x_ref, ls_ref, sqx_ref, *refs):
+    pieces, (lse_ref, sent_ref, mine_ref, pack_ref) = refs[n_parts:-4], refs[-4:]
     n_shards, n_y, rows, _ = pack_ref.shape
     y = lax.axis_index("row") // 2
     early, late = pieces[:n_y], pieces[n_y:]
-    half = rows // 2
+    cut = early_rows(rows)
     for j in range(n_y):
         place = y ^ j
         pack_ref[0, place] = early[j][:rows, :]
-        pack_ref[1, place, :half, :] = early[j][rows:, :]
-        pack_ref[1, place, half:, :] = late[j][:half, :]
+        pack_ref[1, place, :cut, :] = early[j][rows:, :]
+        pack_ref[1, place, cut:, :] = late[j][: rows - cut, :]
         for k in range(2, n_shards):
-            pack_ref[k, place] = late[j][pl.ds(half + (k - 2) * rows, rows), :]
-    sources_pass(tile_ref, ls_ref, sqx_ref, refs[:n_parts], bias_ref, lse_ref)
-
-
-def sources_pass(tile_ref, ls_ref, sqx_ref, parts, bias_ref, lse_ref):
-    f_pot = sqx_ref[...] - merge_all([ref[...] for ref in parts])
-    bias = ls_ref[...] * LOG2E + f_pot - sqx_ref[...]
-    bias_ref[...] = bias
-    blocks = range(bias.shape[0])
-    columns = []
-    for j in range(tile_ref.shape[0] // LANES):
-        at = pl.ds(j * LANES, LANES)
-        scores = [tile_ref[at, pl.ds(b * LANES, LANES)] + bias[b : b + 1, :] for b in blocks]
-        top = scores[0]
-        for block in scores[1:]:
-            top = jnp.maximum(top, block)
-        peak = jnp.max(top, axis=1, keepdims=True)
-        total = jnp.sum(sum(jnp.exp2(block - peak) for block in scores), axis=1, keepdims=True)
-        columns.append(peak + jnp.log2(total))
-    lse_ref[...] = to_dense(columns)
-
-
-def means_kernel(tile_ref, x_ref, bias_ref, total_ref, sent_ref, mine_ref):
-    bias = bias_ref[...]
+            pack_ref[k, place] = late[j][pl.ds((k - 1) * rows - cut, rows), :]
+    bias = source_bias(ls_ref, sqx_ref, refs[:n_parts])
     x = x_ref[...]
-    half = mine_ref.shape[0]
-    n_rows = half // LANES
+    n_rows = mine_ref.shape[0] // LANES
     core = lax.axis_index("row") % 2
     for out_ref, place in ((sent_ref, 1 - core), (mine_ref, core)):
-        total = to_column(total_ref[pl.ds(place * n_rows, n_rows), :])
+        columns = []
         for j in range(n_rows):
-            at = pl.ds(pl.multiple_of(place * half + j * LANES, LANES), LANES)
-            norm = total[j * LANES : (j + 1) * LANES]
-            exps = [
-                jnp.exp2(tile_ref[at, pl.ds(b * LANES, LANES)] + bias[b : b + 1, :] - norm)
-                for b in range(bias.shape[0])
-            ]
+            at = pl.ds(pl.multiple_of((place * n_rows + j) * LANES, LANES), LANES)
+            peak, total, exps = over_sources(tile_ref, at, bias)
+            columns.append(peak + jnp.log2(total))
             weights = jnp.concatenate([block.astype(jnp.bfloat16) for block in exps], axis=1)
-            out_ref[pl.ds(j * LANES, LANES), :] = jnp.dot(weights, x, preferred_element_type=jnp.float32)
-
-
-def add_kernel(one_ref, two_ref, *refs):
-    refs[-1][...] = one_ref[...] + two_ref[...]
+            mean = jnp.dot(weights, x, preferred_element_type=jnp.float32)
+            out_ref[pl.ds(j * LANES, LANES), :] = mean * (1.0 / total)
+        lse_ref[pl.ds(place * n_rows, n_rows), :] = to_dense(columns)
+
+
+def source_bias(ls_ref, sqx_ref, parts):
+    f_pot = sqx_ref[...] - merge_all([ref[...] for ref in parts])
+    return ls_ref[...] * LOG2E + f_pot - sqx_ref[...]
+
+
+def over_sources(tile_ref, at, bias):
+    scores = [tile_ref[at, pl.ds(b * LANES, LANES)] + bias[b : b + 1, :] for b in range(bias.shape[0])]
+    top = scores[0]
+    for block in scores[1:]:
+        top = jnp.maximum(top, block)
+    peak = jnp.max(top, axis=1, keepdims=True)
+    exps = [jnp.exp2(block - peak) for block in scores]
+    return peak, jnp.sum(sum(exps), axis=1, keepdims=True), exps
+
+
+def share_kernel(mine_ref, came_ref, total_ref, lse_ref, came_lse_ref, out_ref):
+    half = mine_ref.shape[0] // LANES
+    at = pl.ds(lax.axis_index("row") % 2 * half, half)
+    total = total_ref[at, :]
+    share, came_share = to_column(jnp.exp2(lse_ref[at, :] - total)), to_column(jnp.exp2(came_lse_ref[at, :] - total))
+    out_ref[...] = mine_ref[...] * share + came_ref[...] * came_share
+
+
+def add_kernel(one_ref, two_ref, *out_refs):
+    rows = out_refs[0].shape[0]
+    for k, ref in enumerate(out_refs):
+        at = pl.ds(k * rows, rows)
+        ref[...] = one_ref[at, :] + two_ref[at, :]
 
 
 def join_kernel(*refs):
@@ -200,15 +212,19 @@
     out_ref[...] = sum(ref[:rows, :] * share for ref, share in zip(parts, shares))
 
 
-def place_kernel(mine_ref, other_ref, out_hbm, sems):
-    half = mine_ref.shape[0]
+def place_kernel(*refs):
+    n = (len(refs) - 2) // 2
+    mine, others, out_hbm, sems = refs[:n], refs[n : 2 * n], refs[-2], refs[-1]
+    rows = mine[0].shape[0]
     core = lax.axis_index("row") % 2
-    mine = pltpu.make_async_copy(mine_ref, out_hbm.at[pl.ds(core * half, half), :], sems.at[0])
-    other = pltpu.make_async_copy(other_ref, out_hbm.at[pl.ds((1 - core) * half, half), :], sems.at[1])
-    mine.start()
-    other.start()
-    mine.wait()
-    other.wait()
+    copies = []
+    for place, pieces in ((core, mine), (1 - core, others)):
+        for k, piece in enumerate(pieces):
+            at = pl.ds(pl.multiple_of((place * n + k) * rows, rows), rows)
+            copies.append(pltpu.make_async_copy(piece, out_hbm.at[at, :], sems.at[len(copies)]))
+            copies[-1].start()
+    for copy in copies:
+        copy.wait()
 
 
 def scores_kernel(near, x_ref, own_ref, mine_ref, other_ref, y_ref, inner_ref):
@@ -265,7 +281,7 @@
 
 
 def image_kernel(flip, inner_ref, y_ref, *refs):
-    bias_refs, (image_ref, scores_ref) = refs[:-3], refs[-2:]
+    bias_refs, (image_ref, scores_ref) = refs[:-2], refs[-2:]
     numer, total, peak = images(flip, inner_ref, y_ref, bias_refs, scores_ref)
     rows = numer.shape[0]
     lse = lanes_of(peak + jnp.log2(total))
@@ -311,41 +327,39 @@
     tile, lse, sqx, sqy = call(
         first_kernel, (f32(n_tgt, n_src), src_dense, src_dense, tgt_dense), target, source, lt
     )
+    cut = early_rows(part.shape[0])
     for step in range(ITERS):
         if step > 0:
             apart = [0, 1] + [k for k in pieces if k > 1]
             lse, late = call(
                 lambda *refs: targets_kernel(n_row, *refs),
-                (src_dense, f32((2 * len(apart) - 5) * part.shape[0] // 2, width)),
-                tile, lt, sqy, *parts, *[pieces[k] for k in apart[2:]],
+                (src_dense, f32((len(apart) - 2) * part.shape[0] - cut, width)),
+                tile, lt, sqy, *parts, *[pieces[k] for k in apart[2:]], early[-1],
             )
             late = along_y(late)
-        for distance in bits_of(n_x):
+        for distance in bits_of(n_col)[:-1]:
             came = swap(lse, "col", distance)
-            if step > 0 or distance > 1:
+            if step > 0 or distance != n_x:
                 lse = merge_all([lse, came])
                 continue
             far = [k for k in pieces if k > 0]
             lse, early, *copies = call(
                 merge_kernel,
-                (src_dense, f32(part.shape[0] * 3 // 2, width), *(part,) * len(far)),
+                (src_dense, f32(part.shape[0] + cut, width), *(part,) * len(far)),
                 lse, came, *[pieces[k] for k in far], early,
             )
             early = along_y(early)
             pieces |= dict(zip(far, copies))
             for bit in bits_of(n_x)[::-1]:
                 pieces |= {k ^ bit: swap(piece, "col", bit) for k, piece in pieces.items() if k ^ bit != 1}
-        parts = [merge_all([lse, swap(lse, "col", (n_z - 1) * n_x)])]
-        parts += [swap(lse, "col", k * n_x) for k in range(n_z - 2, 0, -1)]
+        parts = [lse, swap(lse, "col", n_col // 2)]
         if step < ITERS - 1:
-            src_bias, lse = call(
-                lambda *refs: sources_kernel(n_z - 1, *refs), (src_dense, tgt_dense), tile, ls, sqx, *parts, *early
-            )
+            lse = call(lambda *refs: sources_kernel(2, *refs), tgt_dense, tile, ls, sqx, *parts)
         else:
-            src_bias, lse, came = call(
-                lambda *refs: last_sources_kernel(n_z - 1, *refs),
-                (src_dense, tgt_dense, f32(len(apart) - 1, n_row // 2, *part.shape)),
-                tile, ls, sqx, *parts, *early, *late,
+            lse, sent, mine, came = call(
+                lambda *refs: last_sources_kernel(2, *refs),
+                (tgt_dense, f32(half, width), f32(half, width), f32(len(apart) - 1, n_row // 2, *part.shape)),
+                tile, source, ls, sqx, *parts, *early, *late,
             )
         parts = [lse] + [swap(lse, "row", k) for k in range(1, n_row)]
     total = merge_all(parts)
@@ -353,11 +367,10 @@
     bias = lt * LOG2E + (sqy - total) - sqy
     biases = [bias] + [swap(bias, "col", distance) for distance in apart[1:]]
 
-    sent, mine = call(means_kernel, (f32(half, width), f32(half, width)), tile, source, src_bias, total)
-    mine = call(add_kernel, f32(half, width), mine, swap(sent, "row", 1))
+    mine = call(share_kernel, f32(half, width), mine, swap(sent, "row", 1), total, lse, parts[1])
     rest = bits_of(n_row)[1:]
     for distance in rest[:-1]:
-        mine = call(add_kernel, f32(half, width), mine, swap(mine, "row", distance))
+        mine, = call(add_kernel, (f32(half, width),), mine, swap(mine, "row", distance))
     mine_came = swap(mine, "row", rest[-1])
 
     n_all = len(apart) * n_tgt
@@ -368,20 +381,21 @@
         limit=32,
     )
 
-    def image(flip, after):
+    def image(flip):
         return call(
             lambda *refs: image_kernel(flip, *refs),
             f32(count + EXTRA, width),
-            inner, all_y, *biases[::-1], after,
+            inner, all_y, *biases[::-1],
             scratch=[pltpu.VMEM((count, n_all), jnp.float32)],
         )
 
-    sent = image(1, mine)
-    came = swap(sent, "col", n_x)
-    own = image(0, sent)
-    mine = call(add_kernel, f32(half, width), mine, mine_came, came, own)
+    came = swap(image(1), "col", n_x)
+    own = image(0)
+    n_last = 4
+    mine = call(add_kernel, (f32(half // n_last, width),) * n_last, mine, mine_came)
     target_image = call(
-        place_kernel, f32(n_tgt, width), mine, swap(mine, "row", 1), out_specs=HBM, scratch=[DMA((2,))]
+        place_kernel, f32(n_tgt, width), *mine, *[swap(piece, "row", 1) for piece in mine],
+        out_specs=HBM, scratch=[DMA((2 * n_last,))],
     )
     source_image = call(join_kernel, f32(count, width), own, came)
     return source_image, target_image

time: 80.4 us -> 75.3 us (0.937)
  starting transfers between devices: 32.5 us -> 28.6 us
  waiting for transfers between devices: 31.1 us -> 30.2 us
    ppermute x27 -> x28, starting transfers between devices: 32.5 us -> 28.6 us  [swap(): return lax.ppermute(value, axis, [(i, i ^ distance) for i in range(n)])]
    ppermute x27 -> x28, waiting for transfers between devices: 31.1 us -> 30.2 us  [swap(): return lax.ppermute(value, axis, [(i, i ^ distance) for i in range(n)])]
    pallas_call x14 -> x13, Pallas kernels: 12.4 us -> 12.1 us  [call(): pl.pallas_call(kernel, out_shape=out_shape, in_specs=in_specs or [VMEM] *...]
    unnamed x12 -> x14, local copies, waits for them, and re-layouts: 3.32 us -> 3.33 us
  transfers between devices with their start and end apart: 27 -> 28, of which waited for: 13 -> 17; matrix products, arithmetic and copies ran while one was open for 0% -> 0% of each run, Pallas kernels for 10% -> 10%
where the time goes in v6:
time: 75.3 us; the launch traced here: 75.1 us
  waiting for transfers between devices  30.2 us (40%)
  starting transfers between devices  28.6 us (38%)
  Pallas kernels  12.1 us (16%)
  local copies, waits for them, and re-layouts  3.33 us (4%)
  between operations  0.8 us (1%)
    ppermute x28, waiting for transfers between devices, swap(): return lax.ppermute(value, axis, [(i, i ^ distance) for i in range(n)])  30.2 us
    ppermute x28, starting transfers between devices, swap(): return lax.ppermute(value, axis, [(i, i ^ distance) for i in range(n)])  28.6 us
    pallas_call x13, Pallas kernels, call(): pl.pallas_call(kernel, out_shape=out_shape, in_specs=in_specs or [VMEM] *...  12.1 us
    unnamed x14, local copies, waits for them, and re-layouts  3.33 us
  transfers between devices with their start and end apart: 28, of which 17 were waited for; matrix products, arithmetic and copies ran while one was open for 0% of the time, Pallas kernels for 10%

profile of v6, /device:TPU:0, one launch (start us, length us, event | category | flops | bytes accessed | tf_op | source)
XLA Modules:
  0.0 75.1 jit_solution(17923899087009398032)
XLA Ops:
  0.6 0.0 copy-start.2
  0.6 1.0 %copy-done.2 = bf16[512,512]{1,0:T(8,128)(2,1)S(1)} copy-done((bf16[512,512]{1,0:T(8,128)(2,1)S(1)}, bf16[512,512]{1,0:T(8,128)(2,1)}, u32[]{:S(2)}) %copy-start.2) | copy-done | bytes 524312
  1.7 4.1 %collective-permute-start.2 = (f32[128,512]{1,0:T(8,128)S(1)}, f32[128,512]{1,0:T(8,128)S(1)}, u32[]{:S(2)}, u32[]{:S(2)}) collective-permute-start(f32[128,512]{1,0:T(8,128)S(1)} %shard_map.60), channel_id=1, source_target_pairs={{0,4},{1,5},{2,6},{3,7},{4,0},{5,1},{6,2},{7,3},{8,12},{9,13},{10,... | collective-permute-start | bytes 786440 | tf_op jit(solution)/shard_map/ppermute | solution.py:295
  5.8 1.5 %collective-permute-start.3 = (f32[128,512]{1,0:T(8,128)S(1)}, f32[128,512]{1,0:T(8,128)S(1)}, u32[]{:S(2)}, u32[]{:S(2)}) collective-permute-start(f32[128,512]{1,0:T(8,128)S(1)} %shard_map.60), channel_id=1, source_target_pairs={{0,1},{1,0},{2,3},{3,2},{4,5},{5,4},{6,7},{7,6},{8,9},{9,8},{10,11... | collective-permute-start | bytes 786440 | tf_op jit(solution)/shard_map/ppermute | solution.py:295
  7.3 1.6 %copy-done = bf16[2048,512]{1,0:T(8,128)(2,1)S(1)} copy-done((bf16[2048,512]{1,0:T(8,128)(2,1)S(1)}, bf16[2048,512]{1,0:T(8,128)(2,1)}, u32[]{:S(2)}) %copy-start) | copy-done | bytes 2097176
  8.9 0.7 copy-done.5
  9.6 2.3 %shard_map.59 = (f32[512,2048]{1,0:T(8,128)S(1)}, f32[16,128]{1,0:T(8,128)S(1)}, f32[16,128]{1,0:T(8,128)S(1)}, f32[4,128]{1,0:T(4,128)S(1)}) custom-call(bf16[512,512]{1,0:T(8,128)(2,1)S(1)} %copy-done.2, bf16[2048,512]{1,0:T(8,128)(2,1)S(1)} %copy-done, f32[4,128]{1,0:T(4,128)S(1)} %bitcast.5), custom_call_target="tpu_custom_call" | custom-call | tf_op jit(solution)/shard_map/pallas_call | solution.py:22
  11.9 0.6 collective-permute-start
  12.5 3.1 %collective-permute-done = f32[16,128]{1,0:T(8,128)S(1)} collective-permute-done((f32[16,128]{1,0:T(8,128)S(1)}, f32[16,128]{1,0:T(8,128)S(1)}, u32[]{:S(2)}, u32[]{:S(2)}) %collective-permute-start) | collective-permute-done | bytes 8224 | tf_op jit(solution)/shard_map/ppermute | solution.py:295
  15.6 1.6 %collective-permute-start.1 = (f32[16,128]{1,0:T(8,128)S(1)}, f32[16,128]{1,0:T(8,128)S(1)}, u32[]{:S(2)}, u32[]{:S(2)}) collective-permute-start(f32[16,128]{1,0:T(8,128)S(1)} %multiply_add_fusion.2.one_ref), channel_id=1, source_target_pairs={{0,2},{1,3},{2,0},{3,1},{4,6},{5,7},{6,4},{7,5},{8,10},{9,11},{10,... | collective-permute-start | bytes 24584 | tf_op jit(solution)/shard_map/ppermute | solution.py:295
  17.3 2.1 %collective-permute-done.1.two_ref = f32[16,128]{1,0:T(8,128)S(1)} collective-permute-done((f32[16,128]{1,0:T(8,128)S(1)}, f32[16,128]{1,0:T(8,128)S(1)}, u32[]{:S(2)}, u32[]{:S(2)}) %collective-permute-start.1) | collective-permute-done | bytes 8224 | tf_op jit(solution)/shard_map/ppermute | solution.py:295
  19.3 0.0 collective-permute-done.2.refs_0_
  19.4 1.6 %collective-permute-start.9 = (f32[160,512]{1,0:T(8,128)S(1)}, f32[160,512]{1,0:T(8,128)S(1)}, u32[]{:S(2)}, u32[]{:S(2)}) collective-permute-start(f32[160,512]{1,0:T(8,128)S(1)} %get-tuple-element.27.refs_6_), channel_id=1, source_target_pairs={{0,16},{8,24},{16,0},{24,8},{1,17},{9,25},{17,1},{25,9},{2,18},{10... | collective-permute-start | bytes 983048 | tf_op jit(solution)/shard_map/ppermute | solution.py:295
  21.0 0.5 collective-permute-start.8
  21.5 0.3 collective-permute-start.4
  21.9 4.2 %collective-permute-done.4.refs_4_ = f32[16,128]{1,0:T(8,128)S(1)} collective-permute-done((f32[16,128]{1,0:T(8,128)S(1)}, f32[16,128]{1,0:T(8,128)S(1)}, u32[]{:S(2)}, u32[]{:S(2)}) %collective-permute-start.4) | collective-permute-done | bytes 8224 | tf_op jit(solution)/shard_map/ppermute | solution.py:295
  26.1 1.0 %shard_map.62.refs_3_ = f32[4,128]{1,0:T(4,128)S(1)} custom-call(f32[512,2048]{1,0:T(8,128)S(1)} %get-tuple-element.21.refs_0_, f32[16,128]{1,0:T(8,128)S(1)} %bitcast.3, f32[16,128]{1,0:T(8,128)S(1)} %get-tuple-element.22.refs_2_.refs_3_, f32[16,128]{1,0:T(8,128)S(1)} %get-tuple-element.25.refs_3_, f32[16,128]{1,0:T(8,128)S(1)} %collective-permute-done.4.refs_4_), custom_call_target="tpu_custom_call" | custom-call | tf_op jit(solution)/shard_map/pallas_call | solution.py:22
  27.1 0.0 collective-permute-start.5
  27.1 0.6 collective-permute-start.6
  27.7 1.3 %collective-permute-start.7 = (f32[4,128]{1,0:T(4,128)S(1)}, f32[4,128]{1,0:T(4,128)S(1)}, u32[]{:S(2)}, u32[]{:S(2)}) collective-permute-start(f32[4,128]{1,0:T(4,128)S(1)} %shard_map.62.refs_3_), channel_id=1, source_target_pairs={{0,24},{8,16},{16,8},{24,0},{1,25},{9,17},{17,9},{25,1},{2,26},{10... | collective-permute-start | bytes 6152 | tf_op jit(solution)/shard_map/ppermute | solution.py:295
  29.0 1.8 %collective-permute-done.6.refs_5_ = f32[4,128]{1,0:T(4,128)S(1)} collective-permute-done((f32[4,128]{1,0:T(4,128)S(1)}, f32[4,128]{1,0:T(4,128)S(1)}, u32[]{:S(2)}, u32[]{:S(2)}) %collective-permute-start.6) | collective-permute-done | bytes 2080 | tf_op jit(solution)/shard_map/ppermute | solution.py:295
  30.8 0.0 copy-start.1
  30.8 1.1 %shard_map.63 = (f32[16,128]{1,0:T(8,128)S(1)}, f32[224,512]{1,0:T(8,128)S(1)}) custom-call(f32[512,2048]{1,0:T(8,128)S(1)} %get-tuple-element.21.refs_0_, f32[4,128]{1,0:T(4,128)S(1)} %bitcast.6, f32[4,128]{1,0:T(4,128)S(1)} %get-tuple-element.23.refs_2_, f32[4,128]{1,0:T(4,128)S(1)} %shard_map.62.refs_3_, f32[4,128]{1,0:T(4,128)S(1)} %collective-permute-done.5.refs_4_, ...), custom_call_target="tpu_custom_call" | custom-call | tf_op jit(solution)/shard_map/pallas_call | solution.py:22
  31.9 1.6 %collective-permute-start.10 = (f32[16,128]{1,0:T(8,128)S(1)}, f32[16,128]{1,0:T(8,128)S(1)}, u32[]{:S(2)}, u32[]{:S(2)}) collective-permute-start(f32[16,128]{1,0:T(8,128)S(1)} %get-tuple-element.28), channel_id=1, source_target_pairs={{0,1},{1,0},{2,3},{3,2},{4,5},{5,4},{6,7},{7,6},{8,9},{9,8},{10,11... | collective-permute-start | bytes 24584 | tf_op jit(solution)/shard_map/ppermute | solution.py:295
  33.5 1.4 %collective-permute-start.13 = (f32[224,512]{1,0:T(8,128)S(1)}, f32[224,512]{1,0:T(8,128)S(1)}, u32[]{:S(2)}, u32[]{:S(2)}) collective-permute-start(f32[224,512]{1,0:T(8,128)S(1)} %get-tuple-element.29.refs_8_), channel_id=1, source_target_pairs={{0,16},{8,24},{16,0},{24,8},{1,17},{9,25},{17,1},{25,9},{2,18},{10... | collective-permute-start | bytes 1376264 | tf_op jit(solution)/shard_map/ppermute | solution.py:295
  34.9 0.7 collective-permute-done.10
  35.7 1.6 %collective-permute-start.11 = (f32[16,128]{1,0:T(8,128)S(1)}, f32[16,128]{1,0:T(8,128)S(1)}, u32[]{:S(2)}, u32[]{:S(2)}) collective-permute-start(f32[16,128]{1,0:T(8,128)S(1)} %multiply_add_fusion.1), channel_id=1, source_target_pairs={{0,2},{1,3},{2,0},{3,1},{4,6},{5,7},{6,4},{7,5},{8,10},{9,11},{10,... | collective-permute-start | bytes 24584 | tf_op jit(solution)/shard_map/ppermute | solution.py:295
  37.3 2.1 %collective-permute-done.11 = f32[16,128]{1,0:T(8,128)S(1)} collective-permute-done((f32[16,128]{1,0:T(8,128)S(1)}, f32[16,128]{1,0:T(8,128)S(1)}, u32[]{:S(2)}, u32[]{:S(2)}) %collective-permute-start.11) | collective-permute-done | bytes 8224 | tf_op jit(solution)/shard_map/ppermute | solution.py:295
  39.4 0.0 copy-start.6
  39.4 0.0 copy-start.3
  39.4 1.7 %collective-permute-start.12 = (f32[16,128]{1,0:T(8,128)S(1)}, f32[16,128]{1,0:T(8,128)S(1)}, u32[]{:S(2)}, u32[]{:S(2)}) collective-permute-start(f32[16,128]{1,0:T(8,128)S(1)} %multiply_add_fusion.refs_4_), channel_id=1, source_target_pairs={{0,4},{1,5},{2,6},{3,7},{4,0},{5,1},{6,2},{7,3},{8,12},{9,13},{10,... | collective-permute-start | bytes 24584 | tf_op jit(solution)/shard_map/ppermute | solution.py:295
  41.1 3.0 %collective-permute-done.12.refs_5_ = f32[16,128]{1,0:T(8,128)S(1)} collective-permute-done((f32[16,128]{1,0:T(8,128)S(1)}, f32[16,128]{1,0:T(8,128)S(1)}, u32[]{:S(2)}, u32[]{:S(2)}) %collective-permute-start.12) | collective-permute-done | bytes 8224 | tf_op jit(solution)/shard_map/ppermute | solution.py:295
  44.0 1.7 %collective-permute-done.13.refs_9_ = f32[224,512]{1,0:T(8,128)S(1)} collective-permute-done((f32[224,512]{1,0:T(8,128)S(1)}, f32[224,512]{1,0:T(8,128)S(1)}, u32[]{:S(2)}, u32[]{:S(2)}) %collective-permute-start.13) | collective-permute-done | bytes 458784 | tf_op jit(solution)/shard_map/ppermute | solution.py:295
  45.7 2.0 %shard_map.64 = (f32[4,128]{1,0:T(4,128)S(1)}, f32[256,512]{1,0:T(8,128)S(1)}, f32[256,512]{1,0:T(8,128)S(1)}, f32[3,2,128,512]{3,2,1,0:T(8,128)S(1)}) custom-call(f32[512,2048]{1,0:T(8,128)S(1)} %get-tuple-element.21.refs_0_, bf16[2048,512]{1,0:T(8,128)(2,1)S(1)} %copy-done.1, f32[16,128]{1,0:T(8,128)S(1)} %bitcast.4, ...), custom_call_target="tpu_custom_call" | custom-call | tf_op jit(solution)/shard_map/pallas_call | solution.py:22
  47.7 0.1 collective-permute-start.14
  47.8 0.5 collective-permute-start.22
  48.3 1.2 %collective-permute-start.17 = (f32[4,128]{1,0:T(4,128)S(1)}, f32[4,128]{1,0:T(4,128)S(1)}, u32[]{:S(2)}, u32[]{:S(2)}) collective-permute-start(f32[4,128]{1,0:T(4,128)S(1)} %get-tuple-element.33.lse_ref), channel_id=1, source_target_pairs={{0,24},{8,16},{16,8},{24,0},{1,25},{9,17},{17,9},{25,1},{2,26},{10... | collective-permute-start | bytes 6152 | tf_op jit(solution)/shard_map/ppermute | solution.py:295
  49.5 0.5 collective-permute-start.16
  50.0 0.2 collective-permute-start.15
  50.2 1.1 %collective-permute-done.17 = f32[4,128]{1,0:T(4,128)S(1)} collective-permute-done((f32[4,128]{1,0:T(4,128)S(1)}, f32[4,128]{1,0:T(4,128)S(1)}, u32[]{:S(2)}, u32[]{:S(2)}) %collective-permute-start.17) | collective-permute-done | bytes 2080 | tf_op jit(solution)/shard_map/ppermute | solution.py:295
  51.3 1.8 %collective-permute-done.16 = f32[4,128]{1,0:T(4,128)S(1)} collective-permute-done((f32[4,128]{1,0:T(4,128)S(1)}, f32[4,128]{1,0:T(4,128)S(1)}, u32[]{:S(2)}, u32[]{:S(2)}) %collective-permute-start.16) | collective-permute-done | bytes 2080 | tf_op jit(solution)/shard_map/ppermute | solution.py:295
  53.1 0.3 shard_map.69.one_ref
  53.4 0.6 collective-permute-start.23
  54.0 0.3 collective-permute-start.18
  54.3 2.6 %collective-permute-start.19 = (f32[4,128]{1,0:T(4,128)S(1)}, f32[4,128]{1,0:T(4,128)S(1)}, u32[]{:S(2)}, u32[]{:S(2)}) collective-permute-start(f32[4,128]{1,0:T(4,128)S(1)} %get-tuple-element.40.refs_5_), channel_id=1, source_target_pairs={{0,4},{1,5},{2,6},{3,7},{4,0},{5,1},{6,2},{7,3},{8,12},{9,13},{10,... | collective-permute-start | bytes 6152 | tf_op jit(solution)/shard_map/ppermute | solution.py:295
  56.9 1.5 %collective-permute-start.20 = (f32[4,128]{1,0:T(4,128)S(1)}, f32[4,128]{1,0:T(4,128)S(1)}, u32[]{:S(2)}, u32[]{:S(2)}) collective-permute-start(f32[4,128]{1,0:T(4,128)S(1)} %get-tuple-element.40.refs_5_), channel_id=1, source_target_pairs={{0,1},{1,0},{2,3},{3,2},{4,5},{5,4},{6,7},{7,6},{8,9},{9,8},{10,11... | collective-permute-start | bytes 6152 | tf_op jit(solution)/shard_map/ppermute | solution.py:295
  58.4 1.3 %shard_map.65 = (bf16[2048,512]{1,0:T(8,128)(2,1)S(1)}, f32[512,2048]{1,0:T(8,128)S(1)}) custom-call(bf16[2048,512]{1,0:T(8,128)(2,1)S(1)} %copy-done.1, bf16[512,512]{1,0:T(8,128)(2,1)S(1)} %copy-done.3, f32[3,2,128,512]{3,2,1,0:T(8,128)S(1)} %get-tuple-element.30.refs_2_, f32[3,2,128,512]{3,2,1,0:T(8,128)S(1)} %collective-permute-done.14.refs_3_), custom_call_target="tpu_custom_call" | custom-call | tf_op jit(solution)/shard_map/pallas_call | solution.py:22
  59.8 0.7 collective-permute-done.20.refs_4_
  60.5 0.9 %shard_map.67 = f32[264,512]{1,0:T(8,128)S(1)} custom-call(f32[512,2048]{1,0:T(8,128)S(1)} %get-tuple-element.31.refs_0_, bf16[2048,512]{1,0:T(8,128)(2,1)S(1)} %get-tuple-element.32.refs_1_, f32[4,128]{1,0:T(4,128)S(1)} %collective-permute-done.18.refs_2_, f32[4,128]{1,0:T(4,128)S(1)} %collective-permute-done.19.refs_3_, ...), custom_call_target="tpu_custom_call" | custom-call | tf_op jit(solution)/shard_map/pallas_call | solution.py:22
  61.4 1.6 %collective-permute-start.21 = (f32[264,512]{1,0:T(8,128)S(1)}, f32[264,512]{1,0:T(8,128)S(1)}, u32[]{:S(2)}, u32[]{:S(2)}) collective-permute-start(f32[264,512]{1,0:T(8,128)S(1)} %shard_map.67), channel_id=1, source_target_pairs={{0,2},{1,3},{2,0},{3,1},{4,6},{5,7},{6,4},{7,5},{8,10},{9,11},{10,... | collective-permute-start | bytes 1622024 | tf_op jit(solution)/shard_map/ppermute | solution.py:295
  63.0 3.6 %collective-permute-done.23.two_ref = f32[256,512]{1,0:T(8,128)S(1)} collective-permute-done((f32[256,512]{1,0:T(8,128)S(1)}, f32[256,512]{1,0:T(8,128)S(1)}, u32[]{:S(2)}, u32[]{:S(2)}) %collective-permute-start.23) | collective-permute-done | bytes 524320 | tf_op jit(solution)/shard_map/ppermute | solution.py:295
  66.6 0.1 shard_map.70
  66.7 0.1 collective-permute-start.24
  66.8 0.5 collective-permute-start.25
  67.3 0.1 collective-permute-start.26
  67.4 0.4 collective-permute-start.27
  67.8 0.3 collective-permute-done.24.refs_4_
  68.1 0.2 collective-permute-done.25.refs_5_
  68.3 0.3 collective-permute-done.26.refs_6_
  68.6 0.2 collective-permute-done.27.refs_7_
  68.8 1.0 %shard_map.71 = f32[512,512]{1,0:T(8,128)} custom-call(f32[64,512]{1,0:T(8,128)S(1)} %get-tuple-element.36.refs_0_, f32[64,512]{1,0:T(8,128)S(1)} %get-tuple-element.37.refs_1_, f32[64,512]{1,0:T(8,128)S(1)} %get-tuple-element.38.refs_2_, f32[64,512]{1,0:T(8,128)S(1)} %get-tuple-element.39.refs_3_, f32[64,512]{1,0:T(8,128)S(1)} %collective-permute-done.24.refs_4_, ...), custom_call_target="tpu_custom_call" | custom-call | tf_op jit(solution)/shard_map/pallas_call | solution.py:22
  69.8 0.9 %shard_map.66.refs_0_ = f32[264,512]{1,0:T(8,128)S(1)} custom-call(f32[512,2048]{1,0:T(8,128)S(1)} %get-tuple-element.31.refs_0_, bf16[2048,512]{1,0:T(8,128)(2,1)S(1)} %get-tuple-element.32.refs_1_, f32[4,128]{1,0:T(4,128)S(1)} %collective-permute-done.18.refs_2_, f32[4,128]{1,0:T(4,128)S(1)} %collective-permute-done.19.refs_3_, ...), custom_call_target="tpu_custom_call" | custom-call | tf_op jit(solution)/shard_map/pallas_call | solution.py:22
  70.7 3.3 %collective-permute-done.21.refs_1_ = f32[264,512]{1,0:T(8,128)S(1)} collective-permute-done((f32[264,512]{1,0:T(8,128)S(1)}, f32[264,512]{1,0:T(8,128)S(1)}, u32[]{:S(2)}, u32[]{:S(2)}) %collective-permute-start.21) | collective-permute-done | bytes 540704 | tf_op jit(solution)/shard_map/ppermute | solution.py:295
  74.0 1.1 %shard_map.68 = f32[256,512]{1,0:T(8,128)} custom-call(f32[264,512]{1,0:T(8,128)S(1)} %shard_map.66.refs_0_, f32[264,512]{1,0:T(8,128)S(1)} %collective-permute-done.21.refs_1_), custom_call_target="tpu_custom_call" | custom-call | tf_op jit(solution)/shard_map/pallas_call | solution.py:22
  (23 shorter events, 0.2 us)
Async XLA Ops:
  0.6 1.0 %copy-start.2 = (bf16[512,512]{1,0:T(8,128)(2,1)S(1)}, bf16[512,512]{1,0:T(8,128)(2,1)}, u32[]{:S(2)}) copy-start(bf16[512,512]{1,0:T(8,128)(2,1)} %refs_1_.3) | copy-start | bytes 1572868
  1.7 24.4 %copy-start.4 = (f32[2048]{0:T(1024)S(1)}, f32[2048]{0:T(1024)}, u32[]{:S(2)}) copy-start(f32[2048]{0:T(1024)} %param.6) | copy-start | bytes 24580
  1.7 17.7 %collective-permute-start.2 = (f32[128,512]{1,0:T(8,128)S(1)}, f32[128,512]{1,0:T(8,128)S(1)}, u32[]{:S(2)}, u32[]{:S(2)}) collective-permute-start(f32[128,512]{1,0:T(8,128)S(1)} %shard_map.60), channel_id=1, source_target_pairs={{0,4},{1,5},{2,6},{3,7},{4,0},{5,1},{6,2},{7,3},{8,12},{9,13},{10,... | collective-permute-start | bytes 786440 | tf_op jit(solution)/shard_map/ppermute | solution.py:295
  5.8 13.6 %collective-permute-start.3 = (f32[128,512]{1,0:T(8,128)S(1)}, f32[128,512]{1,0:T(8,128)S(1)}, u32[]{:S(2)}, u32[]{:S(2)}) collective-permute-start(f32[128,512]{1,0:T(8,128)S(1)} %shard_map.60), channel_id=1, source_target_pairs={{0,1},{1,0},{2,3},{3,2},{4,5},{5,4},{6,7},{7,6},{8,9},{9,8},{10,11... | collective-permute-start | bytes 786440 | tf_op jit(solution)/shard_map/ppermute | solution.py:295
  7.3 1.6 %copy-start = (bf16[2048,512]{1,0:T(8,128)(2,1)S(1)}, bf16[2048,512]{1,0:T(8,128)(2,1)}, u32[]{:S(2)}) copy-start(bf16[2048,512]{1,0:T(8,128)(2,1)} %refs_0_.1) | copy-start | bytes 6291460
  8.9 0.7 copy-start.5
  11.9 3.7 %collective-permute-start = (f32[16,128]{1,0:T(8,128)S(1)}, f32[16,128]{1,0:T(8,128)S(1)}, u32[]{:S(2)}, u32[]{:S(2)}) collective-permute-start(f32[16,128]{1,0:T(8,128)S(1)} %get-tuple-element.24), channel_id=1, source_target_pairs={{0,1},{1,0},{2,3},{3,2},{4,5},{5,4},{6,7},{7,6},{8,9},{9,8},{10,11... | collective-permute-start | bytes 24584 | tf_op jit(solution)/shard_map/ppermute | solution.py:295
  15.6 3.7 %collective-permute-start.1 = (f32[16,128]{1,0:T(8,128)S(1)}, f32[16,128]{1,0:T(8,128)S(1)}, u32[]{:S(2)}, u32[]{:S(2)}) collective-permute-start(f32[16,128]{1,0:T(8,128)S(1)} %multiply_add_fusion.2.one_ref), channel_id=1, source_target_pairs={{0,2},{1,3},{2,0},{3,1},{4,6},{5,7},{6,4},{7,5},{8,10},{9,11},{10,... | collective-permute-start | bytes 24584 | tf_op jit(solution)/shard_map/ppermute | solution.py:295
  19.4 11.4 %collective-permute-start.9 = (f32[160,512]{1,0:T(8,128)S(1)}, f32[160,512]{1,0:T(8,128)S(1)}, u32[]{:S(2)}, u32[]{:S(2)}) collective-permute-start(f32[160,512]{1,0:T(8,128)S(1)} %get-tuple-element.27.refs_6_), channel_id=1, source_target_pairs={{0,16},{8,24},{16,0},{24,8},{1,17},{9,25},{17,1},{25,9},{2,18},{10... | collective-permute-start | bytes 983048 | tf_op jit(solution)/shard_map/ppermute | solution.py:295
  21.0 9.8 %collective-permute-start.8 = (f32[128,512]{1,0:T(8,128)S(1)}, f32[128,512]{1,0:T(8,128)S(1)}, u32[]{:S(2)}, u32[]{:S(2)}) collective-permute-start(f32[128,512]{1,0:T(8,128)S(1)} %get-tuple-element.26.refs_7_), channel_id=1, source_target_pairs={{0,1},{1,0},{2,3},{3,2},{4,5},{5,4},{6,7},{7,6},{8,9},{9,8},{10,11... | collective-permute-start | bytes 786440 | tf_op jit(solution)/shard_map/ppermute | solution.py:295
  21.5 4.5 %collective-permute-start.4 = (f32[16,128]{1,0:T(8,128)S(1)}, f32[16,128]{1,0:T(8,128)S(1)}, u32[]{:S(2)}, u32[]{:S(2)}) collective-permute-start(f32[16,128]{1,0:T(8,128)S(1)} %get-tuple-element.25.refs_3_), channel_id=1, source_target_pairs={{0,4},{1,5},{2,6},{3,7},{4,0},{5,1},{6,2},{7,3},{8,12},{9,13},{10,... | collective-permute-start | bytes 24584 | tf_op jit(solution)/shard_map/ppermute | solution.py:295
  27.1 1.9 %collective-permute-start.5 = (f32[4,128]{1,0:T(4,128)S(1)}, f32[4,128]{1,0:T(4,128)S(1)}, u32[]{:S(2)}, u32[]{:S(2)}) collective-permute-start(f32[4,128]{1,0:T(4,128)S(1)} %shard_map.62.refs_3_), channel_id=1, source_target_pairs={{0,8},{8,0},{16,24},{24,16},{1,9},{9,1},{17,25},{25,17},{2,10},{10... | collective-permute-start | bytes 6152 | tf_op jit(solution)/shard_map/ppermute | solution.py:295
  27.1 3.7 %collective-permute-start.6 = (f32[4,128]{1,0:T(4,128)S(1)}, f32[4,128]{1,0:T(4,128)S(1)}, u32[]{:S(2)}, u32[]{:S(2)}) collective-permute-start(f32[4,128]{1,0:T(4,128)S(1)} %shard_map.62.refs_3_), channel_id=1, source_target_pairs={{0,16},{8,24},{16,0},{24,8},{1,17},{9,25},{17,1},{25,9},{2,18},{10... | collective-permute-start | bytes 6152 | tf_op jit(solution)/shard_map/ppermute | solution.py:295
  27.7 3.1 %collective-permute-start.7 = (f32[4,128]{1,0:T(4,128)S(1)}, f32[4,128]{1,0:T(4,128)S(1)}, u32[]{:S(2)}, u32[]{:S(2)}) collective-permute-start(f32[4,128]{1,0:T(4,128)S(1)} %shard_map.62.refs_3_), channel_id=1, source_target_pairs={{0,24},{8,16},{16,8},{24,0},{1,25},{9,17},{17,9},{25,1},{2,26},{10... | collective-permute-start | bytes 6152 | tf_op jit(solution)/shard_map/ppermute | solution.py:295
  30.8 14.9 %copy-start.1 = (bf16[2048,512]{1,0:T(8,128)(2,1)S(1)}, bf16[2048,512]{1,0:T(8,128)(2,1)}, u32[]{:S(2)}) copy-start(bf16[2048,512]{1,0:T(8,128)(2,1)} %refs_0_.1) | copy-start | bytes 6291460
  31.9 3.7 %collective-permute-start.10 = (f32[16,128]{1,0:T(8,128)S(1)}, f32[16,128]{1,0:T(8,128)S(1)}, u32[]{:S(2)}, u32[]{:S(2)}) collective-permute-start(f32[16,128]{1,0:T(8,128)S(1)} %get-tuple-element.28), channel_id=1, source_target_pairs={{0,1},{1,0},{2,3},{3,2},{4,5},{5,4},{6,7},{7,6},{8,9},{9,8},{10,11... | collective-permute-start | bytes 24584 | tf_op jit(solution)/shard_map/ppermute | solution.py:295
  33.5 12.2 %collective-permute-start.13 = (f32[224,512]{1,0:T(8,128)S(1)}, f32[224,512]{1,0:T(8,128)S(1)}, u32[]{:S(2)}, u32[]{:S(2)}) collective-permute-start(f32[224,512]{1,0:T(8,128)S(1)} %get-tuple-element.29.refs_8_), channel_id=1, source_target_pairs={{0,16},{8,24},{16,0},{24,8},{1,17},{9,25},{17,1},{25,9},{2,18},{10... | collective-permute-start | bytes 1376264 | tf_op jit(solution)/shard_map/ppermute | solution.py:295
  35.7 3.7 %collective-permute-start.11 = (f32[16,128]{1,0:T(8,128)S(1)}, f32[16,128]{1,0:T(8,128)S(1)}, u32[]{:S(2)}, u32[]{:S(2)}) collective-permute-start(f32[16,128]{1,0:T(8,128)S(1)} %multiply_add_fusion.1), channel_id=1, source_target_pairs={{0,2},{1,3},{2,0},{3,1},{4,6},{5,7},{6,4},{7,5},{8,10},{9,11},{10,... | collective-permute-start | bytes 24584 | tf_op jit(solution)/shard_map/ppermute | solution.py:295
  39.4 13.7 %copy-start.6 = (f32[512]{0:T(512)S(1)}, f32[512]{0:T(512)}, u32[]{:S(2)}) copy-start(f32[512]{0:T(512)} %param.7) | copy-start | bytes 6148
  39.4 19.0 %copy-start.3 = (bf16[512,512]{1,0:T(8,128)(2,1)S(1)}, bf16[512,512]{1,0:T(8,128)(2,1)}, u32[]{:S(2)}) copy-start(bf16[512,512]{1,0:T(8,128)(2,1)} %refs_1_.3) | copy-start | bytes 1572868
  39.4 4.6 %collective-permute-start.12 = (f32[16,128]{1,0:T(8,128)S(1)}, f32[16,128]{1,0:T(8,128)S(1)}, u32[]{:S(2)}, u32[]{:S(2)}) collective-permute-start(f32[16,128]{1,0:T(8,128)S(1)} %multiply_add_fusion.refs_4_), channel_id=1, source_target_pairs={{0,4},{1,5},{2,6},{3,7},{4,0},{5,1},{6,2},{7,3},{8,12},{9,13},{10,... | collective-permute-start | bytes 24584 | tf_op jit(solution)/shard_map/ppermute | solution.py:295
  47.7 10.7 %collective-permute-start.14 = (f32[3,2,128,512]{3,2,1,0:T(8,128)S(1)}, f32[3,2,128,512]{3,2,1,0:T(8,128)S(1)}, u32[]{:S(2)}, u32[]{:S(2)}) collective-permute-start(f32[3,2,128,512]{3,2,1,0:T(8,128)S(1)} %get-tuple-element.30.refs_2_), channel_id=1, source_target_pairs={{0,8},{8,0},{16,24},{24,16},{1,9},{9,1},{17,25},{25,17},{2,10},{10... | collective-permute-start | bytes 4718600 | tf_op jit(solution)/shard_map/ppermute | solution.py:295
  47.8 5.3 %collective-permute-start.22 = (f32[256,512]{1,0:T(8,128)S(1)}, f32[256,512]{1,0:T(8,128)S(1)}, u32[]{:S(2)}, u32[]{:S(2)}) collective-permute-start(f32[256,512]{1,0:T(8,128)S(1)} %get-tuple-element.35), channel_id=1, source_target_pairs={{0,8},{8,0},{16,24},{24,16},{1,9},{9,1},{17,25},{25,17},{2,10},{10... | collective-permute-start | bytes 1572872 | tf_op jit(solution)/shard_map/ppermute | solution.py:295
  48.3 3.0 %collective-permute-start.17 = (f32[4,128]{1,0:T(4,128)S(1)}, f32[4,128]{1,0:T(4,128)S(1)}, u32[]{:S(2)}, u32[]{:S(2)}) collective-permute-start(f32[4,128]{1,0:T(4,128)S(1)} %get-tuple-element.33.lse_ref), channel_id=1, source_target_pairs={{0,24},{8,16},{16,8},{24,0},{1,25},{9,17},{17,9},{25,1},{2,26},{10... | collective-permute-start | bytes 6152 | tf_op jit(solution)/shard_map/ppermute | solution.py:295
  49.5 3.6 %collective-permute-start.16 = (f32[4,128]{1,0:T(4,128)S(1)}, f32[4,128]{1,0:T(4,128)S(1)}, u32[]{:S(2)}, u32[]{:S(2)}) collective-permute-start(f32[4,128]{1,0:T(4,128)S(1)} %get-tuple-element.33.lse_ref), channel_id=1, source_target_pairs={{0,16},{8,24},{16,0},{24,8},{1,17},{9,25},{17,1},{25,9},{2,18},{10... | collective-permute-start | bytes 6152 | tf_op jit(solution)/shard_map/ppermute | solution.py:295
  50.0 3.1 %collective-permute-start.15 = (f32[4,128]{1,0:T(4,128)S(1)}, f32[4,128]{1,0:T(4,128)S(1)}, u32[]{:S(2)}, u32[]{:S(2)}) collective-permute-start(f32[4,128]{1,0:T(4,128)S(1)} %get-tuple-element.33.lse_ref), channel_id=1, source_target_pairs={{0,8},{8,0},{16,24},{24,16},{1,9},{9,1},{17,25},{25,17},{2,10},{10... | collective-permute-start | bytes 6152 | tf_op jit(solution)/shard_map/ppermute | solution.py:295
  53.4 13.2 %collective-permute-start.23 = (f32[256,512]{1,0:T(8,128)S(1)}, f32[256,512]{1,0:T(8,128)S(1)}, u32[]{:S(2)}, u32[]{:S(2)}) collective-permute-start(f32[256,512]{1,0:T(8,128)S(1)} %shard_map.69.one_ref), channel_id=1, source_target_pairs={{0,16},{8,24},{16,0},{24,8},{1,17},{9,25},{17,1},{25,9},{2,18},{10... | collective-permute-start | bytes 1572872 | tf_op jit(solution)/shard_map/ppermute | solution.py:295
  54.0 5.7 %collective-permute-start.18 = (f32[4,128]{1,0:T(4,128)S(1)}, f32[4,128]{1,0:T(4,128)S(1)}, u32[]{:S(2)}, u32[]{:S(2)}) collective-permute-start(f32[4,128]{1,0:T(4,128)S(1)} %get-tuple-element.40.refs_5_), channel_id=1, source_target_pairs={{0,5},{1,4},{2,7},{3,6},{4,1},{5,0},{6,3},{7,2},{8,13},{9,12},{10,... | collective-permute-start | bytes 6152 | tf_op jit(solution)/shard_map/ppermute | solution.py:295
  54.3 5.4 %collective-permute-start.19 = (f32[4,128]{1,0:T(4,128)S(1)}, f32[4,128]{1,0:T(4,128)S(1)}, u32[]{:S(2)}, u32[]{:S(2)}) collective-permute-start(f32[4,128]{1,0:T(4,128)S(1)} %get-tuple-element.40.refs_5_), channel_id=1, source_target_pairs={{0,4},{1,5},{2,6},{3,7},{4,0},{5,1},{6,2},{7,3},{8,12},{9,13},{10,... | collective-permute-start | bytes 6152 | tf_op jit(solution)/shard_map/ppermute | solution.py:295
  56.9 3.6 %collective-permute-start.20 = (f32[4,128]{1,0:T(4,128)S(1)}, f32[4,128]{1,0:T(4,128)S(1)}, u32[]{:S(2)}, u32[]{:S(2)}) collective-permute-start(f32[4,128]{1,0:T(4,128)S(1)} %get-tuple-element.40.refs_5_), channel_id=1, source_target_pairs={{0,1},{1,0},{2,3},{3,2},{4,5},{5,4},{6,7},{7,6},{8,9},{9,8},{10,11... | collective-permute-start | bytes 6152 | tf_op jit(solution)/shard_map/ppermute | solution.py:295
  61.4 12.7 %collective-permute-start.21 = (f32[264,512]{1,0:T(8,128)S(1)}, f32[264,512]{1,0:T(8,128)S(1)}, u32[]{:S(2)}, u32[]{:S(2)}) collective-permute-start(f32[264,512]{1,0:T(8,128)S(1)} %shard_map.67), channel_id=1, source_target_pairs={{0,2},{1,3},{2,0},{3,1},{4,6},{5,7},{6,4},{7,5},{8,10},{9,11},{10,... | collective-permute-start | bytes 1622024 | tf_op jit(solution)/shard_map/ppermute | solution.py:295
  66.7 1.4 %collective-permute-start.24 = (f32[64,512]{1,0:T(8,128)S(1)}, f32[64,512]{1,0:T(8,128)S(1)}, u32[]{:S(2)}, u32[]{:S(2)}) collective-permute-start(f32[64,512]{1,0:T(8,128)S(1)} %get-tuple-element.36.refs_0_), channel_id=1, source_target_pairs={{0,8},{8,0},{16,24},{24,16},{1,9},{9,1},{17,25},{25,17},{2,10},{10... | collective-permute-start | bytes 393224 | tf_op jit(solution)/shard_map/ppermute | solution.py:295
  66.8 1.5 %collective-permute-start.25 = (f32[64,512]{1,0:T(8,128)S(1)}, f32[64,512]{1,0:T(8,128)S(1)}, u32[]{:S(2)}, u32[]{:S(2)}) collective-permute-start(f32[64,512]{1,0:T(8,128)S(1)} %get-tuple-element.37.refs_1_), channel_id=1, source_target_pairs={{0,8},{8,0},{16,24},{24,16},{1,9},{9,1},{17,25},{25,17},{2,10},{10... | collective-permute-start | bytes 393224 | tf_op jit(solution)/shard_map/ppermute | solution.py:295
  67.3 1.3 %collective-permute-start.26 = (f32[64,512]{1,0:T(8,128)S(1)}, f32[64,512]{1,0:T(8,128)S(1)}, u32[]{:S(2)}, u32[]{:S(2)}) collective-permute-start(f32[64,512]{1,0:T(8,128)S(1)} %get-tuple-element.38.refs_2_), channel_id=1, source_target_pairs={{0,8},{8,0},{16,24},{24,16},{1,9},{9,1},{17,25},{25,17},{2,10},{10... | collective-permute-start | bytes 393224 | tf_op jit(solution)/shard_map/ppermute | solution.py:295
  67.4 1.5 %collective-permute-start.27 = (f32[64,512]{1,0:T(8,128)S(1)}, f32[64,512]{1,0:T(8,128)S(1)}, u32[]{:S(2)}, u32[]{:S(2)}) collective-permute-start(f32[64,512]{1,0:T(8,128)S(1)} %get-tuple-element.39.refs_3_), channel_id=1, source_target_pairs={{0,8},{8,0},{16,24},{24,16},{1,9},{9,1},{17,25},{25,17},{2,10},{10... | collective-permute-start | bytes 393224 | tf_op jit(solution)/shard_map/ppermute | solution.py:295

commit v7 on v6

--- a/solution.py
+++ b/solution.py
@@ -87,14 +87,18 @@
     out_ref[...] = y_ref[pl.ds(pl.multiple_of(lax.axis_index("row") * rows, rows), rows), :].astype(jnp.float32)
 
 
-def first_kernel(y_ref, x_ref, lt_ref, tile_ref, lse_ref, sqx_ref, sqy_ref):
+def norms_kernel(x_ref, sqx_ref):
+    columns = [norms(x_ref[pl.ds(b, LANES), :]) for b in range(0, x_ref.shape[0], LANES)]
+    sqx_ref[...] = to_dense(columns)
+
+
+def first_kernel(y_ref, x_ref, lt_ref, tile_ref, lse_ref, sqy_ref):
     wide = 256
     y = y_ref[...]
     unit = scale(y.shape[1])
     sqy = norms(y)
     sqy_ref[...] = to_dense([sqy[b : b + LANES] for b in range(0, y.shape[0], LANES)])
     bias = to_column(lt_ref[...]) * LOG2E - sqy
-    columns = []
     for b in range(x_ref.shape[0] // wide):
         at = pl.ds(b * wide, wide)
         x = x_ref[at, :]
@@ -103,12 +107,10 @@
         row = over_targets(tile + bias)
         for c in range(wide // LANES):
             lse_ref[pl.ds(b * (wide // LANES) + c, 1), :] = row[:, c * LANES : (c + 1) * LANES]
-        columns += [norms(x[c : c + LANES]) for c in range(0, wide, LANES)]
-    sqx_ref[...] = to_dense(columns)
 
 
 def early_rows(rows):
-    return rows // 4
+    return rows * 7 // 128 * 8
 
 
 def targets_kernel(n_parts, tile_ref, lt_ref, sqy_ref, *refs):
@@ -324,9 +326,8 @@
             held += [swap(one, "row", distance) for one in held]
         return held
 
-    tile, lse, sqx, sqy = call(
-        first_kernel, (f32(n_tgt, n_src), src_dense, src_dense, tgt_dense), target, source, lt
-    )
+    tile, lse, sqy = call(first_kernel, (f32(n_tgt, n_src), src_dense, tgt_dense), target, source, lt)
+    sqx = call(norms_kernel, src_dense, source)
     cut = early_rows(part.shape[0])
     for step in range(ITERS):
         if step > 0:

time: 75.3 us -> 74.3 us (0.987)
  waiting for transfers between devices: 30.2 us -> 28.6 us
    ppermute x28, waiting for transfers between devices: 30.2 us -> 28.6 us  [swap(): return lax.ppermute(value, axis, [(i, i ^ distance) for i in range(n)])]
    pallas_call x13 -> x14, Pallas kernels: 12.1 us -> 12.2 us  [call(): pl.pallas_call(kernel, out_shape=out_shape, in_specs=in_specs or [VMEM] *...]
  transfers between devices with their start and end apart: 28 -> 28, of which waited for: 17 -> 18; matrix products, arithmetic and copies ran while one was open for 0% -> 0% of each run, Pallas kernels for 10% -> 11%
where the time goes in v7:
time: 74.3 us; the launch traced here: 74.1 us
  starting transfers between devices  29.2 us (39%)
  waiting for transfers between devices  28.6 us (38%)
  Pallas kernels  12.2 us (16%)
  local copies, waits for them, and re-layouts  3.33 us (4%)
  between operations  0.78 us (1%)
    ppermute x28, starting transfers between devices, swap(): return lax.ppermute(value, axis, [(i, i ^ distance) for i in range(n)])  29.2 us
    ppermute x28, waiting for transfers between devices, swap(): return lax.ppermute(value, axis, [(i, i ^ distance) for i in range(n)])  28.6 us
    pallas_call x14, Pallas kernels, call(): pl.pallas_call(kernel, out_shape=out_shape, in_specs=in_specs or [VMEM] *...  12.2 us
    unnamed x14, local copies, waits for them, and re-layouts  3.33 us
  transfers between devices with their start and end apart: 28, of which 18 were waited for; matrix products, arithmetic and copies ran while one was open for 0% of the time, Pallas kernels for 11%

profile of v7, /device:TPU:0, one launch (start us, length us, event | category | flops | bytes accessed | tf_op | source)
XLA Modules:
  0.0 74.1 jit_solution(17258608007329847236)
XLA Ops:
  0.6 0.0 copy-start.2
  0.6 1.0 %copy-done.2 = bf16[512,512]{1,0:T(8,128)(2,1)S(1)} copy-done((bf16[512,512]{1,0:T(8,128)(2,1)S(1)}, bf16[512,512]{1,0:T(8,128)(2,1)}, u32[]{:S(2)}) %copy-start.2) | copy-done | bytes 524312
  1.7 4.1 %collective-permute-start.2 = (f32[128,512]{1,0:T(8,128)S(1)}, f32[128,512]{1,0:T(8,128)S(1)}, u32[]{:S(2)}, u32[]{:S(2)}) collective-permute-start(f32[128,512]{1,0:T(8,128)S(1)} %shard_map.61), channel_id=1, source_target_pairs={{0,4},{1,5},{2,6},{3,7},{4,0},{5,1},{6,2},{7,3},{8,12},{9,13},{10,... | collective-permute-start | bytes 786440 | tf_op jit(solution)/shard_map/ppermute | solution.py:297
  5.8 1.5 %collective-permute-start.3 = (f32[128,512]{1,0:T(8,128)S(1)}, f32[128,512]{1,0:T(8,128)S(1)}, u32[]{:S(2)}, u32[]{:S(2)}) collective-permute-start(f32[128,512]{1,0:T(8,128)S(1)} %shard_map.61), channel_id=1, source_target_pairs={{0,1},{1,0},{2,3},{3,2},{4,5},{5,4},{6,7},{7,6},{8,9},{9,8},{10,11... | collective-permute-start | bytes 786440 | tf_op jit(solution)/shard_map/ppermute | solution.py:297
  7.3 1.6 %copy-done = bf16[2048,512]{1,0:T(8,128)(2,1)S(1)} copy-done((bf16[2048,512]{1,0:T(8,128)(2,1)S(1)}, bf16[2048,512]{1,0:T(8,128)(2,1)}, u32[]{:S(2)}) %copy-start) | copy-done | bytes 2097176
  8.9 0.7 copy-done.5
  9.6 1.9 %shard_map.59 = (f32[512,2048]{1,0:T(8,128)S(1)}, f32[16,128]{1,0:T(8,128)S(1)}, f32[4,128]{1,0:T(4,128)S(1)}) custom-call(bf16[512,512]{1,0:T(8,128)(2,1)S(1)} %copy-done.2, bf16[2048,512]{1,0:T(8,128)(2,1)S(1)} %copy-done, f32[4,128]{1,0:T(4,128)S(1)} %bitcast.5), custom_call_target="tpu_custom_call" | custom-call | tf_op jit(solution)/shard_map/pallas_call | solution.py:22
  11.5 0.6 collective-permute-start
  12.1 3.1 %collective-permute-done = f32[16,128]{1,0:T(8,128)S(1)} collective-permute-done((f32[16,128]{1,0:T(8,128)S(1)}, f32[16,128]{1,0:T(8,128)S(1)}, u32[]{:S(2)}, u32[]{:S(2)}) %collective-permute-start) | collective-permute-done | bytes 8224 | tf_op jit(solution)/shard_map/ppermute | solution.py:297
  15.2 1.6 %collective-permute-start.1 = (f32[16,128]{1,0:T(8,128)S(1)}, f32[16,128]{1,0:T(8,128)S(1)}, u32[]{:S(2)}, u32[]{:S(2)}) collective-permute-start(f32[16,128]{1,0:T(8,128)S(1)} %multiply_add_fusion.2.one_ref), channel_id=1, source_target_pairs={{0,2},{1,3},{2,0},{3,1},{4,6},{5,7},{6,4},{7,5},{8,10},{9,11},{10,... | collective-permute-start | bytes 24584 | tf_op jit(solution)/shard_map/ppermute | solution.py:297
  16.8 2.1 %collective-permute-done.1.two_ref = f32[16,128]{1,0:T(8,128)S(1)} collective-permute-done((f32[16,128]{1,0:T(8,128)S(1)}, f32[16,128]{1,0:T(8,128)S(1)}, u32[]{:S(2)}, u32[]{:S(2)}) %collective-permute-start.1) | collective-permute-done | bytes 8224 | tf_op jit(solution)/shard_map/ppermute | solution.py:297
  18.9 0.0 collective-permute-done.2.refs_0_
  19.0 1.6 %collective-permute-start.9 = (f32[184,512]{1,0:T(8,128)S(1)}, f32[184,512]{1,0:T(8,128)S(1)}, u32[]{:S(2)}, u32[]{:S(2)}) collective-permute-start(f32[184,512]{1,0:T(8,128)S(1)} %get-tuple-element.25.refs_6_), channel_id=1, source_target_pairs={{0,16},{8,24},{16,0},{24,8},{1,17},{9,25},{17,1},{25,9},{2,18},{10... | collective-permute-start | bytes 1130504 | tf_op jit(solution)/shard_map/ppermute | solution.py:297
  20.6 0.5 collective-permute-start.8
  21.1 0.3 collective-permute-start.4
  21.4 0.5 shard_map.60.refs_2_.refs_3_
  21.9 3.7 %collective-permute-done.4.refs_4_ = f32[16,128]{1,0:T(8,128)S(1)} collective-permute-done((f32[16,128]{1,0:T(8,128)S(1)}, f32[16,128]{1,0:T(8,128)S(1)}, u32[]{:S(2)}, u32[]{:S(2)}) %collective-permute-start.4) | collective-permute-done | bytes 8224 | tf_op jit(solution)/shard_map/ppermute | solution.py:297
  25.7 1.0 %shard_map.63.refs_3_ = f32[4,128]{1,0:T(4,128)S(1)} custom-call(f32[512,2048]{1,0:T(8,128)S(1)} %get-tuple-element.20.refs_0_, f32[16,128]{1,0:T(8,128)S(1)} %bitcast.3, f32[16,128]{1,0:T(8,128)S(1)} %shard_map.60.refs_2_.refs_3_, f32[16,128]{1,0:T(8,128)S(1)} %get-tuple-element.23.refs_3_, f32[16,128]{1,0:T(8,128)S(1)} %collective-permute-done.4.refs_4_), custom_call_target="tpu_custom_call" | custom-call | tf_op jit(solution)/shard_map/pallas_call | solution.py:22
  26.6 0.0 collective-permute-start.5
  26.7 0.6 collective-permute-start.6
  27.3 1.3 %collective-permute-start.7 = (f32[4,128]{1,0:T(4,128)S(1)}, f32[4,128]{1,0:T(4,128)S(1)}, u32[]{:S(2)}, u32[]{:S(2)}) collective-permute-start(f32[4,128]{1,0:T(4,128)S(1)} %shard_map.63.refs_3_), channel_id=1, source_target_pairs={{0,24},{8,16},{16,8},{24,0},{1,25},{9,17},{17,9},{25,1},{2,26},{10... | collective-permute-start | bytes 6152 | tf_op jit(solution)/shard_map/ppermute | solution.py:297
  28.6 1.8 %collective-permute-done.6.refs_5_ = f32[4,128]{1,0:T(4,128)S(1)} collective-permute-done((f32[4,128]{1,0:T(4,128)S(1)}, f32[4,128]{1,0:T(4,128)S(1)}, u32[]{:S(2)}, u32[]{:S(2)}) %collective-permute-start.6) | collective-permute-done | bytes 2080 | tf_op jit(solution)/shard_map/ppermute | solution.py:297
  30.4 1.1 %shard_map.64 = (f32[16,128]{1,0:T(8,128)S(1)}, f32[200,512]{1,0:T(8,128)S(1)}) custom-call(f32[512,2048]{1,0:T(8,128)S(1)} %get-tuple-element.20.refs_0_, f32[4,128]{1,0:T(4,128)S(1)} %bitcast.6, f32[4,128]{1,0:T(4,128)S(1)} %get-tuple-element.21.refs_2_, f32[4,128]{1,0:T(4,128)S(1)} %shard_map.63.refs_3_, f32[4,128]{1,0:T(4,128)S(1)} %collective-permute-done.5.refs_4_, ...), custom_call_target="tpu_custom_call" | custom-call | tf_op jit(solution)/shard_map/pallas_call | solution.py:22
  31.5 1.6 %collective-permute-start.10 = (f32[16,128]{1,0:T(8,128)S(1)}, f32[16,128]{1,0:T(8,128)S(1)}, u32[]{:S(2)}, u32[]{:S(2)}) collective-permute-start(f32[16,128]{1,0:T(8,128)S(1)} %get-tuple-element.26), channel_id=1, source_target_pairs={{0,1},{1,0},{2,3},{3,2},{4,5},{5,4},{6,7},{7,6},{8,9},{9,8},{10,11... | collective-permute-start | bytes 24584 | tf_op jit(solution)/shard_map/ppermute | solution.py:297
  33.1 1.4 %collective-permute-start.13 = (f32[200,512]{1,0:T(8,128)S(1)}, f32[200,512]{1,0:T(8,128)S(1)}, u32[]{:S(2)}, u32[]{:S(2)}) collective-permute-start(f32[200,512]{1,0:T(8,128)S(1)} %get-tuple-element.27.refs_8_), channel_id=1, source_target_pairs={{0,16},{8,24},{16,0},{24,8},{1,17},{9,25},{17,1},{25,9},{2,18},{10... | collective-permute-start | bytes 1228808 | tf_op jit(solution)/shard_map/ppermute | solution.py:297
  34.5 0.7 collective-permute-done.10
  35.2 1.6 %collective-permute-start.11 = (f32[16,128]{1,0:T(8,128)S(1)}, f32[16,128]{1,0:T(8,128)S(1)}, u32[]{:S(2)}, u32[]{:S(2)}) collective-permute-start(f32[16,128]{1,0:T(8,128)S(1)} %multiply_add_fusion.1), channel_id=1, source_target_pairs={{0,2},{1,3},{2,0},{3,1},{4,6},{5,7},{6,4},{7,5},{8,10},{9,11},{10,... | collective-permute-start | bytes 24584 | tf_op jit(solution)/shard_map/ppermute | solution.py:297
  36.9 2.1 %collective-permute-done.11 = f32[16,128]{1,0:T(8,128)S(1)} collective-permute-done((f32[16,128]{1,0:T(8,128)S(1)}, f32[16,128]{1,0:T(8,128)S(1)}, u32[]{:S(2)}, u32[]{:S(2)}) %collective-permute-start.11) | collective-permute-done | bytes 8224 | tf_op jit(solution)/shard_map/ppermute | solution.py:297
  39.0 0.0 copy-start.3
  39.0 2.1 %collective-permute-start.12 = (f32[16,128]{1,0:T(8,128)S(1)}, f32[16,128]{1,0:T(8,128)S(1)}, u32[]{:S(2)}, u32[]{:S(2)}) collective-permute-start(f32[16,128]{1,0:T(8,128)S(1)} %multiply_add_fusion.refs_4_), channel_id=1, source_target_pairs={{0,4},{1,5},{2,6},{3,7},{4,0},{5,1},{6,2},{7,3},{8,12},{9,13},{10,... | collective-permute-start | bytes 24584 | tf_op jit(solution)/shard_map/ppermute | solution.py:297
  41.1 2.5 %collective-permute-done.12.refs_5_ = f32[16,128]{1,0:T(8,128)S(1)} collective-permute-done((f32[16,128]{1,0:T(8,128)S(1)}, f32[16,128]{1,0:T(8,128)S(1)}, u32[]{:S(2)}, u32[]{:S(2)}) %collective-permute-start.12) | collective-permute-done | bytes 8224 | tf_op jit(solution)/shard_map/ppermute | solution.py:297
  43.6 0.7 collective-permute-done.13.refs_9_
  44.3 2.0 %shard_map.65 = (f32[4,128]{1,0:T(4,128)S(1)}, f32[256,512]{1,0:T(8,128)S(1)}, f32[256,512]{1,0:T(8,128)S(1)}, f32[3,2,128,512]{3,2,1,0:T(8,128)S(1)}) custom-call(f32[512,2048]{1,0:T(8,128)S(1)} %get-tuple-element.20.refs_0_, bf16[2048,512]{1,0:T(8,128)(2,1)S(1)} %copy-done.1, f32[16,128]{1,0:T(8,128)S(1)} %bitcast.4, ...), custom_call_target="tpu_custom_call" | custom-call | tf_op jit(solution)/shard_map/pallas_call | solution.py:22
  46.3 0.1 collective-permute-start.14
  46.3 0.5 collective-permute-start.22
  46.8 1.2 %collective-permute-start.17 = (f32[4,128]{1,0:T(4,128)S(1)}, f32[4,128]{1,0:T(4,128)S(1)}, u32[]{:S(2)}, u32[]{:S(2)}) collective-permute-start(f32[4,128]{1,0:T(4,128)S(1)} %get-tuple-element.31.lse_ref), channel_id=1, source_target_pairs={{0,24},{8,16},{16,8},{24,0},{1,25},{9,17},{17,9},{25,1},{2,26},{10... | collective-permute-start | bytes 6152 | tf_op jit(solution)/shard_map/ppermute | solution.py:297
  48.0 0.5 collective-permute-start.16
  48.5 0.2 collective-permute-start.15
  48.7 1.1 %collective-permute-done.17 = f32[4,128]{1,0:T(4,128)S(1)} collective-permute-done((f32[4,128]{1,0:T(4,128)S(1)}, f32[4,128]{1,0:T(4,128)S(1)}, u32[]{:S(2)}, u32[]{:S(2)}) %collective-permute-start.17) | collective-permute-done | bytes 2080 | tf_op jit(solution)/shard_map/ppermute | solution.py:297
  49.9 1.8 %collective-permute-done.16 = f32[4,128]{1,0:T(4,128)S(1)} collective-permute-done((f32[4,128]{1,0:T(4,128)S(1)}, f32[4,128]{1,0:T(4,128)S(1)}, u32[]{:S(2)}, u32[]{:S(2)}) %collective-permute-start.16) | collective-permute-done | bytes 2080 | tf_op jit(solution)/shard_map/ppermute | solution.py:297
  51.6 0.3 shard_map.70.one_ref
  52.0 0.6 collective-permute-start.23
  52.5 1.3 %collective-permute-start.18 = (f32[4,128]{1,0:T(4,128)S(1)}, f32[4,128]{1,0:T(4,128)S(1)}, u32[]{:S(2)}, u32[]{:S(2)}) collective-permute-start(f32[4,128]{1,0:T(4,128)S(1)} %get-tuple-element.38.refs_5_), channel_id=1, source_target_pairs={{0,5},{1,4},{2,7},{3,6},{4,1},{5,0},{6,3},{7,2},{8,13},{9,12},{10,... | collective-permute-start | bytes 6152 | tf_op jit(solution)/shard_map/ppermute | solution.py:297
  53.9 1.9 %collective-permute-start.19 = (f32[4,128]{1,0:T(4,128)S(1)}, f32[4,128]{1,0:T(4,128)S(1)}, u32[]{:S(2)}, u32[]{:S(2)}) collective-permute-start(f32[4,128]{1,0:T(4,128)S(1)} %get-tuple-element.38.refs_5_), channel_id=1, source_target_pairs={{0,4},{1,5},{2,6},{3,7},{4,0},{5,1},{6,2},{7,3},{8,12},{9,13},{10,... | collective-permute-start | bytes 6152 | tf_op jit(solution)/shard_map/ppermute | solution.py:297
  55.7 1.2 %collective-permute-start.20 = (f32[4,128]{1,0:T(4,128)S(1)}, f32[4,128]{1,0:T(4,128)S(1)}, u32[]{:S(2)}, u32[]{:S(2)}) collective-permute-start(f32[4,128]{1,0:T(4,128)S(1)} %get-tuple-element.38.refs_5_), channel_id=1, source_target_pairs={{0,1},{1,0},{2,3},{3,2},{4,5},{5,4},{6,7},{7,6},{8,9},{9,8},{10,11... | collective-permute-start | bytes 6152 | tf_op jit(solution)/shard_map/ppermute | solution.py:297
  56.9 1.3 %shard_map.66 = (bf16[2048,512]{1,0:T(8,128)(2,1)S(1)}, f32[512,2048]{1,0:T(8,128)S(1)}) custom-call(bf16[2048,512]{1,0:T(8,128)(2,1)S(1)} %copy-done.1, bf16[512,512]{1,0:T(8,128)(2,1)S(1)} %copy-done.3, f32[3,2,128,512]{3,2,1,0:T(8,128)S(1)} %get-tuple-element.28.refs_2_, f32[3,2,128,512]{3,2,1,0:T(8,128)S(1)} %collective-permute-done.14.refs_3_), custom_call_target="tpu_custom_call" | custom-call | tf_op jit(solution)/shard_map/pallas_call | solution.py:22
  58.3 0.1 collective-permute-done.19.refs_3_
  58.4 1.0 %collective-permute-done.20.refs_4_ = f32[4,128]{1,0:T(4,128)S(1)} collective-permute-done((f32[4,128]{1,0:T(4,128)S(1)}, f32[4,128]{1,0:T(4,128)S(1)}, u32[]{:S(2)}, u32[]{:S(2)}) %collective-permute-start.20) | collective-permute-done | bytes 2080 | tf_op jit(solution)/shard_map/ppermute | solution.py:297
  59.3 0.9 %shard_map.68 = f32[264,512]{1,0:T(8,128)S(1)} custom-call(f32[512,2048]{1,0:T(8,128)S(1)} %get-tuple-element.29.refs_0_, bf16[2048,512]{1,0:T(8,128)(2,1)S(1)} %get-tuple-element.30.refs_1_, f32[4,128]{1,0:T(4,128)S(1)} %collective-permute-done.18.refs_2_, f32[4,128]{1,0:T(4,128)S(1)} %collective-permute-done.19.refs_3_, ...), custom_call_target="tpu_custom_call" | custom-call | tf_op jit(solution)/shard_map/pallas_call | solution.py:22
  60.2 1.8 %collective-permute-start.21 = (f32[264,512]{1,0:T(8,128)S(1)}, f32[264,512]{1,0:T(8,128)S(1)}, u32[]{:S(2)}, u32[]{:S(2)}) collective-permute-start(f32[264,512]{1,0:T(8,128)S(1)} %shard_map.68), channel_id=1, source_target_pairs={{0,2},{1,3},{2,0},{3,1},{4,6},{5,7},{6,4},{7,5},{8,10},{9,11},{10,... | collective-permute-start | bytes 1622024 | tf_op jit(solution)/shard_map/ppermute | solution.py:297
  62.0 3.2 %collective-permute-done.23.two_ref = f32[256,512]{1,0:T(8,128)S(1)} collective-permute-done((f32[256,512]{1,0:T(8,128)S(1)}, f32[256,512]{1,0:T(8,128)S(1)}, u32[]{:S(2)}, u32[]{:S(2)}) %collective-permute-start.23) | collective-permute-done | bytes 524320 | tf_op jit(solution)/shard_map/ppermute | solution.py:297
  65.1 0.1 shard_map.71
  65.2 0.1 collective-permute-start.24
  65.3 0.5 collective-permute-start.25
  65.8 0.1 collective-permute-start.26
  65.9 0.4 collective-permute-start.27
  66.3 0.3 collective-permute-done.24.refs_4_
  66.6 0.2 collective-permute-done.25.refs_5_
  66.8 0.3 collective-permute-done.26.refs_6_
  67.1 0.2 collective-permute-done.27.refs_7_
  67.3 1.0 %shard_map.72 = f32[512,512]{1,0:T(8,128)} custom-call(f32[64,512]{1,0:T(8,128)S(1)} %get-tuple-element.34.refs_0_, f32[64,512]{1,0:T(8,128)S(1)} %get-tuple-element.35.refs_1_, f32[64,512]{1,0:T(8,128)S(1)} %get-tuple-element.36.refs_2_, f32[64,512]{1,0:T(8,128)S(1)} %get-tuple-element.37.refs_3_, f32[64,512]{1,0:T(8,128)S(1)} %collective-permute-done.24.refs_4_, ...), custom_call_target="tpu_custom_call" | custom-call | tf_op jit(solution)/shard_map/pallas_call | solution.py:22
  68.4 0.9 %shard_map.67.refs_0_ = f32[264,512]{1,0:T(8,128)S(1)} custom-call(f32[512,2048]{1,0:T(8,128)S(1)} %get-tuple-element.29.refs_0_, bf16[2048,512]{1,0:T(8,128)(2,1)S(1)} %get-tuple-element.30.refs_1_, f32[4,128]{1,0:T(4,128)S(1)} %collective-permute-done.18.refs_2_, f32[4,128]{1,0:T(4,128)S(1)} %collective-permute-done.19.refs_3_, ...), custom_call_target="tpu_custom_call" | custom-call | tf_op jit(solution)/shard_map/pallas_call | solution.py:22
  69.2 3.7 %collective-permute-done.21.refs_1_ = f32[264,512]{1,0:T(8,128)S(1)} collective-permute-done((f32[264,512]{1,0:T(8,128)S(1)}, f32[264,512]{1,0:T(8,128)S(1)}, u32[]{:S(2)}, u32[]{:S(2)}) %collective-permute-start.21) | collective-permute-done | bytes 540704 | tf_op jit(solution)/shard_map/ppermute | solution.py:297
  73.0 1.1 %shard_map.69 = f32[256,512]{1,0:T(8,128)} custom-call(f32[264,512]{1,0:T(8,128)S(1)} %shard_map.67.refs_0_, f32[264,512]{1,0:T(8,128)S(1)} %collective-permute-done.21.refs_1_), custom_call_target="tpu_custom_call" | custom-call | tf_op jit(solution)/shard_map/pallas_call | solution.py:22
  (24 shorter events, 0.2 us)
Async XLA Ops:
  0.6 1.0 %copy-start.2 = (bf16[512,512]{1,0:T(8,128)(2,1)S(1)}, bf16[512,512]{1,0:T(8,128)(2,1)}, u32[]{:S(2)}) copy-start(bf16[512,512]{1,0:T(8,128)(2,1)} %refs_1_.3) | copy-start | bytes 1572868
  1.7 17.2 %collective-permute-start.2 = (f32[128,512]{1,0:T(8,128)S(1)}, f32[128,512]{1,0:T(8,128)S(1)}, u32[]{:S(2)}, u32[]{:S(2)}) collective-permute-start(f32[128,512]{1,0:T(8,128)S(1)} %shard_map.61), channel_id=1, source_target_pairs={{0,4},{1,5},{2,6},{3,7},{4,0},{5,1},{6,2},{7,3},{8,12},{9,13},{10,... | collective-permute-start | bytes 786440 | tf_op jit(solution)/shard_map/ppermute | solution.py:297
  5.8 13.1 %collective-permute-start.3 = (f32[128,512]{1,0:T(8,128)S(1)}, f32[128,512]{1,0:T(8,128)S(1)}, u32[]{:S(2)}, u32[]{:S(2)}) collective-permute-start(f32[128,512]{1,0:T(8,128)S(1)} %shard_map.61), channel_id=1, source_target_pairs={{0,1},{1,0},{2,3},{3,2},{4,5},{5,4},{6,7},{7,6},{8,9},{9,8},{10,11... | collective-permute-start | bytes 786440 | tf_op jit(solution)/shard_map/ppermute | solution.py:297
  7.3 1.6 %copy-start = (bf16[2048,512]{1,0:T(8,128)(2,1)S(1)}, bf16[2048,512]{1,0:T(8,128)(2,1)}, u32[]{:S(2)}) copy-start(bf16[2048,512]{1,0:T(8,128)(2,1)} %refs_0_.1) | copy-start | bytes 6291460
  8.9 0.7 copy-start.5
  9.6 11.9 %copy-start.1 = (bf16[2048,512]{1,0:T(8,128)(2,1)S(1)}, bf16[2048,512]{1,0:T(8,128)(2,1)}, u32[]{:S(2)}) copy-start(bf16[2048,512]{1,0:T(8,128)(2,1)} %refs_0_.1) | copy-start | bytes 6291460
  9.6 16.1 %copy-start.4 = (f32[2048]{0:T(1024)S(1)}, f32[2048]{0:T(1024)}, u32[]{:S(2)}) copy-start(f32[2048]{0:T(1024)} %param.6) | copy-start | bytes 24580
  11.5 3.7 %collective-permute-start = (f32[16,128]{1,0:T(8,128)S(1)}, f32[16,128]{1,0:T(8,128)S(1)}, u32[]{:S(2)}, u32[]{:S(2)}) collective-permute-start(f32[16,128]{1,0:T(8,128)S(1)} %get-tuple-element.22), channel_id=1, source_target_pairs={{0,1},{1,0},{2,3},{3,2},{4,5},{5,4},{6,7},{7,6},{8,9},{9,8},{10,11... | collective-permute-start | bytes 24584 | tf_op jit(solution)/shard_map/ppermute | solution.py:297
  15.2 3.7 %collective-permute-start.1 = (f32[16,128]{1,0:T(8,128)S(1)}, f32[16,128]{1,0:T(8,128)S(1)}, u32[]{:S(2)}, u32[]{:S(2)}) collective-permute-start(f32[16,128]{1,0:T(8,128)S(1)} %multiply_add_fusion.2.one_ref), channel_id=1, source_target_pairs={{0,2},{1,3},{2,0},{3,1},{4,6},{5,7},{6,4},{7,5},{8,10},{9,11},{10,... | collective-permute-start | bytes 24584 | tf_op jit(solution)/shard_map/ppermute | solution.py:297
  19.0 11.4 %collective-permute-start.9 = (f32[184,512]{1,0:T(8,128)S(1)}, f32[184,512]{1,0:T(8,128)S(1)}, u32[]{:S(2)}, u32[]{:S(2)}) collective-permute-start(f32[184,512]{1,0:T(8,128)S(1)} %get-tuple-element.25.refs_6_), channel_id=1, source_target_pairs={{0,16},{8,24},{16,0},{24,8},{1,17},{9,25},{17,1},{25,9},{2,18},{10... | collective-permute-start | bytes 1130504 | tf_op jit(solution)/shard_map/ppermute | solution.py:297
  20.6 9.8 %collective-permute-start.8 = (f32[128,512]{1,0:T(8,128)S(1)}, f32[128,512]{1,0:T(8,128)S(1)}, u32[]{:S(2)}, u32[]{:S(2)}) collective-permute-start(f32[128,512]{1,0:T(8,128)S(1)} %get-tuple-element.24.refs_7_), channel_id=1, source_target_pairs={{0,1},{1,0},{2,3},{3,2},{4,5},{5,4},{6,7},{7,6},{8,9},{9,8},{10,11... | collective-permute-start | bytes 786440 | tf_op jit(solution)/shard_map/ppermute | solution.py:297
  21.1 4.5 %collective-permute-start.4 = (f32[16,128]{1,0:T(8,128)S(1)}, f32[16,128]{1,0:T(8,128)S(1)}, u32[]{:S(2)}, u32[]{:S(2)}) collective-permute-start(f32[16,128]{1,0:T(8,128)S(1)} %get-tuple-element.23.refs_3_), channel_id=1, source_target_pairs={{0,4},{1,5},{2,6},{3,7},{4,0},{5,1},{6,2},{7,3},{8,12},{9,13},{10,... | collective-permute-start | bytes 24584 | tf_op jit(solution)/shard_map/ppermute | solution.py:297
  25.7 4.7 %copy-start.6 = (f32[512]{0:T(512)S(1)}, f32[512]{0:T(512)}, u32[]{:S(2)}) copy-start(f32[512]{0:T(512)} %param.7) | copy-start | bytes 6148
  26.6 1.9 %collective-permute-start.5 = (f32[4,128]{1,0:T(4,128)S(1)}, f32[4,128]{1,0:T(4,128)S(1)}, u32[]{:S(2)}, u32[]{:S(2)}) collective-permute-start(f32[4,128]{1,0:T(4,128)S(1)} %shard_map.63.refs_3_), channel_id=1, source_target_pairs={{0,8},{8,0},{16,24},{24,16},{1,9},{9,1},{17,25},{25,17},{2,10},{10... | collective-permute-start | bytes 6152 | tf_op jit(solution)/shard_map/ppermute | solution.py:297
  26.7 3.7 %collective-permute-start.6 = (f32[4,128]{1,0:T(4,128)S(1)}, f32[4,128]{1,0:T(4,128)S(1)}, u32[]{:S(2)}, u32[]{:S(2)}) collective-permute-start(f32[4,128]{1,0:T(4,128)S(1)} %shard_map.63.refs_3_), channel_id=1, source_target_pairs={{0,16},{8,24},{16,0},{24,8},{1,17},{9,25},{17,1},{25,9},{2,18},{10... | collective-permute-start | bytes 6152 | tf_op jit(solution)/shard_map/ppermute | solution.py:297
  27.3 3.1 %collective-permute-start.7 = (f32[4,128]{1,0:T(4,128)S(1)}, f32[4,128]{1,0:T(4,128)S(1)}, u32[]{:S(2)}, u32[]{:S(2)}) collective-permute-start(f32[4,128]{1,0:T(4,128)S(1)} %shard_map.63.refs_3_), channel_id=1, source_target_pairs={{0,24},{8,16},{16,8},{24,0},{1,25},{9,17},{17,9},{25,1},{2,26},{10... | collective-permute-start | bytes 6152 | tf_op jit(solution)/shard_map/ppermute | solution.py:297
  31.5 3.7 %collective-permute-start.10 = (f32[16,128]{1,0:T(8,128)S(1)}, f32[16,128]{1,0:T(8,128)S(1)}, u32[]{:S(2)}, u32[]{:S(2)}) collective-permute-start(f32[16,128]{1,0:T(8,128)S(1)} %get-tuple-element.26), channel_id=1, source_target_pairs={{0,1},{1,0},{2,3},{3,2},{4,5},{5,4},{6,7},{7,6},{8,9},{9,8},{10,11... | collective-permute-start | bytes 24584 | tf_op jit(solution)/shard_map/ppermute | solution.py:297
  33.1 11.2 %collective-permute-start.13 = (f32[200,512]{1,0:T(8,128)S(1)}, f32[200,512]{1,0:T(8,128)S(1)}, u32[]{:S(2)}, u32[]{:S(2)}) collective-permute-start(f32[200,512]{1,0:T(8,128)S(1)} %get-tuple-element.27.refs_8_), channel_id=1, source_target_pairs={{0,16},{8,24},{16,0},{24,8},{1,17},{9,25},{17,1},{25,9},{2,18},{10... | collective-permute-start | bytes 1228808 | tf_op jit(solution)/shard_map/ppermute | solution.py:297
  35.2 3.7 %collective-permute-start.11 = (f32[16,128]{1,0:T(8,128)S(1)}, f32[16,128]{1,0:T(8,128)S(1)}, u32[]{:S(2)}, u32[]{:S(2)}) collective-permute-start(f32[16,128]{1,0:T(8,128)S(1)} %multiply_add_fusion.1), channel_id=1, source_target_pairs={{0,2},{1,3},{2,0},{3,1},{4,6},{5,7},{6,4},{7,5},{8,10},{9,11},{10,... | collective-permute-start | bytes 24584 | tf_op jit(solution)/shard_map/ppermute | solution.py:297
  39.0 18.0 %copy-start.3 = (bf16[512,512]{1,0:T(8,128)(2,1)S(1)}, bf16[512,512]{1,0:T(8,128)(2,1)}, u32[]{:S(2)}) copy-start(bf16[512,512]{1,0:T(8,128)(2,1)} %refs_1_.3) | copy-start | bytes 1572868
  39.0 4.6 %collective-permute-start.12 = (f32[16,128]{1,0:T(8,128)S(1)}, f32[16,128]{1,0:T(8,128)S(1)}, u32[]{:S(2)}, u32[]{:S(2)}) collective-permute-start(f32[16,128]{1,0:T(8,128)S(1)} %multiply_add_fusion.refs_4_), channel_id=1, source_target_pairs={{0,4},{1,5},{2,6},{3,7},{4,0},{5,1},{6,2},{7,3},{8,12},{9,13},{10,... | collective-permute-start | bytes 24584 | tf_op jit(solution)/shard_map/ppermute | solution.py:297
  46.3 10.7 %collective-permute-start.14 = (f32[3,2,128,512]{3,2,1,0:T(8,128)S(1)}, f32[3,2,128,512]{3,2,1,0:T(8,128)S(1)}, u32[]{:S(2)}, u32[]{:S(2)}) collective-permute-start(f32[3,2,128,512]{3,2,1,0:T(8,128)S(1)} %get-tuple-element.28.refs_2_), channel_id=1, source_target_pairs={{0,8},{8,0},{16,24},{24,16},{1,9},{9,1},{17,25},{25,17},{2,10},{10... | collective-permute-start | bytes 4718600 | tf_op jit(solution)/shard_map/ppermute | solution.py:297
  46.3 5.3 %collective-permute-start.22 = (f32[256,512]{1,0:T(8,128)S(1)}, f32[256,512]{1,0:T(8,128)S(1)}, u32[]{:S(2)}, u32[]{:S(2)}) collective-permute-start(f32[256,512]{1,0:T(8,128)S(1)} %get-tuple-element.33), channel_id=1, source_target_pairs={{0,8},{8,0},{16,24},{24,16},{1,9},{9,1},{17,25},{25,17},{2,10},{10... | collective-permute-start | bytes 1572872 | tf_op jit(solution)/shard_map/ppermute | solution.py:297
  46.8 3.0 %collective-permute-start.17 = (f32[4,128]{1,0:T(4,128)S(1)}, f32[4,128]{1,0:T(4,128)S(1)}, u32[]{:S(2)}, u32[]{:S(2)}) collective-permute-start(f32[4,128]{1,0:T(4,128)S(1)} %get-tuple-element.31.lse_ref), channel_id=1, source_target_pairs={{0,24},{8,16},{16,8},{24,0},{1,25},{9,17},{17,9},{25,1},{2,26},{10... | collective-permute-start | bytes 6152 | tf_op jit(solution)/shard_map/ppermute | solution.py:297
  48.0 3.6 %collective-permute-start.16 = (f32[4,128]{1,0:T(4,128)S(1)}, f32[4,128]{1,0:T(4,128)S(1)}, u32[]{:S(2)}, u32[]{:S(2)}) collective-permute-start(f32[4,128]{1,0:T(4,128)S(1)} %get-tuple-element.31.lse_ref), channel_id=1, source_target_pairs={{0,16},{8,24},{16,0},{24,8},{1,17},{9,25},{17,1},{25,9},{2,18},{10... | collective-permute-start | bytes 6152 | tf_op jit(solution)/shard_map/ppermute | solution.py:297
  48.5 3.1 %collective-permute-start.15 = (f32[4,128]{1,0:T(4,128)S(1)}, f32[4,128]{1,0:T(4,128)S(1)}, u32[]{:S(2)}, u32[]{:S(2)}) collective-permute-start(f32[4,128]{1,0:T(4,128)S(1)} %get-tuple-element.31.lse_ref), channel_id=1, source_target_pairs={{0,8},{8,0},{16,24},{24,16},{1,9},{9,1},{17,25},{25,17},{2,10},{10... | collective-permute-start | bytes 6152 | tf_op jit(solution)/shard_map/ppermute | solution.py:297
  52.0 13.2 %collective-permute-start.23 = (f32[256,512]{1,0:T(8,128)S(1)}, f32[256,512]{1,0:T(8,128)S(1)}, u32[]{:S(2)}, u32[]{:S(2)}) collective-permute-start(f32[256,512]{1,0:T(8,128)S(1)} %shard_map.70.one_ref), channel_id=1, source_target_pairs={{0,16},{8,24},{16,0},{24,8},{1,17},{9,25},{17,1},{25,9},{2,18},{10... | collective-permute-start | bytes 1572872 | tf_op jit(solution)/shard_map/ppermute | solution.py:297
  52.5 5.7 %collective-permute-start.18 = (f32[4,128]{1,0:T(4,128)S(1)}, f32[4,128]{1,0:T(4,128)S(1)}, u32[]{:S(2)}, u32[]{:S(2)}) collective-permute-start(f32[4,128]{1,0:T(4,128)S(1)} %get-tuple-element.38.refs_5_), channel_id=1, source_target_pairs={{0,5},{1,4},{2,7},{3,6},{4,1},{5,0},{6,3},{7,2},{8,13},{9,12},{10,... | collective-permute-start | bytes 6152 | tf_op jit(solution)/shard_map/ppermute | solution.py:297
  53.9 4.5 %collective-permute-start.19 = (f32[4,128]{1,0:T(4,128)S(1)}, f32[4,128]{1,0:T(4,128)S(1)}, u32[]{:S(2)}, u32[]{:S(2)}) collective-permute-start(f32[4,128]{1,0:T(4,128)S(1)} %get-tuple-element.38.refs_5_), channel_id=1, source_target_pairs={{0,4},{1,5},{2,6},{3,7},{4,0},{5,1},{6,2},{7,3},{8,12},{9,13},{10,... | collective-permute-start | bytes 6152 | tf_op jit(solution)/shard_map/ppermute | solution.py:297
  55.7 3.6 %collective-permute-start.20 = (f32[4,128]{1,0:T(4,128)S(1)}, f32[4,128]{1,0:T(4,128)S(1)}, u32[]{:S(2)}, u32[]{:S(2)}) collective-permute-start(f32[4,128]{1,0:T(4,128)S(1)} %get-tuple-element.38.refs_5_), channel_id=1, source_target_pairs={{0,1},{1,0},{2,3},{3,2},{4,5},{5,4},{6,7},{7,6},{8,9},{9,8},{10,11... | collective-permute-start | bytes 6152 | tf_op jit(solution)/shard_map/ppermute | solution.py:297
  60.2 12.8 %collective-permute-start.21 = (f32[264,512]{1,0:T(8,128)S(1)}, f32[264,512]{1,0:T(8,128)S(1)}, u32[]{:S(2)}, u32[]{:S(2)}) collective-permute-start(f32[264,512]{1,0:T(8,128)S(1)} %shard_map.68), channel_id=1, source_target_pairs={{0,2},{1,3},{2,0},{3,1},{4,6},{5,7},{6,4},{7,5},{8,10},{9,11},{10,... | collective-permute-start | bytes 1622024 | tf_op jit(solution)/shard_map/ppermute | solution.py:297
  65.2 1.4 %collective-permute-start.24 = (f32[64,512]{1,0:T(8,128)S(1)}, f32[64,512]{1,0:T(8,128)S(1)}, u32[]{:S(2)}, u32[]{:S(2)}) collective-permute-start(f32[64,512]{1,0:T(8,128)S(1)} %get-tuple-element.34.refs_0_), channel_id=1, source_target_pairs={{0,8},{8,0},{16,24},{24,16},{1,9},{9,1},{17,25},{25,17},{2,10},{10... | collective-permute-start | bytes 393224 | tf_op jit(solution)/shard_map/ppermute | solution.py:297
  65.3 1.5 %collective-permute-start.25 = (f32[64,512]{1,0:T(8,128)S(1)}, f32[64,512]{1,0:T(8,128)S(1)}, u32[]{:S(2)}, u32[]{:S(2)}) collective-permute-start(f32[64,512]{1,0:T(8,128)S(1)} %get-tuple-element.35.refs_1_), channel_id=1, source_target_pairs={{0,8},{8,0},{16,24},{24,16},{1,9},{9,1},{17,25},{25,17},{2,10},{10... | collective-permute-start | bytes 393224 | tf_op jit(solution)/shard_map/ppermute | solution.py:297
  65.8 1.3 %collective-permute-start.26 = (f32[64,512]{1,0:T(8,128)S(1)}, f32[64,512]{1,0:T(8,128)S(1)}, u32[]{:S(2)}, u32[]{:S(2)}) collective-permute-start(f32[64,512]{1,0:T(8,128)S(1)} %get-tuple-element.36.refs_2_), channel_id=1, source_target_pairs={{0,8},{8,0},{16,24},{24,16},{1,9},{9,1},{17,25},{25,17},{2,10},{10... | collective-permute-start | bytes 393224 | tf_op jit(solution)/shard_map/ppermute | solution.py:297
  65.9 1.5 %collective-permute-start.27 = (f32[64,512]{1,0:T(8,128)S(1)}, f32[64,512]{1,0:T(8,128)S(1)}, u32[]{:S(2)}, u32[]{:S(2)}) collective-permute-start(f32[64,512]{1,0:T(8,128)S(1)} %get-tuple-element.37.refs_3_), channel_id=1, source_target_pairs={{0,8},{8,0},{16,24},{24,16},{1,9},{9,1},{17,25},{25,17},{2,10},{10... | collective-permute-start | bytes 393224 | tf_op jit(solution)/shard_map/ppermute | solution.py:297

commit v8 on v7

--- a/solution.py
+++ b/solution.py
@@ -110,7 +110,7 @@
 
 
 def early_rows(rows):
-    return rows * 7 // 128 * 8
+    return rows // 2
 
 
 def targets_kernel(n_parts, tile_ref, lt_ref, sqy_ref, *refs):
@@ -126,10 +126,11 @@
         lse_ref[pl.ds(b, 1), :] = over_targets(tile_ref[:, pl.ds(b * LANES, LANES)] + bias)
 
 
-def merge_kernel(one_ref, two_ref, *refs):
+def merge_kernel(n_parts, *refs):
+    parts, refs = refs[:n_parts], refs[n_parts:]
     n_pieces = len(refs) // 2
     pieces, (out_ref, pack_ref, *copies) = refs[:n_pieces], refs[n_pieces:]
-    out_ref[...] = merge_all([one_ref[...], two_ref[...]])
+    out_ref[...] = merge_all([ref[...] for ref in parts])
     rows = pieces[-1].shape[0]
     pack_ref[:rows, :] = pieces[-1][...]
     pack_ref[rows:, :] = pieces[0][: early_rows(rows), :]
@@ -164,14 +165,15 @@
     n_rows = mine_ref.shape[0] // LANES
     core = lax.axis_index("row") % 2
     for out_ref, place in ((sent_ref, 1 - core), (mine_ref, core)):
-        columns = []
+        columns, totals, weights = [], [], []
         for j in range(n_rows):
             at = pl.ds(pl.multiple_of((place * n_rows + j) * LANES, LANES), LANES)
             peak, total, exps = over_sources(tile_ref, at, bias)
             columns.append(peak + jnp.log2(total))
-            weights = jnp.concatenate([block.astype(jnp.bfloat16) for block in exps], axis=1)
-            mean = jnp.dot(weights, x, preferred_element_type=jnp.float32)
-            out_ref[pl.ds(j * LANES, LANES), :] = mean * (1.0 / total)
+            totals.append(total)
+            weights.append(jnp.concatenate([block.astype(jnp.bfloat16) for block in exps], axis=1))
+        mean = jnp.dot(jnp.concatenate(weights, axis=0), x, preferred_element_type=jnp.float32)
+        out_ref[...] = mean * (1.0 / jnp.concatenate(totals, axis=0))
         lse_ref[pl.ds(place * n_rows, n_rows), :] = to_dense(columns)
 
 
@@ -338,21 +340,23 @@
                 tile, lt, sqy, *parts, *[pieces[k] for k in apart[2:]], early[-1],
             )
             late = along_y(late)
-        for distance in bits_of(n_col)[:-1]:
-            came = swap(lse, "col", distance)
-            if step > 0 or distance != n_x:
-                lse = merge_all([lse, came])
-                continue
+        if step > 0:
+            for distance in bits_of(2 * n_x):
+                lse = merge_all([lse, swap(lse, "col", distance)])
+        else:
+            near = [lse] + [swap(lse, "col", distance) for distance in range(2 * n_x - 1, 0, -1)]
             far = [k for k in pieces if k > 0]
             lse, early, *copies = call(
-                merge_kernel,
+                lambda *refs: merge_kernel(2 * n_x, *refs),
                 (src_dense, f32(part.shape[0] + cut, width), *(part,) * len(far)),
-                lse, came, *[pieces[k] for k in far], early,
+                *near, *[pieces[k] for k in far], early,
             )
             early = along_y(early)
             pieces |= dict(zip(far, copies))
             for bit in bits_of(n_x)[::-1]:
                 pieces |= {k ^ bit: swap(piece, "col", bit) for k, piece in pieces.items() if k ^ bit != 1}
+        for distance in [bit for bit in bits_of(n_col) if bit > n_x][:-1]:
+            lse = merge_all([lse, swap(lse, "col", distance)])
         parts = [lse, swap(lse, "col", n_col // 2)]
         if step < ITERS - 1:
             lse = call(lambda *refs: sources_kernel(2, *refs), tgt_dense, tile, ls, sqx, *parts)

time: 74.3 us -> 74.2 us (level)
    ppermute x28 -> x29, starting transfers between devices: 29.2 us -> 29 us  [swap(): return lax.ppermute(value, axis, [(i, i ^ distance) for i in range(n)])]
    ppermute x28 -> x29, waiting for transfers between devices: 28.6 us -> 28.5 us  [swap(): return lax.ppermute(value, axis, [(i, i ^ distance) for i in range(n)])]
    unnamed x14 -> x12, local copies, waits for them, and re-layouts: 3.33 us -> 3.32 us
  transfers between devices with their start and end apart: 28 -> 29, of which waited for: 18 -> 17; matrix products, arithmetic and copies ran while one was open for 0% -> 0% of each run, Pallas kernels for 11% -> 11%
where the time goes in v8:
time: 74.2 us; the launch traced here: 74 us
  starting transfers between devices  29 us (39%)
  waiting for transfers between devices  28.5 us (38%)
  Pallas kernels  12.3 us (17%)
  local copies, waits for them, and re-layouts  3.32 us (4%)
  between operations  0.79 us (1%)
    ppermute x29, starting transfers between devices, swap(): return lax.ppermute(value, axis, [(i, i ^ distance) for i in range(n)])  29 us
    ppermute x29, waiting for transfers between devices, swap(): return lax.ppermute(value, axis, [(i, i ^ distance) for i in range(n)])  28.5 us
    pallas_call x14, Pallas kernels, call(): pl.pallas_call(kernel, out_shape=out_shape, in_specs=in_specs or [VMEM] *...  12.3 us
    unnamed x12, local copies, waits for them, and re-layouts  3.32 us
  transfers between devices with their start and end apart: 29, of which 17 were waited for; matrix products, arithmetic and copies ran while one was open for 0% of the time, Pallas kernels for 11%

profile of v8, /device:TPU:0, one launch (start us, length us, event | category | flops | bytes accessed | tf_op | source)
XLA Modules:
  0.0 74.0 jit_solution(903868867702472412)
XLA Ops:
  0.6 0.0 copy-start.2
  0.6 1.0 %copy-done.2 = bf16[512,512]{1,0:T(8,128)(2,1)S(1)} copy-done((bf16[512,512]{1,0:T(8,128)(2,1)S(1)}, bf16[512,512]{1,0:T(8,128)(2,1)}, u32[]{:S(2)}) %copy-start.2) | copy-done | bytes 524312
  1.7 4.1 %collective-permute-start.3 = (f32[128,512]{1,0:T(8,128)S(1)}, f32[128,512]{1,0:T(8,128)S(1)}, u32[]{:S(2)}, u32[]{:S(2)}) collective-permute-start(f32[128,512]{1,0:T(8,128)S(1)} %shard_map.61), channel_id=1, source_target_pairs={{0,4},{1,5},{2,6},{3,7},{4,0},{5,1},{6,2},{7,3},{8,12},{9,13},{10,... | collective-permute-start | bytes 786440 | tf_op jit(solution)/shard_map/ppermute | solution.py:299
  5.8 1.5 %collective-permute-start.4 = (f32[128,512]{1,0:T(8,128)S(1)}, f32[128,512]{1,0:T(8,128)S(1)}, u32[]{:S(2)}, u32[]{:S(2)}) collective-permute-start(f32[128,512]{1,0:T(8,128)S(1)} %shard_map.61), channel_id=1, source_target_pairs={{0,1},{1,0},{2,3},{3,2},{4,5},{5,4},{6,7},{7,6},{8,9},{9,8},{10,11... | collective-permute-start | bytes 786440 | tf_op jit(solution)/shard_map/ppermute | solution.py:299
  7.3 1.6 %copy-done = bf16[2048,512]{1,0:T(8,128)(2,1)S(1)} copy-done((bf16[2048,512]{1,0:T(8,128)(2,1)S(1)}, bf16[2048,512]{1,0:T(8,128)(2,1)}, u32[]{:S(2)}) %copy-start) | copy-done | bytes 2097176
  8.9 0.7 copy-done.5
  9.6 1.9 %shard_map.59 = (f32[512,2048]{1,0:T(8,128)S(1)}, f32[16,128]{1,0:T(8,128)S(1)}, f32[4,128]{1,0:T(4,128)S(1)}) custom-call(bf16[512,512]{1,0:T(8,128)(2,1)S(1)} %copy-done.2, bf16[2048,512]{1,0:T(8,128)(2,1)S(1)} %copy-done, f32[4,128]{1,0:T(4,128)S(1)} %bitcast.5), custom_call_target="tpu_custom_call" | custom-call | tf_op jit(solution)/shard_map/pallas_call | solution.py:22
  11.5 1.6 %collective-permute-start = (f32[16,128]{1,0:T(8,128)S(1)}, f32[16,128]{1,0:T(8,128)S(1)}, u32[]{:S(2)}, u32[]{:S(2)}) collective-permute-start(f32[16,128]{1,0:T(8,128)S(1)} %get-tuple-element.22.refs_0_), channel_id=1, source_target_pairs={{0,3},{1,2},{2,1},{3,0},{4,7},{5,6},{6,5},{7,4},{8,11},{9,10},{10,... | collective-permute-start | bytes 24584 | tf_op jit(solution)/shard_map/ppermute | solution.py:299
  13.1 0.4 collective-permute-start.1
  13.5 1.5 %collective-permute-start.2 = (f32[16,128]{1,0:T(8,128)S(1)}, f32[16,128]{1,0:T(8,128)S(1)}, u32[]{:S(2)}, u32[]{:S(2)}) collective-permute-start(f32[16,128]{1,0:T(8,128)S(1)} %get-tuple-element.22.refs_0_), channel_id=1, source_target_pairs={{0,1},{1,0},{2,3},{3,2},{4,5},{5,4},{6,7},{7,6},{8,9},{9,8},{10,11... | collective-permute-start | bytes 24584 | tf_op jit(solution)/shard_map/ppermute | solution.py:299
  15.0 3.9 %collective-permute-done.refs_1_ = f32[16,128]{1,0:T(8,128)S(1)} collective-permute-done((f32[16,128]{1,0:T(8,128)S(1)}, f32[16,128]{1,0:T(8,128)S(1)}, u32[]{:S(2)}, u32[]{:S(2)}) %collective-permute-start) | collective-permute-done | bytes 8224 | tf_op jit(solution)/shard_map/ppermute | solution.py:299
  19.0 0.0 collective-permute-done.2.refs_3_
  19.0 0.0 collective-permute-done.3.refs_4_
  19.0 1.6 %collective-permute-start.10 = (f32[192,512]{1,0:T(8,128)S(1)}, f32[192,512]{1,0:T(8,128)S(1)}, u32[]{:S(2)}, u32[]{:S(2)}) collective-permute-start(f32[192,512]{1,0:T(8,128)S(1)} %get-tuple-element.25.refs_6_), channel_id=1, source_target_pairs={{0,16},{8,24},{16,0},{24,8},{1,17},{9,25},{17,1},{25,9},{2,18},{10... | collective-permute-start | bytes 1179656 | tf_op jit(solution)/shard_map/ppermute | solution.py:299
  20.6 0.6 collective-permute-start.9
  21.3 0.5 shard_map.60.refs_2_.refs_3_
  21.8 4.0 %collective-permute-done.5.refs_4_ = f32[16,128]{1,0:T(8,128)S(1)} collective-permute-done((f32[16,128]{1,0:T(8,128)S(1)}, f32[16,128]{1,0:T(8,128)S(1)}, u32[]{:S(2)}, u32[]{:S(2)}) %collective-permute-start.5) | collective-permute-done | bytes 8224 | tf_op jit(solution)/shard_map/ppermute | solution.py:299
  25.8 1.0 %shard_map.63.refs_3_ = f32[4,128]{1,0:T(4,128)S(1)} custom-call(f32[512,2048]{1,0:T(8,128)S(1)} %get-tuple-element.20.refs_0_, f32[16,128]{1,0:T(8,128)S(1)} %bitcast.3, f32[16,128]{1,0:T(8,128)S(1)} %shard_map.60.refs_2_.refs_3_, f32[16,128]{1,0:T(8,128)S(1)} %get-tuple-element.23.refs_3_, f32[16,128]{1,0:T(8,128)S(1)} %collective-permute-done.5.refs_4_), custom_call_target="tpu_custom_call" | custom-call | tf_op jit(solution)/shard_map/pallas_call | solution.py:22
  26.8 0.0 collective-permute-start.6
  26.9 0.6 collective-permute-start.7
  27.4 1.3 %collective-permute-start.8 = (f32[4,128]{1,0:T(4,128)S(1)}, f32[4,128]{1,0:T(4,128)S(1)}, u32[]{:S(2)}, u32[]{:S(2)}) collective-permute-start(f32[4,128]{1,0:T(4,128)S(1)} %shard_map.63.refs_3_), channel_id=1, source_target_pairs={{0,24},{8,16},{16,8},{24,0},{1,25},{9,17},{17,9},{25,1},{2,26},{10... | collective-permute-start | bytes 6152 | tf_op jit(solution)/shard_map/ppermute | solution.py:299
  28.7 1.8 %collective-permute-done.7.refs_5_ = f32[4,128]{1,0:T(4,128)S(1)} collective-permute-done((f32[4,128]{1,0:T(4,128)S(1)}, f32[4,128]{1,0:T(4,128)S(1)}, u32[]{:S(2)}, u32[]{:S(2)}) %collective-permute-start.7) | collective-permute-done | bytes 2080 | tf_op jit(solution)/shard_map/ppermute | solution.py:299
  30.5 1.1 %shard_map.64 = (f32[16,128]{1,0:T(8,128)S(1)}, f32[192,512]{1,0:T(8,128)S(1)}) custom-call(f32[512,2048]{1,0:T(8,128)S(1)} %get-tuple-element.20.refs_0_, f32[4,128]{1,0:T(4,128)S(1)} %bitcast.6, f32[4,128]{1,0:T(4,128)S(1)} %get-tuple-element.21.refs_2_, f32[4,128]{1,0:T(4,128)S(1)} %shard_map.63.refs_3_, f32[4,128]{1,0:T(4,128)S(1)} %collective-permute-done.6.refs_4_, ...), custom_call_target="tpu_custom_call" | custom-call | tf_op jit(solution)/shard_map/pallas_call | solution.py:22
  31.7 1.4 %collective-permute-start.11 = (f32[16,128]{1,0:T(8,128)S(1)}, f32[16,128]{1,0:T(8,128)S(1)}, u32[]{:S(2)}, u32[]{:S(2)}) collective-permute-start(f32[16,128]{1,0:T(8,128)S(1)} %get-tuple-element.26), channel_id=1, source_target_pairs={{0,1},{1,0},{2,3},{3,2},{4,5},{5,4},{6,7},{7,6},{8,9},{9,8},{10,11... | collective-permute-start | bytes 24584 | tf_op jit(solution)/shard_map/ppermute | solution.py:299
  33.1 1.4 %collective-permute-start.14 = (f32[192,512]{1,0:T(8,128)S(1)}, f32[192,512]{1,0:T(8,128)S(1)}, u32[]{:S(2)}, u32[]{:S(2)}) collective-permute-start(f32[192,512]{1,0:T(8,128)S(1)} %get-tuple-element.27.refs_8_), channel_id=1, source_target_pairs={{0,16},{8,24},{16,0},{24,8},{1,17},{9,25},{17,1},{25,9},{2,18},{10... | collective-permute-start | bytes 1179656 | tf_op jit(solution)/shard_map/ppermute | solution.py:299
  34.5 0.8 %collective-permute-done.11 = f32[16,128]{1,0:T(8,128)S(1)} collective-permute-done((f32[16,128]{1,0:T(8,128)S(1)}, f32[16,128]{1,0:T(8,128)S(1)}, u32[]{:S(2)}, u32[]{:S(2)}) %collective-permute-start.11) | collective-permute-done | bytes 8224 | tf_op jit(solution)/shard_map/ppermute | solution.py:299
  35.4 1.0 %collective-permute-start.12 = (f32[16,128]{1,0:T(8,128)S(1)}, f32[16,128]{1,0:T(8,128)S(1)}, u32[]{:S(2)}, u32[]{:S(2)}) collective-permute-start(f32[16,128]{1,0:T(8,128)S(1)} %multiply_add_fusion.1), channel_id=1, source_target_pairs={{0,2},{1,3},{2,0},{3,1},{4,6},{5,7},{6,4},{7,5},{8,10},{9,11},{10,... | collective-permute-start | bytes 24584 | tf_op jit(solution)/shard_map/ppermute | solution.py:299
  36.4 2.7 %collective-permute-done.12 = f32[16,128]{1,0:T(8,128)S(1)} collective-permute-done((f32[16,128]{1,0:T(8,128)S(1)}, f32[16,128]{1,0:T(8,128)S(1)}, u32[]{:S(2)}, u32[]{:S(2)}) %collective-permute-start.12) | collective-permute-done | bytes 8224 | tf_op jit(solution)/shard_map/ppermute | solution.py:299
  39.1 0.0 copy-start.3
  39.1 1.9 %collective-permute-start.13 = (f32[16,128]{1,0:T(8,128)S(1)}, f32[16,128]{1,0:T(8,128)S(1)}, u32[]{:S(2)}, u32[]{:S(2)}) collective-permute-start(f32[16,128]{1,0:T(8,128)S(1)} %multiply_add_fusion.refs_4_), channel_id=1, source_target_pairs={{0,4},{1,5},{2,6},{3,7},{4,0},{5,1},{6,2},{7,3},{8,12},{9,13},{10,... | collective-permute-start | bytes 24584 | tf_op jit(solution)/shard_map/ppermute | solution.py:299
  41.1 2.7 %collective-permute-done.13.refs_5_ = f32[16,128]{1,0:T(8,128)S(1)} collective-permute-done((f32[16,128]{1,0:T(8,128)S(1)}, f32[16,128]{1,0:T(8,128)S(1)}, u32[]{:S(2)}, u32[]{:S(2)}) %collective-permute-start.13) | collective-permute-done | bytes 8224 | tf_op jit(solution)/shard_map/ppermute | solution.py:299
  43.7 0.2 collective-permute-done.14.refs_9_
  43.9 2.1 %shard_map.65 = (f32[4,128]{1,0:T(4,128)S(1)}, f32[256,512]{1,0:T(8,128)S(1)}, f32[256,512]{1,0:T(8,128)S(1)}, f32[3,2,128,512]{3,2,1,0:T(8,128)S(1)}) custom-call(f32[512,2048]{1,0:T(8,128)S(1)} %get-tuple-element.20.refs_0_, bf16[2048,512]{1,0:T(8,128)(2,1)S(1)} %copy-done.1, f32[16,128]{1,0:T(8,128)S(1)} %bitcast.4, ...), custom_call_target="tpu_custom_call" | custom-call | tf_op jit(solution)/shard_map/pallas_call | solution.py:22
  46.1 0.1 collective-permute-start.15
  46.2 0.5 collective-permute-start.23
  46.7 1.2 %collective-permute-start.18 = (f32[4,128]{1,0:T(4,128)S(1)}, f32[4,128]{1,0:T(4,128)S(1)}, u32[]{:S(2)}, u32[]{:S(2)}) collective-permute-start(f32[4,128]{1,0:T(4,128)S(1)} %get-tuple-element.31.lse_ref), channel_id=1, source_target_pairs={{0,24},{8,16},{16,8},{24,0},{1,25},{9,17},{17,9},{25,1},{2,26},{10... | collective-permute-start | bytes 6152 | tf_op jit(solution)/shard_map/ppermute | solution.py:299
  47.9 0.5 collective-permute-start.17
  48.4 0.2 collective-permute-start.16
  48.5 1.1 %collective-permute-done.18 = f32[4,128]{1,0:T(4,128)S(1)} collective-permute-done((f32[4,128]{1,0:T(4,128)S(1)}, f32[4,128]{1,0:T(4,128)S(1)}, u32[]{:S(2)}, u32[]{:S(2)}) %collective-permute-start.18) | collective-permute-done | bytes 2080 | tf_op jit(solution)/shard_map/ppermute | solution.py:299
  49.7 1.8 %collective-permute-done.17 = f32[4,128]{1,0:T(4,128)S(1)} collective-permute-done((f32[4,128]{1,0:T(4,128)S(1)}, f32[4,128]{1,0:T(4,128)S(1)}, u32[]{:S(2)}, u32[]{:S(2)}) %collective-permute-start.17) | collective-permute-done | bytes 2080 | tf_op jit(solution)/shard_map/ppermute | solution.py:299
  51.5 0.3 shard_map.70.one_ref
  51.8 0.6 collective-permute-start.24
  52.4 1.6 %collective-permute-start.19 = (f32[4,128]{1,0:T(4,128)S(1)}, f32[4,128]{1,0:T(4,128)S(1)}, u32[]{:S(2)}, u32[]{:S(2)}) collective-permute-start(f32[4,128]{1,0:T(4,128)S(1)} %get-tuple-element.38.refs_5_), channel_id=1, source_target_pairs={{0,5},{1,4},{2,7},{3,6},{4,1},{5,0},{6,3},{7,2},{8,13},{9,12},{10,... | collective-permute-start | bytes 6152 | tf_op jit(solution)/shard_map/ppermute | solution.py:299
  54.0 1.9 %collective-permute-start.20 = (f32[4,128]{1,0:T(4,128)S(1)}, f32[4,128]{1,0:T(4,128)S(1)}, u32[]{:S(2)}, u32[]{:S(2)}) collective-permute-start(f32[4,128]{1,0:T(4,128)S(1)} %get-tuple-element.38.refs_5_), channel_id=1, source_target_pairs={{0,4},{1,5},{2,6},{3,7},{4,0},{5,1},{6,2},{7,3},{8,12},{9,13},{10,... | collective-permute-start | bytes 6152 | tf_op jit(solution)/shard_map/ppermute | solution.py:299
  55.9 0.8 %collective-permute-start.21 = (f32[4,128]{1,0:T(4,128)S(1)}, f32[4,128]{1,0:T(4,128)S(1)}, u32[]{:S(2)}, u32[]{:S(2)}) collective-permute-start(f32[4,128]{1,0:T(4,128)S(1)} %get-tuple-element.38.refs_5_), channel_id=1, source_target_pairs={{0,1},{1,0},{2,3},{3,2},{4,5},{5,4},{6,7},{7,6},{8,9},{9,8},{10,11... | collective-permute-start | bytes 6152 | tf_op jit(solution)/shard_map/ppermute | solution.py:299
  56.8 1.3 %shard_map.66 = (bf16[2048,512]{1,0:T(8,128)(2,1)S(1)}, f32[512,2048]{1,0:T(8,128)S(1)}) custom-call(bf16[2048,512]{1,0:T(8,128)(2,1)S(1)} %copy-done.1, bf16[512,512]{1,0:T(8,128)(2,1)S(1)} %copy-done.3, f32[3,2,128,512]{3,2,1,0:T(8,128)S(1)} %get-tuple-element.28.refs_2_, f32[3,2,128,512]{3,2,1,0:T(8,128)S(1)} %collective-permute-done.15.refs_3_), custom_call_target="tpu_custom_call" | custom-call | tf_op jit(solution)/shard_map/pallas_call | solution.py:22
  58.1 0.4 collective-permute-done.20.refs_3_
  58.5 1.0 %collective-permute-done.21.refs_4_ = f32[4,128]{1,0:T(4,128)S(1)} collective-permute-done((f32[4,128]{1,0:T(4,128)S(1)}, f32[4,128]{1,0:T(4,128)S(1)}, u32[]{:S(2)}, u32[]{:S(2)}) %collective-permute-start.21) | collective-permute-done | bytes 2080 | tf_op jit(solution)/shard_map/ppermute | solution.py:299
  59.5 0.9 %shard_map.68 = f32[264,512]{1,0:T(8,128)S(1)} custom-call(f32[512,2048]{1,0:T(8,128)S(1)} %get-tuple-element.29.refs_0_, bf16[2048,512]{1,0:T(8,128)(2,1)S(1)} %get-tuple-element.30.refs_1_, f32[4,128]{1,0:T(4,128)S(1)} %collective-permute-done.19.refs_2_, f32[4,128]{1,0:T(4,128)S(1)} %collective-permute-done.20.refs_3_, ...), custom_call_target="tpu_custom_call" | custom-call | tf_op jit(solution)/shard_map/pallas_call | solution.py:22
  60.4 1.4 %collective-permute-start.22 = (f32[264,512]{1,0:T(8,128)S(1)}, f32[264,512]{1,0:T(8,128)S(1)}, u32[]{:S(2)}, u32[]{:S(2)}) collective-permute-start(f32[264,512]{1,0:T(8,128)S(1)} %shard_map.68), channel_id=1, source_target_pairs={{0,2},{1,3},{2,0},{3,1},{4,6},{5,7},{6,4},{7,5},{8,10},{9,11},{10,... | collective-permute-start | bytes 1622024 | tf_op jit(solution)/shard_map/ppermute | solution.py:299
  61.8 3.2 %collective-permute-done.24.two_ref = f32[256,512]{1,0:T(8,128)S(1)} collective-permute-done((f32[256,512]{1,0:T(8,128)S(1)}, f32[256,512]{1,0:T(8,128)S(1)}, u32[]{:S(2)}, u32[]{:S(2)}) %collective-permute-start.24) | collective-permute-done | bytes 524320 | tf_op jit(solution)/shard_map/ppermute | solution.py:299
  65.0 0.1 shard_map.71
  65.0 0.1 collective-permute-start.25
  65.1 0.5 collective-permute-start.26
  65.6 0.1 collective-permute-start.27
  65.7 0.4 collective-permute-start.28
  66.1 0.3 collective-permute-done.25.refs_4_
  66.5 0.2 collective-permute-done.26.refs_5_
  66.7 0.3 collective-permute-done.27.refs_6_
  67.0 0.2 collective-permute-done.28.refs_7_
  67.2 1.0 %shard_map.72 = f32[512,512]{1,0:T(8,128)} custom-call(f32[64,512]{1,0:T(8,128)S(1)} %get-tuple-element.34.refs_0_, f32[64,512]{1,0:T(8,128)S(1)} %get-tuple-element.35.refs_1_, f32[64,512]{1,0:T(8,128)S(1)} %get-tuple-element.36.refs_2_, f32[64,512]{1,0:T(8,128)S(1)} %get-tuple-element.37.refs_3_, f32[64,512]{1,0:T(8,128)S(1)} %collective-permute-done.25.refs_4_, ...), custom_call_target="tpu_custom_call" | custom-call | tf_op jit(solution)/shard_map/pallas_call | solution.py:22
  68.2 0.9 %shard_map.67.refs_0_ = f32[264,512]{1,0:T(8,128)S(1)} custom-call(f32[512,2048]{1,0:T(8,128)S(1)} %get-tuple-element.29.refs_0_, bf16[2048,512]{1,0:T(8,128)(2,1)S(1)} %get-tuple-element.30.refs_1_, f32[4,128]{1,0:T(4,128)S(1)} %collective-permute-done.19.refs_2_, f32[4,128]{1,0:T(4,128)S(1)} %collective-permute-done.20.refs_3_, ...), custom_call_target="tpu_custom_call" | custom-call | tf_op jit(solution)/shard_map/pallas_call | solution.py:22
  69.1 3.8 %collective-permute-done.22.refs_1_ = f32[264,512]{1,0:T(8,128)S(1)} collective-permute-done((f32[264,512]{1,0:T(8,128)S(1)}, f32[264,512]{1,0:T(8,128)S(1)}, u32[]{:S(2)}, u32[]{:S(2)}) %collective-permute-start.22) | collective-permute-done | bytes 540704 | tf_op jit(solution)/shard_map/ppermute | solution.py:299
  72.9 1.1 %shard_map.69 = f32[256,512]{1,0:T(8,128)} custom-call(f32[264,512]{1,0:T(8,128)S(1)} %shard_map.67.refs_0_, f32[264,512]{1,0:T(8,128)S(1)} %collective-permute-done.22.refs_1_), custom_call_target="tpu_custom_call" | custom-call | tf_op jit(solution)/shard_map/pallas_call | solution.py:22
  (23 shorter events, 0.2 us)
Async XLA Ops:
  0.6 1.0 %copy-start.2 = (bf16[512,512]{1,0:T(8,128)(2,1)S(1)}, bf16[512,512]{1,0:T(8,128)(2,1)}, u32[]{:S(2)}) copy-start(bf16[512,512]{1,0:T(8,128)(2,1)} %refs_1_.3) | copy-start | bytes 1572868
  1.7 17.3 %collective-permute-start.3 = (f32[128,512]{1,0:T(8,128)S(1)}, f32[128,512]{1,0:T(8,128)S(1)}, u32[]{:S(2)}, u32[]{:S(2)}) collective-permute-start(f32[128,512]{1,0:T(8,128)S(1)} %shard_map.61), channel_id=1, source_target_pairs={{0,4},{1,5},{2,6},{3,7},{4,0},{5,1},{6,2},{7,3},{8,12},{9,13},{10,... | collective-permute-start | bytes 786440 | tf_op jit(solution)/shard_map/ppermute | solution.py:299
  5.8 13.2 %collective-permute-start.4 = (f32[128,512]{1,0:T(8,128)S(1)}, f32[128,512]{1,0:T(8,128)S(1)}, u32[]{:S(2)}, u32[]{:S(2)}) collective-permute-start(f32[128,512]{1,0:T(8,128)S(1)} %shard_map.61), channel_id=1, source_target_pairs={{0,1},{1,0},{2,3},{3,2},{4,5},{5,4},{6,7},{7,6},{8,9},{9,8},{10,11... | collective-permute-start | bytes 786440 | tf_op jit(solution)/shard_map/ppermute | solution.py:299
  7.3 1.6 %copy-start = (bf16[2048,512]{1,0:T(8,128)(2,1)S(1)}, bf16[2048,512]{1,0:T(8,128)(2,1)}, u32[]{:S(2)}) copy-start(bf16[2048,512]{1,0:T(8,128)(2,1)} %refs_0_.1) | copy-start | bytes 6291460
  8.9 0.7 copy-start.5
  9.6 11.7 %copy-start.1 = (bf16[2048,512]{1,0:T(8,128)(2,1)S(1)}, bf16[2048,512]{1,0:T(8,128)(2,1)}, u32[]{:S(2)}) copy-start(bf16[2048,512]{1,0:T(8,128)(2,1)} %refs_0_.1) | copy-start | bytes 6291460
  9.6 16.3 %copy-start.4 = (f32[2048]{0:T(1024)S(1)}, f32[2048]{0:T(1024)}, u32[]{:S(2)}) copy-start(f32[2048]{0:T(1024)} %param.6) | copy-start | bytes 24580
  11.5 7.5 %collective-permute-start = (f32[16,128]{1,0:T(8,128)S(1)}, f32[16,128]{1,0:T(8,128)S(1)}, u32[]{:S(2)}, u32[]{:S(2)}) collective-permute-start(f32[16,128]{1,0:T(8,128)S(1)} %get-tuple-element.22.refs_0_), channel_id=1, source_target_pairs={{0,3},{1,2},{2,1},{3,0},{4,7},{5,6},{6,5},{7,4},{8,11},{9,10},{10,... | collective-permute-start | bytes 24584 | tf_op jit(solution)/shard_map/ppermute | solution.py:299
  13.1 5.9 %collective-permute-start.1 = (f32[16,128]{1,0:T(8,128)S(1)}, f32[16,128]{1,0:T(8,128)S(1)}, u32[]{:S(2)}, u32[]{:S(2)}) collective-permute-start(f32[16,128]{1,0:T(8,128)S(1)} %get-tuple-element.22.refs_0_), channel_id=1, source_target_pairs={{0,2},{1,3},{2,0},{3,1},{4,6},{5,7},{6,4},{7,5},{8,10},{9,11},{10,... | collective-permute-start | bytes 24584 | tf_op jit(solution)/shard_map/ppermute | solution.py:299
  13.5 5.4 %collective-permute-start.2 = (f32[16,128]{1,0:T(8,128)S(1)}, f32[16,128]{1,0:T(8,128)S(1)}, u32[]{:S(2)}, u32[]{:S(2)}) collective-permute-start(f32[16,128]{1,0:T(8,128)S(1)} %get-tuple-element.22.refs_0_), channel_id=1, source_target_pairs={{0,1},{1,0},{2,3},{3,2},{4,5},{5,4},{6,7},{7,6},{8,9},{9,8},{10,11... | collective-permute-start | bytes 24584 | tf_op jit(solution)/shard_map/ppermute | solution.py:299
  19.0 11.5 %collective-permute-start.10 = (f32[192,512]{1,0:T(8,128)S(1)}, f32[192,512]{1,0:T(8,128)S(1)}, u32[]{:S(2)}, u32[]{:S(2)}) collective-permute-start(f32[192,512]{1,0:T(8,128)S(1)} %get-tuple-element.25.refs_6_), channel_id=1, source_target_pairs={{0,16},{8,24},{16,0},{24,8},{1,17},{9,25},{17,1},{25,9},{2,18},{10... | collective-permute-start | bytes 1179656 | tf_op jit(solution)/shard_map/ppermute | solution.py:299
  20.6 9.9 %collective-permute-start.9 = (f32[128,512]{1,0:T(8,128)S(1)}, f32[128,512]{1,0:T(8,128)S(1)}, u32[]{:S(2)}, u32[]{:S(2)}) collective-permute-start(f32[128,512]{1,0:T(8,128)S(1)} %get-tuple-element.24.refs_7_), channel_id=1, source_target_pairs={{0,1},{1,0},{2,3},{3,2},{4,5},{5,4},{6,7},{7,6},{8,9},{9,8},{10,11... | collective-permute-start | bytes 786440 | tf_op jit(solution)/shard_map/ppermute | solution.py:299
  21.3 4.5 %collective-permute-start.5 = (f32[16,128]{1,0:T(8,128)S(1)}, f32[16,128]{1,0:T(8,128)S(1)}, u32[]{:S(2)}, u32[]{:S(2)}) collective-permute-start(f32[16,128]{1,0:T(8,128)S(1)} %get-tuple-element.23.refs_3_), channel_id=1, source_target_pairs={{0,4},{1,5},{2,6},{3,7},{4,0},{5,1},{6,2},{7,3},{8,12},{9,13},{10,... | collective-permute-start | bytes 24584 | tf_op jit(solution)/shard_map/ppermute | solution.py:299
  26.8 1.9 %collective-permute-start.6 = (f32[4,128]{1,0:T(4,128)S(1)}, f32[4,128]{1,0:T(4,128)S(1)}, u32[]{:S(2)}, u32[]{:S(2)}) collective-permute-start(f32[4,128]{1,0:T(4,128)S(1)} %shard_map.63.refs_3_), channel_id=1, source_target_pairs={{0,8},{8,0},{16,24},{24,16},{1,9},{9,1},{17,25},{25,17},{2,10},{10... | collective-permute-start | bytes 6152 | tf_op jit(solution)/shard_map/ppermute | solution.py:299
  26.9 3.7 %collective-permute-start.7 = (f32[4,128]{1,0:T(4,128)S(1)}, f32[4,128]{1,0:T(4,128)S(1)}, u32[]{:S(2)}, u32[]{:S(2)}) collective-permute-start(f32[4,128]{1,0:T(4,128)S(1)} %shard_map.63.refs_3_), channel_id=1, source_target_pairs={{0,16},{8,24},{16,0},{24,8},{1,17},{9,25},{17,1},{25,9},{2,18},{10... | collective-permute-start | bytes 6152 | tf_op jit(solution)/shard_map/ppermute | solution.py:299
  27.4 3.1 %collective-permute-start.8 = (f32[4,128]{1,0:T(4,128)S(1)}, f32[4,128]{1,0:T(4,128)S(1)}, u32[]{:S(2)}, u32[]{:S(2)}) collective-permute-start(f32[4,128]{1,0:T(4,128)S(1)} %shard_map.63.refs_3_), channel_id=1, source_target_pairs={{0,24},{8,16},{16,8},{24,0},{1,25},{9,17},{17,9},{25,1},{2,26},{10... | collective-permute-start | bytes 6152 | tf_op jit(solution)/shard_map/ppermute | solution.py:299
  31.7 3.7 %collective-permute-start.11 = (f32[16,128]{1,0:T(8,128)S(1)}, f32[16,128]{1,0:T(8,128)S(1)}, u32[]{:S(2)}, u32[]{:S(2)}) collective-permute-start(f32[16,128]{1,0:T(8,128)S(1)} %get-tuple-element.26), channel_id=1, source_target_pairs={{0,1},{1,0},{2,3},{3,2},{4,5},{5,4},{6,7},{7,6},{8,9},{9,8},{10,11... | collective-permute-start | bytes 24584 | tf_op jit(solution)/shard_map/ppermute | solution.py:299
  33.1 10.8 %collective-permute-start.14 = (f32[192,512]{1,0:T(8,128)S(1)}, f32[192,512]{1,0:T(8,128)S(1)}, u32[]{:S(2)}, u32[]{:S(2)}) collective-permute-start(f32[192,512]{1,0:T(8,128)S(1)} %get-tuple-element.27.refs_8_), channel_id=1, source_target_pairs={{0,16},{8,24},{16,0},{24,8},{1,17},{9,25},{17,1},{25,9},{2,18},{10... | collective-permute-start | bytes 1179656 | tf_op jit(solution)/shard_map/ppermute | solution.py:299
  35.4 3.7 %collective-permute-start.12 = (f32[16,128]{1,0:T(8,128)S(1)}, f32[16,128]{1,0:T(8,128)S(1)}, u32[]{:S(2)}, u32[]{:S(2)}) collective-permute-start(f32[16,128]{1,0:T(8,128)S(1)} %multiply_add_fusion.1), channel_id=1, source_target_pairs={{0,2},{1,3},{2,0},{3,1},{4,6},{5,7},{6,4},{7,5},{8,10},{9,11},{10,... | collective-permute-start | bytes 24584 | tf_op jit(solution)/shard_map/ppermute | solution.py:299
  39.1 17.6 %copy-start.3 = (bf16[512,512]{1,0:T(8,128)(2,1)S(1)}, bf16[512,512]{1,0:T(8,128)(2,1)}, u32[]{:S(2)}) copy-start(bf16[512,512]{1,0:T(8,128)(2,1)} %refs_1_.3) | copy-start | bytes 1572868
  39.1 4.6 %collective-permute-start.13 = (f32[16,128]{1,0:T(8,128)S(1)}, f32[16,128]{1,0:T(8,128)S(1)}, u32[]{:S(2)}, u32[]{:S(2)}) collective-permute-start(f32[16,128]{1,0:T(8,128)S(1)} %multiply_add_fusion.refs_4_), channel_id=1, source_target_pairs={{0,4},{1,5},{2,6},{3,7},{4,0},{5,1},{6,2},{7,3},{8,12},{9,13},{10,... | collective-permute-start | bytes 24584 | tf_op jit(solution)/shard_map/ppermute | solution.py:299
  46.1 10.7 %collective-permute-start.15 = (f32[3,2,128,512]{3,2,1,0:T(8,128)S(1)}, f32[3,2,128,512]{3,2,1,0:T(8,128)S(1)}, u32[]{:S(2)}, u32[]{:S(2)}) collective-permute-start(f32[3,2,128,512]{3,2,1,0:T(8,128)S(1)} %get-tuple-element.28.refs_2_), channel_id=1, source_target_pairs={{0,8},{8,0},{16,24},{24,16},{1,9},{9,1},{17,25},{25,17},{2,10},{10... | collective-permute-start | bytes 4718600 | tf_op jit(solution)/shard_map/ppermute | solution.py:299
  46.2 5.3 %collective-permute-start.23 = (f32[256,512]{1,0:T(8,128)S(1)}, f32[256,512]{1,0:T(8,128)S(1)}, u32[]{:S(2)}, u32[]{:S(2)}) collective-permute-start(f32[256,512]{1,0:T(8,128)S(1)} %get-tuple-element.33), channel_id=1, source_target_pairs={{0,8},{8,0},{16,24},{24,16},{1,9},{9,1},{17,25},{25,17},{2,10},{10... | collective-permute-start | bytes 1572872 | tf_op jit(solution)/shard_map/ppermute | solution.py:299
  46.7 3.0 %collective-permute-start.18 = (f32[4,128]{1,0:T(4,128)S(1)}, f32[4,128]{1,0:T(4,128)S(1)}, u32[]{:S(2)}, u32[]{:S(2)}) collective-permute-start(f32[4,128]{1,0:T(4,128)S(1)} %get-tuple-element.31.lse_ref), channel_id=1, source_target_pairs={{0,24},{8,16},{16,8},{24,0},{1,25},{9,17},{17,9},{25,1},{2,26},{10... | collective-permute-start | bytes 6152 | tf_op jit(solution)/shard_map/ppermute | solution.py:299
  47.9 3.6 %collective-permute-start.17 = (f32[4,128]{1,0:T(4,128)S(1)}, f32[4,128]{1,0:T(4,128)S(1)}, u32[]{:S(2)}, u32[]{:S(2)}) collective-permute-start(f32[4,128]{1,0:T(4,128)S(1)} %get-tuple-element.31.lse_ref), channel_id=1, source_target_pairs={{0,16},{8,24},{16,0},{24,8},{1,17},{9,25},{17,1},{25,9},{2,18},{10... | collective-permute-start | bytes 6152 | tf_op jit(solution)/shard_map/ppermute | solution.py:299
  48.4 3.1 %collective-permute-start.16 = (f32[4,128]{1,0:T(4,128)S(1)}, f32[4,128]{1,0:T(4,128)S(1)}, u32[]{:S(2)}, u32[]{:S(2)}) collective-permute-start(f32[4,128]{1,0:T(4,128)S(1)} %get-tuple-element.31.lse_ref), channel_id=1, source_target_pairs={{0,8},{8,0},{16,24},{24,16},{1,9},{9,1},{17,25},{25,17},{2,10},{10... | collective-permute-start | bytes 6152 | tf_op jit(solution)/shard_map/ppermute | solution.py:299
  51.8 13.2 %collective-permute-start.24 = (f32[256,512]{1,0:T(8,128)S(1)}, f32[256,512]{1,0:T(8,128)S(1)}, u32[]{:S(2)}, u32[]{:S(2)}) collective-permute-start(f32[256,512]{1,0:T(8,128)S(1)} %shard_map.70.one_ref), channel_id=1, source_target_pairs={{0,16},{8,24},{16,0},{24,8},{1,17},{9,25},{17,1},{25,9},{2,18},{10... | collective-permute-start | bytes 1572872 | tf_op jit(solution)/shard_map/ppermute | solution.py:299
  52.4 5.7 %collective-permute-start.19 = (f32[4,128]{1,0:T(4,128)S(1)}, f32[4,128]{1,0:T(4,128)S(1)}, u32[]{:S(2)}, u32[]{:S(2)}) collective-permute-start(f32[4,128]{1,0:T(4,128)S(1)} %get-tuple-element.38.refs_5_), channel_id=1, source_target_pairs={{0,5},{1,4},{2,7},{3,6},{4,1},{5,0},{6,3},{7,2},{8,13},{9,12},{10,... | collective-permute-start | bytes 6152 | tf_op jit(solution)/shard_map/ppermute | solution.py:299
  54.0 4.5 %collective-permute-start.20 = (f32[4,128]{1,0:T(4,128)S(1)}, f32[4,128]{1,0:T(4,128)S(1)}, u32[]{:S(2)}, u32[]{:S(2)}) collective-permute-start(f32[4,128]{1,0:T(4,128)S(1)} %get-tuple-element.38.refs_5_), channel_id=1, source_target_pairs={{0,4},{1,5},{2,6},{3,7},{4,0},{5,1},{6,2},{7,3},{8,12},{9,13},{10,... | collective-permute-start | bytes 6152 | tf_op jit(solution)/shard_map/ppermute | solution.py:299
  55.9 3.6 %collective-permute-start.21 = (f32[4,128]{1,0:T(4,128)S(1)}, f32[4,128]{1,0:T(4,128)S(1)}, u32[]{:S(2)}, u32[]{:S(2)}) collective-permute-start(f32[4,128]{1,0:T(4,128)S(1)} %get-tuple-element.38.refs_5_), channel_id=1, source_target_pairs={{0,1},{1,0},{2,3},{3,2},{4,5},{5,4},{6,7},{7,6},{8,9},{9,8},{10,11... | collective-permute-start | bytes 6152 | tf_op jit(solution)/shard_map/ppermute | solution.py:299
  60.4 12.5 %collective-permute-start.22 = (f32[264,512]{1,0:T(8,128)S(1)}, f32[264,512]{1,0:T(8,128)S(1)}, u32[]{:S(2)}, u32[]{:S(2)}) collective-permute-start(f32[264,512]{1,0:T(8,128)S(1)} %shard_map.68), channel_id=1, source_target_pairs={{0,2},{1,3},{2,0},{3,1},{4,6},{5,7},{6,4},{7,5},{8,10},{9,11},{10,... | collective-permute-start | bytes 1622024 | tf_op jit(solution)/shard_map/ppermute | solution.py:299
  65.0 1.4 %collective-permute-start.25 = (f32[64,512]{1,0:T(8,128)S(1)}, f32[64,512]{1,0:T(8,128)S(1)}, u32[]{:S(2)}, u32[]{:S(2)}) collective-permute-start(f32[64,512]{1,0:T(8,128)S(1)} %get-tuple-element.34.refs_0_), channel_id=1, source_target_pairs={{0,8},{8,0},{16,24},{24,16},{1,9},{9,1},{17,25},{25,17},{2,10},{10... | collective-permute-start | bytes 393224 | tf_op jit(solution)/shard_map/ppermute | solution.py:299
  65.1 1.5 %collective-permute-start.26 = (f32[64,512]{1,0:T(8,128)S(1)}, f32[64,512]{1,0:T(8,128)S(1)}, u32[]{:S(2)}, u32[]{:S(2)}) collective-permute-start(f32[64,512]{1,0:T(8,128)S(1)} %get-tuple-element.35.refs_1_), channel_id=1, source_target_pairs={{0,8},{8,0},{16,24},{24,16},{1,9},{9,1},{17,25},{25,17},{2,10},{10... | collective-permute-start | bytes 393224 | tf_op jit(solution)/shard_map/ppermute | solution.py:299
  65.6 1.3 %collective-permute-start.27 = (f32[64,512]{1,0:T(8,128)S(1)}, f32[64,512]{1,0:T(8,128)S(1)}, u32[]{:S(2)}, u32[]{:S(2)}) collective-permute-start(f32[64,512]{1,0:T(8,128)S(1)} %get-tuple-element.36.refs_2_), channel_id=1, source_target_pairs={{0,8},{8,0},{16,24},{24,16},{1,9},{9,1},{17,25},{25,17},{2,10},{10... | collective-permute-start | bytes 393224 | tf_op jit(solution)/shard_map/ppermute | solution.py:299
  65.7 1.5 %collective-permute-start.28 = (f32[64,512]{1,0:T(8,128)S(1)}, f32[64,512]{1,0:T(8,128)S(1)}, u32[]{:S(2)}, u32[]{:S(2)}) collective-permute-start(f32[64,512]{1,0:T(8,128)S(1)} %get-tuple-element.37.refs_3_), channel_id=1, source_target_pairs={{0,8},{8,0},{16,24},{24,16},{1,9},{9,1},{17,25},{25,17},{2,10},{10... | collective-permute-start | bytes 393224 | tf_op jit(solution)/shard_map/ppermute | solution.py:299

commit v9 on v8

--- a/solution.py
+++ b/solution.py
@@ -147,8 +147,46 @@
     refs[-1][...] = to_dense(columns)
 
 
-def last_sources_kernel(n_parts, tile_ref, x_ref, ls_ref, sqx_ref, *refs):
-    pieces, (lse_ref, sent_ref, mine_ref, pack_ref) = refs[n_parts:-4], refs[-4:]
+def last_sources_kernel(tile_ref, x_ref, ls_ref, sqx_ref, *refs):
+    parts, (lse_ref, sent_ref, mine_ref) = refs[:-4], refs[-3:]
+    bias = source_bias(ls_ref, sqx_ref, parts)
+    x = x_ref[...]
+    n_rows = mine_ref.shape[0] // LANES
+    core = lax.axis_index("row") % 2
+    for out_ref, place in ((sent_ref, 1 - core), (mine_ref, core)):
+        columns = []
+        for j in range(n_rows):
+            at = pl.ds(pl.multiple_of((place * n_rows + j) * LANES, LANES), LANES)
+            peak, total, exps = over_sources(tile_ref, at, bias)
+            columns.append(peak + jnp.log2(total))
+            weights = jnp.concatenate([block.astype(jnp.bfloat16) for block in exps], axis=1)
+            mean = jnp.dot(weights, x, preferred_element_type=jnp.float32)
+            out_ref[pl.ds(j * LANES, LANES), :] = mean * (1.0 / total)
+        lse_ref[pl.ds(place * n_rows, n_rows), :] = to_dense(columns)
+
+
+def source_bias(ls_ref, sqx_ref, parts):
+    f_pot = sqx_ref[...] - merge_all([ref[...] for ref in parts])
+    return ls_ref[...] * LOG2E + f_pot - sqx_ref[...]
+
+
+def over_sources(tile_ref, at, bias):
+    scores = [tile_ref[at, pl.ds(b * LANES, LANES)] + bias[b : b + 1, :] for b in range(bias.shape[0])]
+    top = scores[0]
+    for block in scores[1:]:
+        top = jnp.maximum(top, block)
+    peak = jnp.max(top, axis=1, keepdims=True)
+    exps = [jnp.exp2(block - peak) for block in scores]
+    return peak, jnp.sum(sum(exps), axis=1, keepdims=True), exps
+
+
+def share_kernel(mine_ref, came_ref, total_ref, lse_ref, came_lse_ref, *refs):
+    pieces, (out_ref, pack_ref) = refs[:-2], refs[-2:]
+    half = mine_ref.shape[0] // LANES
+    at = pl.ds(lax.axis_index("row") % 2 * half, half)
+    total = total_ref[at, :]
+    share, came_share = to_column(jnp.exp2(lse_ref[at, :] - total)), to_column(jnp.exp2(came_lse_ref[at, :] - total))
+    out_ref[...] = mine_ref[...] * share + came_ref[...] * came_share
     n_shards, n_y, rows, _ = pack_ref.shape
     y = lax.axis_index("row") // 2
     early, late = pieces[:n_y], pieces[n_y:]
@@ -160,44 +198,6 @@
         pack_ref[1, place, cut:, :] = late[j][: rows - cut, :]
         for k in range(2, n_shards):
             pack_ref[k, place] = late[j][pl.ds((k - 1) * rows - cut, rows), :]
-    bias = source_bias(ls_ref, sqx_ref, refs[:n_parts])
-    x = x_ref[...]
-    n_rows = mine_ref.shape[0] // LANES
-    core = lax.axis_index("row") % 2
-    for out_ref, place in ((sent_ref, 1 - core), (mine_ref, core)):
-        columns, totals, weights = [], [], []
-        for j in range(n_rows):
-            at = pl.ds(pl.multiple_of((place * n_rows + j) * LANES, LANES), LANES)
-            peak, total, exps = over_sources(tile_ref, at, bias)
-            columns.append(peak + jnp.log2(total))
-            totals.append(total)
-            weights.append(jnp.concatenate([block.astype(jnp.bfloat16) for block in exps], axis=1))
-        mean = jnp.dot(jnp.concatenate(weights, axis=0), x, preferred_element_type=jnp.float32)
-        out_ref[...] = mean * (1.0 / jnp.concatenate(totals, axis=0))
-        lse_ref[pl.ds(place * n_rows, n_rows), :] = to_dense(columns)
-
-
-def source_bias(ls_ref, sqx_ref, parts):
-    f_pot = sqx_ref[...] - merge_all([ref[...] for ref in parts])
-    return ls_ref[...] * LOG2E + f_pot - sqx_ref[...]
-
-
-def over_sources(tile_ref, at, bias):
-    scores = [tile_ref[at, pl.ds(b * LANES, LANES)] + bias[b : b + 1, :] for b in range(bias.shape[0])]
-    top = scores[0]
-    for block in scores[1:]:
-        top = jnp.maximum(top, block)
-    peak = jnp.max(top, axis=1, keepdims=True)
-    exps = [jnp.exp2(block - peak) for block in scores]
-    return peak, jnp.sum(sum(exps), axis=1, keepdims=True), exps
-
-
-def share_kernel(mine_ref, came_ref, total_ref, lse_ref, came_lse_ref, out_ref):
-    half = mine_ref.shape[0] // LANES
-    at = pl.ds(lax.axis_index("row") % 2 * half, half)
-    total = total_ref[at, :]
-    share, came_share = to_column(jnp.exp2(lse_ref[at, :] - total)), to_column(jnp.exp2(came_lse_ref[at, :] - total))
-    out_ref[...] = mine_ref[...] * share + came_ref[...] * came_share
 
 
 def add_kernel(one_ref, two_ref, *out_refs):
@@ -341,13 +341,16 @@
             )
             late = along_y(late)
         if step > 0:
-            for distance in bits_of(2 * n_x):
-                lse = merge_all([lse, swap(lse, "col", distance)])
+            rest = bits_of(n_col)
         else:
-            near = [lse] + [swap(lse, "col", distance) for distance in range(2 * n_x - 1, 0, -1)]
+            group, rest = [*bits_of(n_x), n_col // 2], [bit for bit in bits_of(n_col // 2) if bit >= n_x]
+            ways = [0]
+            for bit in group:
+                ways += [way | bit for way in ways]
+            near = [lse] + [swap(lse, "col", way) for way in ways[:0:-1]]
             far = [k for k in pieces if k > 0]
             lse, early, *copies = call(
-                lambda *refs: merge_kernel(2 * n_x, *refs),
+                lambda *refs: merge_kernel(len(ways), *refs),
                 (src_dense, f32(part.shape[0] + cut, width), *(part,) * len(far)),
                 *near, *[pieces[k] for k in far], early,
             )
@@ -355,16 +358,16 @@
             pieces |= dict(zip(far, copies))
             for bit in bits_of(n_x)[::-1]:
                 pieces |= {k ^ bit: swap(piece, "col", bit) for k, piece in pieces.items() if k ^ bit != 1}
-        for distance in [bit for bit in bits_of(n_col) if bit > n_x][:-1]:
+        for distance in rest[:-1]:
             lse = merge_all([lse, swap(lse, "col", distance)])
-        parts = [lse, swap(lse, "col", n_col // 2)]
+        parts = [lse, swap(lse, "col", rest[-1])]
         if step < ITERS - 1:
             lse = call(lambda *refs: sources_kernel(2, *refs), tgt_dense, tile, ls, sqx, *parts)
         else:
-            lse, sent, mine, came = call(
-                lambda *refs: last_sources_kernel(2, *refs),
-                (tgt_dense, f32(half, width), f32(half, width), f32(len(apart) - 1, n_row // 2, *part.shape)),
-                tile, source, ls, sqx, *parts, *early, *late,
+            lse, sent, mine = call(
+                last_sources_kernel,
+                (tgt_dense, f32(half, width), f32(half, width)),
+                tile, source, ls, sqx, *parts, late[-1],
             )
         parts = [lse] + [swap(lse, "row", k) for k in range(1, n_row)]
     total = merge_all(parts)
@@ -372,7 +375,11 @@
     bias = lt * LOG2E + (sqy - total) - sqy
     biases = [bias] + [swap(bias, "col", distance) for distance in apart[1:]]
 
-    mine = call(share_kernel, f32(half, width), mine, swap(sent, "row", 1), total, lse, parts[1])
+    mine, came = call(
+        share_kernel,
+        (f32(half, width), f32(len(apart) - 1, n_row // 2, *part.shape)),
+        mine, swap(sent, "row", 1), total, lse, parts[1], *early, *late,
+    )
     rest = bits_of(n_row)[1:]
     for distance in rest[:-1]:
         mine, = call(add_kernel, (f32(half, width),), mine, swap(mine, "row", distance))

time: 74.2 us -> 74.3 us (level)
  starting transfers between devices: 29 us -> 32.2 us
  waiting for transfers between devices: 28.5 us -> 25.5 us
    ppermute x29, starting transfers between devices: 29 us -> 32.2 us  [swap(): return lax.ppermute(value, axis, [(i, i ^ distance) for i in range(n)])]
    ppermute x29, waiting for transfers between devices: 28.5 us -> 25.5 us  [swap(): return lax.ppermute(value, axis, [(i, i ^ distance) for i in range(n)])]
  transfers between devices with their start and end apart: 29 -> 29, of which waited for: 17 -> 16; matrix products, arithmetic and copies ran while one was open for 0% -> 0% of each run, Pallas kernels for 11% -> 10%
where the time goes in v9:
time: 74.3 us; the launch traced here: 74.1 us
  starting transfers between devices  32.2 us (43%)
  waiting for transfers between devices  25.5 us (34%)
  Pallas kernels  12.1 us (16%)
  local copies, waits for them, and re-layouts  3.32 us (4%)
  between operations  0.8 us (1%)
    ppermute x29, starting transfers between devices, swap(): return lax.ppermute(value, axis, [(i, i ^ distance) for i in range(n)])  32.2 us
    ppermute x29, waiting for transfers between devices, swap(): return lax.ppermute(value, axis, [(i, i ^ distance) for i in range(n)])  25.5 us
    pallas_call x14, Pallas kernels, call(): pl.pallas_call(kernel, out_shape=out_shape, in_specs=in_specs or [VMEM] *...  12.1 us
    unnamed x12, local copies, waits for them, and re-layouts  3.32 us
  transfers between devices with their start and end apart: 29, of which 16 were waited for; matrix products, arithmetic and copies ran while one was open for 0% of the time, Pallas kernels for 10%

profile of v9, /device:TPU:0, one launch (start us, length us, event | category | flops | bytes accessed | tf_op | source)
XLA Modules:
  0.0 74.1 jit_solution(3676577379802173203)
XLA Ops:
  0.6 0.0 copy-start.2
  0.6 1.0 %copy-done.2 = bf16[512,512]{1,0:T(8,128)(2,1)S(1)} copy-done((bf16[512,512]{1,0:T(8,128)(2,1)S(1)}, bf16[512,512]{1,0:T(8,128)(2,1)}, u32[]{:S(2)}) %copy-start.2) | copy-done | bytes 524312
  1.7 4.1 %collective-permute-start.3 = (f32[128,512]{1,0:T(8,128)S(1)}, f32[128,512]{1,0:T(8,128)S(1)}, u32[]{:S(2)}, u32[]{:S(2)}) collective-permute-start(f32[128,512]{1,0:T(8,128)S(1)} %shard_map.61), channel_id=1, source_target_pairs={{0,4},{1,5},{2,6},{3,7},{4,0},{5,1},{6,2},{7,3},{8,12},{9,13},{10,... | collective-permute-start | bytes 786440 | tf_op jit(solution)/shard_map/ppermute | solution.py:299
  5.8 1.5 %collective-permute-start.4 = (f32[128,512]{1,0:T(8,128)S(1)}, f32[128,512]{1,0:T(8,128)S(1)}, u32[]{:S(2)}, u32[]{:S(2)}) collective-permute-start(f32[128,512]{1,0:T(8,128)S(1)} %shard_map.61), channel_id=1, source_target_pairs={{0,1},{1,0},{2,3},{3,2},{4,5},{5,4},{6,7},{7,6},{8,9},{9,8},{10,11... | collective-permute-start | bytes 786440 | tf_op jit(solution)/shard_map/ppermute | solution.py:299
  7.3 1.6 %copy-done = bf16[2048,512]{1,0:T(8,128)(2,1)S(1)} copy-done((bf16[2048,512]{1,0:T(8,128)(2,1)S(1)}, bf16[2048,512]{1,0:T(8,128)(2,1)}, u32[]{:S(2)}) %copy-start) | copy-done | bytes 2097176
  8.9 0.7 copy-done.5
  9.6 1.9 %shard_map.59 = (f32[512,2048]{1,0:T(8,128)S(1)}, f32[16,128]{1,0:T(8,128)S(1)}, f32[4,128]{1,0:T(4,128)S(1)}) custom-call(bf16[512,512]{1,0:T(8,128)(2,1)S(1)} %copy-done.2, bf16[2048,512]{1,0:T(8,128)(2,1)S(1)} %copy-done, f32[4,128]{1,0:T(4,128)S(1)} %bitcast.5), custom_call_target="tpu_custom_call" | custom-call | tf_op jit(solution)/shard_map/pallas_call | solution.py:22
  11.5 0.1 collective-permute-start
  11.6 2.8 %collective-permute-start.1 = (f32[16,128]{1,0:T(8,128)S(1)}, f32[16,128]{1,0:T(8,128)S(1)}, u32[]{:S(2)}, u32[]{:S(2)}) collective-permute-start(f32[16,128]{1,0:T(8,128)S(1)} %get-tuple-element.23.refs_0_), channel_id=1, source_target_pairs={{0,4},{1,5},{2,6},{3,7},{4,0},{5,1},{6,2},{7,3},{8,12},{9,13},{10,... | collective-permute-start | bytes 24584 | tf_op jit(solution)/shard_map/ppermute | solution.py:299
  14.4 1.5 %collective-permute-start.2 = (f32[16,128]{1,0:T(8,128)S(1)}, f32[16,128]{1,0:T(8,128)S(1)}, u32[]{:S(2)}, u32[]{:S(2)}) collective-permute-start(f32[16,128]{1,0:T(8,128)S(1)} %get-tuple-element.23.refs_0_), channel_id=1, source_target_pairs={{0,1},{1,0},{2,3},{3,2},{4,5},{5,4},{6,7},{7,6},{8,9},{9,8},{10,11... | collective-permute-start | bytes 24584 | tf_op jit(solution)/shard_map/ppermute | solution.py:299
  15.9 3.4 %collective-permute-done.refs_1_ = f32[16,128]{1,0:T(8,128)S(1)} collective-permute-done((f32[16,128]{1,0:T(8,128)S(1)}, f32[16,128]{1,0:T(8,128)S(1)}, u32[]{:S(2)}, u32[]{:S(2)}) %collective-permute-start) | collective-permute-done | bytes 8224 | tf_op jit(solution)/shard_map/ppermute | solution.py:299
  19.3 0.0 collective-permute-done.4.refs_5_
  19.4 1.6 %collective-permute-start.10 = (f32[192,512]{1,0:T(8,128)S(1)}, f32[192,512]{1,0:T(8,128)S(1)}, u32[]{:S(2)}, u32[]{:S(2)}) collective-permute-start(f32[192,512]{1,0:T(8,128)S(1)} %get-tuple-element.26.refs_0_), channel_id=1, source_target_pairs={{0,16},{8,24},{16,0},{24,8},{1,17},{9,25},{17,1},{25,9},{2,18},{10... | collective-permute-start | bytes 1179656 | tf_op jit(solution)/shard_map/ppermute | solution.py:299
  21.0 0.6 collective-permute-start.9
  21.6 1.2 %collective-permute-start.5 = (f32[16,128]{1,0:T(8,128)S(1)}, f32[16,128]{1,0:T(8,128)S(1)}, u32[]{:S(2)}, u32[]{:S(2)}) collective-permute-start(f32[16,128]{1,0:T(8,128)S(1)} %get-tuple-element.24.refs_3_), channel_id=1, source_target_pairs={{0,2},{1,3},{2,0},{3,1},{4,6},{5,7},{6,4},{7,5},{8,10},{9,11},{10,... | collective-permute-start | bytes 24584 | tf_op jit(solution)/shard_map/ppermute | solution.py:299
  22.8 0.5 shard_map.60.refs_2_.sqx_ref
  23.3 2.0 %collective-permute-done.5.refs_4_ = f32[16,128]{1,0:T(8,128)S(1)} collective-permute-done((f32[16,128]{1,0:T(8,128)S(1)}, f32[16,128]{1,0:T(8,128)S(1)}, u32[]{:S(2)}, u32[]{:S(2)}) %collective-permute-start.5) | collective-permute-done | bytes 8224 | tf_op jit(solution)/shard_map/ppermute | solution.py:299
  25.3 1.0 %shard_map.63.refs_3_ = f32[4,128]{1,0:T(4,128)S(1)} custom-call(f32[512,2048]{1,0:T(8,128)S(1)} %get-tuple-element.21.refs_0_.tile_ref, f32[16,128]{1,0:T(8,128)S(1)} %bitcast.3, f32[16,128]{1,0:T(8,128)S(1)} %shard_map.60.refs_2_.sqx_ref, f32[16,128]{1,0:T(8,128)S(1)} %get-tuple-element.24.refs_3_, f32[16,128]{1,0:T(8,128)S(1)} %collective-permute-done.5.refs_4_), custom_call_target="tpu_custom_call" | custom-call | tf_op jit(solution)/shard_map/pallas_call | solution.py:22
  26.3 0.0 collective-permute-start.6
  26.3 0.6 collective-permute-start.7
  26.9 1.3 %collective-permute-start.8 = (f32[4,128]{1,0:T(4,128)S(1)}, f32[4,128]{1,0:T(4,128)S(1)}, u32[]{:S(2)}, u32[]{:S(2)}) collective-permute-start(f32[4,128]{1,0:T(4,128)S(1)} %shard_map.63.refs_3_), channel_id=1, source_target_pairs={{0,24},{8,16},{16,8},{24,0},{1,25},{9,17},{17,9},{25,1},{2,26},{10... | collective-permute-start | bytes 6152 | tf_op jit(solution)/shard_map/ppermute | solution.py:299
  28.2 0.0 collective-permute-done.6.refs_4_
  28.2 1.8 %collective-permute-done.7.refs_5_ = f32[4,128]{1,0:T(4,128)S(1)} collective-permute-done((f32[4,128]{1,0:T(4,128)S(1)}, f32[4,128]{1,0:T(4,128)S(1)}, u32[]{:S(2)}, u32[]{:S(2)}) %collective-permute-start.7) | collective-permute-done | bytes 2080 | tf_op jit(solution)/shard_map/ppermute | solution.py:299
  30.0 0.0 collective-permute-done.8.refs_6_
  30.0 1.1 %shard_map.64 = (f32[16,128]{1,0:T(8,128)S(1)}, f32[192,512]{1,0:T(8,128)S(1)}) custom-call(f32[512,2048]{1,0:T(8,128)S(1)} %get-tuple-element.21.refs_0_.tile_ref, f32[4,128]{1,0:T(4,128)S(1)} %bitcast.6, f32[4,128]{1,0:T(4,128)S(1)} %get-tuple-element.22.refs_2_, f32[4,128]{1,0:T(4,128)S(1)} %shard_map.63.refs_3_, ...), custom_call_target="tpu_custom_call" | custom-call | tf_op jit(solution)/shard_map/pallas_call | solution.py:22
  31.1 1.4 %collective-permute-start.11 = (f32[16,128]{1,0:T(8,128)S(1)}, f32[16,128]{1,0:T(8,128)S(1)}, u32[]{:S(2)}, u32[]{:S(2)}) collective-permute-start(f32[16,128]{1,0:T(8,128)S(1)} %get-tuple-element.27), channel_id=1, source_target_pairs={{0,1},{1,0},{2,3},{3,2},{4,5},{5,4},{6,7},{7,6},{8,9},{9,8},{10,11... | collective-permute-start | bytes 24584 | tf_op jit(solution)/shard_map/ppermute | solution.py:299
  32.6 1.4 %collective-permute-start.14 = (f32[192,512]{1,0:T(8,128)S(1)}, f32[192,512]{1,0:T(8,128)S(1)}, u32[]{:S(2)}, u32[]{:S(2)}) collective-permute-start(f32[192,512]{1,0:T(8,128)S(1)} %get-tuple-element.28.refs_2_), channel_id=1, source_target_pairs={{0,16},{8,24},{16,0},{24,8},{1,17},{9,25},{17,1},{25,9},{2,18},{10... | collective-permute-start | bytes 1179656 | tf_op jit(solution)/shard_map/ppermute | solution.py:299
  34.0 0.8 %collective-permute-done.11 = f32[16,128]{1,0:T(8,128)S(1)} collective-permute-done((f32[16,128]{1,0:T(8,128)S(1)}, f32[16,128]{1,0:T(8,128)S(1)}, u32[]{:S(2)}, u32[]{:S(2)}) %collective-permute-start.11) | collective-permute-done | bytes 8224 | tf_op jit(solution)/shard_map/ppermute | solution.py:299
  34.8 1.2 %collective-permute-start.12 = (f32[16,128]{1,0:T(8,128)S(1)}, f32[16,128]{1,0:T(8,128)S(1)}, u32[]{:S(2)}, u32[]{:S(2)}) collective-permute-start(f32[16,128]{1,0:T(8,128)S(1)} %multiply_add_fusion.1), channel_id=1, source_target_pairs={{0,2},{1,3},{2,0},{3,1},{4,6},{5,7},{6,4},{7,5},{8,10},{9,11},{10,... | collective-permute-start | bytes 24584 | tf_op jit(solution)/shard_map/ppermute | solution.py:299
  36.1 2.5 %collective-permute-done.12 = f32[16,128]{1,0:T(8,128)S(1)} collective-permute-done((f32[16,128]{1,0:T(8,128)S(1)}, f32[16,128]{1,0:T(8,128)S(1)}, u32[]{:S(2)}, u32[]{:S(2)}) %collective-permute-start.12) | collective-permute-done | bytes 8224 | tf_op jit(solution)/shard_map/ppermute | solution.py:299
  38.6 2.3 %collective-permute-start.13 = (f32[16,128]{1,0:T(8,128)S(1)}, f32[16,128]{1,0:T(8,128)S(1)}, u32[]{:S(2)}, u32[]{:S(2)}) collective-permute-start(f32[16,128]{1,0:T(8,128)S(1)} %multiply_add_fusion.refs_0_), channel_id=1, source_target_pairs={{0,4},{1,5},{2,6},{3,7},{4,0},{5,1},{6,2},{7,3},{8,12},{9,13},{10,... | collective-permute-start | bytes 24584 | tf_op jit(solution)/shard_map/ppermute | solution.py:299
  40.9 2.3 %collective-permute-done.13.refs_1_ = f32[16,128]{1,0:T(8,128)S(1)} collective-permute-done((f32[16,128]{1,0:T(8,128)S(1)}, f32[16,128]{1,0:T(8,128)S(1)}, u32[]{:S(2)}, u32[]{:S(2)}) %collective-permute-start.13) | collective-permute-done | bytes 8224 | tf_op jit(solution)/shard_map/ppermute | solution.py:299
  43.2 0.2 collective-permute-done.14.refs_2_.refs_3_
  43.4 1.9 %shard_map.65 = (f32[4,128]{1,0:T(4,128)S(1)}, f32[256,512]{1,0:T(8,128)S(1)}, f32[256,512]{1,0:T(8,128)S(1)}) custom-call(f32[512,2048]{1,0:T(8,128)S(1)} %get-tuple-element.21.refs_0_.tile_ref, bf16[2048,512]{1,0:T(8,128)(2,1)S(1)} %copy-done.1, f32[16,128]{1,0:T(8,128)S(1)} %bitcast.4, f32[16,128]{1,0:T(8,128)S(1)} %shard_map.60.refs_2_.sqx_ref, ...), custom_call_target="tpu_custom_call" | custom-call | tf_op jit(solution)/shard_map/pallas_call | solution.py:22
  45.3 0.0 copy-start.3
  45.3 0.1 collective-permute-start.15
  45.4 1.6 %collective-permute-start.18 = (f32[4,128]{1,0:T(4,128)S(1)}, f32[4,128]{1,0:T(4,128)S(1)}, u32[]{:S(2)}, u32[]{:S(2)}) collective-permute-start(f32[4,128]{1,0:T(4,128)S(1)} %get-tuple-element.31.lse_ref), channel_id=1, source_target_pairs={{0,24},{8,16},{16,8},{24,0},{1,25},{9,17},{17,9},{25,1},{2,26},{10... | collective-permute-start | bytes 6152 | tf_op jit(solution)/shard_map/ppermute | solution.py:299
  47.0 0.5 collective-permute-start.17
  47.5 0.9 %collective-permute-done.18 = f32[4,128]{1,0:T(4,128)S(1)} collective-permute-done((f32[4,128]{1,0:T(4,128)S(1)}, f32[4,128]{1,0:T(4,128)S(1)}, u32[]{:S(2)}, u32[]{:S(2)}) %collective-permute-start.18) | collective-permute-done | bytes 2080 | tf_op jit(solution)/shard_map/ppermute | solution.py:299
  48.5 2.1 %collective-permute-done.17 = f32[4,128]{1,0:T(4,128)S(1)} collective-permute-done((f32[4,128]{1,0:T(4,128)S(1)}, f32[4,128]{1,0:T(4,128)S(1)}, u32[]{:S(2)}, u32[]{:S(2)}) %collective-permute-start.17) | collective-permute-done | bytes 2080 | tf_op jit(solution)/shard_map/ppermute | solution.py:299
  50.6 0.4 shard_map.66
  51.0 0.1 collective-permute-start.19
  51.1 0.6 collective-permute-start.24
  51.7 2.6 %collective-permute-start.20 = (f32[4,128]{1,0:T(4,128)S(1)}, f32[4,128]{1,0:T(4,128)S(1)}, u32[]{:S(2)}, u32[]{:S(2)}) collective-permute-start(f32[4,128]{1,0:T(4,128)S(1)} %get-tuple-element.40.refs_5_), channel_id=1, source_target_pairs={{0,5},{1,4},{2,7},{3,6},{4,1},{5,0},{6,3},{7,2},{8,13},{9,12},{10,... | collective-permute-start | bytes 6152 | tf_op jit(solution)/shard_map/ppermute | solution.py:299
  54.4 0.9 %collective-permute-start.21 = (f32[4,128]{1,0:T(4,128)S(1)}, f32[4,128]{1,0:T(4,128)S(1)}, u32[]{:S(2)}, u32[]{:S(2)}) collective-permute-start(f32[4,128]{1,0:T(4,128)S(1)} %get-tuple-element.40.refs_5_), channel_id=1, source_target_pairs={{0,4},{1,5},{2,6},{3,7},{4,0},{5,1},{6,2},{7,3},{8,12},{9,13},{10,... | collective-permute-start | bytes 6152 | tf_op jit(solution)/shard_map/ppermute | solution.py:299
  55.3 0.8 %collective-permute-start.22 = (f32[4,128]{1,0:T(4,128)S(1)}, f32[4,128]{1,0:T(4,128)S(1)}, u32[]{:S(2)}, u32[]{:S(2)}) collective-permute-start(f32[4,128]{1,0:T(4,128)S(1)} %get-tuple-element.40.refs_5_), channel_id=1, source_target_pairs={{0,1},{1,0},{2,3},{3,2},{4,5},{5,4},{6,7},{7,6},{8,9},{9,8},{10,11... | collective-permute-start | bytes 6152 | tf_op jit(solution)/shard_map/ppermute | solution.py:299
  56.1 1.3 %shard_map.67 = (bf16[2048,512]{1,0:T(8,128)(2,1)S(1)}, f32[512,2048]{1,0:T(8,128)S(1)}) custom-call(bf16[2048,512]{1,0:T(8,128)(2,1)S(1)} %copy-done.1, bf16[512,512]{1,0:T(8,128)(2,1)S(1)} %copy-done.3, f32[3,2,128,512]{3,2,1,0:T(8,128)S(1)} %get-tuple-element.32.refs_2_, f32[3,2,128,512]{3,2,1,0:T(8,128)S(1)} %collective-permute-done.19.refs_3_), custom_call_target="tpu_custom_call" | custom-call | tf_op jit(solution)/shard_map/pallas_call | solution.py:22
  57.4 1.4 %collective-permute-done.21.refs_3_ = f32[4,128]{1,0:T(4,128)S(1)} collective-permute-done((f32[4,128]{1,0:T(4,128)S(1)}, f32[4,128]{1,0:T(4,128)S(1)}, u32[]{:S(2)}, u32[]{:S(2)}) %collective-permute-start.21) | collective-permute-done | bytes 2080 | tf_op jit(solution)/shard_map/ppermute | solution.py:299
  58.8 0.9 %shard_map.69 = f32[264,512]{1,0:T(8,128)S(1)} custom-call(f32[512,2048]{1,0:T(8,128)S(1)} %get-tuple-element.33.refs_0_, bf16[2048,512]{1,0:T(8,128)(2,1)S(1)} %get-tuple-element.34.refs_1_, f32[4,128]{1,0:T(4,128)S(1)} %collective-permute-done.20.refs_2_, f32[4,128]{1,0:T(4,128)S(1)} %collective-permute-done.21.refs_3_, ...), custom_call_target="tpu_custom_call" | custom-call | tf_op jit(solution)/shard_map/pallas_call | solution.py:22
  59.7 2.1 %collective-permute-start.23 = (f32[264,512]{1,0:T(8,128)S(1)}, f32[264,512]{1,0:T(8,128)S(1)}, u32[]{:S(2)}, u32[]{:S(2)}) collective-permute-start(f32[264,512]{1,0:T(8,128)S(1)} %shard_map.69), channel_id=1, source_target_pairs={{0,2},{1,3},{2,0},{3,1},{4,6},{5,7},{6,4},{7,5},{8,10},{9,11},{10,... | collective-permute-start | bytes 1622024 | tf_op jit(solution)/shard_map/ppermute | solution.py:299
  61.8 3.7 %collective-permute-done.24.two_ref = f32[256,512]{1,0:T(8,128)S(1)} collective-permute-done((f32[256,512]{1,0:T(8,128)S(1)}, f32[256,512]{1,0:T(8,128)S(1)}, u32[]{:S(2)}, u32[]{:S(2)}) %collective-permute-start.24) | collective-permute-done | bytes 524320 | tf_op jit(solution)/shard_map/ppermute | solution.py:299
  65.5 0.1 shard_map.71
  65.5 0.1 collective-permute-start.25
  65.6 0.5 collective-permute-start.26
  66.1 0.1 collective-permute-start.27
  66.2 0.4 collective-permute-start.28
  66.6 0.3 collective-permute-done.25.refs_4_
  66.9 0.2 collective-permute-done.26.refs_5_
  67.1 0.3 collective-permute-done.27.refs_6_
  67.4 0.2 collective-permute-done.28.refs_7_
  67.6 1.0 %shard_map.72 = f32[512,512]{1,0:T(8,128)} custom-call(f32[64,512]{1,0:T(8,128)S(1)} %get-tuple-element.36.refs_0_, f32[64,512]{1,0:T(8,128)S(1)} %get-tuple-element.37.refs_1_, f32[64,512]{1,0:T(8,128)S(1)} %get-tuple-element.38.refs_2_, f32[64,512]{1,0:T(8,128)S(1)} %get-tuple-element.39.refs_3_, f32[64,512]{1,0:T(8,128)S(1)} %collective-permute-done.25.refs_4_, ...), custom_call_target="tpu_custom_call" | custom-call | tf_op jit(solution)/shard_map/pallas_call | solution.py:22
  68.7 0.9 %shard_map.68.refs_0_ = f32[264,512]{1,0:T(8,128)S(1)} custom-call(f32[512,2048]{1,0:T(8,128)S(1)} %get-tuple-element.33.refs_0_, bf16[2048,512]{1,0:T(8,128)(2,1)S(1)} %get-tuple-element.34.refs_1_, f32[4,128]{1,0:T(4,128)S(1)} %collective-permute-done.20.refs_2_, f32[4,128]{1,0:T(4,128)S(1)} %collective-permute-done.21.refs_3_, ...), custom_call_target="tpu_custom_call" | custom-call | tf_op jit(solution)/shard_map/pallas_call | solution.py:22
  69.5 3.4 %collective-permute-done.23.refs_1_ = f32[264,512]{1,0:T(8,128)S(1)} collective-permute-done((f32[264,512]{1,0:T(8,128)S(1)}, f32[264,512]{1,0:T(8,128)S(1)}, u32[]{:S(2)}, u32[]{:S(2)}) %collective-permute-start.23) | collective-permute-done | bytes 540704 | tf_op jit(solution)/shard_map/ppermute | solution.py:299
  73.0 1.1 %shard_map.70 = f32[256,512]{1,0:T(8,128)} custom-call(f32[264,512]{1,0:T(8,128)S(1)} %shard_map.68.refs_0_, f32[264,512]{1,0:T(8,128)S(1)} %collective-permute-done.23.refs_1_), custom_call_target="tpu_custom_call" | custom-call | tf_op jit(solution)/shard_map/pallas_call | solution.py:22
  (23 shorter events, 0.2 us)
Async XLA Ops:
  0.6 1.0 %copy-start.2 = (bf16[512,512]{1,0:T(8,128)(2,1)S(1)}, bf16[512,512]{1,0:T(8,128)(2,1)}, u32[]{:S(2)}) copy-start(bf16[512,512]{1,0:T(8,128)(2,1)} %refs_1_.1) | copy-start | bytes 1572868
  1.7 17.6 %collective-permute-start.3 = (f32[128,512]{1,0:T(8,128)S(1)}, f32[128,512]{1,0:T(8,128)S(1)}, u32[]{:S(2)}, u32[]{:S(2)}) collective-permute-start(f32[128,512]{1,0:T(8,128)S(1)} %shard_map.61), channel_id=1, source_target_pairs={{0,4},{1,5},{2,6},{3,7},{4,0},{5,1},{6,2},{7,3},{8,12},{9,13},{10,... | collective-permute-start | bytes 786440 | tf_op jit(solution)/shard_map/ppermute | solution.py:299
  5.8 13.5 %collective-permute-start.4 = (f32[128,512]{1,0:T(8,128)S(1)}, f32[128,512]{1,0:T(8,128)S(1)}, u32[]{:S(2)}, u32[]{:S(2)}) collective-permute-start(f32[128,512]{1,0:T(8,128)S(1)} %shard_map.61), channel_id=1, source_target_pairs={{0,1},{1,0},{2,3},{3,2},{4,5},{5,4},{6,7},{7,6},{8,9},{9,8},{10,11... | collective-permute-start | bytes 786440 | tf_op jit(solution)/shard_map/ppermute | solution.py:299
  7.3 1.6 %copy-start = (bf16[2048,512]{1,0:T(8,128)(2,1)S(1)}, bf16[2048,512]{1,0:T(8,128)(2,1)}, u32[]{:S(2)}) copy-start(bf16[2048,512]{1,0:T(8,128)(2,1)} %refs_0_.1) | copy-start | bytes 6291460
  8.9 0.7 copy-start.5
  9.6 13.2 %copy-start.1 = (bf16[2048,512]{1,0:T(8,128)(2,1)S(1)}, bf16[2048,512]{1,0:T(8,128)(2,1)}, u32[]{:S(2)}) copy-start(bf16[2048,512]{1,0:T(8,128)(2,1)} %refs_0_.1) | copy-start | bytes 6291460
  9.6 15.7 %copy-start.4 = (f32[2048]{0:T(1024)S(1)}, f32[2048]{0:T(1024)}, u32[]{:S(2)}) copy-start(f32[2048]{0:T(1024)} %param.6) | copy-start | bytes 24580
  11.5 7.8 %collective-permute-start = (f32[16,128]{1,0:T(8,128)S(1)}, f32[16,128]{1,0:T(8,128)S(1)}, u32[]{:S(2)}, u32[]{:S(2)}) collective-permute-start(f32[16,128]{1,0:T(8,128)S(1)} %get-tuple-element.23.refs_0_), channel_id=1, source_target_pairs={{0,5},{1,4},{2,7},{3,6},{4,1},{5,0},{6,3},{7,2},{8,13},{9,12},{10,... | collective-permute-start | bytes 24584 | tf_op jit(solution)/shard_map/ppermute | solution.py:299
  11.6 7.7 %collective-permute-start.1 = (f32[16,128]{1,0:T(8,128)S(1)}, f32[16,128]{1,0:T(8,128)S(1)}, u32[]{:S(2)}, u32[]{:S(2)}) collective-permute-start(f32[16,128]{1,0:T(8,128)S(1)} %get-tuple-element.23.refs_0_), channel_id=1, source_target_pairs={{0,4},{1,5},{2,6},{3,7},{4,0},{5,1},{6,2},{7,3},{8,12},{9,13},{10,... | collective-permute-start | bytes 24584 | tf_op jit(solution)/shard_map/ppermute | solution.py:299
  14.4 4.9 %collective-permute-start.2 = (f32[16,128]{1,0:T(8,128)S(1)}, f32[16,128]{1,0:T(8,128)S(1)}, u32[]{:S(2)}, u32[]{:S(2)}) collective-permute-start(f32[16,128]{1,0:T(8,128)S(1)} %get-tuple-element.23.refs_0_), channel_id=1, source_target_pairs={{0,1},{1,0},{2,3},{3,2},{4,5},{5,4},{6,7},{7,6},{8,9},{9,8},{10,11... | collective-permute-start | bytes 24584 | tf_op jit(solution)/shard_map/ppermute | solution.py:299
  19.4 10.6 %collective-permute-start.10 = (f32[192,512]{1,0:T(8,128)S(1)}, f32[192,512]{1,0:T(8,128)S(1)}, u32[]{:S(2)}, u32[]{:S(2)}) collective-permute-start(f32[192,512]{1,0:T(8,128)S(1)} %get-tuple-element.26.refs_0_), channel_id=1, source_target_pairs={{0,16},{8,24},{16,0},{24,8},{1,17},{9,25},{17,1},{25,9},{2,18},{10... | collective-permute-start | bytes 1179656 | tf_op jit(solution)/shard_map/ppermute | solution.py:299
  21.0 9.0 %collective-permute-start.9 = (f32[128,512]{1,0:T(8,128)S(1)}, f32[128,512]{1,0:T(8,128)S(1)}, u32[]{:S(2)}, u32[]{:S(2)}) collective-permute-start(f32[128,512]{1,0:T(8,128)S(1)} %get-tuple-element.25.refs_7_), channel_id=1, source_target_pairs={{0,1},{1,0},{2,3},{3,2},{4,5},{5,4},{6,7},{7,6},{8,9},{9,8},{10,11... | collective-permute-start | bytes 786440 | tf_op jit(solution)/shard_map/ppermute | solution.py:299
  21.6 3.7 %collective-permute-start.5 = (f32[16,128]{1,0:T(8,128)S(1)}, f32[16,128]{1,0:T(8,128)S(1)}, u32[]{:S(2)}, u32[]{:S(2)}) collective-permute-start(f32[16,128]{1,0:T(8,128)S(1)} %get-tuple-element.24.refs_3_), channel_id=1, source_target_pairs={{0,2},{1,3},{2,0},{3,1},{4,6},{5,7},{6,4},{7,5},{8,10},{9,11},{10,... | collective-permute-start | bytes 24584 | tf_op jit(solution)/shard_map/ppermute | solution.py:299
  26.3 1.9 %collective-permute-start.6 = (f32[4,128]{1,0:T(4,128)S(1)}, f32[4,128]{1,0:T(4,128)S(1)}, u32[]{:S(2)}, u32[]{:S(2)}) collective-permute-start(f32[4,128]{1,0:T(4,128)S(1)} %shard_map.63.refs_3_), channel_id=1, source_target_pairs={{0,8},{8,0},{16,24},{24,16},{1,9},{9,1},{17,25},{25,17},{2,10},{10... | collective-permute-start | bytes 6152 | tf_op jit(solution)/shard_map/ppermute | solution.py:299
  26.3 3.7 %collective-permute-start.7 = (f32[4,128]{1,0:T(4,128)S(1)}, f32[4,128]{1,0:T(4,128)S(1)}, u32[]{:S(2)}, u32[]{:S(2)}) collective-permute-start(f32[4,128]{1,0:T(4,128)S(1)} %shard_map.63.refs_3_), channel_id=1, source_target_pairs={{0,16},{8,24},{16,0},{24,8},{1,17},{9,25},{17,1},{25,9},{2,18},{10... | collective-permute-start | bytes 6152 | tf_op jit(solution)/shard_map/ppermute | solution.py:299
  26.9 3.1 %collective-permute-start.8 = (f32[4,128]{1,0:T(4,128)S(1)}, f32[4,128]{1,0:T(4,128)S(1)}, u32[]{:S(2)}, u32[]{:S(2)}) collective-permute-start(f32[4,128]{1,0:T(4,128)S(1)} %shard_map.63.refs_3_), channel_id=1, source_target_pairs={{0,24},{8,16},{16,8},{24,0},{1,25},{9,17},{17,9},{25,1},{2,26},{10... | collective-permute-start | bytes 6152 | tf_op jit(solution)/shard_map/ppermute | solution.py:299
  31.1 3.7 %collective-permute-start.11 = (f32[16,128]{1,0:T(8,128)S(1)}, f32[16,128]{1,0:T(8,128)S(1)}, u32[]{:S(2)}, u32[]{:S(2)}) collective-permute-start(f32[16,128]{1,0:T(8,128)S(1)} %get-tuple-element.27), channel_id=1, source_target_pairs={{0,1},{1,0},{2,3},{3,2},{4,5},{5,4},{6,7},{7,6},{8,9},{9,8},{10,11... | collective-permute-start | bytes 24584 | tf_op jit(solution)/shard_map/ppermute | solution.py:299
  32.6 10.8 %collective-permute-start.14 = (f32[192,512]{1,0:T(8,128)S(1)}, f32[192,512]{1,0:T(8,128)S(1)}, u32[]{:S(2)}, u32[]{:S(2)}) collective-permute-start(f32[192,512]{1,0:T(8,128)S(1)} %get-tuple-element.28.refs_2_), channel_id=1, source_target_pairs={{0,16},{8,24},{16,0},{24,8},{1,17},{9,25},{17,1},{25,9},{2,18},{10... | collective-permute-start | bytes 1179656 | tf_op jit(solution)/shard_map/ppermute | solution.py:299
  34.8 3.7 %collective-permute-start.12 = (f32[16,128]{1,0:T(8,128)S(1)}, f32[16,128]{1,0:T(8,128)S(1)}, u32[]{:S(2)}, u32[]{:S(2)}) collective-permute-start(f32[16,128]{1,0:T(8,128)S(1)} %multiply_add_fusion.1), channel_id=1, source_target_pairs={{0,2},{1,3},{2,0},{3,1},{4,6},{5,7},{6,4},{7,5},{8,10},{9,11},{10,... | collective-permute-start | bytes 24584 | tf_op jit(solution)/shard_map/ppermute | solution.py:299
  38.6 4.6 %collective-permute-start.13 = (f32[16,128]{1,0:T(8,128)S(1)}, f32[16,128]{1,0:T(8,128)S(1)}, u32[]{:S(2)}, u32[]{:S(2)}) collective-permute-start(f32[16,128]{1,0:T(8,128)S(1)} %multiply_add_fusion.refs_0_), channel_id=1, source_target_pairs={{0,4},{1,5},{2,6},{3,7},{4,0},{5,1},{6,2},{7,3},{8,12},{9,13},{10,... | collective-permute-start | bytes 24584 | tf_op jit(solution)/shard_map/ppermute | solution.py:299
  45.3 10.8 %copy-start.3 = (bf16[512,512]{1,0:T(8,128)(2,1)S(1)}, bf16[512,512]{1,0:T(8,128)(2,1)}, u32[]{:S(2)}) copy-start(bf16[512,512]{1,0:T(8,128)(2,1)} %refs_1_.1) | copy-start | bytes 1572868
  45.3 5.3 %collective-permute-start.15 = (f32[256,512]{1,0:T(8,128)S(1)}, f32[256,512]{1,0:T(8,128)S(1)}, u32[]{:S(2)}, u32[]{:S(2)}) collective-permute-start(f32[256,512]{1,0:T(8,128)S(1)} %get-tuple-element.30), channel_id=1, source_target_pairs={{0,8},{8,0},{16,24},{24,16},{1,9},{9,1},{17,25},{25,17},{2,10},{10... | collective-permute-start | bytes 1572872 | tf_op jit(solution)/shard_map/ppermute | solution.py:299
  45.4 3.1 %collective-permute-start.18 = (f32[4,128]{1,0:T(4,128)S(1)}, f32[4,128]{1,0:T(4,128)S(1)}, u32[]{:S(2)}, u32[]{:S(2)}) collective-permute-start(f32[4,128]{1,0:T(4,128)S(1)} %get-tuple-element.31.lse_ref), channel_id=1, source_target_pairs={{0,24},{8,16},{16,8},{24,0},{1,25},{9,17},{17,9},{25,1},{2,26},{10... | collective-permute-start | bytes 6152 | tf_op jit(solution)/shard_map/ppermute | solution.py:299
  47.0 3.6 %collective-permute-start.17 = (f32[4,128]{1,0:T(4,128)S(1)}, f32[4,128]{1,0:T(4,128)S(1)}, u32[]{:S(2)}, u32[]{:S(2)}) collective-permute-start(f32[4,128]{1,0:T(4,128)S(1)} %get-tuple-element.31.lse_ref), channel_id=1, source_target_pairs={{0,16},{8,24},{16,0},{24,8},{1,17},{9,25},{17,1},{25,9},{2,18},{10... | collective-permute-start | bytes 6152 | tf_op jit(solution)/shard_map/ppermute | solution.py:299
  47.5 3.1 %collective-permute-start.16 = (f32[4,128]{1,0:T(4,128)S(1)}, f32[4,128]{1,0:T(4,128)S(1)}, u32[]{:S(2)}, u32[]{:S(2)}) collective-permute-start(f32[4,128]{1,0:T(4,128)S(1)} %get-tuple-element.31.lse_ref), channel_id=1, source_target_pairs={{0,8},{8,0},{16,24},{24,16},{1,9},{9,1},{17,25},{25,17},{2,10},{10... | collective-permute-start | bytes 6152 | tf_op jit(solution)/shard_map/ppermute | solution.py:299
  51.0 5.1 %collective-permute-start.19 = (f32[3,2,128,512]{3,2,1,0:T(8,128)S(1)}, f32[3,2,128,512]{3,2,1,0:T(8,128)S(1)}, u32[]{:S(2)}, u32[]{:S(2)}) collective-permute-start(f32[3,2,128,512]{3,2,1,0:T(8,128)S(1)} %get-tuple-element.32.refs_2_), channel_id=1, source_target_pairs={{0,8},{8,0},{16,24},{24,16},{1,9},{9,1},{17,25},{25,17},{2,10},{10... | collective-permute-start | bytes 4718600 | tf_op jit(solution)/shard_map/ppermute | solution.py:299
  51.1 14.3 %collective-permute-start.24 = (f32[256,512]{1,0:T(8,128)S(1)}, f32[256,512]{1,0:T(8,128)S(1)}, u32[]{:S(2)}, u32[]{:S(2)}) collective-permute-start(f32[256,512]{1,0:T(8,128)S(1)} %get-tuple-element.35.one_ref), channel_id=1, source_target_pairs={{0,16},{8,24},{16,0},{24,8},{1,17},{9,25},{17,1},{25,9},{2,18},{10... | collective-permute-start | bytes 1572872 | tf_op jit(solution)/shard_map/ppermute | solution.py:299
  51.7 5.7 %collective-permute-start.20 = (f32[4,128]{1,0:T(4,128)S(1)}, f32[4,128]{1,0:T(4,128)S(1)}, u32[]{:S(2)}, u32[]{:S(2)}) collective-permute-start(f32[4,128]{1,0:T(4,128)S(1)} %get-tuple-element.40.refs_5_), channel_id=1, source_target_pairs={{0,5},{1,4},{2,7},{3,6},{4,1},{5,0},{6,3},{7,2},{8,13},{9,12},{10,... | collective-permute-start | bytes 6152 | tf_op jit(solution)/shard_map/ppermute | solution.py:299
  54.4 4.5 %collective-permute-start.21 = (f32[4,128]{1,0:T(4,128)S(1)}, f32[4,128]{1,0:T(4,128)S(1)}, u32[]{:S(2)}, u32[]{:S(2)}) collective-permute-start(f32[4,128]{1,0:T(4,128)S(1)} %get-tuple-element.40.refs_5_), channel_id=1, source_target_pairs={{0,4},{1,5},{2,6},{3,7},{4,0},{5,1},{6,2},{7,3},{8,12},{9,13},{10,... | collective-permute-start | bytes 6152 | tf_op jit(solution)/shard_map/ppermute | solution.py:299
  55.3 3.6 %collective-permute-start.22 = (f32[4,128]{1,0:T(4,128)S(1)}, f32[4,128]{1,0:T(4,128)S(1)}, u32[]{:S(2)}, u32[]{:S(2)}) collective-permute-start(f32[4,128]{1,0:T(4,128)S(1)} %get-tuple-element.40.refs_5_), channel_id=1, source_target_pairs={{0,1},{1,0},{2,3},{3,2},{4,5},{5,4},{6,7},{7,6},{8,9},{9,8},{10,11... | collective-permute-start | bytes 6152 | tf_op jit(solution)/shard_map/ppermute | solution.py:299
  59.7 13.3 %collective-permute-start.23 = (f32[264,512]{1,0:T(8,128)S(1)}, f32[264,512]{1,0:T(8,128)S(1)}, u32[]{:S(2)}, u32[]{:S(2)}) collective-permute-start(f32[264,512]{1,0:T(8,128)S(1)} %shard_map.69), channel_id=1, source_target_pairs={{0,2},{1,3},{2,0},{3,1},{4,6},{5,7},{6,4},{7,5},{8,10},{9,11},{10,... | collective-permute-start | bytes 1622024 | tf_op jit(solution)/shard_map/ppermute | solution.py:299
  65.5 1.4 %collective-permute-start.25 = (f32[64,512]{1,0:T(8,128)S(1)}, f32[64,512]{1,0:T(8,128)S(1)}, u32[]{:S(2)}, u32[]{:S(2)}) collective-permute-start(f32[64,512]{1,0:T(8,128)S(1)} %get-tuple-element.36.refs_0_), channel_id=1, source_target_pairs={{0,8},{8,0},{16,24},{24,16},{1,9},{9,1},{17,25},{25,17},{2,10},{10... | collective-permute-start | bytes 393224 | tf_op jit(solution)/shard_map/ppermute | solution.py:299
  65.6 1.5 %collective-permute-start.26 = (f32[64,512]{1,0:T(8,128)S(1)}, f32[64,512]{1,0:T(8,128)S(1)}, u32[]{:S(2)}, u32[]{:S(2)}) collective-permute-start(f32[64,512]{1,0:T(8,128)S(1)} %get-tuple-element.37.refs_1_), channel_id=1, source_target_pairs={{0,8},{8,0},{16,24},{24,16},{1,9},{9,1},{17,25},{25,17},{2,10},{10... | collective-permute-start | bytes 393224 | tf_op jit(solution)/shard_map/ppermute | solution.py:299
  66.1 1.3 %collective-permute-start.27 = (f32[64,512]{1,0:T(8,128)S(1)}, f32[64,512]{1,0:T(8,128)S(1)}, u32[]{:S(2)}, u32[]{:S(2)}) collective-permute-start(f32[64,512]{1,0:T(8,128)S(1)} %get-tuple-element.38.refs_2_), channel_id=1, source_target_pairs={{0,8},{8,0},{16,24},{24,16},{1,9},{9,1},{17,25},{25,17},{2,10},{10... | collective-permute-start | bytes 393224 | tf_op jit(solution)/shard_map/ppermute | solution.py:299
  66.2 1.5 %collective-permute-start.28 = (f32[64,512]{1,0:T(8,128)S(1)}, f32[64,512]{1,0:T(8,128)S(1)}, u32[]{:S(2)}, u32[]{:S(2)}) collective-permute-start(f32[64,512]{1,0:T(8,128)S(1)} %get-tuple-element.39.refs_3_), channel_id=1, source_target_pairs={{0,8},{8,0},{16,24},{24,16},{1,9},{9,1},{17,25},{25,17},{2,10},{10... | collective-permute-start | bytes 393224 | tf_op jit(solution)/shard_map/ppermute | solution.py:299

commit v10 on v9

--- a/solution.py
+++ b/solution.py
@@ -207,13 +207,15 @@
         ref[...] = one_ref[at, :] + two_ref[at, :]
 
 
-def join_kernel(*refs):
-    parts, out_ref = refs[:-1], refs[-1]
-    rows = out_ref.shape[0]
-    lses = [ref[rows : rows + pl.cdiv(rows, LANES), :LANES] for ref in parts]
-    whole = merge_all(lses)
-    shares = [to_column(jnp.exp2(lse - whole))[:rows] for lse in lses]
-    out_ref[...] = sum(ref[:rows, :] * share for ref, share in zip(parts, shares))
+def join_kernel(n_pieces, *refs):
+    out_ref = refs[-1]
+    rows = out_ref.shape[0] // n_pieces
+    for k in range(n_pieces):
+        parts = refs[k:-1:n_pieces]
+        lses = [ref[rows : rows + pl.cdiv(rows, LANES), :LANES] for ref in parts]
+        whole = merge_all(lses)
+        shares = [to_column(jnp.exp2(lse - whole))[:rows] for lse in lses]
+        out_ref[pl.ds(k * rows, rows), :] = sum(ref[:rows, :] * share for ref, share in zip(parts, shares))
 
 
 def place_kernel(*refs):
@@ -253,11 +255,11 @@
 EXTRA = 8
 
 
-def images(flip, inner_ref, y_ref, bias_refs, scores_ref):
+def images(start, inner_ref, y_ref, bias_refs, scores_ref):
     rows = scores_ref.shape[0]
     n_shards = len(bias_refs)
     n_tgt = y_ref.shape[0] // n_shards
-    block = pl.ds(flip * rows, rows)
+    block = pl.ds(start, rows)
     peak = jnp.full((rows, 1), -jnp.inf, jnp.float32)
     for k, bias_ref in enumerate(bias_refs[::-1]):
         at = pl.ds(k * n_tgt, n_tgt)
@@ -284,9 +286,9 @@
 EXTRA = 8
 
 
-def image_kernel(flip, inner_ref, y_ref, *refs):
+def image_kernel(start, inner_ref, y_ref, *refs):
     bias_refs, (image_ref, scores_ref) = refs[:-2], refs[-2:]
-    numer, total, peak = images(flip, inner_ref, y_ref, bias_refs, scores_ref)
+    numer, total, peak = images(start, inner_ref, y_ref, bias_refs, scores_ref)
     rows = numer.shape[0]
     lse = lanes_of(peak + jnp.log2(total))
     image_ref[:rows, :] = numer * (1.0 / total)
@@ -340,14 +342,16 @@
                 tile, lt, sqy, *parts, *[pieces[k] for k in apart[2:]], early[-1],
             )
             late = along_y(late)
+        last = n_x if step == 0 else n_col // 2
+        group = [*bits_of(n_x), n_x + n_col // 2 - last]
+        rest = [bit for bit in bits_of(n_col) if bit not in group and bit != last] + [last]
+        ways = [0]
+        for bit in group:
+            ways += [way | bit for way in ways]
+        near = [lse] + [swap(lse, "col", way) for way in ways[:0:-1]]
         if step > 0:
-            rest = bits_of(n_col)
+            lse = merge_all(near[:1] + near[:0:-1])
         else:
-            group, rest = [*bits_of(n_x), n_col // 2], [bit for bit in bits_of(n_col // 2) if bit >= n_x]
-            ways = [0]
-            for bit in group:
-                ways += [way | bit for way in ways]
-            near = [lse] + [swap(lse, "col", way) for way in ways[:0:-1]]
             far = [k for k in pieces if k > 0]
             lse, early, *copies = call(
                 lambda *refs: merge_kernel(len(ways), *refs),
@@ -393,23 +397,26 @@
         limit=32,
     )
 
-    def image(flip):
+    n_images = 2
+    rows = count // n_images
+
+    def image(start):
         return call(
-            lambda *refs: image_kernel(flip, *refs),
-            f32(count + EXTRA, width),
+            lambda *refs: image_kernel(start, *refs),
+            f32(rows + EXTRA, width),
             inner, all_y, *biases[::-1],
-            scratch=[pltpu.VMEM((count, n_all), jnp.float32)],
+            scratch=[pltpu.VMEM((rows, n_all), jnp.float32)],
         )
 
-    came = swap(image(1), "col", n_x)
-    own = image(0)
+    came = [swap(image(count + k * rows), "col", n_x) for k in range(n_images)]
+    own = [image(k * rows) for k in range(n_images)]
     n_last = 4
     mine = call(add_kernel, (f32(half // n_last, width),) * n_last, mine, mine_came)
     target_image = call(
         place_kernel, f32(n_tgt, width), *mine, *[swap(piece, "row", 1) for piece in mine],
         out_specs=HBM, scratch=[DMA((2 * n_last,))],
     )
-    source_image = call(join_kernel, f32(count, width), own, came)
+    source_image = call(lambda *refs: join_kernel(n_images, *refs), f32(count, width), *own, *came)
     return source_image, target_image
 
 

time: 74.3 us -> 74.5 us (level)
  waiting for transfers between devices: 25.5 us -> 23.7 us
  starting transfers between devices: 32.2 us -> 33.6 us
    ppermute x29 -> x31, waiting for transfers between devices: 25.5 us -> 23.7 us  [swap(): return lax.ppermute(value, axis, [(i, i ^ distance) for i in range(n)])]
    ppermute x29 -> x31, starting transfers between devices: 32.2 us -> 33.6 us  [swap(): return lax.ppermute(value, axis, [(i, i ^ distance) for i in range(n)])]
    pallas_call x14 -> x16, Pallas kernels: 12.1 us -> 12.8 us  [call(): pl.pallas_call(kernel, out_shape=out_shape, in_specs=in_specs or [VMEM] *...]
  transfers between devices with their start and end apart: 29 -> 31, of which waited for: 16 -> 15; matrix products, arithmetic and copies ran while one was open for 0% -> 0% of each run, Pallas kernels for 10% -> 11%
where the time goes in v10:
time: 74.5 us; the launch traced here: 74.3 us
  starting transfers between devices  33.6 us (45%)
  waiting for transfers between devices  23.7 us (32%)
  Pallas kernels  12.8 us (17%)
  local copies, waits for them, and re-layouts  3.32 us (4%)
  between operations  0.82 us (1%)
    ppermute x31, starting transfers between devices, swap(): return lax.ppermute(value, axis, [(i, i ^ distance) for i in range(n)])  33.6 us
    ppermute x31, waiting for transfers between devices, swap(): return lax.ppermute(value, axis, [(i, i ^ distance) for i in range(n)])  23.7 us
    pallas_call x16, Pallas kernels, call(): pl.pallas_call(kernel, out_shape=out_shape, in_specs=in_specs or [VMEM] *...  12.8 us
    unnamed x12, local copies, waits for them, and re-layouts  3.32 us
  transfers between devices with their start and end apart: 31, of which 15 were waited for; matrix products, arithmetic and copies ran while one was open for 0% of the time, Pallas kernels for 11%

profile of v10, /device:TPU:0, one launch (start us, length us, event | category | flops | bytes accessed | tf_op | source)
XLA Modules:
  0.0 74.3 jit_solution(10960254271082581255)
XLA Ops:
  0.6 0.0 copy-start.2
  0.6 1.0 %copy-done.2 = bf16[512,512]{1,0:T(8,128)(2,1)S(1)} copy-done((bf16[512,512]{1,0:T(8,128)(2,1)S(1)}, bf16[512,512]{1,0:T(8,128)(2,1)}, u32[]{:S(2)}) %copy-start.2) | copy-done | bytes 524312
  1.7 4.1 %collective-permute-start.3 = (f32[128,512]{1,0:T(8,128)S(1)}, f32[128,512]{1,0:T(8,128)S(1)}, u32[]{:S(2)}, u32[]{:S(2)}) collective-permute-start(f32[128,512]{1,0:T(8,128)S(1)} %shard_map.61), channel_id=1, source_target_pairs={{0,4},{1,5},{2,6},{3,7},{4,0},{5,1},{6,2},{7,3},{8,12},{9,13},{10,... | collective-permute-start | bytes 786440 | tf_op jit(solution)/shard_map/ppermute | solution.py:301
  5.8 1.5 %collective-permute-start.4 = (f32[128,512]{1,0:T(8,128)S(1)}, f32[128,512]{1,0:T(8,128)S(1)}, u32[]{:S(2)}, u32[]{:S(2)}) collective-permute-start(f32[128,512]{1,0:T(8,128)S(1)} %shard_map.61), channel_id=1, source_target_pairs={{0,1},{1,0},{2,3},{3,2},{4,5},{5,4},{6,7},{7,6},{8,9},{9,8},{10,11... | collective-permute-start | bytes 786440 | tf_op jit(solution)/shard_map/ppermute | solution.py:301
  7.3 1.6 %copy-done = bf16[2048,512]{1,0:T(8,128)(2,1)S(1)} copy-done((bf16[2048,512]{1,0:T(8,128)(2,1)S(1)}, bf16[2048,512]{1,0:T(8,128)(2,1)}, u32[]{:S(2)}) %copy-start) | copy-done | bytes 2097176
  8.9 0.7 copy-done.5
  9.6 1.9 %shard_map.59 = (f32[512,2048]{1,0:T(8,128)S(1)}, f32[16,128]{1,0:T(8,128)S(1)}, f32[4,128]{1,0:T(4,128)S(1)}) custom-call(bf16[512,512]{1,0:T(8,128)(2,1)S(1)} %copy-done.2, bf16[2048,512]{1,0:T(8,128)(2,1)S(1)} %copy-done, f32[4,128]{1,0:T(4,128)S(1)} %bitcast.5), custom_call_target="tpu_custom_call" | custom-call | tf_op jit(solution)/shard_map/pallas_call | solution.py:22
  11.5 0.1 collective-permute-start
  11.6 2.8 %collective-permute-start.1 = (f32[16,128]{1,0:T(8,128)S(1)}, f32[16,128]{1,0:T(8,128)S(1)}, u32[]{:S(2)}, u32[]{:S(2)}) collective-permute-start(f32[16,128]{1,0:T(8,128)S(1)} %get-tuple-element.23.refs_0_), channel_id=1, source_target_pairs={{0,4},{1,5},{2,6},{3,7},{4,0},{5,1},{6,2},{7,3},{8,12},{9,13},{10,... | collective-permute-start | bytes 24584 | tf_op jit(solution)/shard_map/ppermute | solution.py:301
  14.4 1.5 %collective-permute-start.2 = (f32[16,128]{1,0:T(8,128)S(1)}, f32[16,128]{1,0:T(8,128)S(1)}, u32[]{:S(2)}, u32[]{:S(2)}) collective-permute-start(f32[16,128]{1,0:T(8,128)S(1)} %get-tuple-element.23.refs_0_), channel_id=1, source_target_pairs={{0,1},{1,0},{2,3},{3,2},{4,5},{5,4},{6,7},{7,6},{8,9},{9,8},{10,11... | collective-permute-start | bytes 24584 | tf_op jit(solution)/shard_map/ppermute | solution.py:301
  15.9 3.4 %collective-permute-done.refs_1_ = f32[16,128]{1,0:T(8,128)S(1)} collective-permute-done((f32[16,128]{1,0:T(8,128)S(1)}, f32[16,128]{1,0:T(8,128)S(1)}, u32[]{:S(2)}, u32[]{:S(2)}) %collective-permute-start) | collective-permute-done | bytes 8224 | tf_op jit(solution)/shard_map/ppermute | solution.py:301
  19.4 1.6 %collective-permute-start.10 = (f32[192,512]{1,0:T(8,128)S(1)}, f32[192,512]{1,0:T(8,128)S(1)}, u32[]{:S(2)}, u32[]{:S(2)}) collective-permute-start(f32[192,512]{1,0:T(8,128)S(1)} %get-tuple-element.26.refs_0_), channel_id=1, source_target_pairs={{0,16},{8,24},{16,0},{24,8},{1,17},{9,25},{17,1},{25,9},{2,18},{10... | collective-permute-start | bytes 1179656 | tf_op jit(solution)/shard_map/ppermute | solution.py:301
  21.0 0.6 collective-permute-start.9
  21.6 1.2 %collective-permute-start.5 = (f32[16,128]{1,0:T(8,128)S(1)}, f32[16,128]{1,0:T(8,128)S(1)}, u32[]{:S(2)}, u32[]{:S(2)}) collective-permute-start(f32[16,128]{1,0:T(8,128)S(1)} %get-tuple-element.24.refs_3_), channel_id=1, source_target_pairs={{0,2},{1,3},{2,0},{3,1},{4,6},{5,7},{6,4},{7,5},{8,10},{9,11},{10,... | collective-permute-start | bytes 24584 | tf_op jit(solution)/shard_map/ppermute | solution.py:301
  22.8 0.5 shard_map.60.refs_2_.sqx_ref
  23.3 2.0 %collective-permute-done.5.refs_4_ = f32[16,128]{1,0:T(8,128)S(1)} collective-permute-done((f32[16,128]{1,0:T(8,128)S(1)}, f32[16,128]{1,0:T(8,128)S(1)}, u32[]{:S(2)}, u32[]{:S(2)}) %collective-permute-start.5) | collective-permute-done | bytes 8224 | tf_op jit(solution)/shard_map/ppermute | solution.py:301
  25.3 1.0 %shard_map.63.refs_3_ = f32[4,128]{1,0:T(4,128)S(1)} custom-call(f32[512,2048]{1,0:T(8,128)S(1)} %get-tuple-element.21.refs_0_.tile_ref, f32[16,128]{1,0:T(8,128)S(1)} %bitcast.3, f32[16,128]{1,0:T(8,128)S(1)} %shard_map.60.refs_2_.sqx_ref, f32[16,128]{1,0:T(8,128)S(1)} %get-tuple-element.24.refs_3_, f32[16,128]{1,0:T(8,128)S(1)} %collective-permute-done.5.refs_4_), custom_call_target="tpu_custom_call" | custom-call | tf_op jit(solution)/shard_map/pallas_call | solution.py:22
  26.3 0.0 collective-permute-start.6
  26.3 0.6 collective-permute-start.7
  26.9 1.3 %collective-permute-start.8 = (f32[4,128]{1,0:T(4,128)S(1)}, f32[4,128]{1,0:T(4,128)S(1)}, u32[]{:S(2)}, u32[]{:S(2)}) collective-permute-start(f32[4,128]{1,0:T(4,128)S(1)} %shard_map.63.refs_3_), channel_id=1, source_target_pairs={{0,24},{8,16},{16,8},{24,0},{1,25},{9,17},{17,9},{25,1},{2,26},{10... | collective-permute-start | bytes 6152 | tf_op jit(solution)/shard_map/ppermute | solution.py:301
  28.2 1.8 %collective-permute-done.7.refs_5_ = f32[4,128]{1,0:T(4,128)S(1)} collective-permute-done((f32[4,128]{1,0:T(4,128)S(1)}, f32[4,128]{1,0:T(4,128)S(1)}, u32[]{:S(2)}, u32[]{:S(2)}) %collective-permute-start.7) | collective-permute-done | bytes 2080 | tf_op jit(solution)/shard_map/ppermute | solution.py:301
  30.0 1.1 %shard_map.64 = (f32[16,128]{1,0:T(8,128)S(1)}, f32[192,512]{1,0:T(8,128)S(1)}) custom-call(f32[512,2048]{1,0:T(8,128)S(1)} %get-tuple-element.21.refs_0_.tile_ref, f32[4,128]{1,0:T(4,128)S(1)} %bitcast.6, f32[4,128]{1,0:T(4,128)S(1)} %get-tuple-element.22.refs_2_, f32[4,128]{1,0:T(4,128)S(1)} %shard_map.63.refs_3_, ...), custom_call_target="tpu_custom_call" | custom-call | tf_op jit(solution)/shard_map/pallas_call | solution.py:22
  31.1 1.5 %collective-permute-start.15 = (f32[192,512]{1,0:T(8,128)S(1)}, f32[192,512]{1,0:T(8,128)S(1)}, u32[]{:S(2)}, u32[]{:S(2)}) collective-permute-start(f32[192,512]{1,0:T(8,128)S(1)} %get-tuple-element.28.refs_2_), channel_id=1, source_target_pairs={{0,16},{8,24},{16,0},{24,8},{1,17},{9,25},{17,1},{25,9},{2,18},{10... | collective-permute-start | bytes 1179656 | tf_op jit(solution)/shard_map/ppermute | solution.py:301
  32.6 1.4 %collective-permute-start.13 = (f32[16,128]{1,0:T(8,128)S(1)}, f32[16,128]{1,0:T(8,128)S(1)}, u32[]{:S(2)}, u32[]{:S(2)}) collective-permute-start(f32[16,128]{1,0:T(8,128)S(1)} %get-tuple-element.27), channel_id=1, source_target_pairs={{0,3},{1,2},{2,1},{3,0},{4,7},{5,6},{6,5},{7,4},{8,11},{9,10},{10,... | collective-permute-start | bytes 24584 | tf_op jit(solution)/shard_map/ppermute | solution.py:301
  34.0 1.4 %collective-permute-start.12 = (f32[16,128]{1,0:T(8,128)S(1)}, f32[16,128]{1,0:T(8,128)S(1)}, u32[]{:S(2)}, u32[]{:S(2)}) collective-permute-start(f32[16,128]{1,0:T(8,128)S(1)} %get-tuple-element.27), channel_id=1, source_target_pairs={{0,2},{1,3},{2,0},{3,1},{4,6},{5,7},{6,4},{7,5},{8,10},{9,11},{10,... | collective-permute-start | bytes 24584 | tf_op jit(solution)/shard_map/ppermute | solution.py:301
  35.5 0.6 collective-permute-start.11
  36.1 1.1 %collective-permute-done.13 = f32[16,128]{1,0:T(8,128)S(1)} collective-permute-done((f32[16,128]{1,0:T(8,128)S(1)}, f32[16,128]{1,0:T(8,128)S(1)}, u32[]{:S(2)}, u32[]{:S(2)}) %collective-permute-start.13) | collective-permute-done | bytes 8224 | tf_op jit(solution)/shard_map/ppermute | solution.py:301
  37.2 0.5 collective-permute-done.12
  37.7 1.4 %collective-permute-done.11 = f32[16,128]{1,0:T(8,128)S(1)} collective-permute-done((f32[16,128]{1,0:T(8,128)S(1)}, f32[16,128]{1,0:T(8,128)S(1)}, u32[]{:S(2)}, u32[]{:S(2)}) %collective-permute-start.11) | collective-permute-done | bytes 8224 | tf_op jit(solution)/shard_map/ppermute | solution.py:301
  39.1 2.1 %collective-permute-start.14 = (f32[16,128]{1,0:T(8,128)S(1)}, f32[16,128]{1,0:T(8,128)S(1)}, u32[]{:S(2)}, u32[]{:S(2)}) collective-permute-start(f32[16,128]{1,0:T(8,128)S(1)} %multiply_add_fusion.refs_0_), channel_id=1, source_target_pairs={{0,4},{1,5},{2,6},{3,7},{4,0},{5,1},{6,2},{7,3},{8,12},{9,13},{10,... | collective-permute-start | bytes 24584 | tf_op jit(solution)/shard_map/ppermute | solution.py:301
  41.2 2.5 %collective-permute-done.14.refs_1_ = f32[16,128]{1,0:T(8,128)S(1)} collective-permute-done((f32[16,128]{1,0:T(8,128)S(1)}, f32[16,128]{1,0:T(8,128)S(1)}, u32[]{:S(2)}, u32[]{:S(2)}) %collective-permute-start.14) | collective-permute-done | bytes 8224 | tf_op jit(solution)/shard_map/ppermute | solution.py:301
  43.8 1.9 %shard_map.65 = (f32[4,128]{1,0:T(4,128)S(1)}, f32[256,512]{1,0:T(8,128)S(1)}, f32[256,512]{1,0:T(8,128)S(1)}) custom-call(f32[512,2048]{1,0:T(8,128)S(1)} %get-tuple-element.21.refs_0_.tile_ref, bf16[2048,512]{1,0:T(8,128)(2,1)S(1)} %copy-done.1, f32[16,128]{1,0:T(8,128)S(1)} %bitcast.4, f32[16,128]{1,0:T(8,128)S(1)} %shard_map.60.refs_2_.sqx_ref, ...), custom_call_target="tpu_custom_call" | custom-call | tf_op jit(solution)/shard_map/pallas_call | solution.py:22
  45.7 0.1 collective-permute-start.16
  45.8 0.7 collective-permute-start.19
  46.4 1.4 %collective-permute-start.18 = (f32[4,128]{1,0:T(4,128)S(1)}, f32[4,128]{1,0:T(4,128)S(1)}, u32[]{:S(2)}, u32[]{:S(2)}) collective-permute-start(f32[4,128]{1,0:T(4,128)S(1)} %get-tuple-element.31.lse_ref), channel_id=1, source_target_pairs={{0,16},{8,24},{16,0},{24,8},{1,17},{9,25},{17,1},{25,9},{2,18},{10... | collective-permute-start | bytes 6152 | tf_op jit(solution)/shard_map/ppermute | solution.py:301
  47.9 0.9 %collective-permute-done.19 = f32[4,128]{1,0:T(4,128)S(1)} collective-permute-done((f32[4,128]{1,0:T(4,128)S(1)}, f32[4,128]{1,0:T(4,128)S(1)}, u32[]{:S(2)}, u32[]{:S(2)}) %collective-permute-start.19) | collective-permute-done | bytes 2080 | tf_op jit(solution)/shard_map/ppermute | solution.py:301
  48.8 1.2 %collective-permute-done.18 = f32[4,128]{1,0:T(4,128)S(1)} collective-permute-done((f32[4,128]{1,0:T(4,128)S(1)}, f32[4,128]{1,0:T(4,128)S(1)}, u32[]{:S(2)}, u32[]{:S(2)}) %collective-permute-start.18) | collective-permute-done | bytes 2080 | tf_op jit(solution)/shard_map/ppermute | solution.py:301
  50.1 0.4 shard_map.66
  50.5 0.1 collective-permute-start.20
  50.6 1.5 %collective-permute-start.26 = (f32[256,512]{1,0:T(8,128)S(1)}, f32[256,512]{1,0:T(8,128)S(1)}, u32[]{:S(2)}, u32[]{:S(2)}) collective-permute-start(f32[256,512]{1,0:T(8,128)S(1)} %get-tuple-element.35.one_ref), channel_id=1, source_target_pairs={{0,16},{8,24},{16,0},{24,8},{1,17},{9,25},{17,1},{25,9},{2,18},{10... | collective-permute-start | bytes 1572872 | tf_op jit(solution)/shard_map/ppermute | solution.py:301
  52.1 2.4 %collective-permute-start.21 = (f32[4,128]{1,0:T(4,128)S(1)}, f32[4,128]{1,0:T(4,128)S(1)}, u32[]{:S(2)}, u32[]{:S(2)}) collective-permute-start(f32[4,128]{1,0:T(4,128)S(1)} %get-tuple-element.40.refs_5_), channel_id=1, source_target_pairs={{0,5},{1,4},{2,7},{3,6},{4,1},{5,0},{6,3},{7,2},{8,13},{9,12},{10,... | collective-permute-start | bytes 6152 | tf_op jit(solution)/shard_map/ppermute | solution.py:301
  54.5 0.6 collective-permute-start.22
  55.1 1.4 %collective-permute-start.23 = (f32[4,128]{1,0:T(4,128)S(1)}, f32[4,128]{1,0:T(4,128)S(1)}, u32[]{:S(2)}, u32[]{:S(2)}) collective-permute-start(f32[4,128]{1,0:T(4,128)S(1)} %get-tuple-element.40.refs_5_), channel_id=1, source_target_pairs={{0,1},{1,0},{2,3},{3,2},{4,5},{5,4},{6,7},{7,6},{8,9},{9,8},{10,11... | collective-permute-start | bytes 6152 | tf_op jit(solution)/shard_map/ppermute | solution.py:301
  56.5 1.3 %shard_map.67 = (bf16[2048,512]{1,0:T(8,128)(2,1)S(1)}, f32[512,2048]{1,0:T(8,128)S(1)}) custom-call(bf16[2048,512]{1,0:T(8,128)(2,1)S(1)} %copy-done.1, bf16[512,512]{1,0:T(8,128)(2,1)S(1)} %copy-done.3, f32[3,2,128,512]{3,2,1,0:T(8,128)S(1)} %get-tuple-element.32.refs_2_, f32[3,2,128,512]{3,2,1,0:T(8,128)S(1)} %collective-permute-done.20.refs_3_), custom_call_target="tpu_custom_call" | custom-call | tf_op jit(solution)/shard_map/pallas_call | solution.py:22
  57.8 1.1 %collective-permute-done.22.refs_3_ = f32[4,128]{1,0:T(4,128)S(1)} collective-permute-done((f32[4,128]{1,0:T(4,128)S(1)}, f32[4,128]{1,0:T(4,128)S(1)}, u32[]{:S(2)}, u32[]{:S(2)}) %collective-permute-start.22) | collective-permute-done | bytes 2080 | tf_op jit(solution)/shard_map/ppermute | solution.py:301
  59.0 0.6 shard_map.70
  59.6 2.1 %collective-permute-start.24 = (f32[136,512]{1,0:T(8,128)S(1)}, f32[136,512]{1,0:T(8,128)S(1)}, u32[]{:S(2)}, u32[]{:S(2)}) collective-permute-start(f32[136,512]{1,0:T(8,128)S(1)} %shard_map.70), channel_id=1, source_target_pairs={{0,2},{1,3},{2,0},{3,1},{4,6},{5,7},{6,4},{7,5},{8,10},{9,11},{10,... | collective-permute-start | bytes 835592 | tf_op jit(solution)/shard_map/ppermute | solution.py:301
  61.6 0.6 shard_map.71
  62.2 0.1 collective-permute-start.25
  62.3 2.6 %collective-permute-done.26.two_ref = f32[256,512]{1,0:T(8,128)S(1)} collective-permute-done((f32[256,512]{1,0:T(8,128)S(1)}, f32[256,512]{1,0:T(8,128)S(1)}, u32[]{:S(2)}, u32[]{:S(2)}) %collective-permute-start.26) | collective-permute-done | bytes 524320 | tf_op jit(solution)/shard_map/ppermute | solution.py:301
  64.9 0.1 shard_map.73
  65.0 0.1 collective-permute-start.27
  65.0 0.5 collective-permute-start.28
  65.5 0.1 collective-permute-start.29
  65.6 0.8 %collective-permute-done.27.refs_4_ = f32[64,512]{1,0:T(8,128)S(1)} collective-permute-done((f32[64,512]{1,0:T(8,128)S(1)}, f32[64,512]{1,0:T(8,128)S(1)}, u32[]{:S(2)}, u32[]{:S(2)}) %collective-permute-start.27) | collective-permute-done | bytes 131104 | tf_op jit(solution)/shard_map/ppermute | solution.py:301
  66.4 0.1 collective-permute-start.30
  66.5 0.0 collective-permute-done.28.refs_5_
  66.6 0.3 collective-permute-done.29.refs_6_
  66.9 0.8 %collective-permute-done.30.refs_7_ = f32[64,512]{1,0:T(8,128)S(1)} collective-permute-done((f32[64,512]{1,0:T(8,128)S(1)}, f32[64,512]{1,0:T(8,128)S(1)}, u32[]{:S(2)}, u32[]{:S(2)}) %collective-permute-start.30) | collective-permute-done | bytes 131104 | tf_op jit(solution)/shard_map/ppermute | solution.py:301
  67.7 1.0 %shard_map.74 = f32[512,512]{1,0:T(8,128)} custom-call(f32[64,512]{1,0:T(8,128)S(1)} %get-tuple-element.36.refs_0_, f32[64,512]{1,0:T(8,128)S(1)} %get-tuple-element.37.refs_1_, f32[64,512]{1,0:T(8,128)S(1)} %get-tuple-element.38.refs_2_, f32[64,512]{1,0:T(8,128)S(1)} %get-tuple-element.39.refs_3_, f32[64,512]{1,0:T(8,128)S(1)} %collective-permute-done.27.refs_4_, ...), custom_call_target="tpu_custom_call" | custom-call | tf_op jit(solution)/shard_map/pallas_call | solution.py:22
  68.7 0.6 shard_map.68.refs_0_
  69.3 0.6 shard_map.69.refs_1_
  70.0 3.2 %collective-permute-done.25.refs_3_ = f32[136,512]{1,0:T(8,128)S(1)} collective-permute-done((f32[136,512]{1,0:T(8,128)S(1)}, f32[136,512]{1,0:T(8,128)S(1)}, u32[]{:S(2)}, u32[]{:S(2)}) %collective-permute-start.25) | collective-permute-done | bytes 278560 | tf_op jit(solution)/shard_map/ppermute | solution.py:301
  73.2 1.1 %shard_map.72 = f32[256,512]{1,0:T(8,128)} custom-call(f32[136,512]{1,0:T(8,128)S(1)} %shard_map.68.refs_0_, f32[136,512]{1,0:T(8,128)S(1)} %shard_map.69.refs_1_, f32[136,512]{1,0:T(8,128)S(1)} %collective-permute-done.24.refs_2_, f32[136,512]{1,0:T(8,128)S(1)} %collective-permute-done.25.refs_3_), custom_call_target="tpu_custom_call" | custom-call | tf_op jit(solution)/shard_map/pallas_call | solution.py:22
  (28 shorter events, 0.2 us)
Async XLA Ops:
  0.6 1.0 %copy-start.2 = (bf16[512,512]{1,0:T(8,128)(2,1)S(1)}, bf16[512,512]{1,0:T(8,128)(2,1)}, u32[]{:S(2)}) copy-start(bf16[512,512]{1,0:T(8,128)(2,1)} %refs_1_.1) | copy-start | bytes 1572868
  1.7 17.6 %collective-permute-start.3 = (f32[128,512]{1,0:T(8,128)S(1)}, f32[128,512]{1,0:T(8,128)S(1)}, u32[]{:S(2)}, u32[]{:S(2)}) collective-permute-start(f32[128,512]{1,0:T(8,128)S(1)} %shard_map.61), channel_id=1, source_target_pairs={{0,4},{1,5},{2,6},{3,7},{4,0},{5,1},{6,2},{7,3},{8,12},{9,13},{10,... | collective-permute-start | bytes 786440 | tf_op jit(solution)/shard_map/ppermute | solution.py:301
  5.8 13.5 %collective-permute-start.4 = (f32[128,512]{1,0:T(8,128)S(1)}, f32[128,512]{1,0:T(8,128)S(1)}, u32[]{:S(2)}, u32[]{:S(2)}) collective-permute-start(f32[128,512]{1,0:T(8,128)S(1)} %shard_map.61), channel_id=1, source_target_pairs={{0,1},{1,0},{2,3},{3,2},{4,5},{5,4},{6,7},{7,6},{8,9},{9,8},{10,11... | collective-permute-start | bytes 786440 | tf_op jit(solution)/shard_map/ppermute | solution.py:301
  7.3 1.6 %copy-start = (bf16[2048,512]{1,0:T(8,128)(2,1)S(1)}, bf16[2048,512]{1,0:T(8,128)(2,1)}, u32[]{:S(2)}) copy-start(bf16[2048,512]{1,0:T(8,128)(2,1)} %refs_0_.1) | copy-start | bytes 6291460
  8.9 0.7 copy-start.5
  9.6 13.2 %copy-start.1 = (bf16[2048,512]{1,0:T(8,128)(2,1)S(1)}, bf16[2048,512]{1,0:T(8,128)(2,1)}, u32[]{:S(2)}) copy-start(bf16[2048,512]{1,0:T(8,128)(2,1)} %refs_0_.1) | copy-start | bytes 6291460
  9.6 15.7 %copy-start.4 = (f32[2048]{0:T(1024)S(1)}, f32[2048]{0:T(1024)}, u32[]{:S(2)}) copy-start(f32[2048]{0:T(1024)} %param.6) | copy-start | bytes 24580
  11.5 7.8 %collective-permute-start = (f32[16,128]{1,0:T(8,128)S(1)}, f32[16,128]{1,0:T(8,128)S(1)}, u32[]{:S(2)}, u32[]{:S(2)}) collective-permute-start(f32[16,128]{1,0:T(8,128)S(1)} %get-tuple-element.23.refs_0_), channel_id=1, source_target_pairs={{0,5},{1,4},{2,7},{3,6},{4,1},{5,0},{6,3},{7,2},{8,13},{9,12},{10,... | collective-permute-start | bytes 24584 | tf_op jit(solution)/shard_map/ppermute | solution.py:301
  11.6 7.7 %collective-permute-start.1 = (f32[16,128]{1,0:T(8,128)S(1)}, f32[16,128]{1,0:T(8,128)S(1)}, u32[]{:S(2)}, u32[]{:S(2)}) collective-permute-start(f32[16,128]{1,0:T(8,128)S(1)} %get-tuple-element.23.refs_0_), channel_id=1, source_target_pairs={{0,4},{1,5},{2,6},{3,7},{4,0},{5,1},{6,2},{7,3},{8,12},{9,13},{10,... | collective-permute-start | bytes 24584 | tf_op jit(solution)/shard_map/ppermute | solution.py:301
  14.4 4.9 %collective-permute-start.2 = (f32[16,128]{1,0:T(8,128)S(1)}, f32[16,128]{1,0:T(8,128)S(1)}, u32[]{:S(2)}, u32[]{:S(2)}) collective-permute-start(f32[16,128]{1,0:T(8,128)S(1)} %get-tuple-element.23.refs_0_), channel_id=1, source_target_pairs={{0,1},{1,0},{2,3},{3,2},{4,5},{5,4},{6,7},{7,6},{8,9},{9,8},{10,11... | collective-permute-start | bytes 24584 | tf_op jit(solution)/shard_map/ppermute | solution.py:301
  19.4 10.6 %collective-permute-start.10 = (f32[192,512]{1,0:T(8,128)S(1)}, f32[192,512]{1,0:T(8,128)S(1)}, u32[]{:S(2)}, u32[]{:S(2)}) collective-permute-start(f32[192,512]{1,0:T(8,128)S(1)} %get-tuple-element.26.refs_0_), channel_id=1, source_target_pairs={{0,16},{8,24},{16,0},{24,8},{1,17},{9,25},{17,1},{25,9},{2,18},{10... | collective-permute-start | bytes 1179656 | tf_op jit(solution)/shard_map/ppermute | solution.py:301
  21.0 9.0 %collective-permute-start.9 = (f32[128,512]{1,0:T(8,128)S(1)}, f32[128,512]{1,0:T(8,128)S(1)}, u32[]{:S(2)}, u32[]{:S(2)}) collective-permute-start(f32[128,512]{1,0:T(8,128)S(1)} %get-tuple-element.25.refs_7_), channel_id=1, source_target_pairs={{0,1},{1,0},{2,3},{3,2},{4,5},{5,4},{6,7},{7,6},{8,9},{9,8},{10,11... | collective-permute-start | bytes 786440 | tf_op jit(solution)/shard_map/ppermute | solution.py:301
  21.6 3.7 %collective-permute-start.5 = (f32[16,128]{1,0:T(8,128)S(1)}, f32[16,128]{1,0:T(8,128)S(1)}, u32[]{:S(2)}, u32[]{:S(2)}) collective-permute-start(f32[16,128]{1,0:T(8,128)S(1)} %get-tuple-element.24.refs_3_), channel_id=1, source_target_pairs={{0,2},{1,3},{2,0},{3,1},{4,6},{5,7},{6,4},{7,5},{8,10},{9,11},{10,... | collective-permute-start | bytes 24584 | tf_op jit(solution)/shard_map/ppermute | solution.py:301
  26.3 1.9 %collective-permute-start.6 = (f32[4,128]{1,0:T(4,128)S(1)}, f32[4,128]{1,0:T(4,128)S(1)}, u32[]{:S(2)}, u32[]{:S(2)}) collective-permute-start(f32[4,128]{1,0:T(4,128)S(1)} %shard_map.63.refs_3_), channel_id=1, source_target_pairs={{0,8},{8,0},{16,24},{24,16},{1,9},{9,1},{17,25},{25,17},{2,10},{10... | collective-permute-start | bytes 6152 | tf_op jit(solution)/shard_map/ppermute | solution.py:301
  26.3 3.7 %collective-permute-start.7 = (f32[4,128]{1,0:T(4,128)S(1)}, f32[4,128]{1,0:T(4,128)S(1)}, u32[]{:S(2)}, u32[]{:S(2)}) collective-permute-start(f32[4,128]{1,0:T(4,128)S(1)} %shard_map.63.refs_3_), channel_id=1, source_target_pairs={{0,16},{8,24},{16,0},{24,8},{1,17},{9,25},{17,1},{25,9},{2,18},{10... | collective-permute-start | bytes 6152 | tf_op jit(solution)/shard_map/ppermute | solution.py:301
  26.9 3.1 %collective-permute-start.8 = (f32[4,128]{1,0:T(4,128)S(1)}, f32[4,128]{1,0:T(4,128)S(1)}, u32[]{:S(2)}, u32[]{:S(2)}) collective-permute-start(f32[4,128]{1,0:T(4,128)S(1)} %shard_map.63.refs_3_), channel_id=1, source_target_pairs={{0,24},{8,16},{16,8},{24,0},{1,25},{9,17},{17,9},{25,1},{2,26},{10... | collective-permute-start | bytes 6152 | tf_op jit(solution)/shard_map/ppermute | solution.py:301
  31.1 12.7 %collective-permute-start.15 = (f32[192,512]{1,0:T(8,128)S(1)}, f32[192,512]{1,0:T(8,128)S(1)}, u32[]{:S(2)}, u32[]{:S(2)}) collective-permute-start(f32[192,512]{1,0:T(8,128)S(1)} %get-tuple-element.28.refs_2_), channel_id=1, source_target_pairs={{0,16},{8,24},{16,0},{24,8},{1,17},{9,25},{17,1},{25,9},{2,18},{10... | collective-permute-start | bytes 1179656 | tf_op jit(solution)/shard_map/ppermute | solution.py:301
  32.6 4.5 %collective-permute-start.13 = (f32[16,128]{1,0:T(8,128)S(1)}, f32[16,128]{1,0:T(8,128)S(1)}, u32[]{:S(2)}, u32[]{:S(2)}) collective-permute-start(f32[16,128]{1,0:T(8,128)S(1)} %get-tuple-element.27), channel_id=1, source_target_pairs={{0,3},{1,2},{2,1},{3,0},{4,7},{5,6},{6,5},{7,4},{8,11},{9,10},{10,... | collective-permute-start | bytes 24584 | tf_op jit(solution)/shard_map/ppermute | solution.py:301
  34.0 3.7 %collective-permute-start.12 = (f32[16,128]{1,0:T(8,128)S(1)}, f32[16,128]{1,0:T(8,128)S(1)}, u32[]{:S(2)}, u32[]{:S(2)}) collective-permute-start(f32[16,128]{1,0:T(8,128)S(1)} %get-tuple-element.27), channel_id=1, source_target_pairs={{0,2},{1,3},{2,0},{3,1},{4,6},{5,7},{6,4},{7,5},{8,10},{9,11},{10,... | collective-permute-start | bytes 24584 | tf_op jit(solution)/shard_map/ppermute | solution.py:301
  35.5 3.7 %collective-permute-start.11 = (f32[16,128]{1,0:T(8,128)S(1)}, f32[16,128]{1,0:T(8,128)S(1)}, u32[]{:S(2)}, u32[]{:S(2)}) collective-permute-start(f32[16,128]{1,0:T(8,128)S(1)} %get-tuple-element.27), channel_id=1, source_target_pairs={{0,1},{1,0},{2,3},{3,2},{4,5},{5,4},{6,7},{7,6},{8,9},{9,8},{10,11... | collective-permute-start | bytes 24584 | tf_op jit(solution)/shard_map/ppermute | solution.py:301
  39.1 4.6 %collective-permute-start.14 = (f32[16,128]{1,0:T(8,128)S(1)}, f32[16,128]{1,0:T(8,128)S(1)}, u32[]{:S(2)}, u32[]{:S(2)}) collective-permute-start(f32[16,128]{1,0:T(8,128)S(1)} %multiply_add_fusion.refs_0_), channel_id=1, source_target_pairs={{0,4},{1,5},{2,6},{3,7},{4,0},{5,1},{6,2},{7,3},{8,12},{9,13},{10,... | collective-permute-start | bytes 24584 | tf_op jit(solution)/shard_map/ppermute | solution.py:301
  45.7 10.8 %copy-start.3 = (bf16[512,512]{1,0:T(8,128)(2,1)S(1)}, bf16[512,512]{1,0:T(8,128)(2,1)}, u32[]{:S(2)}) copy-start(bf16[512,512]{1,0:T(8,128)(2,1)} %refs_1_.1) | copy-start | bytes 1572868
  45.7 4.4 %collective-permute-start.16 = (f32[256,512]{1,0:T(8,128)S(1)}, f32[256,512]{1,0:T(8,128)S(1)}, u32[]{:S(2)}, u32[]{:S(2)}) collective-permute-start(f32[256,512]{1,0:T(8,128)S(1)} %get-tuple-element.30), channel_id=1, source_target_pairs={{0,8},{8,0},{16,24},{24,16},{1,9},{9,1},{17,25},{25,17},{2,10},{10... | collective-permute-start | bytes 1572872 | tf_op jit(solution)/shard_map/ppermute | solution.py:301
  45.8 3.1 %collective-permute-start.19 = (f32[4,128]{1,0:T(4,128)S(1)}, f32[4,128]{1,0:T(4,128)S(1)}, u32[]{:S(2)}, u32[]{:S(2)}) collective-permute-start(f32[4,128]{1,0:T(4,128)S(1)} %get-tuple-element.31.lse_ref), channel_id=1, source_target_pairs={{0,24},{8,16},{16,8},{24,0},{1,25},{9,17},{17,9},{25,1},{2,26},{10... | collective-permute-start | bytes 6152 | tf_op jit(solution)/shard_map/ppermute | solution.py:301
  46.4 3.6 %collective-permute-start.18 = (f32[4,128]{1,0:T(4,128)S(1)}, f32[4,128]{1,0:T(4,128)S(1)}, u32[]{:S(2)}, u32[]{:S(2)}) collective-permute-start(f32[4,128]{1,0:T(4,128)S(1)} %get-tuple-element.31.lse_ref), channel_id=1, source_target_pairs={{0,16},{8,24},{16,0},{24,8},{1,17},{9,25},{17,1},{25,9},{2,18},{10... | collective-permute-start | bytes 6152 | tf_op jit(solution)/shard_map/ppermute | solution.py:301
  47.9 2.1 %collective-permute-start.17 = (f32[4,128]{1,0:T(4,128)S(1)}, f32[4,128]{1,0:T(4,128)S(1)}, u32[]{:S(2)}, u32[]{:S(2)}) collective-permute-start(f32[4,128]{1,0:T(4,128)S(1)} %get-tuple-element.31.lse_ref), channel_id=1, source_target_pairs={{0,8},{8,0},{16,24},{24,16},{1,9},{9,1},{17,25},{25,17},{2,10},{10... | collective-permute-start | bytes 6152 | tf_op jit(solution)/shard_map/ppermute | solution.py:301
  50.5 6.0 %collective-permute-start.20 = (f32[3,2,128,512]{3,2,1,0:T(8,128)S(1)}, f32[3,2,128,512]{3,2,1,0:T(8,128)S(1)}, u32[]{:S(2)}, u32[]{:S(2)}) collective-permute-start(f32[3,2,128,512]{3,2,1,0:T(8,128)S(1)} %get-tuple-element.32.refs_2_), channel_id=1, source_target_pairs={{0,8},{8,0},{16,24},{24,16},{1,9},{9,1},{17,25},{25,17},{2,10},{10... | collective-permute-start | bytes 4718600 | tf_op jit(solution)/shard_map/ppermute | solution.py:301
  50.6 14.3 %collective-permute-start.26 = (f32[256,512]{1,0:T(8,128)S(1)}, f32[256,512]{1,0:T(8,128)S(1)}, u32[]{:S(2)}, u32[]{:S(2)}) collective-permute-start(f32[256,512]{1,0:T(8,128)S(1)} %get-tuple-element.35.one_ref), channel_id=1, source_target_pairs={{0,16},{8,24},{16,0},{24,8},{1,17},{9,25},{17,1},{25,9},{2,18},{10... | collective-permute-start | bytes 1572872 | tf_op jit(solution)/shard_map/ppermute | solution.py:301
  52.1 5.7 %collective-permute-start.21 = (f32[4,128]{1,0:T(4,128)S(1)}, f32[4,128]{1,0:T(4,128)S(1)}, u32[]{:S(2)}, u32[]{:S(2)}) collective-permute-start(f32[4,128]{1,0:T(4,128)S(1)} %get-tuple-element.40.refs_5_), channel_id=1, source_target_pairs={{0,5},{1,4},{2,7},{3,6},{4,1},{5,0},{6,3},{7,2},{8,13},{9,12},{10,... | collective-permute-start | bytes 6152 | tf_op jit(solution)/shard_map/ppermute | solution.py:301
  54.5 4.5 %collective-permute-start.22 = (f32[4,128]{1,0:T(4,128)S(1)}, f32[4,128]{1,0:T(4,128)S(1)}, u32[]{:S(2)}, u32[]{:S(2)}) collective-permute-start(f32[4,128]{1,0:T(4,128)S(1)} %get-tuple-element.40.refs_5_), channel_id=1, source_target_pairs={{0,4},{1,5},{2,6},{3,7},{4,0},{5,1},{6,2},{7,3},{8,12},{9,13},{10,... | collective-permute-start | bytes 6152 | tf_op jit(solution)/shard_map/ppermute | solution.py:301
  55.1 3.9 %collective-permute-start.23 = (f32[4,128]{1,0:T(4,128)S(1)}, f32[4,128]{1,0:T(4,128)S(1)}, u32[]{:S(2)}, u32[]{:S(2)}) collective-permute-start(f32[4,128]{1,0:T(4,128)S(1)} %get-tuple-element.40.refs_5_), channel_id=1, source_target_pairs={{0,1},{1,0},{2,3},{3,2},{4,5},{5,4},{6,7},{7,6},{8,9},{9,8},{10,11... | collective-permute-start | bytes 6152 | tf_op jit(solution)/shard_map/ppermute | solution.py:301
  59.6 10.4 %collective-permute-start.24 = (f32[136,512]{1,0:T(8,128)S(1)}, f32[136,512]{1,0:T(8,128)S(1)}, u32[]{:S(2)}, u32[]{:S(2)}) collective-permute-start(f32[136,512]{1,0:T(8,128)S(1)} %shard_map.70), channel_id=1, source_target_pairs={{0,2},{1,3},{2,0},{3,1},{4,6},{5,7},{6,4},{7,5},{8,10},{9,11},{10,... | collective-permute-start | bytes 835592 | tf_op jit(solution)/shard_map/ppermute | solution.py:301
  62.2 10.9 %collective-permute-start.25 = (f32[136,512]{1,0:T(8,128)S(1)}, f32[136,512]{1,0:T(8,128)S(1)}, u32[]{:S(2)}, u32[]{:S(2)}) collective-permute-start(f32[136,512]{1,0:T(8,128)S(1)} %shard_map.71), channel_id=1, source_target_pairs={{0,2},{1,3},{2,0},{3,1},{4,6},{5,7},{6,4},{7,5},{8,10},{9,11},{10,... | collective-permute-start | bytes 835592 | tf_op jit(solution)/shard_map/ppermute | solution.py:301
  65.0 1.4 %collective-permute-start.27 = (f32[64,512]{1,0:T(8,128)S(1)}, f32[64,512]{1,0:T(8,128)S(1)}, u32[]{:S(2)}, u32[]{:S(2)}) collective-permute-start(f32[64,512]{1,0:T(8,128)S(1)} %get-tuple-element.36.refs_0_), channel_id=1, source_target_pairs={{0,8},{8,0},{16,24},{24,16},{1,9},{9,1},{17,25},{25,17},{2,10},{10... | collective-permute-start | bytes 393224 | tf_op jit(solution)/shard_map/ppermute | solution.py:301
  65.0 1.5 %collective-permute-start.28 = (f32[64,512]{1,0:T(8,128)S(1)}, f32[64,512]{1,0:T(8,128)S(1)}, u32[]{:S(2)}, u32[]{:S(2)}) collective-permute-start(f32[64,512]{1,0:T(8,128)S(1)} %get-tuple-element.37.refs_1_), channel_id=1, source_target_pairs={{0,8},{8,0},{16,24},{24,16},{1,9},{9,1},{17,25},{25,17},{2,10},{10... | collective-permute-start | bytes 393224 | tf_op jit(solution)/shard_map/ppermute | solution.py:301
  65.5 1.3 %collective-permute-start.29 = (f32[64,512]{1,0:T(8,128)S(1)}, f32[64,512]{1,0:T(8,128)S(1)}, u32[]{:S(2)}, u32[]{:S(2)}) collective-permute-start(f32[64,512]{1,0:T(8,128)S(1)} %get-tuple-element.38.refs_2_), channel_id=1, source_target_pairs={{0,8},{8,0},{16,24},{24,16},{1,9},{9,1},{17,25},{25,17},{2,10},{10... | collective-permute-start | bytes 393224 | tf_op jit(solution)/shard_map/ppermute | solution.py:301
  66.4 1.3 %collective-permute-start.30 = (f32[64,512]{1,0:T(8,128)S(1)}, f32[64,512]{1,0:T(8,128)S(1)}, u32[]{:S(2)}, u32[]{:S(2)}) collective-permute-start(f32[64,512]{1,0:T(8,128)S(1)} %get-tuple-element.39.refs_3_), channel_id=1, source_target_pairs={{0,8},{8,0},{16,24},{24,16},{1,9},{9,1},{17,25},{25,17},{2,10},{10... | collective-permute-start | bytes 393224 | tf_op jit(solution)/shard_map/ppermute | solution.py:301

commit v11 on v9

--- a/solution.py
+++ b/solution.py
@@ -138,13 +138,17 @@
         copy[...] = piece[...]
 
 
+ROWS = 64
+
+
 def sources_kernel(n_parts, tile_ref, ls_ref, sqx_ref, *refs):
     bias = source_bias(ls_ref, sqx_ref, refs[:n_parts])
     columns = []
-    for j in range(tile_ref.shape[0] // LANES):
-        peak, total, _ = over_sources(tile_ref, pl.ds(j * LANES, LANES), bias)
+    for j in range(tile_ref.shape[0] // ROWS):
+        peak, total, _ = over_sources(tile_ref, pl.ds(j * ROWS, ROWS), bias)
         columns.append(peak + jnp.log2(total))
-    refs[-1][...] = to_dense(columns)
+    column = jnp.concatenate(columns, axis=0)
+    refs[-1][...] = to_dense([column[b : b + LANES] for b in range(0, column.shape[0], LANES)])
 
 
 def last_sources_kernel(tile_ref, x_ref, ls_ref, sqx_ref, *refs):
@@ -156,12 +160,17 @@
     for out_ref, place in ((sent_ref, 1 - core), (mine_ref, core)):
         columns = []
         for j in range(n_rows):
-            at = pl.ds(pl.multiple_of((place * n_rows + j) * LANES, LANES), LANES)
-            peak, total, exps = over_sources(tile_ref, at, bias)
-            columns.append(peak + jnp.log2(total))
-            weights = jnp.concatenate([block.astype(jnp.bfloat16) for block in exps], axis=1)
-            mean = jnp.dot(weights, x, preferred_element_type=jnp.float32)
-            out_ref[pl.ds(j * LANES, LANES), :] = mean * (1.0 / total)
+            totals, weights = [], []
+            for r in range(0, LANES, ROWS):
+                at = pl.ds(pl.multiple_of((place * n_rows + j) * LANES + r, ROWS), ROWS)
+                peak, total, exps = over_sources(tile_ref, at, bias)
+                columns.append(peak + jnp.log2(total))
+                totals.append(total)
+                weights.append(jnp.concatenate([block.astype(jnp.bfloat16) for block in exps], axis=1))
+            mean = jnp.dot(jnp.concatenate(weights, axis=0), x, preferred_element_type=jnp.float32)
+            out_ref[pl.ds(j * LANES, LANES), :] = mean * (1.0 / jnp.concatenate(totals, axis=0))
+        column = jnp.concatenate(columns, axis=0)
+        columns = [column[b : b + LANES] for b in range(0, column.shape[0], LANES)]
         lse_ref[pl.ds(place * n_rows, n_rows), :] = to_dense(columns)
 
 
@@ -208,12 +217,21 @@
 
 
 def join_kernel(*refs):
-    parts, out_ref = refs[:-1], refs[-1]
-    rows = out_ref.shape[0]
+    parts, (out_hbm, held_ref, sems) = refs[:-3], refs[-3:]
+    rows = held_ref.shape[0]
     lses = [ref[rows : rows + pl.cdiv(rows, LANES), :LANES] for ref in parts]
     whole = merge_all(lses)
     shares = [to_column(jnp.exp2(lse - whole))[:rows] for lse in lses]
-    out_ref[...] = sum(ref[:rows, :] * share for ref, share in zip(parts, shares))
+    n_pieces = sems.shape[0]
+    copies = []
+    for k in range(n_pieces):
+        at = pl.ds(k * rows // n_pieces, rows // n_pieces)
+        begin, end = k * rows // n_pieces, (k + 1) * rows // n_pieces
+        held_ref[at, :] = sum(ref[at, :] * share[begin:end] for ref, share in zip(parts, shares))
+        copies.append(pltpu.make_async_copy(held_ref.at[at, :], out_hbm.at[at, :], sems.at[k]))
+        copies[-1].start()
+    for copy in copies:
+        copy.wait()
 
 
 def place_kernel(*refs):
@@ -409,7 +427,10 @@
         place_kernel, f32(n_tgt, width), *mine, *[swap(piece, "row", 1) for piece in mine],
         out_specs=HBM, scratch=[DMA((2 * n_last,))],
     )
-    source_image = call(join_kernel, f32(count, width), own, came)
+    source_image = call(
+        join_kernel, f32(count, width), own, came,
+        out_specs=HBM, scratch=[pltpu.VMEM((count, width), jnp.float32), DMA((4,))],
+    )
     return source_image, target_image
 
 

time: 74.3 us -> 74.5 us (level)
  no operation moved by 1% of the time
where the time goes in v11:
time: 74.5 us; the launch traced here: 74.3 us
  starting transfers between devices  32.1 us (43%)
  waiting for transfers between devices  25.6 us (34%)
  Pallas kernels  12.3 us (17%)
  local copies, waits for them, and re-layouts  3.32 us (4%)
  between operations  0.8 us (1%)
    ppermute x29, starting transfers between devices, swap(): return lax.ppermute(value, axis, [(i, i ^ distance) for i in range(n)])  32.1 us
    ppermute x29, waiting for transfers between devices, swap(): return lax.ppermute(value, axis, [(i, i ^ distance) for i in range(n)])  25.6 us
    pallas_call x14, Pallas kernels, call(): pl.pallas_call(kernel, out_shape=out_shape, in_specs=in_specs or [VMEM] *...  12.3 us
    unnamed x12, local copies, waits for them, and re-layouts  3.32 us
  transfers between devices with their start and end apart: 29, of which 16 were waited for; matrix products, arithmetic and copies ran while one was open for 0% of the time, Pallas kernels for 10%

profile of v11, /device:TPU:0, one launch (start us, length us, event | category | flops | bytes accessed | tf_op | source)
XLA Modules:
  0.0 74.3 jit_solution(7941167488721330285)
XLA Ops:
  0.6 0.0 copy-start.2
  0.6 1.0 %copy-done.2 = bf16[512,512]{1,0:T(8,128)(2,1)S(1)} copy-done((bf16[512,512]{1,0:T(8,128)(2,1)S(1)}, bf16[512,512]{1,0:T(8,128)(2,1)}, u32[]{:S(2)}) %copy-start.2) | copy-done | bytes 524312
  1.7 4.1 %collective-permute-start.3 = (f32[128,512]{1,0:T(8,128)S(1)}, f32[128,512]{1,0:T(8,128)S(1)}, u32[]{:S(2)}, u32[]{:S(2)}) collective-permute-start(f32[128,512]{1,0:T(8,128)S(1)} %shard_map.61), channel_id=1, source_target_pairs={{0,4},{1,5},{2,6},{3,7},{4,0},{5,1},{6,2},{7,3},{8,12},{9,13},{10,... | collective-permute-start | bytes 786440 | tf_op jit(solution)/shard_map/ppermute | solution.py:317
  5.8 1.5 %collective-permute-start.4 = (f32[128,512]{1,0:T(8,128)S(1)}, f32[128,512]{1,0:T(8,128)S(1)}, u32[]{:S(2)}, u32[]{:S(2)}) collective-permute-start(f32[128,512]{1,0:T(8,128)S(1)} %shard_map.61), channel_id=1, source_target_pairs={{0,1},{1,0},{2,3},{3,2},{4,5},{5,4},{6,7},{7,6},{8,9},{9,8},{10,11... | collective-permute-start | bytes 786440 | tf_op jit(solution)/shard_map/ppermute | solution.py:317
  7.3 1.6 %copy-done = bf16[2048,512]{1,0:T(8,128)(2,1)S(1)} copy-done((bf16[2048,512]{1,0:T(8,128)(2,1)S(1)}, bf16[2048,512]{1,0:T(8,128)(2,1)}, u32[]{:S(2)}) %copy-start) | copy-done | bytes 2097176
  8.9 0.7 copy-done.5
  9.6 1.9 %shard_map.59 = (f32[512,2048]{1,0:T(8,128)S(1)}, f32[16,128]{1,0:T(8,128)S(1)}, f32[4,128]{1,0:T(4,128)S(1)}) custom-call(bf16[512,512]{1,0:T(8,128)(2,1)S(1)} %copy-done.2, bf16[2048,512]{1,0:T(8,128)(2,1)S(1)} %copy-done, f32[4,128]{1,0:T(4,128)S(1)} %bitcast.5), custom_call_target="tpu_custom_call" | custom-call | tf_op jit(solution)/shard_map/pallas_call | solution.py:22
  11.5 0.1 collective-permute-start
  11.6 2.8 %collective-permute-start.1 = (f32[16,128]{1,0:T(8,128)S(1)}, f32[16,128]{1,0:T(8,128)S(1)}, u32[]{:S(2)}, u32[]{:S(2)}) collective-permute-start(f32[16,128]{1,0:T(8,128)S(1)} %get-tuple-element.23.refs_0_), channel_id=1, source_target_pairs={{0,4},{1,5},{2,6},{3,7},{4,0},{5,1},{6,2},{7,3},{8,12},{9,13},{10,... | collective-permute-start | bytes 24584 | tf_op jit(solution)/shard_map/ppermute | solution.py:317
  14.4 1.5 %collective-permute-start.2 = (f32[16,128]{1,0:T(8,128)S(1)}, f32[16,128]{1,0:T(8,128)S(1)}, u32[]{:S(2)}, u32[]{:S(2)}) collective-permute-start(f32[16,128]{1,0:T(8,128)S(1)} %get-tuple-element.23.refs_0_), channel_id=1, source_target_pairs={{0,1},{1,0},{2,3},{3,2},{4,5},{5,4},{6,7},{7,6},{8,9},{9,8},{10,11... | collective-permute-start | bytes 24584 | tf_op jit(solution)/shard_map/ppermute | solution.py:317
  15.9 3.4 %collective-permute-done.refs_1_ = f32[16,128]{1,0:T(8,128)S(1)} collective-permute-done((f32[16,128]{1,0:T(8,128)S(1)}, f32[16,128]{1,0:T(8,128)S(1)}, u32[]{:S(2)}, u32[]{:S(2)}) %collective-permute-start) | collective-permute-done | bytes 8224 | tf_op jit(solution)/shard_map/ppermute | solution.py:317
  19.3 0.0 collective-permute-done.1.refs_2_
  19.3 0.0 collective-permute-done.2.refs_3_
  19.3 0.0 collective-permute-done.3.refs_4_
  19.4 1.6 %collective-permute-start.10 = (f32[192,512]{1,0:T(8,128)S(1)}, f32[192,512]{1,0:T(8,128)S(1)}, u32[]{:S(2)}, u32[]{:S(2)}) collective-permute-start(f32[192,512]{1,0:T(8,128)S(1)} %get-tuple-element.26.refs_0_), channel_id=1, source_target_pairs={{0,16},{8,24},{16,0},{24,8},{1,17},{9,25},{17,1},{25,9},{2,18},{10... | collective-permute-start | bytes 1179656 | tf_op jit(solution)/shard_map/ppermute | solution.py:317
  21.0 0.6 collective-permute-start.9
  21.6 1.2 %collective-permute-start.5 = (f32[16,128]{1,0:T(8,128)S(1)}, f32[16,128]{1,0:T(8,128)S(1)}, u32[]{:S(2)}, u32[]{:S(2)}) collective-permute-start(f32[16,128]{1,0:T(8,128)S(1)} %get-tuple-element.24.refs_3_), channel_id=1, source_target_pairs={{0,2},{1,3},{2,0},{3,1},{4,6},{5,7},{6,4},{7,5},{8,10},{9,11},{10,... | collective-permute-start | bytes 24584 | tf_op jit(solution)/shard_map/ppermute | solution.py:317
  22.8 0.5 shard_map.60.refs_2_.sqx_ref
  23.3 2.0 %collective-permute-done.5.refs_4_ = f32[16,128]{1,0:T(8,128)S(1)} collective-permute-done((f32[16,128]{1,0:T(8,128)S(1)}, f32[16,128]{1,0:T(8,128)S(1)}, u32[]{:S(2)}, u32[]{:S(2)}) %collective-permute-start.5) | collective-permute-done | bytes 8224 | tf_op jit(solution)/shard_map/ppermute | solution.py:317
  25.3 1.1 %shard_map.63.refs_3_ = f32[4,128]{1,0:T(4,128)S(1)} custom-call(f32[512,2048]{1,0:T(8,128)S(1)} %get-tuple-element.21.refs_0_.tile_ref, f32[16,128]{1,0:T(8,128)S(1)} %bitcast.3, f32[16,128]{1,0:T(8,128)S(1)} %shard_map.60.refs_2_.sqx_ref, f32[16,128]{1,0:T(8,128)S(1)} %get-tuple-element.24.refs_3_, f32[16,128]{1,0:T(8,128)S(1)} %collective-permute-done.5.refs_4_), custom_call_target="tpu_custom_call" | custom-call | tf_op jit(solution)/shard_map/pallas_call | solution.py:22
  26.4 0.0 collective-permute-start.6
  26.4 0.6 collective-permute-start.7
  27.0 1.3 %collective-permute-start.8 = (f32[4,128]{1,0:T(4,128)S(1)}, f32[4,128]{1,0:T(4,128)S(1)}, u32[]{:S(2)}, u32[]{:S(2)}) collective-permute-start(f32[4,128]{1,0:T(4,128)S(1)} %shard_map.63.refs_3_), channel_id=1, source_target_pairs={{0,24},{8,16},{16,8},{24,0},{1,25},{9,17},{17,9},{25,1},{2,26},{10... | collective-permute-start | bytes 6152 | tf_op jit(solution)/shard_map/ppermute | solution.py:317
  28.3 1.8 %collective-permute-done.7.refs_5_ = f32[4,128]{1,0:T(4,128)S(1)} collective-permute-done((f32[4,128]{1,0:T(4,128)S(1)}, f32[4,128]{1,0:T(4,128)S(1)}, u32[]{:S(2)}, u32[]{:S(2)}) %collective-permute-start.7) | collective-permute-done | bytes 2080 | tf_op jit(solution)/shard_map/ppermute | solution.py:317
  30.1 1.1 %shard_map.64 = (f32[16,128]{1,0:T(8,128)S(1)}, f32[192,512]{1,0:T(8,128)S(1)}) custom-call(f32[512,2048]{1,0:T(8,128)S(1)} %get-tuple-element.21.refs_0_.tile_ref, f32[4,128]{1,0:T(4,128)S(1)} %bitcast.6, f32[4,128]{1,0:T(4,128)S(1)} %get-tuple-element.22.refs_2_, f32[4,128]{1,0:T(4,128)S(1)} %shard_map.63.refs_3_, ...), custom_call_target="tpu_custom_call" | custom-call | tf_op jit(solution)/shard_map/pallas_call | solution.py:22
  31.2 1.4 %collective-permute-start.11 = (f32[16,128]{1,0:T(8,128)S(1)}, f32[16,128]{1,0:T(8,128)S(1)}, u32[]{:S(2)}, u32[]{:S(2)}) collective-permute-start(f32[16,128]{1,0:T(8,128)S(1)} %get-tuple-element.27), channel_id=1, source_target_pairs={{0,1},{1,0},{2,3},{3,2},{4,5},{5,4},{6,7},{7,6},{8,9},{9,8},{10,11... | collective-permute-start | bytes 24584 | tf_op jit(solution)/shard_map/ppermute | solution.py:317
  32.7 1.4 %collective-permute-start.14 = (f32[192,512]{1,0:T(8,128)S(1)}, f32[192,512]{1,0:T(8,128)S(1)}, u32[]{:S(2)}, u32[]{:S(2)}) collective-permute-start(f32[192,512]{1,0:T(8,128)S(1)} %get-tuple-element.28.refs_2_), channel_id=1, source_target_pairs={{0,16},{8,24},{16,0},{24,8},{1,17},{9,25},{17,1},{25,9},{2,18},{10... | collective-permute-start | bytes 1179656 | tf_op jit(solution)/shard_map/ppermute | solution.py:317
  34.1 0.8 %collective-permute-done.11 = f32[16,128]{1,0:T(8,128)S(1)} collective-permute-done((f32[16,128]{1,0:T(8,128)S(1)}, f32[16,128]{1,0:T(8,128)S(1)}, u32[]{:S(2)}, u32[]{:S(2)}) %collective-permute-start.11) | collective-permute-done | bytes 8224 | tf_op jit(solution)/shard_map/ppermute | solution.py:317
  34.9 1.2 %collective-permute-start.12 = (f32[16,128]{1,0:T(8,128)S(1)}, f32[16,128]{1,0:T(8,128)S(1)}, u32[]{:S(2)}, u32[]{:S(2)}) collective-permute-start(f32[16,128]{1,0:T(8,128)S(1)} %multiply_add_fusion.1), channel_id=1, source_target_pairs={{0,2},{1,3},{2,0},{3,1},{4,6},{5,7},{6,4},{7,5},{8,10},{9,11},{10,... | collective-permute-start | bytes 24584 | tf_op jit(solution)/shard_map/ppermute | solution.py:317
  36.2 2.5 %collective-permute-done.12 = f32[16,128]{1,0:T(8,128)S(1)} collective-permute-done((f32[16,128]{1,0:T(8,128)S(1)}, f32[16,128]{1,0:T(8,128)S(1)}, u32[]{:S(2)}, u32[]{:S(2)}) %collective-permute-start.12) | collective-permute-done | bytes 8224 | tf_op jit(solution)/shard_map/ppermute | solution.py:317
  38.7 2.2 %collective-permute-start.13 = (f32[16,128]{1,0:T(8,128)S(1)}, f32[16,128]{1,0:T(8,128)S(1)}, u32[]{:S(2)}, u32[]{:S(2)}) collective-permute-start(f32[16,128]{1,0:T(8,128)S(1)} %multiply_add_fusion.refs_0_), channel_id=1, source_target_pairs={{0,4},{1,5},{2,6},{3,7},{4,0},{5,1},{6,2},{7,3},{8,12},{9,13},{10,... | collective-permute-start | bytes 24584 | tf_op jit(solution)/shard_map/ppermute | solution.py:317
  40.9 2.4 %collective-permute-done.13.refs_1_ = f32[16,128]{1,0:T(8,128)S(1)} collective-permute-done((f32[16,128]{1,0:T(8,128)S(1)}, f32[16,128]{1,0:T(8,128)S(1)}, u32[]{:S(2)}, u32[]{:S(2)}) %collective-permute-start.13) | collective-permute-done | bytes 8224 | tf_op jit(solution)/shard_map/ppermute | solution.py:317
  43.3 0.2 collective-permute-done.14.refs_2_.refs_3_
  43.5 2.0 %shard_map.65 = (f32[4,128]{1,0:T(4,128)S(1)}, f32[256,512]{1,0:T(8,128)S(1)}, f32[256,512]{1,0:T(8,128)S(1)}) custom-call(f32[512,2048]{1,0:T(8,128)S(1)} %get-tuple-element.21.refs_0_.tile_ref, bf16[2048,512]{1,0:T(8,128)(2,1)S(1)} %copy-done.1, f32[16,128]{1,0:T(8,128)S(1)} %bitcast.4, f32[16,128]{1,0:T(8,128)S(1)} %shard_map.60.refs_2_.sqx_ref, ...), custom_call_target="tpu_custom_call" | custom-call | tf_op jit(solution)/shard_map/pallas_call | solution.py:22
  45.5 0.0 copy-start.3
  45.6 0.1 collective-permute-start.15
  45.6 1.6 %collective-permute-start.18 = (f32[4,128]{1,0:T(4,128)S(1)}, f32[4,128]{1,0:T(4,128)S(1)}, u32[]{:S(2)}, u32[]{:S(2)}) collective-permute-start(f32[4,128]{1,0:T(4,128)S(1)} %get-tuple-element.31.lse_ref), channel_id=1, source_target_pairs={{0,24},{8,16},{16,8},{24,0},{1,25},{9,17},{17,9},{25,1},{2,26},{10... | collective-permute-start | bytes 6152 | tf_op jit(solution)/shard_map/ppermute | solution.py:317
  47.3 0.5 collective-permute-start.17
  47.8 0.9 %collective-permute-done.18 = f32[4,128]{1,0:T(4,128)S(1)} collective-permute-done((f32[4,128]{1,0:T(4,128)S(1)}, f32[4,128]{1,0:T(4,128)S(1)}, u32[]{:S(2)}, u32[]{:S(2)}) %collective-permute-start.18) | collective-permute-done | bytes 2080 | tf_op jit(solution)/shard_map/ppermute | solution.py:317
  48.7 2.1 %collective-permute-done.17 = f32[4,128]{1,0:T(4,128)S(1)} collective-permute-done((f32[4,128]{1,0:T(4,128)S(1)}, f32[4,128]{1,0:T(4,128)S(1)}, u32[]{:S(2)}, u32[]{:S(2)}) %collective-permute-start.17) | collective-permute-done | bytes 2080 | tf_op jit(solution)/shard_map/ppermute | solution.py:317
  50.9 0.4 shard_map.66
  51.3 0.1 collective-permute-start.19
  51.4 0.6 collective-permute-start.24
  51.9 2.6 %collective-permute-start.20 = (f32[4,128]{1,0:T(4,128)S(1)}, f32[4,128]{1,0:T(4,128)S(1)}, u32[]{:S(2)}, u32[]{:S(2)}) collective-permute-start(f32[4,128]{1,0:T(4,128)S(1)} %get-tuple-element.40.refs_5_), channel_id=1, source_target_pairs={{0,5},{1,4},{2,7},{3,6},{4,1},{5,0},{6,3},{7,2},{8,13},{9,12},{10,... | collective-permute-start | bytes 6152 | tf_op jit(solution)/shard_map/ppermute | solution.py:317
  54.6 0.9 %collective-permute-start.21 = (f32[4,128]{1,0:T(4,128)S(1)}, f32[4,128]{1,0:T(4,128)S(1)}, u32[]{:S(2)}, u32[]{:S(2)}) collective-permute-start(f32[4,128]{1,0:T(4,128)S(1)} %get-tuple-element.40.refs_5_), channel_id=1, source_target_pairs={{0,4},{1,5},{2,6},{3,7},{4,0},{5,1},{6,2},{7,3},{8,12},{9,13},{10,... | collective-permute-start | bytes 6152 | tf_op jit(solution)/shard_map/ppermute | solution.py:317
  55.5 0.8 %collective-permute-start.22 = (f32[4,128]{1,0:T(4,128)S(1)}, f32[4,128]{1,0:T(4,128)S(1)}, u32[]{:S(2)}, u32[]{:S(2)}) collective-permute-start(f32[4,128]{1,0:T(4,128)S(1)} %get-tuple-element.40.refs_5_), channel_id=1, source_target_pairs={{0,1},{1,0},{2,3},{3,2},{4,5},{5,4},{6,7},{7,6},{8,9},{9,8},{10,11... | collective-permute-start | bytes 6152 | tf_op jit(solution)/shard_map/ppermute | solution.py:317
  56.3 1.3 %shard_map.67 = (bf16[2048,512]{1,0:T(8,128)(2,1)S(1)}, f32[512,2048]{1,0:T(8,128)S(1)}) custom-call(bf16[2048,512]{1,0:T(8,128)(2,1)S(1)} %copy-done.1, bf16[512,512]{1,0:T(8,128)(2,1)S(1)} %copy-done.3, f32[3,2,128,512]{3,2,1,0:T(8,128)S(1)} %get-tuple-element.32.refs_2_, f32[3,2,128,512]{3,2,1,0:T(8,128)S(1)} %collective-permute-done.19.refs_3_), custom_call_target="tpu_custom_call" | custom-call | tf_op jit(solution)/shard_map/pallas_call | solution.py:22
  57.7 1.4 %collective-permute-done.21.refs_3_ = f32[4,128]{1,0:T(4,128)S(1)} collective-permute-done((f32[4,128]{1,0:T(4,128)S(1)}, f32[4,128]{1,0:T(4,128)S(1)}, u32[]{:S(2)}, u32[]{:S(2)}) %collective-permute-start.21) | collective-permute-done | bytes 2080 | tf_op jit(solution)/shard_map/ppermute | solution.py:317
  59.1 0.9 %shard_map.69 = f32[264,512]{1,0:T(8,128)S(1)} custom-call(f32[512,2048]{1,0:T(8,128)S(1)} %get-tuple-element.33.refs_0_, bf16[2048,512]{1,0:T(8,128)(2,1)S(1)} %get-tuple-element.34.refs_1_, f32[4,128]{1,0:T(4,128)S(1)} %collective-permute-done.20.refs_2_, f32[4,128]{1,0:T(4,128)S(1)} %collective-permute-done.21.refs_3_, ...), custom_call_target="tpu_custom_call" | custom-call | tf_op jit(solution)/shard_map/pallas_call | solution.py:22
  60.0 2.1 %collective-permute-start.23 = (f32[264,512]{1,0:T(8,128)S(1)}, f32[264,512]{1,0:T(8,128)S(1)}, u32[]{:S(2)}, u32[]{:S(2)}) collective-permute-start(f32[264,512]{1,0:T(8,128)S(1)} %shard_map.69), channel_id=1, source_target_pairs={{0,2},{1,3},{2,0},{3,1},{4,6},{5,7},{6,4},{7,5},{8,10},{9,11},{10,... | collective-permute-start | bytes 1622024 | tf_op jit(solution)/shard_map/ppermute | solution.py:317
  62.0 3.7 %collective-permute-done.24.two_ref = f32[256,512]{1,0:T(8,128)S(1)} collective-permute-done((f32[256,512]{1,0:T(8,128)S(1)}, f32[256,512]{1,0:T(8,128)S(1)}, u32[]{:S(2)}, u32[]{:S(2)}) %collective-permute-start.24) | collective-permute-done | bytes 524320 | tf_op jit(solution)/shard_map/ppermute | solution.py:317
  65.7 0.1 shard_map.71
  65.8 0.1 collective-permute-start.25
  65.8 0.5 collective-permute-start.26
  66.3 0.1 collective-permute-start.27
  66.4 0.4 collective-permute-start.28
  66.8 0.3 collective-permute-done.25.refs_4_
  67.2 0.2 collective-permute-done.26.refs_5_
  67.4 0.3 collective-permute-done.27.refs_6_
  67.7 0.2 collective-permute-done.28.refs_7_
  67.9 1.0 %shard_map.72 = f32[512,512]{1,0:T(8,128)} custom-call(f32[64,512]{1,0:T(8,128)S(1)} %get-tuple-element.36.refs_0_, f32[64,512]{1,0:T(8,128)S(1)} %get-tuple-element.37.refs_1_, f32[64,512]{1,0:T(8,128)S(1)} %get-tuple-element.38.refs_2_, f32[64,512]{1,0:T(8,128)S(1)} %get-tuple-element.39.refs_3_, f32[64,512]{1,0:T(8,128)S(1)} %collective-permute-done.25.refs_4_, ...), custom_call_target="tpu_custom_call" | custom-call | tf_op jit(solution)/shard_map/pallas_call | solution.py:22
  68.9 0.9 %shard_map.68.refs_0_ = f32[264,512]{1,0:T(8,128)S(1)} custom-call(f32[512,2048]{1,0:T(8,128)S(1)} %get-tuple-element.33.refs_0_, bf16[2048,512]{1,0:T(8,128)(2,1)S(1)} %get-tuple-element.34.refs_1_, f32[4,128]{1,0:T(4,128)S(1)} %collective-permute-done.20.refs_2_, f32[4,128]{1,0:T(4,128)S(1)} %collective-permute-done.21.refs_3_, ...), custom_call_target="tpu_custom_call" | custom-call | tf_op jit(solution)/shard_map/pallas_call | solution.py:22
  69.8 3.4 %collective-permute-done.23.refs_1_ = f32[264,512]{1,0:T(8,128)S(1)} collective-permute-done((f32[264,512]{1,0:T(8,128)S(1)}, f32[264,512]{1,0:T(8,128)S(1)}, u32[]{:S(2)}, u32[]{:S(2)}) %collective-permute-start.23) | collective-permute-done | bytes 540704 | tf_op jit(solution)/shard_map/ppermute | solution.py:317
  73.2 1.0 %shard_map.70 = f32[256,512]{1,0:T(8,128)} custom-call(f32[264,512]{1,0:T(8,128)S(1)} %shard_map.68.refs_0_, f32[264,512]{1,0:T(8,128)S(1)} %collective-permute-done.23.refs_1_), custom_call_target="tpu_custom_call" | custom-call | tf_op jit(solution)/shard_map/pallas_call | solution.py:22
  (23 shorter events, 0.2 us)
Async XLA Ops:
  0.6 1.0 %copy-start.2 = (bf16[512,512]{1,0:T(8,128)(2,1)S(1)}, bf16[512,512]{1,0:T(8,128)(2,1)}, u32[]{:S(2)}) copy-start(bf16[512,512]{1,0:T(8,128)(2,1)} %refs_1_.1) | copy-start | bytes 1572868
  1.7 17.6 %collective-permute-start.3 = (f32[128,512]{1,0:T(8,128)S(1)}, f32[128,512]{1,0:T(8,128)S(1)}, u32[]{:S(2)}, u32[]{:S(2)}) collective-permute-start(f32[128,512]{1,0:T(8,128)S(1)} %shard_map.61), channel_id=1, source_target_pairs={{0,4},{1,5},{2,6},{3,7},{4,0},{5,1},{6,2},{7,3},{8,12},{9,13},{10,... | collective-permute-start | bytes 786440 | tf_op jit(solution)/shard_map/ppermute | solution.py:317
  5.8 13.5 %collective-permute-start.4 = (f32[128,512]{1,0:T(8,128)S(1)}, f32[128,512]{1,0:T(8,128)S(1)}, u32[]{:S(2)}, u32[]{:S(2)}) collective-permute-start(f32[128,512]{1,0:T(8,128)S(1)} %shard_map.61), channel_id=1, source_target_pairs={{0,1},{1,0},{2,3},{3,2},{4,5},{5,4},{6,7},{7,6},{8,9},{9,8},{10,11... | collective-permute-start | bytes 786440 | tf_op jit(solution)/shard_map/ppermute | solution.py:317
  7.3 1.6 %copy-start = (bf16[2048,512]{1,0:T(8,128)(2,1)S(1)}, bf16[2048,512]{1,0:T(8,128)(2,1)}, u32[]{:S(2)}) copy-start(bf16[2048,512]{1,0:T(8,128)(2,1)} %refs_0_.1) | copy-start | bytes 6291460
  8.9 0.7 copy-start.5
  9.6 13.2 %copy-start.1 = (bf16[2048,512]{1,0:T(8,128)(2,1)S(1)}, bf16[2048,512]{1,0:T(8,128)(2,1)}, u32[]{:S(2)}) copy-start(bf16[2048,512]{1,0:T(8,128)(2,1)} %refs_0_.1) | copy-start | bytes 6291460
  9.6 15.7 %copy-start.4 = (f32[2048]{0:T(1024)S(1)}, f32[2048]{0:T(1024)}, u32[]{:S(2)}) copy-start(f32[2048]{0:T(1024)} %param.6) | copy-start | bytes 24580
  11.5 7.8 %collective-permute-start = (f32[16,128]{1,0:T(8,128)S(1)}, f32[16,128]{1,0:T(8,128)S(1)}, u32[]{:S(2)}, u32[]{:S(2)}) collective-permute-start(f32[16,128]{1,0:T(8,128)S(1)} %get-tuple-element.23.refs_0_), channel_id=1, source_target_pairs={{0,5},{1,4},{2,7},{3,6},{4,1},{5,0},{6,3},{7,2},{8,13},{9,12},{10,... | collective-permute-start | bytes 24584 | tf_op jit(solution)/shard_map/ppermute | solution.py:317
  11.6 7.7 %collective-permute-start.1 = (f32[16,128]{1,0:T(8,128)S(1)}, f32[16,128]{1,0:T(8,128)S(1)}, u32[]{:S(2)}, u32[]{:S(2)}) collective-permute-start(f32[16,128]{1,0:T(8,128)S(1)} %get-tuple-element.23.refs_0_), channel_id=1, source_target_pairs={{0,4},{1,5},{2,6},{3,7},{4,0},{5,1},{6,2},{7,3},{8,12},{9,13},{10,... | collective-permute-start | bytes 24584 | tf_op jit(solution)/shard_map/ppermute | solution.py:317
  14.4 4.9 %collective-permute-start.2 = (f32[16,128]{1,0:T(8,128)S(1)}, f32[16,128]{1,0:T(8,128)S(1)}, u32[]{:S(2)}, u32[]{:S(2)}) collective-permute-start(f32[16,128]{1,0:T(8,128)S(1)} %get-tuple-element.23.refs_0_), channel_id=1, source_target_pairs={{0,1},{1,0},{2,3},{3,2},{4,5},{5,4},{6,7},{7,6},{8,9},{9,8},{10,11... | collective-permute-start | bytes 24584 | tf_op jit(solution)/shard_map/ppermute | solution.py:317
  19.4 10.7 %collective-permute-start.10 = (f32[192,512]{1,0:T(8,128)S(1)}, f32[192,512]{1,0:T(8,128)S(1)}, u32[]{:S(2)}, u32[]{:S(2)}) collective-permute-start(f32[192,512]{1,0:T(8,128)S(1)} %get-tuple-element.26.refs_0_), channel_id=1, source_target_pairs={{0,16},{8,24},{16,0},{24,8},{1,17},{9,25},{17,1},{25,9},{2,18},{10... | collective-permute-start | bytes 1179656 | tf_op jit(solution)/shard_map/ppermute | solution.py:317
  21.0 9.1 %collective-permute-start.9 = (f32[128,512]{1,0:T(8,128)S(1)}, f32[128,512]{1,0:T(8,128)S(1)}, u32[]{:S(2)}, u32[]{:S(2)}) collective-permute-start(f32[128,512]{1,0:T(8,128)S(1)} %get-tuple-element.25.refs_7_), channel_id=1, source_target_pairs={{0,1},{1,0},{2,3},{3,2},{4,5},{5,4},{6,7},{7,6},{8,9},{9,8},{10,11... | collective-permute-start | bytes 786440 | tf_op jit(solution)/shard_map/ppermute | solution.py:317
  21.6 3.7 %collective-permute-start.5 = (f32[16,128]{1,0:T(8,128)S(1)}, f32[16,128]{1,0:T(8,128)S(1)}, u32[]{:S(2)}, u32[]{:S(2)}) collective-permute-start(f32[16,128]{1,0:T(8,128)S(1)} %get-tuple-element.24.refs_3_), channel_id=1, source_target_pairs={{0,2},{1,3},{2,0},{3,1},{4,6},{5,7},{6,4},{7,5},{8,10},{9,11},{10,... | collective-permute-start | bytes 24584 | tf_op jit(solution)/shard_map/ppermute | solution.py:317
  26.4 1.9 %collective-permute-start.6 = (f32[4,128]{1,0:T(4,128)S(1)}, f32[4,128]{1,0:T(4,128)S(1)}, u32[]{:S(2)}, u32[]{:S(2)}) collective-permute-start(f32[4,128]{1,0:T(4,128)S(1)} %shard_map.63.refs_3_), channel_id=1, source_target_pairs={{0,8},{8,0},{16,24},{24,16},{1,9},{9,1},{17,25},{25,17},{2,10},{10... | collective-permute-start | bytes 6152 | tf_op jit(solution)/shard_map/ppermute | solution.py:317
  26.4 3.7 %collective-permute-start.7 = (f32[4,128]{1,0:T(4,128)S(1)}, f32[4,128]{1,0:T(4,128)S(1)}, u32[]{:S(2)}, u32[]{:S(2)}) collective-permute-start(f32[4,128]{1,0:T(4,128)S(1)} %shard_map.63.refs_3_), channel_id=1, source_target_pairs={{0,16},{8,24},{16,0},{24,8},{1,17},{9,25},{17,1},{25,9},{2,18},{10... | collective-permute-start | bytes 6152 | tf_op jit(solution)/shard_map/ppermute | solution.py:317
  27.0 3.1 %collective-permute-start.8 = (f32[4,128]{1,0:T(4,128)S(1)}, f32[4,128]{1,0:T(4,128)S(1)}, u32[]{:S(2)}, u32[]{:S(2)}) collective-permute-start(f32[4,128]{1,0:T(4,128)S(1)} %shard_map.63.refs_3_), channel_id=1, source_target_pairs={{0,24},{8,16},{16,8},{24,0},{1,25},{9,17},{17,9},{25,1},{2,26},{10... | collective-permute-start | bytes 6152 | tf_op jit(solution)/shard_map/ppermute | solution.py:317
  31.2 3.7 %collective-permute-start.11 = (f32[16,128]{1,0:T(8,128)S(1)}, f32[16,128]{1,0:T(8,128)S(1)}, u32[]{:S(2)}, u32[]{:S(2)}) collective-permute-start(f32[16,128]{1,0:T(8,128)S(1)} %get-tuple-element.27), channel_id=1, source_target_pairs={{0,1},{1,0},{2,3},{3,2},{4,5},{5,4},{6,7},{7,6},{8,9},{9,8},{10,11... | collective-permute-start | bytes 24584 | tf_op jit(solution)/shard_map/ppermute | solution.py:317
  32.7 10.8 %collective-permute-start.14 = (f32[192,512]{1,0:T(8,128)S(1)}, f32[192,512]{1,0:T(8,128)S(1)}, u32[]{:S(2)}, u32[]{:S(2)}) collective-permute-start(f32[192,512]{1,0:T(8,128)S(1)} %get-tuple-element.28.refs_2_), channel_id=1, source_target_pairs={{0,16},{8,24},{16,0},{24,8},{1,17},{9,25},{17,1},{25,9},{2,18},{10... | collective-permute-start | bytes 1179656 | tf_op jit(solution)/shard_map/ppermute | solution.py:317
  34.9 3.7 %collective-permute-start.12 = (f32[16,128]{1,0:T(8,128)S(1)}, f32[16,128]{1,0:T(8,128)S(1)}, u32[]{:S(2)}, u32[]{:S(2)}) collective-permute-start(f32[16,128]{1,0:T(8,128)S(1)} %multiply_add_fusion.1), channel_id=1, source_target_pairs={{0,2},{1,3},{2,0},{3,1},{4,6},{5,7},{6,4},{7,5},{8,10},{9,11},{10,... | collective-permute-start | bytes 24584 | tf_op jit(solution)/shard_map/ppermute | solution.py:317
  38.7 4.6 %collective-permute-start.13 = (f32[16,128]{1,0:T(8,128)S(1)}, f32[16,128]{1,0:T(8,128)S(1)}, u32[]{:S(2)}, u32[]{:S(2)}) collective-permute-start(f32[16,128]{1,0:T(8,128)S(1)} %multiply_add_fusion.refs_0_), channel_id=1, source_target_pairs={{0,4},{1,5},{2,6},{3,7},{4,0},{5,1},{6,2},{7,3},{8,12},{9,13},{10,... | collective-permute-start | bytes 24584 | tf_op jit(solution)/shard_map/ppermute | solution.py:317
  45.5 10.8 %copy-start.3 = (bf16[512,512]{1,0:T(8,128)(2,1)S(1)}, bf16[512,512]{1,0:T(8,128)(2,1)}, u32[]{:S(2)}) copy-start(bf16[512,512]{1,0:T(8,128)(2,1)} %refs_1_.1) | copy-start | bytes 1572868
  45.6 5.3 %collective-permute-start.15 = (f32[256,512]{1,0:T(8,128)S(1)}, f32[256,512]{1,0:T(8,128)S(1)}, u32[]{:S(2)}, u32[]{:S(2)}) collective-permute-start(f32[256,512]{1,0:T(8,128)S(1)} %get-tuple-element.30), channel_id=1, source_target_pairs={{0,8},{8,0},{16,24},{24,16},{1,9},{9,1},{17,25},{25,17},{2,10},{10... | collective-permute-start | bytes 1572872 | tf_op jit(solution)/shard_map/ppermute | solution.py:317
  45.6 3.1 %collective-permute-start.18 = (f32[4,128]{1,0:T(4,128)S(1)}, f32[4,128]{1,0:T(4,128)S(1)}, u32[]{:S(2)}, u32[]{:S(2)}) collective-permute-start(f32[4,128]{1,0:T(4,128)S(1)} %get-tuple-element.31.lse_ref), channel_id=1, source_target_pairs={{0,24},{8,16},{16,8},{24,0},{1,25},{9,17},{17,9},{25,1},{2,26},{10... | collective-permute-start | bytes 6152 | tf_op jit(solution)/shard_map/ppermute | solution.py:317
  47.3 3.6 %collective-permute-start.17 = (f32[4,128]{1,0:T(4,128)S(1)}, f32[4,128]{1,0:T(4,128)S(1)}, u32[]{:S(2)}, u32[]{:S(2)}) collective-permute-start(f32[4,128]{1,0:T(4,128)S(1)} %get-tuple-element.31.lse_ref), channel_id=1, source_target_pairs={{0,16},{8,24},{16,0},{24,8},{1,17},{9,25},{17,1},{25,9},{2,18},{10... | collective-permute-start | bytes 6152 | tf_op jit(solution)/shard_map/ppermute | solution.py:317
  47.8 3.1 %collective-permute-start.16 = (f32[4,128]{1,0:T(4,128)S(1)}, f32[4,128]{1,0:T(4,128)S(1)}, u32[]{:S(2)}, u32[]{:S(2)}) collective-permute-start(f32[4,128]{1,0:T(4,128)S(1)} %get-tuple-element.31.lse_ref), channel_id=1, source_target_pairs={{0,8},{8,0},{16,24},{24,16},{1,9},{9,1},{17,25},{25,17},{2,10},{10... | collective-permute-start | bytes 6152 | tf_op jit(solution)/shard_map/ppermute | solution.py:317
  51.3 5.1 %collective-permute-start.19 = (f32[3,2,128,512]{3,2,1,0:T(8,128)S(1)}, f32[3,2,128,512]{3,2,1,0:T(8,128)S(1)}, u32[]{:S(2)}, u32[]{:S(2)}) collective-permute-start(f32[3,2,128,512]{3,2,1,0:T(8,128)S(1)} %get-tuple-element.32.refs_2_), channel_id=1, source_target_pairs={{0,8},{8,0},{16,24},{24,16},{1,9},{9,1},{17,25},{25,17},{2,10},{10... | collective-permute-start | bytes 4718600 | tf_op jit(solution)/shard_map/ppermute | solution.py:317
  51.4 14.3 %collective-permute-start.24 = (f32[256,512]{1,0:T(8,128)S(1)}, f32[256,512]{1,0:T(8,128)S(1)}, u32[]{:S(2)}, u32[]{:S(2)}) collective-permute-start(f32[256,512]{1,0:T(8,128)S(1)} %get-tuple-element.35.one_ref), channel_id=1, source_target_pairs={{0,16},{8,24},{16,0},{24,8},{1,17},{9,25},{17,1},{25,9},{2,18},{10... | collective-permute-start | bytes 1572872 | tf_op jit(solution)/shard_map/ppermute | solution.py:317
  51.9 5.7 %collective-permute-start.20 = (f32[4,128]{1,0:T(4,128)S(1)}, f32[4,128]{1,0:T(4,128)S(1)}, u32[]{:S(2)}, u32[]{:S(2)}) collective-permute-start(f32[4,128]{1,0:T(4,128)S(1)} %get-tuple-element.40.refs_5_), channel_id=1, source_target_pairs={{0,5},{1,4},{2,7},{3,6},{4,1},{5,0},{6,3},{7,2},{8,13},{9,12},{10,... | collective-permute-start | bytes 6152 | tf_op jit(solution)/shard_map/ppermute | solution.py:317
  54.6 4.5 %collective-permute-start.21 = (f32[4,128]{1,0:T(4,128)S(1)}, f32[4,128]{1,0:T(4,128)S(1)}, u32[]{:S(2)}, u32[]{:S(2)}) collective-permute-start(f32[4,128]{1,0:T(4,128)S(1)} %get-tuple-element.40.refs_5_), channel_id=1, source_target_pairs={{0,4},{1,5},{2,6},{3,7},{4,0},{5,1},{6,2},{7,3},{8,12},{9,13},{10,... | collective-permute-start | bytes 6152 | tf_op jit(solution)/shard_map/ppermute | solution.py:317
  55.5 3.6 %collective-permute-start.22 = (f32[4,128]{1,0:T(4,128)S(1)}, f32[4,128]{1,0:T(4,128)S(1)}, u32[]{:S(2)}, u32[]{:S(2)}) collective-permute-start(f32[4,128]{1,0:T(4,128)S(1)} %get-tuple-element.40.refs_5_), channel_id=1, source_target_pairs={{0,1},{1,0},{2,3},{3,2},{4,5},{5,4},{6,7},{7,6},{8,9},{9,8},{10,11... | collective-permute-start | bytes 6152 | tf_op jit(solution)/shard_map/ppermute | solution.py:317
  60.0 13.3 %collective-permute-start.23 = (f32[264,512]{1,0:T(8,128)S(1)}, f32[264,512]{1,0:T(8,128)S(1)}, u32[]{:S(2)}, u32[]{:S(2)}) collective-permute-start(f32[264,512]{1,0:T(8,128)S(1)} %shard_map.69), channel_id=1, source_target_pairs={{0,2},{1,3},{2,0},{3,1},{4,6},{5,7},{6,4},{7,5},{8,10},{9,11},{10,... | collective-permute-start | bytes 1622024 | tf_op jit(solution)/shard_map/ppermute | solution.py:317
  65.8 1.4 %collective-permute-start.25 = (f32[64,512]{1,0:T(8,128)S(1)}, f32[64,512]{1,0:T(8,128)S(1)}, u32[]{:S(2)}, u32[]{:S(2)}) collective-permute-start(f32[64,512]{1,0:T(8,128)S(1)} %get-tuple-element.36.refs_0_), channel_id=1, source_target_pairs={{0,8},{8,0},{16,24},{24,16},{1,9},{9,1},{17,25},{25,17},{2,10},{10... | collective-permute-start | bytes 393224 | tf_op jit(solution)/shard_map/ppermute | solution.py:317
  65.8 1.5 %collective-permute-start.26 = (f32[64,512]{1,0:T(8,128)S(1)}, f32[64,512]{1,0:T(8,128)S(1)}, u32[]{:S(2)}, u32[]{:S(2)}) collective-permute-start(f32[64,512]{1,0:T(8,128)S(1)} %get-tuple-element.37.refs_1_), channel_id=1, source_target_pairs={{0,8},{8,0},{16,24},{24,16},{1,9},{9,1},{17,25},{25,17},{2,10},{10... | collective-permute-start | bytes 393224 | tf_op jit(solution)/shard_map/ppermute | solution.py:317
  66.3 1.3 %collective-permute-start.27 = (f32[64,512]{1,0:T(8,128)S(1)}, f32[64,512]{1,0:T(8,128)S(1)}, u32[]{:S(2)}, u32[]{:S(2)}) collective-permute-start(f32[64,512]{1,0:T(8,128)S(1)} %get-tuple-element.38.refs_2_), channel_id=1, source_target_pairs={{0,8},{8,0},{16,24},{24,16},{1,9},{9,1},{17,25},{25,17},{2,10},{10... | collective-permute-start | bytes 393224 | tf_op jit(solution)/shard_map/ppermute | solution.py:317
  66.4 1.5 %collective-permute-start.28 = (f32[64,512]{1,0:T(8,128)S(1)}, f32[64,512]{1,0:T(8,128)S(1)}, u32[]{:S(2)}, u32[]{:S(2)}) collective-permute-start(f32[64,512]{1,0:T(8,128)S(1)} %get-tuple-element.39.refs_3_), channel_id=1, source_target_pairs={{0,8},{8,0},{16,24},{24,16},{1,9},{9,1},{17,25},{25,17},{2,10},{10... | collective-permute-start | bytes 393224 | tf_op jit(solution)/shard_map/ppermute | solution.py:317

commit v12 on v9

--- a/solution.py
+++ b/solution.py
@@ -180,13 +180,22 @@
     return peak, jnp.sum(sum(exps), axis=1, keepdims=True), exps
 
 
-def share_kernel(mine_ref, came_ref, total_ref, lse_ref, came_lse_ref, *refs):
-    pieces, (out_ref, pack_ref) = refs[:-2], refs[-2:]
+def share_kernel(mine_ref, came_ref, total_ref, lse_ref, came_lse_ref, out_ref):
     half = mine_ref.shape[0] // LANES
     at = pl.ds(lax.axis_index("row") % 2 * half, half)
-    total = total_ref[at, :]
-    share, came_share = to_column(jnp.exp2(lse_ref[at, :] - total)), to_column(jnp.exp2(came_lse_ref[at, :] - total))
+    total = total_ref[0, at, :]
+    share = to_column(jnp.exp2(lse_ref[0, at, :] - total))
+    came_share = to_column(jnp.exp2(came_lse_ref[0, at, :] - total))
     out_ref[...] = mine_ref[...] * share + came_ref[...] * came_share
+
+
+def stack_kernel(*refs):
+    for k, ref in enumerate(refs[-3::-1]):
+        refs[-1][k] = ref[...]
+
+
+def pack_kernel(*refs):
+    pieces, pack_ref = refs[:-2], refs[-1]
     n_shards, n_y, rows, _ = pack_ref.shape
     y = lax.axis_index("row") // 2
     early, late = pieces[:n_y], pieces[n_y:]
@@ -253,15 +262,15 @@
 EXTRA = 8
 
 
-def images(flip, inner_ref, y_ref, bias_refs, scores_ref):
+def images(flip, inner_ref, y_ref, totals_ref, scores_ref):
     rows = scores_ref.shape[0]
-    n_shards = len(bias_refs)
+    n_shards = totals_ref.shape[0]
     n_tgt = y_ref.shape[0] // n_shards
     block = pl.ds(flip * rows, rows)
     peak = jnp.full((rows, 1), -jnp.inf, jnp.float32)
-    for k, bias_ref in enumerate(bias_refs[::-1]):
+    for k in range(n_shards):
         at = pl.ds(k * n_tgt, n_tgt)
-        scores = inner_ref[block, at] + to_row(bias_ref[...])
+        scores = inner_ref[block, at] - to_row(totals_ref[k])
         scores_ref[:, at] = scores
         peak = jnp.maximum(peak, jnp.max(scores, axis=1, keepdims=True))
     total = jnp.zeros((rows, 1), jnp.float32)
@@ -284,9 +293,9 @@
 EXTRA = 8
 
 
-def image_kernel(flip, inner_ref, y_ref, *refs):
-    bias_refs, (image_ref, scores_ref) = refs[:-2], refs[-2:]
-    numer, total, peak = images(flip, inner_ref, y_ref, bias_refs, scores_ref)
+def image_kernel(flip, inner_ref, y_ref, totals_ref, *refs):
+    image_ref, scores_ref = refs[-2:]
+    numer, total, peak = images(flip, inner_ref, y_ref, totals_ref, scores_ref)
     rows = numer.shape[0]
     lse = lanes_of(peak + jnp.log2(total))
     image_ref[:rows, :] = numer * (1.0 / total)
@@ -369,22 +378,10 @@
                 (tgt_dense, f32(half, width), f32(half, width)),
                 tile, source, ls, sqx, *parts, late[-1],
             )
-        parts = [lse] + [swap(lse, "row", k) for k in range(1, n_row)]
-    total = merge_all(parts)
-
-    bias = lt * LOG2E + (sqy - total) - sqy
-    biases = [bias] + [swap(bias, "col", distance) for distance in apart[1:]]
-
-    mine, came = call(
-        share_kernel,
-        (f32(half, width), f32(len(apart) - 1, n_row // 2, *part.shape)),
-        mine, swap(sent, "row", 1), total, lse, parts[1], *early, *late,
-    )
-    rest = bits_of(n_row)[1:]
-    for distance in rest[:-1]:
-        mine, = call(add_kernel, (f32(half, width),), mine, swap(mine, "row", distance))
-    mine_came = swap(mine, "row", rest[-1])
-
+        if step < ITERS - 1:
+            parts = [lse] + [swap(lse, "row", k) for k in range(1, n_row)]
+
+    came = call(pack_kernel, f32(len(apart) - 1, n_row // 2, *part.shape), *early, *late, lse)
     n_all = len(apart) * n_tgt
     all_y, inner = call(
         lambda *refs: scores_kernel(n_x, *refs),
@@ -393,22 +390,35 @@
         limit=32,
     )
 
-    def image(flip):
+    part_total = (lse - sqy) - (lt * LOG2E - sqy)
+    others = [swap(part_total, "col", distance) for distance in apart[:0:-1]]
+    totals = call(stack_kernel, f32(len(apart), *lt.shape), *others, part_total, inner)
+    parts = [totals] + [swap(totals, "row", k) for k in range(1, n_row)]
+    totals = merge_all(parts)
+
+    mine = call(share_kernel, f32(half, width), mine, swap(sent, "row", 1), totals, parts[0], parts[1])
+    rest = bits_of(n_row)[1:]
+    for distance in rest[:-1]:
+        mine, = call(add_kernel, (f32(half, width),), mine, swap(mine, "row", distance))
+    mine_came = swap(mine, "row", rest[-1])
+
+    def image(flip, *after):
         return call(
             lambda *refs: image_kernel(flip, *refs),
             f32(count + EXTRA, width),
-            inner, all_y, *biases[::-1],
+            inner, all_y, totals, *after,
             scratch=[pltpu.VMEM((count, n_all), jnp.float32)],
         )
 
     came = swap(image(1), "col", n_x)
-    own = image(0)
     n_last = 4
     mine = call(add_kernel, (f32(half // n_last, width),) * n_last, mine, mine_came)
+    other = [swap(piece, "row", 1) for piece in mine]
     target_image = call(
-        place_kernel, f32(n_tgt, width), *mine, *[swap(piece, "row", 1) for piece in mine],
+        place_kernel, f32(n_tgt, width), *mine, *other,
         out_specs=HBM, scratch=[DMA((2 * n_last,))],
     )
+    own = image(0, *other)
     source_image = call(join_kernel, f32(count, width), own, came)
     return source_image, target_image
 

time: 74.3 us -> 77.6 us (1.044)
  waiting for transfers between devices: 25.5 us -> 28.5 us
    ppermute x29, waiting for transfers between devices: 25.5 us -> 28.5 us  [swap(): return lax.ppermute(value, axis, [(i, i ^ distance) for i in range(n)])]
    pallas_call x14 -> x16, Pallas kernels: 12.1 us -> 12.2 us  [call(): pl.pallas_call(kernel, out_shape=out_shape, in_specs=in_specs or [VMEM] *...]
  transfers between devices with their start and end apart: 29 -> 29, of which waited for: 16 -> 15; matrix products, arithmetic and copies ran while one was open for 0% -> 0% of each run, Pallas kernels for 10% -> 10%
where the time goes in v12:
time: 77.6 us; the launch traced here: 77.4 us
  starting transfers between devices  32.5 us (42%)
  waiting for transfers between devices  28.5 us (37%)
  Pallas kernels  12.2 us (16%)
  local copies, waits for them, and re-layouts  3.32 us (4%)
  between operations  0.81 us (1%)
    ppermute x29, starting transfers between devices, swap(): return lax.ppermute(value, axis, [(i, i ^ distance) for i in range(n)])  32.5 us
    ppermute x29, waiting for transfers between devices, swap(): return lax.ppermute(value, axis, [(i, i ^ distance) for i in range(n)])  28.5 us
    pallas_call x16, Pallas kernels, call(): pl.pallas_call(kernel, out_shape=out_shape, in_specs=in_specs or [VMEM] *...  12.2 us
    unnamed x12, local copies, waits for them, and re-layouts  3.32 us
  transfers between devices with their start and end apart: 29, of which 15 were waited for; matrix products, arithmetic and copies ran while one was open for 0% of the time, Pallas kernels for 10%

profile of v12, /device:TPU:0, one launch (start us, length us, event | category | flops | bytes accessed | tf_op | source)
XLA Modules:
  0.0 77.4 jit_solution(4967131098094369389)
XLA Ops:
  0.6 0.0 copy-start.2
  0.6 1.0 %copy-done.2 = bf16[512,512]{1,0:T(8,128)(2,1)S(1)} copy-done((bf16[512,512]{1,0:T(8,128)(2,1)S(1)}, bf16[512,512]{1,0:T(8,128)(2,1)}, u32[]{:S(2)}) %copy-start.2) | copy-done | bytes 524312
  1.7 4.1 %collective-permute-start.3 = (f32[128,512]{1,0:T(8,128)S(1)}, f32[128,512]{1,0:T(8,128)S(1)}, u32[]{:S(2)}, u32[]{:S(2)}) collective-permute-start(f32[128,512]{1,0:T(8,128)S(1)} %shard_map.60), channel_id=1, source_target_pairs={{0,4},{1,5},{2,6},{3,7},{4,0},{5,1},{6,2},{7,3},{8,12},{9,13},{10,... | collective-permute-start | bytes 786440 | tf_op jit(solution)/shard_map/ppermute | solution.py:308
  5.8 1.5 %collective-permute-start.4 = (f32[128,512]{1,0:T(8,128)S(1)}, f32[128,512]{1,0:T(8,128)S(1)}, u32[]{:S(2)}, u32[]{:S(2)}) collective-permute-start(f32[128,512]{1,0:T(8,128)S(1)} %shard_map.60), channel_id=1, source_target_pairs={{0,1},{1,0},{2,3},{3,2},{4,5},{5,4},{6,7},{7,6},{8,9},{9,8},{10,11... | collective-permute-start | bytes 786440 | tf_op jit(solution)/shard_map/ppermute | solution.py:308
  7.3 1.6 %copy-done = bf16[2048,512]{1,0:T(8,128)(2,1)S(1)} copy-done((bf16[2048,512]{1,0:T(8,128)(2,1)S(1)}, bf16[2048,512]{1,0:T(8,128)(2,1)}, u32[]{:S(2)}) %copy-start) | copy-done | bytes 2097176
  8.9 0.7 copy-done.5
  9.6 1.9 %shard_map.59 = (f32[512,2048]{1,0:T(8,128)S(1)}, f32[16,128]{1,0:T(8,128)S(1)}, f32[4,128]{1,0:T(4,128)S(1)}) custom-call(bf16[512,512]{1,0:T(8,128)(2,1)S(1)} %copy-done.2, bf16[2048,512]{1,0:T(8,128)(2,1)S(1)} %copy-done, f32[4,128]{1,0:T(4,128)S(1)} %bitcast.5), custom_call_target="tpu_custom_call" | custom-call | tf_op jit(solution)/shard_map/pallas_call | solution.py:22
  11.5 0.1 collective-permute-start
  11.6 2.8 %collective-permute-start.1 = (f32[16,128]{1,0:T(8,128)S(1)}, f32[16,128]{1,0:T(8,128)S(1)}, u32[]{:S(2)}, u32[]{:S(2)}) collective-permute-start(f32[16,128]{1,0:T(8,128)S(1)} %get-tuple-element.19.refs_0_), channel_id=1, source_target_pairs={{0,4},{1,5},{2,6},{3,7},{4,0},{5,1},{6,2},{7,3},{8,12},{9,13},{10,... | collective-permute-start | bytes 24584 | tf_op jit(solution)/shard_map/ppermute | solution.py:308
  14.4 1.5 %collective-permute-start.2 = (f32[16,128]{1,0:T(8,128)S(1)}, f32[16,128]{1,0:T(8,128)S(1)}, u32[]{:S(2)}, u32[]{:S(2)}) collective-permute-start(f32[16,128]{1,0:T(8,128)S(1)} %get-tuple-element.19.refs_0_), channel_id=1, source_target_pairs={{0,1},{1,0},{2,3},{3,2},{4,5},{5,4},{6,7},{7,6},{8,9},{9,8},{10,11... | collective-permute-start | bytes 24584 | tf_op jit(solution)/shard_map/ppermute | solution.py:308
  15.9 3.4 %collective-permute-done.refs_1_ = f32[16,128]{1,0:T(8,128)S(1)} collective-permute-done((f32[16,128]{1,0:T(8,128)S(1)}, f32[16,128]{1,0:T(8,128)S(1)}, u32[]{:S(2)}, u32[]{:S(2)}) %collective-permute-start) | collective-permute-done | bytes 8224 | tf_op jit(solution)/shard_map/ppermute | solution.py:308
  19.3 0.0 collective-permute-done.2.refs_3_
  19.3 0.0 collective-permute-done.3.refs_4_
  19.3 0.0 collective-permute-done.4.refs_5_
  19.4 1.6 %collective-permute-start.5 = (f32[192,512]{1,0:T(8,128)S(1)}, f32[192,512]{1,0:T(8,128)S(1)}, u32[]{:S(2)}, u32[]{:S(2)}) collective-permute-start(f32[192,512]{1,0:T(8,128)S(1)} %get-tuple-element.20.refs_0_), channel_id=1, source_target_pairs={{0,16},{8,24},{16,0},{24,8},{1,17},{9,25},{17,1},{25,9},{2,18},{10... | collective-permute-start | bytes 1179656 | tf_op jit(solution)/shard_map/ppermute | solution.py:308
  21.0 0.6 collective-permute-start.10
  21.6 1.2 %collective-permute-start.6 = (f32[16,128]{1,0:T(8,128)S(1)}, f32[16,128]{1,0:T(8,128)S(1)}, u32[]{:S(2)}, u32[]{:S(2)}) collective-permute-start(f32[16,128]{1,0:T(8,128)S(1)} %get-tuple-element.23.refs_3_), channel_id=1, source_target_pairs={{0,2},{1,3},{2,0},{3,1},{4,6},{5,7},{6,4},{7,5},{8,10},{9,11},{10,... | collective-permute-start | bytes 24584 | tf_op jit(solution)/shard_map/ppermute | solution.py:308
  22.8 0.5 shard_map.62.refs_2_.sqx_ref
  23.3 2.0 %collective-permute-done.6.refs_4_ = f32[16,128]{1,0:T(8,128)S(1)} collective-permute-done((f32[16,128]{1,0:T(8,128)S(1)}, f32[16,128]{1,0:T(8,128)S(1)}, u32[]{:S(2)}, u32[]{:S(2)}) %collective-permute-start.6) | collective-permute-done | bytes 8224 | tf_op jit(solution)/shard_map/ppermute | solution.py:308
  25.3 1.0 %shard_map.63.refs_3_ = f32[4,128]{1,0:T(4,128)S(1)} custom-call(f32[512,2048]{1,0:T(8,128)S(1)} %get-tuple-element.21.refs_0_.tile_ref, f32[16,128]{1,0:T(8,128)S(1)} %bitcast.3, f32[16,128]{1,0:T(8,128)S(1)} %shard_map.62.refs_2_.sqx_ref, f32[16,128]{1,0:T(8,128)S(1)} %get-tuple-element.23.refs_3_, f32[16,128]{1,0:T(8,128)S(1)} %collective-permute-done.6.refs_4_), custom_call_target="tpu_custom_call" | custom-call | tf_op jit(solution)/shard_map/pallas_call | solution.py:22
  26.3 0.0 collective-permute-start.7
  26.3 0.6 collective-permute-start.8
  26.9 1.3 %collective-permute-start.9 = (f32[4,128]{1,0:T(4,128)S(1)}, f32[4,128]{1,0:T(4,128)S(1)}, u32[]{:S(2)}, u32[]{:S(2)}) collective-permute-start(f32[4,128]{1,0:T(4,128)S(1)} %shard_map.63.refs_3_), channel_id=1, source_target_pairs={{0,24},{8,16},{16,8},{24,0},{1,25},{9,17},{17,9},{25,1},{2,26},{10... | collective-permute-start | bytes 6152 | tf_op jit(solution)/shard_map/ppermute | solution.py:308
  28.2 1.8 %collective-permute-done.8.refs_5_ = f32[4,128]{1,0:T(4,128)S(1)} collective-permute-done((f32[4,128]{1,0:T(4,128)S(1)}, f32[4,128]{1,0:T(4,128)S(1)}, u32[]{:S(2)}, u32[]{:S(2)}) %collective-permute-start.8) | collective-permute-done | bytes 2080 | tf_op jit(solution)/shard_map/ppermute | solution.py:308
  30.0 1.1 %shard_map.64 = (f32[16,128]{1,0:T(8,128)S(1)}, f32[192,512]{1,0:T(8,128)S(1)}) custom-call(f32[512,2048]{1,0:T(8,128)S(1)} %get-tuple-element.21.refs_0_.tile_ref, f32[4,128]{1,0:T(4,128)S(1)} %bitcast.6, f32[4,128]{1,0:T(4,128)S(1)} %get-tuple-element.22.refs_2_, f32[4,128]{1,0:T(4,128)S(1)} %shard_map.63.refs_3_, ...), custom_call_target="tpu_custom_call" | custom-call | tf_op jit(solution)/shard_map/pallas_call | solution.py:22
  31.1 1.4 %collective-permute-start.12 = (f32[16,128]{1,0:T(8,128)S(1)}, f32[16,128]{1,0:T(8,128)S(1)}, u32[]{:S(2)}, u32[]{:S(2)}) collective-permute-start(f32[16,128]{1,0:T(8,128)S(1)} %get-tuple-element.26), channel_id=1, source_target_pairs={{0,1},{1,0},{2,3},{3,2},{4,5},{5,4},{6,7},{7,6},{8,9},{9,8},{10,11... | collective-permute-start | bytes 24584 | tf_op jit(solution)/shard_map/ppermute | solution.py:308
  32.6 1.4 %collective-permute-start.11 = (f32[192,512]{1,0:T(8,128)S(1)}, f32[192,512]{1,0:T(8,128)S(1)}, u32[]{:S(2)}, u32[]{:S(2)}) collective-permute-start(f32[192,512]{1,0:T(8,128)S(1)} %get-tuple-element.25.refs_2_), channel_id=1, source_target_pairs={{0,16},{8,24},{16,0},{24,8},{1,17},{9,25},{17,1},{25,9},{2,18},{10... | collective-permute-start | bytes 1179656 | tf_op jit(solution)/shard_map/ppermute | solution.py:308
  34.0 0.8 %collective-permute-done.12 = f32[16,128]{1,0:T(8,128)S(1)} collective-permute-done((f32[16,128]{1,0:T(8,128)S(1)}, f32[16,128]{1,0:T(8,128)S(1)}, u32[]{:S(2)}, u32[]{:S(2)}) %collective-permute-start.12) | collective-permute-done | bytes 8224 | tf_op jit(solution)/shard_map/ppermute | solution.py:308
  34.8 1.2 %collective-permute-start.13 = (f32[16,128]{1,0:T(8,128)S(1)}, f32[16,128]{1,0:T(8,128)S(1)}, u32[]{:S(2)}, u32[]{:S(2)}) collective-permute-start(f32[16,128]{1,0:T(8,128)S(1)} %multiply_add_fusion.2), channel_id=1, source_target_pairs={{0,2},{1,3},{2,0},{3,1},{4,6},{5,7},{6,4},{7,5},{8,10},{9,11},{10,... | collective-permute-start | bytes 24584 | tf_op jit(solution)/shard_map/ppermute | solution.py:308
  36.1 2.5 %collective-permute-done.13 = f32[16,128]{1,0:T(8,128)S(1)} collective-permute-done((f32[16,128]{1,0:T(8,128)S(1)}, f32[16,128]{1,0:T(8,128)S(1)}, u32[]{:S(2)}, u32[]{:S(2)}) %collective-permute-start.13) | collective-permute-done | bytes 8224 | tf_op jit(solution)/shard_map/ppermute | solution.py:308
  38.6 2.3 %collective-permute-start.14 = (f32[16,128]{1,0:T(8,128)S(1)}, f32[16,128]{1,0:T(8,128)S(1)}, u32[]{:S(2)}, u32[]{:S(2)}) collective-permute-start(f32[16,128]{1,0:T(8,128)S(1)} %multiply_add_fusion.1.refs_0_), channel_id=1, source_target_pairs={{0,4},{1,5},{2,6},{3,7},{4,0},{5,1},{6,2},{7,3},{8,12},{9,13},{10,... | collective-permute-start | bytes 24584 | tf_op jit(solution)/shard_map/ppermute | solution.py:308
  40.9 2.3 %collective-permute-done.14.refs_1_ = f32[16,128]{1,0:T(8,128)S(1)} collective-permute-done((f32[16,128]{1,0:T(8,128)S(1)}, f32[16,128]{1,0:T(8,128)S(1)}, u32[]{:S(2)}, u32[]{:S(2)}) %collective-permute-start.14) | collective-permute-done | bytes 8224 | tf_op jit(solution)/shard_map/ppermute | solution.py:308
  43.2 0.2 collective-permute-done.11.refs_2_.refs_3_
  43.4 1.9 %shard_map.65 = (f32[4,128]{1,0:T(4,128)S(1)}, f32[256,512]{1,0:T(8,128)S(1)}, f32[256,512]{1,0:T(8,128)S(1)}) custom-call(f32[512,2048]{1,0:T(8,128)S(1)} %get-tuple-element.21.refs_0_.tile_ref, bf16[2048,512]{1,0:T(8,128)(2,1)S(1)} %copy-done.1, f32[16,128]{1,0:T(8,128)S(1)} %bitcast.4, f32[16,128]{1,0:T(8,128)S(1)} %shard_map.62.refs_2_.sqx_ref, ...), custom_call_target="tpu_custom_call" | custom-call | tf_op jit(solution)/shard_map/pallas_call | solution.py:22
  45.3 0.0 copy-start.3
  45.3 0.1 shard_map.66.refs_2_
  45.5 0.1 collective-permute-start.15
  45.5 0.5 collective-permute-start.22
  46.0 2.6 %collective-permute-start.16 = (f32[4,128]{1,0:T(4,128)S(1)}, f32[4,128]{1,0:T(4,128)S(1)}, u32[]{:S(2)}, u32[]{:S(2)}) collective-permute-start(f32[4,128]{1,0:T(4,128)S(1)} %subtract_subtract_fusion.refs_3_), channel_id=1, source_target_pairs={{0,5},{1,4},{2,7},{3,6},{4,1},{5,0},{6,3},{7,2},{8,13},{9,12},{10,... | collective-permute-start | bytes 6152 | tf_op jit(solution)/shard_map/ppermute | solution.py:308
  48.7 0.9 %collective-permute-start.17 = (f32[4,128]{1,0:T(4,128)S(1)}, f32[4,128]{1,0:T(4,128)S(1)}, u32[]{:S(2)}, u32[]{:S(2)}) collective-permute-start(f32[4,128]{1,0:T(4,128)S(1)} %subtract_subtract_fusion.refs_3_), channel_id=1, source_target_pairs={{0,4},{1,5},{2,6},{3,7},{4,0},{5,1},{6,2},{7,3},{8,12},{9,13},{10,... | collective-permute-start | bytes 6152 | tf_op jit(solution)/shard_map/ppermute | solution.py:308
  49.6 0.9 %collective-permute-start.18 = (f32[4,128]{1,0:T(4,128)S(1)}, f32[4,128]{1,0:T(4,128)S(1)}, u32[]{:S(2)}, u32[]{:S(2)}) collective-permute-start(f32[4,128]{1,0:T(4,128)S(1)} %subtract_subtract_fusion.refs_3_), channel_id=1, source_target_pairs={{0,1},{1,0},{2,3},{3,2},{4,5},{5,4},{6,7},{7,6},{8,9},{9,8},{10,11... | collective-permute-start | bytes 6152 | tf_op jit(solution)/shard_map/ppermute | solution.py:308
  50.4 1.3 %shard_map.67 = (bf16[2048,512]{1,0:T(8,128)(2,1)S(1)}, f32[512,2048]{1,0:T(8,128)S(1)}) custom-call(bf16[2048,512]{1,0:T(8,128)(2,1)S(1)} %copy-done.1, bf16[512,512]{1,0:T(8,128)(2,1)S(1)} %copy-done.3, f32[3,2,128,512]{3,2,1,0:T(8,128)S(1)} %shard_map.66.refs_2_, f32[3,2,128,512]{3,2,1,0:T(8,128)S(1)} %collective-permute-done.15.refs_3_), custom_call_target="tpu_custom_call" | custom-call | tf_op jit(solution)/shard_map/pallas_call | solution.py:22
  51.8 1.4 %collective-permute-done.17.refs_1_ = f32[4,128]{1,0:T(4,128)S(1)} collective-permute-done((f32[4,128]{1,0:T(4,128)S(1)}, f32[4,128]{1,0:T(4,128)S(1)}, u32[]{:S(2)}, u32[]{:S(2)}) %collective-permute-start.17) | collective-permute-done | bytes 2080 | tf_op jit(solution)/shard_map/ppermute | solution.py:308
  53.2 1.5 %collective-permute-start.20 = (f32[4,4,128]{2,1,0:T(4,128)S(1)}, f32[4,4,128]{2,1,0:T(4,128)S(1)}, u32[]{:S(2)}, u32[]{:S(2)}) collective-permute-start(f32[4,4,128]{2,1,0:T(4,128)S(1)} %shard_map.68.lse_ref), channel_id=1, source_target_pairs={{0,16},{8,24},{16,0},{24,8},{1,17},{9,25},{17,1},{25,9},{2,18},{10... | collective-permute-start | bytes 24584 | tf_op jit(solution)/shard_map/ppermute | solution.py:308
  54.7 0.3 collective-permute-start.21
  55.0 1.9 %collective-permute-done.20 = f32[4,4,128]{2,1,0:T(4,128)S(1)} collective-permute-done((f32[4,4,128]{2,1,0:T(4,128)S(1)}, f32[4,4,128]{2,1,0:T(4,128)S(1)}, u32[]{:S(2)}, u32[]{:S(2)}) %collective-permute-start.20) | collective-permute-done | bytes 8224 | tf_op jit(solution)/shard_map/ppermute | solution.py:308
  56.9 0.9 %collective-permute-done.21 = f32[4,4,128]{2,1,0:T(4,128)S(1)} collective-permute-done((f32[4,4,128]{2,1,0:T(4,128)S(1)}, f32[4,4,128]{2,1,0:T(4,128)S(1)}, u32[]{:S(2)}, u32[]{:S(2)}) %collective-permute-start.21) | collective-permute-done | bytes 8224 | tf_op jit(solution)/shard_map/ppermute | solution.py:308
  57.8 0.3 shard_map.69.one_ref
  58.1 0.7 collective-permute-start.23
  58.8 0.9 %shard_map.72 = f32[264,512]{1,0:T(8,128)S(1)} custom-call(f32[512,2048]{1,0:T(8,128)S(1)} %get-tuple-element.28.refs_4_.refs_0_, bf16[2048,512]{1,0:T(8,128)(2,1)S(1)} %get-tuple-element.29.refs_1_, f32[4,4,128]{2,1,0:T(4,128)S(1)} %multiply_add_fusion.total_ref.refs_2_), custom_call_target="tpu_custom_call" | custom-call | tf_op jit(solution)/shard_map/pallas_call | solution.py:22
  59.7 2.1 %collective-permute-start.28 = (f32[264,512]{1,0:T(8,128)S(1)}, f32[264,512]{1,0:T(8,128)S(1)}, u32[]{:S(2)}, u32[]{:S(2)}) collective-permute-start(f32[264,512]{1,0:T(8,128)S(1)} %shard_map.72), channel_id=1, source_target_pairs={{0,2},{1,3},{2,0},{3,1},{4,6},{5,7},{6,4},{7,5},{8,10},{9,11},{10,... | collective-permute-start | bytes 1622024 | tf_op jit(solution)/shard_map/ppermute | solution.py:308
  61.8 10.4 %collective-permute-done.23.two_ref = f32[256,512]{1,0:T(8,128)S(1)} collective-permute-done((f32[256,512]{1,0:T(8,128)S(1)}, f32[256,512]{1,0:T(8,128)S(1)}, u32[]{:S(2)}, u32[]{:S(2)}) %collective-permute-start.23) | collective-permute-done | bytes 524320 | tf_op jit(solution)/shard_map/ppermute | solution.py:308
  72.2 0.1 shard_map.70
  72.2 0.1 collective-permute-start.24
  72.3 0.5 collective-permute-start.25
  72.8 0.1 collective-permute-start.26
  72.9 0.4 collective-permute-start.27
  73.3 0.3 collective-permute-done.24.refs_3_.refs_4_
  73.6 0.2 collective-permute-done.25.refs_4_.refs_5_
  73.8 0.3 collective-permute-done.26.refs_5_.refs_6_
  74.2 0.2 collective-permute-done.27.refs_6_.refs_7_
  74.3 1.0 %shard_map.74 = f32[512,512]{1,0:T(8,128)} custom-call(f32[64,512]{1,0:T(8,128)S(1)} %get-tuple-element.32.refs_0_, f32[64,512]{1,0:T(8,128)S(1)} %get-tuple-element.33.refs_1_, f32[64,512]{1,0:T(8,128)S(1)} %get-tuple-element.34.refs_2_, f32[64,512]{1,0:T(8,128)S(1)} %get-tuple-element.35.refs_3_, f32[64,512]{1,0:T(8,128)S(1)} %collective-permute-done.24.refs_3_.refs_4_, ...), custom_call_target="tpu_custom_call" | custom-call | tf_op jit(solution)/shard_map/pallas_call | solution.py:22
  75.4 0.9 %shard_map.71.refs_0_ = f32[264,512]{1,0:T(8,128)S(1)} custom-call(f32[512,2048]{1,0:T(8,128)S(1)} %get-tuple-element.28.refs_4_.refs_0_, bf16[2048,512]{1,0:T(8,128)(2,1)S(1)} %get-tuple-element.29.refs_1_, f32[4,4,128]{2,1,0:T(4,128)S(1)} %multiply_add_fusion.total_ref.refs_2_, f32[64,512]{1,0:T(8,128)S(1)} %collective-permute-done.24.refs_3_.refs_4_, ...), custom_call_target="tpu_custom_call" | custom-call | tf_op jit(solution)/shard_map/pallas_call | solution.py:22
  76.3 1.1 %shard_map.73 = f32[256,512]{1,0:T(8,128)} custom-call(f32[264,512]{1,0:T(8,128)S(1)} %shard_map.71.refs_0_, f32[264,512]{1,0:T(8,128)S(1)} %collective-permute-done.28.refs_1_), custom_call_target="tpu_custom_call" | custom-call | tf_op jit(solution)/shard_map/pallas_call | solution.py:22
  (26 shorter events, 0.2 us)
Async XLA Ops:
  0.6 1.0 %copy-start.2 = (bf16[512,512]{1,0:T(8,128)(2,1)S(1)}, bf16[512,512]{1,0:T(8,128)(2,1)}, u32[]{:S(2)}) copy-start(bf16[512,512]{1,0:T(8,128)(2,1)} %refs_1_.1) | copy-start | bytes 1572868
  1.7 17.6 %collective-permute-start.3 = (f32[128,512]{1,0:T(8,128)S(1)}, f32[128,512]{1,0:T(8,128)S(1)}, u32[]{:S(2)}, u32[]{:S(2)}) collective-permute-start(f32[128,512]{1,0:T(8,128)S(1)} %shard_map.60), channel_id=1, source_target_pairs={{0,4},{1,5},{2,6},{3,7},{4,0},{5,1},{6,2},{7,3},{8,12},{9,13},{10,... | collective-permute-start | bytes 786440 | tf_op jit(solution)/shard_map/ppermute | solution.py:308
  5.8 13.5 %collective-permute-start.4 = (f32[128,512]{1,0:T(8,128)S(1)}, f32[128,512]{1,0:T(8,128)S(1)}, u32[]{:S(2)}, u32[]{:S(2)}) collective-permute-start(f32[128,512]{1,0:T(8,128)S(1)} %shard_map.60), channel_id=1, source_target_pairs={{0,1},{1,0},{2,3},{3,2},{4,5},{5,4},{6,7},{7,6},{8,9},{9,8},{10,11... | collective-permute-start | bytes 786440 | tf_op jit(solution)/shard_map/ppermute | solution.py:308
  7.3 1.6 %copy-start = (bf16[2048,512]{1,0:T(8,128)(2,1)S(1)}, bf16[2048,512]{1,0:T(8,128)(2,1)}, u32[]{:S(2)}) copy-start(bf16[2048,512]{1,0:T(8,128)(2,1)} %refs_0_.1) | copy-start | bytes 6291460
  8.9 0.7 copy-start.5
  9.6 13.2 %copy-start.1 = (bf16[2048,512]{1,0:T(8,128)(2,1)S(1)}, bf16[2048,512]{1,0:T(8,128)(2,1)}, u32[]{:S(2)}) copy-start(bf16[2048,512]{1,0:T(8,128)(2,1)} %refs_0_.1) | copy-start | bytes 6291460
  9.6 15.7 %copy-start.4 = (f32[2048]{0:T(1024)S(1)}, f32[2048]{0:T(1024)}, u32[]{:S(2)}) copy-start(f32[2048]{0:T(1024)} %param.6) | copy-start | bytes 24580
  11.5 7.8 %collective-permute-start = (f32[16,128]{1,0:T(8,128)S(1)}, f32[16,128]{1,0:T(8,128)S(1)}, u32[]{:S(2)}, u32[]{:S(2)}) collective-permute-start(f32[16,128]{1,0:T(8,128)S(1)} %get-tuple-element.19.refs_0_), channel_id=1, source_target_pairs={{0,5},{1,4},{2,7},{3,6},{4,1},{5,0},{6,3},{7,2},{8,13},{9,12},{10,... | collective-permute-start | bytes 24584 | tf_op jit(solution)/shard_map/ppermute | solution.py:308
  11.6 7.7 %collective-permute-start.1 = (f32[16,128]{1,0:T(8,128)S(1)}, f32[16,128]{1,0:T(8,128)S(1)}, u32[]{:S(2)}, u32[]{:S(2)}) collective-permute-start(f32[16,128]{1,0:T(8,128)S(1)} %get-tuple-element.19.refs_0_), channel_id=1, source_target_pairs={{0,4},{1,5},{2,6},{3,7},{4,0},{5,1},{6,2},{7,3},{8,12},{9,13},{10,... | collective-permute-start | bytes 24584 | tf_op jit(solution)/shard_map/ppermute | solution.py:308
  14.4 4.9 %collective-permute-start.2 = (f32[16,128]{1,0:T(8,128)S(1)}, f32[16,128]{1,0:T(8,128)S(1)}, u32[]{:S(2)}, u32[]{:S(2)}) collective-permute-start(f32[16,128]{1,0:T(8,128)S(1)} %get-tuple-element.19.refs_0_), channel_id=1, source_target_pairs={{0,1},{1,0},{2,3},{3,2},{4,5},{5,4},{6,7},{7,6},{8,9},{9,8},{10,11... | collective-permute-start | bytes 24584 | tf_op jit(solution)/shard_map/ppermute | solution.py:308
  19.4 10.6 %collective-permute-start.5 = (f32[192,512]{1,0:T(8,128)S(1)}, f32[192,512]{1,0:T(8,128)S(1)}, u32[]{:S(2)}, u32[]{:S(2)}) collective-permute-start(f32[192,512]{1,0:T(8,128)S(1)} %get-tuple-element.20.refs_0_), channel_id=1, source_target_pairs={{0,16},{8,24},{16,0},{24,8},{1,17},{9,25},{17,1},{25,9},{2,18},{10... | collective-permute-start | bytes 1179656 | tf_op jit(solution)/shard_map/ppermute | solution.py:308
  21.0 9.0 %collective-permute-start.10 = (f32[128,512]{1,0:T(8,128)S(1)}, f32[128,512]{1,0:T(8,128)S(1)}, u32[]{:S(2)}, u32[]{:S(2)}) collective-permute-start(f32[128,512]{1,0:T(8,128)S(1)} %get-tuple-element.24.refs_7_), channel_id=1, source_target_pairs={{0,1},{1,0},{2,3},{3,2},{4,5},{5,4},{6,7},{7,6},{8,9},{9,8},{10,11... | collective-permute-start | bytes 786440 | tf_op jit(solution)/shard_map/ppermute | solution.py:308
  21.6 3.7 %collective-permute-start.6 = (f32[16,128]{1,0:T(8,128)S(1)}, f32[16,128]{1,0:T(8,128)S(1)}, u32[]{:S(2)}, u32[]{:S(2)}) collective-permute-start(f32[16,128]{1,0:T(8,128)S(1)} %get-tuple-element.23.refs_3_), channel_id=1, source_target_pairs={{0,2},{1,3},{2,0},{3,1},{4,6},{5,7},{6,4},{7,5},{8,10},{9,11},{10,... | collective-permute-start | bytes 24584 | tf_op jit(solution)/shard_map/ppermute | solution.py:308
  26.3 1.9 %collective-permute-start.7 = (f32[4,128]{1,0:T(4,128)S(1)}, f32[4,128]{1,0:T(4,128)S(1)}, u32[]{:S(2)}, u32[]{:S(2)}) collective-permute-start(f32[4,128]{1,0:T(4,128)S(1)} %shard_map.63.refs_3_), channel_id=1, source_target_pairs={{0,8},{8,0},{16,24},{24,16},{1,9},{9,1},{17,25},{25,17},{2,10},{10... | collective-permute-start | bytes 6152 | tf_op jit(solution)/shard_map/ppermute | solution.py:308
  26.3 3.7 %collective-permute-start.8 = (f32[4,128]{1,0:T(4,128)S(1)}, f32[4,128]{1,0:T(4,128)S(1)}, u32[]{:S(2)}, u32[]{:S(2)}) collective-permute-start(f32[4,128]{1,0:T(4,128)S(1)} %shard_map.63.refs_3_), channel_id=1, source_target_pairs={{0,16},{8,24},{16,0},{24,8},{1,17},{9,25},{17,1},{25,9},{2,18},{10... | collective-permute-start | bytes 6152 | tf_op jit(solution)/shard_map/ppermute | solution.py:308
  26.9 3.1 %collective-permute-start.9 = (f32[4,128]{1,0:T(4,128)S(1)}, f32[4,128]{1,0:T(4,128)S(1)}, u32[]{:S(2)}, u32[]{:S(2)}) collective-permute-start(f32[4,128]{1,0:T(4,128)S(1)} %shard_map.63.refs_3_), channel_id=1, source_target_pairs={{0,24},{8,16},{16,8},{24,0},{1,25},{9,17},{17,9},{25,1},{2,26},{10... | collective-permute-start | bytes 6152 | tf_op jit(solution)/shard_map/ppermute | solution.py:308
  31.1 3.7 %collective-permute-start.12 = (f32[16,128]{1,0:T(8,128)S(1)}, f32[16,128]{1,0:T(8,128)S(1)}, u32[]{:S(2)}, u32[]{:S(2)}) collective-permute-start(f32[16,128]{1,0:T(8,128)S(1)} %get-tuple-element.26), channel_id=1, source_target_pairs={{0,1},{1,0},{2,3},{3,2},{4,5},{5,4},{6,7},{7,6},{8,9},{9,8},{10,11... | collective-permute-start | bytes 24584 | tf_op jit(solution)/shard_map/ppermute | solution.py:308
  32.6 10.8 %collective-permute-start.11 = (f32[192,512]{1,0:T(8,128)S(1)}, f32[192,512]{1,0:T(8,128)S(1)}, u32[]{:S(2)}, u32[]{:S(2)}) collective-permute-start(f32[192,512]{1,0:T(8,128)S(1)} %get-tuple-element.25.refs_2_), channel_id=1, source_target_pairs={{0,16},{8,24},{16,0},{24,8},{1,17},{9,25},{17,1},{25,9},{2,18},{10... | collective-permute-start | bytes 1179656 | tf_op jit(solution)/shard_map/ppermute | solution.py:308
  34.8 3.7 %collective-permute-start.13 = (f32[16,128]{1,0:T(8,128)S(1)}, f32[16,128]{1,0:T(8,128)S(1)}, u32[]{:S(2)}, u32[]{:S(2)}) collective-permute-start(f32[16,128]{1,0:T(8,128)S(1)} %multiply_add_fusion.2), channel_id=1, source_target_pairs={{0,2},{1,3},{2,0},{3,1},{4,6},{5,7},{6,4},{7,5},{8,10},{9,11},{10,... | collective-permute-start | bytes 24584 | tf_op jit(solution)/shard_map/ppermute | solution.py:308
  38.6 4.6 %collective-permute-start.14 = (f32[16,128]{1,0:T(8,128)S(1)}, f32[16,128]{1,0:T(8,128)S(1)}, u32[]{:S(2)}, u32[]{:S(2)}) collective-permute-start(f32[16,128]{1,0:T(8,128)S(1)} %multiply_add_fusion.1.refs_0_), channel_id=1, source_target_pairs={{0,4},{1,5},{2,6},{3,7},{4,0},{5,1},{6,2},{7,3},{8,12},{9,13},{10,... | collective-permute-start | bytes 24584 | tf_op jit(solution)/shard_map/ppermute | solution.py:308
  45.3 5.1 %copy-start.3 = (bf16[512,512]{1,0:T(8,128)(2,1)S(1)}, bf16[512,512]{1,0:T(8,128)(2,1)}, u32[]{:S(2)}) copy-start(bf16[512,512]{1,0:T(8,128)(2,1)} %refs_1_.1) | copy-start | bytes 1572868
  45.5 5.0 %collective-permute-start.15 = (f32[3,2,128,512]{3,2,1,0:T(8,128)S(1)}, f32[3,2,128,512]{3,2,1,0:T(8,128)S(1)}, u32[]{:S(2)}, u32[]{:S(2)}) collective-permute-start(f32[3,2,128,512]{3,2,1,0:T(8,128)S(1)} %shard_map.66.refs_2_), channel_id=1, source_target_pairs={{0,8},{8,0},{16,24},{24,16},{1,9},{9,1},{17,25},{25,17},{2,10},{10... | collective-permute-start | bytes 4718600 | tf_op jit(solution)/shard_map/ppermute | solution.py:308
  45.5 12.3 %collective-permute-start.22 = (f32[256,512]{1,0:T(8,128)S(1)}, f32[256,512]{1,0:T(8,128)S(1)}, u32[]{:S(2)}, u32[]{:S(2)}) collective-permute-start(f32[256,512]{1,0:T(8,128)S(1)} %get-tuple-element.31), channel_id=1, source_target_pairs={{0,8},{8,0},{16,24},{24,16},{1,9},{9,1},{17,25},{25,17},{2,10},{10... | collective-permute-start | bytes 1572872 | tf_op jit(solution)/shard_map/ppermute | solution.py:308
  46.0 5.7 %collective-permute-start.16 = (f32[4,128]{1,0:T(4,128)S(1)}, f32[4,128]{1,0:T(4,128)S(1)}, u32[]{:S(2)}, u32[]{:S(2)}) collective-permute-start(f32[4,128]{1,0:T(4,128)S(1)} %subtract_subtract_fusion.refs_3_), channel_id=1, source_target_pairs={{0,5},{1,4},{2,7},{3,6},{4,1},{5,0},{6,3},{7,2},{8,13},{9,12},{10,... | collective-permute-start | bytes 6152 | tf_op jit(solution)/shard_map/ppermute | solution.py:308
  48.7 4.5 %collective-permute-start.17 = (f32[4,128]{1,0:T(4,128)S(1)}, f32[4,128]{1,0:T(4,128)S(1)}, u32[]{:S(2)}, u32[]{:S(2)}) collective-permute-start(f32[4,128]{1,0:T(4,128)S(1)} %subtract_subtract_fusion.refs_3_), channel_id=1, source_target_pairs={{0,4},{1,5},{2,6},{3,7},{4,0},{5,1},{6,2},{7,3},{8,12},{9,13},{10,... | collective-permute-start | bytes 6152 | tf_op jit(solution)/shard_map/ppermute | solution.py:308
  49.6 3.6 %collective-permute-start.18 = (f32[4,128]{1,0:T(4,128)S(1)}, f32[4,128]{1,0:T(4,128)S(1)}, u32[]{:S(2)}, u32[]{:S(2)}) collective-permute-start(f32[4,128]{1,0:T(4,128)S(1)} %subtract_subtract_fusion.refs_3_), channel_id=1, source_target_pairs={{0,1},{1,0},{2,3},{3,2},{4,5},{5,4},{6,7},{7,6},{8,9},{9,8},{10,11... | collective-permute-start | bytes 6152 | tf_op jit(solution)/shard_map/ppermute | solution.py:308
  53.2 1.9 %collective-permute-start.19 = (f32[4,4,128]{2,1,0:T(4,128)S(1)}, f32[4,4,128]{2,1,0:T(4,128)S(1)}, u32[]{:S(2)}, u32[]{:S(2)}) collective-permute-start(f32[4,4,128]{2,1,0:T(4,128)S(1)} %shard_map.68.lse_ref), channel_id=1, source_target_pairs={{0,8},{8,0},{16,24},{24,16},{1,9},{9,1},{17,25},{25,17},{2,10},{10... | collective-permute-start | bytes 24584 | tf_op jit(solution)/shard_map/ppermute | solution.py:308
  53.2 3.7 %collective-permute-start.20 = (f32[4,4,128]{2,1,0:T(4,128)S(1)}, f32[4,4,128]{2,1,0:T(4,128)S(1)}, u32[]{:S(2)}, u32[]{:S(2)}) collective-permute-start(f32[4,4,128]{2,1,0:T(4,128)S(1)} %shard_map.68.lse_ref), channel_id=1, source_target_pairs={{0,16},{8,24},{16,0},{24,8},{1,17},{9,25},{17,1},{25,9},{2,18},{10... | collective-permute-start | bytes 24584 | tf_op jit(solution)/shard_map/ppermute | solution.py:308
  54.7 3.1 %collective-permute-start.21 = (f32[4,4,128]{2,1,0:T(4,128)S(1)}, f32[4,4,128]{2,1,0:T(4,128)S(1)}, u32[]{:S(2)}, u32[]{:S(2)}) collective-permute-start(f32[4,4,128]{2,1,0:T(4,128)S(1)} %shard_map.68.lse_ref), channel_id=1, source_target_pairs={{0,24},{8,16},{16,8},{24,0},{1,25},{9,17},{17,9},{25,1},{2,26},{10... | collective-permute-start | bytes 24584 | tf_op jit(solution)/shard_map/ppermute | solution.py:308
  58.1 14.1 %collective-permute-start.23 = (f32[256,512]{1,0:T(8,128)S(1)}, f32[256,512]{1,0:T(8,128)S(1)}, u32[]{:S(2)}, u32[]{:S(2)}) collective-permute-start(f32[256,512]{1,0:T(8,128)S(1)} %shard_map.69.one_ref), channel_id=1, source_target_pairs={{0,16},{8,24},{16,0},{24,8},{1,17},{9,25},{17,1},{25,9},{2,18},{10... | collective-permute-start | bytes 1572872 | tf_op jit(solution)/shard_map/ppermute | solution.py:308
  59.7 16.5 %collective-permute-start.28 = (f32[264,512]{1,0:T(8,128)S(1)}, f32[264,512]{1,0:T(8,128)S(1)}, u32[]{:S(2)}, u32[]{:S(2)}) collective-permute-start(f32[264,512]{1,0:T(8,128)S(1)} %shard_map.72), channel_id=1, source_target_pairs={{0,2},{1,3},{2,0},{3,1},{4,6},{5,7},{6,4},{7,5},{8,10},{9,11},{10,... | collective-permute-start | bytes 1622024 | tf_op jit(solution)/shard_map/ppermute | solution.py:308
  72.2 1.4 %collective-permute-start.24 = (f32[64,512]{1,0:T(8,128)S(1)}, f32[64,512]{1,0:T(8,128)S(1)}, u32[]{:S(2)}, u32[]{:S(2)}) collective-permute-start(f32[64,512]{1,0:T(8,128)S(1)} %get-tuple-element.32.refs_0_), channel_id=1, source_target_pairs={{0,8},{8,0},{16,24},{24,16},{1,9},{9,1},{17,25},{25,17},{2,10},{10... | collective-permute-start | bytes 393224 | tf_op jit(solution)/shard_map/ppermute | solution.py:308
  72.3 1.5 %collective-permute-start.25 = (f32[64,512]{1,0:T(8,128)S(1)}, f32[64,512]{1,0:T(8,128)S(1)}, u32[]{:S(2)}, u32[]{:S(2)}) collective-permute-start(f32[64,512]{1,0:T(8,128)S(1)} %get-tuple-element.33.refs_1_), channel_id=1, source_target_pairs={{0,8},{8,0},{16,24},{24,16},{1,9},{9,1},{17,25},{25,17},{2,10},{10... | collective-permute-start | bytes 393224 | tf_op jit(solution)/shard_map/ppermute | solution.py:308
  72.8 1.3 %collective-permute-start.26 = (f32[64,512]{1,0:T(8,128)S(1)}, f32[64,512]{1,0:T(8,128)S(1)}, u32[]{:S(2)}, u32[]{:S(2)}) collective-permute-start(f32[64,512]{1,0:T(8,128)S(1)} %get-tuple-element.34.refs_2_), channel_id=1, source_target_pairs={{0,8},{8,0},{16,24},{24,16},{1,9},{9,1},{17,25},{25,17},{2,10},{10... | collective-permute-start | bytes 393224 | tf_op jit(solution)/shard_map/ppermute | solution.py:308
  72.9 1.5 %collective-permute-start.27 = (f32[64,512]{1,0:T(8,128)S(1)}, f32[64,512]{1,0:T(8,128)S(1)}, u32[]{:S(2)}, u32[]{:S(2)}) collective-permute-start(f32[64,512]{1,0:T(8,128)S(1)} %get-tuple-element.35.refs_3_), channel_id=1, source_target_pairs={{0,8},{8,0},{16,24},{24,16},{1,9},{9,1},{17,25},{25,17},{2,10},{10... | collective-permute-start | bytes 393224 | tf_op jit(solution)/shard_map/ppermute | solution.py:308

commit v13 on v9

--- a/solution.py
+++ b/solution.py
@@ -148,21 +148,25 @@
 
 
 def last_sources_kernel(tile_ref, x_ref, ls_ref, sqx_ref, *refs):
-    parts, (lse_ref, sent_ref, mine_ref) = refs[:-4], refs[-3:]
+    parts, (lse_ref, sent_ref, mine_ref, weights_ref) = refs[:-5], refs[-4:]
     bias = source_bias(ls_ref, sqx_ref, parts)
-    x = x_ref[...]
-    n_rows = mine_ref.shape[0] // LANES
+    half = mine_ref.shape[0]
+    n_rows = half // LANES
     core = lax.axis_index("row") % 2
-    for out_ref, place in ((sent_ref, 1 - core), (mine_ref, core)):
+    inverse = []
+    for k, place in enumerate((1 - core, core)):
         columns = []
         for j in range(n_rows):
             at = pl.ds(pl.multiple_of((place * n_rows + j) * LANES, LANES), LANES)
             peak, total, exps = over_sources(tile_ref, at, bias)
             columns.append(peak + jnp.log2(total))
-            weights = jnp.concatenate([block.astype(jnp.bfloat16) for block in exps], axis=1)
-            mean = jnp.dot(weights, x, preferred_element_type=jnp.float32)
-            out_ref[pl.ds(j * LANES, LANES), :] = mean * (1.0 / total)
+            inverse.append(1.0 / total)
+            for b, block in enumerate(exps):
+                weights_ref[pl.ds((k * n_rows + j) * LANES, LANES), pl.ds(b * LANES, LANES)] = block.astype(jnp.bfloat16)
         lse_ref[pl.ds(place * n_rows, n_rows), :] = to_dense(columns)
+    mean = jnp.dot(weights_ref[...], x_ref[...], preferred_element_type=jnp.float32)
+    sent_ref[...] = mean[:half] * jnp.concatenate(inverse[:n_rows], axis=0)
+    mine_ref[...] = mean[half:] * jnp.concatenate(inverse[n_rows:], axis=0)
 
 
 def source_bias(ls_ref, sqx_ref, parts):
@@ -368,6 +372,7 @@
                 last_sources_kernel,
                 (tgt_dense, f32(half, width), f32(half, width)),
                 tile, source, ls, sqx, *parts, late[-1],
+                scratch=[pltpu.VMEM((n_tgt, n_src), jnp.bfloat16)],
             )
         parts = [lse] + [swap(lse, "row", k) for k in range(1, n_row)]
     total = merge_all(parts)

time: 74.3 us -> 74.6 us (level)
  no operation moved by 1% of the time
where the time goes in v13:
time: 74.6 us; the launch traced here: 74.3 us
  starting transfers between devices  32.2 us (43%)
  waiting for transfers between devices  25.5 us (34%)
  Pallas kernels  12.4 us (17%)
  local copies, waits for them, and re-layouts  3.32 us (4%)
  between operations  0.8 us (1%)
    ppermute x29, starting transfers between devices, swap(): return lax.ppermute(value, axis, [(i, i ^ distance) for i in range(n)])  32.2 us
    ppermute x29, waiting for transfers between devices, swap(): return lax.ppermute(value, axis, [(i, i ^ distance) for i in range(n)])  25.5 us
    pallas_call x14, Pallas kernels, call(): pl.pallas_call(kernel, out_shape=out_shape, in_specs=in_specs or [VMEM] *...  12.4 us
    unnamed x12, local copies, waits for them, and re-layouts  3.32 us
  transfers between devices with their start and end apart: 29, of which 16 were waited for; matrix products, arithmetic and copies ran while one was open for 0% of the time, Pallas kernels for 10%

profile of v13, /device:TPU:0, one launch (start us, length us, event | category | flops | bytes accessed | tf_op | source)
XLA Modules:
  0.0 74.3 jit_solution(11517486423825851174)
XLA Ops:
  0.6 0.0 copy-start.2
  0.6 1.0 %copy-done.2 = bf16[512,512]{1,0:T(8,128)(2,1)S(1)} copy-done((bf16[512,512]{1,0:T(8,128)(2,1)S(1)}, bf16[512,512]{1,0:T(8,128)(2,1)}, u32[]{:S(2)}) %copy-start.2) | copy-done | bytes 524312
  1.7 4.1 %collective-permute-start.3 = (f32[128,512]{1,0:T(8,128)S(1)}, f32[128,512]{1,0:T(8,128)S(1)}, u32[]{:S(2)}, u32[]{:S(2)}) collective-permute-start(f32[128,512]{1,0:T(8,128)S(1)} %shard_map.61), channel_id=1, source_target_pairs={{0,4},{1,5},{2,6},{3,7},{4,0},{5,1},{6,2},{7,3},{8,12},{9,13},{10,... | collective-permute-start | bytes 786440 | tf_op jit(solution)/shard_map/ppermute | solution.py:303
  5.8 1.5 %collective-permute-start.4 = (f32[128,512]{1,0:T(8,128)S(1)}, f32[128,512]{1,0:T(8,128)S(1)}, u32[]{:S(2)}, u32[]{:S(2)}) collective-permute-start(f32[128,512]{1,0:T(8,128)S(1)} %shard_map.61), channel_id=1, source_target_pairs={{0,1},{1,0},{2,3},{3,2},{4,5},{5,4},{6,7},{7,6},{8,9},{9,8},{10,11... | collective-permute-start | bytes 786440 | tf_op jit(solution)/shard_map/ppermute | solution.py:303
  7.3 1.6 %copy-done = bf16[2048,512]{1,0:T(8,128)(2,1)S(1)} copy-done((bf16[2048,512]{1,0:T(8,128)(2,1)S(1)}, bf16[2048,512]{1,0:T(8,128)(2,1)}, u32[]{:S(2)}) %copy-start) | copy-done | bytes 2097176
  8.9 0.7 copy-done.5
  9.6 1.9 %shard_map.59 = (f32[512,2048]{1,0:T(8,128)S(1)}, f32[16,128]{1,0:T(8,128)S(1)}, f32[4,128]{1,0:T(4,128)S(1)}) custom-call(bf16[512,512]{1,0:T(8,128)(2,1)S(1)} %copy-done.2, bf16[2048,512]{1,0:T(8,128)(2,1)S(1)} %copy-done, f32[4,128]{1,0:T(4,128)S(1)} %bitcast.5), custom_call_target="tpu_custom_call" | custom-call | tf_op jit(solution)/shard_map/pallas_call | solution.py:22
  11.5 0.1 collective-permute-start
  11.6 2.8 %collective-permute-start.1 = (f32[16,128]{1,0:T(8,128)S(1)}, f32[16,128]{1,0:T(8,128)S(1)}, u32[]{:S(2)}, u32[]{:S(2)}) collective-permute-start(f32[16,128]{1,0:T(8,128)S(1)} %get-tuple-element.23.refs_0_), channel_id=1, source_target_pairs={{0,4},{1,5},{2,6},{3,7},{4,0},{5,1},{6,2},{7,3},{8,12},{9,13},{10,... | collective-permute-start | bytes 24584 | tf_op jit(solution)/shard_map/ppermute | solution.py:303
  14.4 1.5 %collective-permute-start.2 = (f32[16,128]{1,0:T(8,128)S(1)}, f32[16,128]{1,0:T(8,128)S(1)}, u32[]{:S(2)}, u32[]{:S(2)}) collective-permute-start(f32[16,128]{1,0:T(8,128)S(1)} %get-tuple-element.23.refs_0_), channel_id=1, source_target_pairs={{0,1},{1,0},{2,3},{3,2},{4,5},{5,4},{6,7},{7,6},{8,9},{9,8},{10,11... | collective-permute-start | bytes 24584 | tf_op jit(solution)/shard_map/ppermute | solution.py:303
  15.9 3.4 %collective-permute-done.refs_1_ = f32[16,128]{1,0:T(8,128)S(1)} collective-permute-done((f32[16,128]{1,0:T(8,128)S(1)}, f32[16,128]{1,0:T(8,128)S(1)}, u32[]{:S(2)}, u32[]{:S(2)}) %collective-permute-start) | collective-permute-done | bytes 8224 | tf_op jit(solution)/shard_map/ppermute | solution.py:303
  19.3 0.0 collective-permute-done.4.refs_5_
  19.4 1.6 %collective-permute-start.10 = (f32[192,512]{1,0:T(8,128)S(1)}, f32[192,512]{1,0:T(8,128)S(1)}, u32[]{:S(2)}, u32[]{:S(2)}) collective-permute-start(f32[192,512]{1,0:T(8,128)S(1)} %get-tuple-element.26.refs_0_), channel_id=1, source_target_pairs={{0,16},{8,24},{16,0},{24,8},{1,17},{9,25},{17,1},{25,9},{2,18},{10... | collective-permute-start | bytes 1179656 | tf_op jit(solution)/shard_map/ppermute | solution.py:303
  21.0 0.6 collective-permute-start.9
  21.6 1.2 %collective-permute-start.5 = (f32[16,128]{1,0:T(8,128)S(1)}, f32[16,128]{1,0:T(8,128)S(1)}, u32[]{:S(2)}, u32[]{:S(2)}) collective-permute-start(f32[16,128]{1,0:T(8,128)S(1)} %get-tuple-element.24.refs_3_), channel_id=1, source_target_pairs={{0,2},{1,3},{2,0},{3,1},{4,6},{5,7},{6,4},{7,5},{8,10},{9,11},{10,... | collective-permute-start | bytes 24584 | tf_op jit(solution)/shard_map/ppermute | solution.py:303
  22.8 0.5 shard_map.60.refs_2_.sqx_ref
  23.3 2.0 %collective-permute-done.5.refs_4_ = f32[16,128]{1,0:T(8,128)S(1)} collective-permute-done((f32[16,128]{1,0:T(8,128)S(1)}, f32[16,128]{1,0:T(8,128)S(1)}, u32[]{:S(2)}, u32[]{:S(2)}) %collective-permute-start.5) | collective-permute-done | bytes 8224 | tf_op jit(solution)/shard_map/ppermute | solution.py:303
  25.3 1.0 %shard_map.63.refs_3_ = f32[4,128]{1,0:T(4,128)S(1)} custom-call(f32[512,2048]{1,0:T(8,128)S(1)} %get-tuple-element.21.refs_0_.tile_ref, f32[16,128]{1,0:T(8,128)S(1)} %bitcast.3, f32[16,128]{1,0:T(8,128)S(1)} %shard_map.60.refs_2_.sqx_ref, f32[16,128]{1,0:T(8,128)S(1)} %get-tuple-element.24.refs_3_, f32[16,128]{1,0:T(8,128)S(1)} %collective-permute-done.5.refs_4_), custom_call_target="tpu_custom_call" | custom-call | tf_op jit(solution)/shard_map/pallas_call | solution.py:22
  26.3 0.0 collective-permute-start.6
  26.3 0.6 collective-permute-start.7
  26.9 1.3 %collective-permute-start.8 = (f32[4,128]{1,0:T(4,128)S(1)}, f32[4,128]{1,0:T(4,128)S(1)}, u32[]{:S(2)}, u32[]{:S(2)}) collective-permute-start(f32[4,128]{1,0:T(4,128)S(1)} %shard_map.63.refs_3_), channel_id=1, source_target_pairs={{0,24},{8,16},{16,8},{24,0},{1,25},{9,17},{17,9},{25,1},{2,26},{10... | collective-permute-start | bytes 6152 | tf_op jit(solution)/shard_map/ppermute | solution.py:303
  28.2 0.0 collective-permute-done.6.refs_4_
  28.2 1.8 %collective-permute-done.7.refs_5_ = f32[4,128]{1,0:T(4,128)S(1)} collective-permute-done((f32[4,128]{1,0:T(4,128)S(1)}, f32[4,128]{1,0:T(4,128)S(1)}, u32[]{:S(2)}, u32[]{:S(2)}) %collective-permute-start.7) | collective-permute-done | bytes 2080 | tf_op jit(solution)/shard_map/ppermute | solution.py:303
  30.0 0.0 collective-permute-done.8.refs_6_
  30.0 1.1 %shard_map.64 = (f32[16,128]{1,0:T(8,128)S(1)}, f32[192,512]{1,0:T(8,128)S(1)}) custom-call(f32[512,2048]{1,0:T(8,128)S(1)} %get-tuple-element.21.refs_0_.tile_ref, f32[4,128]{1,0:T(4,128)S(1)} %bitcast.6, f32[4,128]{1,0:T(4,128)S(1)} %get-tuple-element.22.refs_2_, f32[4,128]{1,0:T(4,128)S(1)} %shard_map.63.refs_3_, ...), custom_call_target="tpu_custom_call" | custom-call | tf_op jit(solution)/shard_map/pallas_call | solution.py:22
  31.1 1.4 %collective-permute-start.11 = (f32[16,128]{1,0:T(8,128)S(1)}, f32[16,128]{1,0:T(8,128)S(1)}, u32[]{:S(2)}, u32[]{:S(2)}) collective-permute-start(f32[16,128]{1,0:T(8,128)S(1)} %get-tuple-element.27), channel_id=1, source_target_pairs={{0,1},{1,0},{2,3},{3,2},{4,5},{5,4},{6,7},{7,6},{8,9},{9,8},{10,11... | collective-permute-start | bytes 24584 | tf_op jit(solution)/shard_map/ppermute | solution.py:303
  32.6 1.4 %collective-permute-start.14 = (f32[192,512]{1,0:T(8,128)S(1)}, f32[192,512]{1,0:T(8,128)S(1)}, u32[]{:S(2)}, u32[]{:S(2)}) collective-permute-start(f32[192,512]{1,0:T(8,128)S(1)} %get-tuple-element.28.refs_2_), channel_id=1, source_target_pairs={{0,16},{8,24},{16,0},{24,8},{1,17},{9,25},{17,1},{25,9},{2,18},{10... | collective-permute-start | bytes 1179656 | tf_op jit(solution)/shard_map/ppermute | solution.py:303
  34.0 0.8 %collective-permute-done.11 = f32[16,128]{1,0:T(8,128)S(1)} collective-permute-done((f32[16,128]{1,0:T(8,128)S(1)}, f32[16,128]{1,0:T(8,128)S(1)}, u32[]{:S(2)}, u32[]{:S(2)}) %collective-permute-start.11) | collective-permute-done | bytes 8224 | tf_op jit(solution)/shard_map/ppermute | solution.py:303
  34.8 1.2 %collective-permute-start.12 = (f32[16,128]{1,0:T(8,128)S(1)}, f32[16,128]{1,0:T(8,128)S(1)}, u32[]{:S(2)}, u32[]{:S(2)}) collective-permute-start(f32[16,128]{1,0:T(8,128)S(1)} %multiply_add_fusion.1), channel_id=1, source_target_pairs={{0,2},{1,3},{2,0},{3,1},{4,6},{5,7},{6,4},{7,5},{8,10},{9,11},{10,... | collective-permute-start | bytes 24584 | tf_op jit(solution)/shard_map/ppermute | solution.py:303
  36.1 2.5 %collective-permute-done.12 = f32[16,128]{1,0:T(8,128)S(1)} collective-permute-done((f32[16,128]{1,0:T(8,128)S(1)}, f32[16,128]{1,0:T(8,128)S(1)}, u32[]{:S(2)}, u32[]{:S(2)}) %collective-permute-start.12) | collective-permute-done | bytes 8224 | tf_op jit(solution)/shard_map/ppermute | solution.py:303
  38.6 2.3 %collective-permute-start.13 = (f32[16,128]{1,0:T(8,128)S(1)}, f32[16,128]{1,0:T(8,128)S(1)}, u32[]{:S(2)}, u32[]{:S(2)}) collective-permute-start(f32[16,128]{1,0:T(8,128)S(1)} %multiply_add_fusion.refs_0_), channel_id=1, source_target_pairs={{0,4},{1,5},{2,6},{3,7},{4,0},{5,1},{6,2},{7,3},{8,12},{9,13},{10,... | collective-permute-start | bytes 24584 | tf_op jit(solution)/shard_map/ppermute | solution.py:303
  40.9 2.3 %collective-permute-done.13.refs_1_ = f32[16,128]{1,0:T(8,128)S(1)} collective-permute-done((f32[16,128]{1,0:T(8,128)S(1)}, f32[16,128]{1,0:T(8,128)S(1)}, u32[]{:S(2)}, u32[]{:S(2)}) %collective-permute-start.13) | collective-permute-done | bytes 8224 | tf_op jit(solution)/shard_map/ppermute | solution.py:303
  43.2 0.2 collective-permute-done.14.refs_2_.refs_3_
  43.4 2.2 %shard_map.65 = (f32[4,128]{1,0:T(4,128)S(1)}, f32[256,512]{1,0:T(8,128)S(1)}, f32[256,512]{1,0:T(8,128)S(1)}) custom-call(f32[512,2048]{1,0:T(8,128)S(1)} %get-tuple-element.21.refs_0_.tile_ref, bf16[2048,512]{1,0:T(8,128)(2,1)S(1)} %copy-done.1, f32[16,128]{1,0:T(8,128)S(1)} %bitcast.4, f32[16,128]{1,0:T(8,128)S(1)} %shard_map.60.refs_2_.sqx_ref, ...), custom_call_target="tpu_custom_call" | custom-call | tf_op jit(solution)/shard_map/pallas_call | solution.py:22
  45.6 0.0 copy-start.3
  45.6 0.1 collective-permute-start.15
  45.7 1.6 %collective-permute-start.18 = (f32[4,128]{1,0:T(4,128)S(1)}, f32[4,128]{1,0:T(4,128)S(1)}, u32[]{:S(2)}, u32[]{:S(2)}) collective-permute-start(f32[4,128]{1,0:T(4,128)S(1)} %get-tuple-element.31.lse_ref), channel_id=1, source_target_pairs={{0,24},{8,16},{16,8},{24,0},{1,25},{9,17},{17,9},{25,1},{2,26},{10... | collective-permute-start | bytes 6152 | tf_op jit(solution)/shard_map/ppermute | solution.py:303
  47.3 0.5 collective-permute-start.17
  47.8 0.9 %collective-permute-done.18 = f32[4,128]{1,0:T(4,128)S(1)} collective-permute-done((f32[4,128]{1,0:T(4,128)S(1)}, f32[4,128]{1,0:T(4,128)S(1)}, u32[]{:S(2)}, u32[]{:S(2)}) %collective-permute-start.18) | collective-permute-done | bytes 2080 | tf_op jit(solution)/shard_map/ppermute | solution.py:303
  48.7 2.1 %collective-permute-done.17 = f32[4,128]{1,0:T(4,128)S(1)} collective-permute-done((f32[4,128]{1,0:T(4,128)S(1)}, f32[4,128]{1,0:T(4,128)S(1)}, u32[]{:S(2)}, u32[]{:S(2)}) %collective-permute-start.17) | collective-permute-done | bytes 2080 | tf_op jit(solution)/shard_map/ppermute | solution.py:303
  50.9 0.4 shard_map.66
  51.3 0.1 collective-permute-start.19
  51.4 0.6 collective-permute-start.24
  52.0 2.6 %collective-permute-start.20 = (f32[4,128]{1,0:T(4,128)S(1)}, f32[4,128]{1,0:T(4,128)S(1)}, u32[]{:S(2)}, u32[]{:S(2)}) collective-permute-start(f32[4,128]{1,0:T(4,128)S(1)} %get-tuple-element.40.refs_5_), channel_id=1, source_target_pairs={{0,5},{1,4},{2,7},{3,6},{4,1},{5,0},{6,3},{7,2},{8,13},{9,12},{10,... | collective-permute-start | bytes 6152 | tf_op jit(solution)/shard_map/ppermute | solution.py:303
  54.6 0.9 %collective-permute-start.21 = (f32[4,128]{1,0:T(4,128)S(1)}, f32[4,128]{1,0:T(4,128)S(1)}, u32[]{:S(2)}, u32[]{:S(2)}) collective-permute-start(f32[4,128]{1,0:T(4,128)S(1)} %get-tuple-element.40.refs_5_), channel_id=1, source_target_pairs={{0,4},{1,5},{2,6},{3,7},{4,0},{5,1},{6,2},{7,3},{8,12},{9,13},{10,... | collective-permute-start | bytes 6152 | tf_op jit(solution)/shard_map/ppermute | solution.py:303
  55.5 0.9 %collective-permute-start.22 = (f32[4,128]{1,0:T(4,128)S(1)}, f32[4,128]{1,0:T(4,128)S(1)}, u32[]{:S(2)}, u32[]{:S(2)}) collective-permute-start(f32[4,128]{1,0:T(4,128)S(1)} %get-tuple-element.40.refs_5_), channel_id=1, source_target_pairs={{0,1},{1,0},{2,3},{3,2},{4,5},{5,4},{6,7},{7,6},{8,9},{9,8},{10,11... | collective-permute-start | bytes 6152 | tf_op jit(solution)/shard_map/ppermute | solution.py:303
  56.4 1.3 %shard_map.67 = (bf16[2048,512]{1,0:T(8,128)(2,1)S(1)}, f32[512,2048]{1,0:T(8,128)S(1)}) custom-call(bf16[2048,512]{1,0:T(8,128)(2,1)S(1)} %copy-done.1, bf16[512,512]{1,0:T(8,128)(2,1)S(1)} %copy-done.3, f32[3,2,128,512]{3,2,1,0:T(8,128)S(1)} %get-tuple-element.32.refs_2_, f32[3,2,128,512]{3,2,1,0:T(8,128)S(1)} %collective-permute-done.19.refs_3_), custom_call_target="tpu_custom_call" | custom-call | tf_op jit(solution)/shard_map/pallas_call | solution.py:22
  57.7 1.4 %collective-permute-done.21.refs_3_ = f32[4,128]{1,0:T(4,128)S(1)} collective-permute-done((f32[4,128]{1,0:T(4,128)S(1)}, f32[4,128]{1,0:T(4,128)S(1)}, u32[]{:S(2)}, u32[]{:S(2)}) %collective-permute-start.21) | collective-permute-done | bytes 2080 | tf_op jit(solution)/shard_map/ppermute | solution.py:303
  59.1 0.9 %shard_map.69 = f32[264,512]{1,0:T(8,128)S(1)} custom-call(f32[512,2048]{1,0:T(8,128)S(1)} %get-tuple-element.33.refs_0_, bf16[2048,512]{1,0:T(8,128)(2,1)S(1)} %get-tuple-element.34.refs_1_, f32[4,128]{1,0:T(4,128)S(1)} %collective-permute-done.20.refs_2_, f32[4,128]{1,0:T(4,128)S(1)} %collective-permute-done.21.refs_3_, ...), custom_call_target="tpu_custom_call" | custom-call | tf_op jit(solution)/shard_map/pallas_call | solution.py:22
  60.0 2.1 %collective-permute-start.23 = (f32[264,512]{1,0:T(8,128)S(1)}, f32[264,512]{1,0:T(8,128)S(1)}, u32[]{:S(2)}, u32[]{:S(2)}) collective-permute-start(f32[264,512]{1,0:T(8,128)S(1)} %shard_map.69), channel_id=1, source_target_pairs={{0,2},{1,3},{2,0},{3,1},{4,6},{5,7},{6,4},{7,5},{8,10},{9,11},{10,... | collective-permute-start | bytes 1622024 | tf_op jit(solution)/shard_map/ppermute | solution.py:303
  62.1 3.7 %collective-permute-done.24.two_ref = f32[256,512]{1,0:T(8,128)S(1)} collective-permute-done((f32[256,512]{1,0:T(8,128)S(1)}, f32[256,512]{1,0:T(8,128)S(1)}, u32[]{:S(2)}, u32[]{:S(2)}) %collective-permute-start.24) | collective-permute-done | bytes 524320 | tf_op jit(solution)/shard_map/ppermute | solution.py:303
  65.7 0.1 shard_map.71
  65.8 0.1 collective-permute-start.25
  65.9 0.5 collective-permute-start.26
  66.4 0.1 collective-permute-start.27
  66.4 0.4 collective-permute-start.28
  66.9 0.3 collective-permute-done.25.refs_4_
  67.2 0.2 collective-permute-done.26.refs_5_
  67.4 0.3 collective-permute-done.27.refs_6_
  67.7 0.2 collective-permute-done.28.refs_7_
  67.9 1.0 %shard_map.72 = f32[512,512]{1,0:T(8,128)} custom-call(f32[64,512]{1,0:T(8,128)S(1)} %get-tuple-element.36.refs_0_, f32[64,512]{1,0:T(8,128)S(1)} %get-tuple-element.37.refs_1_, f32[64,512]{1,0:T(8,128)S(1)} %get-tuple-element.38.refs_2_, f32[64,512]{1,0:T(8,128)S(1)} %get-tuple-element.39.refs_3_, f32[64,512]{1,0:T(8,128)S(1)} %collective-permute-done.25.refs_4_, ...), custom_call_target="tpu_custom_call" | custom-call | tf_op jit(solution)/shard_map/pallas_call | solution.py:22
  68.9 0.9 %shard_map.68.refs_0_ = f32[264,512]{1,0:T(8,128)S(1)} custom-call(f32[512,2048]{1,0:T(8,128)S(1)} %get-tuple-element.33.refs_0_, bf16[2048,512]{1,0:T(8,128)(2,1)S(1)} %get-tuple-element.34.refs_1_, f32[4,128]{1,0:T(4,128)S(1)} %collective-permute-done.20.refs_2_, f32[4,128]{1,0:T(4,128)S(1)} %collective-permute-done.21.refs_3_, ...), custom_call_target="tpu_custom_call" | custom-call | tf_op jit(solution)/shard_map/pallas_call | solution.py:22
  69.8 3.4 %collective-permute-done.23.refs_1_ = f32[264,512]{1,0:T(8,128)S(1)} collective-permute-done((f32[264,512]{1,0:T(8,128)S(1)}, f32[264,512]{1,0:T(8,128)S(1)}, u32[]{:S(2)}, u32[]{:S(2)}) %collective-permute-start.23) | collective-permute-done | bytes 540704 | tf_op jit(solution)/shard_map/ppermute | solution.py:303
  73.2 1.1 %shard_map.70 = f32[256,512]{1,0:T(8,128)} custom-call(f32[264,512]{1,0:T(8,128)S(1)} %shard_map.68.refs_0_, f32[264,512]{1,0:T(8,128)S(1)} %collective-permute-done.23.refs_1_), custom_call_target="tpu_custom_call" | custom-call | tf_op jit(solution)/shard_map/pallas_call | solution.py:22
  (23 shorter events, 0.2 us)
Async XLA Ops:
  0.6 1.0 %copy-start.2 = (bf16[512,512]{1,0:T(8,128)(2,1)S(1)}, bf16[512,512]{1,0:T(8,128)(2,1)}, u32[]{:S(2)}) copy-start(bf16[512,512]{1,0:T(8,128)(2,1)} %refs_1_.1) | copy-start | bytes 1572868
  1.7 17.6 %collective-permute-start.3 = (f32[128,512]{1,0:T(8,128)S(1)}, f32[128,512]{1,0:T(8,128)S(1)}, u32[]{:S(2)}, u32[]{:S(2)}) collective-permute-start(f32[128,512]{1,0:T(8,128)S(1)} %shard_map.61), channel_id=1, source_target_pairs={{0,4},{1,5},{2,6},{3,7},{4,0},{5,1},{6,2},{7,3},{8,12},{9,13},{10,... | collective-permute-start | bytes 786440 | tf_op jit(solution)/shard_map/ppermute | solution.py:303
  5.8 13.5 %collective-permute-start.4 = (f32[128,512]{1,0:T(8,128)S(1)}, f32[128,512]{1,0:T(8,128)S(1)}, u32[]{:S(2)}, u32[]{:S(2)}) collective-permute-start(f32[128,512]{1,0:T(8,128)S(1)} %shard_map.61), channel_id=1, source_target_pairs={{0,1},{1,0},{2,3},{3,2},{4,5},{5,4},{6,7},{7,6},{8,9},{9,8},{10,11... | collective-permute-start | bytes 786440 | tf_op jit(solution)/shard_map/ppermute | solution.py:303
  7.3 1.6 %copy-start = (bf16[2048,512]{1,0:T(8,128)(2,1)S(1)}, bf16[2048,512]{1,0:T(8,128)(2,1)}, u32[]{:S(2)}) copy-start(bf16[2048,512]{1,0:T(8,128)(2,1)} %refs_0_.1) | copy-start | bytes 6291460
  8.9 0.7 copy-start.5
  9.6 13.2 %copy-start.1 = (bf16[2048,512]{1,0:T(8,128)(2,1)S(1)}, bf16[2048,512]{1,0:T(8,128)(2,1)}, u32[]{:S(2)}) copy-start(bf16[2048,512]{1,0:T(8,128)(2,1)} %refs_0_.1) | copy-start | bytes 6291460
  9.6 15.7 %copy-start.4 = (f32[2048]{0:T(1024)S(1)}, f32[2048]{0:T(1024)}, u32[]{:S(2)}) copy-start(f32[2048]{0:T(1024)} %param.6) | copy-start | bytes 24580
  11.5 7.8 %collective-permute-start = (f32[16,128]{1,0:T(8,128)S(1)}, f32[16,128]{1,0:T(8,128)S(1)}, u32[]{:S(2)}, u32[]{:S(2)}) collective-permute-start(f32[16,128]{1,0:T(8,128)S(1)} %get-tuple-element.23.refs_0_), channel_id=1, source_target_pairs={{0,5},{1,4},{2,7},{3,6},{4,1},{5,0},{6,3},{7,2},{8,13},{9,12},{10,... | collective-permute-start | bytes 24584 | tf_op jit(solution)/shard_map/ppermute | solution.py:303
  11.6 7.7 %collective-permute-start.1 = (f32[16,128]{1,0:T(8,128)S(1)}, f32[16,128]{1,0:T(8,128)S(1)}, u32[]{:S(2)}, u32[]{:S(2)}) collective-permute-start(f32[16,128]{1,0:T(8,128)S(1)} %get-tuple-element.23.refs_0_), channel_id=1, source_target_pairs={{0,4},{1,5},{2,6},{3,7},{4,0},{5,1},{6,2},{7,3},{8,12},{9,13},{10,... | collective-permute-start | bytes 24584 | tf_op jit(solution)/shard_map/ppermute | solution.py:303
  14.4 4.9 %collective-permute-start.2 = (f32[16,128]{1,0:T(8,128)S(1)}, f32[16,128]{1,0:T(8,128)S(1)}, u32[]{:S(2)}, u32[]{:S(2)}) collective-permute-start(f32[16,128]{1,0:T(8,128)S(1)} %get-tuple-element.23.refs_0_), channel_id=1, source_target_pairs={{0,1},{1,0},{2,3},{3,2},{4,5},{5,4},{6,7},{7,6},{8,9},{9,8},{10,11... | collective-permute-start | bytes 24584 | tf_op jit(solution)/shard_map/ppermute | solution.py:303
  19.4 10.6 %collective-permute-start.10 = (f32[192,512]{1,0:T(8,128)S(1)}, f32[192,512]{1,0:T(8,128)S(1)}, u32[]{:S(2)}, u32[]{:S(2)}) collective-permute-start(f32[192,512]{1,0:T(8,128)S(1)} %get-tuple-element.26.refs_0_), channel_id=1, source_target_pairs={{0,16},{8,24},{16,0},{24,8},{1,17},{9,25},{17,1},{25,9},{2,18},{10... | collective-permute-start | bytes 1179656 | tf_op jit(solution)/shard_map/ppermute | solution.py:303
  21.0 9.0 %collective-permute-start.9 = (f32[128,512]{1,0:T(8,128)S(1)}, f32[128,512]{1,0:T(8,128)S(1)}, u32[]{:S(2)}, u32[]{:S(2)}) collective-permute-start(f32[128,512]{1,0:T(8,128)S(1)} %get-tuple-element.25.refs_7_), channel_id=1, source_target_pairs={{0,1},{1,0},{2,3},{3,2},{4,5},{5,4},{6,7},{7,6},{8,9},{9,8},{10,11... | collective-permute-start | bytes 786440 | tf_op jit(solution)/shard_map/ppermute | solution.py:303
  21.6 3.7 %collective-permute-start.5 = (f32[16,128]{1,0:T(8,128)S(1)}, f32[16,128]{1,0:T(8,128)S(1)}, u32[]{:S(2)}, u32[]{:S(2)}) collective-permute-start(f32[16,128]{1,0:T(8,128)S(1)} %get-tuple-element.24.refs_3_), channel_id=1, source_target_pairs={{0,2},{1,3},{2,0},{3,1},{4,6},{5,7},{6,4},{7,5},{8,10},{9,11},{10,... | collective-permute-start | bytes 24584 | tf_op jit(solution)/shard_map/ppermute | solution.py:303
  26.3 1.9 %collective-permute-start.6 = (f32[4,128]{1,0:T(4,128)S(1)}, f32[4,128]{1,0:T(4,128)S(1)}, u32[]{:S(2)}, u32[]{:S(2)}) collective-permute-start(f32[4,128]{1,0:T(4,128)S(1)} %shard_map.63.refs_3_), channel_id=1, source_target_pairs={{0,8},{8,0},{16,24},{24,16},{1,9},{9,1},{17,25},{25,17},{2,10},{10... | collective-permute-start | bytes 6152 | tf_op jit(solution)/shard_map/ppermute | solution.py:303
  26.3 3.7 %collective-permute-start.7 = (f32[4,128]{1,0:T(4,128)S(1)}, f32[4,128]{1,0:T(4,128)S(1)}, u32[]{:S(2)}, u32[]{:S(2)}) collective-permute-start(f32[4,128]{1,0:T(4,128)S(1)} %shard_map.63.refs_3_), channel_id=1, source_target_pairs={{0,16},{8,24},{16,0},{24,8},{1,17},{9,25},{17,1},{25,9},{2,18},{10... | collective-permute-start | bytes 6152 | tf_op jit(solution)/shard_map/ppermute | solution.py:303
  26.9 3.1 %collective-permute-start.8 = (f32[4,128]{1,0:T(4,128)S(1)}, f32[4,128]{1,0:T(4,128)S(1)}, u32[]{:S(2)}, u32[]{:S(2)}) collective-permute-start(f32[4,128]{1,0:T(4,128)S(1)} %shard_map.63.refs_3_), channel_id=1, source_target_pairs={{0,24},{8,16},{16,8},{24,0},{1,25},{9,17},{17,9},{25,1},{2,26},{10... | collective-permute-start | bytes 6152 | tf_op jit(solution)/shard_map/ppermute | solution.py:303
  31.1 3.7 %collective-permute-start.11 = (f32[16,128]{1,0:T(8,128)S(1)}, f32[16,128]{1,0:T(8,128)S(1)}, u32[]{:S(2)}, u32[]{:S(2)}) collective-permute-start(f32[16,128]{1,0:T(8,128)S(1)} %get-tuple-element.27), channel_id=1, source_target_pairs={{0,1},{1,0},{2,3},{3,2},{4,5},{5,4},{6,7},{7,6},{8,9},{9,8},{10,11... | collective-permute-start | bytes 24584 | tf_op jit(solution)/shard_map/ppermute | solution.py:303
  32.6 10.8 %collective-permute-start.14 = (f32[192,512]{1,0:T(8,128)S(1)}, f32[192,512]{1,0:T(8,128)S(1)}, u32[]{:S(2)}, u32[]{:S(2)}) collective-permute-start(f32[192,512]{1,0:T(8,128)S(1)} %get-tuple-element.28.refs_2_), channel_id=1, source_target_pairs={{0,16},{8,24},{16,0},{24,8},{1,17},{9,25},{17,1},{25,9},{2,18},{10... | collective-permute-start | bytes 1179656 | tf_op jit(solution)/shard_map/ppermute | solution.py:303
  34.8 3.7 %collective-permute-start.12 = (f32[16,128]{1,0:T(8,128)S(1)}, f32[16,128]{1,0:T(8,128)S(1)}, u32[]{:S(2)}, u32[]{:S(2)}) collective-permute-start(f32[16,128]{1,0:T(8,128)S(1)} %multiply_add_fusion.1), channel_id=1, source_target_pairs={{0,2},{1,3},{2,0},{3,1},{4,6},{5,7},{6,4},{7,5},{8,10},{9,11},{10,... | collective-permute-start | bytes 24584 | tf_op jit(solution)/shard_map/ppermute | solution.py:303
  38.6 4.6 %collective-permute-start.13 = (f32[16,128]{1,0:T(8,128)S(1)}, f32[16,128]{1,0:T(8,128)S(1)}, u32[]{:S(2)}, u32[]{:S(2)}) collective-permute-start(f32[16,128]{1,0:T(8,128)S(1)} %multiply_add_fusion.refs_0_), channel_id=1, source_target_pairs={{0,4},{1,5},{2,6},{3,7},{4,0},{5,1},{6,2},{7,3},{8,12},{9,13},{10,... | collective-permute-start | bytes 24584 | tf_op jit(solution)/shard_map/ppermute | solution.py:303
  45.6 10.8 %copy-start.3 = (bf16[512,512]{1,0:T(8,128)(2,1)S(1)}, bf16[512,512]{1,0:T(8,128)(2,1)}, u32[]{:S(2)}) copy-start(bf16[512,512]{1,0:T(8,128)(2,1)} %refs_1_.1) | copy-start | bytes 1572868
  45.6 5.3 %collective-permute-start.15 = (f32[256,512]{1,0:T(8,128)S(1)}, f32[256,512]{1,0:T(8,128)S(1)}, u32[]{:S(2)}, u32[]{:S(2)}) collective-permute-start(f32[256,512]{1,0:T(8,128)S(1)} %get-tuple-element.30), channel_id=1, source_target_pairs={{0,8},{8,0},{16,24},{24,16},{1,9},{9,1},{17,25},{25,17},{2,10},{10... | collective-permute-start | bytes 1572872 | tf_op jit(solution)/shard_map/ppermute | solution.py:303
  45.7 3.1 %collective-permute-start.18 = (f32[4,128]{1,0:T(4,128)S(1)}, f32[4,128]{1,0:T(4,128)S(1)}, u32[]{:S(2)}, u32[]{:S(2)}) collective-permute-start(f32[4,128]{1,0:T(4,128)S(1)} %get-tuple-element.31.lse_ref), channel_id=1, source_target_pairs={{0,24},{8,16},{16,8},{24,0},{1,25},{9,17},{17,9},{25,1},{2,26},{10... | collective-permute-start | bytes 6152 | tf_op jit(solution)/shard_map/ppermute | solution.py:303
  47.3 3.6 %collective-permute-start.17 = (f32[4,128]{1,0:T(4,128)S(1)}, f32[4,128]{1,0:T(4,128)S(1)}, u32[]{:S(2)}, u32[]{:S(2)}) collective-permute-start(f32[4,128]{1,0:T(4,128)S(1)} %get-tuple-element.31.lse_ref), channel_id=1, source_target_pairs={{0,16},{8,24},{16,0},{24,8},{1,17},{9,25},{17,1},{25,9},{2,18},{10... | collective-permute-start | bytes 6152 | tf_op jit(solution)/shard_map/ppermute | solution.py:303
  47.8 3.1 %collective-permute-start.16 = (f32[4,128]{1,0:T(4,128)S(1)}, f32[4,128]{1,0:T(4,128)S(1)}, u32[]{:S(2)}, u32[]{:S(2)}) collective-permute-start(f32[4,128]{1,0:T(4,128)S(1)} %get-tuple-element.31.lse_ref), channel_id=1, source_target_pairs={{0,8},{8,0},{16,24},{24,16},{1,9},{9,1},{17,25},{25,17},{2,10},{10... | collective-permute-start | bytes 6152 | tf_op jit(solution)/shard_map/ppermute | solution.py:303
  51.3 5.1 %collective-permute-start.19 = (f32[3,2,128,512]{3,2,1,0:T(8,128)S(1)}, f32[3,2,128,512]{3,2,1,0:T(8,128)S(1)}, u32[]{:S(2)}, u32[]{:S(2)}) collective-permute-start(f32[3,2,128,512]{3,2,1,0:T(8,128)S(1)} %get-tuple-element.32.refs_2_), channel_id=1, source_target_pairs={{0,8},{8,0},{16,24},{24,16},{1,9},{9,1},{17,25},{25,17},{2,10},{10... | collective-permute-start | bytes 4718600 | tf_op jit(solution)/shard_map/ppermute | solution.py:303
  51.4 14.3 %collective-permute-start.24 = (f32[256,512]{1,0:T(8,128)S(1)}, f32[256,512]{1,0:T(8,128)S(1)}, u32[]{:S(2)}, u32[]{:S(2)}) collective-permute-start(f32[256,512]{1,0:T(8,128)S(1)} %get-tuple-element.35.one_ref), channel_id=1, source_target_pairs={{0,16},{8,24},{16,0},{24,8},{1,17},{9,25},{17,1},{25,9},{2,18},{10... | collective-permute-start | bytes 1572872 | tf_op jit(solution)/shard_map/ppermute | solution.py:303
  52.0 5.7 %collective-permute-start.20 = (f32[4,128]{1,0:T(4,128)S(1)}, f32[4,128]{1,0:T(4,128)S(1)}, u32[]{:S(2)}, u32[]{:S(2)}) collective-permute-start(f32[4,128]{1,0:T(4,128)S(1)} %get-tuple-element.40.refs_5_), channel_id=1, source_target_pairs={{0,5},{1,4},{2,7},{3,6},{4,1},{5,0},{6,3},{7,2},{8,13},{9,12},{10,... | collective-permute-start | bytes 6152 | tf_op jit(solution)/shard_map/ppermute | solution.py:303
  54.6 4.5 %collective-permute-start.21 = (f32[4,128]{1,0:T(4,128)S(1)}, f32[4,128]{1,0:T(4,128)S(1)}, u32[]{:S(2)}, u32[]{:S(2)}) collective-permute-start(f32[4,128]{1,0:T(4,128)S(1)} %get-tuple-element.40.refs_5_), channel_id=1, source_target_pairs={{0,4},{1,5},{2,6},{3,7},{4,0},{5,1},{6,2},{7,3},{8,12},{9,13},{10,... | collective-permute-start | bytes 6152 | tf_op jit(solution)/shard_map/ppermute | solution.py:303
  55.5 3.6 %collective-permute-start.22 = (f32[4,128]{1,0:T(4,128)S(1)}, f32[4,128]{1,0:T(4,128)S(1)}, u32[]{:S(2)}, u32[]{:S(2)}) collective-permute-start(f32[4,128]{1,0:T(4,128)S(1)} %get-tuple-element.40.refs_5_), channel_id=1, source_target_pairs={{0,1},{1,0},{2,3},{3,2},{4,5},{5,4},{6,7},{7,6},{8,9},{9,8},{10,11... | collective-permute-start | bytes 6152 | tf_op jit(solution)/shard_map/ppermute | solution.py:303
  60.0 13.3 %collective-permute-start.23 = (f32[264,512]{1,0:T(8,128)S(1)}, f32[264,512]{1,0:T(8,128)S(1)}, u32[]{:S(2)}, u32[]{:S(2)}) collective-permute-start(f32[264,512]{1,0:T(8,128)S(1)} %shard_map.69), channel_id=1, source_target_pairs={{0,2},{1,3},{2,0},{3,1},{4,6},{5,7},{6,4},{7,5},{8,10},{9,11},{10,... | collective-permute-start | bytes 1622024 | tf_op jit(solution)/shard_map/ppermute | solution.py:303
  65.8 1.4 %collective-permute-start.25 = (f32[64,512]{1,0:T(8,128)S(1)}, f32[64,512]{1,0:T(8,128)S(1)}, u32[]{:S(2)}, u32[]{:S(2)}) collective-permute-start(f32[64,512]{1,0:T(8,128)S(1)} %get-tuple-element.36.refs_0_), channel_id=1, source_target_pairs={{0,8},{8,0},{16,24},{24,16},{1,9},{9,1},{17,25},{25,17},{2,10},{10... | collective-permute-start | bytes 393224 | tf_op jit(solution)/shard_map/ppermute | solution.py:303
  65.9 1.5 %collective-permute-start.26 = (f32[64,512]{1,0:T(8,128)S(1)}, f32[64,512]{1,0:T(8,128)S(1)}, u32[]{:S(2)}, u32[]{:S(2)}) collective-permute-start(f32[64,512]{1,0:T(8,128)S(1)} %get-tuple-element.37.refs_1_), channel_id=1, source_target_pairs={{0,8},{8,0},{16,24},{24,16},{1,9},{9,1},{17,25},{25,17},{2,10},{10... | collective-permute-start | bytes 393224 | tf_op jit(solution)/shard_map/ppermute | solution.py:303
  66.4 1.3 %collective-permute-start.27 = (f32[64,512]{1,0:T(8,128)S(1)}, f32[64,512]{1,0:T(8,128)S(1)}, u32[]{:S(2)}, u32[]{:S(2)}) collective-permute-start(f32[64,512]{1,0:T(8,128)S(1)} %get-tuple-element.38.refs_2_), channel_id=1, source_target_pairs={{0,8},{8,0},{16,24},{24,16},{1,9},{9,1},{17,25},{25,17},{2,10},{10... | collective-permute-start | bytes 393224 | tf_op jit(solution)/shard_map/ppermute | solution.py:303
  66.4 1.5 %collective-permute-start.28 = (f32[64,512]{1,0:T(8,128)S(1)}, f32[64,512]{1,0:T(8,128)S(1)}, u32[]{:S(2)}, u32[]{:S(2)}) collective-permute-start(f32[64,512]{1,0:T(8,128)S(1)} %get-tuple-element.39.refs_3_), channel_id=1, source_target_pairs={{0,8},{8,0},{16,24},{24,16},{1,9},{9,1},{17,25},{25,17},{2,10},{10... | collective-permute-start | bytes 393224 | tf_op jit(solution)/shard_map/ppermute | solution.py:303

commit v14 on v9

--- a/solution.py
+++ b/solution.py
@@ -341,7 +341,7 @@
             )
             late = along_y(late)
         if step > 0:
-            rest = bits_of(n_col)
+            rest = [*bits_of(n_x), *[bit for bit in bits_of(n_col) if bit > n_x], n_x]
         else:
             group, rest = [*bits_of(n_x), n_col // 2], [bit for bit in bits_of(n_col // 2) if bit >= n_x]
             ways = [0]

time: 74.3 us -> 74.3 us (level)
  no operation moved by 1% of the time
where the time goes in v14:
time: 74.3 us; the launch traced here: 74.1 us
  starting transfers between devices  32.2 us (43%)
  waiting for transfers between devices  25.6 us (34%)
  Pallas kernels  12.1 us (16%)
  local copies, waits for them, and re-layouts  3.32 us (4%)
  between operations  0.8 us (1%)
    ppermute x29, starting transfers between devices, swap(): return lax.ppermute(value, axis, [(i, i ^ distance) for i in range(n)])  32.2 us
    ppermute x29, waiting for transfers between devices, swap(): return lax.ppermute(value, axis, [(i, i ^ distance) for i in range(n)])  25.6 us
    pallas_call x14, Pallas kernels, call(): pl.pallas_call(kernel, out_shape=out_shape, in_specs=in_specs or [VMEM] *...  12.1 us
    unnamed x12, local copies, waits for them, and re-layouts  3.32 us
  transfers between devices with their start and end apart: 29, of which 16 were waited for; matrix products, arithmetic and copies ran while one was open for 0% of the time, Pallas kernels for 10%

profile of v14, /device:TPU:0, one launch (start us, length us, event | category | flops | bytes accessed | tf_op | source)
XLA Modules:
  0.0 74.1 jit_solution(13048267781012062151)
XLA Ops:
  0.6 0.0 copy-start.2
  0.6 1.0 %copy-done.2 = bf16[512,512]{1,0:T(8,128)(2,1)S(1)} copy-done((bf16[512,512]{1,0:T(8,128)(2,1)S(1)}, bf16[512,512]{1,0:T(8,128)(2,1)}, u32[]{:S(2)}) %copy-start.2) | copy-done | bytes 524312
  1.7 4.1 %collective-permute-start.3 = (f32[128,512]{1,0:T(8,128)S(1)}, f32[128,512]{1,0:T(8,128)S(1)}, u32[]{:S(2)}, u32[]{:S(2)}) collective-permute-start(f32[128,512]{1,0:T(8,128)S(1)} %shard_map.61), channel_id=1, source_target_pairs={{0,4},{1,5},{2,6},{3,7},{4,0},{5,1},{6,2},{7,3},{8,12},{9,13},{10,... | collective-permute-start | bytes 786440 | tf_op jit(solution)/shard_map/ppermute | solution.py:299
  5.8 1.5 %collective-permute-start.4 = (f32[128,512]{1,0:T(8,128)S(1)}, f32[128,512]{1,0:T(8,128)S(1)}, u32[]{:S(2)}, u32[]{:S(2)}) collective-permute-start(f32[128,512]{1,0:T(8,128)S(1)} %shard_map.61), channel_id=1, source_target_pairs={{0,1},{1,0},{2,3},{3,2},{4,5},{5,4},{6,7},{7,6},{8,9},{9,8},{10,11... | collective-permute-start | bytes 786440 | tf_op jit(solution)/shard_map/ppermute | solution.py:299
  7.3 1.6 %copy-done = bf16[2048,512]{1,0:T(8,128)(2,1)S(1)} copy-done((bf16[2048,512]{1,0:T(8,128)(2,1)S(1)}, bf16[2048,512]{1,0:T(8,128)(2,1)}, u32[]{:S(2)}) %copy-start) | copy-done | bytes 2097176
  8.9 0.7 copy-done.5
  9.6 1.9 %shard_map.59 = (f32[512,2048]{1,0:T(8,128)S(1)}, f32[16,128]{1,0:T(8,128)S(1)}, f32[4,128]{1,0:T(4,128)S(1)}) custom-call(bf16[512,512]{1,0:T(8,128)(2,1)S(1)} %copy-done.2, bf16[2048,512]{1,0:T(8,128)(2,1)S(1)} %copy-done, f32[4,128]{1,0:T(4,128)S(1)} %bitcast.5), custom_call_target="tpu_custom_call" | custom-call | tf_op jit(solution)/shard_map/pallas_call | solution.py:22
  11.5 0.1 collective-permute-start
  11.6 2.8 %collective-permute-start.1 = (f32[16,128]{1,0:T(8,128)S(1)}, f32[16,128]{1,0:T(8,128)S(1)}, u32[]{:S(2)}, u32[]{:S(2)}) collective-permute-start(f32[16,128]{1,0:T(8,128)S(1)} %get-tuple-element.23.refs_0_), channel_id=1, source_target_pairs={{0,4},{1,5},{2,6},{3,7},{4,0},{5,1},{6,2},{7,3},{8,12},{9,13},{10,... | collective-permute-start | bytes 24584 | tf_op jit(solution)/shard_map/ppermute | solution.py:299
  14.4 1.5 %collective-permute-start.2 = (f32[16,128]{1,0:T(8,128)S(1)}, f32[16,128]{1,0:T(8,128)S(1)}, u32[]{:S(2)}, u32[]{:S(2)}) collective-permute-start(f32[16,128]{1,0:T(8,128)S(1)} %get-tuple-element.23.refs_0_), channel_id=1, source_target_pairs={{0,1},{1,0},{2,3},{3,2},{4,5},{5,4},{6,7},{7,6},{8,9},{9,8},{10,11... | collective-permute-start | bytes 24584 | tf_op jit(solution)/shard_map/ppermute | solution.py:299
  15.9 3.4 %collective-permute-done.refs_1_ = f32[16,128]{1,0:T(8,128)S(1)} collective-permute-done((f32[16,128]{1,0:T(8,128)S(1)}, f32[16,128]{1,0:T(8,128)S(1)}, u32[]{:S(2)}, u32[]{:S(2)}) %collective-permute-start) | collective-permute-done | bytes 8224 | tf_op jit(solution)/shard_map/ppermute | solution.py:299
  19.3 0.0 collective-permute-done.4.refs_5_
  19.4 1.6 %collective-permute-start.10 = (f32[192,512]{1,0:T(8,128)S(1)}, f32[192,512]{1,0:T(8,128)S(1)}, u32[]{:S(2)}, u32[]{:S(2)}) collective-permute-start(f32[192,512]{1,0:T(8,128)S(1)} %get-tuple-element.26.refs_0_), channel_id=1, source_target_pairs={{0,16},{8,24},{16,0},{24,8},{1,17},{9,25},{17,1},{25,9},{2,18},{10... | collective-permute-start | bytes 1179656 | tf_op jit(solution)/shard_map/ppermute | solution.py:299
  21.0 0.6 collective-permute-start.9
  21.6 1.2 %collective-permute-start.5 = (f32[16,128]{1,0:T(8,128)S(1)}, f32[16,128]{1,0:T(8,128)S(1)}, u32[]{:S(2)}, u32[]{:S(2)}) collective-permute-start(f32[16,128]{1,0:T(8,128)S(1)} %get-tuple-element.24.refs_3_), channel_id=1, source_target_pairs={{0,2},{1,3},{2,0},{3,1},{4,6},{5,7},{6,4},{7,5},{8,10},{9,11},{10,... | collective-permute-start | bytes 24584 | tf_op jit(solution)/shard_map/ppermute | solution.py:299
  22.8 0.5 shard_map.60.refs_2_.sqx_ref
  23.3 2.0 %collective-permute-done.5.refs_4_ = f32[16,128]{1,0:T(8,128)S(1)} collective-permute-done((f32[16,128]{1,0:T(8,128)S(1)}, f32[16,128]{1,0:T(8,128)S(1)}, u32[]{:S(2)}, u32[]{:S(2)}) %collective-permute-start.5) | collective-permute-done | bytes 8224 | tf_op jit(solution)/shard_map/ppermute | solution.py:299
  25.3 1.0 %shard_map.63.refs_3_ = f32[4,128]{1,0:T(4,128)S(1)} custom-call(f32[512,2048]{1,0:T(8,128)S(1)} %get-tuple-element.21.refs_0_.tile_ref, f32[16,128]{1,0:T(8,128)S(1)} %bitcast.3, f32[16,128]{1,0:T(8,128)S(1)} %shard_map.60.refs_2_.sqx_ref, f32[16,128]{1,0:T(8,128)S(1)} %get-tuple-element.24.refs_3_, f32[16,128]{1,0:T(8,128)S(1)} %collective-permute-done.5.refs_4_), custom_call_target="tpu_custom_call" | custom-call | tf_op jit(solution)/shard_map/pallas_call | solution.py:22
  26.3 0.0 collective-permute-start.6
  26.3 0.6 collective-permute-start.7
  26.9 1.3 %collective-permute-start.8 = (f32[4,128]{1,0:T(4,128)S(1)}, f32[4,128]{1,0:T(4,128)S(1)}, u32[]{:S(2)}, u32[]{:S(2)}) collective-permute-start(f32[4,128]{1,0:T(4,128)S(1)} %shard_map.63.refs_3_), channel_id=1, source_target_pairs={{0,24},{8,16},{16,8},{24,0},{1,25},{9,17},{17,9},{25,1},{2,26},{10... | collective-permute-start | bytes 6152 | tf_op jit(solution)/shard_map/ppermute | solution.py:299
  28.2 0.0 collective-permute-done.6.refs_4_
  28.2 1.8 %collective-permute-done.7.refs_5_ = f32[4,128]{1,0:T(4,128)S(1)} collective-permute-done((f32[4,128]{1,0:T(4,128)S(1)}, f32[4,128]{1,0:T(4,128)S(1)}, u32[]{:S(2)}, u32[]{:S(2)}) %collective-permute-start.7) | collective-permute-done | bytes 2080 | tf_op jit(solution)/shard_map/ppermute | solution.py:299
  30.0 0.0 collective-permute-done.8.refs_6_
  30.0 1.1 %shard_map.64 = (f32[16,128]{1,0:T(8,128)S(1)}, f32[192,512]{1,0:T(8,128)S(1)}) custom-call(f32[512,2048]{1,0:T(8,128)S(1)} %get-tuple-element.21.refs_0_.tile_ref, f32[4,128]{1,0:T(4,128)S(1)} %bitcast.6, f32[4,128]{1,0:T(4,128)S(1)} %get-tuple-element.22.refs_2_, f32[4,128]{1,0:T(4,128)S(1)} %shard_map.63.refs_3_, ...), custom_call_target="tpu_custom_call" | custom-call | tf_op jit(solution)/shard_map/pallas_call | solution.py:22
  31.1 1.4 %collective-permute-start.11 = (f32[16,128]{1,0:T(8,128)S(1)}, f32[16,128]{1,0:T(8,128)S(1)}, u32[]{:S(2)}, u32[]{:S(2)}) collective-permute-start(f32[16,128]{1,0:T(8,128)S(1)} %get-tuple-element.27), channel_id=1, source_target_pairs={{0,1},{1,0},{2,3},{3,2},{4,5},{5,4},{6,7},{7,6},{8,9},{9,8},{10,11... | collective-permute-start | bytes 24584 | tf_op jit(solution)/shard_map/ppermute | solution.py:299
  32.6 1.4 %collective-permute-start.14 = (f32[192,512]{1,0:T(8,128)S(1)}, f32[192,512]{1,0:T(8,128)S(1)}, u32[]{:S(2)}, u32[]{:S(2)}) collective-permute-start(f32[192,512]{1,0:T(8,128)S(1)} %get-tuple-element.28.refs_2_), channel_id=1, source_target_pairs={{0,16},{8,24},{16,0},{24,8},{1,17},{9,25},{17,1},{25,9},{2,18},{10... | collective-permute-start | bytes 1179656 | tf_op jit(solution)/shard_map/ppermute | solution.py:299
  34.0 0.8 %collective-permute-done.11 = f32[16,128]{1,0:T(8,128)S(1)} collective-permute-done((f32[16,128]{1,0:T(8,128)S(1)}, f32[16,128]{1,0:T(8,128)S(1)}, u32[]{:S(2)}, u32[]{:S(2)}) %collective-permute-start.11) | collective-permute-done | bytes 8224 | tf_op jit(solution)/shard_map/ppermute | solution.py:299
  34.8 2.1 %collective-permute-start.12 = (f32[16,128]{1,0:T(8,128)S(1)}, f32[16,128]{1,0:T(8,128)S(1)}, u32[]{:S(2)}, u32[]{:S(2)}) collective-permute-start(f32[16,128]{1,0:T(8,128)S(1)} %multiply_add_fusion.1), channel_id=1, source_target_pairs={{0,4},{1,5},{2,6},{3,7},{4,0},{5,1},{6,2},{7,3},{8,12},{9,13},{10,... | collective-permute-start | bytes 24584 | tf_op jit(solution)/shard_map/ppermute | solution.py:299
  36.9 2.5 %collective-permute-done.12 = f32[16,128]{1,0:T(8,128)S(1)} collective-permute-done((f32[16,128]{1,0:T(8,128)S(1)}, f32[16,128]{1,0:T(8,128)S(1)}, u32[]{:S(2)}, u32[]{:S(2)}) %collective-permute-start.12) | collective-permute-done | bytes 8224 | tf_op jit(solution)/shard_map/ppermute | solution.py:299
  39.5 1.4 %collective-permute-start.13 = (f32[16,128]{1,0:T(8,128)S(1)}, f32[16,128]{1,0:T(8,128)S(1)}, u32[]{:S(2)}, u32[]{:S(2)}) collective-permute-start(f32[16,128]{1,0:T(8,128)S(1)} %multiply_add_fusion.refs_0_), channel_id=1, source_target_pairs={{0,2},{1,3},{2,0},{3,1},{4,6},{5,7},{6,4},{7,5},{8,10},{9,11},{10,... | collective-permute-start | bytes 24584 | tf_op jit(solution)/shard_map/ppermute | solution.py:299
  40.9 2.3 %collective-permute-done.13.refs_1_ = f32[16,128]{1,0:T(8,128)S(1)} collective-permute-done((f32[16,128]{1,0:T(8,128)S(1)}, f32[16,128]{1,0:T(8,128)S(1)}, u32[]{:S(2)}, u32[]{:S(2)}) %collective-permute-start.13) | collective-permute-done | bytes 8224 | tf_op jit(solution)/shard_map/ppermute | solution.py:299
  43.2 0.2 collective-permute-done.14.refs_2_.refs_3_
  43.4 1.9 %shard_map.65 = (f32[4,128]{1,0:T(4,128)S(1)}, f32[256,512]{1,0:T(8,128)S(1)}, f32[256,512]{1,0:T(8,128)S(1)}) custom-call(f32[512,2048]{1,0:T(8,128)S(1)} %get-tuple-element.21.refs_0_.tile_ref, bf16[2048,512]{1,0:T(8,128)(2,1)S(1)} %copy-done.1, f32[16,128]{1,0:T(8,128)S(1)} %bitcast.4, f32[16,128]{1,0:T(8,128)S(1)} %shard_map.60.refs_2_.sqx_ref, ...), custom_call_target="tpu_custom_call" | custom-call | tf_op jit(solution)/shard_map/pallas_call | solution.py:22
  45.3 0.0 copy-start.3
  45.3 0.1 collective-permute-start.15
  45.4 1.6 %collective-permute-start.18 = (f32[4,128]{1,0:T(4,128)S(1)}, f32[4,128]{1,0:T(4,128)S(1)}, u32[]{:S(2)}, u32[]{:S(2)}) collective-permute-start(f32[4,128]{1,0:T(4,128)S(1)} %get-tuple-element.31.lse_ref), channel_id=1, source_target_pairs={{0,24},{8,16},{16,8},{24,0},{1,25},{9,17},{17,9},{25,1},{2,26},{10... | collective-permute-start | bytes 6152 | tf_op jit(solution)/shard_map/ppermute | solution.py:299
  47.0 0.5 collective-permute-start.17
  47.5 0.9 %collective-permute-done.18 = f32[4,128]{1,0:T(4,128)S(1)} collective-permute-done((f32[4,128]{1,0:T(4,128)S(1)}, f32[4,128]{1,0:T(4,128)S(1)}, u32[]{:S(2)}, u32[]{:S(2)}) %collective-permute-start.18) | collective-permute-done | bytes 2080 | tf_op jit(solution)/shard_map/ppermute | solution.py:299
  48.5 2.1 %collective-permute-done.17 = f32[4,128]{1,0:T(4,128)S(1)} collective-permute-done((f32[4,128]{1,0:T(4,128)S(1)}, f32[4,128]{1,0:T(4,128)S(1)}, u32[]{:S(2)}, u32[]{:S(2)}) %collective-permute-start.17) | collective-permute-done | bytes 2080 | tf_op jit(solution)/shard_map/ppermute | solution.py:299
  50.6 0.4 shard_map.66
  51.0 0.1 collective-permute-start.19
  51.1 0.6 collective-permute-start.24
  51.7 2.6 %collective-permute-start.20 = (f32[4,128]{1,0:T(4,128)S(1)}, f32[4,128]{1,0:T(4,128)S(1)}, u32[]{:S(2)}, u32[]{:S(2)}) collective-permute-start(f32[4,128]{1,0:T(4,128)S(1)} %get-tuple-element.40.refs_5_), channel_id=1, source_target_pairs={{0,5},{1,4},{2,7},{3,6},{4,1},{5,0},{6,3},{7,2},{8,13},{9,12},{10,... | collective-permute-start | bytes 6152 | tf_op jit(solution)/shard_map/ppermute | solution.py:299
  54.4 0.9 %collective-permute-start.21 = (f32[4,128]{1,0:T(4,128)S(1)}, f32[4,128]{1,0:T(4,128)S(1)}, u32[]{:S(2)}, u32[]{:S(2)}) collective-permute-start(f32[4,128]{1,0:T(4,128)S(1)} %get-tuple-element.40.refs_5_), channel_id=1, source_target_pairs={{0,4},{1,5},{2,6},{3,7},{4,0},{5,1},{6,2},{7,3},{8,12},{9,13},{10,... | collective-permute-start | bytes 6152 | tf_op jit(solution)/shard_map/ppermute | solution.py:299
  55.3 0.8 %collective-permute-start.22 = (f32[4,128]{1,0:T(4,128)S(1)}, f32[4,128]{1,0:T(4,128)S(1)}, u32[]{:S(2)}, u32[]{:S(2)}) collective-permute-start(f32[4,128]{1,0:T(4,128)S(1)} %get-tuple-element.40.refs_5_), channel_id=1, source_target_pairs={{0,1},{1,0},{2,3},{3,2},{4,5},{5,4},{6,7},{7,6},{8,9},{9,8},{10,11... | collective-permute-start | bytes 6152 | tf_op jit(solution)/shard_map/ppermute | solution.py:299
  56.1 1.3 %shard_map.67 = (bf16[2048,512]{1,0:T(8,128)(2,1)S(1)}, f32[512,2048]{1,0:T(8,128)S(1)}) custom-call(bf16[2048,512]{1,0:T(8,128)(2,1)S(1)} %copy-done.1, bf16[512,512]{1,0:T(8,128)(2,1)S(1)} %copy-done.3, f32[3,2,128,512]{3,2,1,0:T(8,128)S(1)} %get-tuple-element.32.refs_2_, f32[3,2,128,512]{3,2,1,0:T(8,128)S(1)} %collective-permute-done.19.refs_3_), custom_call_target="tpu_custom_call" | custom-call | tf_op jit(solution)/shard_map/pallas_call | solution.py:22
  57.4 1.4 %collective-permute-done.21.refs_3_ = f32[4,128]{1,0:T(4,128)S(1)} collective-permute-done((f32[4,128]{1,0:T(4,128)S(1)}, f32[4,128]{1,0:T(4,128)S(1)}, u32[]{:S(2)}, u32[]{:S(2)}) %collective-permute-start.21) | collective-permute-done | bytes 2080 | tf_op jit(solution)/shard_map/ppermute | solution.py:299
  58.8 0.9 %shard_map.69 = f32[264,512]{1,0:T(8,128)S(1)} custom-call(f32[512,2048]{1,0:T(8,128)S(1)} %get-tuple-element.33.refs_0_, bf16[2048,512]{1,0:T(8,128)(2,1)S(1)} %get-tuple-element.34.refs_1_, f32[4,128]{1,0:T(4,128)S(1)} %collective-permute-done.20.refs_2_, f32[4,128]{1,0:T(4,128)S(1)} %collective-permute-done.21.refs_3_, ...), custom_call_target="tpu_custom_call" | custom-call | tf_op jit(solution)/shard_map/pallas_call | solution.py:22
  59.7 2.1 %collective-permute-start.23 = (f32[264,512]{1,0:T(8,128)S(1)}, f32[264,512]{1,0:T(8,128)S(1)}, u32[]{:S(2)}, u32[]{:S(2)}) collective-permute-start(f32[264,512]{1,0:T(8,128)S(1)} %shard_map.69), channel_id=1, source_target_pairs={{0,2},{1,3},{2,0},{3,1},{4,6},{5,7},{6,4},{7,5},{8,10},{9,11},{10,... | collective-permute-start | bytes 1622024 | tf_op jit(solution)/shard_map/ppermute | solution.py:299
  61.8 3.7 %collective-permute-done.24.two_ref = f32[256,512]{1,0:T(8,128)S(1)} collective-permute-done((f32[256,512]{1,0:T(8,128)S(1)}, f32[256,512]{1,0:T(8,128)S(1)}, u32[]{:S(2)}, u32[]{:S(2)}) %collective-permute-start.24) | collective-permute-done | bytes 524320 | tf_op jit(solution)/shard_map/ppermute | solution.py:299
  65.5 0.1 shard_map.71
  65.5 0.1 collective-permute-start.25
  65.6 0.5 collective-permute-start.26
  66.1 0.1 collective-permute-start.27
  66.2 0.4 collective-permute-start.28
  66.6 0.3 collective-permute-done.25.refs_4_
  66.9 0.2 collective-permute-done.26.refs_5_
  67.1 0.3 collective-permute-done.27.refs_6_
  67.4 0.2 collective-permute-done.28.refs_7_
  67.6 1.0 %shard_map.72 = f32[512,512]{1,0:T(8,128)} custom-call(f32[64,512]{1,0:T(8,128)S(1)} %get-tuple-element.36.refs_0_, f32[64,512]{1,0:T(8,128)S(1)} %get-tuple-element.37.refs_1_, f32[64,512]{1,0:T(8,128)S(1)} %get-tuple-element.38.refs_2_, f32[64,512]{1,0:T(8,128)S(1)} %get-tuple-element.39.refs_3_, f32[64,512]{1,0:T(8,128)S(1)} %collective-permute-done.25.refs_4_, ...), custom_call_target="tpu_custom_call" | custom-call | tf_op jit(solution)/shard_map/pallas_call | solution.py:22
  68.7 0.9 %shard_map.68.refs_0_ = f32[264,512]{1,0:T(8,128)S(1)} custom-call(f32[512,2048]{1,0:T(8,128)S(1)} %get-tuple-element.33.refs_0_, bf16[2048,512]{1,0:T(8,128)(2,1)S(1)} %get-tuple-element.34.refs_1_, f32[4,128]{1,0:T(4,128)S(1)} %collective-permute-done.20.refs_2_, f32[4,128]{1,0:T(4,128)S(1)} %collective-permute-done.21.refs_3_, ...), custom_call_target="tpu_custom_call" | custom-call | tf_op jit(solution)/shard_map/pallas_call | solution.py:22
  69.5 3.4 %collective-permute-done.23.refs_1_ = f32[264,512]{1,0:T(8,128)S(1)} collective-permute-done((f32[264,512]{1,0:T(8,128)S(1)}, f32[264,512]{1,0:T(8,128)S(1)}, u32[]{:S(2)}, u32[]{:S(2)}) %collective-permute-start.23) | collective-permute-done | bytes 540704 | tf_op jit(solution)/shard_map/ppermute | solution.py:299
  73.0 1.1 %shard_map.70 = f32[256,512]{1,0:T(8,128)} custom-call(f32[264,512]{1,0:T(8,128)S(1)} %shard_map.68.refs_0_, f32[264,512]{1,0:T(8,128)S(1)} %collective-permute-done.23.refs_1_), custom_call_target="tpu_custom_call" | custom-call | tf_op jit(solution)/shard_map/pallas_call | solution.py:22
  (23 shorter events, 0.2 us)
Async XLA Ops:
  0.6 1.0 %copy-start.2 = (bf16[512,512]{1,0:T(8,128)(2,1)S(1)}, bf16[512,512]{1,0:T(8,128)(2,1)}, u32[]{:S(2)}) copy-start(bf16[512,512]{1,0:T(8,128)(2,1)} %refs_1_.1) | copy-start | bytes 1572868
  1.7 17.6 %collective-permute-start.3 = (f32[128,512]{1,0:T(8,128)S(1)}, f32[128,512]{1,0:T(8,128)S(1)}, u32[]{:S(2)}, u32[]{:S(2)}) collective-permute-start(f32[128,512]{1,0:T(8,128)S(1)} %shard_map.61), channel_id=1, source_target_pairs={{0,4},{1,5},{2,6},{3,7},{4,0},{5,1},{6,2},{7,3},{8,12},{9,13},{10,... | collective-permute-start | bytes 786440 | tf_op jit(solution)/shard_map/ppermute | solution.py:299
  5.8 13.5 %collective-permute-start.4 = (f32[128,512]{1,0:T(8,128)S(1)}, f32[128,512]{1,0:T(8,128)S(1)}, u32[]{:S(2)}, u32[]{:S(2)}) collective-permute-start(f32[128,512]{1,0:T(8,128)S(1)} %shard_map.61), channel_id=1, source_target_pairs={{0,1},{1,0},{2,3},{3,2},{4,5},{5,4},{6,7},{7,6},{8,9},{9,8},{10,11... | collective-permute-start | bytes 786440 | tf_op jit(solution)/shard_map/ppermute | solution.py:299
  7.3 1.6 %copy-start = (bf16[2048,512]{1,0:T(8,128)(2,1)S(1)}, bf16[2048,512]{1,0:T(8,128)(2,1)}, u32[]{:S(2)}) copy-start(bf16[2048,512]{1,0:T(8,128)(2,1)} %refs_0_.1) | copy-start | bytes 6291460
  8.9 0.7 copy-start.5
  9.6 13.2 %copy-start.1 = (bf16[2048,512]{1,0:T(8,128)(2,1)S(1)}, bf16[2048,512]{1,0:T(8,128)(2,1)}, u32[]{:S(2)}) copy-start(bf16[2048,512]{1,0:T(8,128)(2,1)} %refs_0_.1) | copy-start | bytes 6291460
  9.6 15.7 %copy-start.4 = (f32[2048]{0:T(1024)S(1)}, f32[2048]{0:T(1024)}, u32[]{:S(2)}) copy-start(f32[2048]{0:T(1024)} %param.6) | copy-start | bytes 24580
  11.5 7.8 %collective-permute-start = (f32[16,128]{1,0:T(8,128)S(1)}, f32[16,128]{1,0:T(8,128)S(1)}, u32[]{:S(2)}, u32[]{:S(2)}) collective-permute-start(f32[16,128]{1,0:T(8,128)S(1)} %get-tuple-element.23.refs_0_), channel_id=1, source_target_pairs={{0,5},{1,4},{2,7},{3,6},{4,1},{5,0},{6,3},{7,2},{8,13},{9,12},{10,... | collective-permute-start | bytes 24584 | tf_op jit(solution)/shard_map/ppermute | solution.py:299
  11.6 7.7 %collective-permute-start.1 = (f32[16,128]{1,0:T(8,128)S(1)}, f32[16,128]{1,0:T(8,128)S(1)}, u32[]{:S(2)}, u32[]{:S(2)}) collective-permute-start(f32[16,128]{1,0:T(8,128)S(1)} %get-tuple-element.23.refs_0_), channel_id=1, source_target_pairs={{0,4},{1,5},{2,6},{3,7},{4,0},{5,1},{6,2},{7,3},{8,12},{9,13},{10,... | collective-permute-start | bytes 24584 | tf_op jit(solution)/shard_map/ppermute | solution.py:299
  14.4 4.9 %collective-permute-start.2 = (f32[16,128]{1,0:T(8,128)S(1)}, f32[16,128]{1,0:T(8,128)S(1)}, u32[]{:S(2)}, u32[]{:S(2)}) collective-permute-start(f32[16,128]{1,0:T(8,128)S(1)} %get-tuple-element.23.refs_0_), channel_id=1, source_target_pairs={{0,1},{1,0},{2,3},{3,2},{4,5},{5,4},{6,7},{7,6},{8,9},{9,8},{10,11... | collective-permute-start | bytes 24584 | tf_op jit(solution)/shard_map/ppermute | solution.py:299
  19.4 10.6 %collective-permute-start.10 = (f32[192,512]{1,0:T(8,128)S(1)}, f32[192,512]{1,0:T(8,128)S(1)}, u32[]{:S(2)}, u32[]{:S(2)}) collective-permute-start(f32[192,512]{1,0:T(8,128)S(1)} %get-tuple-element.26.refs_0_), channel_id=1, source_target_pairs={{0,16},{8,24},{16,0},{24,8},{1,17},{9,25},{17,1},{25,9},{2,18},{10... | collective-permute-start | bytes 1179656 | tf_op jit(solution)/shard_map/ppermute | solution.py:299
  21.0 9.0 %collective-permute-start.9 = (f32[128,512]{1,0:T(8,128)S(1)}, f32[128,512]{1,0:T(8,128)S(1)}, u32[]{:S(2)}, u32[]{:S(2)}) collective-permute-start(f32[128,512]{1,0:T(8,128)S(1)} %get-tuple-element.25.refs_7_), channel_id=1, source_target_pairs={{0,1},{1,0},{2,3},{3,2},{4,5},{5,4},{6,7},{7,6},{8,9},{9,8},{10,11... | collective-permute-start | bytes 786440 | tf_op jit(solution)/shard_map/ppermute | solution.py:299
  21.6 3.7 %collective-permute-start.5 = (f32[16,128]{1,0:T(8,128)S(1)}, f32[16,128]{1,0:T(8,128)S(1)}, u32[]{:S(2)}, u32[]{:S(2)}) collective-permute-start(f32[16,128]{1,0:T(8,128)S(1)} %get-tuple-element.24.refs_3_), channel_id=1, source_target_pairs={{0,2},{1,3},{2,0},{3,1},{4,6},{5,7},{6,4},{7,5},{8,10},{9,11},{10,... | collective-permute-start | bytes 24584 | tf_op jit(solution)/shard_map/ppermute | solution.py:299
  26.3 1.9 %collective-permute-start.6 = (f32[4,128]{1,0:T(4,128)S(1)}, f32[4,128]{1,0:T(4,128)S(1)}, u32[]{:S(2)}, u32[]{:S(2)}) collective-permute-start(f32[4,128]{1,0:T(4,128)S(1)} %shard_map.63.refs_3_), channel_id=1, source_target_pairs={{0,8},{8,0},{16,24},{24,16},{1,9},{9,1},{17,25},{25,17},{2,10},{10... | collective-permute-start | bytes 6152 | tf_op jit(solution)/shard_map/ppermute | solution.py:299
  26.3 3.7 %collective-permute-start.7 = (f32[4,128]{1,0:T(4,128)S(1)}, f32[4,128]{1,0:T(4,128)S(1)}, u32[]{:S(2)}, u32[]{:S(2)}) collective-permute-start(f32[4,128]{1,0:T(4,128)S(1)} %shard_map.63.refs_3_), channel_id=1, source_target_pairs={{0,16},{8,24},{16,0},{24,8},{1,17},{9,25},{17,1},{25,9},{2,18},{10... | collective-permute-start | bytes 6152 | tf_op jit(solution)/shard_map/ppermute | solution.py:299
  26.9 3.1 %collective-permute-start.8 = (f32[4,128]{1,0:T(4,128)S(1)}, f32[4,128]{1,0:T(4,128)S(1)}, u32[]{:S(2)}, u32[]{:S(2)}) collective-permute-start(f32[4,128]{1,0:T(4,128)S(1)} %shard_map.63.refs_3_), channel_id=1, source_target_pairs={{0,24},{8,16},{16,8},{24,0},{1,25},{9,17},{17,9},{25,1},{2,26},{10... | collective-permute-start | bytes 6152 | tf_op jit(solution)/shard_map/ppermute | solution.py:299
  31.1 3.7 %collective-permute-start.11 = (f32[16,128]{1,0:T(8,128)S(1)}, f32[16,128]{1,0:T(8,128)S(1)}, u32[]{:S(2)}, u32[]{:S(2)}) collective-permute-start(f32[16,128]{1,0:T(8,128)S(1)} %get-tuple-element.27), channel_id=1, source_target_pairs={{0,1},{1,0},{2,3},{3,2},{4,5},{5,4},{6,7},{7,6},{8,9},{9,8},{10,11... | collective-permute-start | bytes 24584 | tf_op jit(solution)/shard_map/ppermute | solution.py:299
  32.6 10.8 %collective-permute-start.14 = (f32[192,512]{1,0:T(8,128)S(1)}, f32[192,512]{1,0:T(8,128)S(1)}, u32[]{:S(2)}, u32[]{:S(2)}) collective-permute-start(f32[192,512]{1,0:T(8,128)S(1)} %get-tuple-element.28.refs_2_), channel_id=1, source_target_pairs={{0,16},{8,24},{16,0},{24,8},{1,17},{9,25},{17,1},{25,9},{2,18},{10... | collective-permute-start | bytes 1179656 | tf_op jit(solution)/shard_map/ppermute | solution.py:299
  34.8 4.6 %collective-permute-start.12 = (f32[16,128]{1,0:T(8,128)S(1)}, f32[16,128]{1,0:T(8,128)S(1)}, u32[]{:S(2)}, u32[]{:S(2)}) collective-permute-start(f32[16,128]{1,0:T(8,128)S(1)} %multiply_add_fusion.1), channel_id=1, source_target_pairs={{0,4},{1,5},{2,6},{3,7},{4,0},{5,1},{6,2},{7,3},{8,12},{9,13},{10,... | collective-permute-start | bytes 24584 | tf_op jit(solution)/shard_map/ppermute | solution.py:299
  39.5 3.7 %collective-permute-start.13 = (f32[16,128]{1,0:T(8,128)S(1)}, f32[16,128]{1,0:T(8,128)S(1)}, u32[]{:S(2)}, u32[]{:S(2)}) collective-permute-start(f32[16,128]{1,0:T(8,128)S(1)} %multiply_add_fusion.refs_0_), channel_id=1, source_target_pairs={{0,2},{1,3},{2,0},{3,1},{4,6},{5,7},{6,4},{7,5},{8,10},{9,11},{10,... | collective-permute-start | bytes 24584 | tf_op jit(solution)/shard_map/ppermute | solution.py:299
  45.3 10.8 %copy-start.3 = (bf16[512,512]{1,0:T(8,128)(2,1)S(1)}, bf16[512,512]{1,0:T(8,128)(2,1)}, u32[]{:S(2)}) copy-start(bf16[512,512]{1,0:T(8,128)(2,1)} %refs_1_.1) | copy-start | bytes 1572868
  45.3 5.3 %collective-permute-start.15 = (f32[256,512]{1,0:T(8,128)S(1)}, f32[256,512]{1,0:T(8,128)S(1)}, u32[]{:S(2)}, u32[]{:S(2)}) collective-permute-start(f32[256,512]{1,0:T(8,128)S(1)} %get-tuple-element.30), channel_id=1, source_target_pairs={{0,8},{8,0},{16,24},{24,16},{1,9},{9,1},{17,25},{25,17},{2,10},{10... | collective-permute-start | bytes 1572872 | tf_op jit(solution)/shard_map/ppermute | solution.py:299
  45.4 3.1 %collective-permute-start.18 = (f32[4,128]{1,0:T(4,128)S(1)}, f32[4,128]{1,0:T(4,128)S(1)}, u32[]{:S(2)}, u32[]{:S(2)}) collective-permute-start(f32[4,128]{1,0:T(4,128)S(1)} %get-tuple-element.31.lse_ref), channel_id=1, source_target_pairs={{0,24},{8,16},{16,8},{24,0},{1,25},{9,17},{17,9},{25,1},{2,26},{10... | collective-permute-start | bytes 6152 | tf_op jit(solution)/shard_map/ppermute | solution.py:299
  47.0 3.6 %collective-permute-start.17 = (f32[4,128]{1,0:T(4,128)S(1)}, f32[4,128]{1,0:T(4,128)S(1)}, u32[]{:S(2)}, u32[]{:S(2)}) collective-permute-start(f32[4,128]{1,0:T(4,128)S(1)} %get-tuple-element.31.lse_ref), channel_id=1, source_target_pairs={{0,16},{8,24},{16,0},{24,8},{1,17},{9,25},{17,1},{25,9},{2,18},{10... | collective-permute-start | bytes 6152 | tf_op jit(solution)/shard_map/ppermute | solution.py:299
  47.5 3.1 %collective-permute-start.16 = (f32[4,128]{1,0:T(4,128)S(1)}, f32[4,128]{1,0:T(4,128)S(1)}, u32[]{:S(2)}, u32[]{:S(2)}) collective-permute-start(f32[4,128]{1,0:T(4,128)S(1)} %get-tuple-element.31.lse_ref), channel_id=1, source_target_pairs={{0,8},{8,0},{16,24},{24,16},{1,9},{9,1},{17,25},{25,17},{2,10},{10... | collective-permute-start | bytes 6152 | tf_op jit(solution)/shard_map/ppermute | solution.py:299
  51.0 5.1 %collective-permute-start.19 = (f32[3,2,128,512]{3,2,1,0:T(8,128)S(1)}, f32[3,2,128,512]{3,2,1,0:T(8,128)S(1)}, u32[]{:S(2)}, u32[]{:S(2)}) collective-permute-start(f32[3,2,128,512]{3,2,1,0:T(8,128)S(1)} %get-tuple-element.32.refs_2_), channel_id=1, source_target_pairs={{0,8},{8,0},{16,24},{24,16},{1,9},{9,1},{17,25},{25,17},{2,10},{10... | collective-permute-start | bytes 4718600 | tf_op jit(solution)/shard_map/ppermute | solution.py:299
  51.1 14.3 %collective-permute-start.24 = (f32[256,512]{1,0:T(8,128)S(1)}, f32[256,512]{1,0:T(8,128)S(1)}, u32[]{:S(2)}, u32[]{:S(2)}) collective-permute-start(f32[256,512]{1,0:T(8,128)S(1)} %get-tuple-element.35.one_ref), channel_id=1, source_target_pairs={{0,16},{8,24},{16,0},{24,8},{1,17},{9,25},{17,1},{25,9},{2,18},{10... | collective-permute-start | bytes 1572872 | tf_op jit(solution)/shard_map/ppermute | solution.py:299
  51.7 5.7 %collective-permute-start.20 = (f32[4,128]{1,0:T(4,128)S(1)}, f32[4,128]{1,0:T(4,128)S(1)}, u32[]{:S(2)}, u32[]{:S(2)}) collective-permute-start(f32[4,128]{1,0:T(4,128)S(1)} %get-tuple-element.40.refs_5_), channel_id=1, source_target_pairs={{0,5},{1,4},{2,7},{3,6},{4,1},{5,0},{6,3},{7,2},{8,13},{9,12},{10,... | collective-permute-start | bytes 6152 | tf_op jit(solution)/shard_map/ppermute | solution.py:299
  54.4 4.5 %collective-permute-start.21 = (f32[4,128]{1,0:T(4,128)S(1)}, f32[4,128]{1,0:T(4,128)S(1)}, u32[]{:S(2)}, u32[]{:S(2)}) collective-permute-start(f32[4,128]{1,0:T(4,128)S(1)} %get-tuple-element.40.refs_5_), channel_id=1, source_target_pairs={{0,4},{1,5},{2,6},{3,7},{4,0},{5,1},{6,2},{7,3},{8,12},{9,13},{10,... | collective-permute-start | bytes 6152 | tf_op jit(solution)/shard_map/ppermute | solution.py:299
  55.3 3.6 %collective-permute-start.22 = (f32[4,128]{1,0:T(4,128)S(1)}, f32[4,128]{1,0:T(4,128)S(1)}, u32[]{:S(2)}, u32[]{:S(2)}) collective-permute-start(f32[4,128]{1,0:T(4,128)S(1)} %get-tuple-element.40.refs_5_), channel_id=1, source_target_pairs={{0,1},{1,0},{2,3},{3,2},{4,5},{5,4},{6,7},{7,6},{8,9},{9,8},{10,11... | collective-permute-start | bytes 6152 | tf_op jit(solution)/shard_map/ppermute | solution.py:299
  59.7 13.3 %collective-permute-start.23 = (f32[264,512]{1,0:T(8,128)S(1)}, f32[264,512]{1,0:T(8,128)S(1)}, u32[]{:S(2)}, u32[]{:S(2)}) collective-permute-start(f32[264,512]{1,0:T(8,128)S(1)} %shard_map.69), channel_id=1, source_target_pairs={{0,2},{1,3},{2,0},{3,1},{4,6},{5,7},{6,4},{7,5},{8,10},{9,11},{10,... | collective-permute-start | bytes 1622024 | tf_op jit(solution)/shard_map/ppermute | solution.py:299
  65.5 1.4 %collective-permute-start.25 = (f32[64,512]{1,0:T(8,128)S(1)}, f32[64,512]{1,0:T(8,128)S(1)}, u32[]{:S(2)}, u32[]{:S(2)}) collective-permute-start(f32[64,512]{1,0:T(8,128)S(1)} %get-tuple-element.36.refs_0_), channel_id=1, source_target_pairs={{0,8},{8,0},{16,24},{24,16},{1,9},{9,1},{17,25},{25,17},{2,10},{10... | collective-permute-start | bytes 393224 | tf_op jit(solution)/shard_map/ppermute | solution.py:299
  65.6 1.5 %collective-permute-start.26 = (f32[64,512]{1,0:T(8,128)S(1)}, f32[64,512]{1,0:T(8,128)S(1)}, u32[]{:S(2)}, u32[]{:S(2)}) collective-permute-start(f32[64,512]{1,0:T(8,128)S(1)} %get-tuple-element.37.refs_1_), channel_id=1, source_target_pairs={{0,8},{8,0},{16,24},{24,16},{1,9},{9,1},{17,25},{25,17},{2,10},{10... | collective-permute-start | bytes 393224 | tf_op jit(solution)/shard_map/ppermute | solution.py:299
  66.1 1.3 %collective-permute-start.27 = (f32[64,512]{1,0:T(8,128)S(1)}, f32[64,512]{1,0:T(8,128)S(1)}, u32[]{:S(2)}, u32[]{:S(2)}) collective-permute-start(f32[64,512]{1,0:T(8,128)S(1)} %get-tuple-element.38.refs_2_), channel_id=1, source_target_pairs={{0,8},{8,0},{16,24},{24,16},{1,9},{9,1},{17,25},{25,17},{2,10},{10... | collective-permute-start | bytes 393224 | tf_op jit(solution)/shard_map/ppermute | solution.py:299
  66.2 1.5 %collective-permute-start.28 = (f32[64,512]{1,0:T(8,128)S(1)}, f32[64,512]{1,0:T(8,128)S(1)}, u32[]{:S(2)}, u32[]{:S(2)}) collective-permute-start(f32[64,512]{1,0:T(8,128)S(1)} %get-tuple-element.39.refs_3_), channel_id=1, source_target_pairs={{0,8},{8,0},{16,24},{24,16},{1,9},{9,1},{17,25},{25,17},{2,10},{10... | collective-permute-start | bytes 393224 | tf_op jit(solution)/shard_map/ppermute | solution.py:299

commit v15 on v8

--- a/solution.py
+++ b/solution.py
@@ -165,15 +165,14 @@
     n_rows = mine_ref.shape[0] // LANES
     core = lax.axis_index("row") % 2
     for out_ref, place in ((sent_ref, 1 - core), (mine_ref, core)):
-        columns, totals, weights = [], [], []
+        columns = []
         for j in range(n_rows):
             at = pl.ds(pl.multiple_of((place * n_rows + j) * LANES, LANES), LANES)
             peak, total, exps = over_sources(tile_ref, at, bias)
             columns.append(peak + jnp.log2(total))
-            totals.append(total)
-            weights.append(jnp.concatenate([block.astype(jnp.bfloat16) for block in exps], axis=1))
-        mean = jnp.dot(jnp.concatenate(weights, axis=0), x, preferred_element_type=jnp.float32)
-        out_ref[...] = mean * (1.0 / jnp.concatenate(totals, axis=0))
+            weights = jnp.concatenate([block.astype(jnp.bfloat16) for block in exps], axis=1)
+            mean = jnp.dot(weights, x, preferred_element_type=jnp.float32)
+            out_ref[pl.ds(j * LANES, LANES), :] = mean * (1.0 / total)
         lse_ref[pl.ds(place * n_rows, n_rows), :] = to_dense(columns)
 
 
@@ -341,13 +340,16 @@
             )
             late = along_y(late)
         if step > 0:
-            for distance in bits_of(2 * n_x):
-                lse = merge_all([lse, swap(lse, "col", distance)])
+            rest = bits_of(n_col)
         else:
-            near = [lse] + [swap(lse, "col", distance) for distance in range(2 * n_x - 1, 0, -1)]
+            group, rest = [*bits_of(n_x), n_col // 2], [bit for bit in bits_of(n_col // 2) if bit >= n_x]
+            ways = [0]
+            for bit in group:
+                ways += [way | bit for way in ways]
+            near = [lse] + [swap(lse, "col", way) for way in ways[:0:-1]]
             far = [k for k in pieces if k > 0]
             lse, early, *copies = call(
-                lambda *refs: merge_kernel(2 * n_x, *refs),
+                lambda *refs: merge_kernel(len(ways), *refs),
                 (src_dense, f32(part.shape[0] + cut, width), *(part,) * len(far)),
                 *near, *[pieces[k] for k in far], early,
             )
@@ -355,9 +357,9 @@
             pieces |= dict(zip(far, copies))
             for bit in bits_of(n_x)[::-1]:
                 pieces |= {k ^ bit: swap(piece, "col", bit) for k, piece in pieces.items() if k ^ bit != 1}
-        for distance in [bit for bit in bits_of(n_col) if bit > n_x][:-1]:
+        for distance in rest[:-1]:
             lse = merge_all([lse, swap(lse, "col", distance)])
-        parts = [lse, swap(lse, "col", n_col // 2)]
+        parts = [lse, swap(lse, "col", rest[-1])]
         if step < ITERS - 1:
             lse = call(lambda *refs: sources_kernel(2, *refs), tgt_dense, tile, ls, sqx, *parts)
         else:

time: 74.2 us -> 73.8 us (level)
  waiting for transfers between devices: 28.5 us -> 24.8 us
  starting transfers between devices: 29 us -> 32.4 us
    ppermute x29, waiting for transfers between devices: 28.5 us -> 24.8 us  [swap(): return lax.ppermute(value, axis, [(i, i ^ distance) for i in range(n)])]
    ppermute x29, starting transfers between devices: 29 us -> 32.4 us  [swap(): return lax.ppermute(value, axis, [(i, i ^ distance) for i in range(n)])]
  transfers between devices with their start and end apart: 29 -> 29, of which waited for: 17 -> 16; matrix products, arithmetic and copies ran while one was open for 0% -> 0% of each run, Pallas kernels for 11% -> 11%
where the time goes in v15:
time: 73.8 us; the launch traced here: 73.6 us
  starting transfers between devices  32.4 us (44%)
  waiting for transfers between devices  24.8 us (34%)
  Pallas kernels  12.2 us (17%)
  local copies, waits for them, and re-layouts  3.32 us (4%)
  between operations  0.79 us (1%)
    ppermute x29, starting transfers between devices, swap(): return lax.ppermute(value, axis, [(i, i ^ distance) for i in range(n)])  32.4 us
    ppermute x29, waiting for transfers between devices, swap(): return lax.ppermute(value, axis, [(i, i ^ distance) for i in range(n)])  24.8 us
    pallas_call x14, Pallas kernels, call(): pl.pallas_call(kernel, out_shape=out_shape, in_specs=in_specs or [VMEM] *...  12.2 us
    unnamed x12, local copies, waits for them, and re-layouts  3.32 us
  transfers between devices with their start and end apart: 29, of which 16 were waited for; matrix products, arithmetic and copies ran while one was open for 0% of the time, Pallas kernels for 11%

profile of v15, /device:TPU:0, one launch (start us, length us, event | category | flops | bytes accessed | tf_op | source)
XLA Modules:
  0.0 73.6 jit_solution(18178852736643505846)
XLA Ops:
  0.6 0.0 copy-start.2
  0.6 1.0 %copy-done.2 = bf16[512,512]{1,0:T(8,128)(2,1)S(1)} copy-done((bf16[512,512]{1,0:T(8,128)(2,1)S(1)}, bf16[512,512]{1,0:T(8,128)(2,1)}, u32[]{:S(2)}) %copy-start.2) | copy-done | bytes 524312
  1.7 4.1 %collective-permute-start.3 = (f32[128,512]{1,0:T(8,128)S(1)}, f32[128,512]{1,0:T(8,128)S(1)}, u32[]{:S(2)}, u32[]{:S(2)}) collective-permute-start(f32[128,512]{1,0:T(8,128)S(1)} %shard_map.61), channel_id=1, source_target_pairs={{0,4},{1,5},{2,6},{3,7},{4,0},{5,1},{6,2},{7,3},{8,12},{9,13},{10,... | collective-permute-start | bytes 786440 | tf_op jit(solution)/shard_map/ppermute | solution.py:298
  5.8 1.5 %collective-permute-start.4 = (f32[128,512]{1,0:T(8,128)S(1)}, f32[128,512]{1,0:T(8,128)S(1)}, u32[]{:S(2)}, u32[]{:S(2)}) collective-permute-start(f32[128,512]{1,0:T(8,128)S(1)} %shard_map.61), channel_id=1, source_target_pairs={{0,1},{1,0},{2,3},{3,2},{4,5},{5,4},{6,7},{7,6},{8,9},{9,8},{10,11... | collective-permute-start | bytes 786440 | tf_op jit(solution)/shard_map/ppermute | solution.py:298
  7.3 1.6 %copy-done = bf16[2048,512]{1,0:T(8,128)(2,1)S(1)} copy-done((bf16[2048,512]{1,0:T(8,128)(2,1)S(1)}, bf16[2048,512]{1,0:T(8,128)(2,1)}, u32[]{:S(2)}) %copy-start) | copy-done | bytes 2097176
  8.9 0.7 copy-done.5
  9.6 1.9 %shard_map.59 = (f32[512,2048]{1,0:T(8,128)S(1)}, f32[16,128]{1,0:T(8,128)S(1)}, f32[4,128]{1,0:T(4,128)S(1)}) custom-call(bf16[512,512]{1,0:T(8,128)(2,1)S(1)} %copy-done.2, bf16[2048,512]{1,0:T(8,128)(2,1)S(1)} %copy-done, f32[4,128]{1,0:T(4,128)S(1)} %bitcast.5), custom_call_target="tpu_custom_call" | custom-call | tf_op jit(solution)/shard_map/pallas_call | solution.py:22
  11.5 0.1 collective-permute-start
  11.6 2.8 %collective-permute-start.1 = (f32[16,128]{1,0:T(8,128)S(1)}, f32[16,128]{1,0:T(8,128)S(1)}, u32[]{:S(2)}, u32[]{:S(2)}) collective-permute-start(f32[16,128]{1,0:T(8,128)S(1)} %get-tuple-element.22.refs_0_), channel_id=1, source_target_pairs={{0,4},{1,5},{2,6},{3,7},{4,0},{5,1},{6,2},{7,3},{8,12},{9,13},{10,... | collective-permute-start | bytes 24584 | tf_op jit(solution)/shard_map/ppermute | solution.py:298
  14.4 1.5 %collective-permute-start.2 = (f32[16,128]{1,0:T(8,128)S(1)}, f32[16,128]{1,0:T(8,128)S(1)}, u32[]{:S(2)}, u32[]{:S(2)}) collective-permute-start(f32[16,128]{1,0:T(8,128)S(1)} %get-tuple-element.22.refs_0_), channel_id=1, source_target_pairs={{0,1},{1,0},{2,3},{3,2},{4,5},{5,4},{6,7},{7,6},{8,9},{9,8},{10,11... | collective-permute-start | bytes 24584 | tf_op jit(solution)/shard_map/ppermute | solution.py:298
  15.9 3.4 %collective-permute-done.refs_1_ = f32[16,128]{1,0:T(8,128)S(1)} collective-permute-done((f32[16,128]{1,0:T(8,128)S(1)}, f32[16,128]{1,0:T(8,128)S(1)}, u32[]{:S(2)}, u32[]{:S(2)}) %collective-permute-start) | collective-permute-done | bytes 8224 | tf_op jit(solution)/shard_map/ppermute | solution.py:298
  19.3 0.0 collective-permute-done.1.refs_2_
  19.4 1.6 %collective-permute-start.10 = (f32[192,512]{1,0:T(8,128)S(1)}, f32[192,512]{1,0:T(8,128)S(1)}, u32[]{:S(2)}, u32[]{:S(2)}) collective-permute-start(f32[192,512]{1,0:T(8,128)S(1)} %get-tuple-element.25.refs_6_), channel_id=1, source_target_pairs={{0,16},{8,24},{16,0},{24,8},{1,17},{9,25},{17,1},{25,9},{2,18},{10... | collective-permute-start | bytes 1179656 | tf_op jit(solution)/shard_map/ppermute | solution.py:298
  21.0 0.6 collective-permute-start.9
  21.6 1.2 %collective-permute-start.5 = (f32[16,128]{1,0:T(8,128)S(1)}, f32[16,128]{1,0:T(8,128)S(1)}, u32[]{:S(2)}, u32[]{:S(2)}) collective-permute-start(f32[16,128]{1,0:T(8,128)S(1)} %get-tuple-element.23.refs_3_), channel_id=1, source_target_pairs={{0,2},{1,3},{2,0},{3,1},{4,6},{5,7},{6,4},{7,5},{8,10},{9,11},{10,... | collective-permute-start | bytes 24584 | tf_op jit(solution)/shard_map/ppermute | solution.py:298
  22.8 0.5 shard_map.60.refs_2_.refs_3_
  23.3 2.0 %collective-permute-done.5.refs_4_ = f32[16,128]{1,0:T(8,128)S(1)} collective-permute-done((f32[16,128]{1,0:T(8,128)S(1)}, f32[16,128]{1,0:T(8,128)S(1)}, u32[]{:S(2)}, u32[]{:S(2)}) %collective-permute-start.5) | collective-permute-done | bytes 8224 | tf_op jit(solution)/shard_map/ppermute | solution.py:298
  25.3 1.0 %shard_map.63.refs_3_ = f32[4,128]{1,0:T(4,128)S(1)} custom-call(f32[512,2048]{1,0:T(8,128)S(1)} %get-tuple-element.20.refs_0_, f32[16,128]{1,0:T(8,128)S(1)} %bitcast.3, f32[16,128]{1,0:T(8,128)S(1)} %shard_map.60.refs_2_.refs_3_, f32[16,128]{1,0:T(8,128)S(1)} %get-tuple-element.23.refs_3_, f32[16,128]{1,0:T(8,128)S(1)} %collective-permute-done.5.refs_4_), custom_call_target="tpu_custom_call" | custom-call | tf_op jit(solution)/shard_map/pallas_call | solution.py:22
  26.3 0.0 collective-permute-start.6
  26.3 0.6 collective-permute-start.7
  26.9 1.3 %collective-permute-start.8 = (f32[4,128]{1,0:T(4,128)S(1)}, f32[4,128]{1,0:T(4,128)S(1)}, u32[]{:S(2)}, u32[]{:S(2)}) collective-permute-start(f32[4,128]{1,0:T(4,128)S(1)} %shard_map.63.refs_3_), channel_id=1, source_target_pairs={{0,24},{8,16},{16,8},{24,0},{1,25},{9,17},{17,9},{25,1},{2,26},{10... | collective-permute-start | bytes 6152 | tf_op jit(solution)/shard_map/ppermute | solution.py:298
  28.2 1.8 %collective-permute-done.7.refs_5_ = f32[4,128]{1,0:T(4,128)S(1)} collective-permute-done((f32[4,128]{1,0:T(4,128)S(1)}, f32[4,128]{1,0:T(4,128)S(1)}, u32[]{:S(2)}, u32[]{:S(2)}) %collective-permute-start.7) | collective-permute-done | bytes 2080 | tf_op jit(solution)/shard_map/ppermute | solution.py:298
  30.0 1.1 %shard_map.64 = (f32[16,128]{1,0:T(8,128)S(1)}, f32[192,512]{1,0:T(8,128)S(1)}) custom-call(f32[512,2048]{1,0:T(8,128)S(1)} %get-tuple-element.20.refs_0_, f32[4,128]{1,0:T(4,128)S(1)} %bitcast.6, f32[4,128]{1,0:T(4,128)S(1)} %get-tuple-element.21.refs_2_, f32[4,128]{1,0:T(4,128)S(1)} %shard_map.63.refs_3_, f32[4,128]{1,0:T(4,128)S(1)} %collective-permute-done.6.refs_4_, ...), custom_call_target="tpu_custom_call" | custom-call | tf_op jit(solution)/shard_map/pallas_call | solution.py:22
  31.1 1.4 %collective-permute-start.11 = (f32[16,128]{1,0:T(8,128)S(1)}, f32[16,128]{1,0:T(8,128)S(1)}, u32[]{:S(2)}, u32[]{:S(2)}) collective-permute-start(f32[16,128]{1,0:T(8,128)S(1)} %get-tuple-element.26), channel_id=1, source_target_pairs={{0,1},{1,0},{2,3},{3,2},{4,5},{5,4},{6,7},{7,6},{8,9},{9,8},{10,11... | collective-permute-start | bytes 24584 | tf_op jit(solution)/shard_map/ppermute | solution.py:298
  32.6 1.4 %collective-permute-start.14 = (f32[192,512]{1,0:T(8,128)S(1)}, f32[192,512]{1,0:T(8,128)S(1)}, u32[]{:S(2)}, u32[]{:S(2)}) collective-permute-start(f32[192,512]{1,0:T(8,128)S(1)} %get-tuple-element.27.refs_8_), channel_id=1, source_target_pairs={{0,16},{8,24},{16,0},{24,8},{1,17},{9,25},{17,1},{25,9},{2,18},{10... | collective-permute-start | bytes 1179656 | tf_op jit(solution)/shard_map/ppermute | solution.py:298
  34.0 0.8 %collective-permute-done.11 = f32[16,128]{1,0:T(8,128)S(1)} collective-permute-done((f32[16,128]{1,0:T(8,128)S(1)}, f32[16,128]{1,0:T(8,128)S(1)}, u32[]{:S(2)}, u32[]{:S(2)}) %collective-permute-start.11) | collective-permute-done | bytes 8224 | tf_op jit(solution)/shard_map/ppermute | solution.py:298
  34.8 1.2 %collective-permute-start.12 = (f32[16,128]{1,0:T(8,128)S(1)}, f32[16,128]{1,0:T(8,128)S(1)}, u32[]{:S(2)}, u32[]{:S(2)}) collective-permute-start(f32[16,128]{1,0:T(8,128)S(1)} %multiply_add_fusion.1), channel_id=1, source_target_pairs={{0,2},{1,3},{2,0},{3,1},{4,6},{5,7},{6,4},{7,5},{8,10},{9,11},{10,... | collective-permute-start | bytes 24584 | tf_op jit(solution)/shard_map/ppermute | solution.py:298
  36.1 2.5 %collective-permute-done.12 = f32[16,128]{1,0:T(8,128)S(1)} collective-permute-done((f32[16,128]{1,0:T(8,128)S(1)}, f32[16,128]{1,0:T(8,128)S(1)}, u32[]{:S(2)}, u32[]{:S(2)}) %collective-permute-start.12) | collective-permute-done | bytes 8224 | tf_op jit(solution)/shard_map/ppermute | solution.py:298
  38.6 0.0 copy-start.3
  38.6 2.3 %collective-permute-start.13 = (f32[16,128]{1,0:T(8,128)S(1)}, f32[16,128]{1,0:T(8,128)S(1)}, u32[]{:S(2)}, u32[]{:S(2)}) collective-permute-start(f32[16,128]{1,0:T(8,128)S(1)} %multiply_add_fusion.refs_4_), channel_id=1, source_target_pairs={{0,4},{1,5},{2,6},{3,7},{4,0},{5,1},{6,2},{7,3},{8,12},{9,13},{10,... | collective-permute-start | bytes 24584 | tf_op jit(solution)/shard_map/ppermute | solution.py:298
  40.9 2.3 %collective-permute-done.13.refs_5_ = f32[16,128]{1,0:T(8,128)S(1)} collective-permute-done((f32[16,128]{1,0:T(8,128)S(1)}, f32[16,128]{1,0:T(8,128)S(1)}, u32[]{:S(2)}, u32[]{:S(2)}) %collective-permute-start.13) | collective-permute-done | bytes 8224 | tf_op jit(solution)/shard_map/ppermute | solution.py:298
  43.2 0.2 collective-permute-done.14.refs_9_
  43.4 2.0 %shard_map.65 = (f32[4,128]{1,0:T(4,128)S(1)}, f32[256,512]{1,0:T(8,128)S(1)}, f32[256,512]{1,0:T(8,128)S(1)}, f32[3,2,128,512]{3,2,1,0:T(8,128)S(1)}) custom-call(f32[512,2048]{1,0:T(8,128)S(1)} %get-tuple-element.20.refs_0_, bf16[2048,512]{1,0:T(8,128)(2,1)S(1)} %copy-done.1, f32[16,128]{1,0:T(8,128)S(1)} %bitcast.4, ...), custom_call_target="tpu_custom_call" | custom-call | tf_op jit(solution)/shard_map/pallas_call | solution.py:22
  45.4 0.1 collective-permute-start.15
  45.5 0.5 collective-permute-start.23
  46.0 1.2 %collective-permute-start.18 = (f32[4,128]{1,0:T(4,128)S(1)}, f32[4,128]{1,0:T(4,128)S(1)}, u32[]{:S(2)}, u32[]{:S(2)}) collective-permute-start(f32[4,128]{1,0:T(4,128)S(1)} %get-tuple-element.31.lse_ref), channel_id=1, source_target_pairs={{0,24},{8,16},{16,8},{24,0},{1,25},{9,17},{17,9},{25,1},{2,26},{10... | collective-permute-start | bytes 6152 | tf_op jit(solution)/shard_map/ppermute | solution.py:298
  47.2 0.5 collective-permute-start.17
  47.7 0.2 collective-permute-start.16
  47.9 1.1 %collective-permute-done.18 = f32[4,128]{1,0:T(4,128)S(1)} collective-permute-done((f32[4,128]{1,0:T(4,128)S(1)}, f32[4,128]{1,0:T(4,128)S(1)}, u32[]{:S(2)}, u32[]{:S(2)}) %collective-permute-start.18) | collective-permute-done | bytes 2080 | tf_op jit(solution)/shard_map/ppermute | solution.py:298
  49.0 1.8 %collective-permute-done.17 = f32[4,128]{1,0:T(4,128)S(1)} collective-permute-done((f32[4,128]{1,0:T(4,128)S(1)}, f32[4,128]{1,0:T(4,128)S(1)}, u32[]{:S(2)}, u32[]{:S(2)}) %collective-permute-start.17) | collective-permute-done | bytes 2080 | tf_op jit(solution)/shard_map/ppermute | solution.py:298
  50.8 0.0 collective-permute-done.16.came_lse_ref
  50.8 0.3 shard_map.70.one_ref
  51.1 0.6 collective-permute-start.24
  51.7 2.7 %collective-permute-start.19 = (f32[4,128]{1,0:T(4,128)S(1)}, f32[4,128]{1,0:T(4,128)S(1)}, u32[]{:S(2)}, u32[]{:S(2)}) collective-permute-start(f32[4,128]{1,0:T(4,128)S(1)} %get-tuple-element.38.refs_5_), channel_id=1, source_target_pairs={{0,5},{1,4},{2,7},{3,6},{4,1},{5,0},{6,3},{7,2},{8,13},{9,12},{10,... | collective-permute-start | bytes 6152 | tf_op jit(solution)/shard_map/ppermute | solution.py:298
  54.4 0.9 %collective-permute-start.20 = (f32[4,128]{1,0:T(4,128)S(1)}, f32[4,128]{1,0:T(4,128)S(1)}, u32[]{:S(2)}, u32[]{:S(2)}) collective-permute-start(f32[4,128]{1,0:T(4,128)S(1)} %get-tuple-element.38.refs_5_), channel_id=1, source_target_pairs={{0,4},{1,5},{2,6},{3,7},{4,0},{5,1},{6,2},{7,3},{8,12},{9,13},{10,... | collective-permute-start | bytes 6152 | tf_op jit(solution)/shard_map/ppermute | solution.py:298
  55.2 0.8 %collective-permute-start.21 = (f32[4,128]{1,0:T(4,128)S(1)}, f32[4,128]{1,0:T(4,128)S(1)}, u32[]{:S(2)}, u32[]{:S(2)}) collective-permute-start(f32[4,128]{1,0:T(4,128)S(1)} %get-tuple-element.38.refs_5_), channel_id=1, source_target_pairs={{0,1},{1,0},{2,3},{3,2},{4,5},{5,4},{6,7},{7,6},{8,9},{9,8},{10,11... | collective-permute-start | bytes 6152 | tf_op jit(solution)/shard_map/ppermute | solution.py:298
  56.1 1.3 %shard_map.66 = (bf16[2048,512]{1,0:T(8,128)(2,1)S(1)}, f32[512,2048]{1,0:T(8,128)S(1)}) custom-call(bf16[2048,512]{1,0:T(8,128)(2,1)S(1)} %copy-done.1, bf16[512,512]{1,0:T(8,128)(2,1)S(1)} %copy-done.3, f32[3,2,128,512]{3,2,1,0:T(8,128)S(1)} %get-tuple-element.28.refs_2_, f32[3,2,128,512]{3,2,1,0:T(8,128)S(1)} %collective-permute-done.15.refs_3_), custom_call_target="tpu_custom_call" | custom-call | tf_op jit(solution)/shard_map/pallas_call | solution.py:22
  57.4 1.4 %collective-permute-done.20.refs_3_ = f32[4,128]{1,0:T(4,128)S(1)} collective-permute-done((f32[4,128]{1,0:T(4,128)S(1)}, f32[4,128]{1,0:T(4,128)S(1)}, u32[]{:S(2)}, u32[]{:S(2)}) %collective-permute-start.20) | collective-permute-done | bytes 2080 | tf_op jit(solution)/shard_map/ppermute | solution.py:298
  58.8 0.9 %shard_map.68 = f32[264,512]{1,0:T(8,128)S(1)} custom-call(f32[512,2048]{1,0:T(8,128)S(1)} %get-tuple-element.29.refs_0_, bf16[2048,512]{1,0:T(8,128)(2,1)S(1)} %get-tuple-element.30.refs_1_, f32[4,128]{1,0:T(4,128)S(1)} %collective-permute-done.19.refs_2_, f32[4,128]{1,0:T(4,128)S(1)} %collective-permute-done.20.refs_3_, ...), custom_call_target="tpu_custom_call" | custom-call | tf_op jit(solution)/shard_map/pallas_call | solution.py:22
  59.7 2.1 %collective-permute-start.22 = (f32[264,512]{1,0:T(8,128)S(1)}, f32[264,512]{1,0:T(8,128)S(1)}, u32[]{:S(2)}, u32[]{:S(2)}) collective-permute-start(f32[264,512]{1,0:T(8,128)S(1)} %shard_map.68), channel_id=1, source_target_pairs={{0,2},{1,3},{2,0},{3,1},{4,6},{5,7},{6,4},{7,5},{8,10},{9,11},{10,... | collective-permute-start | bytes 1622024 | tf_op jit(solution)/shard_map/ppermute | solution.py:298
  61.8 2.5 %collective-permute-done.24.two_ref = f32[256,512]{1,0:T(8,128)S(1)} collective-permute-done((f32[256,512]{1,0:T(8,128)S(1)}, f32[256,512]{1,0:T(8,128)S(1)}, u32[]{:S(2)}, u32[]{:S(2)}) %collective-permute-start.24) | collective-permute-done | bytes 524320 | tf_op jit(solution)/shard_map/ppermute | solution.py:298
  64.3 0.1 shard_map.71
  64.4 0.1 collective-permute-start.25
  64.5 0.5 collective-permute-start.26
  64.9 0.1 collective-permute-start.27
  65.0 0.4 collective-permute-start.28
  65.5 0.3 collective-permute-done.25.refs_4_
  65.8 0.2 collective-permute-done.26.refs_5_
  66.0 0.3 collective-permute-done.27.refs_6_
  66.3 0.2 collective-permute-done.28.refs_7_
  66.5 1.0 %shard_map.72 = f32[512,512]{1,0:T(8,128)} custom-call(f32[64,512]{1,0:T(8,128)S(1)} %get-tuple-element.34.refs_0_, f32[64,512]{1,0:T(8,128)S(1)} %get-tuple-element.35.refs_1_, f32[64,512]{1,0:T(8,128)S(1)} %get-tuple-element.36.refs_2_, f32[64,512]{1,0:T(8,128)S(1)} %get-tuple-element.37.refs_3_, f32[64,512]{1,0:T(8,128)S(1)} %collective-permute-done.25.refs_4_, ...), custom_call_target="tpu_custom_call" | custom-call | tf_op jit(solution)/shard_map/pallas_call | solution.py:22
  67.5 0.9 %shard_map.67.refs_0_ = f32[264,512]{1,0:T(8,128)S(1)} custom-call(f32[512,2048]{1,0:T(8,128)S(1)} %get-tuple-element.29.refs_0_, bf16[2048,512]{1,0:T(8,128)(2,1)S(1)} %get-tuple-element.30.refs_1_, f32[4,128]{1,0:T(4,128)S(1)} %collective-permute-done.19.refs_2_, f32[4,128]{1,0:T(4,128)S(1)} %collective-permute-done.20.refs_3_, ...), custom_call_target="tpu_custom_call" | custom-call | tf_op jit(solution)/shard_map/pallas_call | solution.py:22
  68.4 4.1 %collective-permute-done.22.refs_1_ = f32[264,512]{1,0:T(8,128)S(1)} collective-permute-done((f32[264,512]{1,0:T(8,128)S(1)}, f32[264,512]{1,0:T(8,128)S(1)}, u32[]{:S(2)}, u32[]{:S(2)}) %collective-permute-start.22) | collective-permute-done | bytes 540704 | tf_op jit(solution)/shard_map/ppermute | solution.py:298
  72.5 1.1 %shard_map.69 = f32[256,512]{1,0:T(8,128)} custom-call(f32[264,512]{1,0:T(8,128)S(1)} %shard_map.67.refs_0_, f32[264,512]{1,0:T(8,128)S(1)} %collective-permute-done.22.refs_1_), custom_call_target="tpu_custom_call" | custom-call | tf_op jit(solution)/shard_map/pallas_call | solution.py:22
  (23 shorter events, 0.2 us)
Async XLA Ops:
  0.6 1.0 %copy-start.2 = (bf16[512,512]{1,0:T(8,128)(2,1)S(1)}, bf16[512,512]{1,0:T(8,128)(2,1)}, u32[]{:S(2)}) copy-start(bf16[512,512]{1,0:T(8,128)(2,1)} %refs_1_.3) | copy-start | bytes 1572868
  1.7 17.6 %collective-permute-start.3 = (f32[128,512]{1,0:T(8,128)S(1)}, f32[128,512]{1,0:T(8,128)S(1)}, u32[]{:S(2)}, u32[]{:S(2)}) collective-permute-start(f32[128,512]{1,0:T(8,128)S(1)} %shard_map.61), channel_id=1, source_target_pairs={{0,4},{1,5},{2,6},{3,7},{4,0},{5,1},{6,2},{7,3},{8,12},{9,13},{10,... | collective-permute-start | bytes 786440 | tf_op jit(solution)/shard_map/ppermute | solution.py:298
  5.8 13.5 %collective-permute-start.4 = (f32[128,512]{1,0:T(8,128)S(1)}, f32[128,512]{1,0:T(8,128)S(1)}, u32[]{:S(2)}, u32[]{:S(2)}) collective-permute-start(f32[128,512]{1,0:T(8,128)S(1)} %shard_map.61), channel_id=1, source_target_pairs={{0,1},{1,0},{2,3},{3,2},{4,5},{5,4},{6,7},{7,6},{8,9},{9,8},{10,11... | collective-permute-start | bytes 786440 | tf_op jit(solution)/shard_map/ppermute | solution.py:298
  7.3 1.6 %copy-start = (bf16[2048,512]{1,0:T(8,128)(2,1)S(1)}, bf16[2048,512]{1,0:T(8,128)(2,1)}, u32[]{:S(2)}) copy-start(bf16[2048,512]{1,0:T(8,128)(2,1)} %refs_0_.1) | copy-start | bytes 6291460
  8.9 0.7 copy-start.5
  9.6 13.2 %copy-start.1 = (bf16[2048,512]{1,0:T(8,128)(2,1)S(1)}, bf16[2048,512]{1,0:T(8,128)(2,1)}, u32[]{:S(2)}) copy-start(bf16[2048,512]{1,0:T(8,128)(2,1)} %refs_0_.1) | copy-start | bytes 6291460
  9.6 15.7 %copy-start.4 = (f32[2048]{0:T(1024)S(1)}, f32[2048]{0:T(1024)}, u32[]{:S(2)}) copy-start(f32[2048]{0:T(1024)} %param.6) | copy-start | bytes 24580
  11.5 7.8 %collective-permute-start = (f32[16,128]{1,0:T(8,128)S(1)}, f32[16,128]{1,0:T(8,128)S(1)}, u32[]{:S(2)}, u32[]{:S(2)}) collective-permute-start(f32[16,128]{1,0:T(8,128)S(1)} %get-tuple-element.22.refs_0_), channel_id=1, source_target_pairs={{0,5},{1,4},{2,7},{3,6},{4,1},{5,0},{6,3},{7,2},{8,13},{9,12},{10,... | collective-permute-start | bytes 24584 | tf_op jit(solution)/shard_map/ppermute | solution.py:298
  11.6 7.7 %collective-permute-start.1 = (f32[16,128]{1,0:T(8,128)S(1)}, f32[16,128]{1,0:T(8,128)S(1)}, u32[]{:S(2)}, u32[]{:S(2)}) collective-permute-start(f32[16,128]{1,0:T(8,128)S(1)} %get-tuple-element.22.refs_0_), channel_id=1, source_target_pairs={{0,4},{1,5},{2,6},{3,7},{4,0},{5,1},{6,2},{7,3},{8,12},{9,13},{10,... | collective-permute-start | bytes 24584 | tf_op jit(solution)/shard_map/ppermute | solution.py:298
  14.4 4.9 %collective-permute-start.2 = (f32[16,128]{1,0:T(8,128)S(1)}, f32[16,128]{1,0:T(8,128)S(1)}, u32[]{:S(2)}, u32[]{:S(2)}) collective-permute-start(f32[16,128]{1,0:T(8,128)S(1)} %get-tuple-element.22.refs_0_), channel_id=1, source_target_pairs={{0,1},{1,0},{2,3},{3,2},{4,5},{5,4},{6,7},{7,6},{8,9},{9,8},{10,11... | collective-permute-start | bytes 24584 | tf_op jit(solution)/shard_map/ppermute | solution.py:298
  19.4 10.6 %collective-permute-start.10 = (f32[192,512]{1,0:T(8,128)S(1)}, f32[192,512]{1,0:T(8,128)S(1)}, u32[]{:S(2)}, u32[]{:S(2)}) collective-permute-start(f32[192,512]{1,0:T(8,128)S(1)} %get-tuple-element.25.refs_6_), channel_id=1, source_target_pairs={{0,16},{8,24},{16,0},{24,8},{1,17},{9,25},{17,1},{25,9},{2,18},{10... | collective-permute-start | bytes 1179656 | tf_op jit(solution)/shard_map/ppermute | solution.py:298
  21.0 9.0 %collective-permute-start.9 = (f32[128,512]{1,0:T(8,128)S(1)}, f32[128,512]{1,0:T(8,128)S(1)}, u32[]{:S(2)}, u32[]{:S(2)}) collective-permute-start(f32[128,512]{1,0:T(8,128)S(1)} %get-tuple-element.24.refs_7_), channel_id=1, source_target_pairs={{0,1},{1,0},{2,3},{3,2},{4,5},{5,4},{6,7},{7,6},{8,9},{9,8},{10,11... | collective-permute-start | bytes 786440 | tf_op jit(solution)/shard_map/ppermute | solution.py:298
  21.6 3.7 %collective-permute-start.5 = (f32[16,128]{1,0:T(8,128)S(1)}, f32[16,128]{1,0:T(8,128)S(1)}, u32[]{:S(2)}, u32[]{:S(2)}) collective-permute-start(f32[16,128]{1,0:T(8,128)S(1)} %get-tuple-element.23.refs_3_), channel_id=1, source_target_pairs={{0,2},{1,3},{2,0},{3,1},{4,6},{5,7},{6,4},{7,5},{8,10},{9,11},{10,... | collective-permute-start | bytes 24584 | tf_op jit(solution)/shard_map/ppermute | solution.py:298
  26.3 1.9 %collective-permute-start.6 = (f32[4,128]{1,0:T(4,128)S(1)}, f32[4,128]{1,0:T(4,128)S(1)}, u32[]{:S(2)}, u32[]{:S(2)}) collective-permute-start(f32[4,128]{1,0:T(4,128)S(1)} %shard_map.63.refs_3_), channel_id=1, source_target_pairs={{0,8},{8,0},{16,24},{24,16},{1,9},{9,1},{17,25},{25,17},{2,10},{10... | collective-permute-start | bytes 6152 | tf_op jit(solution)/shard_map/ppermute | solution.py:298
  26.3 3.7 %collective-permute-start.7 = (f32[4,128]{1,0:T(4,128)S(1)}, f32[4,128]{1,0:T(4,128)S(1)}, u32[]{:S(2)}, u32[]{:S(2)}) collective-permute-start(f32[4,128]{1,0:T(4,128)S(1)} %shard_map.63.refs_3_), channel_id=1, source_target_pairs={{0,16},{8,24},{16,0},{24,8},{1,17},{9,25},{17,1},{25,9},{2,18},{10... | collective-permute-start | bytes 6152 | tf_op jit(solution)/shard_map/ppermute | solution.py:298
  26.9 3.1 %collective-permute-start.8 = (f32[4,128]{1,0:T(4,128)S(1)}, f32[4,128]{1,0:T(4,128)S(1)}, u32[]{:S(2)}, u32[]{:S(2)}) collective-permute-start(f32[4,128]{1,0:T(4,128)S(1)} %shard_map.63.refs_3_), channel_id=1, source_target_pairs={{0,24},{8,16},{16,8},{24,0},{1,25},{9,17},{17,9},{25,1},{2,26},{10... | collective-permute-start | bytes 6152 | tf_op jit(solution)/shard_map/ppermute | solution.py:298
  31.1 3.7 %collective-permute-start.11 = (f32[16,128]{1,0:T(8,128)S(1)}, f32[16,128]{1,0:T(8,128)S(1)}, u32[]{:S(2)}, u32[]{:S(2)}) collective-permute-start(f32[16,128]{1,0:T(8,128)S(1)} %get-tuple-element.26), channel_id=1, source_target_pairs={{0,1},{1,0},{2,3},{3,2},{4,5},{5,4},{6,7},{7,6},{8,9},{9,8},{10,11... | collective-permute-start | bytes 24584 | tf_op jit(solution)/shard_map/ppermute | solution.py:298
  32.6 10.8 %collective-permute-start.14 = (f32[192,512]{1,0:T(8,128)S(1)}, f32[192,512]{1,0:T(8,128)S(1)}, u32[]{:S(2)}, u32[]{:S(2)}) collective-permute-start(f32[192,512]{1,0:T(8,128)S(1)} %get-tuple-element.27.refs_8_), channel_id=1, source_target_pairs={{0,16},{8,24},{16,0},{24,8},{1,17},{9,25},{17,1},{25,9},{2,18},{10... | collective-permute-start | bytes 1179656 | tf_op jit(solution)/shard_map/ppermute | solution.py:298
  34.8 3.7 %collective-permute-start.12 = (f32[16,128]{1,0:T(8,128)S(1)}, f32[16,128]{1,0:T(8,128)S(1)}, u32[]{:S(2)}, u32[]{:S(2)}) collective-permute-start(f32[16,128]{1,0:T(8,128)S(1)} %multiply_add_fusion.1), channel_id=1, source_target_pairs={{0,2},{1,3},{2,0},{3,1},{4,6},{5,7},{6,4},{7,5},{8,10},{9,11},{10,... | collective-permute-start | bytes 24584 | tf_op jit(solution)/shard_map/ppermute | solution.py:298
  38.6 17.5 %copy-start.3 = (bf16[512,512]{1,0:T(8,128)(2,1)S(1)}, bf16[512,512]{1,0:T(8,128)(2,1)}, u32[]{:S(2)}) copy-start(bf16[512,512]{1,0:T(8,128)(2,1)} %refs_1_.3) | copy-start | bytes 1572868
  38.6 4.6 %collective-permute-start.13 = (f32[16,128]{1,0:T(8,128)S(1)}, f32[16,128]{1,0:T(8,128)S(1)}, u32[]{:S(2)}, u32[]{:S(2)}) collective-permute-start(f32[16,128]{1,0:T(8,128)S(1)} %multiply_add_fusion.refs_4_), channel_id=1, source_target_pairs={{0,4},{1,5},{2,6},{3,7},{4,0},{5,1},{6,2},{7,3},{8,12},{9,13},{10,... | collective-permute-start | bytes 24584 | tf_op jit(solution)/shard_map/ppermute | solution.py:298
  45.4 10.7 %collective-permute-start.15 = (f32[3,2,128,512]{3,2,1,0:T(8,128)S(1)}, f32[3,2,128,512]{3,2,1,0:T(8,128)S(1)}, u32[]{:S(2)}, u32[]{:S(2)}) collective-permute-start(f32[3,2,128,512]{3,2,1,0:T(8,128)S(1)} %get-tuple-element.28.refs_2_), channel_id=1, source_target_pairs={{0,8},{8,0},{16,24},{24,16},{1,9},{9,1},{17,25},{25,17},{2,10},{10... | collective-permute-start | bytes 4718600 | tf_op jit(solution)/shard_map/ppermute | solution.py:298
  45.5 5.3 %collective-permute-start.23 = (f32[256,512]{1,0:T(8,128)S(1)}, f32[256,512]{1,0:T(8,128)S(1)}, u32[]{:S(2)}, u32[]{:S(2)}) collective-permute-start(f32[256,512]{1,0:T(8,128)S(1)} %get-tuple-element.33), channel_id=1, source_target_pairs={{0,8},{8,0},{16,24},{24,16},{1,9},{9,1},{17,25},{25,17},{2,10},{10... | collective-permute-start | bytes 1572872 | tf_op jit(solution)/shard_map/ppermute | solution.py:298
  46.0 3.0 %collective-permute-start.18 = (f32[4,128]{1,0:T(4,128)S(1)}, f32[4,128]{1,0:T(4,128)S(1)}, u32[]{:S(2)}, u32[]{:S(2)}) collective-permute-start(f32[4,128]{1,0:T(4,128)S(1)} %get-tuple-element.31.lse_ref), channel_id=1, source_target_pairs={{0,24},{8,16},{16,8},{24,0},{1,25},{9,17},{17,9},{25,1},{2,26},{10... | collective-permute-start | bytes 6152 | tf_op jit(solution)/shard_map/ppermute | solution.py:298
  47.2 3.6 %collective-permute-start.17 = (f32[4,128]{1,0:T(4,128)S(1)}, f32[4,128]{1,0:T(4,128)S(1)}, u32[]{:S(2)}, u32[]{:S(2)}) collective-permute-start(f32[4,128]{1,0:T(4,128)S(1)} %get-tuple-element.31.lse_ref), channel_id=1, source_target_pairs={{0,16},{8,24},{16,0},{24,8},{1,17},{9,25},{17,1},{25,9},{2,18},{10... | collective-permute-start | bytes 6152 | tf_op jit(solution)/shard_map/ppermute | solution.py:298
  47.7 3.1 %collective-permute-start.16 = (f32[4,128]{1,0:T(4,128)S(1)}, f32[4,128]{1,0:T(4,128)S(1)}, u32[]{:S(2)}, u32[]{:S(2)}) collective-permute-start(f32[4,128]{1,0:T(4,128)S(1)} %get-tuple-element.31.lse_ref), channel_id=1, source_target_pairs={{0,8},{8,0},{16,24},{24,16},{1,9},{9,1},{17,25},{25,17},{2,10},{10... | collective-permute-start | bytes 6152 | tf_op jit(solution)/shard_map/ppermute | solution.py:298
  51.1 13.2 %collective-permute-start.24 = (f32[256,512]{1,0:T(8,128)S(1)}, f32[256,512]{1,0:T(8,128)S(1)}, u32[]{:S(2)}, u32[]{:S(2)}) collective-permute-start(f32[256,512]{1,0:T(8,128)S(1)} %shard_map.70.one_ref), channel_id=1, source_target_pairs={{0,16},{8,24},{16,0},{24,8},{1,17},{9,25},{17,1},{25,9},{2,18},{10... | collective-permute-start | bytes 1572872 | tf_op jit(solution)/shard_map/ppermute | solution.py:298
  51.7 5.7 %collective-permute-start.19 = (f32[4,128]{1,0:T(4,128)S(1)}, f32[4,128]{1,0:T(4,128)S(1)}, u32[]{:S(2)}, u32[]{:S(2)}) collective-permute-start(f32[4,128]{1,0:T(4,128)S(1)} %get-tuple-element.38.refs_5_), channel_id=1, source_target_pairs={{0,5},{1,4},{2,7},{3,6},{4,1},{5,0},{6,3},{7,2},{8,13},{9,12},{10,... | collective-permute-start | bytes 6152 | tf_op jit(solution)/shard_map/ppermute | solution.py:298
  54.4 4.5 %collective-permute-start.20 = (f32[4,128]{1,0:T(4,128)S(1)}, f32[4,128]{1,0:T(4,128)S(1)}, u32[]{:S(2)}, u32[]{:S(2)}) collective-permute-start(f32[4,128]{1,0:T(4,128)S(1)} %get-tuple-element.38.refs_5_), channel_id=1, source_target_pairs={{0,4},{1,5},{2,6},{3,7},{4,0},{5,1},{6,2},{7,3},{8,12},{9,13},{10,... | collective-permute-start | bytes 6152 | tf_op jit(solution)/shard_map/ppermute | solution.py:298
  55.2 3.6 %collective-permute-start.21 = (f32[4,128]{1,0:T(4,128)S(1)}, f32[4,128]{1,0:T(4,128)S(1)}, u32[]{:S(2)}, u32[]{:S(2)}) collective-permute-start(f32[4,128]{1,0:T(4,128)S(1)} %get-tuple-element.38.refs_5_), channel_id=1, source_target_pairs={{0,1},{1,0},{2,3},{3,2},{4,5},{5,4},{6,7},{7,6},{8,9},{9,8},{10,11... | collective-permute-start | bytes 6152 | tf_op jit(solution)/shard_map/ppermute | solution.py:298
  59.7 12.8 %collective-permute-start.22 = (f32[264,512]{1,0:T(8,128)S(1)}, f32[264,512]{1,0:T(8,128)S(1)}, u32[]{:S(2)}, u32[]{:S(2)}) collective-permute-start(f32[264,512]{1,0:T(8,128)S(1)} %shard_map.68), channel_id=1, source_target_pairs={{0,2},{1,3},{2,0},{3,1},{4,6},{5,7},{6,4},{7,5},{8,10},{9,11},{10,... | collective-permute-start | bytes 1622024 | tf_op jit(solution)/shard_map/ppermute | solution.py:298
  64.4 1.4 %collective-permute-start.25 = (f32[64,512]{1,0:T(8,128)S(1)}, f32[64,512]{1,0:T(8,128)S(1)}, u32[]{:S(2)}, u32[]{:S(2)}) collective-permute-start(f32[64,512]{1,0:T(8,128)S(1)} %get-tuple-element.34.refs_0_), channel_id=1, source_target_pairs={{0,8},{8,0},{16,24},{24,16},{1,9},{9,1},{17,25},{25,17},{2,10},{10... | collective-permute-start | bytes 393224 | tf_op jit(solution)/shard_map/ppermute | solution.py:298
  64.5 1.5 %collective-permute-start.26 = (f32[64,512]{1,0:T(8,128)S(1)}, f32[64,512]{1,0:T(8,128)S(1)}, u32[]{:S(2)}, u32[]{:S(2)}) collective-permute-start(f32[64,512]{1,0:T(8,128)S(1)} %get-tuple-element.35.refs_1_), channel_id=1, source_target_pairs={{0,8},{8,0},{16,24},{24,16},{1,9},{9,1},{17,25},{25,17},{2,10},{10... | collective-permute-start | bytes 393224 | tf_op jit(solution)/shard_map/ppermute | solution.py:298
  64.9 1.3 %collective-permute-start.27 = (f32[64,512]{1,0:T(8,128)S(1)}, f32[64,512]{1,0:T(8,128)S(1)}, u32[]{:S(2)}, u32[]{:S(2)}) collective-permute-start(f32[64,512]{1,0:T(8,128)S(1)} %get-tuple-element.36.refs_2_), channel_id=1, source_target_pairs={{0,8},{8,0},{16,24},{24,16},{1,9},{9,1},{17,25},{25,17},{2,10},{10... | collective-permute-start | bytes 393224 | tf_op jit(solution)/shard_map/ppermute | solution.py:298
  65.0 1.5 %collective-permute-start.28 = (f32[64,512]{1,0:T(8,128)S(1)}, f32[64,512]{1,0:T(8,128)S(1)}, u32[]{:S(2)}, u32[]{:S(2)}) collective-permute-start(f32[64,512]{1,0:T(8,128)S(1)} %get-tuple-element.37.refs_3_), channel_id=1, source_target_pairs={{0,8},{8,0},{16,24},{24,16},{1,9},{9,1},{17,25},{25,17},{2,10},{10... | collective-permute-start | bytes 393224 | tf_op jit(solution)/shard_map/ppermute | solution.py:298

commit v16 on v8

--- a/solution.py
+++ b/solution.py
@@ -192,7 +192,7 @@
     return peak, jnp.sum(sum(exps), axis=1, keepdims=True), exps
 
 
-def share_kernel(mine_ref, came_ref, total_ref, lse_ref, came_lse_ref, out_ref):
+def share_kernel(mine_ref, came_ref, total_ref, lse_ref, came_lse_ref, after_ref, out_ref):
     half = mine_ref.shape[0] // LANES
     at = pl.ds(lax.axis_index("row") % 2 * half, half)
     total = total_ref[at, :]
@@ -253,15 +253,15 @@
 EXTRA = 8
 
 
-def images(flip, inner_ref, y_ref, bias_refs, scores_ref):
+def images(flip, order, inner_ref, y_ref, biases_ref, scores_ref):
     rows = scores_ref.shape[0]
-    n_shards = len(bias_refs)
+    n_shards = len(order)
     n_tgt = y_ref.shape[0] // n_shards
     block = pl.ds(flip * rows, rows)
     peak = jnp.full((rows, 1), -jnp.inf, jnp.float32)
-    for k, bias_ref in enumerate(bias_refs[::-1]):
+    for k, place in enumerate(order):
         at = pl.ds(k * n_tgt, n_tgt)
-        scores = inner_ref[block, at] + to_row(bias_ref[...])
+        scores = inner_ref[block, at] + to_row(biases_ref[place])
         scores_ref[:, at] = scores
         peak = jnp.maximum(peak, jnp.max(scores, axis=1, keepdims=True))
     total = jnp.zeros((rows, 1), jnp.float32)
@@ -284,9 +284,9 @@
 EXTRA = 8
 
 
-def image_kernel(flip, inner_ref, y_ref, *refs):
-    bias_refs, (image_ref, scores_ref) = refs[:-2], refs[-2:]
-    numer, total, peak = images(flip, inner_ref, y_ref, bias_refs, scores_ref)
+def image_kernel(flip, order, inner_ref, y_ref, biases_ref, *refs):
+    image_ref, scores_ref = refs[-2:]
+    numer, total, peak = images(flip, order, inner_ref, y_ref, biases_ref, scores_ref)
     rows = numer.shape[0]
     lse = lanes_of(peak + jnp.log2(total))
     image_ref[:rows, :] = numer * (1.0 / total)
@@ -370,13 +370,11 @@
     total = merge_all(parts)
 
     bias = lt * LOG2E + (sqy - total) - sqy
-    biases = [bias] + [swap(bias, "col", distance) for distance in apart[1:]]
-
-    mine = call(share_kernel, f32(half, width), mine, swap(sent, "row", 1), total, lse, parts[1])
-    rest = bits_of(n_row)[1:]
-    for distance in rest[:-1]:
-        mine, = call(add_kernel, (f32(half, width),), mine, swap(mine, "row", distance))
-    mine_came = swap(mine, "row", rest[-1])
+    biases, held = bias[None], [0]
+    for bit in [bit for bit in bits_of(n_col) if bit != n_x]:
+        biases = jnp.concatenate([biases, swap(biases, "col", bit)], axis=0)
+        held += [way ^ bit for way in held]
+    order = [held.index(way) for way in apart]
 
     n_all = len(apart) * n_tgt
     all_y, inner = call(
@@ -386,22 +384,29 @@
         limit=32,
     )
 
-    def image(flip):
+    mine = call(share_kernel, f32(half, width), mine, swap(sent, "row", 1), total, lse, parts[1], inner)
+    rest = bits_of(n_row)[1:]
+    for distance in rest[:-1]:
+        mine, = call(add_kernel, (f32(half, width),), mine, swap(mine, "row", distance))
+    mine_came = swap(mine, "row", rest[-1])
+
+    def image(flip, *after):
         return call(
-            lambda *refs: image_kernel(flip, *refs),
+            lambda *refs: image_kernel(flip, order, *refs),
             f32(count + EXTRA, width),
-            inner, all_y, *biases[::-1],
+            inner, all_y, biases, *after,
             scratch=[pltpu.VMEM((count, n_all), jnp.float32)],
         )
 
     came = swap(image(1), "col", n_x)
-    own = image(0)
     n_last = 4
     mine = call(add_kernel, (f32(half // n_last, width),) * n_last, mine, mine_came)
+    other = [swap(piece, "row", 1) for piece in mine]
     target_image = call(
-        place_kernel, f32(n_tgt, width), *mine, *[swap(piece, "row", 1) for piece in mine],
+        place_kernel, f32(n_tgt, width), *mine, *other,
         out_specs=HBM, scratch=[DMA((2 * n_last,))],
     )
+    own = image(0, *other)
     source_image = call(join_kernel, f32(count, width), own, came)
     return source_image, target_image
 

time: 74.2 us -> 75.6 us (1.019)
  waiting for transfers between devices: 28.5 us -> 31.3 us
  starting transfers between devices: 29 us -> 27.6 us
    ppermute x29 -> x28, waiting for transfers between devices: 28.5 us -> 31.3 us  [swap(): return lax.ppermute(value, axis, [(i, i ^ distance) for i in range(n)])]
    ppermute x29 -> x28, starting transfers between devices: 29 us -> 27.6 us  [swap(): return lax.ppermute(value, axis, [(i, i ^ distance) for i in range(n)])]
  transfers between devices with their start and end apart: 29 -> 28, of which waited for: 17 -> 16; matrix products, arithmetic and copies ran while one was open for 0% -> 0% of each run, Pallas kernels for 11% -> 10%
where the time goes in v16:
time: 75.6 us; the launch traced here: 75.4 us
  waiting for transfers between devices  31.3 us (41%)
  starting transfers between devices  27.6 us (37%)
  Pallas kernels  12.3 us (16%)
  local copies, waits for them, and re-layouts  3.32 us (4%)
  between operations  0.79 us (1%)
    ppermute x28, waiting for transfers between devices, swap(): return lax.ppermute(value, axis, [(i, i ^ distance) for i in range(n)])  31.3 us
    ppermute x28, starting transfers between devices, swap(): return lax.ppermute(value, axis, [(i, i ^ distance) for i in range(n)])  27.6 us
    pallas_call x14, Pallas kernels, call(): pl.pallas_call(kernel, out_shape=out_shape, in_specs=in_specs or [VMEM] *...  12.3 us
    unnamed x12, local copies, waits for them, and re-layouts  3.32 us
  transfers between devices with their start and end apart: 28, of which 16 were waited for; matrix products, arithmetic and copies ran while one was open for 0% of the time, Pallas kernels for 10%

profile of v16, /device:TPU:0, one launch (start us, length us, event | category | flops | bytes accessed | tf_op | source)
XLA Modules:
  0.0 75.4 jit_solution(16530141925616827073)
XLA Ops:
  0.6 0.0 copy-start.2
  0.6 1.0 %copy-done.2 = bf16[512,512]{1,0:T(8,128)(2,1)S(1)} copy-done((bf16[512,512]{1,0:T(8,128)(2,1)S(1)}, bf16[512,512]{1,0:T(8,128)(2,1)}, u32[]{:S(2)}) %copy-start.2) | copy-done | bytes 524312
  1.7 4.1 %collective-permute-start.3 = (f32[128,512]{1,0:T(8,128)S(1)}, f32[128,512]{1,0:T(8,128)S(1)}, u32[]{:S(2)}, u32[]{:S(2)}) collective-permute-start(f32[128,512]{1,0:T(8,128)S(1)} %shard_map.61), channel_id=1, source_target_pairs={{0,4},{1,5},{2,6},{3,7},{4,0},{5,1},{6,2},{7,3},{8,12},{9,13},{10,... | collective-permute-start | bytes 786440 | tf_op jit(solution)/shard_map/ppermute | solution.py:299
  5.8 1.5 %collective-permute-start.4 = (f32[128,512]{1,0:T(8,128)S(1)}, f32[128,512]{1,0:T(8,128)S(1)}, u32[]{:S(2)}, u32[]{:S(2)}) collective-permute-start(f32[128,512]{1,0:T(8,128)S(1)} %shard_map.61), channel_id=1, source_target_pairs={{0,1},{1,0},{2,3},{3,2},{4,5},{5,4},{6,7},{7,6},{8,9},{9,8},{10,11... | collective-permute-start | bytes 786440 | tf_op jit(solution)/shard_map/ppermute | solution.py:299
  7.3 1.6 %copy-done = bf16[2048,512]{1,0:T(8,128)(2,1)S(1)} copy-done((bf16[2048,512]{1,0:T(8,128)(2,1)S(1)}, bf16[2048,512]{1,0:T(8,128)(2,1)}, u32[]{:S(2)}) %copy-start) | copy-done | bytes 2097176
  8.9 0.7 copy-done.5
  9.6 1.9 %shard_map.59 = (f32[512,2048]{1,0:T(8,128)S(1)}, f32[16,128]{1,0:T(8,128)S(1)}, f32[4,128]{1,0:T(4,128)S(1)}) custom-call(bf16[512,512]{1,0:T(8,128)(2,1)S(1)} %copy-done.2, bf16[2048,512]{1,0:T(8,128)(2,1)S(1)} %copy-done, f32[4,128]{1,0:T(4,128)S(1)} %bitcast.7), custom_call_target="tpu_custom_call" | custom-call | tf_op jit(solution)/shard_map/pallas_call | solution.py:22
  11.5 1.6 %collective-permute-start = (f32[16,128]{1,0:T(8,128)S(1)}, f32[16,128]{1,0:T(8,128)S(1)}, u32[]{:S(2)}, u32[]{:S(2)}) collective-permute-start(f32[16,128]{1,0:T(8,128)S(1)} %get-tuple-element.22.refs_0_), channel_id=1, source_target_pairs={{0,3},{1,2},{2,1},{3,0},{4,7},{5,6},{6,5},{7,4},{8,11},{9,10},{10,... | collective-permute-start | bytes 24584 | tf_op jit(solution)/shard_map/ppermute | solution.py:299
  13.1 0.4 collective-permute-start.1
  13.5 1.5 %collective-permute-start.2 = (f32[16,128]{1,0:T(8,128)S(1)}, f32[16,128]{1,0:T(8,128)S(1)}, u32[]{:S(2)}, u32[]{:S(2)}) collective-permute-start(f32[16,128]{1,0:T(8,128)S(1)} %get-tuple-element.22.refs_0_), channel_id=1, source_target_pairs={{0,1},{1,0},{2,3},{3,2},{4,5},{5,4},{6,7},{7,6},{8,9},{9,8},{10,11... | collective-permute-start | bytes 24584 | tf_op jit(solution)/shard_map/ppermute | solution.py:299
  15.0 3.9 %collective-permute-done.refs_1_ = f32[16,128]{1,0:T(8,128)S(1)} collective-permute-done((f32[16,128]{1,0:T(8,128)S(1)}, f32[16,128]{1,0:T(8,128)S(1)}, u32[]{:S(2)}, u32[]{:S(2)}) %collective-permute-start) | collective-permute-done | bytes 8224 | tf_op jit(solution)/shard_map/ppermute | solution.py:299
  19.0 0.0 collective-permute-done.1.refs_2_
  19.0 0.0 collective-permute-done.2.refs_3_
  19.0 1.6 %collective-permute-start.10 = (f32[192,512]{1,0:T(8,128)S(1)}, f32[192,512]{1,0:T(8,128)S(1)}, u32[]{:S(2)}, u32[]{:S(2)}) collective-permute-start(f32[192,512]{1,0:T(8,128)S(1)} %get-tuple-element.25.refs_6_), channel_id=1, source_target_pairs={{0,16},{8,24},{16,0},{24,8},{1,17},{9,25},{17,1},{25,9},{2,18},{10... | collective-permute-start | bytes 1179656 | tf_op jit(solution)/shard_map/ppermute | solution.py:299
  20.6 0.6 collective-permute-start.9
  21.3 0.5 shard_map.60.refs_2_.refs_3_
  21.8 4.0 %collective-permute-done.5.refs_4_ = f32[16,128]{1,0:T(8,128)S(1)} collective-permute-done((f32[16,128]{1,0:T(8,128)S(1)}, f32[16,128]{1,0:T(8,128)S(1)}, u32[]{:S(2)}, u32[]{:S(2)}) %collective-permute-start.5) | collective-permute-done | bytes 8224 | tf_op jit(solution)/shard_map/ppermute | solution.py:299
  25.8 1.0 %shard_map.63.refs_3_ = f32[4,128]{1,0:T(4,128)S(1)} custom-call(f32[512,2048]{1,0:T(8,128)S(1)} %get-tuple-element.20.refs_0_, f32[16,128]{1,0:T(8,128)S(1)} %bitcast.5, f32[16,128]{1,0:T(8,128)S(1)} %shard_map.60.refs_2_.refs_3_, f32[16,128]{1,0:T(8,128)S(1)} %get-tuple-element.23.refs_3_, f32[16,128]{1,0:T(8,128)S(1)} %collective-permute-done.5.refs_4_), custom_call_target="tpu_custom_call" | custom-call | tf_op jit(solution)/shard_map/pallas_call | solution.py:22
  26.8 0.0 collective-permute-start.6
  26.9 0.6 collective-permute-start.7
  27.4 1.3 %collective-permute-start.8 = (f32[4,128]{1,0:T(4,128)S(1)}, f32[4,128]{1,0:T(4,128)S(1)}, u32[]{:S(2)}, u32[]{:S(2)}) collective-permute-start(f32[4,128]{1,0:T(4,128)S(1)} %shard_map.63.refs_3_), channel_id=1, source_target_pairs={{0,24},{8,16},{16,8},{24,0},{1,25},{9,17},{17,9},{25,1},{2,26},{10... | collective-permute-start | bytes 6152 | tf_op jit(solution)/shard_map/ppermute | solution.py:299
  28.7 0.0 collective-permute-done.6.refs_4_
  28.7 1.8 %collective-permute-done.7.refs_5_ = f32[4,128]{1,0:T(4,128)S(1)} collective-permute-done((f32[4,128]{1,0:T(4,128)S(1)}, f32[4,128]{1,0:T(4,128)S(1)}, u32[]{:S(2)}, u32[]{:S(2)}) %collective-permute-start.7) | collective-permute-done | bytes 2080 | tf_op jit(solution)/shard_map/ppermute | solution.py:299
  30.5 0.0 collective-permute-done.8.refs_6_
  30.5 1.1 %shard_map.64 = (f32[16,128]{1,0:T(8,128)S(1)}, f32[192,512]{1,0:T(8,128)S(1)}) custom-call(f32[512,2048]{1,0:T(8,128)S(1)} %get-tuple-element.20.refs_0_, f32[4,128]{1,0:T(4,128)S(1)} %bitcast.8, f32[4,128]{1,0:T(4,128)S(1)} %get-tuple-element.21.refs_2_, f32[4,128]{1,0:T(4,128)S(1)} %shard_map.63.refs_3_, f32[4,128]{1,0:T(4,128)S(1)} %collective-permute-done.6.refs_4_, ...), custom_call_target="tpu_custom_call" | custom-call | tf_op jit(solution)/shard_map/pallas_call | solution.py:22
  31.6 1.4 %collective-permute-start.11 = (f32[16,128]{1,0:T(8,128)S(1)}, f32[16,128]{1,0:T(8,128)S(1)}, u32[]{:S(2)}, u32[]{:S(2)}) collective-permute-start(f32[16,128]{1,0:T(8,128)S(1)} %get-tuple-element.26), channel_id=1, source_target_pairs={{0,1},{1,0},{2,3},{3,2},{4,5},{5,4},{6,7},{7,6},{8,9},{9,8},{10,11... | collective-permute-start | bytes 24584 | tf_op jit(solution)/shard_map/ppermute | solution.py:299
  33.1 1.4 %collective-permute-start.14 = (f32[192,512]{1,0:T(8,128)S(1)}, f32[192,512]{1,0:T(8,128)S(1)}, u32[]{:S(2)}, u32[]{:S(2)}) collective-permute-start(f32[192,512]{1,0:T(8,128)S(1)} %get-tuple-element.27.refs_8_), channel_id=1, source_target_pairs={{0,16},{8,24},{16,0},{24,8},{1,17},{9,25},{17,1},{25,9},{2,18},{10... | collective-permute-start | bytes 1179656 | tf_op jit(solution)/shard_map/ppermute | solution.py:299
  34.5 0.8 %collective-permute-done.11 = f32[16,128]{1,0:T(8,128)S(1)} collective-permute-done((f32[16,128]{1,0:T(8,128)S(1)}, f32[16,128]{1,0:T(8,128)S(1)}, u32[]{:S(2)}, u32[]{:S(2)}) %collective-permute-start.11) | collective-permute-done | bytes 8224 | tf_op jit(solution)/shard_map/ppermute | solution.py:299
  35.4 1.0 %collective-permute-start.12 = (f32[16,128]{1,0:T(8,128)S(1)}, f32[16,128]{1,0:T(8,128)S(1)}, u32[]{:S(2)}, u32[]{:S(2)}) collective-permute-start(f32[16,128]{1,0:T(8,128)S(1)} %multiply_add_fusion.1), channel_id=1, source_target_pairs={{0,2},{1,3},{2,0},{3,1},{4,6},{5,7},{6,4},{7,5},{8,10},{9,11},{10,... | collective-permute-start | bytes 24584 | tf_op jit(solution)/shard_map/ppermute | solution.py:299
  36.4 2.7 %collective-permute-done.12 = f32[16,128]{1,0:T(8,128)S(1)} collective-permute-done((f32[16,128]{1,0:T(8,128)S(1)}, f32[16,128]{1,0:T(8,128)S(1)}, u32[]{:S(2)}, u32[]{:S(2)}) %collective-permute-start.12) | collective-permute-done | bytes 8224 | tf_op jit(solution)/shard_map/ppermute | solution.py:299
  39.1 0.0 copy-start.3
  39.1 1.9 %collective-permute-start.13 = (f32[16,128]{1,0:T(8,128)S(1)}, f32[16,128]{1,0:T(8,128)S(1)}, u32[]{:S(2)}, u32[]{:S(2)}) collective-permute-start(f32[16,128]{1,0:T(8,128)S(1)} %multiply_add_fusion.refs_4_), channel_id=1, source_target_pairs={{0,4},{1,5},{2,6},{3,7},{4,0},{5,1},{6,2},{7,3},{8,12},{9,13},{10,... | collective-permute-start | bytes 24584 | tf_op jit(solution)/shard_map/ppermute | solution.py:299
  41.1 2.7 %collective-permute-done.13.refs_5_ = f32[16,128]{1,0:T(8,128)S(1)} collective-permute-done((f32[16,128]{1,0:T(8,128)S(1)}, f32[16,128]{1,0:T(8,128)S(1)}, u32[]{:S(2)}, u32[]{:S(2)}) %collective-permute-start.13) | collective-permute-done | bytes 8224 | tf_op jit(solution)/shard_map/ppermute | solution.py:299
  43.7 0.2 collective-permute-done.14.refs_9_
  43.9 2.1 %shard_map.65 = (f32[4,128]{1,0:T(4,128)S(1)}, f32[256,512]{1,0:T(8,128)S(1)}, f32[256,512]{1,0:T(8,128)S(1)}, f32[3,2,128,512]{3,2,1,0:T(8,128)S(1)}) custom-call(f32[512,2048]{1,0:T(8,128)S(1)} %get-tuple-element.20.refs_0_, bf16[2048,512]{1,0:T(8,128)(2,1)S(1)} %copy-done.1, f32[16,128]{1,0:T(8,128)S(1)} %bitcast.6, ...), custom_call_target="tpu_custom_call" | custom-call | tf_op jit(solution)/shard_map/pallas_call | solution.py:22
  46.1 0.1 collective-permute-start.15
  46.2 0.5 collective-permute-start.21
  46.7 1.2 %collective-permute-start.18 = (f32[4,128]{1,0:T(4,128)S(1)}, f32[4,128]{1,0:T(4,128)S(1)}, u32[]{:S(2)}, u32[]{:S(2)}) collective-permute-start(f32[4,128]{1,0:T(4,128)S(1)} %get-tuple-element.31.lse_ref), channel_id=1, source_target_pairs={{0,24},{8,16},{16,8},{24,0},{1,25},{9,17},{17,9},{25,1},{2,26},{10... | collective-permute-start | bytes 6152 | tf_op jit(solution)/shard_map/ppermute | solution.py:299
  47.9 0.5 collective-permute-start.17
  48.4 0.2 collective-permute-start.16
  48.5 1.1 %collective-permute-done.18 = f32[4,128]{1,0:T(4,128)S(1)} collective-permute-done((f32[4,128]{1,0:T(4,128)S(1)}, f32[4,128]{1,0:T(4,128)S(1)}, u32[]{:S(2)}, u32[]{:S(2)}) %collective-permute-start.18) | collective-permute-done | bytes 2080 | tf_op jit(solution)/shard_map/ppermute | solution.py:299
  49.7 1.8 %collective-permute-done.17 = f32[4,128]{1,0:T(4,128)S(1)} collective-permute-done((f32[4,128]{1,0:T(4,128)S(1)}, f32[4,128]{1,0:T(4,128)S(1)}, u32[]{:S(2)}, u32[]{:S(2)}) %collective-permute-start.17) | collective-permute-done | bytes 2080 | tf_op jit(solution)/shard_map/ppermute | solution.py:299
  51.5 1.2 %collective-permute-start.19 = (f32[1,4,128]{2,1,0:T(4,128)S(1)}, f32[1,4,128]{2,1,0:T(4,128)S(1)}, u32[]{:S(2)}, u32[]{:S(2)}) collective-permute-start(f32[1,4,128]{2,1,0:T(4,128)S(1)} %get-tuple-element.38), channel_id=1, source_target_pairs={{0,1},{1,0},{2,3},{3,2},{4,5},{5,4},{6,7},{7,6},{8,9},{9,8},{10,11... | collective-permute-start | bytes 6152 | tf_op jit(solution)/shard_map/ppermute | solution.py:299
  52.7 2.4 %collective-permute-done.19 = f32[1,4,128]{2,1,0:T(4,128)S(1)} collective-permute-done((f32[1,4,128]{2,1,0:T(4,128)S(1)}, f32[1,4,128]{2,1,0:T(4,128)S(1)}, u32[]{:S(2)}, u32[]{:S(2)}) %collective-permute-start.19) | collective-permute-done | bytes 2080 | tf_op jit(solution)/shard_map/ppermute | solution.py:299
  55.1 1.6 %collective-permute-start.20 = (f32[2,4,128]{2,1,0:T(4,128)S(1)}, f32[2,4,128]{2,1,0:T(4,128)S(1)}, u32[]{:S(2)}, u32[]{:S(2)}) collective-permute-start(f32[2,4,128]{2,1,0:T(4,128)S(1)} %pad_maximum_fusion.1), channel_id=1, source_target_pairs={{0,4},{1,5},{2,6},{3,7},{4,0},{5,1},{6,2},{7,3},{8,12},{9,13},{10,... | collective-permute-start | bytes 12296 | tf_op jit(solution)/shard_map/ppermute | solution.py:299
  56.7 1.3 %shard_map.66 = (bf16[2048,512]{1,0:T(8,128)(2,1)S(1)}, f32[512,2048]{1,0:T(8,128)S(1)}) custom-call(bf16[2048,512]{1,0:T(8,128)(2,1)S(1)} %copy-done.1, bf16[512,512]{1,0:T(8,128)(2,1)S(1)} %copy-done.3, f32[3,2,128,512]{3,2,1,0:T(8,128)S(1)} %get-tuple-element.28.refs_2_, f32[3,2,128,512]{3,2,1,0:T(8,128)S(1)} %collective-permute-done.15.refs_3_), custom_call_target="tpu_custom_call" | custom-call | tf_op jit(solution)/shard_map/pallas_call | solution.py:22
  58.1 0.3 shard_map.67.one_ref
  58.4 0.6 collective-permute-start.22
  59.0 0.6 collective-permute-done.20
  59.6 0.9 %shard_map.70 = f32[264,512]{1,0:T(8,128)S(1)} custom-call(f32[512,2048]{1,0:T(8,128)S(1)} %get-tuple-element.29.after_ref.refs_0_, bf16[2048,512]{1,0:T(8,128)(2,1)S(1)} %get-tuple-element.30.refs_1_, f32[4,4,128]{2,1,0:T(4,128)S(1)} %pad_maximum_fusion.refs_2_), custom_call_target="tpu_custom_call" | custom-call | tf_op jit(solution)/shard_map/pallas_call | solution.py:22
  60.5 1.5 %collective-permute-start.27 = (f32[264,512]{1,0:T(8,128)S(1)}, f32[264,512]{1,0:T(8,128)S(1)}, u32[]{:S(2)}, u32[]{:S(2)}) collective-permute-start(f32[264,512]{1,0:T(8,128)S(1)} %shard_map.70), channel_id=1, source_target_pairs={{0,2},{1,3},{2,0},{3,1},{4,6},{5,7},{6,4},{7,5},{8,10},{9,11},{10,... | collective-permute-start | bytes 1622024 | tf_op jit(solution)/shard_map/ppermute | solution.py:299
  62.0 8.1 %collective-permute-done.22.two_ref = f32[256,512]{1,0:T(8,128)S(1)} collective-permute-done((f32[256,512]{1,0:T(8,128)S(1)}, f32[256,512]{1,0:T(8,128)S(1)}, u32[]{:S(2)}, u32[]{:S(2)}) %collective-permute-start.22) | collective-permute-done | bytes 524320 | tf_op jit(solution)/shard_map/ppermute | solution.py:299
  70.2 0.1 shard_map.68
  70.2 0.1 collective-permute-start.23
  70.3 0.5 collective-permute-start.24
  70.8 0.1 collective-permute-start.25
  70.9 0.4 collective-permute-start.26
  71.3 0.3 collective-permute-done.23.refs_3_.refs_4_
  71.7 0.2 collective-permute-done.24.refs_4_.refs_5_
  71.8 0.3 collective-permute-done.25.refs_5_.refs_6_
  72.2 0.2 collective-permute-done.26.refs_6_.refs_7_
  72.4 0.9 %shard_map.69.refs_0_ = f32[264,512]{1,0:T(8,128)S(1)} custom-call(f32[512,2048]{1,0:T(8,128)S(1)} %get-tuple-element.29.after_ref.refs_0_, bf16[2048,512]{1,0:T(8,128)(2,1)S(1)} %get-tuple-element.30.refs_1_, f32[4,4,128]{2,1,0:T(4,128)S(1)} %pad_maximum_fusion.refs_2_, f32[64,512]{1,0:T(8,128)S(1)} %collective-permute-done.23.refs_3_.refs_4_, ...), custom_call_target="tpu_custom_call" | custom-call | tf_op jit(solution)/shard_map/pallas_call | solution.py:22
  73.2 1.0 %shard_map.72 = f32[512,512]{1,0:T(8,128)} custom-call(f32[64,512]{1,0:T(8,128)S(1)} %get-tuple-element.34.refs_0_, f32[64,512]{1,0:T(8,128)S(1)} %get-tuple-element.35.refs_1_, f32[64,512]{1,0:T(8,128)S(1)} %get-tuple-element.36.refs_2_, f32[64,512]{1,0:T(8,128)S(1)} %get-tuple-element.37.refs_3_, f32[64,512]{1,0:T(8,128)S(1)} %collective-permute-done.23.refs_3_.refs_4_, ...), custom_call_target="tpu_custom_call" | custom-call | tf_op jit(solution)/shard_map/pallas_call | solution.py:22
  74.3 1.1 %shard_map.71 = f32[256,512]{1,0:T(8,128)} custom-call(f32[264,512]{1,0:T(8,128)S(1)} %shard_map.69.refs_0_, f32[264,512]{1,0:T(8,128)S(1)} %collective-permute-done.27.refs_1_), custom_call_target="tpu_custom_call" | custom-call | tf_op jit(solution)/shard_map/pallas_call | solution.py:22
  (23 shorter events, 0.2 us)
Async XLA Ops:
  0.6 1.0 %copy-start.2 = (bf16[512,512]{1,0:T(8,128)(2,1)S(1)}, bf16[512,512]{1,0:T(8,128)(2,1)}, u32[]{:S(2)}) copy-start(bf16[512,512]{1,0:T(8,128)(2,1)} %refs_1_.3) | copy-start | bytes 1572868
  1.7 17.3 %collective-permute-start.3 = (f32[128,512]{1,0:T(8,128)S(1)}, f32[128,512]{1,0:T(8,128)S(1)}, u32[]{:S(2)}, u32[]{:S(2)}) collective-permute-start(f32[128,512]{1,0:T(8,128)S(1)} %shard_map.61), channel_id=1, source_target_pairs={{0,4},{1,5},{2,6},{3,7},{4,0},{5,1},{6,2},{7,3},{8,12},{9,13},{10,... | collective-permute-start | bytes 786440 | tf_op jit(solution)/shard_map/ppermute | solution.py:299
  5.8 13.2 %collective-permute-start.4 = (f32[128,512]{1,0:T(8,128)S(1)}, f32[128,512]{1,0:T(8,128)S(1)}, u32[]{:S(2)}, u32[]{:S(2)}) collective-permute-start(f32[128,512]{1,0:T(8,128)S(1)} %shard_map.61), channel_id=1, source_target_pairs={{0,1},{1,0},{2,3},{3,2},{4,5},{5,4},{6,7},{7,6},{8,9},{9,8},{10,11... | collective-permute-start | bytes 786440 | tf_op jit(solution)/shard_map/ppermute | solution.py:299
  7.3 1.6 %copy-start = (bf16[2048,512]{1,0:T(8,128)(2,1)S(1)}, bf16[2048,512]{1,0:T(8,128)(2,1)}, u32[]{:S(2)}) copy-start(bf16[2048,512]{1,0:T(8,128)(2,1)} %refs_0_.1) | copy-start | bytes 6291460
  8.9 0.7 copy-start.5
  9.6 11.7 %copy-start.1 = (bf16[2048,512]{1,0:T(8,128)(2,1)S(1)}, bf16[2048,512]{1,0:T(8,128)(2,1)}, u32[]{:S(2)}) copy-start(bf16[2048,512]{1,0:T(8,128)(2,1)} %refs_0_.1) | copy-start | bytes 6291460
  9.6 16.3 %copy-start.4 = (f32[2048]{0:T(1024)S(1)}, f32[2048]{0:T(1024)}, u32[]{:S(2)}) copy-start(f32[2048]{0:T(1024)} %param.6) | copy-start | bytes 24580
  11.5 7.5 %collective-permute-start = (f32[16,128]{1,0:T(8,128)S(1)}, f32[16,128]{1,0:T(8,128)S(1)}, u32[]{:S(2)}, u32[]{:S(2)}) collective-permute-start(f32[16,128]{1,0:T(8,128)S(1)} %get-tuple-element.22.refs_0_), channel_id=1, source_target_pairs={{0,3},{1,2},{2,1},{3,0},{4,7},{5,6},{6,5},{7,4},{8,11},{9,10},{10,... | collective-permute-start | bytes 24584 | tf_op jit(solution)/shard_map/ppermute | solution.py:299
  13.1 5.9 %collective-permute-start.1 = (f32[16,128]{1,0:T(8,128)S(1)}, f32[16,128]{1,0:T(8,128)S(1)}, u32[]{:S(2)}, u32[]{:S(2)}) collective-permute-start(f32[16,128]{1,0:T(8,128)S(1)} %get-tuple-element.22.refs_0_), channel_id=1, source_target_pairs={{0,2},{1,3},{2,0},{3,1},{4,6},{5,7},{6,4},{7,5},{8,10},{9,11},{10,... | collective-permute-start | bytes 24584 | tf_op jit(solution)/shard_map/ppermute | solution.py:299
  13.5 5.4 %collective-permute-start.2 = (f32[16,128]{1,0:T(8,128)S(1)}, f32[16,128]{1,0:T(8,128)S(1)}, u32[]{:S(2)}, u32[]{:S(2)}) collective-permute-start(f32[16,128]{1,0:T(8,128)S(1)} %get-tuple-element.22.refs_0_), channel_id=1, source_target_pairs={{0,1},{1,0},{2,3},{3,2},{4,5},{5,4},{6,7},{7,6},{8,9},{9,8},{10,11... | collective-permute-start | bytes 24584 | tf_op jit(solution)/shard_map/ppermute | solution.py:299
  19.0 11.5 %collective-permute-start.10 = (f32[192,512]{1,0:T(8,128)S(1)}, f32[192,512]{1,0:T(8,128)S(1)}, u32[]{:S(2)}, u32[]{:S(2)}) collective-permute-start(f32[192,512]{1,0:T(8,128)S(1)} %get-tuple-element.25.refs_6_), channel_id=1, source_target_pairs={{0,16},{8,24},{16,0},{24,8},{1,17},{9,25},{17,1},{25,9},{2,18},{10... | collective-permute-start | bytes 1179656 | tf_op jit(solution)/shard_map/ppermute | solution.py:299
  20.6 9.9 %collective-permute-start.9 = (f32[128,512]{1,0:T(8,128)S(1)}, f32[128,512]{1,0:T(8,128)S(1)}, u32[]{:S(2)}, u32[]{:S(2)}) collective-permute-start(f32[128,512]{1,0:T(8,128)S(1)} %get-tuple-element.24.refs_7_), channel_id=1, source_target_pairs={{0,1},{1,0},{2,3},{3,2},{4,5},{5,4},{6,7},{7,6},{8,9},{9,8},{10,11... | collective-permute-start | bytes 786440 | tf_op jit(solution)/shard_map/ppermute | solution.py:299
  21.3 4.5 %collective-permute-start.5 = (f32[16,128]{1,0:T(8,128)S(1)}, f32[16,128]{1,0:T(8,128)S(1)}, u32[]{:S(2)}, u32[]{:S(2)}) collective-permute-start(f32[16,128]{1,0:T(8,128)S(1)} %get-tuple-element.23.refs_3_), channel_id=1, source_target_pairs={{0,4},{1,5},{2,6},{3,7},{4,0},{5,1},{6,2},{7,3},{8,12},{9,13},{10,... | collective-permute-start | bytes 24584 | tf_op jit(solution)/shard_map/ppermute | solution.py:299
  26.8 1.9 %collective-permute-start.6 = (f32[4,128]{1,0:T(4,128)S(1)}, f32[4,128]{1,0:T(4,128)S(1)}, u32[]{:S(2)}, u32[]{:S(2)}) collective-permute-start(f32[4,128]{1,0:T(4,128)S(1)} %shard_map.63.refs_3_), channel_id=1, source_target_pairs={{0,8},{8,0},{16,24},{24,16},{1,9},{9,1},{17,25},{25,17},{2,10},{10... | collective-permute-start | bytes 6152 | tf_op jit(solution)/shard_map/ppermute | solution.py:299
  26.9 3.7 %collective-permute-start.7 = (f32[4,128]{1,0:T(4,128)S(1)}, f32[4,128]{1,0:T(4,128)S(1)}, u32[]{:S(2)}, u32[]{:S(2)}) collective-permute-start(f32[4,128]{1,0:T(4,128)S(1)} %shard_map.63.refs_3_), channel_id=1, source_target_pairs={{0,16},{8,24},{16,0},{24,8},{1,17},{9,25},{17,1},{25,9},{2,18},{10... | collective-permute-start | bytes 6152 | tf_op jit(solution)/shard_map/ppermute | solution.py:299
  27.4 3.1 %collective-permute-start.8 = (f32[4,128]{1,0:T(4,128)S(1)}, f32[4,128]{1,0:T(4,128)S(1)}, u32[]{:S(2)}, u32[]{:S(2)}) collective-permute-start(f32[4,128]{1,0:T(4,128)S(1)} %shard_map.63.refs_3_), channel_id=1, source_target_pairs={{0,24},{8,16},{16,8},{24,0},{1,25},{9,17},{17,9},{25,1},{2,26},{10... | collective-permute-start | bytes 6152 | tf_op jit(solution)/shard_map/ppermute | solution.py:299
  31.6 3.7 %collective-permute-start.11 = (f32[16,128]{1,0:T(8,128)S(1)}, f32[16,128]{1,0:T(8,128)S(1)}, u32[]{:S(2)}, u32[]{:S(2)}) collective-permute-start(f32[16,128]{1,0:T(8,128)S(1)} %get-tuple-element.26), channel_id=1, source_target_pairs={{0,1},{1,0},{2,3},{3,2},{4,5},{5,4},{6,7},{7,6},{8,9},{9,8},{10,11... | collective-permute-start | bytes 24584 | tf_op jit(solution)/shard_map/ppermute | solution.py:299
  33.1 10.8 %collective-permute-start.14 = (f32[192,512]{1,0:T(8,128)S(1)}, f32[192,512]{1,0:T(8,128)S(1)}, u32[]{:S(2)}, u32[]{:S(2)}) collective-permute-start(f32[192,512]{1,0:T(8,128)S(1)} %get-tuple-element.27.refs_8_), channel_id=1, source_target_pairs={{0,16},{8,24},{16,0},{24,8},{1,17},{9,25},{17,1},{25,9},{2,18},{10... | collective-permute-start | bytes 1179656 | tf_op jit(solution)/shard_map/ppermute | solution.py:299
  35.4 3.7 %collective-permute-start.12 = (f32[16,128]{1,0:T(8,128)S(1)}, f32[16,128]{1,0:T(8,128)S(1)}, u32[]{:S(2)}, u32[]{:S(2)}) collective-permute-start(f32[16,128]{1,0:T(8,128)S(1)} %multiply_add_fusion.1), channel_id=1, source_target_pairs={{0,2},{1,3},{2,0},{3,1},{4,6},{5,7},{6,4},{7,5},{8,10},{9,11},{10,... | collective-permute-start | bytes 24584 | tf_op jit(solution)/shard_map/ppermute | solution.py:299
  39.1 17.6 %copy-start.3 = (bf16[512,512]{1,0:T(8,128)(2,1)S(1)}, bf16[512,512]{1,0:T(8,128)(2,1)}, u32[]{:S(2)}) copy-start(bf16[512,512]{1,0:T(8,128)(2,1)} %refs_1_.3) | copy-start | bytes 1572868
  39.1 4.6 %collective-permute-start.13 = (f32[16,128]{1,0:T(8,128)S(1)}, f32[16,128]{1,0:T(8,128)S(1)}, u32[]{:S(2)}, u32[]{:S(2)}) collective-permute-start(f32[16,128]{1,0:T(8,128)S(1)} %multiply_add_fusion.refs_4_), channel_id=1, source_target_pairs={{0,4},{1,5},{2,6},{3,7},{4,0},{5,1},{6,2},{7,3},{8,12},{9,13},{10,... | collective-permute-start | bytes 24584 | tf_op jit(solution)/shard_map/ppermute | solution.py:299
  46.1 10.6 %collective-permute-start.15 = (f32[3,2,128,512]{3,2,1,0:T(8,128)S(1)}, f32[3,2,128,512]{3,2,1,0:T(8,128)S(1)}, u32[]{:S(2)}, u32[]{:S(2)}) collective-permute-start(f32[3,2,128,512]{3,2,1,0:T(8,128)S(1)} %get-tuple-element.28.refs_2_), channel_id=1, source_target_pairs={{0,8},{8,0},{16,24},{24,16},{1,9},{9,1},{17,25},{25,17},{2,10},{10... | collective-permute-start | bytes 4718600 | tf_op jit(solution)/shard_map/ppermute | solution.py:299
  46.2 11.9 %collective-permute-start.21 = (f32[256,512]{1,0:T(8,128)S(1)}, f32[256,512]{1,0:T(8,128)S(1)}, u32[]{:S(2)}, u32[]{:S(2)}) collective-permute-start(f32[256,512]{1,0:T(8,128)S(1)} %get-tuple-element.33), channel_id=1, source_target_pairs={{0,8},{8,0},{16,24},{24,16},{1,9},{9,1},{17,25},{25,17},{2,10},{10... | collective-permute-start | bytes 1572872 | tf_op jit(solution)/shard_map/ppermute | solution.py:299
  46.7 3.0 %collective-permute-start.18 = (f32[4,128]{1,0:T(4,128)S(1)}, f32[4,128]{1,0:T(4,128)S(1)}, u32[]{:S(2)}, u32[]{:S(2)}) collective-permute-start(f32[4,128]{1,0:T(4,128)S(1)} %get-tuple-element.31.lse_ref), channel_id=1, source_target_pairs={{0,24},{8,16},{16,8},{24,0},{1,25},{9,17},{17,9},{25,1},{2,26},{10... | collective-permute-start | bytes 6152 | tf_op jit(solution)/shard_map/ppermute | solution.py:299
  47.9 3.6 %collective-permute-start.17 = (f32[4,128]{1,0:T(4,128)S(1)}, f32[4,128]{1,0:T(4,128)S(1)}, u32[]{:S(2)}, u32[]{:S(2)}) collective-permute-start(f32[4,128]{1,0:T(4,128)S(1)} %get-tuple-element.31.lse_ref), channel_id=1, source_target_pairs={{0,16},{8,24},{16,0},{24,8},{1,17},{9,25},{17,1},{25,9},{2,18},{10... | collective-permute-start | bytes 6152 | tf_op jit(solution)/shard_map/ppermute | solution.py:299
  48.4 3.1 %collective-permute-start.16 = (f32[4,128]{1,0:T(4,128)S(1)}, f32[4,128]{1,0:T(4,128)S(1)}, u32[]{:S(2)}, u32[]{:S(2)}) collective-permute-start(f32[4,128]{1,0:T(4,128)S(1)} %get-tuple-element.31.lse_ref), channel_id=1, source_target_pairs={{0,8},{8,0},{16,24},{24,16},{1,9},{9,1},{17,25},{25,17},{2,10},{10... | collective-permute-start | bytes 6152 | tf_op jit(solution)/shard_map/ppermute | solution.py:299
  51.5 3.7 %collective-permute-start.19 = (f32[1,4,128]{2,1,0:T(4,128)S(1)}, f32[1,4,128]{2,1,0:T(4,128)S(1)}, u32[]{:S(2)}, u32[]{:S(2)}) collective-permute-start(f32[1,4,128]{2,1,0:T(4,128)S(1)} %get-tuple-element.38), channel_id=1, source_target_pairs={{0,1},{1,0},{2,3},{3,2},{4,5},{5,4},{6,7},{7,6},{8,9},{9,8},{10,11... | collective-permute-start | bytes 6152 | tf_op jit(solution)/shard_map/ppermute | solution.py:299
  55.1 4.5 %collective-permute-start.20 = (f32[2,4,128]{2,1,0:T(4,128)S(1)}, f32[2,4,128]{2,1,0:T(4,128)S(1)}, u32[]{:S(2)}, u32[]{:S(2)}) collective-permute-start(f32[2,4,128]{2,1,0:T(4,128)S(1)} %pad_maximum_fusion.1), channel_id=1, source_target_pairs={{0,4},{1,5},{2,6},{3,7},{4,0},{5,1},{6,2},{7,3},{8,12},{9,13},{10,... | collective-permute-start | bytes 12296 | tf_op jit(solution)/shard_map/ppermute | solution.py:299
  58.4 11.8 %collective-permute-start.22 = (f32[256,512]{1,0:T(8,128)S(1)}, f32[256,512]{1,0:T(8,128)S(1)}, u32[]{:S(2)}, u32[]{:S(2)}) collective-permute-start(f32[256,512]{1,0:T(8,128)S(1)} %shard_map.67.one_ref), channel_id=1, source_target_pairs={{0,16},{8,24},{16,0},{24,8},{1,17},{9,25},{17,1},{25,9},{2,18},{10... | collective-permute-start | bytes 1572872 | tf_op jit(solution)/shard_map/ppermute | solution.py:299
  60.5 13.8 %collective-permute-start.27 = (f32[264,512]{1,0:T(8,128)S(1)}, f32[264,512]{1,0:T(8,128)S(1)}, u32[]{:S(2)}, u32[]{:S(2)}) collective-permute-start(f32[264,512]{1,0:T(8,128)S(1)} %shard_map.70), channel_id=1, source_target_pairs={{0,2},{1,3},{2,0},{3,1},{4,6},{5,7},{6,4},{7,5},{8,10},{9,11},{10,... | collective-permute-start | bytes 1622024 | tf_op jit(solution)/shard_map/ppermute | solution.py:299
  70.2 1.4 %collective-permute-start.23 = (f32[64,512]{1,0:T(8,128)S(1)}, f32[64,512]{1,0:T(8,128)S(1)}, u32[]{:S(2)}, u32[]{:S(2)}) collective-permute-start(f32[64,512]{1,0:T(8,128)S(1)} %get-tuple-element.34.refs_0_), channel_id=1, source_target_pairs={{0,8},{8,0},{16,24},{24,16},{1,9},{9,1},{17,25},{25,17},{2,10},{10... | collective-permute-start | bytes 393224 | tf_op jit(solution)/shard_map/ppermute | solution.py:299
  70.3 1.5 %collective-permute-start.24 = (f32[64,512]{1,0:T(8,128)S(1)}, f32[64,512]{1,0:T(8,128)S(1)}, u32[]{:S(2)}, u32[]{:S(2)}) collective-permute-start(f32[64,512]{1,0:T(8,128)S(1)} %get-tuple-element.35.refs_1_), channel_id=1, source_target_pairs={{0,8},{8,0},{16,24},{24,16},{1,9},{9,1},{17,25},{25,17},{2,10},{10... | collective-permute-start | bytes 393224 | tf_op jit(solution)/shard_map/ppermute | solution.py:299
  70.8 1.3 %collective-permute-start.25 = (f32[64,512]{1,0:T(8,128)S(1)}, f32[64,512]{1,0:T(8,128)S(1)}, u32[]{:S(2)}, u32[]{:S(2)}) collective-permute-start(f32[64,512]{1,0:T(8,128)S(1)} %get-tuple-element.36.refs_2_), channel_id=1, source_target_pairs={{0,8},{8,0},{16,24},{24,16},{1,9},{9,1},{17,25},{25,17},{2,10},{10... | collective-permute-start | bytes 393224 | tf_op jit(solution)/shard_map/ppermute | solution.py:299
  70.9 1.5 %collective-permute-start.26 = (f32[64,512]{1,0:T(8,128)S(1)}, f32[64,512]{1,0:T(8,128)S(1)}, u32[]{:S(2)}, u32[]{:S(2)}) collective-permute-start(f32[64,512]{1,0:T(8,128)S(1)} %get-tuple-element.37.refs_3_), channel_id=1, source_target_pairs={{0,8},{8,0},{16,24},{24,16},{1,9},{9,1},{17,25},{25,17},{2,10},{10... | collective-permute-start | bytes 393224 | tf_op jit(solution)/shard_map/ppermute | solution.py:299

commit v17 on v8

--- a/solution.py
+++ b/solution.py
@@ -262,13 +262,12 @@
     for k, bias_ref in enumerate(bias_refs[::-1]):
         at = pl.ds(k * n_tgt, n_tgt)
         scores = inner_ref[block, at] + to_row(bias_ref[...])
-        scores_ref[:, at] = scores
         peak = jnp.maximum(peak, jnp.max(scores, axis=1, keepdims=True))
     total = jnp.zeros((rows, 1), jnp.float32)
     numer = jnp.zeros((rows, y_ref.shape[1]), jnp.float32)
-    for k in range(n_shards):
+    for k, bias_ref in enumerate(bias_refs[::-1]):
         at = pl.ds(k * n_tgt, n_tgt)
-        plan = jnp.exp2(scores_ref[:, at] - peak)
+        plan = jnp.exp2(inner_ref[block, at] + to_row(bias_ref[...]) - peak)
         total = total + jnp.sum(plan, axis=1, keepdims=True)
         numer = numer + jnp.dot(plan.astype(jnp.bfloat16), y_ref[at, :], preferred_element_type=jnp.float32)
     return numer, total, peak

time: 74.2 us -> 74.2 us (level)
  no operation moved by 1% of the time
where the time goes in v17:
time: 74.2 us; the launch traced here: 74 us
  starting transfers between devices  29 us (39%)
  waiting for transfers between devices  28.5 us (38%)
  Pallas kernels  12.3 us (17%)
  local copies, waits for them, and re-layouts  3.32 us (4%)
  between operations  0.79 us (1%)
    ppermute x29, starting transfers between devices, swap(): return lax.ppermute(value, axis, [(i, i ^ distance) for i in range(n)])  29 us
    ppermute x29, waiting for transfers between devices, swap(): return lax.ppermute(value, axis, [(i, i ^ distance) for i in range(n)])  28.5 us
    pallas_call x14, Pallas kernels, call(): pl.pallas_call(kernel, out_shape=out_shape, in_specs=in_specs or [VMEM] *...  12.3 us
    unnamed x12, local copies, waits for them, and re-layouts  3.32 us
  transfers between devices with their start and end apart: 29, of which 17 were waited for; matrix products, arithmetic and copies ran while one was open for 0% of the time, Pallas kernels for 11%

profile of v17, /device:TPU:0, one launch (start us, length us, event | category | flops | bytes accessed | tf_op | source)
XLA Modules:
  0.0 74.0 jit_solution(903868867702472412)
XLA Ops:
  0.6 0.0 copy-start.2
  0.6 1.0 %copy-done.2 = bf16[512,512]{1,0:T(8,128)(2,1)S(1)} copy-done((bf16[512,512]{1,0:T(8,128)(2,1)S(1)}, bf16[512,512]{1,0:T(8,128)(2,1)}, u32[]{:S(2)}) %copy-start.2) | copy-done | bytes 524312
  1.7 4.1 %collective-permute-start.3 = (f32[128,512]{1,0:T(8,128)S(1)}, f32[128,512]{1,0:T(8,128)S(1)}, u32[]{:S(2)}, u32[]{:S(2)}) collective-permute-start(f32[128,512]{1,0:T(8,128)S(1)} %shard_map.61), channel_id=1, source_target_pairs={{0,4},{1,5},{2,6},{3,7},{4,0},{5,1},{6,2},{7,3},{8,12},{9,13},{10,... | collective-permute-start | bytes 786440 | tf_op jit(solution)/shard_map/ppermute | solution.py:298
  5.8 1.5 %collective-permute-start.4 = (f32[128,512]{1,0:T(8,128)S(1)}, f32[128,512]{1,0:T(8,128)S(1)}, u32[]{:S(2)}, u32[]{:S(2)}) collective-permute-start(f32[128,512]{1,0:T(8,128)S(1)} %shard_map.61), channel_id=1, source_target_pairs={{0,1},{1,0},{2,3},{3,2},{4,5},{5,4},{6,7},{7,6},{8,9},{9,8},{10,11... | collective-permute-start | bytes 786440 | tf_op jit(solution)/shard_map/ppermute | solution.py:298
  7.3 1.6 %copy-done = bf16[2048,512]{1,0:T(8,128)(2,1)S(1)} copy-done((bf16[2048,512]{1,0:T(8,128)(2,1)S(1)}, bf16[2048,512]{1,0:T(8,128)(2,1)}, u32[]{:S(2)}) %copy-start) | copy-done | bytes 2097176
  8.9 0.7 copy-done.5
  9.6 1.9 %shard_map.59 = (f32[512,2048]{1,0:T(8,128)S(1)}, f32[16,128]{1,0:T(8,128)S(1)}, f32[4,128]{1,0:T(4,128)S(1)}) custom-call(bf16[512,512]{1,0:T(8,128)(2,1)S(1)} %copy-done.2, bf16[2048,512]{1,0:T(8,128)(2,1)S(1)} %copy-done, f32[4,128]{1,0:T(4,128)S(1)} %bitcast.5), custom_call_target="tpu_custom_call" | custom-call | tf_op jit(solution)/shard_map/pallas_call | solution.py:22
  11.5 1.6 %collective-permute-start = (f32[16,128]{1,0:T(8,128)S(1)}, f32[16,128]{1,0:T(8,128)S(1)}, u32[]{:S(2)}, u32[]{:S(2)}) collective-permute-start(f32[16,128]{1,0:T(8,128)S(1)} %get-tuple-element.22.refs_0_), channel_id=1, source_target_pairs={{0,3},{1,2},{2,1},{3,0},{4,7},{5,6},{6,5},{7,4},{8,11},{9,10},{10,... | collective-permute-start | bytes 24584 | tf_op jit(solution)/shard_map/ppermute | solution.py:298
  13.1 0.4 collective-permute-start.1
  13.5 1.5 %collective-permute-start.2 = (f32[16,128]{1,0:T(8,128)S(1)}, f32[16,128]{1,0:T(8,128)S(1)}, u32[]{:S(2)}, u32[]{:S(2)}) collective-permute-start(f32[16,128]{1,0:T(8,128)S(1)} %get-tuple-element.22.refs_0_), channel_id=1, source_target_pairs={{0,1},{1,0},{2,3},{3,2},{4,5},{5,4},{6,7},{7,6},{8,9},{9,8},{10,11... | collective-permute-start | bytes 24584 | tf_op jit(solution)/shard_map/ppermute | solution.py:298
  15.0 3.9 %collective-permute-done.refs_1_ = f32[16,128]{1,0:T(8,128)S(1)} collective-permute-done((f32[16,128]{1,0:T(8,128)S(1)}, f32[16,128]{1,0:T(8,128)S(1)}, u32[]{:S(2)}, u32[]{:S(2)}) %collective-permute-start) | collective-permute-done | bytes 8224 | tf_op jit(solution)/shard_map/ppermute | solution.py:298
  19.0 0.0 collective-permute-done.2.refs_3_
  19.0 0.0 collective-permute-done.3.refs_4_
  19.0 1.6 %collective-permute-start.10 = (f32[192,512]{1,0:T(8,128)S(1)}, f32[192,512]{1,0:T(8,128)S(1)}, u32[]{:S(2)}, u32[]{:S(2)}) collective-permute-start(f32[192,512]{1,0:T(8,128)S(1)} %get-tuple-element.25.refs_6_), channel_id=1, source_target_pairs={{0,16},{8,24},{16,0},{24,8},{1,17},{9,25},{17,1},{25,9},{2,18},{10... | collective-permute-start | bytes 1179656 | tf_op jit(solution)/shard_map/ppermute | solution.py:298
  20.6 0.6 collective-permute-start.9
  21.3 0.5 shard_map.60.refs_2_.refs_3_
  21.8 4.0 %collective-permute-done.5.refs_4_ = f32[16,128]{1,0:T(8,128)S(1)} collective-permute-done((f32[16,128]{1,0:T(8,128)S(1)}, f32[16,128]{1,0:T(8,128)S(1)}, u32[]{:S(2)}, u32[]{:S(2)}) %collective-permute-start.5) | collective-permute-done | bytes 8224 | tf_op jit(solution)/shard_map/ppermute | solution.py:298
  25.8 1.0 %shard_map.63.refs_3_ = f32[4,128]{1,0:T(4,128)S(1)} custom-call(f32[512,2048]{1,0:T(8,128)S(1)} %get-tuple-element.20.refs_0_, f32[16,128]{1,0:T(8,128)S(1)} %bitcast.3, f32[16,128]{1,0:T(8,128)S(1)} %shard_map.60.refs_2_.refs_3_, f32[16,128]{1,0:T(8,128)S(1)} %get-tuple-element.23.refs_3_, f32[16,128]{1,0:T(8,128)S(1)} %collective-permute-done.5.refs_4_), custom_call_target="tpu_custom_call" | custom-call | tf_op jit(solution)/shard_map/pallas_call | solution.py:22
  26.8 0.0 collective-permute-start.6
  26.9 0.6 collective-permute-start.7
  27.4 1.3 %collective-permute-start.8 = (f32[4,128]{1,0:T(4,128)S(1)}, f32[4,128]{1,0:T(4,128)S(1)}, u32[]{:S(2)}, u32[]{:S(2)}) collective-permute-start(f32[4,128]{1,0:T(4,128)S(1)} %shard_map.63.refs_3_), channel_id=1, source_target_pairs={{0,24},{8,16},{16,8},{24,0},{1,25},{9,17},{17,9},{25,1},{2,26},{10... | collective-permute-start | bytes 6152 | tf_op jit(solution)/shard_map/ppermute | solution.py:298
  28.7 1.8 %collective-permute-done.7.refs_5_ = f32[4,128]{1,0:T(4,128)S(1)} collective-permute-done((f32[4,128]{1,0:T(4,128)S(1)}, f32[4,128]{1,0:T(4,128)S(1)}, u32[]{:S(2)}, u32[]{:S(2)}) %collective-permute-start.7) | collective-permute-done | bytes 2080 | tf_op jit(solution)/shard_map/ppermute | solution.py:298
  30.5 1.1 %shard_map.64 = (f32[16,128]{1,0:T(8,128)S(1)}, f32[192,512]{1,0:T(8,128)S(1)}) custom-call(f32[512,2048]{1,0:T(8,128)S(1)} %get-tuple-element.20.refs_0_, f32[4,128]{1,0:T(4,128)S(1)} %bitcast.6, f32[4,128]{1,0:T(4,128)S(1)} %get-tuple-element.21.refs_2_, f32[4,128]{1,0:T(4,128)S(1)} %shard_map.63.refs_3_, f32[4,128]{1,0:T(4,128)S(1)} %collective-permute-done.6.refs_4_, ...), custom_call_target="tpu_custom_call" | custom-call | tf_op jit(solution)/shard_map/pallas_call | solution.py:22
  31.7 1.4 %collective-permute-start.11 = (f32[16,128]{1,0:T(8,128)S(1)}, f32[16,128]{1,0:T(8,128)S(1)}, u32[]{:S(2)}, u32[]{:S(2)}) collective-permute-start(f32[16,128]{1,0:T(8,128)S(1)} %get-tuple-element.26), channel_id=1, source_target_pairs={{0,1},{1,0},{2,3},{3,2},{4,5},{5,4},{6,7},{7,6},{8,9},{9,8},{10,11... | collective-permute-start | bytes 24584 | tf_op jit(solution)/shard_map/ppermute | solution.py:298
  33.1 1.4 %collective-permute-start.14 = (f32[192,512]{1,0:T(8,128)S(1)}, f32[192,512]{1,0:T(8,128)S(1)}, u32[]{:S(2)}, u32[]{:S(2)}) collective-permute-start(f32[192,512]{1,0:T(8,128)S(1)} %get-tuple-element.27.refs_8_), channel_id=1, source_target_pairs={{0,16},{8,24},{16,0},{24,8},{1,17},{9,25},{17,1},{25,9},{2,18},{10... | collective-permute-start | bytes 1179656 | tf_op jit(solution)/shard_map/ppermute | solution.py:298
  34.5 0.8 %collective-permute-done.11 = f32[16,128]{1,0:T(8,128)S(1)} collective-permute-done((f32[16,128]{1,0:T(8,128)S(1)}, f32[16,128]{1,0:T(8,128)S(1)}, u32[]{:S(2)}, u32[]{:S(2)}) %collective-permute-start.11) | collective-permute-done | bytes 8224 | tf_op jit(solution)/shard_map/ppermute | solution.py:298
  35.4 1.0 %collective-permute-start.12 = (f32[16,128]{1,0:T(8,128)S(1)}, f32[16,128]{1,0:T(8,128)S(1)}, u32[]{:S(2)}, u32[]{:S(2)}) collective-permute-start(f32[16,128]{1,0:T(8,128)S(1)} %multiply_add_fusion.1), channel_id=1, source_target_pairs={{0,2},{1,3},{2,0},{3,1},{4,6},{5,7},{6,4},{7,5},{8,10},{9,11},{10,... | collective-permute-start | bytes 24584 | tf_op jit(solution)/shard_map/ppermute | solution.py:298
  36.4 2.7 %collective-permute-done.12 = f32[16,128]{1,0:T(8,128)S(1)} collective-permute-done((f32[16,128]{1,0:T(8,128)S(1)}, f32[16,128]{1,0:T(8,128)S(1)}, u32[]{:S(2)}, u32[]{:S(2)}) %collective-permute-start.12) | collective-permute-done | bytes 8224 | tf_op jit(solution)/shard_map/ppermute | solution.py:298
  39.1 0.0 copy-start.3
  39.1 1.9 %collective-permute-start.13 = (f32[16,128]{1,0:T(8,128)S(1)}, f32[16,128]{1,0:T(8,128)S(1)}, u32[]{:S(2)}, u32[]{:S(2)}) collective-permute-start(f32[16,128]{1,0:T(8,128)S(1)} %multiply_add_fusion.refs_4_), channel_id=1, source_target_pairs={{0,4},{1,5},{2,6},{3,7},{4,0},{5,1},{6,2},{7,3},{8,12},{9,13},{10,... | collective-permute-start | bytes 24584 | tf_op jit(solution)/shard_map/ppermute | solution.py:298
  41.1 2.7 %collective-permute-done.13.refs_5_ = f32[16,128]{1,0:T(8,128)S(1)} collective-permute-done((f32[16,128]{1,0:T(8,128)S(1)}, f32[16,128]{1,0:T(8,128)S(1)}, u32[]{:S(2)}, u32[]{:S(2)}) %collective-permute-start.13) | collective-permute-done | bytes 8224 | tf_op jit(solution)/shard_map/ppermute | solution.py:298
  43.7 0.2 collective-permute-done.14.refs_9_
  43.9 2.1 %shard_map.65 = (f32[4,128]{1,0:T(4,128)S(1)}, f32[256,512]{1,0:T(8,128)S(1)}, f32[256,512]{1,0:T(8,128)S(1)}, f32[3,2,128,512]{3,2,1,0:T(8,128)S(1)}) custom-call(f32[512,2048]{1,0:T(8,128)S(1)} %get-tuple-element.20.refs_0_, bf16[2048,512]{1,0:T(8,128)(2,1)S(1)} %copy-done.1, f32[16,128]{1,0:T(8,128)S(1)} %bitcast.4, ...), custom_call_target="tpu_custom_call" | custom-call | tf_op jit(solution)/shard_map/pallas_call | solution.py:22
  46.1 0.1 collective-permute-start.15
  46.2 0.5 collective-permute-start.23
  46.7 1.2 %collective-permute-start.18 = (f32[4,128]{1,0:T(4,128)S(1)}, f32[4,128]{1,0:T(4,128)S(1)}, u32[]{:S(2)}, u32[]{:S(2)}) collective-permute-start(f32[4,128]{1,0:T(4,128)S(1)} %get-tuple-element.31.lse_ref), channel_id=1, source_target_pairs={{0,24},{8,16},{16,8},{24,0},{1,25},{9,17},{17,9},{25,1},{2,26},{10... | collective-permute-start | bytes 6152 | tf_op jit(solution)/shard_map/ppermute | solution.py:298
  47.9 0.5 collective-permute-start.17
  48.4 0.2 collective-permute-start.16
  48.5 1.1 %collective-permute-done.18 = f32[4,128]{1,0:T(4,128)S(1)} collective-permute-done((f32[4,128]{1,0:T(4,128)S(1)}, f32[4,128]{1,0:T(4,128)S(1)}, u32[]{:S(2)}, u32[]{:S(2)}) %collective-permute-start.18) | collective-permute-done | bytes 2080 | tf_op jit(solution)/shard_map/ppermute | solution.py:298
  49.7 1.8 %collective-permute-done.17 = f32[4,128]{1,0:T(4,128)S(1)} collective-permute-done((f32[4,128]{1,0:T(4,128)S(1)}, f32[4,128]{1,0:T(4,128)S(1)}, u32[]{:S(2)}, u32[]{:S(2)}) %collective-permute-start.17) | collective-permute-done | bytes 2080 | tf_op jit(solution)/shard_map/ppermute | solution.py:298
  51.5 0.3 shard_map.70.one_ref
  51.8 0.6 collective-permute-start.24
  52.4 1.6 %collective-permute-start.19 = (f32[4,128]{1,0:T(4,128)S(1)}, f32[4,128]{1,0:T(4,128)S(1)}, u32[]{:S(2)}, u32[]{:S(2)}) collective-permute-start(f32[4,128]{1,0:T(4,128)S(1)} %get-tuple-element.38.refs_5_), channel_id=1, source_target_pairs={{0,5},{1,4},{2,7},{3,6},{4,1},{5,0},{6,3},{7,2},{8,13},{9,12},{10,... | collective-permute-start | bytes 6152 | tf_op jit(solution)/shard_map/ppermute | solution.py:298
  54.0 1.9 %collective-permute-start.20 = (f32[4,128]{1,0:T(4,128)S(1)}, f32[4,128]{1,0:T(4,128)S(1)}, u32[]{:S(2)}, u32[]{:S(2)}) collective-permute-start(f32[4,128]{1,0:T(4,128)S(1)} %get-tuple-element.38.refs_5_), channel_id=1, source_target_pairs={{0,4},{1,5},{2,6},{3,7},{4,0},{5,1},{6,2},{7,3},{8,12},{9,13},{10,... | collective-permute-start | bytes 6152 | tf_op jit(solution)/shard_map/ppermute | solution.py:298
  55.9 0.8 %collective-permute-start.21 = (f32[4,128]{1,0:T(4,128)S(1)}, f32[4,128]{1,0:T(4,128)S(1)}, u32[]{:S(2)}, u32[]{:S(2)}) collective-permute-start(f32[4,128]{1,0:T(4,128)S(1)} %get-tuple-element.38.refs_5_), channel_id=1, source_target_pairs={{0,1},{1,0},{2,3},{3,2},{4,5},{5,4},{6,7},{7,6},{8,9},{9,8},{10,11... | collective-permute-start | bytes 6152 | tf_op jit(solution)/shard_map/ppermute | solution.py:298
  56.8 1.3 %shard_map.66 = (bf16[2048,512]{1,0:T(8,128)(2,1)S(1)}, f32[512,2048]{1,0:T(8,128)S(1)}) custom-call(bf16[2048,512]{1,0:T(8,128)(2,1)S(1)} %copy-done.1, bf16[512,512]{1,0:T(8,128)(2,1)S(1)} %copy-done.3, f32[3,2,128,512]{3,2,1,0:T(8,128)S(1)} %get-tuple-element.28.refs_2_, f32[3,2,128,512]{3,2,1,0:T(8,128)S(1)} %collective-permute-done.15.refs_3_), custom_call_target="tpu_custom_call" | custom-call | tf_op jit(solution)/shard_map/pallas_call | solution.py:22
  58.1 0.4 collective-permute-done.20.refs_3_
  58.5 1.0 %collective-permute-done.21.refs_4_ = f32[4,128]{1,0:T(4,128)S(1)} collective-permute-done((f32[4,128]{1,0:T(4,128)S(1)}, f32[4,128]{1,0:T(4,128)S(1)}, u32[]{:S(2)}, u32[]{:S(2)}) %collective-permute-start.21) | collective-permute-done | bytes 2080 | tf_op jit(solution)/shard_map/ppermute | solution.py:298
  59.5 0.9 %shard_map.68 = f32[264,512]{1,0:T(8,128)S(1)} custom-call(f32[512,2048]{1,0:T(8,128)S(1)} %get-tuple-element.29.refs_0_, bf16[2048,512]{1,0:T(8,128)(2,1)S(1)} %get-tuple-element.30.refs_1_, f32[4,128]{1,0:T(4,128)S(1)} %collective-permute-done.19.refs_2_, f32[4,128]{1,0:T(4,128)S(1)} %collective-permute-done.20.refs_3_, ...), custom_call_target="tpu_custom_call" | custom-call | tf_op jit(solution)/shard_map/pallas_call | solution.py:22
  60.4 1.4 %collective-permute-start.22 = (f32[264,512]{1,0:T(8,128)S(1)}, f32[264,512]{1,0:T(8,128)S(1)}, u32[]{:S(2)}, u32[]{:S(2)}) collective-permute-start(f32[264,512]{1,0:T(8,128)S(1)} %shard_map.68), channel_id=1, source_target_pairs={{0,2},{1,3},{2,0},{3,1},{4,6},{5,7},{6,4},{7,5},{8,10},{9,11},{10,... | collective-permute-start | bytes 1622024 | tf_op jit(solution)/shard_map/ppermute | solution.py:298
  61.8 3.2 %collective-permute-done.24.two_ref = f32[256,512]{1,0:T(8,128)S(1)} collective-permute-done((f32[256,512]{1,0:T(8,128)S(1)}, f32[256,512]{1,0:T(8,128)S(1)}, u32[]{:S(2)}, u32[]{:S(2)}) %collective-permute-start.24) | collective-permute-done | bytes 524320 | tf_op jit(solution)/shard_map/ppermute | solution.py:298
  65.0 0.1 shard_map.71
  65.0 0.1 collective-permute-start.25
  65.1 0.5 collective-permute-start.26
  65.6 0.1 collective-permute-start.27
  65.7 0.4 collective-permute-start.28
  66.1 0.3 collective-permute-done.25.refs_4_
  66.5 0.2 collective-permute-done.26.refs_5_
  66.7 0.3 collective-permute-done.27.refs_6_
  67.0 0.2 collective-permute-done.28.refs_7_
  67.2 1.0 %shard_map.72 = f32[512,512]{1,0:T(8,128)} custom-call(f32[64,512]{1,0:T(8,128)S(1)} %get-tuple-element.34.refs_0_, f32[64,512]{1,0:T(8,128)S(1)} %get-tuple-element.35.refs_1_, f32[64,512]{1,0:T(8,128)S(1)} %get-tuple-element.36.refs_2_, f32[64,512]{1,0:T(8,128)S(1)} %get-tuple-element.37.refs_3_, f32[64,512]{1,0:T(8,128)S(1)} %collective-permute-done.25.refs_4_, ...), custom_call_target="tpu_custom_call" | custom-call | tf_op jit(solution)/shard_map/pallas_call | solution.py:22
  68.2 0.9 %shard_map.67.refs_0_ = f32[264,512]{1,0:T(8,128)S(1)} custom-call(f32[512,2048]{1,0:T(8,128)S(1)} %get-tuple-element.29.refs_0_, bf16[2048,512]{1,0:T(8,128)(2,1)S(1)} %get-tuple-element.30.refs_1_, f32[4,128]{1,0:T(4,128)S(1)} %collective-permute-done.19.refs_2_, f32[4,128]{1,0:T(4,128)S(1)} %collective-permute-done.20.refs_3_, ...), custom_call_target="tpu_custom_call" | custom-call | tf_op jit(solution)/shard_map/pallas_call | solution.py:22
  69.1 3.8 %collective-permute-done.22.refs_1_ = f32[264,512]{1,0:T(8,128)S(1)} collective-permute-done((f32[264,512]{1,0:T(8,128)S(1)}, f32[264,512]{1,0:T(8,128)S(1)}, u32[]{:S(2)}, u32[]{:S(2)}) %collective-permute-start.22) | collective-permute-done | bytes 540704 | tf_op jit(solution)/shard_map/ppermute | solution.py:298
  72.9 1.1 %shard_map.69 = f32[256,512]{1,0:T(8,128)} custom-call(f32[264,512]{1,0:T(8,128)S(1)} %shard_map.67.refs_0_, f32[264,512]{1,0:T(8,128)S(1)} %collective-permute-done.22.refs_1_), custom_call_target="tpu_custom_call" | custom-call | tf_op jit(solution)/shard_map/pallas_call | solution.py:22
  (23 shorter events, 0.2 us)
Async XLA Ops:
  0.6 1.0 %copy-start.2 = (bf16[512,512]{1,0:T(8,128)(2,1)S(1)}, bf16[512,512]{1,0:T(8,128)(2,1)}, u32[]{:S(2)}) copy-start(bf16[512,512]{1,0:T(8,128)(2,1)} %refs_1_.3) | copy-start | bytes 1572868
  1.7 17.3 %collective-permute-start.3 = (f32[128,512]{1,0:T(8,128)S(1)}, f32[128,512]{1,0:T(8,128)S(1)}, u32[]{:S(2)}, u32[]{:S(2)}) collective-permute-start(f32[128,512]{1,0:T(8,128)S(1)} %shard_map.61), channel_id=1, source_target_pairs={{0,4},{1,5},{2,6},{3,7},{4,0},{5,1},{6,2},{7,3},{8,12},{9,13},{10,... | collective-permute-start | bytes 786440 | tf_op jit(solution)/shard_map/ppermute | solution.py:298
  5.8 13.2 %collective-permute-start.4 = (f32[128,512]{1,0:T(8,128)S(1)}, f32[128,512]{1,0:T(8,128)S(1)}, u32[]{:S(2)}, u32[]{:S(2)}) collective-permute-start(f32[128,512]{1,0:T(8,128)S(1)} %shard_map.61), channel_id=1, source_target_pairs={{0,1},{1,0},{2,3},{3,2},{4,5},{5,4},{6,7},{7,6},{8,9},{9,8},{10,11... | collective-permute-start | bytes 786440 | tf_op jit(solution)/shard_map/ppermute | solution.py:298
  7.3 1.6 %copy-start = (bf16[2048,512]{1,0:T(8,128)(2,1)S(1)}, bf16[2048,512]{1,0:T(8,128)(2,1)}, u32[]{:S(2)}) copy-start(bf16[2048,512]{1,0:T(8,128)(2,1)} %refs_0_.1) | copy-start | bytes 6291460
  8.9 0.7 copy-start.5
  9.6 11.7 %copy-start.1 = (bf16[2048,512]{1,0:T(8,128)(2,1)S(1)}, bf16[2048,512]{1,0:T(8,128)(2,1)}, u32[]{:S(2)}) copy-start(bf16[2048,512]{1,0:T(8,128)(2,1)} %refs_0_.1) | copy-start | bytes 6291460
  9.6 16.3 %copy-start.4 = (f32[2048]{0:T(1024)S(1)}, f32[2048]{0:T(1024)}, u32[]{:S(2)}) copy-start(f32[2048]{0:T(1024)} %param.6) | copy-start | bytes 24580
  11.5 7.5 %collective-permute-start = (f32[16,128]{1,0:T(8,128)S(1)}, f32[16,128]{1,0:T(8,128)S(1)}, u32[]{:S(2)}, u32[]{:S(2)}) collective-permute-start(f32[16,128]{1,0:T(8,128)S(1)} %get-tuple-element.22.refs_0_), channel_id=1, source_target_pairs={{0,3},{1,2},{2,1},{3,0},{4,7},{5,6},{6,5},{7,4},{8,11},{9,10},{10,... | collective-permute-start | bytes 24584 | tf_op jit(solution)/shard_map/ppermute | solution.py:298
  13.1 5.9 %collective-permute-start.1 = (f32[16,128]{1,0:T(8,128)S(1)}, f32[16,128]{1,0:T(8,128)S(1)}, u32[]{:S(2)}, u32[]{:S(2)}) collective-permute-start(f32[16,128]{1,0:T(8,128)S(1)} %get-tuple-element.22.refs_0_), channel_id=1, source_target_pairs={{0,2},{1,3},{2,0},{3,1},{4,6},{5,7},{6,4},{7,5},{8,10},{9,11},{10,... | collective-permute-start | bytes 24584 | tf_op jit(solution)/shard_map/ppermute | solution.py:298
  13.5 5.4 %collective-permute-start.2 = (f32[16,128]{1,0:T(8,128)S(1)}, f32[16,128]{1,0:T(8,128)S(1)}, u32[]{:S(2)}, u32[]{:S(2)}) collective-permute-start(f32[16,128]{1,0:T(8,128)S(1)} %get-tuple-element.22.refs_0_), channel_id=1, source_target_pairs={{0,1},{1,0},{2,3},{3,2},{4,5},{5,4},{6,7},{7,6},{8,9},{9,8},{10,11... | collective-permute-start | bytes 24584 | tf_op jit(solution)/shard_map/ppermute | solution.py:298
  19.0 11.5 %collective-permute-start.10 = (f32[192,512]{1,0:T(8,128)S(1)}, f32[192,512]{1,0:T(8,128)S(1)}, u32[]{:S(2)}, u32[]{:S(2)}) collective-permute-start(f32[192,512]{1,0:T(8,128)S(1)} %get-tuple-element.25.refs_6_), channel_id=1, source_target_pairs={{0,16},{8,24},{16,0},{24,8},{1,17},{9,25},{17,1},{25,9},{2,18},{10... | collective-permute-start | bytes 1179656 | tf_op jit(solution)/shard_map/ppermute | solution.py:298
  20.6 9.9 %collective-permute-start.9 = (f32[128,512]{1,0:T(8,128)S(1)}, f32[128,512]{1,0:T(8,128)S(1)}, u32[]{:S(2)}, u32[]{:S(2)}) collective-permute-start(f32[128,512]{1,0:T(8,128)S(1)} %get-tuple-element.24.refs_7_), channel_id=1, source_target_pairs={{0,1},{1,0},{2,3},{3,2},{4,5},{5,4},{6,7},{7,6},{8,9},{9,8},{10,11... | collective-permute-start | bytes 786440 | tf_op jit(solution)/shard_map/ppermute | solution.py:298
  21.3 4.5 %collective-permute-start.5 = (f32[16,128]{1,0:T(8,128)S(1)}, f32[16,128]{1,0:T(8,128)S(1)}, u32[]{:S(2)}, u32[]{:S(2)}) collective-permute-start(f32[16,128]{1,0:T(8,128)S(1)} %get-tuple-element.23.refs_3_), channel_id=1, source_target_pairs={{0,4},{1,5},{2,6},{3,7},{4,0},{5,1},{6,2},{7,3},{8,12},{9,13},{10,... | collective-permute-start | bytes 24584 | tf_op jit(solution)/shard_map/ppermute | solution.py:298
  26.8 1.9 %collective-permute-start.6 = (f32[4,128]{1,0:T(4,128)S(1)}, f32[4,128]{1,0:T(4,128)S(1)}, u32[]{:S(2)}, u32[]{:S(2)}) collective-permute-start(f32[4,128]{1,0:T(4,128)S(1)} %shard_map.63.refs_3_), channel_id=1, source_target_pairs={{0,8},{8,0},{16,24},{24,16},{1,9},{9,1},{17,25},{25,17},{2,10},{10... | collective-permute-start | bytes 6152 | tf_op jit(solution)/shard_map/ppermute | solution.py:298
  26.9 3.7 %collective-permute-start.7 = (f32[4,128]{1,0:T(4,128)S(1)}, f32[4,128]{1,0:T(4,128)S(1)}, u32[]{:S(2)}, u32[]{:S(2)}) collective-permute-start(f32[4,128]{1,0:T(4,128)S(1)} %shard_map.63.refs_3_), channel_id=1, source_target_pairs={{0,16},{8,24},{16,0},{24,8},{1,17},{9,25},{17,1},{25,9},{2,18},{10... | collective-permute-start | bytes 6152 | tf_op jit(solution)/shard_map/ppermute | solution.py:298
  27.4 3.1 %collective-permute-start.8 = (f32[4,128]{1,0:T(4,128)S(1)}, f32[4,128]{1,0:T(4,128)S(1)}, u32[]{:S(2)}, u32[]{:S(2)}) collective-permute-start(f32[4,128]{1,0:T(4,128)S(1)} %shard_map.63.refs_3_), channel_id=1, source_target_pairs={{0,24},{8,16},{16,8},{24,0},{1,25},{9,17},{17,9},{25,1},{2,26},{10... | collective-permute-start | bytes 6152 | tf_op jit(solution)/shard_map/ppermute | solution.py:298
  31.7 3.7 %collective-permute-start.11 = (f32[16,128]{1,0:T(8,128)S(1)}, f32[16,128]{1,0:T(8,128)S(1)}, u32[]{:S(2)}, u32[]{:S(2)}) collective-permute-start(f32[16,128]{1,0:T(8,128)S(1)} %get-tuple-element.26), channel_id=1, source_target_pairs={{0,1},{1,0},{2,3},{3,2},{4,5},{5,4},{6,7},{7,6},{8,9},{9,8},{10,11... | collective-permute-start | bytes 24584 | tf_op jit(solution)/shard_map/ppermute | solution.py:298
  33.1 10.8 %collective-permute-start.14 = (f32[192,512]{1,0:T(8,128)S(1)}, f32[192,512]{1,0:T(8,128)S(1)}, u32[]{:S(2)}, u32[]{:S(2)}) collective-permute-start(f32[192,512]{1,0:T(8,128)S(1)} %get-tuple-element.27.refs_8_), channel_id=1, source_target_pairs={{0,16},{8,24},{16,0},{24,8},{1,17},{9,25},{17,1},{25,9},{2,18},{10... | collective-permute-start | bytes 1179656 | tf_op jit(solution)/shard_map/ppermute | solution.py:298
  35.4 3.7 %collective-permute-start.12 = (f32[16,128]{1,0:T(8,128)S(1)}, f32[16,128]{1,0:T(8,128)S(1)}, u32[]{:S(2)}, u32[]{:S(2)}) collective-permute-start(f32[16,128]{1,0:T(8,128)S(1)} %multiply_add_fusion.1), channel_id=1, source_target_pairs={{0,2},{1,3},{2,0},{3,1},{4,6},{5,7},{6,4},{7,5},{8,10},{9,11},{10,... | collective-permute-start | bytes 24584 | tf_op jit(solution)/shard_map/ppermute | solution.py:298
  39.1 17.6 %copy-start.3 = (bf16[512,512]{1,0:T(8,128)(2,1)S(1)}, bf16[512,512]{1,0:T(8,128)(2,1)}, u32[]{:S(2)}) copy-start(bf16[512,512]{1,0:T(8,128)(2,1)} %refs_1_.3) | copy-start | bytes 1572868
  39.1 4.6 %collective-permute-start.13 = (f32[16,128]{1,0:T(8,128)S(1)}, f32[16,128]{1,0:T(8,128)S(1)}, u32[]{:S(2)}, u32[]{:S(2)}) collective-permute-start(f32[16,128]{1,0:T(8,128)S(1)} %multiply_add_fusion.refs_4_), channel_id=1, source_target_pairs={{0,4},{1,5},{2,6},{3,7},{4,0},{5,1},{6,2},{7,3},{8,12},{9,13},{10,... | collective-permute-start | bytes 24584 | tf_op jit(solution)/shard_map/ppermute | solution.py:298
  46.1 10.7 %collective-permute-start.15 = (f32[3,2,128,512]{3,2,1,0:T(8,128)S(1)}, f32[3,2,128,512]{3,2,1,0:T(8,128)S(1)}, u32[]{:S(2)}, u32[]{:S(2)}) collective-permute-start(f32[3,2,128,512]{3,2,1,0:T(8,128)S(1)} %get-tuple-element.28.refs_2_), channel_id=1, source_target_pairs={{0,8},{8,0},{16,24},{24,16},{1,9},{9,1},{17,25},{25,17},{2,10},{10... | collective-permute-start | bytes 4718600 | tf_op jit(solution)/shard_map/ppermute | solution.py:298
  46.2 5.3 %collective-permute-start.23 = (f32[256,512]{1,0:T(8,128)S(1)}, f32[256,512]{1,0:T(8,128)S(1)}, u32[]{:S(2)}, u32[]{:S(2)}) collective-permute-start(f32[256,512]{1,0:T(8,128)S(1)} %get-tuple-element.33), channel_id=1, source_target_pairs={{0,8},{8,0},{16,24},{24,16},{1,9},{9,1},{17,25},{25,17},{2,10},{10... | collective-permute-start | bytes 1572872 | tf_op jit(solution)/shard_map/ppermute | solution.py:298
  46.7 3.0 %collective-permute-start.18 = (f32[4,128]{1,0:T(4,128)S(1)}, f32[4,128]{1,0:T(4,128)S(1)}, u32[]{:S(2)}, u32[]{:S(2)}) collective-permute-start(f32[4,128]{1,0:T(4,128)S(1)} %get-tuple-element.31.lse_ref), channel_id=1, source_target_pairs={{0,24},{8,16},{16,8},{24,0},{1,25},{9,17},{17,9},{25,1},{2,26},{10... | collective-permute-start | bytes 6152 | tf_op jit(solution)/shard_map/ppermute | solution.py:298
  47.9 3.6 %collective-permute-start.17 = (f32[4,128]{1,0:T(4,128)S(1)}, f32[4,128]{1,0:T(4,128)S(1)}, u32[]{:S(2)}, u32[]{:S(2)}) collective-permute-start(f32[4,128]{1,0:T(4,128)S(1)} %get-tuple-element.31.lse_ref), channel_id=1, source_target_pairs={{0,16},{8,24},{16,0},{24,8},{1,17},{9,25},{17,1},{25,9},{2,18},{10... | collective-permute-start | bytes 6152 | tf_op jit(solution)/shard_map/ppermute | solution.py:298
  48.4 3.1 %collective-permute-start.16 = (f32[4,128]{1,0:T(4,128)S(1)}, f32[4,128]{1,0:T(4,128)S(1)}, u32[]{:S(2)}, u32[]{:S(2)}) collective-permute-start(f32[4,128]{1,0:T(4,128)S(1)} %get-tuple-element.31.lse_ref), channel_id=1, source_target_pairs={{0,8},{8,0},{16,24},{24,16},{1,9},{9,1},{17,25},{25,17},{2,10},{10... | collective-permute-start | bytes 6152 | tf_op jit(solution)/shard_map/ppermute | solution.py:298
  51.8 13.2 %collective-permute-start.24 = (f32[256,512]{1,0:T(8,128)S(1)}, f32[256,512]{1,0:T(8,128)S(1)}, u32[]{:S(2)}, u32[]{:S(2)}) collective-permute-start(f32[256,512]{1,0:T(8,128)S(1)} %shard_map.70.one_ref), channel_id=1, source_target_pairs={{0,16},{8,24},{16,0},{24,8},{1,17},{9,25},{17,1},{25,9},{2,18},{10... | collective-permute-start | bytes 1572872 | tf_op jit(solution)/shard_map/ppermute | solution.py:298
  52.4 5.7 %collective-permute-start.19 = (f32[4,128]{1,0:T(4,128)S(1)}, f32[4,128]{1,0:T(4,128)S(1)}, u32[]{:S(2)}, u32[]{:S(2)}) collective-permute-start(f32[4,128]{1,0:T(4,128)S(1)} %get-tuple-element.38.refs_5_), channel_id=1, source_target_pairs={{0,5},{1,4},{2,7},{3,6},{4,1},{5,0},{6,3},{7,2},{8,13},{9,12},{10,... | collective-permute-start | bytes 6152 | tf_op jit(solution)/shard_map/ppermute | solution.py:298
  54.0 4.5 %collective-permute-start.20 = (f32[4,128]{1,0:T(4,128)S(1)}, f32[4,128]{1,0:T(4,128)S(1)}, u32[]{:S(2)}, u32[]{:S(2)}) collective-permute-start(f32[4,128]{1,0:T(4,128)S(1)} %get-tuple-element.38.refs_5_), channel_id=1, source_target_pairs={{0,4},{1,5},{2,6},{3,7},{4,0},{5,1},{6,2},{7,3},{8,12},{9,13},{10,... | collective-permute-start | bytes 6152 | tf_op jit(solution)/shard_map/ppermute | solution.py:298
  55.9 3.6 %collective-permute-start.21 = (f32[4,128]{1,0:T(4,128)S(1)}, f32[4,128]{1,0:T(4,128)S(1)}, u32[]{:S(2)}, u32[]{:S(2)}) collective-permute-start(f32[4,128]{1,0:T(4,128)S(1)} %get-tuple-element.38.refs_5_), channel_id=1, source_target_pairs={{0,1},{1,0},{2,3},{3,2},{4,5},{5,4},{6,7},{7,6},{8,9},{9,8},{10,11... | collective-permute-start | bytes 6152 | tf_op jit(solution)/shard_map/ppermute | solution.py:298
  60.4 12.5 %collective-permute-start.22 = (f32[264,512]{1,0:T(8,128)S(1)}, f32[264,512]{1,0:T(8,128)S(1)}, u32[]{:S(2)}, u32[]{:S(2)}) collective-permute-start(f32[264,512]{1,0:T(8,128)S(1)} %shard_map.68), channel_id=1, source_target_pairs={{0,2},{1,3},{2,0},{3,1},{4,6},{5,7},{6,4},{7,5},{8,10},{9,11},{10,... | collective-permute-start | bytes 1622024 | tf_op jit(solution)/shard_map/ppermute | solution.py:298
  65.0 1.4 %collective-permute-start.25 = (f32[64,512]{1,0:T(8,128)S(1)}, f32[64,512]{1,0:T(8,128)S(1)}, u32[]{:S(2)}, u32[]{:S(2)}) collective-permute-start(f32[64,512]{1,0:T(8,128)S(1)} %get-tuple-element.34.refs_0_), channel_id=1, source_target_pairs={{0,8},{8,0},{16,24},{24,16},{1,9},{9,1},{17,25},{25,17},{2,10},{10... | collective-permute-start | bytes 393224 | tf_op jit(solution)/shard_map/ppermute | solution.py:298
  65.1 1.5 %collective-permute-start.26 = (f32[64,512]{1,0:T(8,128)S(1)}, f32[64,512]{1,0:T(8,128)S(1)}, u32[]{:S(2)}, u32[]{:S(2)}) collective-permute-start(f32[64,512]{1,0:T(8,128)S(1)} %get-tuple-element.35.refs_1_), channel_id=1, source_target_pairs={{0,8},{8,0},{16,24},{24,16},{1,9},{9,1},{17,25},{25,17},{2,10},{10... | collective-permute-start | bytes 393224 | tf_op jit(solution)/shard_map/ppermute | solution.py:298
  65.6 1.3 %collective-permute-start.27 = (f32[64,512]{1,0:T(8,128)S(1)}, f32[64,512]{1,0:T(8,128)S(1)}, u32[]{:S(2)}, u32[]{:S(2)}) collective-permute-start(f32[64,512]{1,0:T(8,128)S(1)} %get-tuple-element.36.refs_2_), channel_id=1, source_target_pairs={{0,8},{8,0},{16,24},{24,16},{1,9},{9,1},{17,25},{25,17},{2,10},{10... | collective-permute-start | bytes 393224 | tf_op jit(solution)/shard_map/ppermute | solution.py:298
  65.7 1.5 %collective-permute-start.28 = (f32[64,512]{1,0:T(8,128)S(1)}, f32[64,512]{1,0:T(8,128)S(1)}, u32[]{:S(2)}, u32[]{:S(2)}) collective-permute-start(f32[64,512]{1,0:T(8,128)S(1)} %get-tuple-element.37.refs_3_), channel_id=1, source_target_pairs={{0,8},{8,0},{16,24},{24,16},{1,9},{9,1},{17,25},{25,17},{2,10},{10... | collective-permute-start | bytes 393224 | tf_op jit(solution)/shard_map/ppermute | solution.py:298

commit v18 on v8

--- a/solution.py
+++ b/solution.py
@@ -165,15 +165,14 @@
     n_rows = mine_ref.shape[0] // LANES
     core = lax.axis_index("row") % 2
     for out_ref, place in ((sent_ref, 1 - core), (mine_ref, core)):
-        columns, totals, weights = [], [], []
+        columns = []
         for j in range(n_rows):
             at = pl.ds(pl.multiple_of((place * n_rows + j) * LANES, LANES), LANES)
             peak, total, exps = over_sources(tile_ref, at, bias)
             columns.append(peak + jnp.log2(total))
-            totals.append(total)
-            weights.append(jnp.concatenate([block.astype(jnp.bfloat16) for block in exps], axis=1))
-        mean = jnp.dot(jnp.concatenate(weights, axis=0), x, preferred_element_type=jnp.float32)
-        out_ref[...] = mean * (1.0 / jnp.concatenate(totals, axis=0))
+            weights = jnp.concatenate([block.astype(jnp.bfloat16) for block in exps], axis=1)
+            mean = jnp.dot(weights, x, preferred_element_type=jnp.float32)
+            out_ref[pl.ds(j * LANES, LANES), :] = mean * (1.0 / total)
         lse_ref[pl.ds(place * n_rows, n_rows), :] = to_dense(columns)
 
 

time: 74.2 us -> 74 us (level)
  no operation moved by 1% of the time
where the time goes in v18:
time: 74 us; the launch traced here: 73.8 us
  starting transfers between devices  29 us (39%)
  waiting for transfers between devices  28.5 us (39%)
  Pallas kernels  12.2 us (16%)
  local copies, waits for them, and re-layouts  3.32 us (4%)
  between operations  0.79 us (1%)
    ppermute x29, starting transfers between devices, swap(): return lax.ppermute(value, axis, [(i, i ^ distance) for i in range(n)])  29 us
    ppermute x29, waiting for transfers between devices, swap(): return lax.ppermute(value, axis, [(i, i ^ distance) for i in range(n)])  28.5 us
    pallas_call x14, Pallas kernels, call(): pl.pallas_call(kernel, out_shape=out_shape, in_specs=in_specs or [VMEM] *...  12.2 us
    unnamed x12, local copies, waits for them, and re-layouts  3.32 us
  transfers between devices with their start and end apart: 29, of which 17 were waited for; matrix products, arithmetic and copies ran while one was open for 0% of the time, Pallas kernels for 11%

profile of v18, /device:TPU:0, one launch (start us, length us, event | category | flops | bytes accessed | tf_op | source)
XLA Modules:
  0.0 73.8 jit_solution(18041776952999500968)
XLA Ops:
  0.6 0.0 copy-start.2
  0.6 1.0 %copy-done.2 = bf16[512,512]{1,0:T(8,128)(2,1)S(1)} copy-done((bf16[512,512]{1,0:T(8,128)(2,1)S(1)}, bf16[512,512]{1,0:T(8,128)(2,1)}, u32[]{:S(2)}) %copy-start.2) | copy-done | bytes 524312
  1.7 4.1 %collective-permute-start.3 = (f32[128,512]{1,0:T(8,128)S(1)}, f32[128,512]{1,0:T(8,128)S(1)}, u32[]{:S(2)}, u32[]{:S(2)}) collective-permute-start(f32[128,512]{1,0:T(8,128)S(1)} %shard_map.61), channel_id=1, source_target_pairs={{0,4},{1,5},{2,6},{3,7},{4,0},{5,1},{6,2},{7,3},{8,12},{9,13},{10,... | collective-permute-start | bytes 786440 | tf_op jit(solution)/shard_map/ppermute | solution.py:298
  5.8 1.5 %collective-permute-start.4 = (f32[128,512]{1,0:T(8,128)S(1)}, f32[128,512]{1,0:T(8,128)S(1)}, u32[]{:S(2)}, u32[]{:S(2)}) collective-permute-start(f32[128,512]{1,0:T(8,128)S(1)} %shard_map.61), channel_id=1, source_target_pairs={{0,1},{1,0},{2,3},{3,2},{4,5},{5,4},{6,7},{7,6},{8,9},{9,8},{10,11... | collective-permute-start | bytes 786440 | tf_op jit(solution)/shard_map/ppermute | solution.py:298
  7.3 1.6 %copy-done = bf16[2048,512]{1,0:T(8,128)(2,1)S(1)} copy-done((bf16[2048,512]{1,0:T(8,128)(2,1)S(1)}, bf16[2048,512]{1,0:T(8,128)(2,1)}, u32[]{:S(2)}) %copy-start) | copy-done | bytes 2097176
  8.9 0.7 copy-done.5
  9.6 1.9 %shard_map.59 = (f32[512,2048]{1,0:T(8,128)S(1)}, f32[16,128]{1,0:T(8,128)S(1)}, f32[4,128]{1,0:T(4,128)S(1)}) custom-call(bf16[512,512]{1,0:T(8,128)(2,1)S(1)} %copy-done.2, bf16[2048,512]{1,0:T(8,128)(2,1)S(1)} %copy-done, f32[4,128]{1,0:T(4,128)S(1)} %bitcast.5), custom_call_target="tpu_custom_call" | custom-call | tf_op jit(solution)/shard_map/pallas_call | solution.py:22
  11.5 1.6 %collective-permute-start = (f32[16,128]{1,0:T(8,128)S(1)}, f32[16,128]{1,0:T(8,128)S(1)}, u32[]{:S(2)}, u32[]{:S(2)}) collective-permute-start(f32[16,128]{1,0:T(8,128)S(1)} %get-tuple-element.22.refs_0_), channel_id=1, source_target_pairs={{0,3},{1,2},{2,1},{3,0},{4,7},{5,6},{6,5},{7,4},{8,11},{9,10},{10,... | collective-permute-start | bytes 24584 | tf_op jit(solution)/shard_map/ppermute | solution.py:298
  13.1 0.4 collective-permute-start.1
  13.5 1.5 %collective-permute-start.2 = (f32[16,128]{1,0:T(8,128)S(1)}, f32[16,128]{1,0:T(8,128)S(1)}, u32[]{:S(2)}, u32[]{:S(2)}) collective-permute-start(f32[16,128]{1,0:T(8,128)S(1)} %get-tuple-element.22.refs_0_), channel_id=1, source_target_pairs={{0,1},{1,0},{2,3},{3,2},{4,5},{5,4},{6,7},{7,6},{8,9},{9,8},{10,11... | collective-permute-start | bytes 24584 | tf_op jit(solution)/shard_map/ppermute | solution.py:298
  15.0 3.9 %collective-permute-done.refs_1_ = f32[16,128]{1,0:T(8,128)S(1)} collective-permute-done((f32[16,128]{1,0:T(8,128)S(1)}, f32[16,128]{1,0:T(8,128)S(1)}, u32[]{:S(2)}, u32[]{:S(2)}) %collective-permute-start) | collective-permute-done | bytes 8224 | tf_op jit(solution)/shard_map/ppermute | solution.py:298
  19.0 0.0 collective-permute-done.3.refs_4_
  19.0 0.0 collective-permute-done.4.refs_5_
  19.0 1.6 %collective-permute-start.10 = (f32[192,512]{1,0:T(8,128)S(1)}, f32[192,512]{1,0:T(8,128)S(1)}, u32[]{:S(2)}, u32[]{:S(2)}) collective-permute-start(f32[192,512]{1,0:T(8,128)S(1)} %get-tuple-element.25.refs_6_), channel_id=1, source_target_pairs={{0,16},{8,24},{16,0},{24,8},{1,17},{9,25},{17,1},{25,9},{2,18},{10... | collective-permute-start | bytes 1179656 | tf_op jit(solution)/shard_map/ppermute | solution.py:298
  20.6 0.6 collective-permute-start.9
  21.3 0.5 shard_map.60.refs_2_.refs_3_
  21.8 4.0 %collective-permute-done.5.refs_4_ = f32[16,128]{1,0:T(8,128)S(1)} collective-permute-done((f32[16,128]{1,0:T(8,128)S(1)}, f32[16,128]{1,0:T(8,128)S(1)}, u32[]{:S(2)}, u32[]{:S(2)}) %collective-permute-start.5) | collective-permute-done | bytes 8224 | tf_op jit(solution)/shard_map/ppermute | solution.py:298
  25.8 1.0 %shard_map.63.refs_3_ = f32[4,128]{1,0:T(4,128)S(1)} custom-call(f32[512,2048]{1,0:T(8,128)S(1)} %get-tuple-element.20.refs_0_, f32[16,128]{1,0:T(8,128)S(1)} %bitcast.3, f32[16,128]{1,0:T(8,128)S(1)} %shard_map.60.refs_2_.refs_3_, f32[16,128]{1,0:T(8,128)S(1)} %get-tuple-element.23.refs_3_, f32[16,128]{1,0:T(8,128)S(1)} %collective-permute-done.5.refs_4_), custom_call_target="tpu_custom_call" | custom-call | tf_op jit(solution)/shard_map/pallas_call | solution.py:22
  26.8 0.0 collective-permute-start.6
  26.9 0.6 collective-permute-start.7
  27.4 1.3 %collective-permute-start.8 = (f32[4,128]{1,0:T(4,128)S(1)}, f32[4,128]{1,0:T(4,128)S(1)}, u32[]{:S(2)}, u32[]{:S(2)}) collective-permute-start(f32[4,128]{1,0:T(4,128)S(1)} %shard_map.63.refs_3_), channel_id=1, source_target_pairs={{0,24},{8,16},{16,8},{24,0},{1,25},{9,17},{17,9},{25,1},{2,26},{10... | collective-permute-start | bytes 6152 | tf_op jit(solution)/shard_map/ppermute | solution.py:298
  28.7 1.8 %collective-permute-done.7.refs_5_ = f32[4,128]{1,0:T(4,128)S(1)} collective-permute-done((f32[4,128]{1,0:T(4,128)S(1)}, f32[4,128]{1,0:T(4,128)S(1)}, u32[]{:S(2)}, u32[]{:S(2)}) %collective-permute-start.7) | collective-permute-done | bytes 2080 | tf_op jit(solution)/shard_map/ppermute | solution.py:298
  30.5 1.1 %shard_map.64 = (f32[16,128]{1,0:T(8,128)S(1)}, f32[192,512]{1,0:T(8,128)S(1)}) custom-call(f32[512,2048]{1,0:T(8,128)S(1)} %get-tuple-element.20.refs_0_, f32[4,128]{1,0:T(4,128)S(1)} %bitcast.6, f32[4,128]{1,0:T(4,128)S(1)} %get-tuple-element.21.refs_2_, f32[4,128]{1,0:T(4,128)S(1)} %shard_map.63.refs_3_, f32[4,128]{1,0:T(4,128)S(1)} %collective-permute-done.6.refs_4_, ...), custom_call_target="tpu_custom_call" | custom-call | tf_op jit(solution)/shard_map/pallas_call | solution.py:22
  31.7 1.4 %collective-permute-start.11 = (f32[16,128]{1,0:T(8,128)S(1)}, f32[16,128]{1,0:T(8,128)S(1)}, u32[]{:S(2)}, u32[]{:S(2)}) collective-permute-start(f32[16,128]{1,0:T(8,128)S(1)} %get-tuple-element.26), channel_id=1, source_target_pairs={{0,1},{1,0},{2,3},{3,2},{4,5},{5,4},{6,7},{7,6},{8,9},{9,8},{10,11... | collective-permute-start | bytes 24584 | tf_op jit(solution)/shard_map/ppermute | solution.py:298
  33.1 1.4 %collective-permute-start.14 = (f32[192,512]{1,0:T(8,128)S(1)}, f32[192,512]{1,0:T(8,128)S(1)}, u32[]{:S(2)}, u32[]{:S(2)}) collective-permute-start(f32[192,512]{1,0:T(8,128)S(1)} %get-tuple-element.27.refs_8_), channel_id=1, source_target_pairs={{0,16},{8,24},{16,0},{24,8},{1,17},{9,25},{17,1},{25,9},{2,18},{10... | collective-permute-start | bytes 1179656 | tf_op jit(solution)/shard_map/ppermute | solution.py:298
  34.5 0.8 %collective-permute-done.11 = f32[16,128]{1,0:T(8,128)S(1)} collective-permute-done((f32[16,128]{1,0:T(8,128)S(1)}, f32[16,128]{1,0:T(8,128)S(1)}, u32[]{:S(2)}, u32[]{:S(2)}) %collective-permute-start.11) | collective-permute-done | bytes 8224 | tf_op jit(solution)/shard_map/ppermute | solution.py:298
  35.4 1.0 %collective-permute-start.12 = (f32[16,128]{1,0:T(8,128)S(1)}, f32[16,128]{1,0:T(8,128)S(1)}, u32[]{:S(2)}, u32[]{:S(2)}) collective-permute-start(f32[16,128]{1,0:T(8,128)S(1)} %multiply_add_fusion.1), channel_id=1, source_target_pairs={{0,2},{1,3},{2,0},{3,1},{4,6},{5,7},{6,4},{7,5},{8,10},{9,11},{10,... | collective-permute-start | bytes 24584 | tf_op jit(solution)/shard_map/ppermute | solution.py:298
  36.4 2.7 %collective-permute-done.12 = f32[16,128]{1,0:T(8,128)S(1)} collective-permute-done((f32[16,128]{1,0:T(8,128)S(1)}, f32[16,128]{1,0:T(8,128)S(1)}, u32[]{:S(2)}, u32[]{:S(2)}) %collective-permute-start.12) | collective-permute-done | bytes 8224 | tf_op jit(solution)/shard_map/ppermute | solution.py:298
  39.1 0.0 copy-start.3
  39.1 1.9 %collective-permute-start.13 = (f32[16,128]{1,0:T(8,128)S(1)}, f32[16,128]{1,0:T(8,128)S(1)}, u32[]{:S(2)}, u32[]{:S(2)}) collective-permute-start(f32[16,128]{1,0:T(8,128)S(1)} %multiply_add_fusion.refs_4_), channel_id=1, source_target_pairs={{0,4},{1,5},{2,6},{3,7},{4,0},{5,1},{6,2},{7,3},{8,12},{9,13},{10,... | collective-permute-start | bytes 24584 | tf_op jit(solution)/shard_map/ppermute | solution.py:298
  41.1 2.7 %collective-permute-done.13.refs_5_ = f32[16,128]{1,0:T(8,128)S(1)} collective-permute-done((f32[16,128]{1,0:T(8,128)S(1)}, f32[16,128]{1,0:T(8,128)S(1)}, u32[]{:S(2)}, u32[]{:S(2)}) %collective-permute-start.13) | collective-permute-done | bytes 8224 | tf_op jit(solution)/shard_map/ppermute | solution.py:298
  43.7 0.2 collective-permute-done.14.refs_9_
  43.9 2.0 %shard_map.65 = (f32[4,128]{1,0:T(4,128)S(1)}, f32[256,512]{1,0:T(8,128)S(1)}, f32[256,512]{1,0:T(8,128)S(1)}, f32[3,2,128,512]{3,2,1,0:T(8,128)S(1)}) custom-call(f32[512,2048]{1,0:T(8,128)S(1)} %get-tuple-element.20.refs_0_, bf16[2048,512]{1,0:T(8,128)(2,1)S(1)} %copy-done.1, f32[16,128]{1,0:T(8,128)S(1)} %bitcast.4, ...), custom_call_target="tpu_custom_call" | custom-call | tf_op jit(solution)/shard_map/pallas_call | solution.py:22
  46.0 0.1 collective-permute-start.15
  46.0 0.5 collective-permute-start.23
  46.5 1.2 %collective-permute-start.18 = (f32[4,128]{1,0:T(4,128)S(1)}, f32[4,128]{1,0:T(4,128)S(1)}, u32[]{:S(2)}, u32[]{:S(2)}) collective-permute-start(f32[4,128]{1,0:T(4,128)S(1)} %get-tuple-element.31.lse_ref), channel_id=1, source_target_pairs={{0,24},{8,16},{16,8},{24,0},{1,25},{9,17},{17,9},{25,1},{2,26},{10... | collective-permute-start | bytes 6152 | tf_op jit(solution)/shard_map/ppermute | solution.py:298
  47.7 0.5 collective-permute-start.17
  48.2 0.2 collective-permute-start.16
  48.4 1.1 %collective-permute-done.18 = f32[4,128]{1,0:T(4,128)S(1)} collective-permute-done((f32[4,128]{1,0:T(4,128)S(1)}, f32[4,128]{1,0:T(4,128)S(1)}, u32[]{:S(2)}, u32[]{:S(2)}) %collective-permute-start.18) | collective-permute-done | bytes 2080 | tf_op jit(solution)/shard_map/ppermute | solution.py:298
  49.5 1.8 %collective-permute-done.17 = f32[4,128]{1,0:T(4,128)S(1)} collective-permute-done((f32[4,128]{1,0:T(4,128)S(1)}, f32[4,128]{1,0:T(4,128)S(1)}, u32[]{:S(2)}, u32[]{:S(2)}) %collective-permute-start.17) | collective-permute-done | bytes 2080 | tf_op jit(solution)/shard_map/ppermute | solution.py:298
  51.3 0.3 shard_map.70.one_ref
  51.7 0.6 collective-permute-start.24
  52.2 1.6 %collective-permute-start.19 = (f32[4,128]{1,0:T(4,128)S(1)}, f32[4,128]{1,0:T(4,128)S(1)}, u32[]{:S(2)}, u32[]{:S(2)}) collective-permute-start(f32[4,128]{1,0:T(4,128)S(1)} %get-tuple-element.38.refs_5_), channel_id=1, source_target_pairs={{0,5},{1,4},{2,7},{3,6},{4,1},{5,0},{6,3},{7,2},{8,13},{9,12},{10,... | collective-permute-start | bytes 6152 | tf_op jit(solution)/shard_map/ppermute | solution.py:298
  53.9 1.9 %collective-permute-start.20 = (f32[4,128]{1,0:T(4,128)S(1)}, f32[4,128]{1,0:T(4,128)S(1)}, u32[]{:S(2)}, u32[]{:S(2)}) collective-permute-start(f32[4,128]{1,0:T(4,128)S(1)} %get-tuple-element.38.refs_5_), channel_id=1, source_target_pairs={{0,4},{1,5},{2,6},{3,7},{4,0},{5,1},{6,2},{7,3},{8,12},{9,13},{10,... | collective-permute-start | bytes 6152 | tf_op jit(solution)/shard_map/ppermute | solution.py:298
  55.8 0.8 %collective-permute-start.21 = (f32[4,128]{1,0:T(4,128)S(1)}, f32[4,128]{1,0:T(4,128)S(1)}, u32[]{:S(2)}, u32[]{:S(2)}) collective-permute-start(f32[4,128]{1,0:T(4,128)S(1)} %get-tuple-element.38.refs_5_), channel_id=1, source_target_pairs={{0,1},{1,0},{2,3},{3,2},{4,5},{5,4},{6,7},{7,6},{8,9},{9,8},{10,11... | collective-permute-start | bytes 6152 | tf_op jit(solution)/shard_map/ppermute | solution.py:298
  56.6 1.3 %shard_map.66 = (bf16[2048,512]{1,0:T(8,128)(2,1)S(1)}, f32[512,2048]{1,0:T(8,128)S(1)}) custom-call(bf16[2048,512]{1,0:T(8,128)(2,1)S(1)} %copy-done.1, bf16[512,512]{1,0:T(8,128)(2,1)S(1)} %copy-done.3, f32[3,2,128,512]{3,2,1,0:T(8,128)S(1)} %get-tuple-element.28.refs_2_, f32[3,2,128,512]{3,2,1,0:T(8,128)S(1)} %collective-permute-done.15.refs_3_), custom_call_target="tpu_custom_call" | custom-call | tf_op jit(solution)/shard_map/pallas_call | solution.py:22
  58.0 0.4 collective-permute-done.20.refs_3_
  58.4 1.0 %collective-permute-done.21.refs_4_ = f32[4,128]{1,0:T(4,128)S(1)} collective-permute-done((f32[4,128]{1,0:T(4,128)S(1)}, f32[4,128]{1,0:T(4,128)S(1)}, u32[]{:S(2)}, u32[]{:S(2)}) %collective-permute-start.21) | collective-permute-done | bytes 2080 | tf_op jit(solution)/shard_map/ppermute | solution.py:298
  59.4 0.9 %shard_map.68 = f32[264,512]{1,0:T(8,128)S(1)} custom-call(f32[512,2048]{1,0:T(8,128)S(1)} %get-tuple-element.29.refs_0_, bf16[2048,512]{1,0:T(8,128)(2,1)S(1)} %get-tuple-element.30.refs_1_, f32[4,128]{1,0:T(4,128)S(1)} %collective-permute-done.19.refs_2_, f32[4,128]{1,0:T(4,128)S(1)} %collective-permute-done.20.refs_3_, ...), custom_call_target="tpu_custom_call" | custom-call | tf_op jit(solution)/shard_map/pallas_call | solution.py:22
  60.3 1.4 %collective-permute-start.22 = (f32[264,512]{1,0:T(8,128)S(1)}, f32[264,512]{1,0:T(8,128)S(1)}, u32[]{:S(2)}, u32[]{:S(2)}) collective-permute-start(f32[264,512]{1,0:T(8,128)S(1)} %shard_map.68), channel_id=1, source_target_pairs={{0,2},{1,3},{2,0},{3,1},{4,6},{5,7},{6,4},{7,5},{8,10},{9,11},{10,... | collective-permute-start | bytes 1622024 | tf_op jit(solution)/shard_map/ppermute | solution.py:298
  61.6 3.2 %collective-permute-done.24.two_ref = f32[256,512]{1,0:T(8,128)S(1)} collective-permute-done((f32[256,512]{1,0:T(8,128)S(1)}, f32[256,512]{1,0:T(8,128)S(1)}, u32[]{:S(2)}, u32[]{:S(2)}) %collective-permute-start.24) | collective-permute-done | bytes 524320 | tf_op jit(solution)/shard_map/ppermute | solution.py:298
  64.8 0.1 shard_map.71
  64.9 0.1 collective-permute-start.25
  65.0 0.5 collective-permute-start.26
  65.5 0.1 collective-permute-start.27
  65.6 0.4 collective-permute-start.28
  66.0 0.3 collective-permute-done.25.refs_4_
  66.3 0.2 collective-permute-done.26.refs_5_
  66.5 0.3 collective-permute-done.27.refs_6_
  66.8 0.2 collective-permute-done.28.refs_7_
  67.0 1.0 %shard_map.72 = f32[512,512]{1,0:T(8,128)} custom-call(f32[64,512]{1,0:T(8,128)S(1)} %get-tuple-element.34.refs_0_, f32[64,512]{1,0:T(8,128)S(1)} %get-tuple-element.35.refs_1_, f32[64,512]{1,0:T(8,128)S(1)} %get-tuple-element.36.refs_2_, f32[64,512]{1,0:T(8,128)S(1)} %get-tuple-element.37.refs_3_, f32[64,512]{1,0:T(8,128)S(1)} %collective-permute-done.25.refs_4_, ...), custom_call_target="tpu_custom_call" | custom-call | tf_op jit(solution)/shard_map/pallas_call | solution.py:22
  68.1 0.9 %shard_map.67.refs_0_ = f32[264,512]{1,0:T(8,128)S(1)} custom-call(f32[512,2048]{1,0:T(8,128)S(1)} %get-tuple-element.29.refs_0_, bf16[2048,512]{1,0:T(8,128)(2,1)S(1)} %get-tuple-element.30.refs_1_, f32[4,128]{1,0:T(4,128)S(1)} %collective-permute-done.19.refs_2_, f32[4,128]{1,0:T(4,128)S(1)} %collective-permute-done.20.refs_3_, ...), custom_call_target="tpu_custom_call" | custom-call | tf_op jit(solution)/shard_map/pallas_call | solution.py:22
  68.9 3.8 %collective-permute-done.22.refs_1_ = f32[264,512]{1,0:T(8,128)S(1)} collective-permute-done((f32[264,512]{1,0:T(8,128)S(1)}, f32[264,512]{1,0:T(8,128)S(1)}, u32[]{:S(2)}, u32[]{:S(2)}) %collective-permute-start.22) | collective-permute-done | bytes 540704 | tf_op jit(solution)/shard_map/ppermute | solution.py:298
  72.7 1.1 %shard_map.69 = f32[256,512]{1,0:T(8,128)} custom-call(f32[264,512]{1,0:T(8,128)S(1)} %shard_map.67.refs_0_, f32[264,512]{1,0:T(8,128)S(1)} %collective-permute-done.22.refs_1_), custom_call_target="tpu_custom_call" | custom-call | tf_op jit(solution)/shard_map/pallas_call | solution.py:22
  (23 shorter events, 0.2 us)
Async XLA Ops:
  0.6 1.0 %copy-start.2 = (bf16[512,512]{1,0:T(8,128)(2,1)S(1)}, bf16[512,512]{1,0:T(8,128)(2,1)}, u32[]{:S(2)}) copy-start(bf16[512,512]{1,0:T(8,128)(2,1)} %refs_1_.3) | copy-start | bytes 1572868
  1.7 17.3 %collective-permute-start.3 = (f32[128,512]{1,0:T(8,128)S(1)}, f32[128,512]{1,0:T(8,128)S(1)}, u32[]{:S(2)}, u32[]{:S(2)}) collective-permute-start(f32[128,512]{1,0:T(8,128)S(1)} %shard_map.61), channel_id=1, source_target_pairs={{0,4},{1,5},{2,6},{3,7},{4,0},{5,1},{6,2},{7,3},{8,12},{9,13},{10,... | collective-permute-start | bytes 786440 | tf_op jit(solution)/shard_map/ppermute | solution.py:298
  5.8 13.2 %collective-permute-start.4 = (f32[128,512]{1,0:T(8,128)S(1)}, f32[128,512]{1,0:T(8,128)S(1)}, u32[]{:S(2)}, u32[]{:S(2)}) collective-permute-start(f32[128,512]{1,0:T(8,128)S(1)} %shard_map.61), channel_id=1, source_target_pairs={{0,1},{1,0},{2,3},{3,2},{4,5},{5,4},{6,7},{7,6},{8,9},{9,8},{10,11... | collective-permute-start | bytes 786440 | tf_op jit(solution)/shard_map/ppermute | solution.py:298
  7.3 1.6 %copy-start = (bf16[2048,512]{1,0:T(8,128)(2,1)S(1)}, bf16[2048,512]{1,0:T(8,128)(2,1)}, u32[]{:S(2)}) copy-start(bf16[2048,512]{1,0:T(8,128)(2,1)} %refs_0_.1) | copy-start | bytes 6291460
  8.9 0.7 copy-start.5
  9.6 11.7 %copy-start.1 = (bf16[2048,512]{1,0:T(8,128)(2,1)S(1)}, bf16[2048,512]{1,0:T(8,128)(2,1)}, u32[]{:S(2)}) copy-start(bf16[2048,512]{1,0:T(8,128)(2,1)} %refs_0_.1) | copy-start | bytes 6291460
  9.6 16.3 %copy-start.4 = (f32[2048]{0:T(1024)S(1)}, f32[2048]{0:T(1024)}, u32[]{:S(2)}) copy-start(f32[2048]{0:T(1024)} %param.6) | copy-start | bytes 24580
  11.5 7.5 %collective-permute-start = (f32[16,128]{1,0:T(8,128)S(1)}, f32[16,128]{1,0:T(8,128)S(1)}, u32[]{:S(2)}, u32[]{:S(2)}) collective-permute-start(f32[16,128]{1,0:T(8,128)S(1)} %get-tuple-element.22.refs_0_), channel_id=1, source_target_pairs={{0,3},{1,2},{2,1},{3,0},{4,7},{5,6},{6,5},{7,4},{8,11},{9,10},{10,... | collective-permute-start | bytes 24584 | tf_op jit(solution)/shard_map/ppermute | solution.py:298
  13.1 5.9 %collective-permute-start.1 = (f32[16,128]{1,0:T(8,128)S(1)}, f32[16,128]{1,0:T(8,128)S(1)}, u32[]{:S(2)}, u32[]{:S(2)}) collective-permute-start(f32[16,128]{1,0:T(8,128)S(1)} %get-tuple-element.22.refs_0_), channel_id=1, source_target_pairs={{0,2},{1,3},{2,0},{3,1},{4,6},{5,7},{6,4},{7,5},{8,10},{9,11},{10,... | collective-permute-start | bytes 24584 | tf_op jit(solution)/shard_map/ppermute | solution.py:298
  13.5 5.4 %collective-permute-start.2 = (f32[16,128]{1,0:T(8,128)S(1)}, f32[16,128]{1,0:T(8,128)S(1)}, u32[]{:S(2)}, u32[]{:S(2)}) collective-permute-start(f32[16,128]{1,0:T(8,128)S(1)} %get-tuple-element.22.refs_0_), channel_id=1, source_target_pairs={{0,1},{1,0},{2,3},{3,2},{4,5},{5,4},{6,7},{7,6},{8,9},{9,8},{10,11... | collective-permute-start | bytes 24584 | tf_op jit(solution)/shard_map/ppermute | solution.py:298
  19.0 11.5 %collective-permute-start.10 = (f32[192,512]{1,0:T(8,128)S(1)}, f32[192,512]{1,0:T(8,128)S(1)}, u32[]{:S(2)}, u32[]{:S(2)}) collective-permute-start(f32[192,512]{1,0:T(8,128)S(1)} %get-tuple-element.25.refs_6_), channel_id=1, source_target_pairs={{0,16},{8,24},{16,0},{24,8},{1,17},{9,25},{17,1},{25,9},{2,18},{10... | collective-permute-start | bytes 1179656 | tf_op jit(solution)/shard_map/ppermute | solution.py:298
  20.6 9.9 %collective-permute-start.9 = (f32[128,512]{1,0:T(8,128)S(1)}, f32[128,512]{1,0:T(8,128)S(1)}, u32[]{:S(2)}, u32[]{:S(2)}) collective-permute-start(f32[128,512]{1,0:T(8,128)S(1)} %get-tuple-element.24.refs_7_), channel_id=1, source_target_pairs={{0,1},{1,0},{2,3},{3,2},{4,5},{5,4},{6,7},{7,6},{8,9},{9,8},{10,11... | collective-permute-start | bytes 786440 | tf_op jit(solution)/shard_map/ppermute | solution.py:298
  21.3 4.5 %collective-permute-start.5 = (f32[16,128]{1,0:T(8,128)S(1)}, f32[16,128]{1,0:T(8,128)S(1)}, u32[]{:S(2)}, u32[]{:S(2)}) collective-permute-start(f32[16,128]{1,0:T(8,128)S(1)} %get-tuple-element.23.refs_3_), channel_id=1, source_target_pairs={{0,4},{1,5},{2,6},{3,7},{4,0},{5,1},{6,2},{7,3},{8,12},{9,13},{10,... | collective-permute-start | bytes 24584 | tf_op jit(solution)/shard_map/ppermute | solution.py:298
  26.8 1.9 %collective-permute-start.6 = (f32[4,128]{1,0:T(4,128)S(1)}, f32[4,128]{1,0:T(4,128)S(1)}, u32[]{:S(2)}, u32[]{:S(2)}) collective-permute-start(f32[4,128]{1,0:T(4,128)S(1)} %shard_map.63.refs_3_), channel_id=1, source_target_pairs={{0,8},{8,0},{16,24},{24,16},{1,9},{9,1},{17,25},{25,17},{2,10},{10... | collective-permute-start | bytes 6152 | tf_op jit(solution)/shard_map/ppermute | solution.py:298
  26.9 3.7 %collective-permute-start.7 = (f32[4,128]{1,0:T(4,128)S(1)}, f32[4,128]{1,0:T(4,128)S(1)}, u32[]{:S(2)}, u32[]{:S(2)}) collective-permute-start(f32[4,128]{1,0:T(4,128)S(1)} %shard_map.63.refs_3_), channel_id=1, source_target_pairs={{0,16},{8,24},{16,0},{24,8},{1,17},{9,25},{17,1},{25,9},{2,18},{10... | collective-permute-start | bytes 6152 | tf_op jit(solution)/shard_map/ppermute | solution.py:298
  27.4 3.1 %collective-permute-start.8 = (f32[4,128]{1,0:T(4,128)S(1)}, f32[4,128]{1,0:T(4,128)S(1)}, u32[]{:S(2)}, u32[]{:S(2)}) collective-permute-start(f32[4,128]{1,0:T(4,128)S(1)} %shard_map.63.refs_3_), channel_id=1, source_target_pairs={{0,24},{8,16},{16,8},{24,0},{1,25},{9,17},{17,9},{25,1},{2,26},{10... | collective-permute-start | bytes 6152 | tf_op jit(solution)/shard_map/ppermute | solution.py:298
  31.7 3.7 %collective-permute-start.11 = (f32[16,128]{1,0:T(8,128)S(1)}, f32[16,128]{1,0:T(8,128)S(1)}, u32[]{:S(2)}, u32[]{:S(2)}) collective-permute-start(f32[16,128]{1,0:T(8,128)S(1)} %get-tuple-element.26), channel_id=1, source_target_pairs={{0,1},{1,0},{2,3},{3,2},{4,5},{5,4},{6,7},{7,6},{8,9},{9,8},{10,11... | collective-permute-start | bytes 24584 | tf_op jit(solution)/shard_map/ppermute | solution.py:298
  33.1 10.8 %collective-permute-start.14 = (f32[192,512]{1,0:T(8,128)S(1)}, f32[192,512]{1,0:T(8,128)S(1)}, u32[]{:S(2)}, u32[]{:S(2)}) collective-permute-start(f32[192,512]{1,0:T(8,128)S(1)} %get-tuple-element.27.refs_8_), channel_id=1, source_target_pairs={{0,16},{8,24},{16,0},{24,8},{1,17},{9,25},{17,1},{25,9},{2,18},{10... | collective-permute-start | bytes 1179656 | tf_op jit(solution)/shard_map/ppermute | solution.py:298
  35.4 3.7 %collective-permute-start.12 = (f32[16,128]{1,0:T(8,128)S(1)}, f32[16,128]{1,0:T(8,128)S(1)}, u32[]{:S(2)}, u32[]{:S(2)}) collective-permute-start(f32[16,128]{1,0:T(8,128)S(1)} %multiply_add_fusion.1), channel_id=1, source_target_pairs={{0,2},{1,3},{2,0},{3,1},{4,6},{5,7},{6,4},{7,5},{8,10},{9,11},{10,... | collective-permute-start | bytes 24584 | tf_op jit(solution)/shard_map/ppermute | solution.py:298
  39.1 17.5 %copy-start.3 = (bf16[512,512]{1,0:T(8,128)(2,1)S(1)}, bf16[512,512]{1,0:T(8,128)(2,1)}, u32[]{:S(2)}) copy-start(bf16[512,512]{1,0:T(8,128)(2,1)} %refs_1_.3) | copy-start | bytes 1572868
  39.1 4.6 %collective-permute-start.13 = (f32[16,128]{1,0:T(8,128)S(1)}, f32[16,128]{1,0:T(8,128)S(1)}, u32[]{:S(2)}, u32[]{:S(2)}) collective-permute-start(f32[16,128]{1,0:T(8,128)S(1)} %multiply_add_fusion.refs_4_), channel_id=1, source_target_pairs={{0,4},{1,5},{2,6},{3,7},{4,0},{5,1},{6,2},{7,3},{8,12},{9,13},{10,... | collective-permute-start | bytes 24584 | tf_op jit(solution)/shard_map/ppermute | solution.py:298
  46.0 10.7 %collective-permute-start.15 = (f32[3,2,128,512]{3,2,1,0:T(8,128)S(1)}, f32[3,2,128,512]{3,2,1,0:T(8,128)S(1)}, u32[]{:S(2)}, u32[]{:S(2)}) collective-permute-start(f32[3,2,128,512]{3,2,1,0:T(8,128)S(1)} %get-tuple-element.28.refs_2_), channel_id=1, source_target_pairs={{0,8},{8,0},{16,24},{24,16},{1,9},{9,1},{17,25},{25,17},{2,10},{10... | collective-permute-start | bytes 4718600 | tf_op jit(solution)/shard_map/ppermute | solution.py:298
  46.0 5.3 %collective-permute-start.23 = (f32[256,512]{1,0:T(8,128)S(1)}, f32[256,512]{1,0:T(8,128)S(1)}, u32[]{:S(2)}, u32[]{:S(2)}) collective-permute-start(f32[256,512]{1,0:T(8,128)S(1)} %get-tuple-element.33), channel_id=1, source_target_pairs={{0,8},{8,0},{16,24},{24,16},{1,9},{9,1},{17,25},{25,17},{2,10},{10... | collective-permute-start | bytes 1572872 | tf_op jit(solution)/shard_map/ppermute | solution.py:298
  46.5 3.0 %collective-permute-start.18 = (f32[4,128]{1,0:T(4,128)S(1)}, f32[4,128]{1,0:T(4,128)S(1)}, u32[]{:S(2)}, u32[]{:S(2)}) collective-permute-start(f32[4,128]{1,0:T(4,128)S(1)} %get-tuple-element.31.lse_ref), channel_id=1, source_target_pairs={{0,24},{8,16},{16,8},{24,0},{1,25},{9,17},{17,9},{25,1},{2,26},{10... | collective-permute-start | bytes 6152 | tf_op jit(solution)/shard_map/ppermute | solution.py:298
  47.7 3.6 %collective-permute-start.17 = (f32[4,128]{1,0:T(4,128)S(1)}, f32[4,128]{1,0:T(4,128)S(1)}, u32[]{:S(2)}, u32[]{:S(2)}) collective-permute-start(f32[4,128]{1,0:T(4,128)S(1)} %get-tuple-element.31.lse_ref), channel_id=1, source_target_pairs={{0,16},{8,24},{16,0},{24,8},{1,17},{9,25},{17,1},{25,9},{2,18},{10... | collective-permute-start | bytes 6152 | tf_op jit(solution)/shard_map/ppermute | solution.py:298
  48.2 3.1 %collective-permute-start.16 = (f32[4,128]{1,0:T(4,128)S(1)}, f32[4,128]{1,0:T(4,128)S(1)}, u32[]{:S(2)}, u32[]{:S(2)}) collective-permute-start(f32[4,128]{1,0:T(4,128)S(1)} %get-tuple-element.31.lse_ref), channel_id=1, source_target_pairs={{0,8},{8,0},{16,24},{24,16},{1,9},{9,1},{17,25},{25,17},{2,10},{10... | collective-permute-start | bytes 6152 | tf_op jit(solution)/shard_map/ppermute | solution.py:298
  51.7 13.2 %collective-permute-start.24 = (f32[256,512]{1,0:T(8,128)S(1)}, f32[256,512]{1,0:T(8,128)S(1)}, u32[]{:S(2)}, u32[]{:S(2)}) collective-permute-start(f32[256,512]{1,0:T(8,128)S(1)} %shard_map.70.one_ref), channel_id=1, source_target_pairs={{0,16},{8,24},{16,0},{24,8},{1,17},{9,25},{17,1},{25,9},{2,18},{10... | collective-permute-start | bytes 1572872 | tf_op jit(solution)/shard_map/ppermute | solution.py:298
  52.2 5.7 %collective-permute-start.19 = (f32[4,128]{1,0:T(4,128)S(1)}, f32[4,128]{1,0:T(4,128)S(1)}, u32[]{:S(2)}, u32[]{:S(2)}) collective-permute-start(f32[4,128]{1,0:T(4,128)S(1)} %get-tuple-element.38.refs_5_), channel_id=1, source_target_pairs={{0,5},{1,4},{2,7},{3,6},{4,1},{5,0},{6,3},{7,2},{8,13},{9,12},{10,... | collective-permute-start | bytes 6152 | tf_op jit(solution)/shard_map/ppermute | solution.py:298
  53.9 4.5 %collective-permute-start.20 = (f32[4,128]{1,0:T(4,128)S(1)}, f32[4,128]{1,0:T(4,128)S(1)}, u32[]{:S(2)}, u32[]{:S(2)}) collective-permute-start(f32[4,128]{1,0:T(4,128)S(1)} %get-tuple-element.38.refs_5_), channel_id=1, source_target_pairs={{0,4},{1,5},{2,6},{3,7},{4,0},{5,1},{6,2},{7,3},{8,12},{9,13},{10,... | collective-permute-start | bytes 6152 | tf_op jit(solution)/shard_map/ppermute | solution.py:298
  55.8 3.6 %collective-permute-start.21 = (f32[4,128]{1,0:T(4,128)S(1)}, f32[4,128]{1,0:T(4,128)S(1)}, u32[]{:S(2)}, u32[]{:S(2)}) collective-permute-start(f32[4,128]{1,0:T(4,128)S(1)} %get-tuple-element.38.refs_5_), channel_id=1, source_target_pairs={{0,1},{1,0},{2,3},{3,2},{4,5},{5,4},{6,7},{7,6},{8,9},{9,8},{10,11... | collective-permute-start | bytes 6152 | tf_op jit(solution)/shard_map/ppermute | solution.py:298
  60.3 12.5 %collective-permute-start.22 = (f32[264,512]{1,0:T(8,128)S(1)}, f32[264,512]{1,0:T(8,128)S(1)}, u32[]{:S(2)}, u32[]{:S(2)}) collective-permute-start(f32[264,512]{1,0:T(8,128)S(1)} %shard_map.68), channel_id=1, source_target_pairs={{0,2},{1,3},{2,0},{3,1},{4,6},{5,7},{6,4},{7,5},{8,10},{9,11},{10,... | collective-permute-start | bytes 1622024 | tf_op jit(solution)/shard_map/ppermute | solution.py:298
  64.9 1.4 %collective-permute-start.25 = (f32[64,512]{1,0:T(8,128)S(1)}, f32[64,512]{1,0:T(8,128)S(1)}, u32[]{:S(2)}, u32[]{:S(2)}) collective-permute-start(f32[64,512]{1,0:T(8,128)S(1)} %get-tuple-element.34.refs_0_), channel_id=1, source_target_pairs={{0,8},{8,0},{16,24},{24,16},{1,9},{9,1},{17,25},{25,17},{2,10},{10... | collective-permute-start | bytes 393224 | tf_op jit(solution)/shard_map/ppermute | solution.py:298
  65.0 1.5 %collective-permute-start.26 = (f32[64,512]{1,0:T(8,128)S(1)}, f32[64,512]{1,0:T(8,128)S(1)}, u32[]{:S(2)}, u32[]{:S(2)}) collective-permute-start(f32[64,512]{1,0:T(8,128)S(1)} %get-tuple-element.35.refs_1_), channel_id=1, source_target_pairs={{0,8},{8,0},{16,24},{24,16},{1,9},{9,1},{17,25},{25,17},{2,10},{10... | collective-permute-start | bytes 393224 | tf_op jit(solution)/shard_map/ppermute | solution.py:298
  65.5 1.3 %collective-permute-start.27 = (f32[64,512]{1,0:T(8,128)S(1)}, f32[64,512]{1,0:T(8,128)S(1)}, u32[]{:S(2)}, u32[]{:S(2)}) collective-permute-start(f32[64,512]{1,0:T(8,128)S(1)} %get-tuple-element.36.refs_2_), channel_id=1, source_target_pairs={{0,8},{8,0},{16,24},{24,16},{1,9},{9,1},{17,25},{25,17},{2,10},{10... | collective-permute-start | bytes 393224 | tf_op jit(solution)/shard_map/ppermute | solution.py:298
  65.6 1.5 %collective-permute-start.28 = (f32[64,512]{1,0:T(8,128)S(1)}, f32[64,512]{1,0:T(8,128)S(1)}, u32[]{:S(2)}, u32[]{:S(2)}) collective-permute-start(f32[64,512]{1,0:T(8,128)S(1)} %get-tuple-element.37.refs_3_), channel_id=1, source_target_pairs={{0,8},{8,0},{16,24},{24,16},{1,9},{9,1},{17,25},{25,17},{2,10},{10... | collective-permute-start | bytes 393224 | tf_op jit(solution)/shard_map/ppermute | solution.py:298
